TPU v7x, 32 devices: a whole 2x2x4 slice. The times are simulated.
32 devices in a mesh: grp: 4 (over y, x), feat: 8 (over z, core).
Axes of the slice: x: 2, y: 2, z: 4, core: 2. Of those that a mesh axis runs over, the one named last changes fastest.
Arguments:
- resid: bfloat16 [4, 512, 2304], P(None, 'grp'), may hold values from -6 to 6
- w_enc: bfloat16 [4, 2304, 8192], P(None, None, 'feat'), may hold values from -0.125 to 0.125
- b_enc: float32 [4, 8192], P(None, 'feat'), may hold values from -3 to 3
- w_dec: bfloat16 [4, 4, 8192, 2304], P(None, 'grp', 'feat'), may hold values from -0.0625 to 0.0625
- targets: bfloat16 [4, 512, 2304], P('grp'), may hold values from -6 to 6
- start_layer: int32 [4, 8], P(None, 'feat'), may hold values from 0 to 3, as said below
Outputs:
- active: bfloat16 [512, 4, 8192], P('grp', None, 'feat')
- recon: bfloat16 [4, 512, 2304], P('grp', 'feat')
- recon_loss: float32 [], replicated
- feat_grad: float32 [512, 4, 8192], P('grp', None, 'feat')
Inputs may be any that keep to these rules, and one draw needn't show every extreme that they name: `start_layer`: each column is nondecreasing over source layers; in every column the first source feeds from target 0 and the last source feeds only target 4 - 1.
All inputs are finite; a program needn't handle non-finite values.
Results may differ from a plain program's by a relative error of at most 0.0049.
Values may be sent and summed in bfloat16 or wider, within the bound.
No kernel may reach another device: no remote copies, remote signals or barrier semaphores. Data moves between devices by JAX's collectives and lax.ppermute only.
A program may use at most 128 MiB of HBM per device.

v0:
```python
from functools import partial

import jax
import jax.numpy as jnp
from jax import lax
from jax.sharding import PartitionSpec as P


def per_device(resid, w_enc, b_enc, w_dec, targets, start_layer):
    sources = resid.shape[0]
    targets_here = w_dec.shape[1]
    model_width = resid.shape[2]
    block_width = w_dec.shape[2]
    group_index = lax.axis_index("grp")
    target_ids = group_index * targets_here + jnp.arange(targets_here, dtype=jnp.int32)
    feeds_mask = target_ids[None, :] >= start_layer[:, 0][:, None]
    feeds_value = feeds_mask.astype(jnp.float32)

    def masked(source, target, product):
        return feeds_value[source, target] * product()

    encoded = []
    for source in range(sources):
        pre_act = (
            jnp.dot(resid[source], w_enc[source], preferred_element_type=jnp.float32)
            + b_enc[source]
        )
        encoded.append(jnp.maximum(pre_act, 0.0).astype(jnp.bfloat16))
    active = jnp.stack(encoded, axis=1)
    piece_rows = lax.all_gather(active, "grp", axis=0, tiled=True)
    row_count = piece_rows.shape[0]
    target = 0
    summed = jnp.zeros((row_count, model_width), jnp.float32)
    for source in range(sources):
        product = partial(
            jnp.dot,
            piece_rows[:, source],
            w_dec[source, target],
            preferred_element_type=jnp.float32,
        )
        summed = summed + masked(source, target, product)
    outputs = [summed]
    partial_sums = jnp.stack(outputs, axis=0)
    tokens = partial_sums.shape[1]
    rows_feat = tokens // lax.axis_size("feat")
    my_first = lax.axis_index("feat") * rows_feat
    recon_rows = lax.psum_scatter(partial_sums, "feat", scatter_dimension=1, tiled=True)
    own_targets = lax.dynamic_slice_in_dim(targets, my_first, rows_feat, 1)
    difference = recon_rows - own_targets.astype(jnp.float32)
    error_all = lax.all_gather(difference.astype(jnp.bfloat16), "feat", axis=1, tiled=True)
    squares = jnp.sum(difference * difference)
    entries = targets_here * lax.axis_size("grp") * tokens * model_width
    recon_loss = lax.psum(squares, ("grp", "feat")) / entries
    row_count = active.shape[0] * lax.axis_size("grp")
    error_block = lax.slice_in_dim(error_all, 0, row_count, axis=1)
    gradients = []
    for source in range(sources):
        summed = jnp.zeros((row_count, block_width), jnp.float32)
        target = 0
        product = partial(
            lax.dot_general,
            error_block[target],
            w_dec[source, target],
            (((1,), (1,)), ((), ())),
            preferred_element_type=jnp.float32,
        )
        summed = summed + masked(source, target, product)
        gradients.append(summed)
    feat_grad = lax.psum_scatter(
        jnp.stack(gradients, axis=1), "grp", scatter_dimension=0, tiled=True
    )
    return (active, recon_rows.astype(jnp.bfloat16), recon_loss, feat_grad)


def solution(mesh):
    in_specs = (
        P(None, "grp", None),
        P(None, None, "feat"),
        P(None, "feat"),
        P(None, "grp", "feat", None),
        P("grp", None, None),
        P(None, "feat"),
    )
    out_specs = (P("grp", None, "feat"), P("grp", "feat", None), P(), P("grp", None, "feat"))
    return jax.shard_map(
        per_device, mesh=mesh, in_specs=in_specs, out_specs=out_specs, check_vma=False
    )
```

profile of v0, /device:TPU:0, one launch (start us, length us, event | category | flops | bytes accessed | tf_op | source)
XLA Modules:
  0.0 322.2 jit_solution(11560471258321017621)
XLA Ops:
  7.2 0.0 copy-start.2
  7.2 0.0 all-gather.3.cloned.1.call-start
  7.2 0.9 fusion.113
  8.2 3.3 %fusion.95 = bf16[128,1,1024]{2,0,1:T(8,128)(2,1)S(1)} fusion(bf16[4,2304,1024]{2,1,0:T(8,128)(2,1)} %param.7, bf16[4,128,2304]{2,1,0:T(8,128)(2,1)} %param.6, f32[1024]{0:T(1024)S(1)} %bitcast.142), kind=kOutput, calls=%fused_computation.62 | convolution fusion | flops 604372992 | bytes 5574656 | tf_op jit(solution)/shard_map/dot_general | solution.py:25
  11.5 0.0 copy-done.2
  11.5 3.1 fusion.92
  14.6 3.1 fusion.101
  17.8 0.0 copy-start.4
  17.8 3.1 fusion.98
  20.9 0.0 slice-start
  20.9 1.1 pad_maximum_fusion.1
  22.0 0.0 all-gather.3.cloned.1.call-update
  22.0 0.0 reduce-scatter.3.cloned.1.call-start
  22.1 0.0 copy-done.4
  22.1 0.7 fusion.114
  22.8 54.8 %all-gather.3.cloned.1.call-done = bf16[512,4,1024]{2,0,1:T(8,128)(2,1)} async-done(((bf16[128,4,1024]{2,0,1:T(8,128)(2,1)}), bf16[512,4,1024]{2,0,1:T(8,128)(2,1)}) %all-gather.3.cloned.1.call-update) | async-done | bytes 4194320 | tf_op jit(solution)/shard_map/all_gather | solution.py:30
  77.6 0.0 copy-start.1
  77.6 0.0 slice-start.1
  77.6 0.0 slice-start.2
  77.6 8.3 %convolution_multiply_fusion = f32[512,2304]{1,0:T(8,128)} fusion(bf16[4,1,1024,2304]{3,2,1,0:T(8,128)(2,1)} %param.9, f32[]{:T(128)} %bitcast.25, bf16[512,4,1024]{2,0,1:T(8,128)(2,1)} %all-gather.3.cloned.1.call-done), kind=kOutput, calls=%fused_computation.1 | convolution fusion | flops 2417098752 | bytes 10486272 | tf_op jit(solution)/shard_map/dot_general | solution.py:20
  86.0 0.0 copy-done.1
  86.0 7.8 %convolution_multiply_fusion.1 = f32[512,2304]{1,0:T(8,128)} fusion(bf16[4,1,1024,2304]{3,2,1,0:T(8,128)(2,1)} %param.9, f32[]{:T(128)} %bitcast.22, bf16[512,4,1024]{2,0,1:T(8,128)(2,1)S(1)} %copy-done.1), kind=kOutput, calls=%fused_computation.2 | convolution fusion | flops 2417098752 | bytes 10486272 | tf_op jit(solution)/shard_map/dot_general | solution.py:20
  93.7 0.0 slice-done
  93.7 0.0 slice-done.1
  93.7 0.0 slice-done.2
  93.7 0.0 slice-done.3
  93.7 0.0 slice-done.4
  93.8 5.0 %convolution_multiply_fusion.2 = f32[512,2304]{1,0:T(8,128)} fusion(bf16[4,1,1024,2304]{3,2,1,0:T(8,128)(2,1)S(1)} %bitcast.144, f32[]{:T(128)} %bitcast.19, bf16[512,4,1024]{2,0,1:T(8,128)(2,1)S(1)} %copy-done.1), kind=kOutput, calls=%fused_computation.3 | convolution fusion | flops 2417098752 | bytes 10485764 | tf_op jit(solution)/shard_map/dot_general | solution.py:20
  98.7 10.6 %fusion.3 = f32[1,512,2304]{2,1,0:T(8,128)} fusion(f32[512,2304]{1,0:T(8,128)} %convolution_multiply_fusion, f32[512,2304]{1,0:T(8,128)} %convolution_multiply_fusion.1, f32[512,2304]{1,0:T(8,128)} %convolution_multiply_fusion.2, bf16[4,1,1024,2304]{3,2,1,0:T(8,128)(2,1)S(1)} %bitcast.144, f32[]{:T(128)} %bitcast.16, bf16[512,4,1024]{2,0,1:T(8,128)(2,1)S(1)} %copy-done.1), kind=kOutput, calls=%fused_computation.8 | convolution fusion | flops 2420637696 | bytes 24641540 | tf_op jit(solution)/shard_map/dot_general | solution.py:20
  109.3 0.0 reduce-scatter.3.cloned.1.call-update
  109.3 0.0 all-gather.5.cloned.1.call-start
  109.4 55.0 %reduce-scatter.3.cloned.1.call-done = f32[1,64,2304]{2,1,0:T(8,128)} async-done(((f32[1,512,2304]{2,1,0:T(8,128)}), f32[1,64,2304]{2,1,0:T(8,128)}) %reduce-scatter.3.cloned.1.call-update) | async-done | bytes 589840 | tf_op jit(solution)/shard_map/reduce_scatter | solution.py:47
  164.4 2.9 fusion.112
  167.3 0.0 all-gather.5.cloned.1.call-update
  167.3 0.2 reduce-scatter.5.cloned.1.call-start
  167.6 29.9 %all-gather.5.cloned.1.call-done = bf16[1,512,2304]{2,1,0:T(8,128)(2,1)} async-done(((bf16[1,64,2304]{2,1,0:T(8,128)(2,1)}), bf16[1,512,2304]{2,1,0:T(8,128)(2,1)}) %all-gather.5.cloned.1.call-update) | async-done | bytes 2359312 | tf_op jit(solution)/shard_map/all_gather | solution.py:50
  197.5 6.6 %multiply_bitcast_fusion.2 = f32[512,1,1024]{2,0,1:T(8,128)S(1)} fusion(bf16[4,1,1024,2304]{3,2,1,0:T(8,128)(2,1)} %param.9, bf16[1,512,2304]{2,1,0:T(8,128)(2,1)} %all-gather.5.cloned.1.call-done, f32[]{:T(128)} %bitcast.19), kind=kOutput, calls=%fused_computation.47 | convolution fusion | flops 2416443392 | bytes 9175552 | tf_op jit(solution)/shard_map/dot_general | solution.py:20
  204.1 0.0 copy-done.3
  204.1 5.2 %multiply_bitcast_fusion.1 = f32[512,1,1024]{2,0,1:T(8,128)S(1)} fusion(bf16[4,1,1024,2304]{3,2,1,0:T(8,128)(2,1)} %param.9, bf16[1,512,2304]{2,1,0:T(8,128)(2,1)S(1)} %copy-done.3, f32[]{:T(128)} %bitcast.22), kind=kOutput, calls=%fused_computation.46 | convolution fusion | flops 2416443392 | bytes 9175552 | tf_op jit(solution)/shard_map/dot_general | solution.py:20
  209.3 5.2 %multiply_bitcast_fusion = f32[512,1,1024]{2,0,1:T(8,128)S(1)} fusion(bf16[4,1,1024,2304]{3,2,1,0:T(8,128)(2,1)} %param.9, bf16[1,512,2304]{2,1,0:T(8,128)(2,1)S(1)} %copy-done.3, f32[]{:T(128)} %bitcast.25), kind=kOutput, calls=%fused_computation.45 | convolution fusion | flops 2416443392 | bytes 9175552 | tf_op jit(solution)/shard_map/dot_general | solution.py:20
  214.4 5.2 %multiply_bitcast_fusion.3 = f32[512,1,1024]{2,0,1:T(8,128)S(1)} fusion(bf16[4,1,1024,2304]{3,2,1,0:T(8,128)(2,1)} %param.9, bf16[1,512,2304]{2,1,0:T(8,128)(2,1)S(1)} %copy-done.3, f32[]{:T(128)} %bitcast.16), kind=kOutput, calls=%fused_computation.48 | convolution fusion | flops 2416443392 | bytes 9175552 | tf_op jit(solution)/shard_map/dot_general | solution.py:20
  219.6 3.7 %pad_maximum_fusion = f32[512,4,1024]{2,0,1:T(8,128)} fusion(f32[512,1,1024]{2,0,1:T(8,128)S(1)} %multiply_bitcast_fusion, f32[512,1,1024]{2,0,1:T(8,128)S(1)} %multiply_bitcast_fusion.1, f32[512,1,1024]{2,0,1:T(8,128)S(1)} %multiply_bitcast_fusion.2, f32[512,1,1024]{2,0,1:T(8,128)S(1)} %multiply_bitcast_fusion.3), kind=kLoop, calls=%fused_computation | loop fusion | flops 6291456 | bytes 16777216 | tf_op jit(solution)/shard_map/stack | solution.py:70
  223.3 0.0 reduce-scatter.5.cloned.1.call-update
  223.3 1.2 copy-done
  224.5 1.8 copy.10
  226.3 40.3 %psum.7 = f32[]{:T(128)} all-reduce(f32[]{:T(128)} %get-tuple-element.9), channel_id=1, replica_groups=mesh['grp'=4,'feat'=8] {'grp','feat'}, use_global_device_ids=true, to_apply=%region_2.0 | all-reduce | flops 1 | bytes 8 | tf_op jit(solution)/shard_map/psum | solution.py:53
  267.3 43.0 %reduce-scatter.5.cloned.1.call-done = f32[128,4,1024]{2,0,1:T(8,128)} async-done(((f32[512,4,1024]{2,0,1:T(8,128)}), f32[128,4,1024]{2,0,1:T(8,128)}) %reduce-scatter.5.cloned.1.call-update) | async-done | bytes 2097168 | tf_op jit(solution)/shard_map/reduce_scatter | solution.py:69
  310.2 4.3 %copy.11 = f32[128,4,1024]{2,1,0:T(4,128)} copy(f32[128,4,1024]{2,0,1:T(8,128)} %reduce-scatter.5.cloned.1.call-done) | data formatting | bytes 4194304
  (6 shorter events, 0.0 us)
Async XLA Ops:
  7.2 4.3 %copy-start.2 = (bf16[4,128,2304]{2,1,0:T(8,128)(2,1)S(1)}, bf16[4,128,2304]{2,1,0:T(8,128)(2,1)}, u32[]{:S(2)}) copy-start(bf16[4,128,2304]{2,1,0:T(8,128)(2,1)} %param.6) | copy-start | bytes 7077892
  7.2 70.4 %all-gather.3.cloned.1.call-start = ((), (), s32[]{:S(2)}) async-start(), calls=%async_computation.2 | async-start | bytes 5242880 | tf_op jit(solution)/shard_map/all_gather | solution.py:30
  17.8 4.3 %copy-start.4 = (s32[4,1]{0,1:T(1,128)S(1)}, s32[4,1]{0,1:T(1,128)}, u32[]{:S(2)}) copy-start(s32[4,1]{0,1:T(1,128)} %param.11) | copy-start | bytes 52
  20.9 72.8 %slice-start = ((s8[18874368]{0:T(1024)(128)(4,1)}), s8[2097152]{0:T(1024)(128)(4,1)S(1)}, s32[]{:S(2)}) async-start(s8[18874368]{0:T(1024)(128)(4,1)} %bitcast.143), calls=%async_computation.6 | async-start | bytes 4194304
  22.0 142.4 %reduce-scatter.3.cloned.1.call-start = ((), (), s32[]{:S(2)}) async-start(), calls=%async_computation.3 | async-start | bytes 5308416 | tf_op jit(solution)/shard_map/reduce_scatter | solution.py:47
  77.6 8.3 %copy-start.1 = (bf16[512,4,1024]{2,0,1:T(8,128)(2,1)S(1)}, bf16[512,4,1024]{2,0,1:T(8,128)(2,1)}, u32[]{:S(2)}) copy-start(bf16[512,4,1024]{2,0,1:T(8,128)(2,1)} %all-gather.3.cloned.1.call-done) | copy-start | bytes 12582916
  77.6 16.1 %slice-start.1 = ((s8[18874368]{0:T(1024)(128)(4,1)}), s8[4194304]{0:T(1024)(128)(4,1)S(1)}, s32[]{:S(2)}) async-start(s8[18874368]{0:T(1024)(128)(4,1)} %bitcast.143), calls=%async_computation.7 | async-start | bytes 8388608
  77.6 16.1 %slice-start.2 = ((s8[18874368]{0:T(1024)(128)(4,1)}), s8[4194304]{0:T(1024)(128)(4,1)S(1)}, s32[]{:S(2)}) async-start(s8[18874368]{0:T(1024)(128)(4,1)} %bitcast.143), calls=%async_computation.8 | async-start | bytes 8388608
  86.0 7.8 %slice-start.3 = ((s8[18874368]{0:T(1024)(128)(4,1)}), s8[4194304]{0:T(1024)(128)(4,1)S(1)}, s32[]{:S(2)}) async-start(s8[18874368]{0:T(1024)(128)(4,1)} %bitcast.143), calls=%async_computation.9 | async-start | bytes 8388608
  86.0 7.8 %slice-start.4 = ((s8[18874368]{0:T(1024)(128)(4,1)}), s8[4194304]{0:T(1024)(128)(4,1)S(1)}, s32[]{:S(2)}) async-start(s8[18874368]{0:T(1024)(128)(4,1)} %bitcast.143), calls=%async_computation.10 | async-start | bytes 8388608
  109.3 88.1 %all-gather.5.cloned.1.call-start = ((), (), s32[]{:S(2)}) async-start(), calls=%async_computation.4 | async-start | bytes 2654208 | tf_op jit(solution)/shard_map/all_gather | solution.py:50
  167.3 142.9 %reduce-scatter.5.cloned.1.call-start = ((), (), s32[]{:S(2)}) async-start(), calls=%async_computation.5 | async-start | bytes 10485760 | tf_op jit(solution)/shard_map/reduce_scatter | solution.py:69
  197.5 6.6 %copy-start.3 = (bf16[1,512,2304]{2,1,0:T(8,128)(2,1)S(1)}, bf16[1,512,2304]{2,1,0:T(8,128)(2,1)}, u32[]{:S(2)}) copy-start(bf16[1,512,2304]{2,1,0:T(8,128)(2,1)} %all-gather.5.cloned.1.call-done) | copy-start | bytes 7077892
  223.3 1.2 copy-start
Sparse Core Ops, SparseCore 0:
  22.2 55.3 all-gather.2
  109.5 54.9 reduce-scatter.2
  167.4 29.9 all-gather.4
  223.5 86.7 reduce-scatter.4
where the time goes:
time: 323 us; the launch traced here: 322 us
  waiting for transfers between devices  183 us (57%)
  matrix products  66.5 us (21%)
  blocking collectives  40.3 us (12%)
  between operations  15.7 us (5%)
  local copies, waits for them, and re-layouts  8.89 us (3%)
  other arithmetic  7.64 us (2%)
    reduce_scatter x1, waiting for transfers between devices, per_device(): lax.psum_scatter(partial_sums, 'feat', scatter_dimension=1, tiled=True)  55 us
    all_gather x1, waiting for transfers between devices, per_device(): piece_rows = lax.all_gather(active, 'grp', axis=0, tiled=True)  54.8 us
    dot_general x8, matrix products, masked(): return feeds_value[source, target] * product()  53.8 us
    reduce_scatter x1, waiting for transfers between devices, per_device(): lax.psum_scatter(jnp.stack(gradients, axis=1), 'grp', scatter_dimension=0...  43 us
    psum x1, blocking collectives, per_device(): recon_loss = lax.psum(squares, ('grp', 'feat')) / entries  40.3 us
    all_gather x1, waiting for transfers between devices, per_device(): lax.all_gather(difference.astype(jnp.bfloat16), 'feat', axis=1, tiled=True)  29.9 us
    dot_general x4, matrix products, per_device(): jnp.dot(resid[source], w_enc[source], preferred_element_type=jnp.float32)  12.7 us
    unnamed x22, local copies, waits for them, and re-layouts  7.28 us
  transfers between devices with their start and end apart: 4, of which 4 were waited for; matrix products, arithmetic and copies ran while one was open for 1% of the time, Pallas kernels for 0%

commit v1 on v0

v1 whole, which is shorter than its diff:
```python
from functools import partial

import jax
import jax.numpy as jnp
from jax import lax
from jax.experimental import pallas as pl
from jax.experimental.pallas import tpu as pltpu
from jax.sharding import PartitionSpec as P

BF16 = jnp.bfloat16
F32 = jnp.float32
WANTED_CHUNKS = 2
ROW_TILE = 16


def pick_tile(size, wanted):
    if size % wanted:
        return size
    return wanted


def swap(x, axis, size, offset):
    return lax.ppermute(x, axis, [(i, i ^ offset) for i in range(size)])


class Plan:
    def __init__(self, resid, w_dec):
        self.sources, self.rows, self.model = resid.shape
        self.width = w_dec.shape[2]
        self.groups = lax.axis_size("grp")
        self.feats = lax.axis_size("feat")
        self.depth = self.feats // 2
        self.tokens = self.rows * self.groups
        self.rows_feat = self.tokens // self.feats
        self.per_group = self.rows // self.rows_feat
        self.pairs = self.per_group // 2
        self.chunks = WANTED_CHUNKS
        while self.rows_feat % (self.chunks * ROW_TILE):
            self.chunks -= 1
        self.piece = self.rows_feat // self.chunks
        self.block = self.per_group * self.piece
        bits = [1 << i for i in range(self.groups.bit_length() - 1)]
        self.lanes = [bits[i:] + bits[:i] for i in range(len(bits))]
        starts = [i * self.sources // len(bits) for i in range(len(bits) + 1)]
        self.lane_sources = list(zip(starts[:-1], starts[1:]))


def encode_kernel(plan, resid_ref, w_ref, b_ref, *outs):
    product = jnp.dot(resid_ref[0], w_ref[0], preferred_element_type=F32)
    value = jnp.maximum(product + b_ref[0], 0.0).astype(BF16)
    outs[-1][0] = value
    for c in range(plan.chunks):
        for b in range(plan.per_group):
            first = (b * plan.chunks + c) * plan.piece
            outs[c][0, b * plan.piece:(b + 1) * plan.piece, :] = value[first:first + plan.piece]


def encode(plan, lane, resid, w_enc, b_enc):
    lo, hi = plan.lane_sources[lane]
    n = hi - lo
    tile = pick_tile(plan.width, 256)
    out_shape = [jax.ShapeDtypeStruct((n, plan.block, plan.width), BF16)] * plan.chunks
    out_shape.append(jax.ShapeDtypeStruct((n, plan.rows, plan.width), BF16))
    out_specs = [pl.BlockSpec((1, plan.block, tile), lambda s, j: (s, 0, j))] * plan.chunks
    out_specs.append(pl.BlockSpec((1, plan.rows, tile), lambda s, j: (s, 0, j)))
    return pl.pallas_call(
        partial(encode_kernel, plan),
        grid=(n, plan.width // tile),
        in_specs=[
            pl.BlockSpec((1, plan.rows, plan.model), lambda s, j: (s + lo, 0, 0)),
            pl.BlockSpec((1, plan.model, tile), lambda s, j: (s + lo, 0, j)),
            pl.BlockSpec((1, 1, tile), lambda s, j: (s + lo, 0, j)),
        ],
        out_specs=out_specs,
        out_shape=out_shape,
        cost_estimate=pl.CostEstimate(
            flops=2 * n * plan.rows * plan.model * plan.width,
            bytes_accessed=2 * n * plan.model * plan.width,
            transcendentals=0,
        ),
        compiler_params=pltpu.CompilerParams(vmem_limit_bytes=32 << 20),
        name="encode",
    )(resid, w_enc, b_enc[:, None, :])


def decode_kernel(plan, index_ref, *refs):
    n_in = plan.groups * len(plan.lanes)
    pieces, w_ref, send_ref, keep_ref, x_ref = refs[:n_in], refs[n_in], *refs[n_in + 1:]
    half = plan.groups * plan.pairs * plan.piece
    core = index_ref[0]

    @pl.when(pl.program_id(0) == 0)
    def _():
        for lane, (lo, hi) in enumerate(plan.lane_sources):
            for s in range(lo, hi):
                feeds = index_ref[1 + s] > 0
                for j in range(plan.groups):
                    ref = pieces[lane * plan.groups + j]
                    for b in range(plan.pairs):
                        for h in range(2):
                            owner = 1 - core if h == 0 else core
                            first = pl.multiple_of((2 * b + owner) * plan.piece, ROW_TILE)
                            rows = ref[s - lo, pl.ds(first, plan.piece), :]
                            to = h * half + (j * plan.pairs + b) * plan.piece
                            x_ref[to:to + plan.piece, s * plan.width:(s + 1) * plan.width] = (
                                jnp.where(feeds, rows, jnp.zeros_like(rows))
                            )

    w = w_ref[:, 0].reshape(plan.sources * plan.width, w_ref.shape[3])
    product = jnp.dot(x_ref[...], w, preferred_element_type=F32)
    send_ref[...] = product[:half].astype(BF16)
    keep_ref[...] = product[half:]


def decode(plan, index, pieces, w_dec):
    tile = pick_tile(plan.model, 256)
    half = plan.groups * plan.pairs * plan.piece
    whole = pl.BlockSpec(memory_space=pltpu.VMEM)
    depth = plan.sources * plan.width
    return pl.pallas_call(
        partial(decode_kernel, plan),
        grid=(plan.model // tile,),
        in_specs=[pl.BlockSpec(memory_space=pltpu.SMEM)]
        + [whole] * len(pieces)
        + [pl.BlockSpec((plan.sources, 1, plan.width, tile), lambda j: (0, 0, 0, j))],
        out_specs=[pl.BlockSpec((half, tile), lambda j: (0, j))] * 2,
        out_shape=[
            jax.ShapeDtypeStruct((half, plan.model), BF16),
            jax.ShapeDtypeStruct((half, plan.model), F32),
        ],
        scratch_shapes=[pltpu.VMEM((2 * half, depth), BF16)],
        cost_estimate=pl.CostEstimate(
            flops=4 * half * depth * plan.model,
            bytes_accessed=2 * depth * plan.model,
            transcendentals=0,
        ),
        compiler_params=pltpu.CompilerParams(vmem_limit_bytes=32 << 20),
        name="decode",
    )(index, *pieces, w_dec)


def lane_order(plan, lane):
    first, rest = plan.lanes[lane][0], plan.lanes[lane][1:]
    kept = [0]
    for bit in reversed(rest):
        kept = [j | bit for j in kept] + kept
    return first, kept


def gradient_kernel(plan, lane, index_ref, *refs):
    n_in = 2 * plan.depth
    errors, w_ref, outs, e_ref = refs[:n_in], refs[n_in], refs[n_in + 1:-1], refs[-1]
    lo, hi = plan.lane_sources[lane]
    first, kept = lane_order(plan, lane)

    @pl.when((pl.program_id(0) == 0) & (pl.program_id(1) == 0))
    def _():
        for i in range(n_in):
            at = pl.multiple_of(index_ref[1 + plan.sources + i] * plan.piece, ROW_TILE)
            e_ref[pl.ds(at, plan.piece), :] = errors[i][...]

    product = lax.dot_general(
        e_ref[...], w_ref[0, 0], (((1,), (1,)), ((), ())), preferred_element_type=F32
    )
    feeds = index_ref[1 + lo + pl.program_id(0)] > 0
    product = jnp.where(feeds, product, 0.0)
    n = len(kept)
    for p, j in enumerate(kept):
        away = (j ^ first) * plan.block
        outs[p][0] = product[away:away + plan.block].astype(BF16)
        outs[n + p][0] = product[j * plan.block:(j + 1) * plan.block]


def gradient(plan, lane, index, errors, w_dec):
    lo, hi = plan.lane_sources[lane]
    n = hi - lo
    tile = pick_tile(plan.width, 256)
    half = plan.groups // 2
    shape = (n, plan.block, plan.width)
    whole = pl.BlockSpec(memory_space=pltpu.VMEM)
    rows = plan.groups * plan.block
    outs = pl.pallas_call(
        partial(gradient_kernel, plan, lane),
        grid=(n, plan.width // tile),
        in_specs=[pl.BlockSpec(memory_space=pltpu.SMEM)]
        + [whole] * len(errors)
        + [pl.BlockSpec((1, 1, tile, plan.model), lambda s, j: (s + lo, 0, j, 0))],
        out_specs=[pl.BlockSpec((1, plan.block, tile), lambda s, j: (s, 0, j))] * (2 * half),
        out_shape=[jax.ShapeDtypeStruct(shape, BF16)] * half
        + [jax.ShapeDtypeStruct(shape, F32)] * half,
        scratch_shapes=[pltpu.VMEM((rows, plan.model), BF16)],
        cost_estimate=pl.CostEstimate(
            flops=2 * n * rows * plan.model * plan.width,
            bytes_accessed=2 * n * plan.model * plan.width,
            transcendentals=0,
        ),
        compiler_params=pltpu.CompilerParams(vmem_limit_bytes=32 << 20),
        name="gradient",
    )(index, *errors, w_dec)
    return outs[:half], outs[half:]


def per_device(resid, w_enc, b_enc, w_dec, targets, start_layer):
    plan = Plan(resid, w_dec)
    group = lax.axis_index("grp").astype(jnp.int32)
    feat = lax.axis_index("feat").astype(jnp.int32)
    core, level = feat % 2, feat // 2
    groups, feats = plan.groups, plan.feats

    def block_of(level_to):
        return ((level_to // plan.pairs) ^ group) * plan.pairs + level_to % plan.pairs

    feeds = (group >= start_layer[:, 0]).astype(jnp.int32)
    places = [block_of(level ^ d) * 2 + core for d in range(plan.depth)]
    places += [block_of(level ^ d) * 2 + 1 - core for d in range(plan.depth)]
    index = jnp.concatenate([core[None], feeds, jnp.stack(places)])

    encoded = [encode(plan, i, resid, w_enc, b_enc) for i in range(len(plan.lanes))]
    active = jnp.stack(
        [e[-1][s] for e in encoded for s in range(e[-1].shape[0])], axis=1
    )

    gathered = []
    for c in range(plan.chunks):
        pieces = []
        for lane, bits in enumerate(plan.lanes):
            held = {0: encoded[lane][c]}
            for bit in bits:
                held.update(
                    {j | bit: swap(x, "grp", groups, bit) for j, x in list(held.items())}
                )
            pieces += [held[j] for j in range(groups)]
        gathered.append(pieces)

    recon_parts, squares = [], 0.0
    lane_results = [[] for _ in plan.lanes]
    for c in range(plan.chunks):
        send, keep = decode(plan, index, gathered[c], w_dec)
        other = swap(send, "feat", feats, 1)

        def part(level_to):
            first = block_of(level_to) * plan.piece
            mine = lax.dynamic_slice_in_dim(keep, first, plan.piece, 0)
            theirs = lax.dynamic_slice_in_dim(other, first, plan.piece, 0)
            return mine + theirs.astype(F32)

        arrived = [
            swap(part(level ^ d).astype(BF16), "feat", feats, 2 * d)
            for d in range(plan.depth - 1, 0, -1)
        ]
        recon_rows = part(level)
        for rows in arrived:
            recon_rows = recon_rows + rows.astype(F32)
        first = feat * plan.rows_feat + c * plan.piece
        own_targets = lax.dynamic_slice_in_dim(targets[0], first, plan.piece, 0)
        difference = recon_rows - own_targets.astype(F32)
        recon_parts.append(recon_rows.astype(BF16))
        squares = squares + jnp.sum(difference * difference)

        error = difference.astype(BF16)
        errors = [error] + [
            swap(error, "feat", feats, 2 * d) for d in range(1, plan.depth)
        ]
        errors += [swap(e, "feat", feats, 1) for e in errors]

        for lane, bits in enumerate(plan.lanes):
            away, kept = gradient(plan, lane, index, errors, w_dec)
            for step, bit in enumerate(bits):
                got = [swap(x, "grp", groups, bit) for x in away]
                total = [x + y.astype(F32) for x, y in zip(kept, got)]
                cut = len(total) // 2
                away = [x.astype(BF16) for x in total[:cut]]
                kept = total[cut:]
            lane_results[lane].append(total[0])

    loss = jnp.full((8, 128), squares, F32)
    for bit in (1 << i for i in range(feats.bit_length() - 1)):
        loss = loss + swap(loss, "feat", feats, bit)
    for bit in (1 << i for i in range(groups.bit_length() - 1)):
        loss = loss + swap(loss, "grp", groups, bit)
    entries = targets.shape[0] * groups * plan.tokens * plan.model
    recon_loss = loss[0, 0] / entries

    recon = jnp.concatenate(recon_parts, axis=0)[None]
    per_source = []
    for lane, (lo, hi) in enumerate(plan.lane_sources):
        parts = [
            r.reshape(hi - lo, plan.per_group, 1, plan.piece, plan.width)
            for r in lane_results[lane]
        ]
        per_source.append(
            jnp.concatenate(parts, axis=2).reshape(hi - lo, plan.rows, plan.width)
        )
    feat_grad = jnp.concatenate(per_source, axis=0).transpose(1, 0, 2)
    return active, recon, recon_loss, feat_grad


def solution(mesh):
    in_specs = (
        P(None, "grp", None),
        P(None, None, "feat"),
        P(None, "feat"),
        P(None, "grp", "feat", None),
        P("grp", None, None),
        P(None, "feat"),
    )
    out_specs = (P("grp", None, "feat"), P("grp", "feat", None), P(), P("grp", None, "feat"))
    return jax.shard_map(
        per_device, mesh=mesh, in_specs=in_specs, out_specs=out_specs, check_vma=False
    )
```

time: 323 us -> 229 us (0.71)
  waiting for transfers between devices: 183 us -> 58.6 us
  matrix products: 66.5 us -> 0 us
  starting transfers between devices: 0.34 us -> 64.8 us
  Pallas kernels: 0 us -> 48.1 us
  blocking collectives: 40.3 us -> 0 us
  local copies, waits for them, and re-layouts: 8.89 us -> 42.3 us
  between operations: 15.7 us -> 4.13 us
    reduce_scatter x2 -> x0, waiting for transfers between devices: 98 us -> none  [the longest x1 55 us: per_device(): lax.psum_scatter(partial_sums, 'feat', scatter_dimension=1, tiled=True)]
    all_gather x2 -> x0, waiting for transfers between devices: 84.7 us -> none  [the longest x1 54.8 us: per_device(): piece_rows = lax.all_gather(active, 'grp', axis=0, tiled=True)]
    dot_general x12 -> x0, matrix products: 66.5 us -> none  [the longest x8 53.8 us: masked(): return feeds_value[source, target] * product()]
    ppermute x0 -> x51, starting transfers between devices: none -> 64.8 us  [swap(): return lax.ppermute(x, axis, [(i, i ^ offset) for i in range(size)])]
    ppermute x0 -> x51, waiting for transfers between devices: none -> 58.6 us  [swap(): return lax.ppermute(x, axis, [(i, i ^ offset) for i in range(size)])]
    pallas_call x0 -> x8, Pallas kernels: none -> 48.1 us  [the longest x4 21 us: gradient(): pl.pallas_call(partial(gradient_kernel, plan, lane), grid=(n, plan.width...]
    psum x1 -> x0, blocking collectives: 40.3 us -> none  [per_device(): recon_loss = lax.psum(squares, ('grp', 'feat')) / entries]
    unnamed x22 -> x39, local copies, waits for them, and re-layouts: 7.28 us -> 38.3 us
  transfers between devices with their start and end apart: 4 -> 51, of which waited for: 4 -> 15; matrix products, arithmetic and copies ran while one was open for 1% -> 4% of each run, Pallas kernels for 0% -> 19%
where the time goes in v1:
time: 229 us; the launch traced here: 228 us
  starting transfers between devices  64.8 us (28%)
  waiting for transfers between devices  58.6 us (26%)
  Pallas kernels  48.1 us (21%)
  local copies, waits for them, and re-layouts  42.3 us (18%)
  other arithmetic  10.2 us (4%)
  between operations  4.13 us (2%)
    ppermute x51, starting transfers between devices, swap(): return lax.ppermute(x, axis, [(i, i ^ offset) for i in range(size)])  64.8 us
    ppermute x51, waiting for transfers between devices, swap(): return lax.ppermute(x, axis, [(i, i ^ offset) for i in range(size)])  58.6 us
    unnamed x39, local copies, waits for them, and re-layouts  38.3 us
    pallas_call x4, Pallas kernels, gradient(): pl.pallas_call(partial(gradient_kernel, plan, lane), grid=(n, plan.width...  21 us
    pallas_call x2, Pallas kernels, decode(): pl.pallas_call(partial(decode_kernel, plan), grid=(plan.model // tile,),...  18.8 us
    pallas_call x2, Pallas kernels, encode(): pl.pallas_call(partial(encode_kernel, plan), grid=(n, plan.width // tile)...  8.32 us
  transfers between devices with their start and end apart: 51, of which 15 were waited for; matrix products, arithmetic and copies ran while one was open for 4% of the time, Pallas kernels for 19%

profile of v1, /device:TPU:0, one launch (start us, length us, event | category | flops | bytes accessed | tf_op | source)
XLA Modules:
  0.0 228.1 jit_solution(11355189552374461962)
XLA Ops:
  1.4 6.4 %copy-done.3 = bf16[4,2304,1024]{2,1,0:T(8,128)(2,1)S(1)} copy-done((bf16[4,2304,1024]{2,1,0:T(8,128)(2,1)S(1)}, bf16[4,2304,1024]{2,1,0:T(8,128)(2,1)}, u32[]{:S(2)}) %copy-start.3) | copy-done | bytes 18874392
  7.7 1.7 copy-done.4
  9.4 4.2 %encode.3 = (bf16[2,64,1024]{2,1,0:T(8,128)(2,1)S(1)}, bf16[2,64,1024]{2,1,0:T(8,128)(2,1)S(1)}, bf16[2,128,1024]{2,1,0:T(8,128)(2,1)S(1)}) custom-call(bf16[4,128,2304]{2,1,0:T(8,128)(2,1)S(1)} %copy-done.4, bf16[4,2304,1024]{2,1,0:T(8,128)(2,1)S(1)} %copy-done.3, f32[4,1,1024]{2,1,0:T(1,128)S(1)} %broadcast_in_dim.13.b_ref), custom_call_target="tpu_custom_call" | custom-call | flops 1207959552 | bytes 9437184 | tf_op jit(solution)/shard_map/encode/pallas_call | solution.py:66
  14.4 3.0 %collective-permute-start.4 = (bf16[2,64,1024]{2,1,0:T(8,128)(2,1)S(1)}, bf16[2,64,1024]{2,1,0:T(8,128)(2,1)S(1)}, u32[]{:S(2)}, u32[]{:S(2)}) collective-permute-start(bf16[2,64,1024]{2,1,0:T(8,128)(2,1)S(1)} %get-tuple-element.33.refs_4_), channel_id=1, source_target_pairs={{0,16},{8,24},{16,0},{24,8},{1,17},{9,25},{17,1},{25,9},{2,18},{10... | collective-permute-start | bytes 786440 | tf_op jit(solution)/shard_map/ppermute | solution.py:23
  17.4 4.1 %encode.2 = (bf16[2,64,1024]{2,1,0:T(8,128)(2,1)S(1)}, bf16[2,64,1024]{2,1,0:T(8,128)(2,1)S(1)}, bf16[2,128,1024]{2,1,0:T(8,128)(2,1)S(1)}) custom-call(bf16[4,128,2304]{2,1,0:T(8,128)(2,1)S(1)} %copy-done.4, bf16[4,2304,1024]{2,1,0:T(8,128)(2,1)S(1)} %copy-done.3, f32[4,1,1024]{2,1,0:T(1,128)S(1)} %broadcast_in_dim.13.b_ref), custom_call_target="tpu_custom_call" | custom-call | flops 1207959552 | bytes 9437184 | tf_op jit(solution)/shard_map/encode/pallas_call | solution.py:66
  21.5 2.0 collective-permute-start.10
  23.6 1.9 collective-permute-start
  27.8 2.3 collective-permute-done.14.refs_6_
  30.1 2.0 collective-permute-start.15
  34.5 2.0 collective-permute-done.13.refs_5_
  37.2 2.0 collective-permute-start.3
  39.2 2.9 %collective-permute-done.refs_1_ = bf16[2,64,1024]{2,1,0:T(8,128)(2,1)S(1)} collective-permute-done((bf16[2,64,1024]{2,1,0:T(8,128)(2,1)S(1)}, bf16[2,64,1024]{2,1,0:T(8,128)(2,1)S(1)}, u32[]{:S(2)}, u32[]{:S(2)}) %collective-permute-start) | collective-permute-done | bytes 262176 | tf_op jit(solution)/shard_map/ppermute | solution.py:23
  42.1 2.0 collective-permute-start.1
  47.8 2.0 collective-permute-start.2
  49.8 6.4 %copy-done = bf16[4,1,1024,2304]{3,2,1,0:T(8,128)(2,1)S(1)} copy-done((bf16[4,1,1024,2304]{3,2,1,0:T(8,128)(2,1)S(1)}, bf16[4,1,1024,2304]{3,2,1,0:T(8,128)(2,1)}, u32[]{:S(2)}) %copy-start) | copy-done | bytes 18874392
  60.0 9.6 %decode.3 = (bf16[128,2304]{1,0:T(8,128)(2,1)}, f32[128,2304]{1,0:T(8,128)S(1)}) custom-call(s32[13]{0:T(128)S(1)} %concatenate.15.index_ref, bf16[2,64,1024]{2,1,0:T(8,128)(2,1)S(1)} %copy-done.11, bf16[2,64,1024]{2,1,0:T(8,128)(2,1)S(1)} %copy-done.13, bf16[2,64,1024]{2,1,0:T(8,128)(2,1)S(1)} %copy-done.17, ...), custom_call_target="tpu_custom_call" | custom-call | flops 4831838208 | bytes 18874368 | tf_op jit(solution)/shard_map/decode/pallas_call | solution.py:120
  69.7 6.4 %copy-done.1 = bf16[4,1,1024,2304]{3,2,1,0:T(8,128)(2,1)S(1)} copy-done((bf16[4,1,1024,2304]{3,2,1,0:T(8,128)(2,1)S(1)}, bf16[4,1,1024,2304]{3,2,1,0:T(8,128)(2,1)}, u32[]{:S(2)}) %copy-start.1) | copy-done | bytes 18874392
  78.0 9.1 %decode.2 = (bf16[128,2304]{1,0:T(8,128)(2,1)}, f32[128,2304]{1,0:T(8,128)S(1)}) custom-call(s32[13]{0:T(128)S(1)} %concatenate.15.index_ref, bf16[2,64,1024]{2,1,0:T(8,128)(2,1)S(1)} %copy-done.7, bf16[2,64,1024]{2,1,0:T(8,128)(2,1)S(1)} %copy-done.9, bf16[2,64,1024]{2,1,0:T(8,128)(2,1)S(1)} %collective-permute-done.1.refs_2_, ...), custom_call_target="tpu_custom_call" | custom-call | flops 4831838208 | bytes 18874368 | tf_op jit(solution)/shard_map/decode/pallas_call | solution.py:120
  88.7 3.7 %collective-permute-start.17 = (bf16[32,2304]{1,0:T(8,128)(2,1)S(1)}, bf16[32,2304]{1,0:T(8,128)(2,1)}, u32[]{:S(2)}, u32[]{:S(2)}) collective-permute-start(bf16[32,2304]{1,0:T(8,128)(2,1)S(1)} %get-tuple-element.71), channel_id=1, source_target_pairs={{0,6},{1,7},{2,4},{3,5},{4,2},{5,3},{6,0},{7,1},{8,14},{9,15},{10,... | collective-permute-start | bytes 442376 | tf_op jit(solution)/shard_map/ppermute | solution.py:23
  93.2 1.8 add_convert_fusion.9
  95.0 3.6 %collective-permute-start.7 = (bf16[32,2304]{1,0:T(8,128)(2,1)}, bf16[32,2304]{1,0:T(8,128)(2,1)}, u32[]{:S(2)}, u32[]{:S(2)}) collective-permute-start(bf16[32,2304]{1,0:T(8,128)(2,1)} %get-tuple-element.68), channel_id=1, source_target_pairs={{0,6},{1,7},{2,4},{3,5},{4,2},{5,3},{6,0},{7,1},{8,14},{9,15},{10,... | collective-permute-start | bytes 442376 | tf_op jit(solution)/shard_map/ppermute | solution.py:23
  98.6 2.7 %collective-permute-start.8 = (bf16[32,2304]{1,0:T(8,128)(2,1)S(1)}, bf16[32,2304]{1,0:T(8,128)(2,1)}, u32[]{:S(2)}, u32[]{:S(2)}) collective-permute-start(bf16[32,2304]{1,0:T(8,128)(2,1)S(1)} %get-tuple-element.70), channel_id=1, source_target_pairs={{0,4},{1,5},{2,6},{3,7},{4,0},{5,1},{6,2},{7,3},{8,12},{9,13},{10,... | collective-permute-start | bytes 442376 | tf_op jit(solution)/shard_map/ppermute | solution.py:23
  101.3 8.8 %collective-permute-done.18 = bf16[32,2304]{1,0:T(8,128)(2,1)} collective-permute-done((bf16[32,2304]{1,0:T(8,128)(2,1)S(1)}, bf16[32,2304]{1,0:T(8,128)(2,1)}, u32[]{:S(2)}, u32[]{:S(2)}) %collective-permute-start.18) | collective-permute-done | bytes 147488 | tf_op jit(solution)/shard_map/ppermute | solution.py:23
  110.1 7.7 %collective-permute-done.8 = bf16[32,2304]{1,0:T(8,128)(2,1)} collective-permute-done((bf16[32,2304]{1,0:T(8,128)(2,1)S(1)}, bf16[32,2304]{1,0:T(8,128)(2,1)}, u32[]{:S(2)}, u32[]{:S(2)}) %collective-permute-start.8) | collective-permute-done | bytes 147488 | tf_op jit(solution)/shard_map/ppermute | solution.py:23
  117.8 1.6 fusion
  119.5 1.7 multiply_reduce_fusion
  123.7 3.6 %collective-permute-done.21 = f32[8,128]{1,0:T(8,128)S(1)} collective-permute-done((f32[8,128]{1,0:T(8,128)S(1)}, f32[8,128]{1,0:T(8,128)S(1)}, u32[]{:S(2)}, u32[]{:S(2)}) %collective-permute-start.21) | collective-permute-done | bytes 4128 | tf_op jit(solution)/shard_map/ppermute | solution.py:23
  128.3 3.5 %collective-permute-done.22 = f32[8,128]{1,0:T(8,128)S(1)} collective-permute-done((f32[8,128]{1,0:T(8,128)S(1)}, f32[8,128]{1,0:T(8,128)S(1)}, u32[]{:S(2)}, u32[]{:S(2)}) %collective-permute-start.22) | collective-permute-done | bytes 4128 | tf_op jit(solution)/shard_map/ppermute | solution.py:23
  133.3 2.1 collective-permute-done.23
  137.0 2.5 %collective-permute-start.27 = (bf16[32,2304]{1,0:T(8,128)(2,1)S(1)}, bf16[32,2304]{1,0:T(8,128)(2,1)S(1)}, u32[]{:S(2)}, u32[]{:S(2)}) collective-permute-start(bf16[32,2304]{1,0:T(8,128)(2,1)S(1)} %get-tuple-element.62.refs_0_), channel_id=1, source_target_pairs={{0,6},{1,7},{2,4},{3,5},{4,2},{5,3},{6,0},{7,1},{8,14},{9,15},{10,... | collective-permute-start | bytes 442376 | tf_op jit(solution)/shard_map/ppermute | solution.py:23
  141.0 1.9 collective-permute-start.36
  144.1 1.8 copy.12
  145.9 7.5 %collective-permute-start.25 = (bf16[32,2304]{1,0:T(8,128)(2,1)S(1)}, bf16[32,2304]{1,0:T(8,128)(2,1)S(1)}, u32[]{:S(2)}, u32[]{:S(2)}) collective-permute-start(bf16[32,2304]{1,0:T(8,128)(2,1)S(1)} %get-tuple-element.62.refs_0_), channel_id=1, source_target_pairs={{0,2},{1,3},{2,0},{3,1},{4,6},{5,7},{6,4},{7,5},{8,10},{9,11},{10,... | collective-permute-start | bytes 442376 | tf_op jit(solution)/shard_map/ppermute | solution.py:23
  153.4 3.7 %collective-permute-done.26.refs_2_ = bf16[32,2304]{1,0:T(8,128)(2,1)S(1)} collective-permute-done((bf16[32,2304]{1,0:T(8,128)(2,1)S(1)}, bf16[32,2304]{1,0:T(8,128)(2,1)S(1)}, u32[]{:S(2)}, u32[]{:S(2)}) %collective-permute-start.26) | collective-permute-done | bytes 147488 | tf_op jit(solution)/shard_map/ppermute | solution.py:23
  157.6 4.0 %collective-permute-done.36.refs_2_ = bf16[32,2304]{1,0:T(8,128)(2,1)S(1)} collective-permute-done((bf16[32,2304]{1,0:T(8,128)(2,1)S(1)}, bf16[32,2304]{1,0:T(8,128)(2,1)S(1)}, u32[]{:S(2)}, u32[]{:S(2)}) %collective-permute-start.36) | collective-permute-done | bytes 147488 | tf_op jit(solution)/shard_map/ppermute | solution.py:23
  165.2 6.4 %copy-done.2 = bf16[4,1,1024,2304]{3,2,1,0:T(8,128)(2,1)S(1)} copy-done((bf16[4,1,1024,2304]{3,2,1,0:T(8,128)(2,1)S(1)}, bf16[4,1,1024,2304]{3,2,1,0:T(8,128)(2,1)}, u32[]{:S(2)}) %copy-start.2) | copy-done | bytes 18874392
  171.5 5.2 %gradient.7 = (bf16[2,64,1024]{2,1,0:T(8,128)(2,1)S(1)}, bf16[2,64,1024]{2,1,0:T(8,128)(2,1)S(1)}, f32[2,64,1024]{2,1,0:T(8,128)S(1)}, f32[2,64,1024]{2,1,0:T(8,128)S(1)}) custom-call(s32[13]{0:T(128)S(1)} %concatenate.15.index_ref, bf16[32,2304]{1,0:T(8,128)(2,1)S(1)} %get-tuple-element.66.refs_0_, bf16[32,2304]{1,0:T(8,128)(2,1)S(1)} %collective-permute-done.35.refs_1_, ...), custom_call_target="tpu_custom_call" | custom-call | flops 2415919104 | bytes 9437184 | tf_op jit(solution)/shard_map/gradient/pallas_call | solution.py:182
  176.7 1.6 collective-permute-start.48
  178.3 5.2 %gradient.5 = (bf16[2,64,1024]{2,1,0:T(8,128)(2,1)S(1)}, bf16[2,64,1024]{2,1,0:T(8,128)(2,1)S(1)}, f32[2,64,1024]{2,1,0:T(8,128)S(1)}, f32[2,64,1024]{2,1,0:T(8,128)S(1)}) custom-call(s32[13]{0:T(128)S(1)} %concatenate.15.index_ref, bf16[32,2304]{1,0:T(8,128)(2,1)S(1)} %get-tuple-element.66.refs_0_, bf16[32,2304]{1,0:T(8,128)(2,1)S(1)} %collective-permute-done.35.refs_1_, ...), custom_call_target="tpu_custom_call" | custom-call | flops 2415919104 | bytes 9437184 | tf_op jit(solution)/shard_map/gradient/pallas_call | solution.py:182
  186.2 5.2 %gradient.6 = (bf16[2,64,1024]{2,1,0:T(8,128)(2,1)S(1)}, bf16[2,64,1024]{2,1,0:T(8,128)(2,1)S(1)}, f32[2,64,1024]{2,1,0:T(8,128)S(1)}, f32[2,64,1024]{2,1,0:T(8,128)S(1)}) custom-call(s32[13]{0:T(128)S(1)} %concatenate.15.index_ref, bf16[32,2304]{1,0:T(8,128)(2,1)S(1)} %get-tuple-element.62.refs_0_, bf16[32,2304]{1,0:T(8,128)(2,1)S(1)} %collective-permute-done.25.refs_1_, ...), custom_call_target="tpu_custom_call" | custom-call | flops 2415919104 | bytes 9437184 | tf_op jit(solution)/shard_map/gradient/pallas_call | solution.py:182
  191.4 1.6 collective-permute-start.45
  192.9 5.4 %gradient.4 = (bf16[2,64,1024]{2,1,0:T(8,128)(2,1)S(1)}, bf16[2,64,1024]{2,1,0:T(8,128)(2,1)S(1)}, f32[2,64,1024]{2,1,0:T(8,128)S(1)}, f32[2,64,1024]{2,1,0:T(8,128)S(1)}) custom-call(s32[13]{0:T(128)S(1)} %concatenate.15.index_ref, bf16[32,2304]{1,0:T(8,128)(2,1)S(1)} %get-tuple-element.62.refs_0_, bf16[32,2304]{1,0:T(8,128)(2,1)S(1)} %collective-permute-done.25.refs_1_, ...), custom_call_target="tpu_custom_call" | custom-call | flops 2415919104 | bytes 9437184 | tf_op jit(solution)/shard_map/gradient/pallas_call | solution.py:182
  199.0 1.6 collective-permute-start.33
  200.6 4.7 %collective-permute-done.46 = bf16[2,64,1024]{2,1,0:T(8,128)(2,1)S(1)} collective-permute-done((bf16[2,64,1024]{2,1,0:T(8,128)(2,1)S(1)}, bf16[2,64,1024]{2,1,0:T(8,128)(2,1)S(1)}, u32[]{:S(2)}, u32[]{:S(2)}) %collective-permute-start.46) | collective-permute-done | bytes 262176 | tf_op jit(solution)/shard_map/ppermute | solution.py:23
  207.6 2.2 collective-permute-start.44
  209.8 4.8 %collective-permute-done.50 = bf16[2,64,1024]{2,1,0:T(8,128)(2,1)S(1)} collective-permute-done((bf16[2,64,1024]{2,1,0:T(8,128)(2,1)S(1)}, bf16[2,64,1024]{2,1,0:T(8,128)(2,1)S(1)}, u32[]{:S(2)}, u32[]{:S(2)}) %collective-permute-start.50) | collective-permute-done | bytes 262176 | tf_op jit(solution)/shard_map/ppermute | solution.py:23
  216.7 5.8 %collective-permute-done.47 = bf16[2,64,1024]{2,1,0:T(8,128)(2,1)S(1)} collective-permute-done((bf16[2,64,1024]{2,1,0:T(8,128)(2,1)S(1)}, bf16[2,64,1024]{2,1,0:T(8,128)(2,1)S(1)}, u32[]{:S(2)}, u32[]{:S(2)}) %collective-permute-start.47) | collective-permute-done | bytes 262176 | tf_op jit(solution)/shard_map/ppermute | solution.py:23
  224.7 2.3 maximum_bitcast_fusion
  (132 shorter events, 39.8 us)
Async XLA Ops:
  14.4 11.2 %collective-permute-start.4 = (bf16[2,64,1024]{2,1,0:T(8,128)(2,1)S(1)}, bf16[2,64,1024]{2,1,0:T(8,128)(2,1)S(1)}, u32[]{:S(2)}, u32[]{:S(2)}) collective-permute-start(bf16[2,64,1024]{2,1,0:T(8,128)(2,1)S(1)} %get-tuple-element.33.refs_4_), channel_id=1, source_target_pairs={{0,16},{8,24},{16,0},{24,8},{1,17},{9,25},{17,1},{25,9},{2,18},{10... | collective-permute-start | bytes 786440 | tf_op jit(solution)/shard_map/ppermute | solution.py:23
  17.3 12.7 %collective-permute-start.14 = (bf16[2,64,1024]{2,1,0:T(8,128)(2,1)S(1)}, bf16[2,64,1024]{2,1,0:T(8,128)(2,1)S(1)}, u32[]{:S(2)}, u32[]{:S(2)}) collective-permute-start(bf16[2,64,1024]{2,1,0:T(8,128)(2,1)S(1)} %get-tuple-element.37.refs_4_), channel_id=1, source_target_pairs={{0,16},{8,24},{16,0},{24,8},{1,17},{9,25},{17,1},{25,9},{2,18},{10... | collective-permute-start | bytes 786440 | tf_op jit(solution)/shard_map/ppermute | solution.py:23
  21.5 10.6 %collective-permute-start.10 = (bf16[2,64,1024]{2,1,0:T(8,128)(2,1)S(1)}, bf16[2,64,1024]{2,1,0:T(8,128)(2,1)S(1)}, u32[]{:S(2)}, u32[]{:S(2)}) collective-permute-start(bf16[2,64,1024]{2,1,0:T(8,128)(2,1)S(1)} %get-tuple-element.36.refs_0_), channel_id=1, source_target_pairs={{0,8},{8,0},{16,24},{24,16},{1,9},{9,1},{17,25},{25,17},{2,10},{10... | collective-permute-start | bytes 786440 | tf_op jit(solution)/shard_map/ppermute | solution.py:23
  23.6 12.9 %collective-permute-start.13 = (bf16[2,64,1024]{2,1,0:T(8,128)(2,1)S(1)}, bf16[2,64,1024]{2,1,0:T(8,128)(2,1)S(1)}, u32[]{:S(2)}, u32[]{:S(2)}) collective-permute-start(bf16[2,64,1024]{2,1,0:T(8,128)(2,1)S(1)} %get-tuple-element.37.refs_4_), channel_id=1, source_target_pairs={{0,8},{8,0},{16,24},{24,16},{1,9},{9,1},{17,25},{25,17},{2,10},{10... | collective-permute-start | bytes 786440 | tf_op jit(solution)/shard_map/ppermute | solution.py:23
  23.6 18.4 %collective-permute-start = (bf16[2,64,1024]{2,1,0:T(8,128)(2,1)S(1)}, bf16[2,64,1024]{2,1,0:T(8,128)(2,1)S(1)}, u32[]{:S(2)}, u32[]{:S(2)}) collective-permute-start(bf16[2,64,1024]{2,1,0:T(8,128)(2,1)S(1)} %get-tuple-element.32.refs_0_), channel_id=1, source_target_pairs={{0,8},{8,0},{16,24},{24,16},{1,9},{9,1},{17,25},{25,17},{2,10},{10... | collective-permute-start | bytes 786440 | tf_op jit(solution)/shard_map/ppermute | solution.py:23
  25.6 18.5 %collective-permute-start.11 = (bf16[2,64,1024]{2,1,0:T(8,128)(2,1)S(1)}, bf16[2,64,1024]{2,1,0:T(8,128)(2,1)S(1)}, u32[]{:S(2)}, u32[]{:S(2)}) collective-permute-start(bf16[2,64,1024]{2,1,0:T(8,128)(2,1)S(1)} %get-tuple-element.36.refs_0_), channel_id=1, source_target_pairs={{0,16},{8,24},{16,0},{24,8},{1,17},{9,25},{17,1},{25,9},{2,18},{10... | collective-permute-start | bytes 786440 | tf_op jit(solution)/shard_map/ppermute | solution.py:23
  30.1 17.7 %collective-permute-start.15 = (bf16[2,64,1024]{2,1,0:T(8,128)(2,1)S(1)}, bf16[2,64,1024]{2,1,0:T(8,128)(2,1)}, u32[]{:S(2)}, u32[]{:S(2)}) collective-permute-start(bf16[2,64,1024]{2,1,0:T(8,128)(2,1)S(1)} %collective-permute-done.14.refs_6_), channel_id=1, source_target_pairs={{0,8},{8,0},{16,24},{24,16},{1,9},{9,1},{17,25},{25,17},{2,10},{10... | collective-permute-start | bytes 786440 | tf_op jit(solution)/shard_map/ppermute | solution.py:23
  32.1 17.7 %collective-permute-start.12 = (bf16[2,64,1024]{2,1,0:T(8,128)(2,1)S(1)}, bf16[2,64,1024]{2,1,0:T(8,128)(2,1)}, u32[]{:S(2)}, u32[]{:S(2)}) collective-permute-start(bf16[2,64,1024]{2,1,0:T(8,128)(2,1)S(1)} %collective-permute-done.10.refs_1_), channel_id=1, source_target_pairs={{0,16},{8,24},{16,0},{24,8},{1,17},{9,25},{17,1},{25,9},{2,18},{10... | collective-permute-start | bytes 786440 | tf_op jit(solution)/shard_map/ppermute | solution.py:23
  37.2 32.5 %collective-permute-start.3 = (bf16[2,64,1024]{2,1,0:T(8,128)(2,1)S(1)}, bf16[2,64,1024]{2,1,0:T(8,128)(2,1)S(1)}, u32[]{:S(2)}, u32[]{:S(2)}) collective-permute-start(bf16[2,64,1024]{2,1,0:T(8,128)(2,1)S(1)} %get-tuple-element.33.refs_4_), channel_id=1, source_target_pairs={{0,8},{8,0},{16,24},{24,16},{1,9},{9,1},{17,25},{25,17},{2,10},{10... | collective-permute-start | bytes 786440 | tf_op jit(solution)/shard_map/ppermute | solution.py:23
  42.1 27.6 %collective-permute-start.1 = (bf16[2,64,1024]{2,1,0:T(8,128)(2,1)S(1)}, bf16[2,64,1024]{2,1,0:T(8,128)(2,1)S(1)}, u32[]{:S(2)}, u32[]{:S(2)}) collective-permute-start(bf16[2,64,1024]{2,1,0:T(8,128)(2,1)S(1)} %get-tuple-element.32.refs_0_), channel_id=1, source_target_pairs={{0,16},{8,24},{16,0},{24,8},{1,17},{9,25},{17,1},{25,9},{2,18},{10... | collective-permute-start | bytes 786440 | tf_op jit(solution)/shard_map/ppermute | solution.py:23
  44.8 24.9 %collective-permute-start.5 = (bf16[2,64,1024]{2,1,0:T(8,128)(2,1)S(1)}, bf16[2,64,1024]{2,1,0:T(8,128)(2,1)S(1)}, u32[]{:S(2)}, u32[]{:S(2)}) collective-permute-start(bf16[2,64,1024]{2,1,0:T(8,128)(2,1)S(1)} %collective-permute-done.4.refs_6_), channel_id=1, source_target_pairs={{0,8},{8,0},{16,24},{24,16},{1,9},{9,1},{17,25},{25,17},{2,10},{10... | collective-permute-start | bytes 786440 | tf_op jit(solution)/shard_map/ppermute | solution.py:23
  47.8 21.9 %collective-permute-start.2 = (bf16[2,64,1024]{2,1,0:T(8,128)(2,1)S(1)}, bf16[2,64,1024]{2,1,0:T(8,128)(2,1)S(1)}, u32[]{:S(2)}, u32[]{:S(2)}) collective-permute-start(bf16[2,64,1024]{2,1,0:T(8,128)(2,1)S(1)} %collective-permute-done.refs_1_), channel_id=1, source_target_pairs={{0,16},{8,24},{16,0},{24,8},{1,17},{9,25},{17,1},{25,9},{2,18},{10... | collective-permute-start | bytes 786440 | tf_op jit(solution)/shard_map/ppermute | solution.py:23
  69.6 17.9 %collective-permute-start.16 = (bf16[128,2304]{1,0:T(8,128)(2,1)}, bf16[128,2304]{1,0:T(8,128)(2,1)}, u32[]{:S(2)}, u32[]{:S(2)}) collective-permute-start(bf16[128,2304]{1,0:T(8,128)(2,1)} %get-tuple-element.39), channel_id=1, source_target_pairs={{0,1},{1,0},{2,3},{3,2},{4,5},{5,4},{6,7},{7,6},{8,9},{9,8},{10,11... | collective-permute-start | bytes 1769480 | tf_op jit(solution)/shard_map/ppermute | solution.py:23
  87.1 6.1 %collective-permute-start.6 = (bf16[128,2304]{1,0:T(8,128)(2,1)}, bf16[128,2304]{1,0:T(8,128)(2,1)}, u32[]{:S(2)}, u32[]{:S(2)}) collective-permute-start(bf16[128,2304]{1,0:T(8,128)(2,1)} %get-tuple-element.35), channel_id=1, source_target_pairs={{0,1},{1,0},{2,3},{3,2},{4,5},{5,4},{6,7},{7,6},{8,9},{9,8},{10,11... | collective-permute-start | bytes 1769480 | tf_op jit(solution)/shard_map/ppermute | solution.py:23
  88.7 9.9 %collective-permute-start.17 = (bf16[32,2304]{1,0:T(8,128)(2,1)S(1)}, bf16[32,2304]{1,0:T(8,128)(2,1)}, u32[]{:S(2)}, u32[]{:S(2)}) collective-permute-start(bf16[32,2304]{1,0:T(8,128)(2,1)S(1)} %get-tuple-element.71), channel_id=1, source_target_pairs={{0,6},{1,7},{2,4},{3,5},{4,2},{5,3},{6,0},{7,1},{8,14},{9,15},{10,... | collective-permute-start | bytes 442376 | tf_op jit(solution)/shard_map/ppermute | solution.py:23
  92.4 9.0 %collective-permute-start.19 = (bf16[32,2304]{1,0:T(8,128)(2,1)S(1)}, bf16[32,2304]{1,0:T(8,128)(2,1)}, u32[]{:S(2)}, u32[]{:S(2)}) collective-permute-start(bf16[32,2304]{1,0:T(8,128)(2,1)S(1)} %get-tuple-element.72), channel_id=1, source_target_pairs={{0,2},{1,3},{2,0},{3,1},{4,6},{5,7},{6,4},{7,5},{8,10},{9,11},{10,... | collective-permute-start | bytes 442376 | tf_op jit(solution)/shard_map/ppermute | solution.py:23
  92.4 17.8 %collective-permute-start.18 = (bf16[32,2304]{1,0:T(8,128)(2,1)S(1)}, bf16[32,2304]{1,0:T(8,128)(2,1)}, u32[]{:S(2)}, u32[]{:S(2)}) collective-permute-start(bf16[32,2304]{1,0:T(8,128)(2,1)S(1)} %get-tuple-element.73), channel_id=1, source_target_pairs={{0,4},{1,5},{2,6},{3,7},{4,0},{5,1},{6,2},{7,3},{8,12},{9,13},{10,... | collective-permute-start | bytes 442376 | tf_op jit(solution)/shard_map/ppermute | solution.py:23
  95.0 15.1 %collective-permute-start.7 = (bf16[32,2304]{1,0:T(8,128)(2,1)}, bf16[32,2304]{1,0:T(8,128)(2,1)}, u32[]{:S(2)}, u32[]{:S(2)}) collective-permute-start(bf16[32,2304]{1,0:T(8,128)(2,1)} %get-tuple-element.68), channel_id=1, source_target_pairs={{0,6},{1,7},{2,4},{3,5},{4,2},{5,3},{6,0},{7,1},{8,14},{9,15},{10,... | collective-permute-start | bytes 442376 | tf_op jit(solution)/shard_map/ppermute | solution.py:23
  98.6 11.5 %collective-permute-start.9 = (bf16[32,2304]{1,0:T(8,128)(2,1)}, bf16[32,2304]{1,0:T(8,128)(2,1)}, u32[]{:S(2)}, u32[]{:S(2)}) collective-permute-start(bf16[32,2304]{1,0:T(8,128)(2,1)} %get-tuple-element.69), channel_id=1, source_target_pairs={{0,2},{1,3},{2,0},{3,1},{4,6},{5,7},{6,4},{7,5},{8,10},{9,11},{10,... | collective-permute-start | bytes 442376 | tf_op jit(solution)/shard_map/ppermute | solution.py:23
  98.6 19.2 %collective-permute-start.8 = (bf16[32,2304]{1,0:T(8,128)(2,1)S(1)}, bf16[32,2304]{1,0:T(8,128)(2,1)}, u32[]{:S(2)}, u32[]{:S(2)}) collective-permute-start(bf16[32,2304]{1,0:T(8,128)(2,1)S(1)} %get-tuple-element.70), channel_id=1, source_target_pairs={{0,4},{1,5},{2,6},{3,7},{4,0},{5,1},{6,2},{7,3},{8,12},{9,13},{10,... | collective-permute-start | bytes 442376 | tf_op jit(solution)/shard_map/ppermute | solution.py:23
  123.7 3.6 %collective-permute-start.21 = (f32[8,128]{1,0:T(8,128)S(1)}, f32[8,128]{1,0:T(8,128)S(1)}, u32[]{:S(2)}, u32[]{:S(2)}) collective-permute-start(f32[8,128]{1,0:T(8,128)S(1)} %broadcast_add_fusion), channel_id=1, source_target_pairs={{0,2},{1,3},{2,0},{3,1},{4,6},{5,7},{6,4},{7,5},{8,10},{9,11},{10,... | collective-permute-start | bytes 12296 | tf_op jit(solution)/shard_map/ppermute | solution.py:23
  127.3 4.5 %collective-permute-start.22 = (f32[8,128]{1,0:T(8,128)S(1)}, f32[8,128]{1,0:T(8,128)S(1)}, u32[]{:S(2)}, u32[]{:S(2)}) collective-permute-start(f32[8,128]{1,0:T(8,128)S(1)} %fusion.3), channel_id=1, source_target_pairs={{0,4},{1,5},{2,6},{3,7},{4,0},{5,1},{6,2},{7,3},{8,12},{9,13},{10,... | collective-permute-start | bytes 12296 | tf_op jit(solution)/shard_map/ppermute | solution.py:23
  131.8 3.6 %collective-permute-start.23 = (f32[8,128]{1,0:T(8,128)S(1)}, f32[8,128]{1,0:T(8,128)S(1)}, u32[]{:S(2)}, u32[]{:S(2)}) collective-permute-start(f32[8,128]{1,0:T(8,128)S(1)} %add.229), channel_id=1, source_target_pairs={{0,8},{8,0},{16,24},{24,16},{1,9},{9,1},{17,25},{25,17},{2,10},{10... | collective-permute-start | bytes 12296 | tf_op jit(solution)/shard_map/ppermute | solution.py:23
  135.4 7.5 %collective-permute-start.24 = (f32[8,128]{1,0:T(8,128)S(1)}, f32[8,128]{1,0:T(8,128)S(1)}, u32[]{:S(2)}, u32[]{:S(2)}) collective-permute-start(f32[8,128]{1,0:T(8,128)S(1)} %add.230), channel_id=1, source_target_pairs={{0,16},{8,24},{16,0},{24,8},{1,17},{9,25},{17,1},{25,9},{2,18},{10... | collective-permute-start | bytes 12296 | tf_op jit(solution)/shard_map/ppermute | solution.py:23
  137.0 8.9 %collective-permute-start.27 = (bf16[32,2304]{1,0:T(8,128)(2,1)S(1)}, bf16[32,2304]{1,0:T(8,128)(2,1)S(1)}, u32[]{:S(2)}, u32[]{:S(2)}) collective-permute-start(bf16[32,2304]{1,0:T(8,128)(2,1)S(1)} %get-tuple-element.62.refs_0_), channel_id=1, source_target_pairs={{0,6},{1,7},{2,4},{3,5},{4,2},{5,3},{6,0},{7,1},{8,14},{9,15},{10,... | collective-permute-start | bytes 442376 | tf_op jit(solution)/shard_map/ppermute | solution.py:23
  139.6 17.5 %collective-permute-start.26 = (bf16[32,2304]{1,0:T(8,128)(2,1)S(1)}, bf16[32,2304]{1,0:T(8,128)(2,1)S(1)}, u32[]{:S(2)}, u32[]{:S(2)}) collective-permute-start(bf16[32,2304]{1,0:T(8,128)(2,1)S(1)} %get-tuple-element.62.refs_0_), channel_id=1, source_target_pairs={{0,4},{1,5},{2,6},{3,7},{4,0},{5,1},{6,2},{7,3},{8,12},{9,13},{10,... | collective-permute-start | bytes 442376 | tf_op jit(solution)/shard_map/ppermute | solution.py:23
  139.6 17.5 %collective-permute-start.37 = (bf16[32,2304]{1,0:T(8,128)(2,1)S(1)}, bf16[32,2304]{1,0:T(8,128)(2,1)S(1)}, u32[]{:S(2)}, u32[]{:S(2)}) collective-permute-start(bf16[32,2304]{1,0:T(8,128)(2,1)S(1)} %get-tuple-element.66.refs_0_), channel_id=1, source_target_pairs={{0,6},{1,7},{2,4},{3,5},{4,2},{5,3},{6,0},{7,1},{8,14},{9,15},{10,... | collective-permute-start | bytes 442376 | tf_op jit(solution)/shard_map/ppermute | solution.py:23
  141.0 20.6 %collective-permute-start.36 = (bf16[32,2304]{1,0:T(8,128)(2,1)S(1)}, bf16[32,2304]{1,0:T(8,128)(2,1)S(1)}, u32[]{:S(2)}, u32[]{:S(2)}) collective-permute-start(bf16[32,2304]{1,0:T(8,128)(2,1)S(1)} %get-tuple-element.66.refs_0_), channel_id=1, source_target_pairs={{0,4},{1,5},{2,6},{3,7},{4,0},{5,1},{6,2},{7,3},{8,12},{9,13},{10,... | collective-permute-start | bytes 442376 | tf_op jit(solution)/shard_map/ppermute | solution.py:23
  142.9 18.7 %collective-permute-start.35 = (bf16[32,2304]{1,0:T(8,128)(2,1)S(1)}, bf16[32,2304]{1,0:T(8,128)(2,1)S(1)}, u32[]{:S(2)}, u32[]{:S(2)}) collective-permute-start(bf16[32,2304]{1,0:T(8,128)(2,1)S(1)} %get-tuple-element.66.refs_0_), channel_id=1, source_target_pairs={{0,2},{1,3},{2,0},{3,1},{4,6},{5,7},{6,4},{7,5},{8,10},{9,11},{10,... | collective-permute-start | bytes 442376 | tf_op jit(solution)/shard_map/ppermute | solution.py:23
  145.9 18.1 %collective-permute-start.25 = (bf16[32,2304]{1,0:T(8,128)(2,1)S(1)}, bf16[32,2304]{1,0:T(8,128)(2,1)S(1)}, u32[]{:S(2)}, u32[]{:S(2)}) collective-permute-start(bf16[32,2304]{1,0:T(8,128)(2,1)S(1)} %get-tuple-element.62.refs_0_), channel_id=1, source_target_pairs={{0,2},{1,3},{2,0},{3,1},{4,6},{5,7},{6,4},{7,5},{8,10},{9,11},{10,... | collective-permute-start | bytes 442376 | tf_op jit(solution)/shard_map/ppermute | solution.py:23
  157.1 7.1 %collective-permute-start.38 = (bf16[32,2304]{1,0:T(8,128)(2,1)S(1)}, bf16[32,2304]{1,0:T(8,128)(2,1)S(1)}, u32[]{:S(2)}, u32[]{:S(2)}) collective-permute-start(bf16[32,2304]{1,0:T(8,128)(2,1)S(1)} %get-tuple-element.66.refs_0_), channel_id=1, source_target_pairs={{0,1},{1,0},{2,3},{3,2},{4,5},{5,4},{6,7},{7,6},{8,9},{9,8},{10,11... | collective-permute-start | bytes 442376 | tf_op jit(solution)/shard_map/ppermute | solution.py:23
  157.1 7.5 %collective-permute-start.41 = (bf16[32,2304]{1,0:T(8,128)(2,1)S(1)}, bf16[32,2304]{1,0:T(8,128)(2,1)S(1)}, u32[]{:S(2)}, u32[]{:S(2)}) collective-permute-start(bf16[32,2304]{1,0:T(8,128)(2,1)S(1)} %collective-permute-done.37.refs_3_), channel_id=1, source_target_pairs={{0,1},{1,0},{2,3},{3,2},{4,5},{5,4},{6,7},{7,6},{8,9},{9,8},{10,11... | collective-permute-start | bytes 442376 | tf_op jit(solution)/shard_map/ppermute | solution.py:23
  164.1 19.5 %collective-permute-start.28 = (bf16[32,2304]{1,0:T(8,128)(2,1)S(1)}, bf16[32,2304]{1,0:T(8,128)(2,1)S(1)}, u32[]{:S(2)}, u32[]{:S(2)}) collective-permute-start(bf16[32,2304]{1,0:T(8,128)(2,1)S(1)} %get-tuple-element.62.refs_0_), channel_id=1, source_target_pairs={{0,1},{1,0},{2,3},{3,2},{4,5},{5,4},{6,7},{7,6},{8,9},{9,8},{10,11... | collective-permute-start | bytes 442376 | tf_op jit(solution)/shard_map/ppermute | solution.py:23
  164.2 20.0 %collective-permute-start.31 = (bf16[32,2304]{1,0:T(8,128)(2,1)S(1)}, bf16[32,2304]{1,0:T(8,128)(2,1)S(1)}, u32[]{:S(2)}, u32[]{:S(2)}) collective-permute-start(bf16[32,2304]{1,0:T(8,128)(2,1)S(1)} %collective-permute-done.27.refs_3_), channel_id=1, source_target_pairs={{0,1},{1,0},{2,3},{3,2},{4,5},{5,4},{6,7},{7,6},{8,9},{9,8},{10,11... | collective-permute-start | bytes 442376 | tf_op jit(solution)/shard_map/ppermute | solution.py:23
  164.7 21.0 %collective-permute-start.30 = (bf16[32,2304]{1,0:T(8,128)(2,1)S(1)}, bf16[32,2304]{1,0:T(8,128)(2,1)S(1)}, u32[]{:S(2)}, u32[]{:S(2)}) collective-permute-start(bf16[32,2304]{1,0:T(8,128)(2,1)S(1)} %collective-permute-done.26.refs_2_), channel_id=1, source_target_pairs={{0,1},{1,0},{2,3},{3,2},{4,5},{5,4},{6,7},{7,6},{8,9},{9,8},{10,11... | collective-permute-start | bytes 442376 | tf_op jit(solution)/shard_map/ppermute | solution.py:23
  164.7 21.4 %collective-permute-start.29 = (bf16[32,2304]{1,0:T(8,128)(2,1)S(1)}, bf16[32,2304]{1,0:T(8,128)(2,1)S(1)}, u32[]{:S(2)}, u32[]{:S(2)}) collective-permute-start(bf16[32,2304]{1,0:T(8,128)(2,1)S(1)} %collective-permute-done.25.refs_1_), channel_id=1, source_target_pairs={{0,1},{1,0},{2,3},{3,2},{4,5},{5,4},{6,7},{7,6},{8,9},{9,8},{10,11... | collective-permute-start | bytes 442376 | tf_op jit(solution)/shard_map/ppermute | solution.py:23
  176.7 30.8 %collective-permute-start.48 = (bf16[2,64,1024]{2,1,0:T(8,128)(2,1)S(1)}, bf16[2,64,1024]{2,1,0:T(8,128)(2,1)S(1)}, u32[]{:S(2)}, u32[]{:S(2)}) collective-permute-start(bf16[2,64,1024]{2,1,0:T(8,128)(2,1)S(1)} %get-tuple-element.53), channel_id=1, source_target_pairs={{0,16},{8,24},{16,0},{24,8},{1,17},{9,25},{17,1},{25,9},{2,18},{10... | collective-permute-start | bytes 786440 | tf_op jit(solution)/shard_map/ppermute | solution.py:23
  183.5 14.8 %collective-permute-start.49 = (bf16[2,64,1024]{2,1,0:T(8,128)(2,1)S(1)}, bf16[2,64,1024]{2,1,0:T(8,128)(2,1)S(1)}, u32[]{:S(2)}, u32[]{:S(2)}) collective-permute-start(bf16[2,64,1024]{2,1,0:T(8,128)(2,1)S(1)} %get-tuple-element.55), channel_id=1, source_target_pairs={{0,16},{8,24},{16,0},{24,8},{1,17},{9,25},{17,1},{25,9},{2,18},{10... | collective-permute-start | bytes 786440 | tf_op jit(solution)/shard_map/ppermute | solution.py:23
  184.1 39.4 %collective-permute-start.42 = (bf16[2,64,1024]{2,1,0:T(8,128)(2,1)S(1)}, bf16[2,64,1024]{2,1,0:T(8,128)(2,1)S(1)}, u32[]{:S(2)}, u32[]{:S(2)}) collective-permute-start(bf16[2,64,1024]{2,1,0:T(8,128)(2,1)S(1)} %get-tuple-element.45), channel_id=1, source_target_pairs={{0,8},{8,0},{16,24},{24,16},{1,9},{9,1},{17,25},{25,17},{2,10},{10... | collective-permute-start | bytes 786440 | tf_op jit(solution)/shard_map/ppermute | solution.py:23
  185.6 13.4 %collective-permute-start.43 = (bf16[2,64,1024]{2,1,0:T(8,128)(2,1)S(1)}, bf16[2,64,1024]{2,1,0:T(8,128)(2,1)S(1)}, u32[]{:S(2)}, u32[]{:S(2)}) collective-permute-start(bf16[2,64,1024]{2,1,0:T(8,128)(2,1)S(1)} %get-tuple-element.47), channel_id=1, source_target_pairs={{0,8},{8,0},{16,24},{24,16},{1,9},{9,1},{17,25},{25,17},{2,10},{10... | collective-permute-start | bytes 786440 | tf_op jit(solution)/shard_map/ppermute | solution.py:23
  191.4 24.8 %collective-permute-start.45 = (bf16[2,64,1024]{2,1,0:T(8,128)(2,1)S(1)}, bf16[2,64,1024]{2,1,0:T(8,128)(2,1)S(1)}, u32[]{:S(2)}, u32[]{:S(2)}) collective-permute-start(bf16[2,64,1024]{2,1,0:T(8,128)(2,1)S(1)} %get-tuple-element.49), channel_id=1, source_target_pairs={{0,16},{8,24},{16,0},{24,8},{1,17},{9,25},{17,1},{25,9},{2,18},{10... | collective-permute-start | bytes 786440 | tf_op jit(solution)/shard_map/ppermute | solution.py:23
  198.3 7.0 %collective-permute-start.46 = (bf16[2,64,1024]{2,1,0:T(8,128)(2,1)S(1)}, bf16[2,64,1024]{2,1,0:T(8,128)(2,1)S(1)}, u32[]{:S(2)}, u32[]{:S(2)}) collective-permute-start(bf16[2,64,1024]{2,1,0:T(8,128)(2,1)S(1)} %get-tuple-element.51), channel_id=1, source_target_pairs={{0,16},{8,24},{16,0},{24,8},{1,17},{9,25},{17,1},{25,9},{2,18},{10... | collective-permute-start | bytes 786440 | tf_op jit(solution)/shard_map/ppermute | solution.py:23
  199.0 7.9 %collective-permute-start.33 = (bf16[2,64,1024]{2,1,0:T(8,128)(2,1)S(1)}, bf16[2,64,1024]{2,1,0:T(8,128)(2,1)S(1)}, u32[]{:S(2)}, u32[]{:S(2)}) collective-permute-start(bf16[2,64,1024]{2,1,0:T(8,128)(2,1)S(1)} %get-tuple-element.43), channel_id=1, source_target_pairs={{0,8},{8,0},{16,24},{24,16},{1,9},{9,1},{17,25},{25,17},{2,10},{10... | collective-permute-start | bytes 786440 | tf_op jit(solution)/shard_map/ppermute | solution.py:23
  205.3 9.2 %collective-permute-start.50 = (bf16[2,64,1024]{2,1,0:T(8,128)(2,1)S(1)}, bf16[2,64,1024]{2,1,0:T(8,128)(2,1)S(1)}, u32[]{:S(2)}, u32[]{:S(2)}) collective-permute-start(bf16[2,64,1024]{2,1,0:T(8,128)(2,1)S(1)} %add_convert_fusion), channel_id=1, source_target_pairs={{0,8},{8,0},{16,24},{24,16},{1,9},{9,1},{17,25},{25,17},{2,10},{10... | collective-permute-start | bytes 786440 | tf_op jit(solution)/shard_map/ppermute | solution.py:23
  206.9 16.8 %collective-permute-start.32 = (bf16[2,64,1024]{2,1,0:T(8,128)(2,1)S(1)}, bf16[2,64,1024]{2,1,0:T(8,128)(2,1)S(1)}, u32[]{:S(2)}, u32[]{:S(2)}) collective-permute-start(bf16[2,64,1024]{2,1,0:T(8,128)(2,1)S(1)} %get-tuple-element.41), channel_id=1, source_target_pairs={{0,8},{8,0},{16,24},{24,16},{1,9},{9,1},{17,25},{25,17},{2,10},{10... | collective-permute-start | bytes 786440 | tf_op jit(solution)/shard_map/ppermute | solution.py:23
  207.6 16.0 %collective-permute-start.44 = (bf16[2,64,1024]{2,1,0:T(8,128)(2,1)S(1)}, bf16[2,64,1024]{2,1,0:T(8,128)(2,1)S(1)}, u32[]{:S(2)}, u32[]{:S(2)}) collective-permute-start(bf16[2,64,1024]{2,1,0:T(8,128)(2,1)S(1)} %add_convert_fusion.2), channel_id=1, source_target_pairs={{0,16},{8,24},{16,0},{24,8},{1,17},{9,25},{17,1},{25,9},{2,18},{10... | collective-permute-start | bytes 786440 | tf_op jit(solution)/shard_map/ppermute | solution.py:23
  214.6 8.0 %collective-permute-start.47 = (bf16[2,64,1024]{2,1,0:T(8,128)(2,1)S(1)}, bf16[2,64,1024]{2,1,0:T(8,128)(2,1)S(1)}, u32[]{:S(2)}, u32[]{:S(2)}) collective-permute-start(bf16[2,64,1024]{2,1,0:T(8,128)(2,1)S(1)} %add_convert_fusion.1), channel_id=1, source_target_pairs={{0,8},{8,0},{16,24},{24,16},{1,9},{9,1},{17,25},{25,17},{2,10},{10... | collective-permute-start | bytes 786440 | tf_op jit(solution)/shard_map/ppermute | solution.py:23
  216.2 7.5 %collective-permute-start.34 = (bf16[2,64,1024]{2,1,0:T(8,128)(2,1)S(1)}, bf16[2,64,1024]{2,1,0:T(8,128)(2,1)S(1)}, u32[]{:S(2)}, u32[]{:S(2)}) collective-permute-start(bf16[2,64,1024]{2,1,0:T(8,128)(2,1)S(1)} %add_convert_fusion.3), channel_id=1, source_target_pairs={{0,16},{8,24},{16,0},{24,8},{1,17},{9,25},{17,1},{25,9},{2,18},{10... | collective-permute-start | bytes 786440 | tf_op jit(solution)/shard_map/ppermute | solution.py:23
  (22 other events, 137.0 us)

commit v2 on v1

--- a/solution.py
+++ b/solution.py
@@ -11,6 +11,8 @@
 F32 = jnp.float32
 WANTED_CHUNKS = 2
 ROW_TILE = 16
+VMEM_BYTES = 46 << 20
+SMALL_COST = pl.CostEstimate(flops=1 << 20, bytes_accessed=1 << 10, transcendentals=0)
 
 
 def pick_tile(size, wanted):
@@ -21,6 +23,12 @@
 
 def swap(x, axis, size, offset):
     return lax.ppermute(x, axis, [(i, i ^ offset) for i in range(size)])
+
+
+def after(values, earlier):
+    if not earlier:
+        return list(values)
+    return list(lax.optimization_barrier(list(values) + list(earlier)))[:len(values)]
 
 
 class Plan:
@@ -45,9 +53,10 @@
         self.lane_sources = list(zip(starts[:-1], starts[1:]))
 
 
-def encode_kernel(plan, resid_ref, w_ref, b_ref, *outs):
+def encode_kernel(plan, first_source, resid_ref, w_ref, b_ref, *outs):
     product = jnp.dot(resid_ref[0], w_ref[0], preferred_element_type=F32)
-    value = jnp.maximum(product + b_ref[0], 0.0).astype(BF16)
+    bias = b_ref[pl.ds(first_source + pl.program_id(0), 1), :]
+    value = jnp.maximum(product + bias, 0.0).astype(BF16)
     outs[-1][0] = value
     for c in range(plan.chunks):
         for b in range(plan.per_group):
@@ -64,23 +73,19 @@
     out_specs = [pl.BlockSpec((1, plan.block, tile), lambda s, j: (s, 0, j))] * plan.chunks
     out_specs.append(pl.BlockSpec((1, plan.rows, tile), lambda s, j: (s, 0, j)))
     return pl.pallas_call(
-        partial(encode_kernel, plan),
+        partial(encode_kernel, plan, lo),
         grid=(n, plan.width // tile),
         in_specs=[
             pl.BlockSpec((1, plan.rows, plan.model), lambda s, j: (s + lo, 0, 0)),
             pl.BlockSpec((1, plan.model, tile), lambda s, j: (s + lo, 0, j)),
-            pl.BlockSpec((1, 1, tile), lambda s, j: (s + lo, 0, j)),
+            pl.BlockSpec((plan.sources, tile), lambda s, j: (0, j)),
         ],
         out_specs=out_specs,
         out_shape=out_shape,
-        cost_estimate=pl.CostEstimate(
-            flops=2 * n * plan.rows * plan.model * plan.width,
-            bytes_accessed=2 * n * plan.model * plan.width,
-            transcendentals=0,
-        ),
-        compiler_params=pltpu.CompilerParams(vmem_limit_bytes=32 << 20),
+        cost_estimate=SMALL_COST,
+        compiler_params=pltpu.CompilerParams(vmem_limit_bytes=VMEM_BYTES),
         name="encode",
-    )(resid, w_enc, b_enc[:, None, :])
+    )(resid, w_enc, b_enc)
 
 
 def decode_kernel(plan, index_ref, *refs):
@@ -129,12 +134,8 @@
             jax.ShapeDtypeStruct((half, plan.model), F32),
         ],
         scratch_shapes=[pltpu.VMEM((2 * half, depth), BF16)],
-        cost_estimate=pl.CostEstimate(
-            flops=4 * half * depth * plan.model,
-            bytes_accessed=2 * depth * plan.model,
-            transcendentals=0,
-        ),
-        compiler_params=pltpu.CompilerParams(vmem_limit_bytes=32 << 20),
+        cost_estimate=SMALL_COST,
+        compiler_params=pltpu.CompilerParams(vmem_limit_bytes=VMEM_BYTES),
         name="decode",
     )(index, *pieces, w_dec)
 
@@ -150,6 +151,8 @@
 def gradient_kernel(plan, lane, index_ref, *refs):
     n_in = 2 * plan.depth
     errors, w_ref, outs, e_ref = refs[:n_in], refs[n_in], refs[n_in + 1:-1], refs[-1]
+    if lane == 0:
+        squares_ref, outs = outs[-1], outs[:-1]
     lo, hi = plan.lane_sources[lane]
     first, kept = lane_order(plan, lane)
 
@@ -158,10 +161,19 @@
         for i in range(n_in):
             at = pl.multiple_of(index_ref[1 + plan.sources + i] * plan.piece, ROW_TILE)
             e_ref[pl.ds(at, plan.piece), :] = errors[i][...]
+        if lane == 0:
+            total = jnp.zeros((8, 128), F32)
+            for row in range(0, e_ref.shape[0], ROW_TILE):
+                value = e_ref[row:row + ROW_TILE, :].astype(F32)
+                value = value * value
+                value = value[:8] + value[8:]
+                for col in range(0, plan.model, 128):
+                    total = total + value[:, col:col + 128]
+            squares_ref[...] = total
 
     product = lax.dot_general(
-        e_ref[...], w_ref[0, 0], (((1,), (1,)), ((), ())), preferred_element_type=F32
-    )
+        w_ref[0, 0], e_ref[...], (((1,), (1,)), ((), ())), preferred_element_type=F32
+    ).T
     feeds = index_ref[1 + lo + pl.program_id(0)] > 0
     product = jnp.where(feeds, product, 0.0)
     n = len(kept)
@@ -174,30 +186,30 @@
 def gradient(plan, lane, index, errors, w_dec):
     lo, hi = plan.lane_sources[lane]
     n = hi - lo
-    tile = pick_tile(plan.width, 256)
+    tile = pick_tile(plan.width, 512)
     half = plan.groups // 2
     shape = (n, plan.block, plan.width)
     whole = pl.BlockSpec(memory_space=pltpu.VMEM)
     rows = plan.groups * plan.block
+    extra_specs = [pl.BlockSpec((8, 128), lambda s, j: (0, 0))] if lane == 0 else []
+    extra_shape = [jax.ShapeDtypeStruct((8, 128), F32)] if lane == 0 else []
     outs = pl.pallas_call(
         partial(gradient_kernel, plan, lane),
         grid=(n, plan.width // tile),
         in_specs=[pl.BlockSpec(memory_space=pltpu.SMEM)]
         + [whole] * len(errors)
         + [pl.BlockSpec((1, 1, tile, plan.model), lambda s, j: (s + lo, 0, j, 0))],
-        out_specs=[pl.BlockSpec((1, plan.block, tile), lambda s, j: (s, 0, j))] * (2 * half),
+        out_specs=[pl.BlockSpec((1, plan.block, tile), lambda s, j: (s, 0, j))] * (2 * half)
+        + extra_specs,
         out_shape=[jax.ShapeDtypeStruct(shape, BF16)] * half
-        + [jax.ShapeDtypeStruct(shape, F32)] * half,
+        + [jax.ShapeDtypeStruct(shape, F32)] * half
+        + extra_shape,
         scratch_shapes=[pltpu.VMEM((rows, plan.model), BF16)],
-        cost_estimate=pl.CostEstimate(
-            flops=2 * n * rows * plan.model * plan.width,
-            bytes_accessed=2 * n * plan.model * plan.width,
-            transcendentals=0,
-        ),
-        compiler_params=pltpu.CompilerParams(vmem_limit_bytes=32 << 20),
+        cost_estimate=SMALL_COST,
+        compiler_params=pltpu.CompilerParams(vmem_limit_bytes=VMEM_BYTES),
         name="gradient",
     )(index, *errors, w_dec)
-    return outs[:half], outs[half:]
+    return outs[:half], outs[half:2 * half], outs[2 * half:]
 
 
 def per_device(resid, w_enc, b_enc, w_dec, targets, start_layer):
@@ -221,21 +233,29 @@
     )
 
     gathered = []
+    earlier = []
     for c in range(plan.chunks):
+        own = after([e[c] for e in encoded], earlier)
         pieces = []
         for lane, bits in enumerate(plan.lanes):
-            held = {0: encoded[lane][c]}
+            held = {0: own[lane]}
             for bit in bits:
                 held.update(
                     {j | bit: swap(x, "grp", groups, bit) for j, x in list(held.items())}
                 )
             pieces += [held[j] for j in range(groups)]
         gathered.append(pieces)
-
-    recon_parts, squares = [], 0.0
+        earlier = [pieces[groups - 1]]
+
+    level_bits = [1 << i for i in range(plan.depth.bit_length() - 1)]
+    recon_parts = []
+    squares = jnp.zeros((8, 128), F32)
     lane_results = [[] for _ in plan.lanes]
+    behind, before_parts, before_recon, before_gradient = [], [], [], []
     for c in range(plan.chunks):
-        send, keep = decode(plan, index, gathered[c], w_dec)
+        pieces = after(gathered[c], behind)
+        send, keep = decode(plan, index, pieces, w_dec)
+        keep, = after([keep], before_parts)
         other = swap(send, "feat", feats, 1)
 
         def part(level_to):
@@ -244,38 +264,45 @@
             theirs = lax.dynamic_slice_in_dim(other, first, plan.piece, 0)
             return mine + theirs.astype(F32)
 
-        arrived = [
-            swap(part(level ^ d).astype(BF16), "feat", feats, 2 * d)
-            for d in range(plan.depth - 1, 0, -1)
-        ]
-        recon_rows = part(level)
-        for rows in arrived:
-            recon_rows = recon_rows + rows.astype(F32)
+        held = {d: part(level ^ d) for d in range(plan.depth)}
+        for bit in level_bits:
+            sends = {d: held.pop(d).astype(BF16) for d in sorted(held) if d & bit}
+            behind = list(sends.values())
+            for d in sorted(sends, reverse=True):
+                arrived = swap(sends[d], "feat", feats, 2 * bit)
+                held[d ^ bit] = held[d ^ bit] + arrived.astype(F32)
+        recon_rows, = after([held[0]], before_recon)
         first = feat * plan.rows_feat + c * plan.piece
         own_targets = lax.dynamic_slice_in_dim(targets[0], first, plan.piece, 0)
         difference = recon_rows - own_targets.astype(F32)
         recon_parts.append(recon_rows.astype(BF16))
-        squares = squares + jnp.sum(difference * difference)
-
-        error = difference.astype(BF16)
-        errors = [error] + [
-            swap(error, "feat", feats, 2 * d) for d in range(1, plan.depth)
-        ]
+
+        held = {0: difference.astype(BF16)}
+        before_parts = [held[0]]
+        for bit in reversed(level_bits):
+            held.update(
+                {d | bit: swap(x, "feat", feats, 2 * bit) for d, x in list(held.items())}
+            )
+        errors = [held[d] for d in range(plan.depth)]
         errors += [swap(e, "feat", feats, 1) for e in errors]
-
+        errors = after(errors, before_gradient)
+
+        before_recon, before_gradient = [], []
         for lane, bits in enumerate(plan.lanes):
-            away, kept = gradient(plan, lane, index, errors, w_dec)
+            away, kept, extra = gradient(plan, lane, index, errors, w_dec)
+            before_recon += away
+            if extra:
+                squares = squares + extra[0]
             for step, bit in enumerate(bits):
                 got = [swap(x, "grp", groups, bit) for x in away]
                 total = [x + y.astype(F32) for x, y in zip(kept, got)]
                 cut = len(total) // 2
                 away = [x.astype(BF16) for x in total[:cut]]
+                before_gradient += away
                 kept = total[cut:]
             lane_results[lane].append(total[0])
 
-    loss = jnp.full((8, 128), squares, F32)
-    for bit in (1 << i for i in range(feats.bit_length() - 1)):
-        loss = loss + swap(loss, "feat", feats, bit)
+    loss = jnp.full((8, 128), jnp.sum(squares), F32)
     for bit in (1 << i for i in range(groups.bit_length() - 1)):
         loss = loss + swap(loss, "grp", groups, bit)
     entries = targets.shape[0] * groups * plan.tokens * plan.model

time: 229 us -> 210 us (0.917)
  local copies, waits for them, and re-layouts: 42.3 us -> 23.5 us
  Pallas kernels: 48.1 us -> 66 us
  starting transfers between devices: 64.8 us -> 46.9 us
  other arithmetic: 10.2 us -> 15 us
  waiting for transfers between devices: 58.6 us -> 54.4 us
    unnamed x39 -> x63, local copies, waits for them, and re-layouts: 38.3 us -> 18.4 us
    ppermute x51 -> x48, starting transfers between devices: 64.8 us -> 46.9 us  [swap(): return lax.ppermute(x, axis, [(i, i ^ offset) for i in range(size)])]
    pallas_call x2, Pallas kernels: 18.8 us -> 24.8 us  [decode(): pl.pallas_call(partial(decode_kernel, plan), grid=(plan.model // tile,),...]
    pallas_call x2, Pallas kernels: 8.32 us -> 14.4 us  [encode(): pl.pallas_call(partial(encode_kernel, plan, lo), grid=(n, plan.width // t...]
    pallas_call x4, Pallas kernels: 21 us -> 26.8 us  [gradient(): pl.pallas_call(partial(gradient_kernel, plan, lane), grid=(n, plan.width...]
    ppermute x51 -> x48, waiting for transfers between devices: 58.6 us -> 54.4 us  [swap(): return lax.ppermute(x, axis, [(i, i ^ offset) for i in range(size)])]
    convert_element_type x3 -> x6, other arithmetic: 4.59 us -> 8.01 us  [the longest x4 5.16 us: per_device(): sends = {d: held.pop(d).astype(BF16) for d in sorted(held) if d & bit}]
  transfers between devices with their start and end apart: 51 -> 48, of which waited for: 15 -> 18; matrix products, arithmetic and copies ran while one was open for 4% -> 9% of each run, Pallas kernels for 19% -> 22%
where the time goes in v2:
time: 210 us; the launch traced here: 209 us
  Pallas kernels  66 us (31%)
  waiting for transfers between devices  54.4 us (26%)
  starting transfers between devices  46.9 us (22%)
  local copies, waits for them, and re-layouts  23.5 us (11%)
  other arithmetic  15 us (7%)
  between operations  2.8 us (1%)
    ppermute x48, waiting for transfers between devices, swap(): return lax.ppermute(x, axis, [(i, i ^ offset) for i in range(size)])  54.4 us
    ppermute x48, starting transfers between devices, swap(): return lax.ppermute(x, axis, [(i, i ^ offset) for i in range(size)])  46.9 us
    pallas_call x4, Pallas kernels, gradient(): pl.pallas_call(partial(gradient_kernel, plan, lane), grid=(n, plan.width...  26.8 us
    pallas_call x2, Pallas kernels, decode(): pl.pallas_call(partial(decode_kernel, plan), grid=(plan.model // tile,),...  24.8 us
    unnamed x63, local copies, waits for them, and re-layouts  18.4 us
    pallas_call x2, Pallas kernels, encode(): pl.pallas_call(partial(encode_kernel, plan, lo), grid=(n, plan.width // t...  14.4 us
    convert_element_type x4, other arithmetic, per_device(): sends = {d: held.pop(d).astype(BF16) for d in sorted(held) if d & bit}  5.16 us
  transfers between devices with their start and end apart: 48, of which 18 were waited for; matrix products, arithmetic and copies ran while one was open for 9% of the time, Pallas kernels for 22%

profile of v2, /device:TPU:0, one launch (start us, length us, event | category | flops | bytes accessed | tf_op | source)
XLA Modules:
  0.0 208.5 jit_solution(5638001003515722313)
XLA Ops:
  0.6 1.7 copy-done
  3.0 7.2 %encode.3 = (bf16[2,64,1024]{2,1,0:T(8,128)(2,1)S(1)}, bf16[2,64,1024]{2,1,0:T(8,128)(2,1)S(1)}, bf16[2,128,1024]{2,1,0:T(8,128)(2,1)S(1)}) custom-call(bf16[4,128,2304]{2,1,0:T(8,128)(2,1)S(1)} %copy-done, bf16[4,2304,1024]{2,1,0:T(8,128)(2,1)} %w_ref.3, f32[4,1024]{1,0:T(4,128)S(1)} %copy-done.19), custom_call_target="tpu_custom_call" | custom-call | flops 1048576 | bytes 1024 | tf_op jit(solution)/shard_map/encode/pallas_call | solution.py:75
  10.2 3.0 %collective-permute-start.4 = (bf16[2,64,1024]{2,1,0:T(8,128)(2,1)S(1)}, bf16[2,64,1024]{2,1,0:T(8,128)(2,1)S(1)}, u32[]{:S(2)}, u32[]{:S(2)}) collective-permute-start(bf16[2,64,1024]{2,1,0:T(8,128)(2,1)S(1)} %get-tuple-element.55.refs_4_), channel_id=1, source_target_pairs={{0,16},{8,24},{16,0},{24,8},{1,17},{9,25},{17,1},{25,9},{2,18},{10... | collective-permute-start | bytes 786440 | tf_op jit(solution)/shard_map/ppermute | solution.py:25
  13.3 7.2 %encode.2 = (bf16[2,64,1024]{2,1,0:T(8,128)(2,1)S(1)}, bf16[2,64,1024]{2,1,0:T(8,128)(2,1)S(1)}, bf16[2,128,1024]{2,1,0:T(8,128)(2,1)S(1)}) custom-call(bf16[4,128,2304]{2,1,0:T(8,128)(2,1)S(1)} %copy-done, bf16[4,2304,1024]{2,1,0:T(8,128)(2,1)} %w_ref.3, f32[4,1024]{1,0:T(4,128)S(1)} %copy-done.20), custom_call_target="tpu_custom_call" | custom-call | flops 1048576 | bytes 1024 | tf_op jit(solution)/shard_map/encode/pallas_call | solution.py:75
  20.5 1.6 collective-permute-start
  22.6 1.9 collective-permute-start.5
  24.6 5.2 %collective-permute-done.refs_1_ = bf16[2,64,1024]{2,1,0:T(8,128)(2,1)S(1)} collective-permute-done((bf16[2,64,1024]{2,1,0:T(8,128)(2,1)S(1)}, bf16[2,64,1024]{2,1,0:T(8,128)(2,1)S(1)}, u32[]{:S(2)}, u32[]{:S(2)}) %collective-permute-start) | collective-permute-done | bytes 262176 | tf_op jit(solution)/shard_map/ppermute | solution.py:25
  31.1 4.3 %collective-permute-done.3.refs_5_ = bf16[2,64,1024]{2,1,0:T(8,128)(2,1)S(1)} collective-permute-done((bf16[2,64,1024]{2,1,0:T(8,128)(2,1)S(1)}, bf16[2,64,1024]{2,1,0:T(8,128)(2,1)S(1)}, u32[]{:S(2)}, u32[]{:S(2)}) %collective-permute-start.3) | collective-permute-done | bytes 262176 | tf_op jit(solution)/shard_map/ppermute | solution.py:25
  36.8 2.7 %collective-permute-done.5.refs_7_ = bf16[2,64,1024]{2,1,0:T(8,128)(2,1)S(1)} collective-permute-done((bf16[2,64,1024]{2,1,0:T(8,128)(2,1)S(1)}, bf16[2,64,1024]{2,1,0:T(8,128)(2,1)S(1)}, u32[]{:S(2)}, u32[]{:S(2)}) %collective-permute-start.5) | collective-permute-done | bytes 262176 | tf_op jit(solution)/shard_map/ppermute | solution.py:25
  44.7 12.6 %decode.2 = (bf16[128,2304]{1,0:T(8,128)(2,1)}, f32[128,2304]{1,0:T(8,128)S(1)}) custom-call(s32[13]{0:T(128)S(1)} %copy-done.21, bf16[2,64,1024]{2,1,0:T(8,128)(2,1)S(1)} %get-tuple-element.54.refs_0_, bf16[2,64,1024]{2,1,0:T(8,128)(2,1)S(1)} %copy-done.6, bf16[2,64,1024]{2,1,0:T(8,128)(2,1)S(1)} %copy-done.10, ...), custom_call_target="tpu_custom_call" | custom-call | flops 1048576 | bytes 1024 | tf_op jit(solution)/shard_map/decode/pallas_call | solution.py:125
  57.3 1.5 collective-permute-start.10
  59.7 1.7 add_convert_fusion.9
  61.4 1.6 collective-permute-start.8
  63.0 1.2 collective-permute-start.11
  66.5 1.4 collective-permute-done.14.refs_6_
  68.5 1.6 collective-permute-start.7
  70.1 1.7 add_convert_fusion.7
  71.7 1.8 collective-permute-done.11.refs_2_
  74.3 2.6 %collective-permute-start.9 = (bf16[32,2304]{1,0:T(8,128)(2,1)}, bf16[32,2304]{1,0:T(8,128)(2,1)}, u32[]{:S(2)}, u32[]{:S(2)}) collective-permute-start(bf16[32,2304]{1,0:T(8,128)(2,1)} %add_convert_fusion.7), channel_id=1, source_target_pairs={{0,4},{1,5},{2,6},{3,7},{4,0},{5,1},{6,2},{7,3},{8,12},{9,13},{10,... | collective-permute-start | bytes 442376 | tf_op jit(solution)/shard_map/ppermute | solution.py:25
  76.9 1.7 collective-permute-done.12.refs_3_
  84.0 12.2 %decode.3 = (bf16[128,2304]{1,0:T(8,128)(2,1)S(1)}, f32[128,2304]{1,0:T(8,128)S(1)}) custom-call(s32[13]{0:T(128)S(1)} %copy-done.22, bf16[2,64,1024]{2,1,0:T(8,128)(2,1)S(1)} %copy-done.4, bf16[2,64,1024]{2,1,0:T(8,128)(2,1)S(1)} %copy-done.14, bf16[2,64,1024]{2,1,0:T(8,128)(2,1)S(1)} %copy-done.18, bf16[2,64,1024]{2,1,0:T(8,128)(2,1)} %collective-permute-done.12.refs_3_, ...), custom_call_target="tpu_custom_call" | custom-call | flops 1048576 | bytes 1024 | tf_op jit(solution)/shard_map/decode/pallas_call | solution.py:125
  96.3 1.9 fusion.3
  98.2 2.6 %collective-permute-start.21 = (bf16[32,2304]{1,0:T(8,128)(2,1)S(1)}, bf16[32,2304]{1,0:T(8,128)(2,1)S(1)}, u32[]{:S(2)}, u32[]{:S(2)}) collective-permute-start(bf16[32,2304]{1,0:T(8,128)(2,1)S(1)} %get-tuple-element.105.refs_0_), channel_id=1, source_target_pairs={{0,4},{1,5},{2,6},{3,7},{4,0},{5,1},{6,2},{7,3},{8,12},{9,13},{10,... | collective-permute-start | bytes 442376 | tf_op jit(solution)/shard_map/ppermute | solution.py:25
  100.8 1.6 collective-permute-start.20
  102.4 6.2 %collective-permute-done.21.refs_2_ = bf16[32,2304]{1,0:T(8,128)(2,1)S(1)} collective-permute-done((bf16[32,2304]{1,0:T(8,128)(2,1)S(1)}, bf16[32,2304]{1,0:T(8,128)(2,1)S(1)}, u32[]{:S(2)}, u32[]{:S(2)}) %collective-permute-start.21) | collective-permute-done | bytes 147488 | tf_op jit(solution)/shard_map/ppermute | solution.py:25
  110.6 3.4 %collective-permute-done.22.refs_3_ = bf16[32,2304]{1,0:T(8,128)(2,1)S(1)} collective-permute-done((bf16[32,2304]{1,0:T(8,128)(2,1)S(1)}, bf16[32,2304]{1,0:T(8,128)(2,1)S(1)}, u32[]{:S(2)}, u32[]{:S(2)}) %collective-permute-start.22) | collective-permute-done | bytes 147488 | tf_op jit(solution)/shard_map/ppermute | solution.py:25
  117.5 1.2 pad_maximum_fusion
  118.7 1.8 copy.12
  121.5 6.5 %gradient.5 = (bf16[2,64,1024]{2,1,0:T(8,128)(2,1)S(1)}, bf16[2,64,1024]{2,1,0:T(8,128)(2,1)S(1)}, f32[2,64,1024]{2,1,0:T(8,128)S(1)}, f32[2,64,1024]{2,1,0:T(8,128)S(1)}) custom-call(s32[13]{0:T(128)S(1)} %copy-done.23, bf16[32,2304]{1,0:T(8,128)(2,1)S(1)} %get-tuple-element.105.refs_0_, bf16[32,2304]{1,0:T(8,128)(2,1)S(1)} %collective-permute-done.20.refs_1_, ...), custom_call_target="tpu_custom_call" | custom-call | flops 1048576 | bytes 1024 | tf_op jit(solution)/shard_map/gradient/pallas_call | solution.py:196
  128.6 1.5 collective-permute-start.43
  130.1 6.8 %gradient.4 = (bf16[2,64,1024]{2,1,0:T(8,128)(2,1)S(1)}, bf16[2,64,1024]{2,1,0:T(8,128)(2,1)S(1)}, f32[2,64,1024]{2,1,0:T(8,128)S(1)}, f32[2,64,1024]{2,1,0:T(8,128)S(1)}, f32[8,128]{1,0:T(8,128)S(1)}) custom-call(s32[13]{0:T(128)S(1)} %copy-done.23, bf16[32,2304]{1,0:T(8,128)(2,1)S(1)} %get-tuple-element.105.refs_0_, ...), custom_call_target="tpu_custom_call" | custom-call | flops 1048576 | bytes 1024 | tf_op jit(solution)/shard_map/gradient/pallas_call | solution.py:196
  138.5 2.7 %collective-permute-start.19 = (bf16[32,2304]{1,0:T(8,128)(2,1)S(1)}, bf16[32,2304]{1,0:T(8,128)(2,1)S(1)}, u32[]{:S(2)}, u32[]{:S(2)}) collective-permute-start(bf16[32,2304]{1,0:T(8,128)(2,1)S(1)} %add_convert_fusion.4), channel_id=1, source_target_pairs={{0,4},{1,5},{2,6},{3,7},{4,0},{5,1},{6,2},{7,3},{8,12},{9,13},{10,... | collective-permute-start | bytes 442376 | tf_op jit(solution)/shard_map/ppermute | solution.py:25
  141.3 1.6 collective-permute-start.44
  142.8 4.7 %collective-permute-done.19 = bf16[32,2304]{1,0:T(8,128)(2,1)S(1)} collective-permute-done((bf16[32,2304]{1,0:T(8,128)(2,1)S(1)}, bf16[32,2304]{1,0:T(8,128)(2,1)S(1)}, u32[]{:S(2)}, u32[]{:S(2)}) %collective-permute-start.19) | collective-permute-done | bytes 147488 | tf_op jit(solution)/shard_map/ppermute | solution.py:25
  148.8 4.1 %collective-permute-start.27 = (bf16[32,2304]{1,0:T(8,128)(2,1)S(1)}, bf16[32,2304]{1,0:T(8,128)(2,1)S(1)}, u32[]{:S(2)}, u32[]{:S(2)}) collective-permute-start(bf16[32,2304]{1,0:T(8,128)(2,1)S(1)} %get-tuple-element.81.refs_0_), channel_id=1, source_target_pairs={{0,2},{1,3},{2,0},{3,1},{4,6},{5,7},{6,4},{7,5},{8,10},{9,11},{10,... | collective-permute-start | bytes 442376 | tf_op jit(solution)/shard_map/ppermute | solution.py:25
  152.9 4.8 %collective-permute-done.28.refs_2_ = bf16[32,2304]{1,0:T(8,128)(2,1)S(1)} collective-permute-done((bf16[32,2304]{1,0:T(8,128)(2,1)S(1)}, bf16[32,2304]{1,0:T(8,128)(2,1)S(1)}, u32[]{:S(2)}, u32[]{:S(2)}) %collective-permute-start.28) | collective-permute-done | bytes 147488 | tf_op jit(solution)/shard_map/ppermute | solution.py:25
  158.4 1.5 collective-permute-start.38
  160.9 1.9 collective-permute-done.29.refs_3_
  163.0 1.2 collective-permute-done.33.refs_7_
  164.2 6.5 %gradient.7 = (bf16[2,64,1024]{2,1,0:T(8,128)(2,1)S(1)}, bf16[2,64,1024]{2,1,0:T(8,128)(2,1)S(1)}, f32[2,64,1024]{2,1,0:T(8,128)S(1)}, f32[2,64,1024]{2,1,0:T(8,128)S(1)}) custom-call(s32[13]{0:T(128)S(1)} %copy-done.23, bf16[32,2304]{1,0:T(8,128)(2,1)S(1)} %get-tuple-element.81.refs_0_, bf16[32,2304]{1,0:T(8,128)(2,1)S(1)} %collective-permute-done.27.refs_1_, ...), custom_call_target="tpu_custom_call" | custom-call | flops 1048576 | bytes 1024 | tf_op jit(solution)/shard_map/gradient/pallas_call | solution.py:196
  171.7 7.0 %gradient.6 = (bf16[2,64,1024]{2,1,0:T(8,128)(2,1)S(1)}, bf16[2,64,1024]{2,1,0:T(8,128)(2,1)S(1)}, f32[2,64,1024]{2,1,0:T(8,128)S(1)}, f32[2,64,1024]{2,1,0:T(8,128)S(1)}, f32[8,128]{1,0:T(8,128)S(1)}) custom-call(s32[13]{0:T(128)S(1)} %copy-done.23, bf16[32,2304]{1,0:T(8,128)(2,1)S(1)} %get-tuple-element.81.refs_0_, ...), custom_call_target="tpu_custom_call" | custom-call | flops 1048576 | bytes 1024 | tf_op jit(solution)/shard_map/gradient/pallas_call | solution.py:196
  181.2 1.6 collective-permute-start.45
  183.3 1.5 collective-permute-start.41
  187.1 2.0 collective-permute-done.37
  190.9 6.7 %collective-permute-done.41 = bf16[2,64,1024]{2,1,0:T(8,128)(2,1)S(1)} collective-permute-done((bf16[2,64,1024]{2,1,0:T(8,128)(2,1)S(1)}, bf16[2,64,1024]{2,1,0:T(8,128)(2,1)S(1)}, u32[]{:S(2)}, u32[]{:S(2)}) %collective-permute-start.41) | collective-permute-done | bytes 262176 | tf_op jit(solution)/shard_map/ppermute | solution.py:25
  198.2 3.2 %collective-permute-done.47 = bf16[2,64,1024]{2,1,0:T(8,128)(2,1)S(1)} collective-permute-done((bf16[2,64,1024]{2,1,0:T(8,128)(2,1)S(1)}, bf16[2,64,1024]{2,1,0:T(8,128)(2,1)S(1)}, u32[]{:S(2)}, u32[]{:S(2)}) %collective-permute-start.47) | collective-permute-done | bytes 262176 | tf_op jit(solution)/shard_map/ppermute | solution.py:25
  202.5 1.6 collective-permute-done.42
  205.1 2.3 %maximum_bitcast_fusion = f32[128,4,1024]{2,1,0:T(4,128)} fusion(f32[2,128,1024]{2,0,1:T(2,128)S(1)} %bitcast.36, f32[2,128,1024]{2,0,1:T(2,128)S(1)} %bitcast.37), kind=kLoop, calls=%fused_computation | loop fusion | flops 524288 | bytes 4194304 | tf_op jit(solution)/shard_map/transpose | solution.py:321
  (150 shorter events, 41.0 us)
Async XLA Ops:
  10.2 12.4 %collective-permute-start.4 = (bf16[2,64,1024]{2,1,0:T(8,128)(2,1)S(1)}, bf16[2,64,1024]{2,1,0:T(8,128)(2,1)S(1)}, u32[]{:S(2)}, u32[]{:S(2)}) collective-permute-start(bf16[2,64,1024]{2,1,0:T(8,128)(2,1)S(1)} %get-tuple-element.55.refs_4_), channel_id=1, source_target_pairs={{0,16},{8,24},{16,0},{24,8},{1,17},{9,25},{17,1},{25,9},{2,18},{10... | collective-permute-start | bytes 786440 | tf_op jit(solution)/shard_map/ppermute | solution.py:25
  20.5 9.3 %collective-permute-start = (bf16[2,64,1024]{2,1,0:T(8,128)(2,1)S(1)}, bf16[2,64,1024]{2,1,0:T(8,128)(2,1)S(1)}, u32[]{:S(2)}, u32[]{:S(2)}) collective-permute-start(bf16[2,64,1024]{2,1,0:T(8,128)(2,1)S(1)} %get-tuple-element.54.refs_0_), channel_id=1, source_target_pairs={{0,8},{8,0},{16,24},{24,16},{1,9},{9,1},{17,25},{25,17},{2,10},{10... | collective-permute-start | bytes 786440 | tf_op jit(solution)/shard_map/ppermute | solution.py:25
  22.0 13.4 %collective-permute-start.3 = (bf16[2,64,1024]{2,1,0:T(8,128)(2,1)S(1)}, bf16[2,64,1024]{2,1,0:T(8,128)(2,1)S(1)}, u32[]{:S(2)}, u32[]{:S(2)}) collective-permute-start(bf16[2,64,1024]{2,1,0:T(8,128)(2,1)S(1)} %get-tuple-element.55.refs_4_), channel_id=1, source_target_pairs={{0,8},{8,0},{16,24},{24,16},{1,9},{9,1},{17,25},{25,17},{2,10},{10... | collective-permute-start | bytes 786440 | tf_op jit(solution)/shard_map/ppermute | solution.py:25
  22.6 13.5 %collective-permute-start.1 = (bf16[2,64,1024]{2,1,0:T(8,128)(2,1)S(1)}, bf16[2,64,1024]{2,1,0:T(8,128)(2,1)S(1)}, u32[]{:S(2)}, u32[]{:S(2)}) collective-permute-start(bf16[2,64,1024]{2,1,0:T(8,128)(2,1)S(1)} %get-tuple-element.54.refs_0_), channel_id=1, source_target_pairs={{0,16},{8,24},{16,0},{24,8},{1,17},{9,25},{17,1},{25,9},{2,18},{10... | collective-permute-start | bytes 786440 | tf_op jit(solution)/shard_map/ppermute | solution.py:25
  22.6 16.9 %collective-permute-start.5 = (bf16[2,64,1024]{2,1,0:T(8,128)(2,1)S(1)}, bf16[2,64,1024]{2,1,0:T(8,128)(2,1)S(1)}, u32[]{:S(2)}, u32[]{:S(2)}) collective-permute-start(bf16[2,64,1024]{2,1,0:T(8,128)(2,1)S(1)} %collective-permute-done.4.refs_6_), channel_id=1, source_target_pairs={{0,8},{8,0},{16,24},{24,16},{1,9},{9,1},{17,25},{25,17},{2,10},{10... | collective-permute-start | bytes 786440 | tf_op jit(solution)/shard_map/ppermute | solution.py:25
  29.8 10.5 %collective-permute-start.2 = (bf16[2,64,1024]{2,1,0:T(8,128)(2,1)S(1)}, bf16[2,64,1024]{2,1,0:T(8,128)(2,1)}, u32[]{:S(2)}, u32[]{:S(2)}) collective-permute-start(bf16[2,64,1024]{2,1,0:T(8,128)(2,1)S(1)} %collective-permute-done.refs_1_), channel_id=1, source_target_pairs={{0,16},{8,24},{16,0},{24,8},{1,17},{9,25},{17,1},{25,9},{2,18},{10... | collective-permute-start | bytes 786440 | tf_op jit(solution)/shard_map/ppermute | solution.py:25
  57.3 2.3 %collective-permute-start.6 = (bf16[128,2304]{1,0:T(8,128)(2,1)}, bf16[128,2304]{1,0:T(8,128)(2,1)}, u32[]{:S(2)}, u32[]{:S(2)}) collective-permute-start(bf16[128,2304]{1,0:T(8,128)(2,1)} %get-tuple-element.57), channel_id=1, source_target_pairs={{0,1},{1,0},{2,3},{3,2},{4,5},{5,4},{6,7},{7,6},{8,9},{9,8},{10,11... | collective-permute-start | bytes 1769480 | tf_op jit(solution)/shard_map/ppermute | solution.py:25
  57.3 8.7 %collective-permute-start.10 = (bf16[2,64,1024]{2,1,0:T(8,128)(2,1)S(1)}, bf16[2,64,1024]{2,1,0:T(8,128)(2,1)S(1)}, u32[]{:S(2)}, u32[]{:S(2)}) collective-permute-start(bf16[2,64,1024]{2,1,0:T(8,128)(2,1)S(1)} %get-tuple-element.62.refs_0_), channel_id=1, source_target_pairs={{0,8},{8,0},{16,24},{24,16},{1,9},{9,1},{17,25},{25,17},{2,10},{10... | collective-permute-start | bytes 786440 | tf_op jit(solution)/shard_map/ppermute | solution.py:25
  58.8 9.1 %collective-permute-start.14 = (bf16[2,64,1024]{2,1,0:T(8,128)(2,1)S(1)}, bf16[2,64,1024]{2,1,0:T(8,128)(2,1)S(1)}, u32[]{:S(2)}, u32[]{:S(2)}) collective-permute-start(bf16[2,64,1024]{2,1,0:T(8,128)(2,1)S(1)} %get-tuple-element.66.refs_4_), channel_id=1, source_target_pairs={{0,16},{8,24},{16,0},{24,8},{1,17},{9,25},{17,1},{25,9},{2,18},{10... | collective-permute-start | bytes 786440 | tf_op jit(solution)/shard_map/ppermute | solution.py:25
  61.4 7.1 %collective-permute-start.8 = (bf16[32,2304]{1,0:T(8,128)(2,1)}, bf16[32,2304]{1,0:T(8,128)(2,1)}, u32[]{:S(2)}, u32[]{:S(2)}) collective-permute-start(bf16[32,2304]{1,0:T(8,128)(2,1)} %get-tuple-element.109), channel_id=1, source_target_pairs={{0,2},{1,3},{2,0},{3,1},{4,6},{5,7},{6,4},{7,5},{8,10},{9,11},{10,... | collective-permute-start | bytes 442376 | tf_op jit(solution)/shard_map/ppermute | solution.py:25
  63.0 10.6 %collective-permute-start.11 = (bf16[2,64,1024]{2,1,0:T(8,128)(2,1)S(1)}, bf16[2,64,1024]{2,1,0:T(8,128)(2,1)S(1)}, u32[]{:S(2)}, u32[]{:S(2)}) collective-permute-start(bf16[2,64,1024]{2,1,0:T(8,128)(2,1)S(1)} %get-tuple-element.62.refs_0_), channel_id=1, source_target_pairs={{0,16},{8,24},{16,0},{24,8},{1,17},{9,25},{17,1},{25,9},{2,18},{10... | collective-permute-start | bytes 786440 | tf_op jit(solution)/shard_map/ppermute | solution.py:25
  64.2 12.7 %collective-permute-start.13 = (bf16[2,64,1024]{2,1,0:T(8,128)(2,1)S(1)}, bf16[2,64,1024]{2,1,0:T(8,128)(2,1)}, u32[]{:S(2)}, u32[]{:S(2)}) collective-permute-start(bf16[2,64,1024]{2,1,0:T(8,128)(2,1)S(1)} %get-tuple-element.66.refs_4_), channel_id=1, source_target_pairs={{0,8},{8,0},{16,24},{24,16},{1,9},{9,1},{17,25},{25,17},{2,10},{10... | collective-permute-start | bytes 786440 | tf_op jit(solution)/shard_map/ppermute | solution.py:25
  66.0 12.6 %collective-permute-start.12 = (bf16[2,64,1024]{2,1,0:T(8,128)(2,1)S(1)}, bf16[2,64,1024]{2,1,0:T(8,128)(2,1)}, u32[]{:S(2)}, u32[]{:S(2)}) collective-permute-start(bf16[2,64,1024]{2,1,0:T(8,128)(2,1)S(1)} %collective-permute-done.10.refs_1_), channel_id=1, source_target_pairs={{0,16},{8,24},{16,0},{24,8},{1,17},{9,25},{17,1},{25,9},{2,18},{10... | collective-permute-start | bytes 786440 | tf_op jit(solution)/shard_map/ppermute | solution.py:25
  67.9 10.6 %collective-permute-start.15 = (bf16[2,64,1024]{2,1,0:T(8,128)(2,1)S(1)}, bf16[2,64,1024]{2,1,0:T(8,128)(2,1)}, u32[]{:S(2)}, u32[]{:S(2)}) collective-permute-start(bf16[2,64,1024]{2,1,0:T(8,128)(2,1)S(1)} %collective-permute-done.14.refs_6_), channel_id=1, source_target_pairs={{0,8},{8,0},{16,24},{24,16},{1,9},{9,1},{17,25},{25,17},{2,10},{10... | collective-permute-start | bytes 786440 | tf_op jit(solution)/shard_map/ppermute | solution.py:25
  68.5 27.8 %collective-permute-start.7 = (bf16[32,2304]{1,0:T(8,128)(2,1)}, bf16[32,2304]{1,0:T(8,128)(2,1)}, u32[]{:S(2)}, u32[]{:S(2)}) collective-permute-start(bf16[32,2304]{1,0:T(8,128)(2,1)} %get-tuple-element.108), channel_id=1, source_target_pairs={{0,2},{1,3},{2,0},{3,1},{4,6},{5,7},{6,4},{7,5},{8,10},{9,11},{10,... | collective-permute-start | bytes 442376 | tf_op jit(solution)/shard_map/ppermute | solution.py:25
  74.3 22.0 %collective-permute-start.9 = (bf16[32,2304]{1,0:T(8,128)(2,1)}, bf16[32,2304]{1,0:T(8,128)(2,1)}, u32[]{:S(2)}, u32[]{:S(2)}) collective-permute-start(bf16[32,2304]{1,0:T(8,128)(2,1)} %add_convert_fusion.7), channel_id=1, source_target_pairs={{0,4},{1,5},{2,6},{3,7},{4,0},{5,1},{6,2},{7,3},{8,12},{9,13},{10,... | collective-permute-start | bytes 442376 | tf_op jit(solution)/shard_map/ppermute | solution.py:25
  96.2 17.8 %collective-permute-start.16 = (bf16[128,2304]{1,0:T(8,128)(2,1)S(1)}, bf16[128,2304]{1,0:T(8,128)(2,1)S(1)}, u32[]{:S(2)}, u32[]{:S(2)}) collective-permute-start(bf16[128,2304]{1,0:T(8,128)(2,1)S(1)} %get-tuple-element.72), channel_id=1, source_target_pairs={{0,1},{1,0},{2,3},{3,2},{4,5},{5,4},{6,7},{7,6},{8,9},{9,8},{10,11... | collective-permute-start | bytes 1769480 | tf_op jit(solution)/shard_map/ppermute | solution.py:25
  98.2 10.4 %collective-permute-start.21 = (bf16[32,2304]{1,0:T(8,128)(2,1)S(1)}, bf16[32,2304]{1,0:T(8,128)(2,1)S(1)}, u32[]{:S(2)}, u32[]{:S(2)}) collective-permute-start(bf16[32,2304]{1,0:T(8,128)(2,1)S(1)} %get-tuple-element.105.refs_0_), channel_id=1, source_target_pairs={{0,4},{1,5},{2,6},{3,7},{4,0},{5,1},{6,2},{7,3},{8,12},{9,13},{10,... | collective-permute-start | bytes 442376 | tf_op jit(solution)/shard_map/ppermute | solution.py:25
  100.8 9.7 %collective-permute-start.20 = (bf16[32,2304]{1,0:T(8,128)(2,1)S(1)}, bf16[32,2304]{1,0:T(8,128)(2,1)S(1)}, u32[]{:S(2)}, u32[]{:S(2)}) collective-permute-start(bf16[32,2304]{1,0:T(8,128)(2,1)S(1)} %get-tuple-element.105.refs_0_), channel_id=1, source_target_pairs={{0,2},{1,3},{2,0},{3,1},{4,6},{5,7},{6,4},{7,5},{8,10},{9,11},{10,... | collective-permute-start | bytes 442376 | tf_op jit(solution)/shard_map/ppermute | solution.py:25
  108.6 5.4 %collective-permute-start.22 = (bf16[32,2304]{1,0:T(8,128)(2,1)S(1)}, bf16[32,2304]{1,0:T(8,128)(2,1)S(1)}, u32[]{:S(2)}, u32[]{:S(2)}) collective-permute-start(bf16[32,2304]{1,0:T(8,128)(2,1)S(1)} %collective-permute-done.21.refs_2_), channel_id=1, source_target_pairs={{0,2},{1,3},{2,0},{3,1},{4,6},{5,7},{6,4},{7,5},{8,10},{9,11},{10,... | collective-permute-start | bytes 442376 | tf_op jit(solution)/shard_map/ppermute | solution.py:25
  110.0 10.4 %collective-permute-start.23 = (bf16[32,2304]{1,0:T(8,128)(2,1)S(1)}, bf16[32,2304]{1,0:T(8,128)(2,1)S(1)}, u32[]{:S(2)}, u32[]{:S(2)}) collective-permute-start(bf16[32,2304]{1,0:T(8,128)(2,1)S(1)} %get-tuple-element.105.refs_0_), channel_id=1, source_target_pairs={{0,1},{1,0},{2,3},{3,2},{4,5},{5,4},{6,7},{7,6},{8,9},{9,8},{10,11... | collective-permute-start | bytes 442376 | tf_op jit(solution)/shard_map/ppermute | solution.py:25
  110.0 11.5 %collective-permute-start.25 = (bf16[32,2304]{1,0:T(8,128)(2,1)S(1)}, bf16[32,2304]{1,0:T(8,128)(2,1)S(1)}, u32[]{:S(2)}, u32[]{:S(2)}) collective-permute-start(bf16[32,2304]{1,0:T(8,128)(2,1)S(1)} %collective-permute-done.21.refs_2_), channel_id=1, source_target_pairs={{0,1},{1,0},{2,3},{3,2},{4,5},{5,4},{6,7},{7,6},{8,9},{9,8},{10,11... | collective-permute-start | bytes 442376 | tf_op jit(solution)/shard_map/ppermute | solution.py:25
  110.5 11.0 %collective-permute-start.24 = (bf16[32,2304]{1,0:T(8,128)(2,1)S(1)}, bf16[32,2304]{1,0:T(8,128)(2,1)S(1)}, u32[]{:S(2)}, u32[]{:S(2)}) collective-permute-start(bf16[32,2304]{1,0:T(8,128)(2,1)S(1)} %collective-permute-done.20.refs_1_), channel_id=1, source_target_pairs={{0,1},{1,0},{2,3},{3,2},{4,5},{5,4},{6,7},{7,6},{8,9},{9,8},{10,11... | collective-permute-start | bytes 442376 | tf_op jit(solution)/shard_map/ppermute | solution.py:25
  114.0 7.5 %collective-permute-start.26 = (bf16[32,2304]{1,0:T(8,128)(2,1)S(1)}, bf16[32,2304]{1,0:T(8,128)(2,1)S(1)}, u32[]{:S(2)}, u32[]{:S(2)}) collective-permute-start(bf16[32,2304]{1,0:T(8,128)(2,1)S(1)} %collective-permute-done.22.refs_3_), channel_id=1, source_target_pairs={{0,1},{1,0},{2,3},{3,2},{4,5},{5,4},{6,7},{7,6},{8,9},{9,8},{10,11... | collective-permute-start | bytes 442376 | tf_op jit(solution)/shard_map/ppermute | solution.py:25
  115.6 21.9 %collective-permute-start.18 = (bf16[32,2304]{1,0:T(8,128)(2,1)}, bf16[32,2304]{1,0:T(8,128)(2,1)}, u32[]{:S(2)}, u32[]{:S(2)}) collective-permute-start(bf16[32,2304]{1,0:T(8,128)(2,1)} %get-tuple-element.107), channel_id=1, source_target_pairs={{0,2},{1,3},{2,0},{3,1},{4,6},{5,7},{6,4},{7,5},{8,10},{9,11},{10,... | collective-permute-start | bytes 442376 | tf_op jit(solution)/shard_map/ppermute | solution.py:25
  120.4 22.4 %collective-permute-start.17 = (bf16[32,2304]{1,0:T(8,128)(2,1)S(1)}, bf16[32,2304]{1,0:T(8,128)(2,1)S(1)}, u32[]{:S(2)}, u32[]{:S(2)}) collective-permute-start(bf16[32,2304]{1,0:T(8,128)(2,1)S(1)} %copy-done.29), channel_id=1, source_target_pairs={{0,2},{1,3},{2,0},{3,1},{4,6},{5,7},{6,4},{7,5},{8,10},{9,11},{10,... | collective-permute-start | bytes 442376 | tf_op jit(solution)/shard_map/ppermute | solution.py:25
  128.0 13.2 %collective-permute-start.35 = (bf16[2,64,1024]{2,1,0:T(8,128)(2,1)S(1)}, bf16[2,64,1024]{2,1,0:T(8,128)(2,1)S(1)}, u32[]{:S(2)}, u32[]{:S(2)}) collective-permute-start(bf16[2,64,1024]{2,1,0:T(8,128)(2,1)S(1)} %get-tuple-element.75), channel_id=1, source_target_pairs={{0,16},{8,24},{16,0},{24,8},{1,17},{9,25},{17,1},{25,9},{2,18},{10... | collective-permute-start | bytes 786440 | tf_op jit(solution)/shard_map/ppermute | solution.py:25
  128.6 29.8 %collective-permute-start.43 = (bf16[2,64,1024]{2,1,0:T(8,128)(2,1)S(1)}, bf16[2,64,1024]{2,1,0:T(8,128)(2,1)S(1)}, u32[]{:S(2)}, u32[]{:S(2)}) collective-permute-start(bf16[2,64,1024]{2,1,0:T(8,128)(2,1)S(1)} %get-tuple-element.76), channel_id=1, source_target_pairs={{0,16},{8,24},{16,0},{24,8},{1,17},{9,25},{17,1},{25,9},{2,18},{10... | collective-permute-start | bytes 786440 | tf_op jit(solution)/shard_map/ppermute | solution.py:25
  136.9 11.7 %collective-permute-start.34 = (bf16[2,64,1024]{2,1,0:T(8,128)(2,1)S(1)}, bf16[2,64,1024]{2,1,0:T(8,128)(2,1)S(1)}, u32[]{:S(2)}, u32[]{:S(2)}) collective-permute-start(bf16[2,64,1024]{2,1,0:T(8,128)(2,1)S(1)} %get-tuple-element.73), channel_id=1, source_target_pairs={{0,8},{8,0},{16,24},{24,16},{1,9},{9,1},{17,25},{25,17},{2,10},{10... | collective-permute-start | bytes 786440 | tf_op jit(solution)/shard_map/ppermute | solution.py:25
  138.5 9.0 %collective-permute-start.19 = (bf16[32,2304]{1,0:T(8,128)(2,1)S(1)}, bf16[32,2304]{1,0:T(8,128)(2,1)S(1)}, u32[]{:S(2)}, u32[]{:S(2)}) collective-permute-start(bf16[32,2304]{1,0:T(8,128)(2,1)S(1)} %add_convert_fusion.4), channel_id=1, source_target_pairs={{0,4},{1,5},{2,6},{3,7},{4,0},{5,1},{6,2},{7,3},{8,12},{9,13},{10,... | collective-permute-start | bytes 442376 | tf_op jit(solution)/shard_map/ppermute | solution.py:25
  141.3 19.2 %collective-permute-start.44 = (bf16[2,64,1024]{2,1,0:T(8,128)(2,1)S(1)}, bf16[2,64,1024]{2,1,0:T(8,128)(2,1)S(1)}, u32[]{:S(2)}, u32[]{:S(2)}) collective-permute-start(bf16[2,64,1024]{2,1,0:T(8,128)(2,1)S(1)} %add_convert_fusion.2), channel_id=1, source_target_pairs={{0,8},{8,0},{16,24},{24,16},{1,9},{9,1},{17,25},{25,17},{2,10},{10... | collective-permute-start | bytes 786440 | tf_op jit(solution)/shard_map/ppermute | solution.py:25
  148.5 9.2 %collective-permute-start.28 = (bf16[32,2304]{1,0:T(8,128)(2,1)S(1)}, bf16[32,2304]{1,0:T(8,128)(2,1)S(1)}, u32[]{:S(2)}, u32[]{:S(2)}) collective-permute-start(bf16[32,2304]{1,0:T(8,128)(2,1)S(1)} %get-tuple-element.81.refs_0_), channel_id=1, source_target_pairs={{0,4},{1,5},{2,6},{3,7},{4,0},{5,1},{6,2},{7,3},{8,12},{9,13},{10,... | collective-permute-start | bytes 442376 | tf_op jit(solution)/shard_map/ppermute | solution.py:25
  148.7 11.2 %collective-permute-start.30 = (bf16[32,2304]{1,0:T(8,128)(2,1)S(1)}, bf16[32,2304]{1,0:T(8,128)(2,1)S(1)}, u32[]{:S(2)}, u32[]{:S(2)}) collective-permute-start(bf16[32,2304]{1,0:T(8,128)(2,1)S(1)} %get-tuple-element.81.refs_0_), channel_id=1, source_target_pairs={{0,1},{1,0},{2,3},{3,2},{4,5},{5,4},{6,7},{7,6},{8,9},{9,8},{10,11... | collective-permute-start | bytes 442376 | tf_op jit(solution)/shard_map/ppermute | solution.py:25
  148.8 11.7 %collective-permute-start.27 = (bf16[32,2304]{1,0:T(8,128)(2,1)S(1)}, bf16[32,2304]{1,0:T(8,128)(2,1)S(1)}, u32[]{:S(2)}, u32[]{:S(2)}) collective-permute-start(bf16[32,2304]{1,0:T(8,128)(2,1)S(1)} %get-tuple-element.81.refs_0_), channel_id=1, source_target_pairs={{0,2},{1,3},{2,0},{3,1},{4,6},{5,7},{6,4},{7,5},{8,10},{9,11},{10,... | collective-permute-start | bytes 442376 | tf_op jit(solution)/shard_map/ppermute | solution.py:25
  157.7 5.1 %collective-permute-start.29 = (bf16[32,2304]{1,0:T(8,128)(2,1)S(1)}, bf16[32,2304]{1,0:T(8,128)(2,1)S(1)}, u32[]{:S(2)}, u32[]{:S(2)}) collective-permute-start(bf16[32,2304]{1,0:T(8,128)(2,1)S(1)} %collective-permute-done.28.refs_2_), channel_id=1, source_target_pairs={{0,2},{1,3},{2,0},{3,1},{4,6},{5,7},{6,4},{7,5},{8,10},{9,11},{10,... | collective-permute-start | bytes 442376 | tf_op jit(solution)/shard_map/ppermute | solution.py:25
  158.4 22.6 %collective-permute-start.38 = (bf16[2,64,1024]{2,1,0:T(8,128)(2,1)S(1)}, bf16[2,64,1024]{2,1,0:T(8,128)(2,1)S(1)}, u32[]{:S(2)}, u32[]{:S(2)}) collective-permute-start(bf16[2,64,1024]{2,1,0:T(8,128)(2,1)S(1)} %get-tuple-element.74), channel_id=1, source_target_pairs={{0,8},{8,0},{16,24},{24,16},{1,9},{9,1},{17,25},{25,17},{2,10},{10... | collective-permute-start | bytes 786440 | tf_op jit(solution)/shard_map/ppermute | solution.py:25
  159.9 21.1 %collective-permute-start.39 = (bf16[2,64,1024]{2,1,0:T(8,128)(2,1)S(1)}, bf16[2,64,1024]{2,1,0:T(8,128)(2,1)S(1)}, u32[]{:S(2)}, u32[]{:S(2)}) collective-permute-start(bf16[2,64,1024]{2,1,0:T(8,128)(2,1)S(1)} %add_convert_fusion.3), channel_id=1, source_target_pairs={{0,16},{8,24},{16,0},{24,8},{1,17},{9,25},{17,1},{25,9},{2,18},{10... | collective-permute-start | bytes 786440 | tf_op jit(solution)/shard_map/ppermute | solution.py:25
  160.4 2.5 %collective-permute-start.32 = (bf16[32,2304]{1,0:T(8,128)(2,1)S(1)}, bf16[32,2304]{1,0:T(8,128)(2,1)S(1)}, u32[]{:S(2)}, u32[]{:S(2)}) collective-permute-start(bf16[32,2304]{1,0:T(8,128)(2,1)S(1)} %collective-permute-done.28.refs_2_), channel_id=1, source_target_pairs={{0,1},{1,0},{2,3},{3,2},{4,5},{5,4},{6,7},{7,6},{8,9},{9,8},{10,11... | collective-permute-start | bytes 442376 | tf_op jit(solution)/shard_map/ppermute | solution.py:25
  160.4 2.5 %collective-permute-start.31 = (bf16[32,2304]{1,0:T(8,128)(2,1)S(1)}, bf16[32,2304]{1,0:T(8,128)(2,1)S(1)}, u32[]{:S(2)}, u32[]{:S(2)}) collective-permute-start(bf16[32,2304]{1,0:T(8,128)(2,1)S(1)} %collective-permute-done.27.refs_1_), channel_id=1, source_target_pairs={{0,1},{1,0},{2,3},{3,2},{4,5},{5,4},{6,7},{7,6},{8,9},{9,8},{10,11... | collective-permute-start | bytes 442376 | tf_op jit(solution)/shard_map/ppermute | solution.py:25
  162.8 1.4 collective-permute-start.33
  170.7 15.3 %collective-permute-start.46 = (bf16[2,64,1024]{2,1,0:T(8,128)(2,1)S(1)}, bf16[2,64,1024]{2,1,0:T(8,128)(2,1)S(1)}, u32[]{:S(2)}, u32[]{:S(2)}) collective-permute-start(bf16[2,64,1024]{2,1,0:T(8,128)(2,1)S(1)} %get-tuple-element.99), channel_id=1, source_target_pairs={{0,16},{8,24},{16,0},{24,8},{1,17},{9,25},{17,1},{25,9},{2,18},{10... | collective-permute-start | bytes 786440 | tf_op jit(solution)/shard_map/ppermute | solution.py:25
  179.9 4.9 %collective-permute-start.36 = (f32[8,128]{1,0:T(8,128)S(1)}, f32[8,128]{1,0:T(8,128)S(1)}, u32[]{:S(2)}, u32[]{:S(2)}) collective-permute-start(f32[8,128]{1,0:T(8,128)S(1)} %broadcast_in_dim.11), channel_id=1, source_target_pairs={{0,8},{8,0},{16,24},{24,16},{1,9},{9,1},{17,25},{25,17},{2,10},{10... | collective-permute-start | bytes 12296 | tf_op jit(solution)/shard_map/ppermute | solution.py:25
  181.2 17.1 %collective-permute-start.45 = (bf16[2,64,1024]{2,1,0:T(8,128)(2,1)S(1)}, bf16[2,64,1024]{2,1,0:T(8,128)(2,1)S(1)}, u32[]{:S(2)}, u32[]{:S(2)}) collective-permute-start(bf16[2,64,1024]{2,1,0:T(8,128)(2,1)S(1)} %get-tuple-element.97), channel_id=1, source_target_pairs={{0,16},{8,24},{16,0},{24,8},{1,17},{9,25},{17,1},{25,9},{2,18},{10... | collective-permute-start | bytes 786440 | tf_op jit(solution)/shard_map/ppermute | solution.py:25
  182.7 19.8 %collective-permute-start.40 = (bf16[2,64,1024]{2,1,0:T(8,128)(2,1)S(1)}, bf16[2,64,1024]{2,1,0:T(8,128)(2,1)S(1)}, u32[]{:S(2)}, u32[]{:S(2)}) collective-permute-start(bf16[2,64,1024]{2,1,0:T(8,128)(2,1)S(1)} %get-tuple-element.92), channel_id=1, source_target_pairs={{0,8},{8,0},{16,24},{24,16},{1,9},{9,1},{17,25},{25,17},{2,10},{10... | collective-permute-start | bytes 786440 | tf_op jit(solution)/shard_map/ppermute | solution.py:25
  183.3 14.3 %collective-permute-start.41 = (bf16[2,64,1024]{2,1,0:T(8,128)(2,1)S(1)}, bf16[2,64,1024]{2,1,0:T(8,128)(2,1)S(1)}, u32[]{:S(2)}, u32[]{:S(2)}) collective-permute-start(bf16[2,64,1024]{2,1,0:T(8,128)(2,1)S(1)} %get-tuple-element.94), channel_id=1, source_target_pairs={{0,8},{8,0},{16,24},{24,16},{1,9},{9,1},{17,25},{25,17},{2,10},{10... | collective-permute-start | bytes 786440 | tf_op jit(solution)/shard_map/ppermute | solution.py:25
  185.4 3.7 %collective-permute-start.37 = (f32[8,128]{1,0:T(8,128)S(1)}, f32[8,128]{1,0:T(8,128)S(1)}, u32[]{:S(2)}, u32[]{:S(2)}) collective-permute-start(f32[8,128]{1,0:T(8,128)S(1)} %broadcast_add_fusion), channel_id=1, source_target_pairs={{0,16},{8,24},{16,0},{24,8},{1,17},{9,25},{17,1},{25,9},{2,18},{10... | collective-permute-start | bytes 12296 | tf_op jit(solution)/shard_map/ppermute | solution.py:25
  186.1 15.4 %collective-permute-start.47 = (bf16[2,64,1024]{2,1,0:T(8,128)(2,1)S(1)}, bf16[2,64,1024]{2,1,0:T(8,128)(2,1)S(1)}, u32[]{:S(2)}, u32[]{:S(2)}) collective-permute-start(bf16[2,64,1024]{2,1,0:T(8,128)(2,1)S(1)} %add_convert_fusion), channel_id=1, source_target_pairs={{0,8},{8,0},{16,24},{24,16},{1,9},{9,1},{17,25},{25,17},{2,10},{10... | collective-permute-start | bytes 786440 | tf_op jit(solution)/shard_map/ppermute | solution.py:25
  197.7 6.4 %collective-permute-start.42 = (bf16[2,64,1024]{2,1,0:T(8,128)(2,1)S(1)}, bf16[2,64,1024]{2,1,0:T(8,128)(2,1)S(1)}, u32[]{:S(2)}, u32[]{:S(2)}) collective-permute-start(bf16[2,64,1024]{2,1,0:T(8,128)(2,1)S(1)} %add_convert_fusion.1), channel_id=1, source_target_pairs={{0,16},{8,24},{16,0},{24,8},{1,17},{9,25},{17,1},{25,9},{2,18},{10... | collective-permute-start | bytes 786440 | tf_op jit(solution)/shard_map/ppermute | solution.py:25
  (31 other events, 216.8 us)

commit v3 on v0

v3 whole, which is shorter than its diff:
```python
from functools import partial

import jax
import jax.numpy as jnp
from jax import lax
from jax.experimental import pallas as pl
from jax.experimental.pallas import tpu as pltpu
from jax.sharding import PartitionSpec as P

BF16 = jnp.bfloat16
F32 = jnp.float32
WANTED_CHUNKS = 2
ROW_TILE = 16
IN_FLIGHT = 4
VMEM_BYTES = 44 << 20
ENCODE_VMEM_BYTES = 59 << 20
SMALL_COST = pl.CostEstimate(flops=1 << 20, bytes_accessed=1 << 10, transcendentals=0)
FAR = pl.BlockSpec(memory_space=pltpu.HBM)
ANYWHERE = pl.BlockSpec(memory_space=pl.ANY)
SCALARS = pl.BlockSpec(memory_space=pltpu.SMEM)
NEAR = pl.BlockSpec(memory_space=pltpu.VMEM)


def pick_tile(size, wanted):
    return wanted if size % wanted == 0 else size


def swap(x, axis, size, offset):
    return lax.ppermute(x, axis, [(i, i ^ offset) for i in range(size)])


def after(values, earlier):
    if not earlier:
        return list(values)
    return list(lax.optimization_barrier(list(values) + list(earlier)))[:len(values)]


class Plan:
    def __init__(self, resid, w_dec):
        self.sources, self.rows, self.model = resid.shape
        self.width = w_dec.shape[2]
        self.groups = lax.axis_size("grp")
        self.feats = lax.axis_size("feat")
        self.depth = self.feats // 2
        self.tokens = self.rows * self.groups
        self.rows_feat = self.tokens // self.feats
        self.per_group = self.rows // self.rows_feat
        self.pairs = self.per_group // 2
        self.chunks = WANTED_CHUNKS
        while self.rows_feat % (self.chunks * ROW_TILE):
            self.chunks -= 1
        self.piece = self.rows_feat // self.chunks
        self.block = self.per_group * self.piece
        self.chunk_rows = self.groups * self.block
        bits = [1 << i for i in range(self.groups.bit_length() - 1)]
        self.lanes = [bits[i:] + bits[:i] for i in range(len(bits))]
        starts = [i * self.sources // len(bits) for i in range(len(bits) + 1)]
        self.lane_sources = list(zip(starts[:-1], starts[1:]))
        self.level_bits = [1 << i for i in range(self.depth.bit_length() - 1)]

    def kept_order(self, lane):
        kept = [0]
        for bit in reversed(self.lanes[lane][1:]):
            kept = [j | bit for j in kept] + kept
        return kept


class Stream:
    def __init__(self, copies):
        self.copies = copies
        self.started = 0
        self.more(IN_FLIGHT)

    def more(self, count):
        for copy in self.copies[self.started:self.started + count]:
            copy.start()
        self.started += count

    def wait(self, i):
        self.copies[i].wait()
        self.more(1)


def call(kernel, name, in_specs, out_shape, scratch, args, vmem=VMEM_BYTES, **options):
    return pl.pallas_call(
        kernel,
        in_specs=in_specs,
        out_shape=out_shape,
        scratch_shapes=scratch,
        cost_estimate=SMALL_COST,
        compiler_params=pltpu.CompilerParams(vmem_limit_bytes=vmem),
        name=name,
        **options,
    )(*args)


def encode_kernel(plan, lane, resid_ref, w_ref, b_ref, *refs):
    outs, (x_buf, w_buf, b_buf, total, x_sem, w_sem) = refs[:-6], refs[-6:]
    lo, hi = plan.lane_sources[lane]
    depth = w_buf.shape[1] // (w_sem.shape[0] // (hi - lo))
    steps = plan.model // depth
    near = [
        pltpu.make_async_copy(resid_ref.at[pl.ds(lo, hi - lo)], x_buf, x_sem.at[0]),
        pltpu.make_async_copy(b_ref, b_buf, x_sem.at[1]),
    ]
    near[0].start()
    stream = Stream([
        pltpu.make_async_copy(
            w_ref.at[lo + s, pl.ds(i * depth, depth)],
            w_buf.at[s, pl.ds(i * depth, depth)],
            w_sem.at[s * steps + i],
        )
        for s in range(hi - lo)
        for i in range(steps)
    ])
    near[1].start()
    near[0].wait()
    for s in range(hi - lo):
        for i in range(steps):
            stream.wait(s * steps + i)
            part = slice(i * depth, (i + 1) * depth)
            product = jnp.dot(
                x_buf[s, :, part], w_buf[s, part, :], preferred_element_type=F32
            )
            if i:
                product = total[...] + product
            if i < steps - 1:
                total[...] = product
        if s == 0:
            near[1].wait()
        value = jnp.maximum(product + b_buf[lo + s:lo + s + 1, :], 0.0).astype(BF16)
        outs[-1][s] = value
        for c in range(plan.chunks):
            for b in range(plan.per_group):
                first = (b * plan.chunks + c) * plan.piece
                outs[c][s, b * plan.piece:(b + 1) * plan.piece, :] = (
                    value[first:first + plan.piece]
                )


def encode(plan, lane, resid, w_enc, b_enc):
    lo, hi = plan.lane_sources[lane]
    n = hi - lo
    steps = plan.model // pick_tile(plan.model, 768)
    out_shape = [jax.ShapeDtypeStruct((n, plan.block, plan.width), BF16)] * plan.chunks
    out_shape.append(jax.ShapeDtypeStruct((n, plan.rows, plan.width), BF16))
    return call(
        partial(encode_kernel, plan, lane),
        "encode",
        [FAR, FAR, FAR],
        out_shape,
        [
            pltpu.VMEM((n, plan.rows, plan.model), BF16),
            pltpu.VMEM((n, plan.model, plan.width), BF16),
            pltpu.VMEM((plan.sources, plan.width), F32),
            pltpu.VMEM((plan.rows, plan.width), F32),
            pltpu.SemaphoreType.DMA((2,)),
            pltpu.SemaphoreType.DMA((n * steps,)),
        ],
        (resid, w_enc, b_enc),
        vmem=ENCODE_VMEM_BYTES,
    )


def decode_kernel(plan, index_ref, *refs):
    n_in = plan.groups * len(plan.lanes)
    pieces, w_ref = refs[:n_in], refs[n_in]
    send_ref, keeps = refs[n_in + 1], refs[n_in + 2:-5]
    x_buf, w_buf, total, x_sem, w_sem = refs[-5:]
    half = plan.chunk_rows // 2
    core = index_ref[0]
    depth = pick_tile(plan.width, 256)
    steps = plan.width // depth

    placing = []
    for lane, (lo, hi) in enumerate(plan.lane_sources):
        for j in range(plan.groups):
            for b in range(plan.pairs):
                place = index_ref[1 + plan.sources + j * plan.pairs + b] * plan.piece
                for owner in range(2):
                    to = pl.multiple_of(place + jnp.where(core == owner, half, 0), ROW_TILE)
                    placing.append(pltpu.make_async_copy(
                        pieces[lane * plan.groups + j].at[
                            :, pl.ds((2 * b + owner) * plan.piece, plan.piece)
                        ],
                        x_buf.at[pl.ds(lo, hi - lo), pl.ds(to, plan.piece)],
                        x_sem.at[len(placing)],
                    ))
    for copy in placing:
        copy.start()
    stream = Stream([
        pltpu.make_async_copy(
            w_ref.at[s, 0, pl.ds(i * depth, depth)],
            w_buf.at[s, pl.ds(i * depth, depth)],
            w_sem.at[s * steps + i],
        )
        for s in range(plan.sources)
        for i in range(steps)
    ])
    for copy in placing:
        copy.wait()
    for s in range(plan.sources):
        @pl.when(index_ref[1 + s] == 0)
        def _(s=s):
            x_buf[s] = jnp.zeros(x_buf.shape[1:], BF16)

    for s in range(plan.sources):
        for i in range(steps):
            stream.wait(s * steps + i)
            part = slice(i * depth, (i + 1) * depth)
            product = jnp.dot(
                x_buf[s, :, part], w_buf[s, part, :], preferred_element_type=F32
            )
            if s + i:
                product = total[...] + product
            if s * steps + i < plan.sources * steps - 1:
                total[...] = product
    send_ref[...] = product[:half].astype(BF16)
    for d in range(plan.depth):
        keeps[d][...] = product[half + d * plan.piece:half + (d + 1) * plan.piece]


def decode(plan, index, pieces, w_dec):
    half = plan.chunk_rows // 2
    steps = plan.width // pick_tile(plan.width, 256)
    outs = call(
        partial(decode_kernel, plan),
        "decode",
        [SCALARS] + [ANYWHERE] * len(pieces) + [FAR],
        [jax.ShapeDtypeStruct((half, plan.model), BF16)]
        + [jax.ShapeDtypeStruct((plan.piece, plan.model), F32)] * plan.depth,
        [
            pltpu.VMEM((plan.sources, plan.chunk_rows, plan.width), BF16),
            pltpu.VMEM((plan.sources, plan.width, plan.model), BF16),
            pltpu.VMEM((plan.chunk_rows, plan.model), F32),
            pltpu.SemaphoreType.DMA((len(pieces) * plan.per_group,)),
            pltpu.SemaphoreType.DMA((plan.sources * steps,)),
        ],
        (index, *pieces, w_dec),
    )
    return outs[0], outs[1:]


def gradient_kernel(plan, lane, index_ref, *refs):
    n_in = 2 * plan.depth
    errors, w_ref, outs = refs[:n_in], refs[n_in], refs[n_in + 1:-4]
    e_buf, w_buf, e_sem, w_sem = refs[-4:]
    lo, hi = plan.lane_sources[lane]
    first, kept = plan.lanes[lane][0], plan.kept_order(lane)
    base = 1 + plan.sources + plan.groups * plan.pairs
    depth = pick_tile(plan.width, 512)
    steps = plan.width // depth

    placing = [
        pltpu.make_async_copy(
            errors[i],
            e_buf.at[
                pl.ds(pl.multiple_of(index_ref[base + i] * plan.piece, ROW_TILE), plan.piece)
            ],
            e_sem.at[i],
        )
        for i in range(n_in)
    ]
    for copy in placing:
        copy.start()
    stream = Stream([
        pltpu.make_async_copy(
            w_ref.at[lo + s, 0, pl.ds(i * depth, depth)],
            w_buf.at[s, pl.ds(i * depth, depth)],
            w_sem.at[s * steps + i],
        )
        for s in range(hi - lo)
        for i in range(steps)
    ])
    for copy in placing:
        copy.wait()
    if lane == 0:
        total = jnp.zeros((8, 128), F32)
        for row in range(0, plan.chunk_rows, ROW_TILE):
            value = e_buf[row:row + ROW_TILE, :].astype(F32)
            value = value * value
            value = value[:8] + value[8:]
            for col in range(0, plan.model, 128):
                total = total + value[:, col:col + 128]
        outs[-1][...] = total

    n = len(kept)
    for s in range(hi - lo):
        feeds = index_ref[1 + lo + s] > 0
        for i in range(steps):
            stream.wait(s * steps + i)
            part = slice(i * depth, (i + 1) * depth)
            product = lax.dot_general(
                w_buf[s, part, :], e_buf[...], (((1,), (1,)), ((), ())),
                preferred_element_type=F32,
            ).T
            product = jnp.where(feeds, product, 0.0)
            for p, j in enumerate(kept):
                away = (j ^ first) * plan.block
                outs[p][s, :, part] = product[away:away + plan.block].astype(BF16)
                outs[n + p][s, :, part] = product[j * plan.block:(j + 1) * plan.block]


def gradient(plan, lane, index, errors, w_dec):
    lo, hi = plan.lane_sources[lane]
    n = hi - lo
    steps = plan.width // pick_tile(plan.width, 512)
    half = plan.groups // 2
    shape = (n, plan.block, plan.width)
    out_shape = [jax.ShapeDtypeStruct(shape, BF16)] * half
    out_shape += [jax.ShapeDtypeStruct(shape, F32)] * half
    if lane == 0:
        out_shape.append(jax.ShapeDtypeStruct((8, 128), F32))
    outs = call(
        partial(gradient_kernel, plan, lane),
        "gradient",
        [SCALARS] + [ANYWHERE] * len(errors) + [FAR],
        out_shape,
        [
            pltpu.VMEM((plan.chunk_rows, plan.model), BF16),
            pltpu.VMEM((n, plan.width, plan.model), BF16),
            pltpu.SemaphoreType.DMA((len(errors),)),
            pltpu.SemaphoreType.DMA((n * steps,)),
        ],
        (index, *errors, w_dec),
    )
    return outs[:half], outs[half:2 * half], outs[2 * half:]


def finish_kernel(plan, chunk, with_previous, *refs):
    lanes = len(plan.lanes)
    kept, got = refs[:lanes], refs[lanes:2 * lanes]
    out_ref, stage, sem = refs[-3:]
    for lane, (lo, hi) in enumerate(plan.lane_sources):
        for s in range(lo, hi):
            stage[:, s, :] = kept[lane][s - lo] + got[lane][s - lo].astype(F32)
    copies = [
        pltpu.make_async_copy(
            stage.at[pl.ds(b * plan.piece, plan.piece)],
            out_ref.at[pl.ds((b * plan.chunks + chunk) * plan.piece, plan.piece)],
            sem.at[b],
        )
        for b in range(plan.per_group)
    ]
    for copy in copies:
        copy.start()
    for copy in copies:
        copy.wait()


def finish(plan, chunk, kept, got, previous):
    options = {}
    if previous is not None:
        options["input_output_aliases"] = {2 * len(kept): 0}
    previous = [] if previous is None else [previous]
    return call(
        partial(finish_kernel, plan, chunk, bool(previous)),
        "finish",
        [NEAR] * (2 * len(kept)) + [FAR] * len(previous),
        jax.ShapeDtypeStruct((plan.rows, plan.sources, plan.width), F32),
        [
            pltpu.VMEM((plan.block, plan.sources, plan.width), F32),
            pltpu.SemaphoreType.DMA((plan.per_group,)),
        ],
        (*kept, *got, *previous),
        out_specs=FAR,
        **options,
    )


def per_device(resid, w_enc, b_enc, w_dec, targets, start_layer):
    plan = Plan(resid, w_dec)
    group = lax.axis_index("grp").astype(jnp.int32)
    feat = lax.axis_index("feat").astype(jnp.int32)
    core, level = feat % 2, feat // 2
    groups, feats, chunks = plan.groups, plan.feats, plan.chunks

    feeds = (group >= start_layer[:, 0]).astype(jnp.int32)
    offsets = [
        ((group ^ j) * plan.pairs + b) ^ level
        for j in range(groups)
        for b in range(plan.pairs)
    ]
    places = []
    for other in range(2):
        for d in range(plan.depth):
            owner = level ^ d
            place = ((owner // plan.pairs) ^ group) * plan.pairs + owner % plan.pairs
            places.append(place * 2 + (core ^ other))
    index = jnp.concatenate([core[None], feeds, jnp.stack(offsets), jnp.stack(places)])

    encoded = [encode(plan, i, resid, w_enc, b_enc) for i in range(len(plan.lanes))]
    active = jnp.stack(
        [e[-1][s] for e in encoded for s in range(e[-1].shape[0])], axis=1
    )

    gathered, arrivals = [], []
    earlier = []
    for c in range(chunks):
        own = after([e[c] for e in encoded], earlier)
        pieces, first_arrivals = [], []
        for lane, bits in enumerate(plan.lanes):
            held = {0: own[lane]}
            for bit in bits:
                held.update(
                    {j | bit: swap(x, "grp", groups, bit) for j, x in list(held.items())}
                )
            pieces += [held[j] for j in range(groups)]
            first_arrivals += [held[bit] for bit in bits]
        gathered.append(pieces)
        arrivals.append(first_arrivals)
        earlier = [first_arrivals[0]]

    recon_parts = []
    squares = jnp.zeros((8, 128), F32)
    before_decode, before_gradient, after_gradient = [], [], []
    unfinished = []
    pending = None

    def exchange_errors(state, earlier):
        c, recon_rows = state
        recon_rows, = after([recon_rows], earlier)
        first = feat * plan.rows_feat + c * plan.piece
        own_targets = lax.dynamic_slice_in_dim(targets[0], first, plan.piece, 0)
        difference = recon_rows - own_targets.astype(F32)
        recon_parts.append(recon_rows.astype(BF16))
        error = difference.astype(BF16)
        held = {0: error}
        for bit in reversed(plan.level_bits):
            held.update(
                {d | bit: swap(x, "feat", feats, 2 * bit) for d, x in list(held.items())}
            )
        errors = [held[d] for d in range(plan.depth)]
        return error, errors + [swap(e, "feat", feats, 1) for e in errors]

    def exchange_gradients(errors):
        nonlocal squares, before_gradient, after_gradient
        errors = after(errors, before_gradient)
        before_gradient, after_gradient = [], []
        kept_all, got_all = [], []
        for lane, bits in enumerate(plan.lanes):
            away, kept, extra = gradient(plan, lane, index, errors, w_dec)
            after_gradient += away
            if extra:
                squares = squares + extra[0]
            for step, bit in enumerate(bits):
                got = [swap(x, "grp", groups, bit) for x in away]
                cut = len(got) // 2
                if cut:
                    total = [x + y.astype(F32) for x, y in zip(kept, got)]
                    away = [x.astype(BF16) for x in total[:cut]]
                    before_gradient += away
                    kept = total[cut:]
            kept_all.append(kept[0])
            got_all.append(got[0])
        unfinished.append((kept_all, got_all))

    for c in range(chunks):
        pieces = after(gathered[c], before_decode)
        send, keeps = decode(plan, index, pieces, w_dec)
        ready = []
        if c + 1 < chunks:
            send, = after([send], arrivals[c + 1])
        if pending is not None:
            error, errors = exchange_errors(pending, [send])
            ready = [error]
        other = swap(send, "feat", feats, 1)
        other, = after([other], ready)
        held = {
            d: keeps[d] + other[d * plan.piece:(d + 1) * plan.piece].astype(F32)
            for d in range(plan.depth)
        }
        for bit in plan.level_bits:
            sends = {d: held.pop(d).astype(BF16) for d in sorted(held) if d & bit}
            before_decode = list(sends.values())
            for d in sorted(sends, reverse=True):
                arrived = swap(sends[d], "feat", feats, 2 * bit)
                held[d ^ bit] = held[d ^ bit] + arrived.astype(F32)
        if pending is not None:
            exchange_gradients(errors)
        pending = (c, held[0])
    error, errors = exchange_errors(pending, after_gradient)
    exchange_gradients(errors)

    feat_grad = None
    for c, (kept, got) in enumerate(unfinished):
        if c + 1 < chunks:
            tied = after(kept + got, after_gradient)
            kept, got = tied[:len(kept)], tied[len(kept):]
        feat_grad = finish(plan, c, kept, got, feat_grad)

    loss = jnp.full((8, 128), jnp.sum(squares), F32)
    for bit in (1 << i for i in range(groups.bit_length() - 1)):
        loss = loss + swap(loss, "grp", groups, bit)
    entries = targets.shape[0] * groups * plan.tokens * plan.model
    recon_loss = loss[0, 0] / entries
    recon = jnp.concatenate(recon_parts, axis=0)[None]
    return active, recon, recon_loss, feat_grad


def solution(mesh):
    in_specs = (
        P(None, "grp", None),
        P(None, None, "feat"),
        P(None, "feat"),
        P(None, "grp", "feat", None),
        P("grp", None, None),
        P(None, "feat"),
    )
    out_specs = (P("grp", None, "feat"), P("grp", "feat", None), P(), P("grp", None, "feat"))
    return jax.shard_map(
        per_device, mesh=mesh, in_specs=in_specs, out_specs=out_specs, check_vma=False
    )
```

time: 323 us -> 195 us (0.60)
  waiting for transfers between devices: 183 us -> 53.2 us
  Pallas kernels: 0 us -> 75.5 us
  matrix products: 66.5 us -> 0 us
  starting transfers between devices: 0.34 us -> 45.8 us
  blocking collectives: 40.3 us -> 0 us
  between operations: 15.7 us -> 2.83 us
    reduce_scatter x2 -> x0, waiting for transfers between devices: 98 us -> none  [the longest x1 55 us: per_device(): lax.psum_scatter(partial_sums, 'feat', scatter_dimension=1, tiled=True)]
    all_gather x2 -> x0, waiting for transfers between devices: 84.7 us -> none  [the longest x1 54.8 us: per_device(): piece_rows = lax.all_gather(active, 'grp', axis=0, tiled=True)]
    pallas_call x0 -> x10, Pallas kernels: none -> 75.5 us  [call(): pl.pallas_call(kernel, in_specs=in_specs, out_shape=out_shape, scratch_sh...]
    dot_general x12 -> x0, matrix products: 66.5 us -> none  [the longest x8 53.8 us: masked(): return feeds_value[source, target] * product()]
    ppermute x0 -> x48, waiting for transfers between devices: none -> 53.2 us  [swap(): return lax.ppermute(x, axis, [(i, i ^ offset) for i in range(size)])]
    ppermute x0 -> x48, starting transfers between devices: none -> 45.8 us  [swap(): return lax.ppermute(x, axis, [(i, i ^ offset) for i in range(size)])]
    psum x1 -> x0, blocking collectives: 40.3 us -> none  [per_device(): recon_loss = lax.psum(squares, ('grp', 'feat')) / entries]
    another operation x2 -> x1, other arithmetic: 4.77 us -> 0.13 us  [per_device(): jnp.stack([e[-1][s] for e in encoded for s in range(e[-1].shape[0])], axi...]
  transfers between devices with their start and end apart: 4 -> 48, of which waited for: 4 -> 16; matrix products, arithmetic and copies ran while one was open for 1% -> 6% of each run, Pallas kernels for 0% -> 35%
where the time goes in v3:
time: 195 us
  Pallas kernels  75.5 us (39%)
  waiting for transfers between devices  53.2 us (27%)
  starting transfers between devices  45.8 us (23%)
  other arithmetic  10.4 us (5%)
  local copies, waits for them, and re-layouts  7.39 us (4%)
  between operations  2.83 us (1%)
    pallas_call x10, Pallas kernels, call(): pl.pallas_call(kernel, in_specs=in_specs, out_shape=out_shape, scratch_sh...  75.5 us
    ppermute x48, waiting for transfers between devices, swap(): return lax.ppermute(x, axis, [(i, i ^ offset) for i in range(size)])  53.2 us
    ppermute x48, starting transfers between devices, swap(): return lax.ppermute(x, axis, [(i, i ^ offset) for i in range(size)])  45.8 us
    unnamed x25, local copies, waits for them, and re-layouts  6.07 us
  transfers between devices with their start and end apart: 48, of which 16 were waited for; matrix products, arithmetic and copies ran while one was open for 6% of the time, Pallas kernels for 35%

profile of v3, /device:TPU:0, one launch (start us, length us, event | category | flops | bytes accessed | tf_op | source)
XLA Modules:
  0.0 195.1 jit_solution(11161969951616082041)
XLA Ops:
  0.6 5.7 %encode.3 = (bf16[2,64,1024]{2,1,0:T(8,128)(2,1)}, bf16[2,64,1024]{2,1,0:T(8,128)(2,1)}, bf16[2,128,1024]{2,1,0:T(8,128)(2,1)}) custom-call(bf16[4,128,2304]{2,1,0:T(8,128)(2,1)} %resid_ref.3, bf16[4,2304,1024]{2,1,0:T(8,128)(2,1)} %w_ref.3, f32[4,1024]{1,0:T(4,128)} %b_ref.3), custom_call_target="tpu_custom_call" | custom-call | flops 1048576 | bytes 1024 | tf_op jit(solution)/shard_map/encode/pallas_call | solution.py:85
  6.4 3.0 %collective-permute-start.4 = (bf16[2,64,1024]{2,1,0:T(8,128)(2,1)}, bf16[2,64,1024]{2,1,0:T(8,128)(2,1)S(1)}, u32[]{:S(2)}, u32[]{:S(2)}) collective-permute-start(bf16[2,64,1024]{2,1,0:T(8,128)(2,1)} %get-tuple-element.67.refs_4_), channel_id=1, source_target_pairs={{0,16},{8,24},{16,0},{24,8},{1,17},{9,25},{17,1},{25,9},{2,18},{10... | collective-permute-start | bytes 786440 | tf_op jit(solution)/shard_map/ppermute | solution.py:29
  9.4 5.8 %encode.2 = (bf16[2,64,1024]{2,1,0:T(8,128)(2,1)}, bf16[2,64,1024]{2,1,0:T(8,128)(2,1)}, bf16[2,128,1024]{2,1,0:T(8,128)(2,1)}) custom-call(bf16[4,128,2304]{2,1,0:T(8,128)(2,1)} %resid_ref.3, bf16[4,2304,1024]{2,1,0:T(8,128)(2,1)} %w_ref.3, f32[4,1024]{1,0:T(4,128)} %b_ref.3), custom_call_target="tpu_custom_call" | custom-call | flops 1048576 | bytes 1024 | tf_op jit(solution)/shard_map/encode/pallas_call | solution.py:85
  15.2 1.6 collective-permute-start
  17.4 1.9 collective-permute-start.5
  19.3 5.4 %collective-permute-done.refs_1_ = bf16[2,64,1024]{2,1,0:T(8,128)(2,1)S(1)} collective-permute-done((bf16[2,64,1024]{2,1,0:T(8,128)(2,1)}, bf16[2,64,1024]{2,1,0:T(8,128)(2,1)S(1)}, u32[]{:S(2)}, u32[]{:S(2)}) %collective-permute-start) | collective-permute-done | bytes 262176 | tf_op jit(solution)/shard_map/ppermute | solution.py:29
  24.7 2.0 %collective-permute-start.7 = (bf16[2,64,1024]{2,1,0:T(8,128)(2,1)}, bf16[2,64,1024]{2,1,0:T(8,128)(2,1)S(1)}, u32[]{:S(2)}, u32[]{:S(2)}) collective-permute-start(bf16[2,64,1024]{2,1,0:T(8,128)(2,1)} %get-tuple-element.78.refs_0_), channel_id=1, source_target_pairs={{0,16},{8,24},{16,0},{24,8},{1,17},{9,25},{17,1},{25,9},{2,18},{10... | collective-permute-start | bytes 786440 | tf_op jit(solution)/shard_map/ppermute | solution.py:29
  26.7 3.6 %collective-permute-done.3.refs_5_ = bf16[2,64,1024]{2,1,0:T(8,128)(2,1)S(1)} collective-permute-done((bf16[2,64,1024]{2,1,0:T(8,128)(2,1)S(1)}, bf16[2,64,1024]{2,1,0:T(8,128)(2,1)S(1)}, u32[]{:S(2)}, u32[]{:S(2)}) %collective-permute-start.3) | collective-permute-done | bytes 262176 | tf_op jit(solution)/shard_map/ppermute | solution.py:29
  30.3 1.5 collective-permute-start.6
  32.3 3.6 %collective-permute-done.5.refs_7_ = bf16[2,64,1024]{2,1,0:T(8,128)(2,1)S(1)} collective-permute-done((bf16[2,64,1024]{2,1,0:T(8,128)(2,1)S(1)}, bf16[2,64,1024]{2,1,0:T(8,128)(2,1)S(1)}, u32[]{:S(2)}, u32[]{:S(2)}) %collective-permute-start.5) | collective-permute-done | bytes 262176 | tf_op jit(solution)/shard_map/ppermute | solution.py:29
  40.3 11.0 %decode.2 = (bf16[128,2304]{1,0:T(8,128)(2,1)S(1)}, f32[32,2304]{1,0:T(8,128)S(1)}, f32[32,2304]{1,0:T(8,128)S(1)}, f32[32,2304]{1,0:T(8,128)S(1)}, f32[32,2304]{1,0:T(8,128)S(1)}) custom-call(s32[17]{0:T(128)S(1)} %concatenate.6.index_ref, bf16[2,64,1024]{2,1,0:T(8,128)(2,1)S(1)} %copy-done.3, bf16[2,64,1024]{2,1,0:T(8,128)(2,1)S(1)} %collective-permute-done.refs_1_, ...), custom_call_target="tpu_custom_call" | custom-call | flops 1048576 | bytes 1024 | tf_op jit(solution)/shard_map/decode/pallas_call | solution.py:85
  51.5 2.0 %collective-permute-done.10 = bf16[128,2304]{1,0:T(8,128)(2,1)S(1)} collective-permute-done((bf16[128,2304]{1,0:T(8,128)(2,1)S(1)}, bf16[128,2304]{1,0:T(8,128)(2,1)S(1)}, u32[]{:S(2)}, u32[]{:S(2)}) %collective-permute-start.10) | collective-permute-done | bytes 589856 | tf_op jit(solution)/shard_map/ppermute | solution.py:29
  54.3 2.1 %collective-permute-start.12 = (bf16[32,2304]{1,0:T(8,128)(2,1)S(1)}, bf16[32,2304]{1,0:T(8,128)(2,1)S(1)}, u32[]{:S(2)}, u32[]{:S(2)}) collective-permute-start(bf16[32,2304]{1,0:T(8,128)(2,1)S(1)} %get-tuple-element.131), channel_id=1, source_target_pairs={{0,2},{1,3},{2,0},{3,1},{4,6},{5,7},{6,4},{7,5},{8,10},{9,11},{10,... | collective-permute-start | bytes 442376 | tf_op jit(solution)/shard_map/ppermute | solution.py:29
  56.3 1.5 collective-permute-start.14
  57.9 1.5 collective-permute-start.15
  61.2 2.7 %collective-permute-start.13 = (bf16[32,2304]{1,0:T(8,128)(2,1)}, bf16[32,2304]{1,0:T(8,128)(2,1)}, u32[]{:S(2)}, u32[]{:S(2)}) collective-permute-start(bf16[32,2304]{1,0:T(8,128)(2,1)} %add_convert_fusion.7), channel_id=1, source_target_pairs={{0,4},{1,5},{2,6},{3,7},{4,0},{5,1},{6,2},{7,3},{8,12},{9,13},{10,... | collective-permute-start | bytes 442376 | tf_op jit(solution)/shard_map/ppermute | solution.py:29
  64.4 1.2 collective-permute-done.15.refs_7_
  65.6 11.0 %decode.3 = (bf16[128,2304]{1,0:T(8,128)(2,1)S(1)}, f32[32,2304]{1,0:T(8,128)S(1)}, f32[32,2304]{1,0:T(8,128)S(1)}, f32[32,2304]{1,0:T(8,128)S(1)}, f32[32,2304]{1,0:T(8,128)S(1)}) custom-call(s32[17]{0:T(128)S(1)} %concatenate.6.index_ref, bf16[2,64,1024]{2,1,0:T(8,128)(2,1)S(1)} %copy-done.1, bf16[2,64,1024]{2,1,0:T(8,128)(2,1)S(1)} %collective-permute-done.6.refs_1_, ...), custom_call_target="tpu_custom_call" | custom-call | flops 1048576 | bytes 1024 | tf_op jit(solution)/shard_map/decode/pallas_call | solution.py:85
  76.8 1.2 convert_add_fusion.5
  78.0 1.0 fusion.3
  78.9 2.7 %collective-permute-start.21 = (bf16[32,2304]{1,0:T(8,128)(2,1)S(1)}, bf16[32,2304]{1,0:T(8,128)(2,1)S(1)}, u32[]{:S(2)}, u32[]{:S(2)}) collective-permute-start(bf16[32,2304]{1,0:T(8,128)(2,1)S(1)} %get-tuple-element.139.refs_0_), channel_id=1, source_target_pairs={{0,4},{1,5},{2,6},{3,7},{4,0},{5,1},{6,2},{7,3},{8,12},{9,13},{10,... | collective-permute-start | bytes 442376 | tf_op jit(solution)/shard_map/ppermute | solution.py:29
  82.0 7.2 %collective-permute-done.21.refs_2_ = bf16[32,2304]{1,0:T(8,128)(2,1)S(1)} collective-permute-done((bf16[32,2304]{1,0:T(8,128)(2,1)S(1)}, bf16[32,2304]{1,0:T(8,128)(2,1)S(1)}, u32[]{:S(2)}, u32[]{:S(2)}) %collective-permute-start.21) | collective-permute-done | bytes 147488 | tf_op jit(solution)/shard_map/ppermute | solution.py:29
  90.0 2.0 %collective-permute-start.18 = (bf16[32,2304]{1,0:T(8,128)(2,1)S(1)}, bf16[32,2304]{1,0:T(8,128)(2,1)S(1)}, u32[]{:S(2)}, u32[]{:S(2)}) collective-permute-start(bf16[32,2304]{1,0:T(8,128)(2,1)S(1)} %get-tuple-element.129), channel_id=1, source_target_pairs={{0,2},{1,3},{2,0},{3,1},{4,6},{5,7},{6,4},{7,5},{8,10},{9,11},{10,... | collective-permute-start | bytes 442376 | tf_op jit(solution)/shard_map/ppermute | solution.py:29
  92.7 3.3 %collective-permute-done.22.refs_3_ = bf16[32,2304]{1,0:T(8,128)(2,1)S(1)} collective-permute-done((bf16[32,2304]{1,0:T(8,128)(2,1)S(1)}, bf16[32,2304]{1,0:T(8,128)(2,1)S(1)}, u32[]{:S(2)}, u32[]{:S(2)}) %collective-permute-start.22) | collective-permute-done | bytes 147488 | tf_op jit(solution)/shard_map/ppermute | solution.py:29
  96.0 2.2 %collective-permute-done.18 = bf16[32,2304]{1,0:T(8,128)(2,1)S(1)} collective-permute-done((bf16[32,2304]{1,0:T(8,128)(2,1)S(1)}, bf16[32,2304]{1,0:T(8,128)(2,1)S(1)}, u32[]{:S(2)}, u32[]{:S(2)}) %collective-permute-start.18) | collective-permute-done | bytes 147488 | tf_op jit(solution)/shard_map/ppermute | solution.py:29
  99.2 2.5 %collective-permute-start.19 = (bf16[32,2304]{1,0:T(8,128)(2,1)}, bf16[32,2304]{1,0:T(8,128)(2,1)}, u32[]{:S(2)}, u32[]{:S(2)}) collective-permute-start(bf16[32,2304]{1,0:T(8,128)(2,1)} %add_convert_fusion.4), channel_id=1, source_target_pairs={{0,4},{1,5},{2,6},{3,7},{4,0},{5,1},{6,2},{7,3},{8,12},{9,13},{10,... | collective-permute-start | bytes 442376 | tf_op jit(solution)/shard_map/ppermute | solution.py:29
  101.9 1.8 copy.11
  103.6 10.0 %gradient.5 = (bf16[2,64,1024]{2,1,0:T(8,128)(2,1)S(1)}, bf16[2,64,1024]{2,1,0:T(8,128)(2,1)S(1)}, f32[2,64,1024]{2,1,0:T(8,128)S(1)}, f32[2,64,1024]{2,1,0:T(8,128)S(1)}) custom-call(s32[17]{0:T(128)S(1)} %concatenate.6.index_ref, bf16[32,2304]{1,0:T(8,128)(2,1)S(1)} %get-tuple-element.139.refs_0_, bf16[32,2304]{1,0:T(8,128)(2,1)S(1)} %collective-permute-done.20.refs_1_, ...), custom_call_target="tpu_custom_call" | custom-call | flops 1048576 | bytes 1024 | tf_op jit(solution)/shard_map/gradient/pallas_call | solution.py:85
  114.2 1.6 collective-permute-start.45
  115.8 9.8 %gradient.4 = (bf16[2,64,1024]{2,1,0:T(8,128)(2,1)S(1)}, bf16[2,64,1024]{2,1,0:T(8,128)(2,1)S(1)}, f32[2,64,1024]{2,1,0:T(8,128)S(1)}, f32[2,64,1024]{2,1,0:T(8,128)S(1)}, f32[8,128]{1,0:T(8,128)S(1)}) custom-call(s32[17]{0:T(128)S(1)} %concatenate.6.index_ref, bf16[32,2304]{1,0:T(8,128)(2,1)S(1)} %get-tuple-element.139.refs_0_, ...), custom_call_target="tpu_custom_call" | custom-call | flops 1048576 | bytes 1024 | tf_op jit(solution)/shard_map/gradient/pallas_call | solution.py:85
  125.6 1.6 collective-permute-start.34
  127.7 1.0 convert_add_fusion.4
  130.2 1.8 collective-permute-start.27
  132.1 5.1 %collective-permute-done.28.refs_2_ = bf16[32,2304]{1,0:T(8,128)(2,1)S(1)} collective-permute-done((bf16[32,2304]{1,0:T(8,128)(2,1)S(1)}, bf16[32,2304]{1,0:T(8,128)(2,1)S(1)}, u32[]{:S(2)}, u32[]{:S(2)}) %collective-permute-start.28) | collective-permute-done | bytes 147488 | tf_op jit(solution)/shard_map/ppermute | solution.py:29
  137.9 4.4 %collective-permute-done.29.refs_3_ = bf16[32,2304]{1,0:T(8,128)(2,1)S(1)} collective-permute-done((bf16[32,2304]{1,0:T(8,128)(2,1)S(1)}, bf16[32,2304]{1,0:T(8,128)(2,1)S(1)}, u32[]{:S(2)}, u32[]{:S(2)}) %collective-permute-start.29) | collective-permute-done | bytes 147488 | tf_op jit(solution)/shard_map/ppermute | solution.py:29
  142.4 1.6 collective-permute-start.47
  144.4 9.8 %gradient.6 = (bf16[2,64,1024]{2,1,0:T(8,128)(2,1)S(1)}, bf16[2,64,1024]{2,1,0:T(8,128)(2,1)S(1)}, f32[2,64,1024]{2,1,0:T(8,128)S(1)}, f32[2,64,1024]{2,1,0:T(8,128)S(1)}, f32[8,128]{1,0:T(8,128)S(1)}) custom-call(s32[17]{0:T(128)S(1)} %concatenate.6.index_ref, bf16[32,2304]{1,0:T(8,128)(2,1)S(1)} %get-tuple-element.101.refs_0_, ...), custom_call_target="tpu_custom_call" | custom-call | flops 1048576 | bytes 1024 | tf_op jit(solution)/shard_map/gradient/pallas_call | solution.py:85
  156.4 10.1 %gradient.7 = (bf16[2,64,1024]{2,1,0:T(8,128)(2,1)S(1)}, bf16[2,64,1024]{2,1,0:T(8,128)(2,1)S(1)}, f32[2,64,1024]{2,1,0:T(8,128)S(1)}, f32[2,64,1024]{2,1,0:T(8,128)S(1)}) custom-call(s32[17]{0:T(128)S(1)} %concatenate.6.index_ref, bf16[32,2304]{1,0:T(8,128)(2,1)S(1)} %get-tuple-element.101.refs_0_, bf16[32,2304]{1,0:T(8,128)(2,1)S(1)} %collective-permute-done.27.refs_1_, ...), custom_call_target="tpu_custom_call" | custom-call | flops 1048576 | bytes 1024 | tf_op jit(solution)/shard_map/gradient/pallas_call | solution.py:85
  166.4 1.4 collective-permute-start.42
  170.0 1.4 collective-permute-start.39
  171.3 1.5 collective-permute-start.38
  173.4 1.2 finish.2.refs_4_
  174.6 1.2 collective-permute-done.37
  177.7 1.4 collective-permute-start.43
  179.1 7.2 %collective-permute-done.40 = bf16[2,64,1024]{2,1,0:T(8,128)(2,1)S(1)} collective-permute-done((bf16[2,64,1024]{2,1,0:T(8,128)(2,1)S(1)}, bf16[2,64,1024]{2,1,0:T(8,128)(2,1)S(1)}, u32[]{:S(2)}, u32[]{:S(2)}) %collective-permute-start.40) | collective-permute-done | bytes 262176 | tf_op jit(solution)/shard_map/ppermute | solution.py:29
  187.2 2.5 %collective-permute-done.43.refs_3_ = bf16[2,64,1024]{2,1,0:T(8,128)(2,1)S(1)} collective-permute-done((bf16[2,64,1024]{2,1,0:T(8,128)(2,1)S(1)}, bf16[2,64,1024]{2,1,0:T(8,128)(2,1)S(1)}, u32[]{:S(2)}, u32[]{:S(2)}) %collective-permute-start.43) | collective-permute-done | bytes 262176 | tf_op jit(solution)/shard_map/ppermute | solution.py:29
  189.6 3.1 %collective-permute-done.41.refs_2_ = bf16[2,64,1024]{2,1,0:T(8,128)(2,1)S(1)} collective-permute-done((bf16[2,64,1024]{2,1,0:T(8,128)(2,1)S(1)}, bf16[2,64,1024]{2,1,0:T(8,128)(2,1)S(1)}, u32[]{:S(2)}, u32[]{:S(2)}) %collective-permute-start.41) | collective-permute-done | bytes 262176 | tf_op jit(solution)/shard_map/ppermute | solution.py:29
  192.7 1.2 finish.3
  (110 shorter events, 22.7 us)
Async XLA Ops:
  6.4 11.0 %collective-permute-start.4 = (bf16[2,64,1024]{2,1,0:T(8,128)(2,1)}, bf16[2,64,1024]{2,1,0:T(8,128)(2,1)S(1)}, u32[]{:S(2)}, u32[]{:S(2)}) collective-permute-start(bf16[2,64,1024]{2,1,0:T(8,128)(2,1)} %get-tuple-element.67.refs_4_), channel_id=1, source_target_pairs={{0,16},{8,24},{16,0},{24,8},{1,17},{9,25},{17,1},{25,9},{2,18},{10... | collective-permute-start | bytes 786440 | tf_op jit(solution)/shard_map/ppermute | solution.py:29
  15.2 9.5 %collective-permute-start = (bf16[2,64,1024]{2,1,0:T(8,128)(2,1)}, bf16[2,64,1024]{2,1,0:T(8,128)(2,1)S(1)}, u32[]{:S(2)}, u32[]{:S(2)}) collective-permute-start(bf16[2,64,1024]{2,1,0:T(8,128)(2,1)} %get-tuple-element.66.refs_0_), channel_id=1, source_target_pairs={{0,8},{8,0},{16,24},{24,16},{1,9},{9,1},{17,25},{25,17},{2,10},{10... | collective-permute-start | bytes 786440 | tf_op jit(solution)/shard_map/ppermute | solution.py:29
  16.8 13.6 %collective-permute-start.3 = (bf16[2,64,1024]{2,1,0:T(8,128)(2,1)S(1)}, bf16[2,64,1024]{2,1,0:T(8,128)(2,1)S(1)}, u32[]{:S(2)}, u32[]{:S(2)}) collective-permute-start(bf16[2,64,1024]{2,1,0:T(8,128)(2,1)S(1)} %copy-done.2), channel_id=1, source_target_pairs={{0,8},{8,0},{16,24},{24,16},{1,9},{9,1},{17,25},{25,17},{2,10},{10... | collective-permute-start | bytes 786440 | tf_op jit(solution)/shard_map/ppermute | solution.py:29
  17.3 14.5 %collective-permute-start.1 = (bf16[2,64,1024]{2,1,0:T(8,128)(2,1)}, bf16[2,64,1024]{2,1,0:T(8,128)(2,1)S(1)}, u32[]{:S(2)}, u32[]{:S(2)}) collective-permute-start(bf16[2,64,1024]{2,1,0:T(8,128)(2,1)} %get-tuple-element.66.refs_0_), channel_id=1, source_target_pairs={{0,16},{8,24},{16,0},{24,8},{1,17},{9,25},{17,1},{25,9},{2,18},{10... | collective-permute-start | bytes 786440 | tf_op jit(solution)/shard_map/ppermute | solution.py:29
  17.4 18.6 %collective-permute-start.5 = (bf16[2,64,1024]{2,1,0:T(8,128)(2,1)S(1)}, bf16[2,64,1024]{2,1,0:T(8,128)(2,1)S(1)}, u32[]{:S(2)}, u32[]{:S(2)}) collective-permute-start(bf16[2,64,1024]{2,1,0:T(8,128)(2,1)S(1)} %collective-permute-done.4.refs_6_), channel_id=1, source_target_pairs={{0,8},{8,0},{16,24},{24,16},{1,9},{9,1},{17,25},{25,17},{2,10},{10... | collective-permute-start | bytes 786440 | tf_op jit(solution)/shard_map/ppermute | solution.py:29
  24.7 12.1 %collective-permute-start.2 = (bf16[2,64,1024]{2,1,0:T(8,128)(2,1)S(1)}, bf16[2,64,1024]{2,1,0:T(8,128)(2,1)S(1)}, u32[]{:S(2)}, u32[]{:S(2)}) collective-permute-start(bf16[2,64,1024]{2,1,0:T(8,128)(2,1)S(1)} %collective-permute-done.refs_1_), channel_id=1, source_target_pairs={{0,16},{8,24},{16,0},{24,8},{1,17},{9,25},{17,1},{25,9},{2,18},{10... | collective-permute-start | bytes 786440 | tf_op jit(solution)/shard_map/ppermute | solution.py:29
  24.7 26.6 %collective-permute-start.7 = (bf16[2,64,1024]{2,1,0:T(8,128)(2,1)}, bf16[2,64,1024]{2,1,0:T(8,128)(2,1)S(1)}, u32[]{:S(2)}, u32[]{:S(2)}) collective-permute-start(bf16[2,64,1024]{2,1,0:T(8,128)(2,1)} %get-tuple-element.78.refs_0_), channel_id=1, source_target_pairs={{0,16},{8,24},{16,0},{24,8},{1,17},{9,25},{17,1},{25,9},{2,18},{10... | collective-permute-start | bytes 786440 | tf_op jit(solution)/shard_map/ppermute | solution.py:29
  30.3 21.0 %collective-permute-start.6 = (bf16[2,64,1024]{2,1,0:T(8,128)(2,1)}, bf16[2,64,1024]{2,1,0:T(8,128)(2,1)S(1)}, u32[]{:S(2)}, u32[]{:S(2)}) collective-permute-start(bf16[2,64,1024]{2,1,0:T(8,128)(2,1)} %get-tuple-element.78.refs_0_), channel_id=1, source_target_pairs={{0,8},{8,0},{16,24},{24,16},{1,9},{9,1},{17,25},{25,17},{2,10},{10... | collective-permute-start | bytes 786440 | tf_op jit(solution)/shard_map/ppermute | solution.py:29
  31.8 19.5 %collective-permute-start.9 = (bf16[2,64,1024]{2,1,0:T(8,128)(2,1)S(1)}, bf16[2,64,1024]{2,1,0:T(8,128)(2,1)S(1)}, u32[]{:S(2)}, u32[]{:S(2)}) collective-permute-start(bf16[2,64,1024]{2,1,0:T(8,128)(2,1)S(1)} %copy-done), channel_id=1, source_target_pairs={{0,8},{8,0},{16,24},{24,16},{1,9},{9,1},{17,25},{25,17},{2,10},{10... | collective-permute-start | bytes 786440 | tf_op jit(solution)/shard_map/ppermute | solution.py:29
  36.6 14.7 %collective-permute-start.8 = (bf16[2,64,1024]{2,1,0:T(8,128)(2,1)S(1)}, bf16[2,64,1024]{2,1,0:T(8,128)(2,1)S(1)}, u32[]{:S(2)}, u32[]{:S(2)}) collective-permute-start(bf16[2,64,1024]{2,1,0:T(8,128)(2,1)S(1)} %copy-done), channel_id=1, source_target_pairs={{0,16},{8,24},{16,0},{24,8},{1,17},{9,25},{17,1},{25,9},{2,18},{10... | collective-permute-start | bytes 786440 | tf_op jit(solution)/shard_map/ppermute | solution.py:29
  51.4 2.1 %collective-permute-start.10 = (bf16[128,2304]{1,0:T(8,128)(2,1)S(1)}, bf16[128,2304]{1,0:T(8,128)(2,1)S(1)}, u32[]{:S(2)}, u32[]{:S(2)}) collective-permute-start(bf16[128,2304]{1,0:T(8,128)(2,1)S(1)} %get-tuple-element.74), channel_id=1, source_target_pairs={{0,1},{1,0},{2,3},{3,2},{4,5},{5,4},{6,7},{7,6},{8,9},{9,8},{10,11... | collective-permute-start | bytes 1769480 | tf_op jit(solution)/shard_map/ppermute | solution.py:29
  54.3 6.2 %collective-permute-start.12 = (bf16[32,2304]{1,0:T(8,128)(2,1)S(1)}, bf16[32,2304]{1,0:T(8,128)(2,1)S(1)}, u32[]{:S(2)}, u32[]{:S(2)}) collective-permute-start(bf16[32,2304]{1,0:T(8,128)(2,1)S(1)} %get-tuple-element.131), channel_id=1, source_target_pairs={{0,2},{1,3},{2,0},{3,1},{4,6},{5,7},{6,4},{7,5},{8,10},{9,11},{10,... | collective-permute-start | bytes 442376 | tf_op jit(solution)/shard_map/ppermute | solution.py:29
  56.3 8.1 %collective-permute-start.14 = (bf16[2,64,1024]{2,1,0:T(8,128)(2,1)S(1)}, bf16[2,64,1024]{2,1,0:T(8,128)(2,1)S(1)}, u32[]{:S(2)}, u32[]{:S(2)}) collective-permute-start(bf16[2,64,1024]{2,1,0:T(8,128)(2,1)S(1)} %collective-permute-done.6.refs_1_), channel_id=1, source_target_pairs={{0,16},{8,24},{16,0},{24,8},{1,17},{9,25},{17,1},{25,9},{2,18},{10... | collective-permute-start | bytes 786440 | tf_op jit(solution)/shard_map/ppermute | solution.py:29
  57.9 7.8 %collective-permute-start.15 = (bf16[2,64,1024]{2,1,0:T(8,128)(2,1)S(1)}, bf16[2,64,1024]{2,1,0:T(8,128)(2,1)S(1)}, u32[]{:S(2)}, u32[]{:S(2)}) collective-permute-start(bf16[2,64,1024]{2,1,0:T(8,128)(2,1)S(1)} %collective-permute-done.8.refs_6_), channel_id=1, source_target_pairs={{0,8},{8,0},{16,24},{24,16},{1,9},{9,1},{17,25},{25,17},{2,10},{10... | collective-permute-start | bytes 786440 | tf_op jit(solution)/shard_map/ppermute | solution.py:29
  59.3 17.4 %collective-permute-start.11 = (bf16[32,2304]{1,0:T(8,128)(2,1)}, bf16[32,2304]{1,0:T(8,128)(2,1)}, u32[]{:S(2)}, u32[]{:S(2)}) collective-permute-start(bf16[32,2304]{1,0:T(8,128)(2,1)} %get-tuple-element.130), channel_id=1, source_target_pairs={{0,2},{1,3},{2,0},{3,1},{4,6},{5,7},{6,4},{7,5},{8,10},{9,11},{10,... | collective-permute-start | bytes 442376 | tf_op jit(solution)/shard_map/ppermute | solution.py:29
  61.2 15.6 %collective-permute-start.13 = (bf16[32,2304]{1,0:T(8,128)(2,1)}, bf16[32,2304]{1,0:T(8,128)(2,1)}, u32[]{:S(2)}, u32[]{:S(2)}) collective-permute-start(bf16[32,2304]{1,0:T(8,128)(2,1)} %add_convert_fusion.7), channel_id=1, source_target_pairs={{0,4},{1,5},{2,6},{3,7},{4,0},{5,1},{6,2},{7,3},{8,12},{9,13},{10,... | collective-permute-start | bytes 442376 | tf_op jit(solution)/shard_map/ppermute | solution.py:29
  76.7 12.6 %collective-permute-start.16 = (bf16[128,2304]{1,0:T(8,128)(2,1)S(1)}, bf16[128,2304]{1,0:T(8,128)(2,1)S(1)}, u32[]{:S(2)}, u32[]{:S(2)}) collective-permute-start(bf16[128,2304]{1,0:T(8,128)(2,1)S(1)} %get-tuple-element.86), channel_id=1, source_target_pairs={{0,1},{1,0},{2,3},{3,2},{4,5},{5,4},{6,7},{7,6},{8,9},{9,8},{10,11... | collective-permute-start | bytes 1769480 | tf_op jit(solution)/shard_map/ppermute | solution.py:29
  78.9 10.3 %collective-permute-start.21 = (bf16[32,2304]{1,0:T(8,128)(2,1)S(1)}, bf16[32,2304]{1,0:T(8,128)(2,1)S(1)}, u32[]{:S(2)}, u32[]{:S(2)}) collective-permute-start(bf16[32,2304]{1,0:T(8,128)(2,1)S(1)} %get-tuple-element.139.refs_0_), channel_id=1, source_target_pairs={{0,4},{1,5},{2,6},{3,7},{4,0},{5,1},{6,2},{7,3},{8,12},{9,13},{10,... | collective-permute-start | bytes 442376 | tf_op jit(solution)/shard_map/ppermute | solution.py:29
  81.6 11.1 %collective-permute-start.20 = (bf16[32,2304]{1,0:T(8,128)(2,1)S(1)}, bf16[32,2304]{1,0:T(8,128)(2,1)S(1)}, u32[]{:S(2)}, u32[]{:S(2)}) collective-permute-start(bf16[32,2304]{1,0:T(8,128)(2,1)S(1)} %get-tuple-element.139.refs_0_), channel_id=1, source_target_pairs={{0,2},{1,3},{2,0},{3,1},{4,6},{5,7},{6,4},{7,5},{8,10},{9,11},{10,... | collective-permute-start | bytes 442376 | tf_op jit(solution)/shard_map/ppermute | solution.py:29
  89.3 6.7 %collective-permute-start.22 = (bf16[32,2304]{1,0:T(8,128)(2,1)S(1)}, bf16[32,2304]{1,0:T(8,128)(2,1)S(1)}, u32[]{:S(2)}, u32[]{:S(2)}) collective-permute-start(bf16[32,2304]{1,0:T(8,128)(2,1)S(1)} %collective-permute-done.21.refs_2_), channel_id=1, source_target_pairs={{0,2},{1,3},{2,0},{3,1},{4,6},{5,7},{6,4},{7,5},{8,10},{9,11},{10,... | collective-permute-start | bytes 442376 | tf_op jit(solution)/shard_map/ppermute | solution.py:29
  90.0 8.2 %collective-permute-start.18 = (bf16[32,2304]{1,0:T(8,128)(2,1)S(1)}, bf16[32,2304]{1,0:T(8,128)(2,1)S(1)}, u32[]{:S(2)}, u32[]{:S(2)}) collective-permute-start(bf16[32,2304]{1,0:T(8,128)(2,1)S(1)} %get-tuple-element.129), channel_id=1, source_target_pairs={{0,2},{1,3},{2,0},{3,1},{4,6},{5,7},{6,4},{7,5},{8,10},{9,11},{10,... | collective-permute-start | bytes 442376 | tf_op jit(solution)/shard_map/ppermute | solution.py:29
  92.1 7.1 %collective-permute-start.23 = (bf16[32,2304]{1,0:T(8,128)(2,1)S(1)}, bf16[32,2304]{1,0:T(8,128)(2,1)S(1)}, u32[]{:S(2)}, u32[]{:S(2)}) collective-permute-start(bf16[32,2304]{1,0:T(8,128)(2,1)S(1)} %get-tuple-element.139.refs_0_), channel_id=1, source_target_pairs={{0,1},{1,0},{2,3},{3,2},{4,5},{5,4},{6,7},{7,6},{8,9},{9,8},{10,11... | collective-permute-start | bytes 442376 | tf_op jit(solution)/shard_map/ppermute | solution.py:29
  92.1 11.5 %collective-permute-start.25 = (bf16[32,2304]{1,0:T(8,128)(2,1)S(1)}, bf16[32,2304]{1,0:T(8,128)(2,1)S(1)}, u32[]{:S(2)}, u32[]{:S(2)}) collective-permute-start(bf16[32,2304]{1,0:T(8,128)(2,1)S(1)} %collective-permute-done.21.refs_2_), channel_id=1, source_target_pairs={{0,1},{1,0},{2,3},{3,2},{4,5},{5,4},{6,7},{7,6},{8,9},{9,8},{10,11... | collective-permute-start | bytes 442376 | tf_op jit(solution)/shard_map/ppermute | solution.py:29
  92.6 11.0 %collective-permute-start.24 = (bf16[32,2304]{1,0:T(8,128)(2,1)S(1)}, bf16[32,2304]{1,0:T(8,128)(2,1)S(1)}, u32[]{:S(2)}, u32[]{:S(2)}) collective-permute-start(bf16[32,2304]{1,0:T(8,128)(2,1)S(1)} %collective-permute-done.20.refs_1_), channel_id=1, source_target_pairs={{0,1},{1,0},{2,3},{3,2},{4,5},{5,4},{6,7},{7,6},{8,9},{9,8},{10,11... | collective-permute-start | bytes 442376 | tf_op jit(solution)/shard_map/ppermute | solution.py:29
  96.0 7.7 %collective-permute-start.26 = (bf16[32,2304]{1,0:T(8,128)(2,1)S(1)}, bf16[32,2304]{1,0:T(8,128)(2,1)S(1)}, u32[]{:S(2)}, u32[]{:S(2)}) collective-permute-start(bf16[32,2304]{1,0:T(8,128)(2,1)S(1)} %collective-permute-done.22.refs_3_), channel_id=1, source_target_pairs={{0,1},{1,0},{2,3},{3,2},{4,5},{5,4},{6,7},{7,6},{8,9},{9,8},{10,11... | collective-permute-start | bytes 442376 | tf_op jit(solution)/shard_map/ppermute | solution.py:29
  98.2 28.9 %collective-permute-start.17 = (bf16[32,2304]{1,0:T(8,128)(2,1)}, bf16[32,2304]{1,0:T(8,128)(2,1)}, u32[]{:S(2)}, u32[]{:S(2)}) collective-permute-start(bf16[32,2304]{1,0:T(8,128)(2,1)} %get-tuple-element.128), channel_id=1, source_target_pairs={{0,2},{1,3},{2,0},{3,1},{4,6},{5,7},{6,4},{7,5},{8,10},{9,11},{10,... | collective-permute-start | bytes 442376 | tf_op jit(solution)/shard_map/ppermute | solution.py:29
  99.2 28.5 %collective-permute-start.19 = (bf16[32,2304]{1,0:T(8,128)(2,1)}, bf16[32,2304]{1,0:T(8,128)(2,1)}, u32[]{:S(2)}, u32[]{:S(2)}) collective-permute-start(bf16[32,2304]{1,0:T(8,128)(2,1)} %add_convert_fusion.4), channel_id=1, source_target_pairs={{0,4},{1,5},{2,6},{3,7},{4,0},{5,1},{6,2},{7,3},{8,12},{9,13},{10,... | collective-permute-start | bytes 442376 | tf_op jit(solution)/shard_map/ppermute | solution.py:29
  113.7 23.5 %collective-permute-start.35 = (bf16[2,64,1024]{2,1,0:T(8,128)(2,1)S(1)}, bf16[2,64,1024]{2,1,0:T(8,128)(2,1)S(1)}, u32[]{:S(2)}, u32[]{:S(2)}) collective-permute-start(bf16[2,64,1024]{2,1,0:T(8,128)(2,1)S(1)} %get-tuple-element.95), channel_id=1, source_target_pairs={{0,16},{8,24},{16,0},{24,8},{1,17},{9,25},{17,1},{25,9},{2,18},{10... | collective-permute-start | bytes 786440 | tf_op jit(solution)/shard_map/ppermute | solution.py:29
  114.2 16.0 %collective-permute-start.45 = (bf16[2,64,1024]{2,1,0:T(8,128)(2,1)S(1)}, bf16[2,64,1024]{2,1,0:T(8,128)(2,1)S(1)}, u32[]{:S(2)}, u32[]{:S(2)}) collective-permute-start(bf16[2,64,1024]{2,1,0:T(8,128)(2,1)S(1)} %get-tuple-element.96), channel_id=1, source_target_pairs={{0,16},{8,24},{16,0},{24,8},{1,17},{9,25},{17,1},{25,9},{2,18},{10... | collective-permute-start | bytes 786440 | tf_op jit(solution)/shard_map/ppermute | solution.py:29
  125.6 11.8 %collective-permute-start.34 = (bf16[2,64,1024]{2,1,0:T(8,128)(2,1)S(1)}, bf16[2,64,1024]{2,1,0:T(8,128)(2,1)S(1)}, u32[]{:S(2)}, u32[]{:S(2)}) collective-permute-start(bf16[2,64,1024]{2,1,0:T(8,128)(2,1)S(1)} %get-tuple-element.93), channel_id=1, source_target_pairs={{0,8},{8,0},{16,24},{24,16},{1,9},{9,1},{17,25},{25,17},{2,10},{10... | collective-permute-start | bytes 786440 | tf_op jit(solution)/shard_map/ppermute | solution.py:29
  127.1 29.2 %collective-permute-start.44 = (bf16[2,64,1024]{2,1,0:T(8,128)(2,1)S(1)}, bf16[2,64,1024]{2,1,0:T(8,128)(2,1)S(1)}, u32[]{:S(2)}, u32[]{:S(2)}) collective-permute-start(bf16[2,64,1024]{2,1,0:T(8,128)(2,1)S(1)} %get-tuple-element.94), channel_id=1, source_target_pairs={{0,8},{8,0},{16,24},{24,16},{1,9},{9,1},{17,25},{25,17},{2,10},{10... | collective-permute-start | bytes 786440 | tf_op jit(solution)/shard_map/ppermute | solution.py:29
  129.7 7.5 %collective-permute-start.28 = (bf16[32,2304]{1,0:T(8,128)(2,1)S(1)}, bf16[32,2304]{1,0:T(8,128)(2,1)S(1)}, u32[]{:S(2)}, u32[]{:S(2)}) collective-permute-start(bf16[32,2304]{1,0:T(8,128)(2,1)S(1)} %get-tuple-element.101.refs_0_), channel_id=1, source_target_pairs={{0,4},{1,5},{2,6},{3,7},{4,0},{5,1},{6,2},{7,3},{8,12},{9,13},{10,... | collective-permute-start | bytes 442376 | tf_op jit(solution)/shard_map/ppermute | solution.py:29
  130.2 7.6 %collective-permute-start.27 = (bf16[32,2304]{1,0:T(8,128)(2,1)S(1)}, bf16[32,2304]{1,0:T(8,128)(2,1)S(1)}, u32[]{:S(2)}, u32[]{:S(2)}) collective-permute-start(bf16[32,2304]{1,0:T(8,128)(2,1)S(1)} %get-tuple-element.101.refs_0_), channel_id=1, source_target_pairs={{0,2},{1,3},{2,0},{3,1},{4,6},{5,7},{6,4},{7,5},{8,10},{9,11},{10,... | collective-permute-start | bytes 442376 | tf_op jit(solution)/shard_map/ppermute | solution.py:29
  137.2 5.1 %collective-permute-start.29 = (bf16[32,2304]{1,0:T(8,128)(2,1)S(1)}, bf16[32,2304]{1,0:T(8,128)(2,1)S(1)}, u32[]{:S(2)}, u32[]{:S(2)}) collective-permute-start(bf16[32,2304]{1,0:T(8,128)(2,1)S(1)} %collective-permute-done.28.refs_2_), channel_id=1, source_target_pairs={{0,2},{1,3},{2,0},{3,1},{4,6},{5,7},{6,4},{7,5},{8,10},{9,11},{10,... | collective-permute-start | bytes 442376 | tf_op jit(solution)/shard_map/ppermute | solution.py:29
  137.2 5.2 %collective-permute-start.30 = (bf16[32,2304]{1,0:T(8,128)(2,1)S(1)}, bf16[32,2304]{1,0:T(8,128)(2,1)S(1)}, u32[]{:S(2)}, u32[]{:S(2)}) collective-permute-start(bf16[32,2304]{1,0:T(8,128)(2,1)S(1)} %get-tuple-element.101.refs_0_), channel_id=1, source_target_pairs={{0,1},{1,0},{2,3},{3,2},{4,5},{5,4},{6,7},{7,6},{8,9},{9,8},{10,11... | collective-permute-start | bytes 442376 | tf_op jit(solution)/shard_map/ppermute | solution.py:29
  137.3 6.6 %collective-permute-start.32 = (bf16[32,2304]{1,0:T(8,128)(2,1)S(1)}, bf16[32,2304]{1,0:T(8,128)(2,1)S(1)}, u32[]{:S(2)}, u32[]{:S(2)}) collective-permute-start(bf16[32,2304]{1,0:T(8,128)(2,1)S(1)} %collective-permute-done.28.refs_2_), channel_id=1, source_target_pairs={{0,1},{1,0},{2,3},{3,2},{4,5},{5,4},{6,7},{7,6},{8,9},{9,8},{10,11... | collective-permute-start | bytes 442376 | tf_op jit(solution)/shard_map/ppermute | solution.py:29
  137.8 6.6 %collective-permute-start.31 = (bf16[32,2304]{1,0:T(8,128)(2,1)S(1)}, bf16[32,2304]{1,0:T(8,128)(2,1)S(1)}, u32[]{:S(2)}, u32[]{:S(2)}) collective-permute-start(bf16[32,2304]{1,0:T(8,128)(2,1)S(1)} %collective-permute-done.27.refs_1_), channel_id=1, source_target_pairs={{0,1},{1,0},{2,3},{3,2},{4,5},{5,4},{6,7},{7,6},{8,9},{9,8},{10,11... | collective-permute-start | bytes 442376 | tf_op jit(solution)/shard_map/ppermute | solution.py:29
  142.3 2.1 %collective-permute-start.33 = (bf16[32,2304]{1,0:T(8,128)(2,1)S(1)}, bf16[32,2304]{1,0:T(8,128)(2,1)S(1)}, u32[]{:S(2)}, u32[]{:S(2)}) collective-permute-start(bf16[32,2304]{1,0:T(8,128)(2,1)S(1)} %collective-permute-done.29.refs_3_), channel_id=1, source_target_pairs={{0,1},{1,0},{2,3},{3,2},{4,5},{5,4},{6,7},{7,6},{8,9},{9,8},{10,11... | collective-permute-start | bytes 442376 | tf_op jit(solution)/shard_map/ppermute | solution.py:29
  142.4 28.9 %collective-permute-start.47 = (bf16[2,64,1024]{2,1,0:T(8,128)(2,1)S(1)}, bf16[2,64,1024]{2,1,0:T(8,128)(2,1)S(1)}, u32[]{:S(2)}, u32[]{:S(2)}) collective-permute-start(bf16[2,64,1024]{2,1,0:T(8,128)(2,1)S(1)} %add_convert_fusion.2), channel_id=1, source_target_pairs={{0,8},{8,0},{16,24},{24,16},{1,9},{9,1},{17,25},{25,17},{2,10},{10... | collective-permute-start | bytes 786440 | tf_op jit(solution)/shard_map/ppermute | solution.py:29
  144.0 28.9 %collective-permute-start.46 = (bf16[2,64,1024]{2,1,0:T(8,128)(2,1)S(1)}, bf16[2,64,1024]{2,1,0:T(8,128)(2,1)S(1)}, u32[]{:S(2)}, u32[]{:S(2)}) collective-permute-start(bf16[2,64,1024]{2,1,0:T(8,128)(2,1)S(1)} %add_convert_fusion.3), channel_id=1, source_target_pairs={{0,16},{8,24},{16,0},{24,8},{1,17},{9,25},{17,1},{25,9},{2,18},{10... | collective-permute-start | bytes 786440 | tf_op jit(solution)/shard_map/ppermute | solution.py:29
  155.5 12.4 %collective-permute-start.36 = (f32[8,128]{1,0:T(8,128)S(1)}, f32[8,128]{1,0:T(8,128)S(1)}, u32[]{:S(2)}, u32[]{:S(2)}) collective-permute-start(f32[8,128]{1,0:T(8,128)S(1)} %broadcast_in_dim.11), channel_id=1, source_target_pairs={{0,8},{8,0},{16,24},{24,16},{1,9},{9,1},{17,25},{25,17},{2,10},{10... | collective-permute-start | bytes 12296 | tf_op jit(solution)/shard_map/ppermute | solution.py:29
  166.4 11.2 %collective-permute-start.42 = (bf16[2,64,1024]{2,1,0:T(8,128)(2,1)S(1)}, bf16[2,64,1024]{2,1,0:T(8,128)(2,1)S(1)}, u32[]{:S(2)}, u32[]{:S(2)}) collective-permute-start(bf16[2,64,1024]{2,1,0:T(8,128)(2,1)S(1)} %get-tuple-element.117), channel_id=1, source_target_pairs={{0,16},{8,24},{16,0},{24,8},{1,17},{9,25},{17,1},{25,9},{2,18},{10... | collective-permute-start | bytes 786440 | tf_op jit(solution)/shard_map/ppermute | solution.py:29
  168.5 7.3 %collective-permute-start.37 = (f32[8,128]{1,0:T(8,128)S(1)}, f32[8,128]{1,0:T(8,128)S(1)}, u32[]{:S(2)}, u32[]{:S(2)}) collective-permute-start(f32[8,128]{1,0:T(8,128)S(1)} %broadcast_add_fusion), channel_id=1, source_target_pairs={{0,16},{8,24},{16,0},{24,8},{1,17},{9,25},{17,1},{25,9},{2,18},{10... | collective-permute-start | bytes 12296 | tf_op jit(solution)/shard_map/ppermute | solution.py:29
  170.0 17.0 %collective-permute-start.39 = (bf16[2,64,1024]{2,1,0:T(8,128)(2,1)S(1)}, bf16[2,64,1024]{2,1,0:T(8,128)(2,1)S(1)}, u32[]{:S(2)}, u32[]{:S(2)}) collective-permute-start(bf16[2,64,1024]{2,1,0:T(8,128)(2,1)S(1)} %get-tuple-element.113), channel_id=1, source_target_pairs={{0,16},{8,24},{16,0},{24,8},{1,17},{9,25},{17,1},{25,9},{2,18},{10... | collective-permute-start | bytes 786440 | tf_op jit(solution)/shard_map/ppermute | solution.py:29
  171.3 15.7 %collective-permute-start.38 = (bf16[2,64,1024]{2,1,0:T(8,128)(2,1)S(1)}, bf16[2,64,1024]{2,1,0:T(8,128)(2,1)S(1)}, u32[]{:S(2)}, u32[]{:S(2)}) collective-permute-start(bf16[2,64,1024]{2,1,0:T(8,128)(2,1)S(1)} %get-tuple-element.111), channel_id=1, source_target_pairs={{0,8},{8,0},{16,24},{24,16},{1,9},{9,1},{17,25},{25,17},{2,10},{10... | collective-permute-start | bytes 786440 | tf_op jit(solution)/shard_map/ppermute | solution.py:29
  172.8 13.4 %collective-permute-start.40 = (bf16[2,64,1024]{2,1,0:T(8,128)(2,1)S(1)}, bf16[2,64,1024]{2,1,0:T(8,128)(2,1)S(1)}, u32[]{:S(2)}, u32[]{:S(2)}) collective-permute-start(bf16[2,64,1024]{2,1,0:T(8,128)(2,1)S(1)} %get-tuple-element.115), channel_id=1, source_target_pairs={{0,8},{8,0},{16,24},{24,16},{1,9},{9,1},{17,25},{25,17},{2,10},{10... | collective-permute-start | bytes 786440 | tf_op jit(solution)/shard_map/ppermute | solution.py:29
  177.7 11.9 %collective-permute-start.43 = (bf16[2,64,1024]{2,1,0:T(8,128)(2,1)S(1)}, bf16[2,64,1024]{2,1,0:T(8,128)(2,1)S(1)}, u32[]{:S(2)}, u32[]{:S(2)}) collective-permute-start(bf16[2,64,1024]{2,1,0:T(8,128)(2,1)S(1)} %add_convert_fusion), channel_id=1, source_target_pairs={{0,8},{8,0},{16,24},{24,16},{1,9},{9,1},{17,25},{25,17},{2,10},{10... | collective-permute-start | bytes 786440 | tf_op jit(solution)/shard_map/ppermute | solution.py:29
  186.3 6.4 %collective-permute-start.41 = (bf16[2,64,1024]{2,1,0:T(8,128)(2,1)S(1)}, bf16[2,64,1024]{2,1,0:T(8,128)(2,1)S(1)}, u32[]{:S(2)}, u32[]{:S(2)}) collective-permute-start(bf16[2,64,1024]{2,1,0:T(8,128)(2,1)S(1)} %add_convert_fusion.1), channel_id=1, source_target_pairs={{0,16},{8,24},{16,0},{24,8},{1,17},{9,25},{17,1},{25,9},{2,18},{10... | collective-permute-start | bytes 786440 | tf_op jit(solution)/shard_map/ppermute | solution.py:29
  (12 other events, 150.6 us)

commit v4 on v3

--- a/solution.py
+++ b/solution.py
@@ -4,6 +4,7 @@
 import jax.numpy as jnp
 from jax import lax
 from jax.experimental import pallas as pl
+from jax.experimental.layout import Layout, with_layout_constraint
 from jax.experimental.pallas import tpu as pltpu
 from jax.sharding import PartitionSpec as P
 
@@ -13,7 +14,7 @@
 ROW_TILE = 16
 IN_FLIGHT = 4
 VMEM_BYTES = 44 << 20
-ENCODE_VMEM_BYTES = 59 << 20
+MOST_VMEM_BYTES = 59 << 20
 SMALL_COST = pl.CostEstimate(flops=1 << 20, bytes_accessed=1 << 10, transcendentals=0)
 FAR = pl.BlockSpec(memory_space=pltpu.HBM)
 ANYWHERE = pl.BlockSpec(memory_space=pl.ANY)
@@ -158,7 +159,7 @@
             pltpu.SemaphoreType.DMA((n * steps,)),
         ],
         (resid, w_enc, b_enc),
-        vmem=ENCODE_VMEM_BYTES,
+        vmem=MOST_VMEM_BYTES,
     )
 
 
@@ -237,30 +238,27 @@
             pltpu.SemaphoreType.DMA((plan.sources * steps,)),
         ],
         (index, *pieces, w_dec),
+        vmem=MOST_VMEM_BYTES,
     )
     return outs[0], outs[1:]
 
 
-def gradient_kernel(plan, lane, index_ref, *refs):
-    n_in = 2 * plan.depth
-    errors, w_ref, outs = refs[:n_in], refs[n_in], refs[n_in + 1:-4]
-    e_buf, w_buf, e_sem, w_sem = refs[-4:]
+def gradient_kernel(plan, lane, index_ref, errors_ref, w_ref, *refs):
+    outs, (e_buf, w_buf, e_sem, w_sem) = refs[:-4], refs[-4:]
     lo, hi = plan.lane_sources[lane]
     first, kept = plan.lanes[lane][0], plan.kept_order(lane)
-    base = 1 + plan.sources + plan.groups * plan.pairs
-    depth = pick_tile(plan.width, 512)
+    depth = pick_tile(plan.width, 256)
     steps = plan.width // depth
-
-    placing = [
-        pltpu.make_async_copy(
-            errors[i],
-            e_buf.at[
-                pl.ds(pl.multiple_of(index_ref[base + i] * plan.piece, ROW_TILE), plan.piece)
-            ],
-            e_sem.at[i],
-        )
-        for i in range(n_in)
-    ]
+    group = index_ref[1 + plan.sources + plan.groups * plan.pairs]
+
+    placing = []
+    for j in range(plan.groups):
+        rows = pl.multiple_of((group ^ j) * plan.block, ROW_TILE)
+        placing.append(pltpu.make_async_copy(
+            errors_ref.at[pl.ds(rows, plan.block)],
+            e_buf.at[pl.ds(j * plan.block, plan.block)],
+            e_sem.at[j],
+        ))
     for copy in placing:
         copy.start()
     stream = Stream([
@@ -291,9 +289,9 @@
             stream.wait(s * steps + i)
             part = slice(i * depth, (i + 1) * depth)
             product = lax.dot_general(
-                w_buf[s, part, :], e_buf[...], (((1,), (1,)), ((), ())),
+                e_buf[...], w_buf[s, part, :], (((1,), (1,)), ((), ())),
                 preferred_element_type=F32,
-            ).T
+            )
             product = jnp.where(feeds, product, 0.0)
             for p, j in enumerate(kept):
                 away = (j ^ first) * plan.block
@@ -304,7 +302,7 @@
 def gradient(plan, lane, index, errors, w_dec):
     lo, hi = plan.lane_sources[lane]
     n = hi - lo
-    steps = plan.width // pick_tile(plan.width, 512)
+    steps = plan.width // pick_tile(plan.width, 256)
     half = plan.groups // 2
     shape = (n, plan.block, plan.width)
     out_shape = [jax.ShapeDtypeStruct(shape, BF16)] * half
@@ -314,15 +312,15 @@
     outs = call(
         partial(gradient_kernel, plan, lane),
         "gradient",
-        [SCALARS] + [ANYWHERE] * len(errors) + [FAR],
+        [SCALARS, ANYWHERE, FAR],
         out_shape,
         [
             pltpu.VMEM((plan.chunk_rows, plan.model), BF16),
             pltpu.VMEM((n, plan.width, plan.model), BF16),
-            pltpu.SemaphoreType.DMA((len(errors),)),
+            pltpu.SemaphoreType.DMA((plan.groups,)),
             pltpu.SemaphoreType.DMA((n * steps,)),
         ],
-        (index, *errors, w_dec),
+        (index, errors, w_dec),
     )
     return outs[:half], outs[half:2 * half], outs[2 * half:]
 
@@ -381,18 +379,13 @@
         for j in range(groups)
         for b in range(plan.pairs)
     ]
-    places = []
-    for other in range(2):
-        for d in range(plan.depth):
-            owner = level ^ d
-            place = ((owner // plan.pairs) ^ group) * plan.pairs + owner % plan.pairs
-            places.append(place * 2 + (core ^ other))
-    index = jnp.concatenate([core[None], feeds, jnp.stack(offsets), jnp.stack(places)])
+    index = jnp.concatenate([core[None], feeds, jnp.stack(offsets), group[None]])
 
     encoded = [encode(plan, i, resid, w_enc, b_enc) for i in range(len(plan.lanes))]
     active = jnp.stack(
         [e[-1][s] for e in encoded for s in range(e[-1].shape[0])], axis=1
     )
+    active = with_layout_constraint(active, Layout((0, 1, 2)))
 
     gathered, arrivals = [], []
     earlier = []
@@ -400,7 +393,10 @@
         own = after([e[c] for e in encoded], earlier)
         pieces, first_arrivals = [], []
         for lane, bits in enumerate(plan.lanes):
-            held = {0: own[lane]}
+            mine = own[lane]
+            if not c:
+                mine, = after([mine], first_arrivals[-len(bits):])
+            held = {0: mine}
             for bit in bits:
                 held.update(
                     {j | bit: swap(x, "grp", groups, bit) for j, x in list(held.items())}
@@ -409,11 +405,11 @@
             first_arrivals += [held[bit] for bit in bits]
         gathered.append(pieces)
         arrivals.append(first_arrivals)
-        earlier = [first_arrivals[0]]
+        earlier = first_arrivals
 
     recon_parts = []
     squares = jnp.zeros((8, 128), F32)
-    before_decode, before_gradient, after_gradient = [], [], []
+    before_decode, before_gradient, after_gradient = [active], [], []
     unfinished = []
     pending = None
 
@@ -425,26 +421,24 @@
         difference = recon_rows - own_targets.astype(F32)
         recon_parts.append(recon_rows.astype(BF16))
         error = difference.astype(BF16)
-        held = {0: error}
-        for bit in reversed(plan.level_bits):
-            held.update(
-                {d | bit: swap(x, "feat", feats, 2 * bit) for d, x in list(held.items())}
-            )
-        errors = [held[d] for d in range(plan.depth)]
-        return error, errors + [swap(e, "feat", feats, 1) for e in errors]
+        return error, lax.all_gather(error, "feat", axis=0, tiled=True)
 
     def exchange_gradients(errors):
         nonlocal squares, before_gradient, after_gradient
-        errors = after(errors, before_gradient)
+        errors, = after([errors], before_gradient)
         before_gradient, after_gradient = [], []
         kept_all, got_all = [], []
         for lane, bits in enumerate(plan.lanes):
             away, kept, extra = gradient(plan, lane, index, errors, w_dec)
             after_gradient += away
+            if got_all:
+                away = after(away, first_got)
             if extra:
                 squares = squares + extra[0]
             for step, bit in enumerate(bits):
                 got = [swap(x, "grp", groups, bit) for x in away]
+                if not step:
+                    first_got = got[:1]
                 cut = len(got) // 2
                 if cut:
                     total = [x + y.astype(F32) for x, y in zip(kept, got)]

time: 195 us -> 217 us (1.11)
  between operations: 2.83 us -> 16.3 us
  waiting for transfers between devices: 53.2 us -> 63 us
  other arithmetic: 10.4 us -> 15 us
  starting transfers between devices: 45.8 us -> 41.6 us
  Pallas kernels: 75.5 us -> 73.2 us
    all_gather x0 -> x2, waiting for transfers between devices: none -> 7.3 us  [exchange_errors(): return (error, lax.all_gather(error, 'feat', axis=0, tiled=True))]
    ppermute x48 -> x34, starting transfers between devices: 45.8 us -> 41.3 us  [swap(): return lax.ppermute(x, axis, [(i, i ^ offset) for i in range(size)])]
    another operation x1, other arithmetic: 0.13 us -> 3.4 us  [per_device(): jnp.stack([e[-1][s] for e in encoded for s in range(e[-1].shape[0])], axi...]
    another operation x2 -> x6, local copies, waits for them, and re-layouts: 0.07 us -> 2.72 us  [per_device(): jnp.stack([e[-1][s] for e in encoded for s in range(e[-1].shape[0])], axi...]
    unnamed x25 -> x38, local copies, waits for them, and re-layouts: 6.07 us -> 3.5 us
    ppermute x48 -> x34, waiting for transfers between devices: 53.2 us -> 55.6 us  [swap(): return lax.ppermute(x, axis, [(i, i ^ offset) for i in range(size)])]
    pallas_call x10, Pallas kernels: 75.5 us -> 73.2 us  [call(): pl.pallas_call(kernel, in_specs=in_specs, out_shape=out_shape, scratch_sh...]
  transfers between devices with their start and end apart: 48 -> 36, of which waited for: 16 -> 18; matrix products, arithmetic and copies ran while one was open for 6% -> 8% of each run, Pallas kernels for 35% -> 23%
where the time goes in v4:
time: 217 us
  Pallas kernels  73.2 us (34%)
  waiting for transfers between devices  63 us (29%)
  starting transfers between devices  41.6 us (19%)
  between operations  16.3 us (8%)
  other arithmetic  15 us (7%)
  local copies, waits for them, and re-layouts  8.01 us (4%)
    pallas_call x10, Pallas kernels, call(): pl.pallas_call(kernel, in_specs=in_specs, out_shape=out_shape, scratch_sh...  73.2 us
    ppermute x34, waiting for transfers between devices, swap(): return lax.ppermute(x, axis, [(i, i ^ offset) for i in range(size)])  55.6 us
    ppermute x34, starting transfers between devices, swap(): return lax.ppermute(x, axis, [(i, i ^ offset) for i in range(size)])  41.3 us
    all_gather x2, waiting for transfers between devices, exchange_errors(): return (error, lax.all_gather(error, 'feat', axis=0, tiled=True))  7.3 us
  transfers between devices with their start and end apart: 36, of which 18 were waited for; matrix products, arithmetic and copies ran while one was open for 8% of the time, Pallas kernels for 23%

profile of v4, /device:TPU:0, one launch (start us, length us, event | category | flops | bytes accessed | tf_op | source)
XLA Modules:
  0.0 217.1 jit_solution(10677371018928275368)
XLA Ops:
  7.2 5.7 %encode.2 = (bf16[2,64,1024]{2,1,0:T(8,128)(2,1)}, bf16[2,64,1024]{2,1,0:T(8,128)(2,1)}, bf16[2,128,1024]{2,1,0:T(8,128)(2,1)}) custom-call(bf16[4,128,2304]{2,1,0:T(8,128)(2,1)} %resid_ref.3, bf16[4,2304,1024]{2,1,0:T(8,128)(2,1)} %w_ref.7, f32[4,1024]{1,0:T(4,128)} %b_ref.3), custom_call_target="tpu_custom_call" | custom-call | flops 1048576 | bytes 1024 | tf_op jit(solution)/shard_map/encode/pallas_call | solution.py:86
  12.9 3.0 %collective-permute-start.1 = (bf16[2,64,1024]{2,1,0:T(8,128)(2,1)}, bf16[2,64,1024]{2,1,0:T(8,128)(2,1)S(1)}, u32[]{:S(2)}, u32[]{:S(2)}) collective-permute-start(bf16[2,64,1024]{2,1,0:T(8,128)(2,1)} %get-tuple-element.75.refs_0_), channel_id=1, source_target_pairs={{0,16},{8,24},{16,0},{24,8},{1,17},{9,25},{17,1},{25,9},{2,18},{10... | collective-permute-start | bytes 786440 | tf_op jit(solution)/shard_map/ppermute | solution.py:30
  16.0 1.5 collective-permute-start
  17.5 5.7 %encode.3 = (bf16[2,64,1024]{2,1,0:T(8,128)(2,1)}, bf16[2,64,1024]{2,1,0:T(8,128)(2,1)}, bf16[2,128,1024]{2,1,0:T(8,128)(2,1)}) custom-call(bf16[4,128,2304]{2,1,0:T(8,128)(2,1)} %resid_ref.3, bf16[4,2304,1024]{2,1,0:T(8,128)(2,1)} %w_ref.7, f32[4,1024]{1,0:T(4,128)} %b_ref.3), custom_call_target="tpu_custom_call" | custom-call | flops 1048576 | bytes 1024 | tf_op jit(solution)/shard_map/encode/pallas_call | solution.py:86
  24.3 1.6 collective-permute-start.3
  25.9 1.5 collective-permute-start.2
  28.6 4.9 %collective-permute-done.4.refs_6_ = bf16[2,64,1024]{2,1,0:T(8,128)(2,1)} collective-permute-done((bf16[2,64,1024]{2,1,0:T(8,128)(2,1)}, bf16[2,64,1024]{2,1,0:T(8,128)(2,1)}, u32[]{:S(2)}, u32[]{:S(2)}) %collective-permute-start.4) | collective-permute-done | bytes 262176 | tf_op jit(solution)/shard_map/ppermute | solution.py:30
  33.9 1.6 collective-permute-start.6
  36.0 1.7 collective-permute-start.8
  37.6 1.4 collective-permute-done.2.refs_3_
  39.0 1.5 collective-permute-start.5
  42.8 3.4 %pad_maximum_fusion = bf16[128,4,1024]{2,1,0:T(4,128)(2,1)} fusion(bf16[128,1,1024]{2,1,0:T(2,128)(2,1)S(1)} %copy.14, bf16[128,1,1024]{2,1,0:T(2,128)(2,1)S(1)} %copy.13, bf16[128,1,1024]{2,1,0:T(2,128)(2,1)S(1)} %copy.12, bf16[128,1,1024]{2,1,0:T(2,128)(2,1)S(1)} %copy.11), kind=kLoop, calls=%fused_computation | loop fusion | flops 4194304 | bytes 2097152 | tf_op jit(solution)/shard_map/stack | solution.py:385
  46.2 3.4 %collective-permute-done.5.refs_7_ = bf16[2,64,1024]{2,1,0:T(8,128)(2,1)} collective-permute-done((bf16[2,64,1024]{2,1,0:T(8,128)(2,1)}, bf16[2,64,1024]{2,1,0:T(8,128)(2,1)}, u32[]{:S(2)}, u32[]{:S(2)}) %collective-permute-start.5) | collective-permute-done | bytes 262176 | tf_op jit(solution)/shard_map/ppermute | solution.py:30
  49.6 12.6 %decode.2 = (bf16[128,2304]{1,0:T(8,128)(2,1)}, f32[32,2304]{1,0:T(8,128)}, f32[32,2304]{1,0:T(8,128)}, f32[32,2304]{1,0:T(8,128)}, f32[32,2304]{1,0:T(8,128)}) custom-call(s32[10]{0:T(128)} %concatenate.6.index_ref, bf16[2,64,1024]{2,1,0:T(8,128)(2,1)} %get-tuple-element.75.refs_0_, bf16[2,64,1024]{2,1,0:T(8,128)(2,1)} %copy-done.13, ...), custom_call_target="tpu_custom_call" | custom-call | flops 1048576 | bytes 1024 | tf_op jit(solution)/shard_map/decode/pallas_call | solution.py:86
  62.3 2.2 %collective-permute-done.10 = bf16[128,2304]{1,0:T(8,128)(2,1)S(1)} collective-permute-done((bf16[128,2304]{1,0:T(8,128)(2,1)}, bf16[128,2304]{1,0:T(8,128)(2,1)S(1)}, u32[]{:S(2)}, u32[]{:S(2)}) %collective-permute-start.10) | collective-permute-done | bytes 589856 | tf_op jit(solution)/shard_map/ppermute | solution.py:30
  65.7 1.6 collective-permute-start.12
  69.8 2.2 %collective-permute-done.12 = bf16[32,2304]{1,0:T(8,128)(2,1)S(1)} collective-permute-done((bf16[32,2304]{1,0:T(8,128)(2,1)S(1)}, bf16[32,2304]{1,0:T(8,128)(2,1)S(1)}, u32[]{:S(2)}, u32[]{:S(2)}) %collective-permute-start.12) | collective-permute-done | bytes 147488 | tf_op jit(solution)/shard_map/ppermute | solution.py:30
  73.0 2.5 %collective-permute-start.13 = (bf16[32,2304]{1,0:T(8,128)(2,1)S(1)}, bf16[32,2304]{1,0:T(8,128)(2,1)S(1)}, u32[]{:S(2)}, u32[]{:S(2)}) collective-permute-start(bf16[32,2304]{1,0:T(8,128)(2,1)S(1)} %add_convert_fusion.7), channel_id=1, source_target_pairs={{0,4},{1,5},{2,6},{3,7},{4,0},{5,1},{6,2},{7,3},{8,12},{9,13},{10,... | collective-permute-start | bytes 442376 | tf_op jit(solution)/shard_map/ppermute | solution.py:30
  77.0 12.4 %decode.3 = (bf16[128,2304]{1,0:T(8,128)(2,1)}, f32[32,2304]{1,0:T(8,128)}, f32[32,2304]{1,0:T(8,128)}, f32[32,2304]{1,0:T(8,128)}, f32[32,2304]{1,0:T(8,128)}) custom-call(s32[10]{0:T(128)} %concatenate.6.index_ref, bf16[2,64,1024]{2,1,0:T(8,128)(2,1)} %get-tuple-element.93.refs_0_, bf16[2,64,1024]{2,1,0:T(8,128)(2,1)} %collective-permute-done.6.refs_1_, ...), custom_call_target="tpu_custom_call" | custom-call | flops 1048576 | bytes 1024 | tf_op jit(solution)/shard_map/decode/pallas_call | solution.py:86
  89.6 1.8 fusion.3
  91.8 2.2 collective-permute-start.18
  94.1 4.6 %collective-permute-done.18 = bf16[32,2304]{1,0:T(8,128)(2,1)S(1)} collective-permute-done((bf16[32,2304]{1,0:T(8,128)(2,1)S(1)}, bf16[32,2304]{1,0:T(8,128)(2,1)S(1)}, u32[]{:S(2)}, u32[]{:S(2)}) %collective-permute-start.18) | collective-permute-done | bytes 147488 | tf_op jit(solution)/shard_map/ppermute | solution.py:30
  98.7 2.5 %collective-permute-start.19 = (bf16[32,2304]{1,0:T(8,128)(2,1)S(1)}, bf16[32,2304]{1,0:T(8,128)(2,1)S(1)}, u32[]{:S(2)}, u32[]{:S(2)}) collective-permute-start(bf16[32,2304]{1,0:T(8,128)(2,1)S(1)} %add_convert_fusion.4), channel_id=1, source_target_pairs={{0,4},{1,5},{2,6},{3,7},{4,0},{5,1},{6,2},{7,3},{8,12},{9,13},{10,... | collective-permute-start | bytes 442376 | tf_op jit(solution)/shard_map/ppermute | solution.py:30
  101.2 2.1 collective-permute-done.17
  103.3 11.8 %collective-permute-done.19 = bf16[32,2304]{1,0:T(8,128)(2,1)S(1)} collective-permute-done((bf16[32,2304]{1,0:T(8,128)(2,1)S(1)}, bf16[32,2304]{1,0:T(8,128)(2,1)S(1)}, u32[]{:S(2)}, u32[]{:S(2)}) %collective-permute-start.19) | collective-permute-done | bytes 147488 | tf_op jit(solution)/shard_map/ppermute | solution.py:30
  115.1 3.8 %all-gather.3.cloned.1.call-done.errors_ref = bf16[256,2304]{1,0:T(8,128)(2,1)} async-done(((bf16[32,2304]{1,0:T(8,128)(2,1)}), bf16[256,2304]{1,0:T(8,128)(2,1)}) %all-gather.3.cloned.1.call-update) | async-done | bytes 1179664 | tf_op jit(solution)/shard_map/all_gather | solution.py:424
  118.9 1.3 copy-done.1
  120.2 8.5 %gradient.5 = (bf16[2,64,1024]{2,1,0:T(8,128)(2,1)S(1)}, bf16[2,64,1024]{2,1,0:T(8,128)(2,1)S(1)}, f32[2,64,1024]{2,1,0:T(8,128)S(1)}, f32[2,64,1024]{2,1,0:T(8,128)S(1)}) custom-call(s32[10]{0:T(128)S(1)} %copy-done.2, bf16[256,2304]{1,0:T(8,128)(2,1)S(1)} %copy-done.1, bf16[4,1,1024,2304]{3,2,1,0:T(8,128)(2,1)} %w_ref.11), custom_call_target="tpu_custom_call" | custom-call | flops 1048576 | bytes 1024 | tf_op jit(solution)/shard_map/gradient/pallas_call | solution.py:86
  128.7 8.5 %gradient.4 = (bf16[2,64,1024]{2,1,0:T(8,128)(2,1)S(1)}, bf16[2,64,1024]{2,1,0:T(8,128)(2,1)S(1)}, f32[2,64,1024]{2,1,0:T(8,128)S(1)}, f32[2,64,1024]{2,1,0:T(8,128)S(1)}, f32[8,128]{1,0:T(8,128)S(1)}) custom-call(s32[10]{0:T(128)S(1)} %copy-done.2, bf16[256,2304]{1,0:T(8,128)(2,1)S(1)} %copy-done.1, bf16[4,1,1024,2304]{3,2,1,0:T(8,128)(2,1)} %w_ref.11), custom_call_target="tpu_custom_call" | custom-call | flops 1048576 | bytes 1024 | tf_op jit(solution)/shard_map/gradient/pallas_call | solution.py:86
  137.2 1.7 fusion
  138.9 1.4 collective-permute-start.20
  141.0 7.1 %collective-permute-done.20 = bf16[2,64,1024]{2,1,0:T(8,128)(2,1)S(1)} collective-permute-done((bf16[2,64,1024]{2,1,0:T(8,128)(2,1)S(1)}, bf16[2,64,1024]{2,1,0:T(8,128)(2,1)S(1)}, u32[]{:S(2)}, u32[]{:S(2)}) %collective-permute-start.20) | collective-permute-done | bytes 262176 | tf_op jit(solution)/shard_map/ppermute | solution.py:30
  148.1 1.3 collective-permute-start.21
  149.4 1.7 maximum_bitcast_fusion
  152.6 1.3 collective-permute-start.32
  153.9 3.4 %collective-permute-done.21 = bf16[2,64,1024]{2,1,0:T(8,128)(2,1)S(1)} collective-permute-done((bf16[2,64,1024]{2,1,0:T(8,128)(2,1)S(1)}, bf16[2,64,1024]{2,1,0:T(8,128)(2,1)S(1)}, u32[]{:S(2)}, u32[]{:S(2)}) %collective-permute-start.21) | collective-permute-done | bytes 262176 | tf_op jit(solution)/shard_map/ppermute | solution.py:30
  157.4 3.5 %all-gather.5.cloned.1.call-done.errors_ref = bf16[256,2304]{1,0:T(8,128)(2,1)} async-done(((bf16[32,2304]{1,0:T(8,128)(2,1)}), bf16[256,2304]{1,0:T(8,128)(2,1)}) %all-gather.5.cloned.1.call-update) | async-done | bytes 1179664 | tf_op jit(solution)/shard_map/all_gather | solution.py:424
  162.2 8.5 %gradient.6 = (bf16[2,64,1024]{2,1,0:T(8,128)(2,1)S(1)}, bf16[2,64,1024]{2,1,0:T(8,128)(2,1)S(1)}, f32[2,64,1024]{2,1,0:T(8,128)S(1)}, f32[2,64,1024]{2,1,0:T(8,128)S(1)}, f32[8,128]{1,0:T(8,128)S(1)}) custom-call(s32[10]{0:T(128)S(1)} %copy-done.2, bf16[256,2304]{1,0:T(8,128)(2,1)S(1)} %copy-done, bf16[4,1,1024,2304]{3,2,1,0:T(8,128)(2,1)} %w_ref.11), custom_call_target="tpu_custom_call" | custom-call | flops 1048576 | bytes 1024 | tf_op jit(solution)/shard_map/gradient/pallas_call | solution.py:86
  172.0 1.5 collective-permute-start.22
  175.2 1.5 collective-permute-start.25
  177.3 1.5 collective-permute-start.23
  179.5 8.8 %gradient.7 = (bf16[2,64,1024]{2,1,0:T(8,128)(2,1)S(1)}, bf16[2,64,1024]{2,1,0:T(8,128)(2,1)S(1)}, f32[2,64,1024]{2,1,0:T(8,128)S(1)}, f32[2,64,1024]{2,1,0:T(8,128)S(1)}) custom-call(s32[10]{0:T(128)S(1)} %copy-done.2, bf16[256,2304]{1,0:T(8,128)(2,1)S(1)} %copy-done, bf16[4,1,1024,2304]{3,2,1,0:T(8,128)(2,1)} %w_ref.11), custom_call_target="tpu_custom_call" | custom-call | flops 1048576 | bytes 1024 | tf_op jit(solution)/shard_map/gradient/pallas_call | solution.py:86
  189.6 1.3 collective-permute-start.28
  193.6 1.3 collective-permute-start.27
  194.9 4.0 %collective-permute-done.28 = bf16[2,64,1024]{2,1,0:T(8,128)(2,1)S(1)} collective-permute-done((bf16[2,64,1024]{2,1,0:T(8,128)(2,1)S(1)}, bf16[2,64,1024]{2,1,0:T(8,128)(2,1)S(1)}, u32[]{:S(2)}, u32[]{:S(2)}) %collective-permute-start.28) | collective-permute-done | bytes 262176 | tf_op jit(solution)/shard_map/ppermute | solution.py:30
  198.9 1.5 collective-permute-start.29
  200.6 3.9 %collective-permute-done.26 = bf16[2,64,1024]{2,1,0:T(8,128)(2,1)S(1)} collective-permute-done((bf16[2,64,1024]{2,1,0:T(8,128)(2,1)S(1)}, bf16[2,64,1024]{2,1,0:T(8,128)(2,1)S(1)}, u32[]{:S(2)}, u32[]{:S(2)}) %collective-permute-start.26) | collective-permute-done | bytes 262176 | tf_op jit(solution)/shard_map/ppermute | solution.py:30
  204.6 3.3 %collective-permute-done.27.refs_2_ = bf16[2,64,1024]{2,1,0:T(8,128)(2,1)S(1)} collective-permute-done((bf16[2,64,1024]{2,1,0:T(8,128)(2,1)S(1)}, bf16[2,64,1024]{2,1,0:T(8,128)(2,1)S(1)}, u32[]{:S(2)}, u32[]{:S(2)}) %collective-permute-start.27) | collective-permute-done | bytes 262176 | tf_op jit(solution)/shard_map/ppermute | solution.py:30
  (105 shorter events, 24.7 us)
Async XLA Ops:
  7.2 111.8 %all-gather.3.cloned.1.call-start = ((), (), s32[]{:S(2)}) async-start(), calls=%async_computation | async-start | bytes 1327104 | tf_op jit(solution)/shard_map/all_gather | solution.py:424
  12.9 15.6 %copy-start.3 = (bf16[2,128,1024]{2,1,0:T(8,128)(2,1)S(1)}, bf16[2,128,1024]{2,1,0:T(8,128)(2,1)}, u32[]{:S(2)}) copy-start(bf16[2,128,1024]{2,1,0:T(8,128)(2,1)} %get-tuple-element.70) | copy-start | bytes 1572868
  12.9 10.3 %collective-permute-start.1 = (bf16[2,64,1024]{2,1,0:T(8,128)(2,1)}, bf16[2,64,1024]{2,1,0:T(8,128)(2,1)S(1)}, u32[]{:S(2)}, u32[]{:S(2)}) collective-permute-start(bf16[2,64,1024]{2,1,0:T(8,128)(2,1)} %get-tuple-element.75.refs_0_), channel_id=1, source_target_pairs={{0,16},{8,24},{16,0},{24,8},{1,17},{9,25},{17,1},{25,9},{2,18},{10... | collective-permute-start | bytes 786440 | tf_op jit(solution)/shard_map/ppermute | solution.py:30
  16.0 8.0 %collective-permute-start = (bf16[2,64,1024]{2,1,0:T(8,128)(2,1)}, bf16[2,64,1024]{2,1,0:T(8,128)(2,1)S(1)}, u32[]{:S(2)}, u32[]{:S(2)}) collective-permute-start(bf16[2,64,1024]{2,1,0:T(8,128)(2,1)} %get-tuple-element.75.refs_0_), channel_id=1, source_target_pairs={{0,8},{8,0},{16,24},{24,16},{1,9},{9,1},{17,25},{25,17},{2,10},{10... | collective-permute-start | bytes 786440 | tf_op jit(solution)/shard_map/ppermute | solution.py:30
  23.2 10.4 %copy-start.9 = (bf16[2,64,1024]{2,1,0:T(8,128)(2,1)S(1)}, bf16[2,64,1024]{2,1,0:T(8,128)(2,1)}, u32[]{:S(2)}) copy-start(bf16[2,64,1024]{2,1,0:T(8,128)(2,1)} %get-tuple-element.93.refs_0_) | copy-start | bytes 786436
  23.2 12.4 %copy-start.10 = (bf16[2,64,1024]{2,1,0:T(8,128)(2,1)S(1)}, bf16[2,64,1024]{2,1,0:T(8,128)(2,1)}, u32[]{:S(2)}) copy-start(bf16[2,64,1024]{2,1,0:T(8,128)(2,1)} %get-tuple-element.97.refs_4_) | copy-start | bytes 786436
  23.2 17.3 %copy-start.18 = (s32[4,1]{0,1:T(1,128)S(1)}, s32[4,1]{0,1:T(1,128)}, u32[]{:S(2)}) copy-start(s32[4,1]{0,1:T(1,128)} %param.11) | copy-start | bytes 52
  23.2 17.7 %copy-start.12 = (bf16[2,64,1024]{2,1,0:T(8,128)(2,1)}, bf16[2,64,1024]{2,1,0:T(8,128)(2,1)S(1)}, u32[]{:S(2)}) copy-start(bf16[2,64,1024]{2,1,0:T(8,128)(2,1)S(1)} %collective-permute-done.1.refs_2_) | copy-start | bytes 786436
  24.0 17.0 %copy-start.13 = (bf16[2,64,1024]{2,1,0:T(8,128)(2,1)}, bf16[2,64,1024]{2,1,0:T(8,128)(2,1)S(1)}, u32[]{:S(2)}) copy-start(bf16[2,64,1024]{2,1,0:T(8,128)(2,1)S(1)} %collective-permute-done.refs_1_) | copy-start | bytes 786436
  24.0 9.6 %collective-permute-start.4 = (bf16[2,64,1024]{2,1,0:T(8,128)(2,1)}, bf16[2,64,1024]{2,1,0:T(8,128)(2,1)}, u32[]{:S(2)}, u32[]{:S(2)}) collective-permute-start(bf16[2,64,1024]{2,1,0:T(8,128)(2,1)} %get-tuple-element.79.refs_4_), channel_id=1, source_target_pairs={{0,16},{8,24},{16,0},{24,8},{1,17},{9,25},{17,1},{25,9},{2,18},{10... | collective-permute-start | bytes 786440 | tf_op jit(solution)/shard_map/ppermute | solution.py:30
  24.3 9.2 %collective-permute-start.3 = (bf16[2,64,1024]{2,1,0:T(8,128)(2,1)}, bf16[2,64,1024]{2,1,0:T(8,128)(2,1)S(1)}, u32[]{:S(2)}, u32[]{:S(2)}) collective-permute-start(bf16[2,64,1024]{2,1,0:T(8,128)(2,1)} %get-tuple-element.79.refs_4_), channel_id=1, source_target_pairs={{0,8},{8,0},{16,24},{24,16},{1,9},{9,1},{17,25},{25,17},{2,10},{10... | collective-permute-start | bytes 786440 | tf_op jit(solution)/shard_map/ppermute | solution.py:30
  25.9 13.1 %collective-permute-start.2 = (bf16[2,64,1024]{2,1,0:T(8,128)(2,1)S(1)}, bf16[2,64,1024]{2,1,0:T(8,128)(2,1)S(1)}, u32[]{:S(2)}, u32[]{:S(2)}) collective-permute-start(bf16[2,64,1024]{2,1,0:T(8,128)(2,1)S(1)} %collective-permute-done.refs_1_), channel_id=1, source_target_pairs={{0,16},{8,24},{16,0},{24,8},{1,17},{9,25},{17,1},{25,9},{2,18},{10... | collective-permute-start | bytes 786440 | tf_op jit(solution)/shard_map/ppermute | solution.py:30
  33.5 8.3 %copy-start.14 = (bf16[2,64,1024]{2,1,0:T(8,128)(2,1)}, bf16[2,64,1024]{2,1,0:T(8,128)(2,1)S(1)}, u32[]{:S(2)}) copy-start(bf16[2,64,1024]{2,1,0:T(8,128)(2,1)S(1)} %collective-permute-done.3.refs_5_) | copy-start | bytes 786436
  33.5 28.7 %collective-permute-start.7 = (bf16[2,64,1024]{2,1,0:T(8,128)(2,1)S(1)}, bf16[2,64,1024]{2,1,0:T(8,128)(2,1)S(1)}, u32[]{:S(2)}, u32[]{:S(2)}) collective-permute-start(bf16[2,64,1024]{2,1,0:T(8,128)(2,1)S(1)} %copy-done.9), channel_id=1, source_target_pairs={{0,16},{8,24},{16,0},{24,8},{1,17},{9,25},{17,1},{25,9},{2,18},{10... | collective-permute-start | bytes 786440 | tf_op jit(solution)/shard_map/ppermute | solution.py:30
  33.9 28.3 %collective-permute-start.6 = (bf16[2,64,1024]{2,1,0:T(8,128)(2,1)S(1)}, bf16[2,64,1024]{2,1,0:T(8,128)(2,1)}, u32[]{:S(2)}, u32[]{:S(2)}) collective-permute-start(bf16[2,64,1024]{2,1,0:T(8,128)(2,1)S(1)} %copy-done.9), channel_id=1, source_target_pairs={{0,8},{8,0},{16,24},{24,16},{1,9},{9,1},{17,25},{25,17},{2,10},{10... | collective-permute-start | bytes 786440 | tf_op jit(solution)/shard_map/ppermute | solution.py:30
  35.6 26.7 %collective-permute-start.9 = (bf16[2,64,1024]{2,1,0:T(8,128)(2,1)S(1)}, bf16[2,64,1024]{2,1,0:T(8,128)(2,1)}, u32[]{:S(2)}, u32[]{:S(2)}) collective-permute-start(bf16[2,64,1024]{2,1,0:T(8,128)(2,1)S(1)} %copy-done.10), channel_id=1, source_target_pairs={{0,8},{8,0},{16,24},{24,16},{1,9},{9,1},{17,25},{25,17},{2,10},{10... | collective-permute-start | bytes 786440 | tf_op jit(solution)/shard_map/ppermute | solution.py:30
  36.0 26.3 %collective-permute-start.8 = (bf16[2,64,1024]{2,1,0:T(8,128)(2,1)S(1)}, bf16[2,64,1024]{2,1,0:T(8,128)(2,1)}, u32[]{:S(2)}, u32[]{:S(2)}) collective-permute-start(bf16[2,64,1024]{2,1,0:T(8,128)(2,1)S(1)} %copy-done.10), channel_id=1, source_target_pairs={{0,16},{8,24},{16,0},{24,8},{1,17},{9,25},{17,1},{25,9},{2,18},{10... | collective-permute-start | bytes 786440 | tf_op jit(solution)/shard_map/ppermute | solution.py:30
  39.0 10.6 %collective-permute-start.5 = (bf16[2,64,1024]{2,1,0:T(8,128)(2,1)}, bf16[2,64,1024]{2,1,0:T(8,128)(2,1)}, u32[]{:S(2)}, u32[]{:S(2)}) collective-permute-start(bf16[2,64,1024]{2,1,0:T(8,128)(2,1)} %collective-permute-done.4.refs_6_), channel_id=1, source_target_pairs={{0,8},{8,0},{16,24},{24,16},{1,9},{9,1},{17,25},{25,17},{2,10},{10... | collective-permute-start | bytes 786440 | tf_op jit(solution)/shard_map/ppermute | solution.py:30
  62.2 13.9 %copy-start.11 = (bf16[2,64,1024]{2,1,0:T(8,128)(2,1)}, bf16[2,64,1024]{2,1,0:T(8,128)(2,1)S(1)}, u32[]{:S(2)}) copy-start(bf16[2,64,1024]{2,1,0:T(8,128)(2,1)S(1)} %collective-permute-done.7.refs_2_) | copy-start | bytes 786436
  62.3 2.3 %collective-permute-start.10 = (bf16[128,2304]{1,0:T(8,128)(2,1)}, bf16[128,2304]{1,0:T(8,128)(2,1)S(1)}, u32[]{:S(2)}, u32[]{:S(2)}) collective-permute-start(bf16[128,2304]{1,0:T(8,128)(2,1)} %get-tuple-element.89), channel_id=1, source_target_pairs={{0,1},{1,0},{2,3},{3,2},{4,5},{5,4},{6,7},{7,6},{8,9},{9,8},{10,11... | collective-permute-start | bytes 1769480 | tf_op jit(solution)/shard_map/ppermute | solution.py:30
  65.7 6.3 %collective-permute-start.12 = (bf16[32,2304]{1,0:T(8,128)(2,1)S(1)}, bf16[32,2304]{1,0:T(8,128)(2,1)S(1)}, u32[]{:S(2)}, u32[]{:S(2)}) collective-permute-start(bf16[32,2304]{1,0:T(8,128)(2,1)S(1)} %get-tuple-element.139), channel_id=1, source_target_pairs={{0,2},{1,3},{2,0},{3,1},{4,6},{5,7},{6,4},{7,5},{8,10},{9,11},{10,... | collective-permute-start | bytes 442376 | tf_op jit(solution)/shard_map/ppermute | solution.py:30
  67.3 8.3 %collective-permute-start.14 = (bf16[2,64,1024]{2,1,0:T(8,128)(2,1)}, bf16[2,64,1024]{2,1,0:T(8,128)(2,1)S(1)}, u32[]{:S(2)}, u32[]{:S(2)}) collective-permute-start(bf16[2,64,1024]{2,1,0:T(8,128)(2,1)} %collective-permute-done.6.refs_1_), channel_id=1, source_target_pairs={{0,16},{8,24},{16,0},{24,8},{1,17},{9,25},{17,1},{25,9},{2,18},{10... | collective-permute-start | bytes 786440 | tf_op jit(solution)/shard_map/ppermute | solution.py:30
  68.1 8.0 %collective-permute-start.15 = (bf16[2,64,1024]{2,1,0:T(8,128)(2,1)}, bf16[2,64,1024]{2,1,0:T(8,128)(2,1)S(1)}, u32[]{:S(2)}, u32[]{:S(2)}) collective-permute-start(bf16[2,64,1024]{2,1,0:T(8,128)(2,1)} %collective-permute-done.8.refs_6_), channel_id=1, source_target_pairs={{0,8},{8,0},{16,24},{24,16},{1,9},{9,1},{17,25},{25,17},{2,10},{10... | collective-permute-start | bytes 786440 | tf_op jit(solution)/shard_map/ppermute | solution.py:30
  69.3 20.2 %collective-permute-start.11 = (bf16[32,2304]{1,0:T(8,128)(2,1)S(1)}, bf16[32,2304]{1,0:T(8,128)(2,1)S(1)}, u32[]{:S(2)}, u32[]{:S(2)}) collective-permute-start(bf16[32,2304]{1,0:T(8,128)(2,1)S(1)} %get-tuple-element.138), channel_id=1, source_target_pairs={{0,2},{1,3},{2,0},{3,1},{4,6},{5,7},{6,4},{7,5},{8,10},{9,11},{10,... | collective-permute-start | bytes 442376 | tf_op jit(solution)/shard_map/ppermute | solution.py:30
  73.0 16.5 %collective-permute-start.13 = (bf16[32,2304]{1,0:T(8,128)(2,1)S(1)}, bf16[32,2304]{1,0:T(8,128)(2,1)S(1)}, u32[]{:S(2)}, u32[]{:S(2)}) collective-permute-start(bf16[32,2304]{1,0:T(8,128)(2,1)S(1)} %add_convert_fusion.7), channel_id=1, source_target_pairs={{0,4},{1,5},{2,6},{3,7},{4,0},{5,1},{6,2},{7,3},{8,12},{9,13},{10,... | collective-permute-start | bytes 442376 | tf_op jit(solution)/shard_map/ppermute | solution.py:30
  75.5 14.0 %copy-start.4 = (f32[32,2304]{1,0:T(8,128)S(1)}, f32[32,2304]{1,0:T(8,128)}, u32[]{:S(2)}) copy-start(f32[32,2304]{1,0:T(8,128)} %get-tuple-element.83) | copy-start | bytes 884740
  89.4 9.3 %copy-start.6 = (f32[32,2304]{1,0:T(8,128)S(1)}, f32[32,2304]{1,0:T(8,128)}, u32[]{:S(2)}) copy-start(f32[32,2304]{1,0:T(8,128)} %get-tuple-element.106) | copy-start | bytes 884740
  89.4 25.6 %copy-start.5 = (f32[32,2304]{1,0:T(8,128)S(1)}, f32[32,2304]{1,0:T(8,128)}, u32[]{:S(2)}) copy-start(f32[32,2304]{1,0:T(8,128)} %get-tuple-element.103) | copy-start | bytes 884740
  89.4 2.3 %collective-permute-start.16 = (bf16[128,2304]{1,0:T(8,128)(2,1)}, bf16[128,2304]{1,0:T(8,128)(2,1)S(1)}, u32[]{:S(2)}, u32[]{:S(2)}) collective-permute-start(bf16[128,2304]{1,0:T(8,128)(2,1)} %get-tuple-element.101), channel_id=1, source_target_pairs={{0,1},{1,0},{2,3},{3,2},{4,5},{5,4},{6,7},{7,6},{8,9},{9,8},{10,11... | collective-permute-start | bytes 1769480 | tf_op jit(solution)/shard_map/ppermute | solution.py:30
  89.6 29.3 %copy-start.2 = (s32[10]{0:T(128)S(1)}, s32[10]{0:T(128)}, u32[]{:S(2)}) copy-start(s32[10]{0:T(128)} %concatenate.6.index_ref) | copy-start | bytes 124
  91.5 69.5 %all-gather.5.cloned.1.call-start = ((), (), s32[]{:S(2)}) async-start(), calls=%async_computation.1 | async-start | bytes 1327104 | tf_op jit(solution)/shard_map/all_gather | solution.py:424
  91.8 6.9 %collective-permute-start.18 = (bf16[32,2304]{1,0:T(8,128)(2,1)S(1)}, bf16[32,2304]{1,0:T(8,128)(2,1)S(1)}, u32[]{:S(2)}, u32[]{:S(2)}) collective-permute-start(bf16[32,2304]{1,0:T(8,128)(2,1)S(1)} %get-tuple-element.137), channel_id=1, source_target_pairs={{0,2},{1,3},{2,0},{3,1},{4,6},{5,7},{6,4},{7,5},{8,10},{9,11},{10,... | collective-permute-start | bytes 442376 | tf_op jit(solution)/shard_map/ppermute | solution.py:30
  94.0 9.3 %collective-permute-start.17 = (bf16[32,2304]{1,0:T(8,128)(2,1)S(1)}, bf16[32,2304]{1,0:T(8,128)(2,1)S(1)}, u32[]{:S(2)}, u32[]{:S(2)}) collective-permute-start(bf16[32,2304]{1,0:T(8,128)(2,1)S(1)} %get-tuple-element.136), channel_id=1, source_target_pairs={{0,2},{1,3},{2,0},{3,1},{4,6},{5,7},{6,4},{7,5},{8,10},{9,11},{10,... | collective-permute-start | bytes 442376 | tf_op jit(solution)/shard_map/ppermute | solution.py:30
  98.7 16.4 %collective-permute-start.19 = (bf16[32,2304]{1,0:T(8,128)(2,1)S(1)}, bf16[32,2304]{1,0:T(8,128)(2,1)S(1)}, u32[]{:S(2)}, u32[]{:S(2)}) collective-permute-start(bf16[32,2304]{1,0:T(8,128)(2,1)S(1)} %add_convert_fusion.4), channel_id=1, source_target_pairs={{0,4},{1,5},{2,6},{3,7},{4,0},{5,1},{6,2},{7,3},{8,12},{9,13},{10,... | collective-permute-start | bytes 442376 | tf_op jit(solution)/shard_map/ppermute | solution.py:30
  138.9 9.2 %collective-permute-start.20 = (bf16[2,64,1024]{2,1,0:T(8,128)(2,1)S(1)}, bf16[2,64,1024]{2,1,0:T(8,128)(2,1)S(1)}, u32[]{:S(2)}, u32[]{:S(2)}) collective-permute-start(bf16[2,64,1024]{2,1,0:T(8,128)(2,1)S(1)} %get-tuple-element.108), channel_id=1, source_target_pairs={{0,8},{8,0},{16,24},{24,16},{1,9},{9,1},{17,25},{25,17},{2,10},{10... | collective-permute-start | bytes 786440 | tf_op jit(solution)/shard_map/ppermute | solution.py:30
  140.3 33.2 %collective-permute-start.30 = (bf16[2,64,1024]{2,1,0:T(8,128)(2,1)S(1)}, bf16[2,64,1024]{2,1,0:T(8,128)(2,1)}, u32[]{:S(2)}, u32[]{:S(2)}) collective-permute-start(bf16[2,64,1024]{2,1,0:T(8,128)(2,1)S(1)} %get-tuple-element.109), channel_id=1, source_target_pairs={{0,8},{8,0},{16,24},{24,16},{1,9},{9,1},{17,25},{25,17},{2,10},{10... | collective-permute-start | bytes 786440 | tf_op jit(solution)/shard_map/ppermute | solution.py:30
  148.1 9.2 %collective-permute-start.21 = (bf16[2,64,1024]{2,1,0:T(8,128)(2,1)S(1)}, bf16[2,64,1024]{2,1,0:T(8,128)(2,1)S(1)}, u32[]{:S(2)}, u32[]{:S(2)}) collective-permute-start(bf16[2,64,1024]{2,1,0:T(8,128)(2,1)S(1)} %get-tuple-element.116), channel_id=1, source_target_pairs={{0,16},{8,24},{16,0},{24,8},{1,17},{9,25},{17,1},{25,9},{2,18},{10... | collective-permute-start | bytes 786440 | tf_op jit(solution)/shard_map/ppermute | solution.py:30
  151.2 27.7 %collective-permute-start.31 = (bf16[2,64,1024]{2,1,0:T(8,128)(2,1)S(1)}, bf16[2,64,1024]{2,1,0:T(8,128)(2,1)S(1)}, u32[]{:S(2)}, u32[]{:S(2)}) collective-permute-start(bf16[2,64,1024]{2,1,0:T(8,128)(2,1)S(1)} %get-tuple-element.131), channel_id=1, source_target_pairs={{0,16},{8,24},{16,0},{24,8},{1,17},{9,25},{17,1},{25,9},{2,18},{10... | collective-permute-start | bytes 786440 | tf_op jit(solution)/shard_map/ppermute | solution.py:30
  152.6 35.7 %collective-permute-start.32 = (bf16[2,64,1024]{2,1,0:T(8,128)(2,1)}, bf16[2,64,1024]{2,1,0:T(8,128)(2,1)S(1)}, u32[]{:S(2)}, u32[]{:S(2)}) collective-permute-start(bf16[2,64,1024]{2,1,0:T(8,128)(2,1)} %add_convert_fusion.3), channel_id=1, source_target_pairs={{0,16},{8,24},{16,0},{24,8},{1,17},{9,25},{17,1},{25,9},{2,18},{10... | collective-permute-start | bytes 786440 | tf_op jit(solution)/shard_map/ppermute | solution.py:30
  172.0 4.6 %collective-permute-start.22 = (f32[8,128]{1,0:T(8,128)S(1)}, f32[8,128]{1,0:T(8,128)S(1)}, u32[]{:S(2)}, u32[]{:S(2)}) collective-permute-start(f32[8,128]{1,0:T(8,128)S(1)} %broadcast_in_dim.15), channel_id=1, source_target_pairs={{0,8},{8,0},{16,24},{24,16},{1,9},{9,1},{17,25},{25,17},{2,10},{10... | collective-permute-start | bytes 12296 | tf_op jit(solution)/shard_map/ppermute | solution.py:30
  174.5 13.8 %collective-permute-start.33 = (bf16[2,64,1024]{2,1,0:T(8,128)(2,1)S(1)}, bf16[2,64,1024]{2,1,0:T(8,128)(2,1)S(1)}, u32[]{:S(2)}, u32[]{:S(2)}) collective-permute-start(bf16[2,64,1024]{2,1,0:T(8,128)(2,1)S(1)} %add_convert_fusion.2), channel_id=1, source_target_pairs={{0,8},{8,0},{16,24},{24,16},{1,9},{9,1},{17,25},{25,17},{2,10},{10... | collective-permute-start | bytes 786440 | tf_op jit(solution)/shard_map/ppermute | solution.py:30
  175.2 14.4 %collective-permute-start.25 = (bf16[2,64,1024]{2,1,0:T(8,128)(2,1)S(1)}, bf16[2,64,1024]{2,1,0:T(8,128)(2,1)S(1)}, u32[]{:S(2)}, u32[]{:S(2)}) collective-permute-start(bf16[2,64,1024]{2,1,0:T(8,128)(2,1)S(1)} %get-tuple-element.124), channel_id=1, source_target_pairs={{0,8},{8,0},{16,24},{24,16},{1,9},{9,1},{17,25},{25,17},{2,10},{10... | collective-permute-start | bytes 786440 | tf_op jit(solution)/shard_map/ppermute | solution.py:30
  177.3 13.6 %collective-permute-start.23 = (f32[8,128]{1,0:T(8,128)S(1)}, f32[8,128]{1,0:T(8,128)S(1)}, u32[]{:S(2)}, u32[]{:S(2)}) collective-permute-start(f32[8,128]{1,0:T(8,128)S(1)} %broadcast_add_fusion), channel_id=1, source_target_pairs={{0,16},{8,24},{16,0},{24,8},{1,17},{9,25},{17,1},{25,9},{2,18},{10... | collective-permute-start | bytes 12296 | tf_op jit(solution)/shard_map/ppermute | solution.py:30
  178.9 21.6 %collective-permute-start.24 = (bf16[2,64,1024]{2,1,0:T(8,128)(2,1)S(1)}, bf16[2,64,1024]{2,1,0:T(8,128)(2,1)S(1)}, u32[]{:S(2)}, u32[]{:S(2)}) collective-permute-start(bf16[2,64,1024]{2,1,0:T(8,128)(2,1)S(1)} %get-tuple-element.120), channel_id=1, source_target_pairs={{0,8},{8,0},{16,24},{24,16},{1,9},{9,1},{17,25},{25,17},{2,10},{10... | collective-permute-start | bytes 786440 | tf_op jit(solution)/shard_map/ppermute | solution.py:30
  189.6 9.3 %collective-permute-start.28 = (bf16[2,64,1024]{2,1,0:T(8,128)(2,1)S(1)}, bf16[2,64,1024]{2,1,0:T(8,128)(2,1)S(1)}, u32[]{:S(2)}, u32[]{:S(2)}) collective-permute-start(bf16[2,64,1024]{2,1,0:T(8,128)(2,1)S(1)} %get-tuple-element.128), channel_id=1, source_target_pairs={{0,16},{8,24},{16,0},{24,8},{1,17},{9,25},{17,1},{25,9},{2,18},{10... | collective-permute-start | bytes 786440 | tf_op jit(solution)/shard_map/ppermute | solution.py:30
  192.7 11.8 %collective-permute-start.26 = (bf16[2,64,1024]{2,1,0:T(8,128)(2,1)S(1)}, bf16[2,64,1024]{2,1,0:T(8,128)(2,1)S(1)}, u32[]{:S(2)}, u32[]{:S(2)}) collective-permute-start(bf16[2,64,1024]{2,1,0:T(8,128)(2,1)S(1)} %get-tuple-element.125), channel_id=1, source_target_pairs={{0,16},{8,24},{16,0},{24,8},{1,17},{9,25},{17,1},{25,9},{2,18},{10... | collective-permute-start | bytes 786440 | tf_op jit(solution)/shard_map/ppermute | solution.py:30
  193.6 14.3 %collective-permute-start.27 = (bf16[2,64,1024]{2,1,0:T(8,128)(2,1)S(1)}, bf16[2,64,1024]{2,1,0:T(8,128)(2,1)S(1)}, u32[]{:S(2)}, u32[]{:S(2)}) collective-permute-start(bf16[2,64,1024]{2,1,0:T(8,128)(2,1)S(1)} %add_convert_fusion.1), channel_id=1, source_target_pairs={{0,16},{8,24},{16,0},{24,8},{1,17},{9,25},{17,1},{25,9},{2,18},{10... | collective-permute-start | bytes 786440 | tf_op jit(solution)/shard_map/ppermute | solution.py:30
  198.9 9.0 %collective-permute-start.29 = (bf16[2,64,1024]{2,1,0:T(8,128)(2,1)S(1)}, bf16[2,64,1024]{2,1,0:T(8,128)(2,1)S(1)}, u32[]{:S(2)}, u32[]{:S(2)}) collective-permute-start(bf16[2,64,1024]{2,1,0:T(8,128)(2,1)S(1)} %add_convert_fusion), channel_id=1, source_target_pairs={{0,8},{8,0},{16,24},{24,16},{1,9},{9,1},{17,25},{25,17},{2,10},{10... | collective-permute-start | bytes 786440 | tf_op jit(solution)/shard_map/ppermute | solution.py:30
  (7 other events, 11.4 us)
Sparse Core Ops, SparseCore 0:
  91.6 27.3 all-gather.2
  139.0 21.8 all-gather.4

commit v5 on v3

v5 whole, which is shorter than its diff:
```python
from functools import partial

import jax
import jax.numpy as jnp
from jax import lax
from jax.experimental import pallas as pl
from jax.experimental.layout import Layout, with_layout_constraint
from jax.experimental.pallas import tpu as pltpu
from jax.sharding import PartitionSpec as P

BF16 = jnp.bfloat16
F32 = jnp.float32
WANTED_CHUNKS = 2
ROW_TILE = 16
IN_FLIGHT = 3
WEIGHT_SLOTS = 5
VMEM_BYTES = 44 << 20
MOST_VMEM_BYTES = 59 << 20
SMALL_COST = pl.CostEstimate(flops=1 << 20, bytes_accessed=1 << 10, transcendentals=0)
FAR = pl.BlockSpec(memory_space=pltpu.HBM)
ANYWHERE = pl.BlockSpec(memory_space=pl.ANY)
SCALARS = pl.BlockSpec(memory_space=pltpu.SMEM)
NEAR = pl.BlockSpec(memory_space=pltpu.VMEM)


def pick_tile(size, wanted):
    return wanted if size % wanted == 0 else size


def swap(x, axis, size, offset):
    return lax.ppermute(x, axis, [(i, i ^ offset) for i in range(size)])


def after(values, earlier):
    if not earlier:
        return list(values)
    return list(lax.optimization_barrier(list(values) + list(earlier)))[:len(values)]


class Plan:
    def __init__(self, resid, w_dec):
        self.sources, self.rows, self.model = resid.shape
        self.width = w_dec.shape[2]
        self.groups = lax.axis_size("grp")
        self.feats = lax.axis_size("feat")
        self.depth = self.feats // 2
        self.tokens = self.rows * self.groups
        self.rows_feat = self.tokens // self.feats
        self.per_group = self.rows // self.rows_feat
        self.pairs = self.per_group // 2
        self.chunks = WANTED_CHUNKS
        while self.rows_feat % (self.chunks * ROW_TILE):
            self.chunks -= 1
        self.piece = self.rows_feat // self.chunks
        self.block = self.per_group * self.piece
        self.chunk_rows = self.groups * self.block
        bits = [1 << i for i in range(self.groups.bit_length() - 1)]
        self.lanes = [bits[i:] + bits[:i] for i in range(len(bits))]
        starts = [i * self.sources // len(bits) for i in range(len(bits) + 1)]
        self.lane_sources = list(zip(starts[:-1], starts[1:]))
        self.level_bits = [1 << i for i in range(self.depth.bit_length() - 1)]

    def kept_order(self, lane):
        kept = [0]
        for bit in reversed(self.lanes[lane][1:]):
            kept = [j | bit for j in kept] + kept
        return kept


class Stream:
    def __init__(self, copies):
        self.copies = copies
        self.started = 0
        self.more(IN_FLIGHT)

    def more(self, count):
        for copy in self.copies[self.started:self.started + count]:
            copy.start()
        self.started += count

    def wait(self, i):
        self.copies[i].wait()
        self.more(1)


def call(kernel, name, in_specs, out_shape, scratch, args, vmem=VMEM_BYTES, **options):
    return pl.pallas_call(
        kernel,
        in_specs=in_specs,
        out_shape=out_shape,
        scratch_shapes=scratch,
        cost_estimate=SMALL_COST,
        compiler_params=pltpu.CompilerParams(vmem_limit_bytes=vmem),
        name=name,
        **options,
    )(*args)


def encode_kernel(plan, lane, resid_ref, w_ref, b_ref, *refs):
    outs, (x_buf, w_buf, b_buf, total, x_sem, w_sem) = refs[:-6], refs[-6:]
    lo, hi = plan.lane_sources[lane]
    depth = w_buf.shape[1] // (w_sem.shape[0] // (hi - lo))
    steps = plan.model // depth
    near = [
        pltpu.make_async_copy(resid_ref.at[pl.ds(lo, hi - lo)], x_buf, x_sem.at[0]),
        pltpu.make_async_copy(b_ref, b_buf, x_sem.at[1]),
    ]
    near[0].start()
    stream = Stream([
        pltpu.make_async_copy(
            w_ref.at[lo + s, pl.ds(i * depth, depth)],
            w_buf.at[s, pl.ds(i * depth, depth)],
            w_sem.at[s * steps + i],
        )
        for s in range(hi - lo)
        for i in range(steps)
    ])
    near[1].start()
    near[0].wait()
    for s in range(hi - lo):
        for i in range(steps):
            stream.wait(s * steps + i)
            part = slice(i * depth, (i + 1) * depth)
            product = jnp.dot(
                x_buf[s, :, part], w_buf[s, part, :], preferred_element_type=F32
            )
            if i:
                product = total[...] + product
            if i < steps - 1:
                total[...] = product
        if s == 0:
            near[1].wait()
        outs[0][s] = jnp.maximum(product + b_buf[lo + s:lo + s + 1, :], 0.0).astype(BF16)


def encode(plan, lane, resid, w_enc, b_enc):
    lo, hi = plan.lane_sources[lane]
    n = hi - lo
    steps = plan.model // pick_tile(plan.model, 768)
    return call(
        partial(encode_kernel, plan, lane),
        "encode",
        [FAR, FAR, FAR],
        jax.ShapeDtypeStruct((n, plan.rows, plan.width), BF16),
        [
            pltpu.VMEM((n, plan.rows, plan.model), BF16),
            pltpu.VMEM((n, plan.model, plan.width), BF16),
            pltpu.VMEM((plan.sources, plan.width), F32),
            pltpu.VMEM((plan.rows, plan.width), F32),
            pltpu.SemaphoreType.DMA((2,)),
            pltpu.SemaphoreType.DMA((n * steps,)),
        ],
        (resid, w_enc, b_enc),
        vmem=MOST_VMEM_BYTES,
    )


def decode_kernel(plan, index_ref, *refs):
    n_in = plan.groups * len(plan.lanes)
    pieces, w_ref, outs = refs[:n_in], refs[n_in], refs[n_in + 1:-5]
    x_buf, w_buf, total, x_sem, w_sem = refs[-5:]
    half = plan.tokens // 2
    core = index_ref[0]
    depth = w_buf.shape[1]
    steps = plan.width // depth

    placing = []
    for lane, (lo, hi) in enumerate(plan.lane_sources):
        for j in range(plan.groups):
            for b in range(plan.pairs):
                place = index_ref[1 + plan.sources + j * plan.pairs + b] * plan.rows_feat
                for owner in range(2):
                    to = pl.multiple_of(place + jnp.where(core == owner, half, 0), ROW_TILE)
                    placing.append(pltpu.make_async_copy(
                        pieces[lane * plan.groups + j].at[
                            :, pl.ds((2 * b + owner) * plan.rows_feat, plan.rows_feat)
                        ],
                        x_buf.at[pl.ds(lo, hi - lo), pl.ds(to, plan.rows_feat)],
                        x_sem.at[len(placing)],
                    ))
    for copy in placing:
        copy.start()
    stream = Stream([
        pltpu.make_async_copy(
            w_ref.at[s, 0, pl.ds(i * depth, depth)],
            w_buf.at[(s * steps + i) % w_buf.shape[0]],
            w_sem.at[s * steps + i],
        )
        for s in range(plan.sources)
        for i in range(steps)
    ])
    for copy in placing:
        copy.wait()
    for s in range(plan.sources):
        @pl.when(index_ref[1 + s] == 0)
        def _(s=s):
            x_buf[s] = jnp.zeros(x_buf.shape[1:], BF16)

    tile = pick_tile(plan.model, 768)
    for s in range(plan.sources):
        for i in range(steps):
            stream.wait(s * steps + i)
            w_ref = w_buf.at[(s * steps + i) % w_buf.shape[0]]
            part = slice(i * depth, (i + 1) * depth)
            last = s * steps + i == plan.sources * steps - 1
            for n in range(0, plan.model, tile):
                cols = slice(n, n + tile)
                product = jnp.dot(
                    x_buf[s, :, part], w_ref[:, cols], preferred_element_type=F32
                )
                if s + i:
                    product = total[:, cols] + product
                if not last:
                    total[:, cols] = product
                    continue
                for c in range(plan.chunks):
                    for d in range(plan.depth):
                        first = d * plan.rows_feat + c * plan.piece
                        outs[c][d * plan.piece:(d + 1) * plan.piece, cols] = (
                            product[first:first + plan.piece].astype(BF16)
                        )
                        outs[plan.chunks + c * plan.depth + d][:, cols] = (
                            product[half + first:half + first + plan.piece]
                        )


def decode(plan, index, pieces, w_dec):
    step = pick_tile(plan.width, 512)
    steps = plan.width // step
    chunks, depth = plan.chunks, plan.depth
    outs = call(
        partial(decode_kernel, plan),
        "decode",
        [SCALARS] + [ANYWHERE] * len(pieces) + [FAR],
        [jax.ShapeDtypeStruct((depth * plan.piece, plan.model), BF16)] * chunks
        + [jax.ShapeDtypeStruct((plan.piece, plan.model), F32)] * (chunks * depth),
        [
            pltpu.VMEM((plan.sources, plan.tokens, plan.width), BF16),
            pltpu.VMEM((WEIGHT_SLOTS, step, plan.model), BF16),
            pltpu.VMEM((plan.tokens, plan.model), F32),
            pltpu.SemaphoreType.DMA((len(pieces) * plan.per_group,)),
            pltpu.SemaphoreType.DMA((plan.sources * steps,)),
        ],
        (index, *pieces, w_dec),
    )
    sends, keeps = outs[:chunks], outs[chunks:]
    return sends, [keeps[c * depth:(c + 1) * depth] for c in range(chunks)]


def gradient_kernel(plan, index_ref, *refs):
    n_in = 2 * plan.depth
    errors, w_ref, outs = refs[:n_in], refs[n_in], refs[n_in + 1:-4]
    e_buf, w_buf, e_sem, w_sem = refs[-4:]
    depth = pick_tile(plan.width, 256)
    steps = plan.width // depth
    base = 1 + plan.sources + plan.groups * plan.pairs

    placing = [
        pltpu.make_async_copy(
            errors[i],
            e_buf.at[
                pl.ds(pl.multiple_of(index_ref[base + i] * plan.piece, ROW_TILE), plan.piece)
            ],
            e_sem.at[i],
        )
        for i in range(n_in)
    ]
    for copy in placing:
        copy.start()
    stream = Stream([
        pltpu.make_async_copy(
            w_ref.at[s, 0, pl.ds(i * depth, depth)],
            w_buf.at[s, pl.ds(i * depth, depth)],
            w_sem.at[s * steps + i],
        )
        for s in range(plan.sources)
        for i in range(steps)
    ])
    for copy in placing:
        copy.wait()

    half = plan.groups // 2
    for lane, (lo, hi) in enumerate(plan.lane_sources):
        first, kept = plan.lanes[lane][0], plan.kept_order(lane)
        away, keep = outs[2 * lane * half:][:half], outs[(2 * lane + 1) * half:][:half]
        for s in range(lo, hi):
            feeds = index_ref[1 + s] > 0
            for i in range(steps):
                stream.wait(s * steps + i)
                part = slice(i * depth, (i + 1) * depth)
                product = lax.dot_general(
                    e_buf[...], w_buf[s, part, :], (((1,), (1,)), ((), ())),
                    preferred_element_type=F32,
                )
                product = jnp.where(feeds, product, 0.0)
                for p, j in enumerate(kept):
                    far = (j ^ first) * plan.block
                    away[p][s - lo, :, part] = product[far:far + plan.block].astype(BF16)
                    keep[p][s - lo, :, part] = product[j * plan.block:(j + 1) * plan.block]

    total = jnp.zeros((8, 128), F32)
    for row in range(0, plan.chunk_rows, ROW_TILE):
        value = e_buf[row:row + ROW_TILE, :].astype(F32)
        value = value * value
        value = value[:8] + value[8:]
        for col in range(0, plan.model, 128):
            total = total + value[:, col:col + 128]
    outs[-1][...] = total


def gradient(plan, index, errors, w_dec):
    steps = plan.width // pick_tile(plan.width, 256)
    half = plan.groups // 2
    out_shape = []
    for lo, hi in plan.lane_sources:
        shape = (hi - lo, plan.block, plan.width)
        out_shape += [jax.ShapeDtypeStruct(shape, BF16)] * half
        out_shape += [jax.ShapeDtypeStruct(shape, F32)] * half
    outs = call(
        partial(gradient_kernel, plan),
        "gradient",
        [SCALARS] + [ANYWHERE] * len(errors) + [FAR],
        out_shape + [jax.ShapeDtypeStruct((8, 128), F32)],
        [
            pltpu.VMEM((plan.chunk_rows, plan.model), BF16),
            pltpu.VMEM((plan.sources, plan.width, plan.model), BF16),
            pltpu.SemaphoreType.DMA((len(errors),)),
            pltpu.SemaphoreType.DMA((plan.sources * steps,)),
        ],
        (index, *errors, w_dec),
    )
    lanes = [outs[2 * i * half:2 * (i + 1) * half] for i in range(len(plan.lanes))]
    return [(lane[:half], lane[half:]) for lane in lanes], outs[-1]


def finish_kernel(plan, chunk, with_previous, *refs):
    lanes = len(plan.lanes)
    kept, got = refs[:lanes], refs[lanes:2 * lanes]
    out_ref, stage, sem = refs[-3:]
    for lane, (lo, hi) in enumerate(plan.lane_sources):
        for s in range(lo, hi):
            stage[:, s, :] = kept[lane][s - lo] + got[lane][s - lo].astype(F32)
    copies = [
        pltpu.make_async_copy(
            stage.at[pl.ds(b * plan.piece, plan.piece)],
            out_ref.at[pl.ds((b * plan.chunks + chunk) * plan.piece, plan.piece)],
            sem.at[b],
        )
        for b in range(plan.per_group)
    ]
    for copy in copies:
        copy.start()
    for copy in copies:
        copy.wait()


def finish(plan, chunk, kept, got, previous):
    options = {}
    if previous is not None:
        options["input_output_aliases"] = {2 * len(kept): 0}
    previous = [] if previous is None else [previous]
    return call(
        partial(finish_kernel, plan, chunk, bool(previous)),
        "finish",
        [NEAR] * (2 * len(kept)) + [FAR] * len(previous),
        jax.ShapeDtypeStruct((plan.rows, plan.sources, plan.width), F32),
        [
            pltpu.VMEM((plan.block, plan.sources, plan.width), F32),
            pltpu.SemaphoreType.DMA((plan.per_group,)),
        ],
        (*kept, *got, *previous),
        out_specs=FAR,
        **options,
    )


def per_device(resid, w_enc, b_enc, w_dec, targets, start_layer):
    plan = Plan(resid, w_dec)
    group = lax.axis_index("grp").astype(jnp.int32)
    feat = lax.axis_index("feat").astype(jnp.int32)
    core, level = feat % 2, feat // 2
    groups, feats, chunks = plan.groups, plan.feats, plan.chunks

    feeds = (group >= start_layer[:, 0]).astype(jnp.int32)
    offsets = [
        ((group ^ j) * plan.pairs + b) ^ level
        for j in range(groups)
        for b in range(plan.pairs)
    ]
    places = []
    for other in range(2):
        for d in range(plan.depth):
            owner = level ^ d
            place = ((owner // plan.pairs) ^ group) * plan.pairs + owner % plan.pairs
            places.append(place * 2 + (core ^ other))
    index = jnp.concatenate([core[None], feeds, jnp.stack(offsets), jnp.stack(places)])

    encoded = [encode(plan, i, resid, w_enc, b_enc) for i in range(len(plan.lanes))]
    active = jnp.stack([e[s] for e in encoded for s in range(e.shape[0])], axis=1)
    active = with_layout_constraint(active, Layout((0, 1, 2)))

    pieces, arrived = [], []
    for lane, bits in enumerate(plan.lanes):
        mine, = after([encoded[lane]], arrived)
        held = {0: mine}
        for bit in bits:
            held.update(
                {j | bit: swap(x, "grp", groups, bit) for j, x in list(held.items())}
            )
        pieces += [held[j] for j in range(groups)]
        arrived = [held[bit] for bit in bits]

    sends, keeps = decode(plan, index, after(pieces, [active]), w_dec)
    partial_rows = []
    earlier = []
    for c in range(chunks):
        other = swap(sends[c], "feat", feats, 1)
        held = {
            d: keeps[c][d] + other[d * plan.piece:(d + 1) * plan.piece].astype(F32)
            for d in range(plan.depth)
        }
        for bit in plan.level_bits:
            away = {d: held.pop(d).astype(BF16) for d in sorted(held, reverse=True) if d & bit}
            if bit == plan.level_bits[0]:
                away = dict(zip(away, after(away.values(), earlier)))
            got = {d: swap(x, "feat", feats, 2 * bit) for d, x in away.items()}
            if bit == plan.level_bits[0]:
                earlier = list(got.values())[:1]
            for d, x in got.items():
                held[d ^ bit] = held[d ^ bit] + x.astype(F32)
        partial_rows.append(held[0])

    recon_parts, errors, first_errors = [], [], []
    for c in range(chunks):
        recon_rows, = after([partial_rows[c]], first_errors[-1:])
        first = feat * plan.rows_feat + c * plan.piece
        own_targets = lax.dynamic_slice_in_dim(targets[0], first, plan.piece, 0)
        difference = recon_rows - own_targets.astype(F32)
        recon_parts.append(recon_rows.astype(BF16))
        held = {0: difference.astype(BF16)}
        for bit in reversed(plan.level_bits):
            held.update(
                {d | bit: swap(x, "feat", feats, 2 * bit) for d, x in list(held.items())}
            )
        first_errors.append(held[plan.level_bits[-1]])
        every = [held[d] for d in range(plan.depth)]
        errors.append(every + [swap(e, "feat", feats, 1) for e in every])

    squares = jnp.zeros((8, 128), F32)
    feat_grad = None
    earlier, first_got = [], []
    for c in range(chunks):
        ready = after(errors[c], [e[0] for e in errors[c + 1:c + 2]] + first_got)
        lanes, total = gradient(plan, index, ready, w_dec)
        squares = squares + total
        kept_all, got_all, second, first_got = [], [], [], []
        for bits, (away, kept) in zip(plan.lanes, lanes):
            away = after(away, earlier)
            for step, bit in enumerate(bits):
                got = [swap(x, "grp", groups, bit) for x in away]
                cut = len(got) // 2
                if cut:
                    sums = [x + y.astype(F32) for x, y in zip(kept, got)]
                    away, kept = [x.astype(BF16) for x in sums[:cut]], sums[cut:]
                    if not step:
                        first_got.append(got[0])
                        second += away
                        away = after(away, [] if feat_grad is None else [feat_grad])
            kept_all.append(kept[0])
            got_all.append(got[0])
        feat_grad = finish(plan, c, kept_all, got_all, feat_grad)
        earlier = second

    squares, = after([squares], first_got)
    loss = jnp.full((8, 128), jnp.sum(squares), F32)
    for bit in (1 << i for i in range(groups.bit_length() - 1)):
        loss = loss + swap(loss, "grp", groups, bit)
    entries = targets.shape[0] * groups * plan.tokens * plan.model
    recon_loss = loss[0, 0] / entries
    recon = jnp.concatenate(recon_parts, axis=0)[None]
    return active, recon, recon_loss, feat_grad


def solution(mesh):
    in_specs = (
        P(None, "grp", None),
        P(None, None, "feat"),
        P(None, "feat"),
        P(None, "grp", "feat", None),
        P("grp", None, None),
        P(None, "feat"),
    )
    out_specs = (P("grp", None, "feat"), P("grp", "feat", None), P(), P("grp", None, "feat"))
    return jax.shard_map(
        per_device, mesh=mesh, in_specs=in_specs, out_specs=out_specs, check_vma=False
    )
```

time: 195 us -> 188 us (0.964)
  Pallas kernels: 75.5 us -> 63.3 us
  starting transfers between devices: 45.8 us -> 38.7 us
  waiting for transfers between devices: 53.2 us -> 60.2 us
  local copies, waits for them, and re-layouts: 7.39 us -> 11.5 us
    pallas_call x10 -> x7, Pallas kernels: 75.5 us -> 63.3 us  [call(): pl.pallas_call(kernel, in_specs=in_specs, out_shape=out_shape, scratch_sh...]
    ppermute x48 -> x42, starting transfers between devices: 45.8 us -> 38.7 us  [swap(): return lax.ppermute(x, axis, [(i, i ^ offset) for i in range(size)])]
    ppermute x48 -> x42, waiting for transfers between devices: 53.2 us -> 60.2 us  [swap(): return lax.ppermute(x, axis, [(i, i ^ offset) for i in range(size)])]
    another operation x2 -> x6, local copies, waits for them, and re-layouts: 0.07 us -> 6.63 us  [per_device(): jnp.stack([e[s] for e in encoded for s in range(e.shape[0])], axis=1)]
    another operation x1, other arithmetic: 0.13 us -> 4.92 us  [per_device(): jnp.stack([e[s] for e in encoded for s in range(e.shape[0])], axis=1)]
    unnamed x25 -> x28, local copies, waits for them, and re-layouts: 6.07 us -> 3.63 us
    add x6, other arithmetic: 2.47 us -> 0.31 us  [the longest x4 0.25 us: per_device(): sums = [x + y.astype(F32) for x, y in zip(kept, got)]]
    convert_element_type x10 -> x9, other arithmetic: 5.13 us -> 3.39 us  [the longest x4 1.18 us: per_device(): held.pop(d).astype(BF16)]
  transfers between devices with their start and end apart: 48 -> 42, of which waited for: 16 -> 15; matrix products, arithmetic and copies ran while one was open for 6% -> 10% of each run, Pallas kernels for 35% -> 21%
where the time goes in v5:
time: 188 us
  Pallas kernels  63.3 us (34%)
  waiting for transfers between devices  60.2 us (32%)
  starting transfers between devices  38.7 us (21%)
  local copies, waits for them, and re-layouts  11.5 us (6%)
  other arithmetic  11.3 us (6%)
  between operations  2.79 us (1%)
    pallas_call x7, Pallas kernels, call(): pl.pallas_call(kernel, in_specs=in_specs, out_shape=out_shape, scratch_sh...  63.3 us
    ppermute x42, waiting for transfers between devices, swap(): return lax.ppermute(x, axis, [(i, i ^ offset) for i in range(size)])  60.2 us
    ppermute x42, starting transfers between devices, swap(): return lax.ppermute(x, axis, [(i, i ^ offset) for i in range(size)])  38.7 us
    another operation x6, local copies, waits for them, and re-layouts, per_device(): jnp.stack([e[s] for e in encoded for s in range(e.shape[0])], axis=1)  6.63 us
    another operation x1, other arithmetic, per_device(): jnp.stack([e[s] for e in encoded for s in range(e.shape[0])], axis=1)  4.92 us
  transfers between devices with their start and end apart: 42, of which 15 were waited for; matrix products, arithmetic and copies ran while one was open for 10% of the time, Pallas kernels for 21%

profile of v5, /device:TPU:0, one launch (start us, length us, event | category | flops | bytes accessed | tf_op | source)
XLA Modules:
  0.0 187.7 jit_solution(15747819126054119770)
XLA Ops:
  0.6 5.6 %encode.2.refs_0_ = bf16[2,128,1024]{2,1,0:T(8,128)(2,1)} custom-call(bf16[4,128,2304]{2,1,0:T(8,128)(2,1)} %resid_ref.3, bf16[4,2304,1024]{2,1,0:T(8,128)(2,1)} %w_ref.3, f32[4,1024]{1,0:T(4,128)} %b_ref.3), custom_call_target="tpu_custom_call" | custom-call | flops 1048576 | bytes 1024 | tf_op jit(solution)/shard_map/encode/pallas_call | solution.py:87
  6.2 3.0 %collective-permute-start = (bf16[2,128,1024]{2,1,0:T(8,128)(2,1)}, bf16[2,128,1024]{2,1,0:T(8,128)(2,1)S(1)}, u32[]{:S(2)}, u32[]{:S(2)}) collective-permute-start(bf16[2,128,1024]{2,1,0:T(8,128)(2,1)} %encode.2.refs_0_), channel_id=1, source_target_pairs={{0,8},{8,0},{16,24},{24,16},{1,9},{9,1},{17,25},{25,17},{2,10},{10... | collective-permute-start | bytes 1572872 | tf_op jit(solution)/shard_map/ppermute | solution.py:31
  9.2 1.5 collective-permute-start.1
  10.7 5.6 %encode.3.refs_4_ = bf16[2,128,1024]{2,1,0:T(8,128)(2,1)} custom-call(bf16[4,128,2304]{2,1,0:T(8,128)(2,1)} %resid_ref.3, bf16[4,2304,1024]{2,1,0:T(8,128)(2,1)} %w_ref.3, f32[4,1024]{1,0:T(4,128)} %b_ref.3), custom_call_target="tpu_custom_call" | custom-call | flops 1048576 | bytes 1024 | tf_op jit(solution)/shard_map/encode/pallas_call | solution.py:87
  16.3 5.0 %collective-permute-done.refs_1_ = bf16[2,128,1024]{2,1,0:T(8,128)(2,1)S(1)} collective-permute-done((bf16[2,128,1024]{2,1,0:T(8,128)(2,1)}, bf16[2,128,1024]{2,1,0:T(8,128)(2,1)S(1)}, u32[]{:S(2)}, u32[]{:S(2)}) %collective-permute-start) | collective-permute-done | bytes 524320 | tf_op jit(solution)/shard_map/ppermute | solution.py:31
  21.4 1.5 collective-permute-done.1.refs_2_
  22.8 1.5 collective-permute-start.4
  25.4 12.5 %collective-permute-done.4.refs_6_ = bf16[2,128,1024]{2,1,0:T(8,128)(2,1)S(1)} collective-permute-done((bf16[2,128,1024]{2,1,0:T(8,128)(2,1)}, bf16[2,128,1024]{2,1,0:T(8,128)(2,1)S(1)}, u32[]{:S(2)}, u32[]{:S(2)}) %collective-permute-start.4) | collective-permute-done | bytes 524320 | tf_op jit(solution)/shard_map/ppermute | solution.py:31
  38.3 1.8 slice_bitcast_fusion.1
  40.0 1.2 copy.11
  41.3 1.2 copy.12
  42.5 1.2 copy.13
  43.7 1.2 copy.14
  45.0 4.9 %pad_maximum_fusion = bf16[128,4,1024]{2,1,0:T(4,128)(2,1)} fusion(bf16[128,1,1024]{2,1,0:T(2,128)(2,1)} %copy.14, bf16[128,1,1024]{2,1,0:T(2,128)(2,1)} %copy.13, bf16[128,1,1024]{2,1,0:T(2,128)(2,1)} %copy.12, bf16[128,1,1024]{2,1,0:T(2,128)(2,1)} %copy.11), kind=kLoop, calls=%fused_computation | loop fusion | flops 4194304 | bytes 2097152 | tf_op jit(solution)/shard_map/stack | solution.py:399
  49.9 16.7 %decode.1 = (bf16[128,2304]{1,0:T(8,128)(2,1)S(1)}, bf16[128,2304]{1,0:T(8,128)(2,1)S(1)}, f32[32,2304]{1,0:T(8,128)S(1)}, f32[32,2304]{1,0:T(8,128)S(1)}, f32[3...) custom-call(s32[17]{0:T(128)S(1)} %concatenate.6.index_ref, ...), custom_call_target="tpu_custom_call" | custom-call | flops 1048576 | bytes 1024 | tf_op jit(solution)/shard_map/decode/pallas_call | solution.py:87
  70.4 2.0 %collective-permute-done.6 = bf16[128,2304]{1,0:T(8,128)(2,1)S(1)} collective-permute-done((bf16[128,2304]{1,0:T(8,128)(2,1)S(1)}, bf16[128,2304]{1,0:T(8,128)(2,1)S(1)}, u32[]{:S(2)}, u32[]{:S(2)}) %collective-permute-start.6) | collective-permute-done | bytes 589856 | tf_op jit(solution)/shard_map/ppermute | solution.py:31
  72.4 1.9 %collective-permute-start.8 = (bf16[32,2304]{1,0:T(8,128)(2,1)S(1)}, bf16[32,2304]{1,0:T(8,128)(2,1)S(1)}, u32[]{:S(2)}, u32[]{:S(2)}) collective-permute-start(bf16[32,2304]{1,0:T(8,128)(2,1)S(1)} %get-tuple-element.133), channel_id=1, source_target_pairs={{0,2},{1,3},{2,0},{3,1},{4,6},{5,7},{6,4},{7,5},{8,10},{9,11},{10,... | collective-permute-start | bytes 442376 | tf_op jit(solution)/shard_map/ppermute | solution.py:31
  74.6 4.6 %collective-permute-done.8 = bf16[32,2304]{1,0:T(8,128)(2,1)S(1)} collective-permute-done((bf16[32,2304]{1,0:T(8,128)(2,1)S(1)}, bf16[32,2304]{1,0:T(8,128)(2,1)S(1)}, u32[]{:S(2)}, u32[]{:S(2)}) %collective-permute-start.8) | collective-permute-done | bytes 147488 | tf_op jit(solution)/shard_map/ppermute | solution.py:31
  79.2 1.0 add_convert_fusion.7
  80.2 3.0 %collective-permute-start.9 = (bf16[32,2304]{1,0:T(8,128)(2,1)S(1)}, bf16[32,2304]{1,0:T(8,128)(2,1)S(1)}, u32[]{:S(2)}, u32[]{:S(2)}) collective-permute-start(bf16[32,2304]{1,0:T(8,128)(2,1)S(1)} %add_convert_fusion.7), channel_id=1, source_target_pairs={{0,4},{1,5},{2,6},{3,7},{4,0},{5,1},{6,2},{7,3},{8,12},{9,13},{10,... | collective-permute-start | bytes 442376 | tf_op jit(solution)/shard_map/ppermute | solution.py:31
  83.2 1.6 collective-permute-start.12
  85.3 3.1 %collective-permute-done.9 = bf16[32,2304]{1,0:T(8,128)(2,1)S(1)} collective-permute-done((bf16[32,2304]{1,0:T(8,128)(2,1)S(1)}, bf16[32,2304]{1,0:T(8,128)(2,1)S(1)}, u32[]{:S(2)}, u32[]{:S(2)}) %collective-permute-start.9) | collective-permute-done | bytes 147488 | tf_op jit(solution)/shard_map/ppermute | solution.py:31
  88.5 1.0 fusion.2
  89.5 2.4 %collective-permute-start.14 = (bf16[32,2304]{1,0:T(8,128)(2,1)S(1)}, bf16[32,2304]{1,0:T(8,128)(2,1)S(1)}, u32[]{:S(2)}, u32[]{:S(2)}) collective-permute-start(bf16[32,2304]{1,0:T(8,128)(2,1)S(1)} %get-tuple-element.89.refs_0_), channel_id=1, source_target_pairs={{0,4},{1,5},{2,6},{3,7},{4,0},{5,1},{6,2},{7,3},{8,12},{9,13},{10,... | collective-permute-start | bytes 442376 | tf_op jit(solution)/shard_map/ppermute | solution.py:31
  91.9 1.5 collective-permute-done.12
  94.3 7.4 %collective-permute-done.14.refs_2_ = bf16[32,2304]{1,0:T(8,128)(2,1)S(1)} collective-permute-done((bf16[32,2304]{1,0:T(8,128)(2,1)S(1)}, bf16[32,2304]{1,0:T(8,128)(2,1)S(1)}, u32[]{:S(2)}, u32[]{:S(2)}) %collective-permute-start.14) | collective-permute-done | bytes 147488 | tf_op jit(solution)/shard_map/ppermute | solution.py:31
  102.1 1.2 collective-permute-done.13
  103.9 2.9 %collective-permute-done.16.refs_3_ = bf16[32,2304]{1,0:T(8,128)(2,1)S(1)} collective-permute-done((bf16[32,2304]{1,0:T(8,128)(2,1)S(1)}, bf16[32,2304]{1,0:T(8,128)(2,1)S(1)}, u32[]{:S(2)}, u32[]{:S(2)}) %collective-permute-start.16) | collective-permute-done | bytes 147488 | tf_op jit(solution)/shard_map/ppermute | solution.py:31
  107.8 2.0 %collective-permute-start.22 = (bf16[32,2304]{1,0:T(8,128)(2,1)S(1)}, bf16[32,2304]{1,0:T(8,128)(2,1)S(1)}, u32[]{:S(2)}, u32[]{:S(2)}) collective-permute-start(bf16[32,2304]{1,0:T(8,128)(2,1)S(1)} %get-tuple-element.100.refs_0_), channel_id=1, source_target_pairs={{0,4},{1,5},{2,6},{3,7},{4,0},{5,1},{6,2},{7,3},{8,12},{9,13},{10,... | collective-permute-start | bytes 442376 | tf_op jit(solution)/shard_map/ppermute | solution.py:31
  109.9 2.0 %collective-permute-start.21 = (bf16[32,2304]{1,0:T(8,128)(2,1)S(1)}, bf16[32,2304]{1,0:T(8,128)(2,1)S(1)}, u32[]{:S(2)}, u32[]{:S(2)}) collective-permute-start(bf16[32,2304]{1,0:T(8,128)(2,1)S(1)} %get-tuple-element.100.refs_0_), channel_id=1, source_target_pairs={{0,2},{1,3},{2,0},{3,1},{4,6},{5,7},{6,4},{7,5},{8,10},{9,11},{10,... | collective-permute-start | bytes 442376 | tf_op jit(solution)/shard_map/ppermute | solution.py:31
  111.9 16.4 %gradient.2 = (bf16[2,64,1024]{2,1,0:T(8,128)(2,1)S(1)}, bf16[2,64,1024]{2,1,0:T(8,128)(2,1)S(1)}, f32[2,64,1024]{2,1,0:T(8,128)S(1)}, f32[2,64,1024]{2,1,0:T(8,...) custom-call(s32[17]{0:T(128)S(1)} %concatenate.6.index_ref, ...), custom_call_target="tpu_custom_call" | custom-call | flops 1048576 | bytes 1024 | tf_op jit(solution)/shard_map/gradient/pallas_call | solution.py:87
  128.3 1.4 collective-permute-start.29
  129.7 1.2 collective-permute-start.28
  132.0 5.1 %collective-permute-done.29 = bf16[2,64,1024]{2,1,0:T(8,128)(2,1)S(1)} collective-permute-done((bf16[2,64,1024]{2,1,0:T(8,128)(2,1)S(1)}, bf16[2,64,1024]{2,1,0:T(8,128)(2,1)S(1)}, u32[]{:S(2)}, u32[]{:S(2)}) %collective-permute-start.29) | collective-permute-done | bytes 262176 | tf_op jit(solution)/shard_map/ppermute | solution.py:31
  137.0 1.4 collective-permute-start.37
  139.1 1.2 collective-permute-start.36
  140.4 1.0 collective-permute-start.39
  142.1 16.6 %gradient.3 = (bf16[2,64,1024]{2,1,0:T(8,128)(2,1)S(1)}, bf16[2,64,1024]{2,1,0:T(8,128)(2,1)S(1)}, f32[2,64,1024]{2,1,0:T(8,128)S(1)}, f32[2,64,1024]{2,1,0:T(8,...) custom-call(s32[17]{0:T(128)S(1)} %concatenate.6.index_ref, ...), custom_call_target="tpu_custom_call" | custom-call | flops 1048576 | bytes 1024 | tf_op jit(solution)/shard_map/gradient/pallas_call | solution.py:87
  158.7 1.4 collective-permute-start.31
  160.1 1.1 collective-permute-start.30
  163.2 1.2 finish.2.refs_4_
  164.4 3.6 %collective-permute-done.31 = bf16[2,64,1024]{2,1,0:T(8,128)(2,1)S(1)} collective-permute-done((bf16[2,64,1024]{2,1,0:T(8,128)(2,1)S(1)}, bf16[2,64,1024]{2,1,0:T(8,128)(2,1)S(1)}, u32[]{:S(2)}, u32[]{:S(2)}) %collective-permute-start.31) | collective-permute-done | bytes 262176 | tf_op jit(solution)/shard_map/ppermute | solution.py:31
  168.0 1.3 collective-permute-done.30
  169.5 1.1 collective-permute-start.41
  172.6 1.0 collective-permute-start.32
  173.7 5.4 %collective-permute-done.32 = f32[8,128]{1,0:T(8,128)S(1)} collective-permute-done((f32[8,128]{1,0:T(8,128)S(1)}, f32[8,128]{1,0:T(8,128)S(1)}, u32[]{:S(2)}, u32[]{:S(2)}) %collective-permute-start.32) | collective-permute-done | bytes 4128 | tf_op jit(solution)/shard_map/ppermute | solution.py:31
  180.6 2.9 %collective-permute-done.33 = f32[8,128]{1,0:T(8,128)S(1)} collective-permute-done((f32[8,128]{1,0:T(8,128)S(1)}, f32[8,128]{1,0:T(8,128)S(1)}, u32[]{:S(2)}, u32[]{:S(2)}) %collective-permute-start.33) | collective-permute-done | bytes 4128 | tf_op jit(solution)/shard_map/ppermute | solution.py:31
  185.3 1.2 finish.3
  (101 shorter events, 18.1 us)
Async XLA Ops:
  6.2 18.1 %copy-start = (bf16[2,128,1024]{2,1,0:T(8,128)(2,1)S(1)}, bf16[2,128,1024]{2,1,0:T(8,128)(2,1)}, u32[]{:S(2)}) copy-start(bf16[2,128,1024]{2,1,0:T(8,128)(2,1)} %encode.2.refs_0_) | copy-start | bytes 1572868
  6.2 15.1 %collective-permute-start = (bf16[2,128,1024]{2,1,0:T(8,128)(2,1)}, bf16[2,128,1024]{2,1,0:T(8,128)(2,1)S(1)}, u32[]{:S(2)}, u32[]{:S(2)}) collective-permute-start(bf16[2,128,1024]{2,1,0:T(8,128)(2,1)} %encode.2.refs_0_), channel_id=1, source_target_pairs={{0,8},{8,0},{16,24},{24,16},{1,9},{9,1},{17,25},{25,17},{2,10},{10... | collective-permute-start | bytes 1572872 | tf_op jit(solution)/shard_map/ppermute | solution.py:31
  9.2 13.6 %collective-permute-start.1 = (bf16[2,128,1024]{2,1,0:T(8,128)(2,1)}, bf16[2,128,1024]{2,1,0:T(8,128)(2,1)S(1)}, u32[]{:S(2)}, u32[]{:S(2)}) collective-permute-start(bf16[2,128,1024]{2,1,0:T(8,128)(2,1)} %encode.2.refs_0_), channel_id=1, source_target_pairs={{0,16},{8,24},{16,0},{24,8},{1,17},{9,25},{17,1},{25,9},{2,18},{10... | collective-permute-start | bytes 1572872 | tf_op jit(solution)/shard_map/ppermute | solution.py:31
  22.8 15.1 %collective-permute-start.4 = (bf16[2,128,1024]{2,1,0:T(8,128)(2,1)}, bf16[2,128,1024]{2,1,0:T(8,128)(2,1)S(1)}, u32[]{:S(2)}, u32[]{:S(2)}) collective-permute-start(bf16[2,128,1024]{2,1,0:T(8,128)(2,1)} %encode.3.refs_4_), channel_id=1, source_target_pairs={{0,16},{8,24},{16,0},{24,8},{1,17},{9,25},{17,1},{25,9},{2,18},{10... | collective-permute-start | bytes 1572872 | tf_op jit(solution)/shard_map/ppermute | solution.py:31
  24.4 20.5 %copy-start.13 = (s32[4,1]{0,1:T(1,128)S(1)}, s32[4,1]{0,1:T(1,128)}, u32[]{:S(2)}) copy-start(s32[4,1]{0,1:T(1,128)} %param.11) | copy-start | bytes 52
  24.4 25.5 %collective-permute-start.3 = (bf16[2,128,1024]{2,1,0:T(8,128)(2,1)}, bf16[2,128,1024]{2,1,0:T(8,128)(2,1)S(1)}, u32[]{:S(2)}, u32[]{:S(2)}) collective-permute-start(bf16[2,128,1024]{2,1,0:T(8,128)(2,1)} %encode.3.refs_4_), channel_id=1, source_target_pairs={{0,8},{8,0},{16,24},{24,16},{1,9},{9,1},{17,25},{25,17},{2,10},{10... | collective-permute-start | bytes 1572872 | tf_op jit(solution)/shard_map/ppermute | solution.py:31
  25.0 24.9 %collective-permute-start.2 = (bf16[2,128,1024]{2,1,0:T(8,128)(2,1)S(1)}, bf16[2,128,1024]{2,1,0:T(8,128)(2,1)}, u32[]{:S(2)}, u32[]{:S(2)}) collective-permute-start(bf16[2,128,1024]{2,1,0:T(8,128)(2,1)S(1)} %collective-permute-done.refs_1_), channel_id=1, source_target_pairs={{0,16},{8,24},{16,0},{24,8},{1,17},{9,25},{17,1},{25,9},{2,18},{10... | collective-permute-start | bytes 1572872 | tf_op jit(solution)/shard_map/ppermute | solution.py:31
  37.9 12.0 %collective-permute-start.5 = (bf16[2,128,1024]{2,1,0:T(8,128)(2,1)S(1)}, bf16[2,128,1024]{2,1,0:T(8,128)(2,1)}, u32[]{:S(2)}, u32[]{:S(2)}) collective-permute-start(bf16[2,128,1024]{2,1,0:T(8,128)(2,1)S(1)} %collective-permute-done.4.refs_6_), channel_id=1, source_target_pairs={{0,8},{8,0},{16,24},{24,16},{1,9},{9,1},{17,25},{25,17},{2,10},{10... | collective-permute-start | bytes 1572872 | tf_op jit(solution)/shard_map/ppermute | solution.py:31
  70.3 12.9 %copy-start.7 = (f32[32,2304]{1,0:T(8,128)S(1)}, f32[32,2304]{1,0:T(8,128)}, u32[]{:S(2)}) copy-start(f32[32,2304]{1,0:T(8,128)} %copy-done.6) | copy-start | bytes 884740
  70.3 12.9 %copy-start.9 = (f32[32,2304]{1,0:T(8,128)S(1)}, f32[32,2304]{1,0:T(8,128)}, u32[]{:S(2)}) copy-start(f32[32,2304]{1,0:T(8,128)} %copy-done.8) | copy-start | bytes 884740
  70.3 18.2 %copy-start.5 = (f32[32,2304]{1,0:T(8,128)S(1)}, f32[32,2304]{1,0:T(8,128)}, u32[]{:S(2)}) copy-start(f32[32,2304]{1,0:T(8,128)} %copy-done.4) | copy-start | bytes 884740
  70.3 2.1 %collective-permute-start.6 = (bf16[128,2304]{1,0:T(8,128)(2,1)S(1)}, bf16[128,2304]{1,0:T(8,128)(2,1)S(1)}, u32[]{:S(2)}, u32[]{:S(2)}) collective-permute-start(bf16[128,2304]{1,0:T(8,128)(2,1)S(1)} %get-tuple-element.77), channel_id=1, source_target_pairs={{0,1},{1,0},{2,3},{3,2},{4,5},{5,4},{6,7},{7,6},{8,9},{9,8},{10,11... | collective-permute-start | bytes 1769480 | tf_op jit(solution)/shard_map/ppermute | solution.py:31
  72.4 21.1 %copy-start.3 = (f32[32,2304]{1,0:T(8,128)S(1)}, f32[32,2304]{1,0:T(8,128)}, u32[]{:S(2)}) copy-start(f32[32,2304]{1,0:T(8,128)} %copy-done.2) | copy-start | bytes 884740
  72.4 6.7 %collective-permute-start.8 = (bf16[32,2304]{1,0:T(8,128)(2,1)S(1)}, bf16[32,2304]{1,0:T(8,128)(2,1)S(1)}, u32[]{:S(2)}, u32[]{:S(2)}) collective-permute-start(bf16[32,2304]{1,0:T(8,128)(2,1)S(1)} %get-tuple-element.133), channel_id=1, source_target_pairs={{0,2},{1,3},{2,0},{3,1},{4,6},{5,7},{6,4},{7,5},{8,10},{9,11},{10,... | collective-permute-start | bytes 442376 | tf_op jit(solution)/shard_map/ppermute | solution.py:31
  74.4 8.8 %collective-permute-start.10 = (bf16[128,2304]{1,0:T(8,128)(2,1)}, bf16[128,2304]{1,0:T(8,128)(2,1)S(1)}, u32[]{:S(2)}, u32[]{:S(2)}) collective-permute-start(bf16[128,2304]{1,0:T(8,128)(2,1)} %copy-done.11), channel_id=1, source_target_pairs={{0,1},{1,0},{2,3},{3,2},{4,5},{5,4},{6,7},{7,6},{8,9},{9,8},{10,11... | collective-permute-start | bytes 1769480 | tf_op jit(solution)/shard_map/ppermute | solution.py:31
  74.4 11.0 %collective-permute-start.7 = (bf16[32,2304]{1,0:T(8,128)(2,1)S(1)}, bf16[32,2304]{1,0:T(8,128)(2,1)S(1)}, u32[]{:S(2)}, u32[]{:S(2)}) collective-permute-start(bf16[32,2304]{1,0:T(8,128)(2,1)S(1)} %get-tuple-element.132), channel_id=1, source_target_pairs={{0,2},{1,3},{2,0},{3,1},{4,6},{5,7},{6,4},{7,5},{8,10},{9,11},{10,... | collective-permute-start | bytes 442376 | tf_op jit(solution)/shard_map/ppermute | solution.py:31
  80.2 8.3 %collective-permute-start.9 = (bf16[32,2304]{1,0:T(8,128)(2,1)S(1)}, bf16[32,2304]{1,0:T(8,128)(2,1)S(1)}, u32[]{:S(2)}, u32[]{:S(2)}) collective-permute-start(bf16[32,2304]{1,0:T(8,128)(2,1)S(1)} %add_convert_fusion.7), channel_id=1, source_target_pairs={{0,4},{1,5},{2,6},{3,7},{4,0},{5,1},{6,2},{7,3},{8,12},{9,13},{10,... | collective-permute-start | bytes 442376 | tf_op jit(solution)/shard_map/ppermute | solution.py:31
  83.2 10.2 %collective-permute-start.12 = (bf16[32,2304]{1,0:T(8,128)(2,1)S(1)}, bf16[32,2304]{1,0:T(8,128)(2,1)S(1)}, u32[]{:S(2)}, u32[]{:S(2)}) collective-permute-start(bf16[32,2304]{1,0:T(8,128)(2,1)S(1)} %get-tuple-element.87), channel_id=1, source_target_pairs={{0,2},{1,3},{2,0},{3,1},{4,6},{5,7},{6,4},{7,5},{8,10},{9,11},{10,... | collective-permute-start | bytes 442376 | tf_op jit(solution)/shard_map/ppermute | solution.py:31
  84.8 17.3 %collective-permute-start.11 = (bf16[32,2304]{1,0:T(8,128)(2,1)S(1)}, bf16[32,2304]{1,0:T(8,128)(2,1)S(1)}, u32[]{:S(2)}, u32[]{:S(2)}) collective-permute-start(bf16[32,2304]{1,0:T(8,128)(2,1)S(1)} %get-tuple-element.85), channel_id=1, source_target_pairs={{0,2},{1,3},{2,0},{3,1},{4,6},{5,7},{6,4},{7,5},{8,10},{9,11},{10,... | collective-permute-start | bytes 442376 | tf_op jit(solution)/shard_map/ppermute | solution.py:31
  89.5 12.2 %collective-permute-start.14 = (bf16[32,2304]{1,0:T(8,128)(2,1)S(1)}, bf16[32,2304]{1,0:T(8,128)(2,1)S(1)}, u32[]{:S(2)}, u32[]{:S(2)}) collective-permute-start(bf16[32,2304]{1,0:T(8,128)(2,1)S(1)} %get-tuple-element.89.refs_0_), channel_id=1, source_target_pairs={{0,4},{1,5},{2,6},{3,7},{4,0},{5,1},{6,2},{7,3},{8,12},{9,13},{10,... | collective-permute-start | bytes 442376 | tf_op jit(solution)/shard_map/ppermute | solution.py:31
  93.5 9.8 %collective-permute-start.13 = (bf16[32,2304]{1,0:T(8,128)(2,1)S(1)}, bf16[32,2304]{1,0:T(8,128)(2,1)S(1)}, u32[]{:S(2)}, u32[]{:S(2)}) collective-permute-start(bf16[32,2304]{1,0:T(8,128)(2,1)S(1)} %add_convert_fusion.4), channel_id=1, source_target_pairs={{0,4},{1,5},{2,6},{3,7},{4,0},{5,1},{6,2},{7,3},{8,12},{9,13},{10,... | collective-permute-start | bytes 442376 | tf_op jit(solution)/shard_map/ppermute | solution.py:31
  93.6 9.9 %collective-permute-start.15 = (bf16[32,2304]{1,0:T(8,128)(2,1)S(1)}, bf16[32,2304]{1,0:T(8,128)(2,1)S(1)}, u32[]{:S(2)}, u32[]{:S(2)}) collective-permute-start(bf16[32,2304]{1,0:T(8,128)(2,1)S(1)} %get-tuple-element.89.refs_0_), channel_id=1, source_target_pairs={{0,2},{1,3},{2,0},{3,1},{4,6},{5,7},{6,4},{7,5},{8,10},{9,11},{10,... | collective-permute-start | bytes 442376 | tf_op jit(solution)/shard_map/ppermute | solution.py:31
  94.3 15.6 %collective-permute-start.17 = (bf16[32,2304]{1,0:T(8,128)(2,1)S(1)}, bf16[32,2304]{1,0:T(8,128)(2,1)S(1)}, u32[]{:S(2)}, u32[]{:S(2)}) collective-permute-start(bf16[32,2304]{1,0:T(8,128)(2,1)S(1)} %get-tuple-element.89.refs_0_), channel_id=1, source_target_pairs={{0,1},{1,0},{2,3},{3,2},{4,5},{5,4},{6,7},{7,6},{8,9},{9,8},{10,11... | collective-permute-start | bytes 442376 | tf_op jit(solution)/shard_map/ppermute | solution.py:31
  101.7 5.1 %collective-permute-start.16 = (bf16[32,2304]{1,0:T(8,128)(2,1)S(1)}, bf16[32,2304]{1,0:T(8,128)(2,1)S(1)}, u32[]{:S(2)}, u32[]{:S(2)}) collective-permute-start(bf16[32,2304]{1,0:T(8,128)(2,1)S(1)} %collective-permute-done.14.refs_2_), channel_id=1, source_target_pairs={{0,2},{1,3},{2,0},{3,1},{4,6},{5,7},{6,4},{7,5},{8,10},{9,11},{10,... | collective-permute-start | bytes 442376 | tf_op jit(solution)/shard_map/ppermute | solution.py:31
  103.4 8.5 %collective-permute-start.19 = (bf16[32,2304]{1,0:T(8,128)(2,1)S(1)}, bf16[32,2304]{1,0:T(8,128)(2,1)S(1)}, u32[]{:S(2)}, u32[]{:S(2)}) collective-permute-start(bf16[32,2304]{1,0:T(8,128)(2,1)S(1)} %collective-permute-done.14.refs_2_), channel_id=1, source_target_pairs={{0,1},{1,0},{2,3},{3,2},{4,5},{5,4},{6,7},{7,6},{8,9},{9,8},{10,11... | collective-permute-start | bytes 442376 | tf_op jit(solution)/shard_map/ppermute | solution.py:31
  103.5 8.4 %collective-permute-start.18 = (bf16[32,2304]{1,0:T(8,128)(2,1)S(1)}, bf16[32,2304]{1,0:T(8,128)(2,1)S(1)}, u32[]{:S(2)}, u32[]{:S(2)}) collective-permute-start(bf16[32,2304]{1,0:T(8,128)(2,1)S(1)} %collective-permute-done.15.refs_1_), channel_id=1, source_target_pairs={{0,1},{1,0},{2,3},{3,2},{4,5},{5,4},{6,7},{7,6},{8,9},{9,8},{10,11... | collective-permute-start | bytes 442376 | tf_op jit(solution)/shard_map/ppermute | solution.py:31
  106.9 5.0 %collective-permute-start.20 = (bf16[32,2304]{1,0:T(8,128)(2,1)S(1)}, bf16[32,2304]{1,0:T(8,128)(2,1)S(1)}, u32[]{:S(2)}, u32[]{:S(2)}) collective-permute-start(bf16[32,2304]{1,0:T(8,128)(2,1)S(1)} %collective-permute-done.16.refs_3_), channel_id=1, source_target_pairs={{0,1},{1,0},{2,3},{3,2},{4,5},{5,4},{6,7},{7,6},{8,9},{9,8},{10,11... | collective-permute-start | bytes 442376 | tf_op jit(solution)/shard_map/ppermute | solution.py:31
  107.8 23.9 %collective-permute-start.22 = (bf16[32,2304]{1,0:T(8,128)(2,1)S(1)}, bf16[32,2304]{1,0:T(8,128)(2,1)S(1)}, u32[]{:S(2)}, u32[]{:S(2)}) collective-permute-start(bf16[32,2304]{1,0:T(8,128)(2,1)S(1)} %get-tuple-element.100.refs_0_), channel_id=1, source_target_pairs={{0,4},{1,5},{2,6},{3,7},{4,0},{5,1},{6,2},{7,3},{8,12},{9,13},{10,... | collective-permute-start | bytes 442376 | tf_op jit(solution)/shard_map/ppermute | solution.py:31
  109.9 28.6 %collective-permute-start.21 = (bf16[32,2304]{1,0:T(8,128)(2,1)S(1)}, bf16[32,2304]{1,0:T(8,128)(2,1)S(1)}, u32[]{:S(2)}, u32[]{:S(2)}) collective-permute-start(bf16[32,2304]{1,0:T(8,128)(2,1)S(1)} %get-tuple-element.100.refs_0_), channel_id=1, source_target_pairs={{0,2},{1,3},{2,0},{3,1},{4,6},{5,7},{6,4},{7,5},{8,10},{9,11},{10,... | collective-permute-start | bytes 442376 | tf_op jit(solution)/shard_map/ppermute | solution.py:31
  111.9 26.7 %collective-permute-start.24 = (bf16[32,2304]{1,0:T(8,128)(2,1)S(1)}, bf16[32,2304]{1,0:T(8,128)(2,1)S(1)}, u32[]{:S(2)}, u32[]{:S(2)}) collective-permute-start(bf16[32,2304]{1,0:T(8,128)(2,1)S(1)} %get-tuple-element.100.refs_0_), channel_id=1, source_target_pairs={{0,1},{1,0},{2,3},{3,2},{4,5},{5,4},{6,7},{7,6},{8,9},{9,8},{10,11... | collective-permute-start | bytes 442376 | tf_op jit(solution)/shard_map/ppermute | solution.py:31
  128.3 8.8 %collective-permute-start.29 = (bf16[2,64,1024]{2,1,0:T(8,128)(2,1)S(1)}, bf16[2,64,1024]{2,1,0:T(8,128)(2,1)S(1)}, u32[]{:S(2)}, u32[]{:S(2)}) collective-permute-start(bf16[2,64,1024]{2,1,0:T(8,128)(2,1)S(1)} %get-tuple-element.99), channel_id=1, source_target_pairs={{0,16},{8,24},{16,0},{24,8},{1,17},{9,25},{17,1},{25,9},{2,18},{10... | collective-permute-start | bytes 786440 | tf_op jit(solution)/shard_map/ppermute | solution.py:31
  129.7 10.6 %collective-permute-start.28 = (bf16[2,64,1024]{2,1,0:T(8,128)(2,1)S(1)}, bf16[2,64,1024]{2,1,0:T(8,128)(2,1)S(1)}, u32[]{:S(2)}, u32[]{:S(2)}) collective-permute-start(bf16[2,64,1024]{2,1,0:T(8,128)(2,1)S(1)} %get-tuple-element.98), channel_id=1, source_target_pairs={{0,8},{8,0},{16,24},{24,16},{1,9},{9,1},{17,25},{25,17},{2,10},{10... | collective-permute-start | bytes 786440 | tf_op jit(solution)/shard_map/ppermute | solution.py:31
  131.7 7.4 %collective-permute-start.23 = (bf16[32,2304]{1,0:T(8,128)(2,1)S(1)}, bf16[32,2304]{1,0:T(8,128)(2,1)S(1)}, u32[]{:S(2)}, u32[]{:S(2)}) collective-permute-start(bf16[32,2304]{1,0:T(8,128)(2,1)S(1)} %collective-permute-done.22.refs_2_), channel_id=1, source_target_pairs={{0,2},{1,3},{2,0},{3,1},{4,6},{5,7},{6,4},{7,5},{8,10},{9,11},{10,... | collective-permute-start | bytes 442376 | tf_op jit(solution)/shard_map/ppermute | solution.py:31
  137.0 23.1 %collective-permute-start.37 = (bf16[2,64,1024]{2,1,0:T(8,128)(2,1)S(1)}, bf16[2,64,1024]{2,1,0:T(8,128)(2,1)S(1)}, u32[]{:S(2)}, u32[]{:S(2)}) collective-permute-start(bf16[2,64,1024]{2,1,0:T(8,128)(2,1)S(1)} %get-tuple-element.126), channel_id=1, source_target_pairs={{0,16},{8,24},{16,0},{24,8},{1,17},{9,25},{17,1},{25,9},{2,18},{10... | collective-permute-start | bytes 786440 | tf_op jit(solution)/shard_map/ppermute | solution.py:31
  138.5 2.9 %collective-permute-start.26 = (bf16[32,2304]{1,0:T(8,128)(2,1)S(1)}, bf16[32,2304]{1,0:T(8,128)(2,1)S(1)}, u32[]{:S(2)}, u32[]{:S(2)}) collective-permute-start(bf16[32,2304]{1,0:T(8,128)(2,1)S(1)} %collective-permute-done.22.refs_2_), channel_id=1, source_target_pairs={{0,1},{1,0},{2,3},{3,2},{4,5},{5,4},{6,7},{7,6},{8,9},{9,8},{10,11... | collective-permute-start | bytes 442376 | tf_op jit(solution)/shard_map/ppermute | solution.py:31
  138.6 1.8 collective-permute-start.25
  139.1 22.2 %collective-permute-start.36 = (bf16[2,64,1024]{2,1,0:T(8,128)(2,1)S(1)}, bf16[2,64,1024]{2,1,0:T(8,128)(2,1)S(1)}, u32[]{:S(2)}, u32[]{:S(2)}) collective-permute-start(bf16[2,64,1024]{2,1,0:T(8,128)(2,1)S(1)} %get-tuple-element.124), channel_id=1, source_target_pairs={{0,8},{8,0},{16,24},{24,16},{1,9},{9,1},{17,25},{25,17},{2,10},{10... | collective-permute-start | bytes 786440 | tf_op jit(solution)/shard_map/ppermute | solution.py:31
  140.3 1.8 collective-permute-start.27
  140.4 21.8 %collective-permute-start.39 = (bf16[2,64,1024]{2,1,0:T(8,128)(2,1)S(1)}, bf16[2,64,1024]{2,1,0:T(8,128)(2,1)S(1)}, u32[]{:S(2)}, u32[]{:S(2)}) collective-permute-start(bf16[2,64,1024]{2,1,0:T(8,128)(2,1)S(1)} %add_convert_fusion.2), channel_id=1, source_target_pairs={{0,8},{8,0},{16,24},{24,16},{1,9},{9,1},{17,25},{25,17},{2,10},{10... | collective-permute-start | bytes 786440 | tf_op jit(solution)/shard_map/ppermute | solution.py:31
  141.4 21.8 %collective-permute-start.38 = (bf16[2,64,1024]{2,1,0:T(8,128)(2,1)S(1)}, bf16[2,64,1024]{2,1,0:T(8,128)(2,1)S(1)}, u32[]{:S(2)}, u32[]{:S(2)}) collective-permute-start(bf16[2,64,1024]{2,1,0:T(8,128)(2,1)S(1)} %add_convert_fusion.3), channel_id=1, source_target_pairs={{0,16},{8,24},{16,0},{24,8},{1,17},{9,25},{17,1},{25,9},{2,18},{10... | collective-permute-start | bytes 786440 | tf_op jit(solution)/shard_map/ppermute | solution.py:31
  158.7 9.3 %collective-permute-start.31 = (bf16[2,64,1024]{2,1,0:T(8,128)(2,1)S(1)}, bf16[2,64,1024]{2,1,0:T(8,128)(2,1)S(1)}, u32[]{:S(2)}, u32[]{:S(2)}) collective-permute-start(bf16[2,64,1024]{2,1,0:T(8,128)(2,1)S(1)} %get-tuple-element.116), channel_id=1, source_target_pairs={{0,16},{8,24},{16,0},{24,8},{1,17},{9,25},{17,1},{25,9},{2,18},{10... | collective-permute-start | bytes 786440 | tf_op jit(solution)/shard_map/ppermute | solution.py:31
  160.1 9.2 %collective-permute-start.30 = (bf16[2,64,1024]{2,1,0:T(8,128)(2,1)S(1)}, bf16[2,64,1024]{2,1,0:T(8,128)(2,1)S(1)}, u32[]{:S(2)}, u32[]{:S(2)}) collective-permute-start(bf16[2,64,1024]{2,1,0:T(8,128)(2,1)S(1)} %get-tuple-element.113), channel_id=1, source_target_pairs={{0,8},{8,0},{16,24},{24,16},{1,9},{9,1},{17,25},{25,17},{2,10},{10... | collective-permute-start | bytes 786440 | tf_op jit(solution)/shard_map/ppermute | solution.py:31
  161.3 12.4 %collective-permute-start.35 = (bf16[2,64,1024]{2,1,0:T(8,128)(2,1)S(1)}, bf16[2,64,1024]{2,1,0:T(8,128)(2,1)S(1)}, u32[]{:S(2)}, u32[]{:S(2)}) collective-permute-start(bf16[2,64,1024]{2,1,0:T(8,128)(2,1)S(1)} %get-tuple-element.121), channel_id=1, source_target_pairs={{0,16},{8,24},{16,0},{24,8},{1,17},{9,25},{17,1},{25,9},{2,18},{10... | collective-permute-start | bytes 786440 | tf_op jit(solution)/shard_map/ppermute | solution.py:31
  162.2 18.4 %collective-permute-start.34 = (bf16[2,64,1024]{2,1,0:T(8,128)(2,1)S(1)}, bf16[2,64,1024]{2,1,0:T(8,128)(2,1)S(1)}, u32[]{:S(2)}, u32[]{:S(2)}) collective-permute-start(bf16[2,64,1024]{2,1,0:T(8,128)(2,1)S(1)} %get-tuple-element.119), channel_id=1, source_target_pairs={{0,8},{8,0},{16,24},{24,16},{1,9},{9,1},{17,25},{25,17},{2,10},{10... | collective-permute-start | bytes 786440 | tf_op jit(solution)/shard_map/ppermute | solution.py:31
  169.5 15.8 %collective-permute-start.41 = (bf16[2,64,1024]{2,1,0:T(8,128)(2,1)S(1)}, bf16[2,64,1024]{2,1,0:T(8,128)(2,1)S(1)}, u32[]{:S(2)}, u32[]{:S(2)}) collective-permute-start(bf16[2,64,1024]{2,1,0:T(8,128)(2,1)S(1)} %get-tuple-element.129), channel_id=1, source_target_pairs={{0,8},{8,0},{16,24},{24,16},{1,9},{9,1},{17,25},{25,17},{2,10},{10... | collective-permute-start | bytes 786440 | tf_op jit(solution)/shard_map/ppermute | solution.py:31
  170.6 14.7 %collective-permute-start.40 = (bf16[2,64,1024]{2,1,0:T(8,128)(2,1)S(1)}, bf16[2,64,1024]{2,1,0:T(8,128)(2,1)S(1)}, u32[]{:S(2)}, u32[]{:S(2)}) collective-permute-start(bf16[2,64,1024]{2,1,0:T(8,128)(2,1)S(1)} %get-tuple-element.127), channel_id=1, source_target_pairs={{0,16},{8,24},{16,0},{24,8},{1,17},{9,25},{17,1},{25,9},{2,18},{10... | collective-permute-start | bytes 786440 | tf_op jit(solution)/shard_map/ppermute | solution.py:31
  172.6 6.5 %collective-permute-start.32 = (f32[8,128]{1,0:T(8,128)S(1)}, f32[8,128]{1,0:T(8,128)S(1)}, u32[]{:S(2)}, u32[]{:S(2)}) collective-permute-start(f32[8,128]{1,0:T(8,128)S(1)} %broadcast_in_dim.11), channel_id=1, source_target_pairs={{0,8},{8,0},{16,24},{24,16},{1,9},{9,1},{17,25},{25,17},{2,10},{10... | collective-permute-start | bytes 12296 | tf_op jit(solution)/shard_map/ppermute | solution.py:31
  179.8 3.7 %collective-permute-start.33 = (f32[8,128]{1,0:T(8,128)S(1)}, f32[8,128]{1,0:T(8,128)S(1)}, u32[]{:S(2)}, u32[]{:S(2)}) collective-permute-start(f32[8,128]{1,0:T(8,128)S(1)} %broadcast_add_fusion), channel_id=1, source_target_pairs={{0,16},{8,24},{16,0},{24,8},{1,17},{9,25},{17,1},{25,9},{2,18},{10... | collective-permute-start | bytes 12296 | tf_op jit(solution)/shard_map/ppermute | solution.py:31
  (8 other events, 15.6 us)

commit v6 on v5

--- a/solution.py
+++ b/solution.py
@@ -12,8 +12,7 @@
 F32 = jnp.float32
 WANTED_CHUNKS = 2
 ROW_TILE = 16
-IN_FLIGHT = 3
-WEIGHT_SLOTS = 5
+WEIGHT_SLOTS = 4
 VMEM_BYTES = 44 << 20
 MOST_VMEM_BYTES = 59 << 20
 SMALL_COST = pl.CostEstimate(flops=1 << 20, bytes_accessed=1 << 10, transcendentals=0)
@@ -67,20 +66,24 @@
         return kept
 
 
-class Stream:
-    def __init__(self, copies):
-        self.copies = copies
-        self.started = 0
-        self.more(IN_FLIGHT)
-
-    def more(self, count):
-        for copy in self.copies[self.started:self.started + count]:
+def streamed(count, slots, copies_of, body):
+    for i in range(min(slots - 1, count)):
+        for copy in copies_of(i, i):
             copy.start()
-        self.started += count
-
-    def wait(self, i):
-        self.copies[i].wait()
-        self.more(1)
+
+    @pl.loop(0, count)
+    def _(i):
+        ahead = i + slots - 1
+
+        @pl.when(ahead < count)
+        def _():
+            for copy in copies_of(ahead, lax.rem(ahead, slots)):
+                copy.start()
+
+        slot = lax.rem(i, slots)
+        for copy in copies_of(i, slot):
+            copy.wait()
+        body(i, slot)
 
 
 def call(kernel, name, in_specs, out_shape, scratch, args, vmem=VMEM_BYTES, **options):
@@ -96,59 +99,46 @@
     )(*args)
 
 
-def encode_kernel(plan, lane, resid_ref, w_ref, b_ref, *refs):
-    outs, (x_buf, w_buf, b_buf, total, x_sem, w_sem) = refs[:-6], refs[-6:]
-    lo, hi = plan.lane_sources[lane]
-    depth = w_buf.shape[1] // (w_sem.shape[0] // (hi - lo))
-    steps = plan.model // depth
+def encode_kernel(plan, source, resid_ref, w_ref, b_ref, out_ref, x_buf, w_buf, b_buf, x_sem, w_sem):
+    tile = w_buf.shape[2]
     near = [
-        pltpu.make_async_copy(resid_ref.at[pl.ds(lo, hi - lo)], x_buf, x_sem.at[0]),
+        pltpu.make_async_copy(resid_ref.at[source], x_buf, x_sem.at[0]),
         pltpu.make_async_copy(b_ref, b_buf, x_sem.at[1]),
     ]
-    near[0].start()
-    stream = Stream([
-        pltpu.make_async_copy(
-            w_ref.at[lo + s, pl.ds(i * depth, depth)],
-            w_buf.at[s, pl.ds(i * depth, depth)],
-            w_sem.at[s * steps + i],
-        )
-        for s in range(hi - lo)
-        for i in range(steps)
-    ])
-    near[1].start()
-    near[0].wait()
-    for s in range(hi - lo):
-        for i in range(steps):
-            stream.wait(s * steps + i)
-            part = slice(i * depth, (i + 1) * depth)
-            product = jnp.dot(
-                x_buf[s, :, part], w_buf[s, part, :], preferred_element_type=F32
-            )
-            if i:
-                product = total[...] + product
-            if i < steps - 1:
-                total[...] = product
-        if s == 0:
-            near[1].wait()
-        outs[0][s] = jnp.maximum(product + b_buf[lo + s:lo + s + 1, :], 0.0).astype(BF16)
-
-
-def encode(plan, lane, resid, w_enc, b_enc):
-    lo, hi = plan.lane_sources[lane]
-    n = hi - lo
-    steps = plan.model // pick_tile(plan.model, 768)
+    for copy in near:
+        copy.start()
+
+    def copies_of(i, slot):
+        cols = pl.ds(pl.multiple_of(i * tile, tile), tile)
+        return [pltpu.make_async_copy(w_ref.at[source, :, cols], w_buf.at[slot], w_sem.at[slot])]
+
+    def step(i, slot):
+        @pl.when(i == 0)
+        def _():
+            for copy in near:
+                copy.wait()
+
+        cols = pl.ds(pl.multiple_of(i * tile, tile), tile)
+        product = jnp.dot(x_buf[...], w_buf[slot], preferred_element_type=F32)
+        value = jnp.maximum(product + b_buf[source:source + 1, cols], 0.0)
+        out_ref[:, cols] = value.astype(BF16)
+
+    streamed(plan.width // tile, w_buf.shape[0], copies_of, step)
+
+
+def encode(plan, source, resid, w_enc, b_enc):
+    tile = pick_tile(plan.width, 256)
     return call(
-        partial(encode_kernel, plan, lane),
+        partial(encode_kernel, plan, source),
         "encode",
         [FAR, FAR, FAR],
-        jax.ShapeDtypeStruct((n, plan.rows, plan.width), BF16),
+        jax.ShapeDtypeStruct((plan.rows, plan.width), BF16),
         [
-            pltpu.VMEM((n, plan.rows, plan.model), BF16),
-            pltpu.VMEM((n, plan.model, plan.width), BF16),
+            pltpu.VMEM((plan.rows, plan.model), BF16),
+            pltpu.VMEM((WEIGHT_SLOTS + 1, plan.model, tile), BF16),
             pltpu.VMEM((plan.sources, plan.width), F32),
-            pltpu.VMEM((plan.rows, plan.width), F32),
             pltpu.SemaphoreType.DMA((2,)),
-            pltpu.SemaphoreType.DMA((n * steps,)),
+            pltpu.SemaphoreType.DMA((WEIGHT_SLOTS + 1,)),
         ],
         (resid, w_enc, b_enc),
         vmem=MOST_VMEM_BYTES,
@@ -156,95 +146,85 @@
 
 
 def decode_kernel(plan, index_ref, *refs):
-    n_in = plan.groups * len(plan.lanes)
-    pieces, w_ref, outs = refs[:n_in], refs[n_in], refs[n_in + 1:-5]
-    x_buf, w_buf, total, x_sem, w_sem = refs[-5:]
+    n_in = plan.groups * plan.sources
+    pieces, w_ref, outs = refs[:n_in], refs[n_in], refs[n_in + 1:-4]
+    x_buf, w_buf, x_sem, w_sem = refs[-4:]
     half = plan.tokens // 2
     core = index_ref[0]
-    depth = w_buf.shape[1]
-    steps = plan.width // depth
+    tile = w_buf.shape[2]
 
     placing = []
-    for lane, (lo, hi) in enumerate(plan.lane_sources):
-        for j in range(plan.groups):
-            for b in range(plan.pairs):
-                place = index_ref[1 + plan.sources + j * plan.pairs + b] * plan.rows_feat
-                for owner in range(2):
-                    to = pl.multiple_of(place + jnp.where(core == owner, half, 0), ROW_TILE)
+    for j in range(plan.groups):
+        for b in range(plan.pairs):
+            place = index_ref[1 + plan.sources + j * plan.pairs + b] * plan.rows_feat
+            for owner in range(2):
+                to = pl.multiple_of(place + jnp.where(core == owner, half, 0), ROW_TILE)
+                for s in range(plan.sources):
                     placing.append(pltpu.make_async_copy(
-                        pieces[lane * plan.groups + j].at[
-                            :, pl.ds((2 * b + owner) * plan.rows_feat, plan.rows_feat)
+                        pieces[s * plan.groups + j].at[
+                            pl.ds((2 * b + owner) * plan.rows_feat, plan.rows_feat)
                         ],
-                        x_buf.at[pl.ds(lo, hi - lo), pl.ds(to, plan.rows_feat)],
+                        x_buf.at[
+                            pl.ds(to, plan.rows_feat), pl.ds(s * plan.width, plan.width)
+                        ],
                         x_sem.at[len(placing)],
                     ))
     for copy in placing:
         copy.start()
-    stream = Stream([
-        pltpu.make_async_copy(
-            w_ref.at[s, 0, pl.ds(i * depth, depth)],
-            w_buf.at[(s * steps + i) % w_buf.shape[0]],
-            w_sem.at[s * steps + i],
-        )
-        for s in range(plan.sources)
-        for i in range(steps)
-    ])
-    for copy in placing:
-        copy.wait()
-    for s in range(plan.sources):
-        @pl.when(index_ref[1 + s] == 0)
-        def _(s=s):
-            x_buf[s] = jnp.zeros(x_buf.shape[1:], BF16)
-
-    tile = pick_tile(plan.model, 768)
-    for s in range(plan.sources):
-        for i in range(steps):
-            stream.wait(s * steps + i)
-            w_ref = w_buf.at[(s * steps + i) % w_buf.shape[0]]
-            part = slice(i * depth, (i + 1) * depth)
-            last = s * steps + i == plan.sources * steps - 1
-            for n in range(0, plan.model, tile):
-                cols = slice(n, n + tile)
-                product = jnp.dot(
-                    x_buf[s, :, part], w_ref[:, cols], preferred_element_type=F32
-                )
-                if s + i:
-                    product = total[:, cols] + product
-                if not last:
-                    total[:, cols] = product
-                    continue
-                for c in range(plan.chunks):
-                    for d in range(plan.depth):
-                        first = d * plan.rows_feat + c * plan.piece
-                        outs[c][d * plan.piece:(d + 1) * plan.piece, cols] = (
-                            product[first:first + plan.piece].astype(BF16)
-                        )
-                        outs[plan.chunks + c * plan.depth + d][:, cols] = (
-                            product[half + first:half + first + plan.piece]
-                        )
+
+    def copies_of(i, slot):
+        cols = pl.ds(pl.multiple_of(i * tile, tile), tile)
+        return [
+            pltpu.make_async_copy(
+                w_ref.at[s, 0, :, cols],
+                w_buf.at[slot, pl.ds(s * plan.width, plan.width)],
+                w_sem.at[slot, s],
+            )
+            for s in range(plan.sources)
+        ]
+
+    def step(i, slot):
+        @pl.when(i == 0)
+        def _():
+            for copy in placing:
+                copy.wait()
+            for s in range(plan.sources):
+                @pl.when(index_ref[1 + s] == 0)
+                def _(s=s):
+                    x_buf[:, s * plan.width:(s + 1) * plan.width] = jnp.zeros(
+                        (plan.tokens, plan.width), BF16
+                    )
+
+        cols = pl.ds(pl.multiple_of(i * tile, tile), tile)
+        product = jnp.dot(x_buf[...], w_buf[slot], preferred_element_type=F32)
+        for c in range(plan.chunks):
+            for d in range(plan.depth):
+                first = d * plan.rows_feat + c * plan.piece
+                to = slice(d * plan.piece, (d + 1) * plan.piece)
+                outs[c][to, cols] = product[first:first + plan.piece].astype(BF16)
+                outs[plan.chunks + c][to, cols] = product[half + first:half + first + plan.piece]
+
+    streamed(plan.model // tile, w_buf.shape[0], copies_of, step)
 
 
 def decode(plan, index, pieces, w_dec):
-    step = pick_tile(plan.width, 512)
-    steps = plan.width // step
-    chunks, depth = plan.chunks, plan.depth
+    tile = pick_tile(plan.model, 256)
+    shape = (plan.depth * plan.piece, plan.model)
     outs = call(
         partial(decode_kernel, plan),
         "decode",
         [SCALARS] + [ANYWHERE] * len(pieces) + [FAR],
-        [jax.ShapeDtypeStruct((depth * plan.piece, plan.model), BF16)] * chunks
-        + [jax.ShapeDtypeStruct((plan.piece, plan.model), F32)] * (chunks * depth),
+        [jax.ShapeDtypeStruct(shape, BF16)] * plan.chunks
+        + [jax.ShapeDtypeStruct(shape, F32)] * plan.chunks,
         [
-            pltpu.VMEM((plan.sources, plan.tokens, plan.width), BF16),
-            pltpu.VMEM((WEIGHT_SLOTS, step, plan.model), BF16),
-            pltpu.VMEM((plan.tokens, plan.model), F32),
+            pltpu.VMEM((plan.tokens, plan.sources * plan.width), BF16),
+            pltpu.VMEM((WEIGHT_SLOTS, plan.sources * plan.width, tile), BF16),
             pltpu.SemaphoreType.DMA((len(pieces) * plan.per_group,)),
-            pltpu.SemaphoreType.DMA((plan.sources * steps,)),
+            pltpu.SemaphoreType.DMA((WEIGHT_SLOTS, plan.sources)),
         ],
         (index, *pieces, w_dec),
     )
-    sends, keeps = outs[:chunks], outs[chunks:]
-    return sends, [keeps[c * depth:(c + 1) * depth] for c in range(chunks)]
+    return outs[:plan.chunks], outs[plan.chunks:]
 
 
 def gradient_kernel(plan, index_ref, *refs):
@@ -267,49 +247,55 @@
     ]
     for copy in placing:
         copy.start()
-    stream = Stream([
-        pltpu.make_async_copy(
-            w_ref.at[s, 0, pl.ds(i * depth, depth)],
-            w_buf.at[s, pl.ds(i * depth, depth)],
-            w_sem.at[s * steps + i],
+    def copies_of(i, slot):
+        rows = pl.ds(pl.multiple_of(lax.rem(i, steps) * depth, depth), depth)
+        return [pltpu.make_async_copy(
+            w_ref.at[lax.div(i, steps), 0, rows], w_buf.at[slot], w_sem.at[slot]
+        )]
+
+    half = plan.groups // 2
+
+    def step(i, slot):
+        @pl.when(i == 0)
+        def _():
+            for copy in placing:
+                copy.wait()
+
+        source = lax.div(i, steps)
+        cols = pl.ds(pl.multiple_of(lax.rem(i, steps) * depth, depth), depth)
+        product = lax.dot_general(
+            e_buf[...], w_buf[slot], (((1,), (1,)), ((), ())), preferred_element_type=F32
         )
-        for s in range(plan.sources)
-        for i in range(steps)
-    ])
-    for copy in placing:
-        copy.wait()
-
-    half = plan.groups // 2
-    for lane, (lo, hi) in enumerate(plan.lane_sources):
-        first, kept = plan.lanes[lane][0], plan.kept_order(lane)
-        away, keep = outs[2 * lane * half:][:half], outs[(2 * lane + 1) * half:][:half]
-        for s in range(lo, hi):
-            feeds = index_ref[1 + s] > 0
-            for i in range(steps):
-                stream.wait(s * steps + i)
-                part = slice(i * depth, (i + 1) * depth)
-                product = lax.dot_general(
-                    e_buf[...], w_buf[s, part, :], (((1,), (1,)), ((), ())),
-                    preferred_element_type=F32,
-                )
-                product = jnp.where(feeds, product, 0.0)
+        product = jnp.where(index_ref[1 + source] > 0, product, 0.0)
+        for lane, (lo, hi) in enumerate(plan.lane_sources):
+            first, kept = plan.lanes[lane][0], plan.kept_order(lane)
+            away, keep = outs[2 * lane * half:][:half], outs[(2 * lane + 1) * half:][:half]
+
+            @pl.when((source >= lo) & (source < hi))
+            def _():
                 for p, j in enumerate(kept):
                     far = (j ^ first) * plan.block
-                    away[p][s - lo, :, part] = product[far:far + plan.block].astype(BF16)
-                    keep[p][s - lo, :, part] = product[j * plan.block:(j + 1) * plan.block]
-
-    total = jnp.zeros((8, 128), F32)
-    for row in range(0, plan.chunk_rows, ROW_TILE):
-        value = e_buf[row:row + ROW_TILE, :].astype(F32)
+                    away[p][source - lo, :, cols] = product[far:far + plan.block].astype(BF16)
+                    keep[p][source - lo, :, cols] = product[j * plan.block:(j + 1) * plan.block]
+
+    streamed(plan.sources * steps, w_buf.shape[0], copies_of, step)
+
+    def add_squares(i, total):
+        rows = pl.ds(pl.multiple_of(i * ROW_TILE, ROW_TILE), ROW_TILE)
+        value = e_buf[rows, :].astype(F32)
         value = value * value
         value = value[:8] + value[8:]
         for col in range(0, plan.model, 128):
             total = total + value[:, col:col + 128]
-    outs[-1][...] = total
+        return total
+
+    outs[-1][...] = lax.fori_loop(
+        0, plan.chunk_rows // ROW_TILE, add_squares, jnp.zeros((8, 128), F32)
+    )
 
 
 def gradient(plan, index, errors, w_dec):
-    steps = plan.width // pick_tile(plan.width, 256)
+    depth = pick_tile(plan.width, 256)
     half = plan.groups // 2
     out_shape = []
     for lo, hi in plan.lane_sources:
@@ -323,9 +309,9 @@
         out_shape + [jax.ShapeDtypeStruct((8, 128), F32)],
         [
             pltpu.VMEM((plan.chunk_rows, plan.model), BF16),
-            pltpu.VMEM((plan.sources, plan.width, plan.model), BF16),
+            pltpu.VMEM((2 * WEIGHT_SLOTS, depth, plan.model), BF16),
             pltpu.SemaphoreType.DMA((len(errors),)),
-            pltpu.SemaphoreType.DMA((plan.sources * steps,)),
+            pltpu.SemaphoreType.DMA((2 * WEIGHT_SLOTS,)),
         ],
         (index, *errors, w_dec),
     )
@@ -395,20 +381,20 @@
             places.append(place * 2 + (core ^ other))
     index = jnp.concatenate([core[None], feeds, jnp.stack(offsets), jnp.stack(places)])
 
-    encoded = [encode(plan, i, resid, w_enc, b_enc) for i in range(len(plan.lanes))]
-    active = jnp.stack([e[s] for e in encoded for s in range(e.shape[0])], axis=1)
-    active = with_layout_constraint(active, Layout((0, 1, 2)))
+    encoded = [encode(plan, s, resid, w_enc, b_enc) for s in range(plan.sources)]
+    active = with_layout_constraint(jnp.stack(encoded, axis=1), Layout((0, 1, 2)))
 
     pieces, arrived = [], []
-    for lane, bits in enumerate(plan.lanes):
-        mine, = after([encoded[lane]], arrived)
+    for s, mine in enumerate(encoded):
+        bits = plan.lanes[s % len(plan.lanes)]
+        mine, = after([mine], arrived[s - 2] if s >= 2 else [])
         held = {0: mine}
         for bit in bits:
             held.update(
                 {j | bit: swap(x, "grp", groups, bit) for j, x in list(held.items())}
             )
         pieces += [held[j] for j in range(groups)]
-        arrived = [held[bit] for bit in bits]
+        arrived.append([held[bit] for bit in bits])
 
     sends, keeps = decode(plan, index, after(pieces, [active]), w_dec)
     partial_rows = []
@@ -416,7 +402,8 @@
     for c in range(chunks):
         other = swap(sends[c], "feat", feats, 1)
         held = {
-            d: keeps[c][d] + other[d * plan.piece:(d + 1) * plan.piece].astype(F32)
+            d: keeps[c][d * plan.piece:(d + 1) * plan.piece]
+            + other[d * plan.piece:(d + 1) * plan.piece].astype(F32)
             for d in range(plan.depth)
         }
         for bit in plan.level_bits:
@@ -471,10 +458,11 @@
         feat_grad = finish(plan, c, kept_all, got_all, feat_grad)
         earlier = second
 
-    squares, = after([squares], first_got)
     loss = jnp.full((8, 128), jnp.sum(squares), F32)
-    for bit in (1 << i for i in range(groups.bit_length() - 1)):
+    for i, bit in enumerate(1 << i for i in range(groups.bit_length() - 1)):
         loss = loss + swap(loss, "grp", groups, bit)
+        if not i:
+            loss, = after([loss], first_got)
     entries = targets.shape[0] * groups * plan.tokens * plan.model
     recon_loss = loss[0, 0] / entries
     recon = jnp.concatenate(recon_parts, axis=0)[None]

time: 188 us -> 186 us (0.989)
  waiting for transfers between devices: 60.2 us -> 41.6 us
  local copies, waits for them, and re-layouts: 11.5 us -> 21.8 us
  starting transfers between devices: 38.7 us -> 46.9 us
  Pallas kernels: 63.3 us -> 59.4 us
    ppermute x42 -> x48, waiting for transfers between devices: 60.2 us -> 41.6 us  [swap(): return lax.ppermute(x, axis, [(i, i ^ offset) for i in range(size)])]
    unnamed x28 -> x60, local copies, waits for them, and re-layouts: 3.63 us -> 14.8 us
    ppermute x42 -> x48, starting transfers between devices: 38.7 us -> 46.9 us  [swap(): return lax.ppermute(x, axis, [(i, i ^ offset) for i in range(size)])]
    pallas_call x7 -> x9, Pallas kernels: 63.3 us -> 59.4 us  [call(): pl.pallas_call(kernel, in_specs=in_specs, out_shape=out_shape, scratch_sh...]
    another operation x6 -> x4, local copies, waits for them, and re-layouts: 6.63 us -> 5.8 us  [per_device(): jnp.stack(encoded, axis=1)]
  transfers between devices with their start and end apart: 42 -> 48, of which waited for: 15 -> 15; matrix products, arithmetic and copies ran while one was open for 10% -> 11% of each run, Pallas kernels for 21% -> 21%
where the time goes in v6:
time: 186 us; the launch traced here: 185 us
  Pallas kernels  59.4 us (32%)
  starting transfers between devices  46.9 us (25%)
  waiting for transfers between devices  41.6 us (22%)
  local copies, waits for them, and re-layouts  21.8 us (12%)
  other arithmetic  12.5 us (7%)
  between operations  2.88 us (2%)
    pallas_call x9, Pallas kernels, call(): pl.pallas_call(kernel, in_specs=in_specs, out_shape=out_shape, scratch_sh...  59.4 us
    ppermute x48, starting transfers between devices, swap(): return lax.ppermute(x, axis, [(i, i ^ offset) for i in range(size)])  46.9 us
    ppermute x48, waiting for transfers between devices, swap(): return lax.ppermute(x, axis, [(i, i ^ offset) for i in range(size)])  41.6 us
    unnamed x60, local copies, waits for them, and re-layouts  14.8 us
    another operation x4, local copies, waits for them, and re-layouts, per_device(): jnp.stack(encoded, axis=1)  5.8 us
    another operation x1, other arithmetic, per_device(): jnp.stack(encoded, axis=1)  4.96 us
  transfers between devices with their start and end apart: 48, of which 15 were waited for; matrix products, arithmetic and copies ran while one was open for 11% of the time, Pallas kernels for 21%

profile of v6, /device:TPU:0, one launch (start us, length us, event | category | flops | bytes accessed | tf_op | source)
XLA Modules:
  0.0 185.0 jit_solution(3162104984429724042)
XLA Ops:
  0.6 4.1 %encode.5.refs_4_ = bf16[128,1024]{1,0:T(8,128)(2,1)} custom-call(bf16[4,128,2304]{2,1,0:T(8,128)(2,1)} %resid_ref.7, bf16[4,2304,1024]{2,1,0:T(8,128)(2,1)} %w_ref.7, f32[4,1024]{1,0:T(4,128)} %b_ref.7), custom_call_target="tpu_custom_call" | custom-call | flops 1048576 | bytes 1024 | tf_op jit(solution)/shard_map/encode/pallas_call | solution.py:90
  4.8 3.0 %collective-permute-start.4 = (bf16[128,1024]{1,0:T(8,128)(2,1)}, bf16[128,1024]{1,0:T(8,128)(2,1)S(1)}, u32[]{:S(2)}, u32[]{:S(2)}) collective-permute-start(bf16[128,1024]{1,0:T(8,128)(2,1)} %encode.5.refs_4_), channel_id=1, source_target_pairs={{0,16},{8,24},{16,0},{24,8},{1,17},{9,25},{17,1},{25,9},{2,18},{10... | collective-permute-start | bytes 786440 | tf_op jit(solution)/shard_map/ppermute | solution.py:30
  7.8 1.5 collective-permute-start.3
  9.3 4.1 %encode.4.refs_0_ = bf16[128,1024]{1,0:T(8,128)(2,1)} custom-call(bf16[4,128,2304]{2,1,0:T(8,128)(2,1)} %resid_ref.7, bf16[4,2304,1024]{2,1,0:T(8,128)(2,1)} %w_ref.7, f32[4,1024]{1,0:T(4,128)} %b_ref.7), custom_call_target="tpu_custom_call" | custom-call | flops 1048576 | bytes 1024 | tf_op jit(solution)/shard_map/encode/pallas_call | solution.py:90
  14.1 4.1 %encode.7.refs_12_ = bf16[128,1024]{1,0:T(8,128)(2,1)} custom-call(bf16[4,128,2304]{2,1,0:T(8,128)(2,1)} %resid_ref.7, bf16[4,2304,1024]{2,1,0:T(8,128)(2,1)} %w_ref.7, f32[4,1024]{1,0:T(4,128)} %b_ref.7), custom_call_target="tpu_custom_call" | custom-call | flops 1048576 | bytes 1024 | tf_op jit(solution)/shard_map/encode/pallas_call | solution.py:90
  18.3 4.2 %encode.6.refs_8_ = bf16[128,1024]{1,0:T(8,128)(2,1)} custom-call(bf16[4,128,2304]{2,1,0:T(8,128)(2,1)} %resid_ref.7, bf16[4,2304,1024]{2,1,0:T(8,128)(2,1)} %w_ref.7, f32[4,1024]{1,0:T(4,128)} %b_ref.7), custom_call_target="tpu_custom_call" | custom-call | flops 1048576 | bytes 1024 | tf_op jit(solution)/shard_map/encode/pallas_call | solution.py:90
  22.5 2.0 %collective-permute-start.10 = (bf16[128,1024]{1,0:T(8,128)(2,1)S(1)}, bf16[128,1024]{1,0:T(8,128)(2,1)S(1)}, u32[]{:S(2)}, u32[]{:S(2)}) collective-permute-start(bf16[128,1024]{1,0:T(8,128)(2,1)S(1)} %copy-done.2), channel_id=1, source_target_pairs={{0,16},{8,24},{16,0},{24,8},{1,17},{9,25},{17,1},{25,9},{2,18},{10... | collective-permute-start | bytes 786440 | tf_op jit(solution)/shard_map/ppermute | solution.py:30
  25.3 1.5 collective-permute-start.6
  27.4 2.0 %collective-permute-start.2 = (bf16[128,1024]{1,0:T(8,128)(2,1)S(1)}, bf16[128,1024]{1,0:T(8,128)(2,1)S(1)}, u32[]{:S(2)}, u32[]{:S(2)}) collective-permute-start(bf16[128,1024]{1,0:T(8,128)(2,1)S(1)} %collective-permute-done.refs_1_), channel_id=1, source_target_pairs={{0,16},{8,24},{16,0},{24,8},{1,17},{9,25},{17,1},{25,9},{2,18},{10... | collective-permute-start | bytes 786440 | tf_op jit(solution)/shard_map/ppermute | solution.py:30
  29.3 2.5 %collective-permute-done.10.refs_14_ = bf16[128,1024]{1,0:T(8,128)(2,1)S(1)} collective-permute-done((bf16[128,1024]{1,0:T(8,128)(2,1)S(1)}, bf16[128,1024]{1,0:T(8,128)(2,1)S(1)}, u32[]{:S(2)}, u32[]{:S(2)}) %collective-permute-start.10) | collective-permute-done | bytes 262176 | tf_op jit(solution)/shard_map/ppermute | solution.py:30
  31.8 1.9 %collective-permute-start.5 = (bf16[128,1024]{1,0:T(8,128)(2,1)S(1)}, bf16[128,1024]{1,0:T(8,128)(2,1)S(1)}, u32[]{:S(2)}, u32[]{:S(2)}) collective-permute-start(bf16[128,1024]{1,0:T(8,128)(2,1)S(1)} %collective-permute-done.4.refs_6_), channel_id=1, source_target_pairs={{0,8},{8,0},{16,24},{24,16},{1,9},{9,1},{17,25},{25,17},{2,10},{10... | collective-permute-start | bytes 786440 | tf_op jit(solution)/shard_map/ppermute | solution.py:30
  34.7 1.5 collective-permute-start.11
  36.2 1.2 collective-permute-done.7.refs_10_
  37.4 2.0 %collective-permute-start.8 = (bf16[128,1024]{1,0:T(8,128)(2,1)S(1)}, bf16[128,1024]{1,0:T(8,128)(2,1)}, u32[]{:S(2)}, u32[]{:S(2)}) collective-permute-start(bf16[128,1024]{1,0:T(8,128)(2,1)S(1)} %collective-permute-done.6.refs_9_), channel_id=1, source_target_pairs={{0,16},{8,24},{16,0},{24,8},{1,17},{9,25},{17,1},{25,9},{2,18},{10... | collective-permute-start | bytes 786440 | tf_op jit(solution)/shard_map/ppermute | solution.py:30
  39.4 1.2 copy.11
  40.6 1.2 copy.12
  41.8 2.2 %copy.13 = bf16[128,1,1024]{2,1,0:T(2,128)(2,1)} copy(bf16[128,1,1024]{2,0,1:T(8,128)(2,1)} %bitcast.31) | data formatting | bytes 524288 | tf_op jit(solution)/shard_map/stack | solution.py:385
  44.0 1.2 copy.14
  45.3 5.0 %pad_maximum_fusion = bf16[128,4,1024]{2,1,0:T(4,128)(2,1)} fusion(bf16[128,1,1024]{2,1,0:T(2,128)(2,1)} %copy.14, bf16[128,1,1024]{2,1,0:T(2,128)(2,1)} %copy.13, bf16[128,1,1024]{2,1,0:T(2,128)(2,1)} %copy.12, bf16[128,1,1024]{2,1,0:T(2,128)(2,1)} %copy.11), kind=kLoop, calls=%fused_computation | loop fusion | flops 4194304 | bytes 2097152 | tf_op jit(solution)/shard_map/stack | solution.py:385
  62.7 15.0 %decode.1 = (bf16[128,2304]{1,0:T(8,128)(2,1)S(1)}, bf16[128,2304]{1,0:T(8,128)(2,1)S(1)}, f32[128,2304]{1,0:T(8,128)S(1)}, f32[128,2304]{1,0:T(8,128)S(1)}) custom-call(s32[17]{0:T(128)S(1)} %concatenate.6.index_ref, bf16[128,1024]{1,0:T(8,128)(2,1)S(1)} %copy-done.1, bf16[128,1024]{1,0:T(8,128)(2,1)S(1)} %copy-done.9, bf16[128,1024]{1,0:T(8,128)(2,1)S(1)} %copy-done.11, ...), custom_call_target="tpu_custom_call" | custom-call | flops 1048576 | bytes 1024 | tf_op jit(solution)/shard_map/decode/pallas_call | solution.py:90
  78.5 2.0 %collective-permute-done.12 = bf16[128,2304]{1,0:T(8,128)(2,1)S(1)} collective-permute-done((bf16[128,2304]{1,0:T(8,128)(2,1)S(1)}, bf16[128,2304]{1,0:T(8,128)(2,1)S(1)}, u32[]{:S(2)}, u32[]{:S(2)}) %collective-permute-start.12) | collective-permute-done | bytes 589856 | tf_op jit(solution)/shard_map/ppermute | solution.py:30
  81.4 1.6 collective-permute-start.14
  83.5 4.8 %collective-permute-done.14 = bf16[32,2304]{1,0:T(8,128)(2,1)} collective-permute-done((bf16[32,2304]{1,0:T(8,128)(2,1)S(1)}, bf16[32,2304]{1,0:T(8,128)(2,1)}, u32[]{:S(2)}, u32[]{:S(2)}) %collective-permute-start.14) | collective-permute-done | bytes 147488 | tf_op jit(solution)/shard_map/ppermute | solution.py:30
  89.3 2.6 %collective-permute-start.15 = (bf16[32,2304]{1,0:T(8,128)(2,1)S(1)}, bf16[32,2304]{1,0:T(8,128)(2,1)S(1)}, u32[]{:S(2)}, u32[]{:S(2)}) collective-permute-start(bf16[32,2304]{1,0:T(8,128)(2,1)S(1)} %add_convert_fusion.7), channel_id=1, source_target_pairs={{0,4},{1,5},{2,6},{3,7},{4,0},{5,1},{6,2},{7,3},{8,12},{9,13},{10,... | collective-permute-start | bytes 442376 | tf_op jit(solution)/shard_map/ppermute | solution.py:30
  92.7 1.5 collective-permute-start.18
  94.7 2.6 %collective-permute-done.15 = bf16[32,2304]{1,0:T(8,128)(2,1)S(1)} collective-permute-done((bf16[32,2304]{1,0:T(8,128)(2,1)S(1)}, bf16[32,2304]{1,0:T(8,128)(2,1)S(1)}, u32[]{:S(2)}, u32[]{:S(2)}) %collective-permute-start.15) | collective-permute-done | bytes 147488 | tf_op jit(solution)/shard_map/ppermute | solution.py:30
  97.3 1.1 fusion.3
  98.4 2.2 %collective-permute-start.20 = (bf16[32,2304]{1,0:T(8,128)(2,1)S(1)}, bf16[32,2304]{1,0:T(8,128)(2,1)S(1)}, u32[]{:S(2)}, u32[]{:S(2)}) collective-permute-start(bf16[32,2304]{1,0:T(8,128)(2,1)S(1)} %get-tuple-element.95.refs_0_), channel_id=1, source_target_pairs={{0,4},{1,5},{2,6},{3,7},{4,0},{5,1},{6,2},{7,3},{8,12},{9,13},{10,... | collective-permute-start | bytes 442376 | tf_op jit(solution)/shard_map/ppermute | solution.py:30
  100.6 1.9 %collective-permute-done.18 = bf16[32,2304]{1,0:T(8,128)(2,1)S(1)} collective-permute-done((bf16[32,2304]{1,0:T(8,128)(2,1)S(1)}, bf16[32,2304]{1,0:T(8,128)(2,1)S(1)}, u32[]{:S(2)}, u32[]{:S(2)}) %collective-permute-start.18) | collective-permute-done | bytes 147488 | tf_op jit(solution)/shard_map/ppermute | solution.py:30
  103.5 7.3 %collective-permute-done.20.refs_2_ = bf16[32,2304]{1,0:T(8,128)(2,1)S(1)} collective-permute-done((bf16[32,2304]{1,0:T(8,128)(2,1)S(1)}, bf16[32,2304]{1,0:T(8,128)(2,1)S(1)}, u32[]{:S(2)}, u32[]{:S(2)}) %collective-permute-start.20) | collective-permute-done | bytes 147488 | tf_op jit(solution)/shard_map/ppermute | solution.py:30
  114.0 1.9 %collective-permute-done.22.refs_3_ = bf16[32,2304]{1,0:T(8,128)(2,1)S(1)} collective-permute-done((bf16[32,2304]{1,0:T(8,128)(2,1)S(1)}, bf16[32,2304]{1,0:T(8,128)(2,1)S(1)}, u32[]{:S(2)}, u32[]{:S(2)}) %collective-permute-start.22) | collective-permute-done | bytes 147488 | tf_op jit(solution)/shard_map/ppermute | solution.py:30
  116.9 2.2 %collective-permute-start.28 = (bf16[32,2304]{1,0:T(8,128)(2,1)S(1)}, bf16[32,2304]{1,0:T(8,128)(2,1)S(1)}, u32[]{:S(2)}, u32[]{:S(2)}) collective-permute-start(bf16[32,2304]{1,0:T(8,128)(2,1)S(1)} %get-tuple-element.106.refs_0_), channel_id=1, source_target_pairs={{0,4},{1,5},{2,6},{3,7},{4,0},{5,1},{6,2},{7,3},{8,12},{9,13},{10,... | collective-permute-start | bytes 442376 | tf_op jit(solution)/shard_map/ppermute | solution.py:30
  119.1 2.0 %collective-permute-start.27 = (bf16[32,2304]{1,0:T(8,128)(2,1)S(1)}, bf16[32,2304]{1,0:T(8,128)(2,1)S(1)}, u32[]{:S(2)}, u32[]{:S(2)}) collective-permute-start(bf16[32,2304]{1,0:T(8,128)(2,1)S(1)} %get-tuple-element.106.refs_0_), channel_id=1, source_target_pairs={{0,2},{1,3},{2,0},{3,1},{4,6},{5,7},{6,4},{7,5},{8,10},{9,11},{10,... | collective-permute-start | bytes 442376 | tf_op jit(solution)/shard_map/ppermute | solution.py:30
  121.2 12.7 %gradient.2 = (bf16[2,64,1024]{2,1,0:T(8,128)(2,1)S(1)}, bf16[2,64,1024]{2,1,0:T(8,128)(2,1)S(1)}, f32[2,64,1024]{2,1,0:T(8,128)S(1)}, f32[2,64,1024]{2,1,0:T(8,...) custom-call(s32[17]{0:T(128)S(1)} %concatenate.6.index_ref, ...), custom_call_target="tpu_custom_call" | custom-call | flops 1048576 | bytes 1024 | tf_op jit(solution)/shard_map/gradient/pallas_call | solution.py:90
  134.3 1.6 collective-permute-start.34
  136.9 5.7 %collective-permute-done.35 = bf16[2,64,1024]{2,1,0:T(8,128)(2,1)S(1)} collective-permute-done((bf16[2,64,1024]{2,1,0:T(8,128)(2,1)S(1)}, bf16[2,64,1024]{2,1,0:T(8,128)(2,1)S(1)}, u32[]{:S(2)}, u32[]{:S(2)}) %collective-permute-start.35) | collective-permute-done | bytes 262176 | tf_op jit(solution)/shard_map/ppermute | solution.py:30
  142.7 1.2 collective-permute-start.43
  143.9 1.1 collective-permute-start.42
  146.0 1.2 collective-permute-start.44
  147.2 12.7 %gradient.3 = (bf16[2,64,1024]{2,1,0:T(8,128)(2,1)S(1)}, bf16[2,64,1024]{2,1,0:T(8,128)(2,1)S(1)}, f32[2,64,1024]{2,1,0:T(8,128)S(1)}, f32[2,64,1024]{2,1,0:T(8,...) custom-call(s32[17]{0:T(128)S(1)} %concatenate.6.index_ref, ...), custom_call_target="tpu_custom_call" | custom-call | flops 1048576 | bytes 1024 | tf_op jit(solution)/shard_map/gradient/pallas_call | solution.py:90
  161.4 1.1 collective-permute-start.37
  164.3 4.8 %collective-permute-done.36 = f32[8,128]{1,0:T(8,128)S(1)} collective-permute-done((f32[8,128]{1,0:T(8,128)S(1)}, f32[8,128]{1,0:T(8,128)S(1)}, u32[]{:S(2)}, u32[]{:S(2)}) %collective-permute-start.36) | collective-permute-done | bytes 4128 | tf_op jit(solution)/shard_map/ppermute | solution.py:30
  170.7 1.6 collective-permute-start.40
  172.4 1.2 finish.2.refs_4_
  174.3 1.1 collective-permute-start.46
  177.2 2.5 %collective-permute-done.40 = bf16[2,64,1024]{2,1,0:T(8,128)(2,1)S(1)} collective-permute-done((bf16[2,64,1024]{2,1,0:T(8,128)(2,1)S(1)}, bf16[2,64,1024]{2,1,0:T(8,128)(2,1)S(1)}, u32[]{:S(2)}, u32[]{:S(2)}) %collective-permute-start.40) | collective-permute-done | bytes 262176 | tf_op jit(solution)/shard_map/ppermute | solution.py:30
  179.8 1.7 collective-permute-done.39
  182.7 1.2 finish.3
  (144 shorter events, 35.8 us)
Async XLA Ops:
  4.8 17.7 %collective-permute-start.4 = (bf16[128,1024]{1,0:T(8,128)(2,1)}, bf16[128,1024]{1,0:T(8,128)(2,1)S(1)}, u32[]{:S(2)}, u32[]{:S(2)}) collective-permute-start(bf16[128,1024]{1,0:T(8,128)(2,1)} %encode.5.refs_4_), channel_id=1, source_target_pairs={{0,16},{8,24},{16,0},{24,8},{1,17},{9,25},{17,1},{25,9},{2,18},{10... | collective-permute-start | bytes 786440 | tf_op jit(solution)/shard_map/ppermute | solution.py:30
  7.8 14.7 %collective-permute-start.3 = (bf16[128,1024]{1,0:T(8,128)(2,1)}, bf16[128,1024]{1,0:T(8,128)(2,1)S(1)}, u32[]{:S(2)}, u32[]{:S(2)}) collective-permute-start(bf16[128,1024]{1,0:T(8,128)(2,1)} %encode.5.refs_4_), channel_id=1, source_target_pairs={{0,8},{8,0},{16,24},{24,16},{1,9},{9,1},{17,25},{25,17},{2,10},{10... | collective-permute-start | bytes 786440 | tf_op jit(solution)/shard_map/ppermute | solution.py:30
  13.4 11.1 %collective-permute-start = (bf16[128,1024]{1,0:T(8,128)(2,1)}, bf16[128,1024]{1,0:T(8,128)(2,1)S(1)}, u32[]{:S(2)}, u32[]{:S(2)}) collective-permute-start(bf16[128,1024]{1,0:T(8,128)(2,1)} %encode.4.refs_0_), channel_id=1, source_target_pairs={{0,8},{8,0},{16,24},{24,16},{1,9},{9,1},{17,25},{25,17},{2,10},{10... | collective-permute-start | bytes 786440 | tf_op jit(solution)/shard_map/ppermute | solution.py:30
  14.0 10.5 %collective-permute-start.1 = (bf16[128,1024]{1,0:T(8,128)(2,1)}, bf16[128,1024]{1,0:T(8,128)(2,1)S(1)}, u32[]{:S(2)}, u32[]{:S(2)}) collective-permute-start(bf16[128,1024]{1,0:T(8,128)(2,1)} %encode.4.refs_0_), channel_id=1, source_target_pairs={{0,16},{8,24},{16,0},{24,8},{1,17},{9,25},{17,1},{25,9},{2,18},{10... | collective-permute-start | bytes 786440 | tf_op jit(solution)/shard_map/ppermute | solution.py:30
  22.5 9.3 %collective-permute-start.10 = (bf16[128,1024]{1,0:T(8,128)(2,1)S(1)}, bf16[128,1024]{1,0:T(8,128)(2,1)S(1)}, u32[]{:S(2)}, u32[]{:S(2)}) collective-permute-start(bf16[128,1024]{1,0:T(8,128)(2,1)S(1)} %copy-done.2), channel_id=1, source_target_pairs={{0,16},{8,24},{16,0},{24,8},{1,17},{9,25},{17,1},{25,9},{2,18},{10... | collective-permute-start | bytes 786440 | tf_op jit(solution)/shard_map/ppermute | solution.py:30
  25.3 9.5 %collective-permute-start.6 = (bf16[128,1024]{1,0:T(8,128)(2,1)}, bf16[128,1024]{1,0:T(8,128)(2,1)S(1)}, u32[]{:S(2)}, u32[]{:S(2)}) collective-permute-start(bf16[128,1024]{1,0:T(8,128)(2,1)} %encode.6.refs_8_), channel_id=1, source_target_pairs={{0,8},{8,0},{16,24},{24,16},{1,9},{9,1},{17,25},{25,17},{2,10},{10... | collective-permute-start | bytes 786440 | tf_op jit(solution)/shard_map/ppermute | solution.py:30
  26.8 10.7 %collective-permute-start.7 = (bf16[128,1024]{1,0:T(8,128)(2,1)}, bf16[128,1024]{1,0:T(8,128)(2,1)S(1)}, u32[]{:S(2)}, u32[]{:S(2)}) collective-permute-start(bf16[128,1024]{1,0:T(8,128)(2,1)} %encode.6.refs_8_), channel_id=1, source_target_pairs={{0,16},{8,24},{16,0},{24,8},{1,17},{9,25},{17,1},{25,9},{2,18},{10... | collective-permute-start | bytes 786440 | tf_op jit(solution)/shard_map/ppermute | solution.py:30
  27.3 23.0 %collective-permute-start.9 = (bf16[128,1024]{1,0:T(8,128)(2,1)S(1)}, bf16[128,1024]{1,0:T(8,128)(2,1)S(1)}, u32[]{:S(2)}, u32[]{:S(2)}) collective-permute-start(bf16[128,1024]{1,0:T(8,128)(2,1)S(1)} %copy-done.2), channel_id=1, source_target_pairs={{0,8},{8,0},{16,24},{24,16},{1,9},{9,1},{17,25},{25,17},{2,10},{10... | collective-permute-start | bytes 786440 | tf_op jit(solution)/shard_map/ppermute | solution.py:30
  27.4 23.6 %collective-permute-start.2 = (bf16[128,1024]{1,0:T(8,128)(2,1)S(1)}, bf16[128,1024]{1,0:T(8,128)(2,1)S(1)}, u32[]{:S(2)}, u32[]{:S(2)}) collective-permute-start(bf16[128,1024]{1,0:T(8,128)(2,1)S(1)} %collective-permute-done.refs_1_), channel_id=1, source_target_pairs={{0,16},{8,24},{16,0},{24,8},{1,17},{9,25},{17,1},{25,9},{2,18},{10... | collective-permute-start | bytes 786440 | tf_op jit(solution)/shard_map/ppermute | solution.py:30
  31.8 19.9 %collective-permute-start.5 = (bf16[128,1024]{1,0:T(8,128)(2,1)S(1)}, bf16[128,1024]{1,0:T(8,128)(2,1)S(1)}, u32[]{:S(2)}, u32[]{:S(2)}) collective-permute-start(bf16[128,1024]{1,0:T(8,128)(2,1)S(1)} %collective-permute-done.4.refs_6_), channel_id=1, source_target_pairs={{0,8},{8,0},{16,24},{24,16},{1,9},{9,1},{17,25},{25,17},{2,10},{10... | collective-permute-start | bytes 786440 | tf_op jit(solution)/shard_map/ppermute | solution.py:30
  34.7 17.7 %collective-permute-start.11 = (bf16[128,1024]{1,0:T(8,128)(2,1)S(1)}, bf16[128,1024]{1,0:T(8,128)(2,1)S(1)}, u32[]{:S(2)}, u32[]{:S(2)}) collective-permute-start(bf16[128,1024]{1,0:T(8,128)(2,1)S(1)} %collective-permute-done.10.refs_14_), channel_id=1, source_target_pairs={{0,8},{8,0},{16,24},{24,16},{1,9},{9,1},{17,25},{25,17},{2,10},{10... | collective-permute-start | bytes 786440 | tf_op jit(solution)/shard_map/ppermute | solution.py:30
  37.4 15.7 %collective-permute-start.8 = (bf16[128,1024]{1,0:T(8,128)(2,1)S(1)}, bf16[128,1024]{1,0:T(8,128)(2,1)}, u32[]{:S(2)}, u32[]{:S(2)}) collective-permute-start(bf16[128,1024]{1,0:T(8,128)(2,1)S(1)} %collective-permute-done.6.refs_9_), channel_id=1, source_target_pairs={{0,16},{8,24},{16,0},{24,8},{1,17},{9,25},{17,1},{25,9},{2,18},{10... | collective-permute-start | bytes 786440 | tf_op jit(solution)/shard_map/ppermute | solution.py:30
  78.5 2.0 %collective-permute-start.12 = (bf16[128,2304]{1,0:T(8,128)(2,1)S(1)}, bf16[128,2304]{1,0:T(8,128)(2,1)S(1)}, u32[]{:S(2)}, u32[]{:S(2)}) collective-permute-start(bf16[128,2304]{1,0:T(8,128)(2,1)S(1)} %get-tuple-element.89), channel_id=1, source_target_pairs={{0,1},{1,0},{2,3},{3,2},{4,5},{5,4},{6,7},{7,6},{8,9},{9,8},{10,11... | collective-permute-start | bytes 1769480 | tf_op jit(solution)/shard_map/ppermute | solution.py:30
  81.4 6.9 %collective-permute-start.14 = (bf16[32,2304]{1,0:T(8,128)(2,1)S(1)}, bf16[32,2304]{1,0:T(8,128)(2,1)}, u32[]{:S(2)}, u32[]{:S(2)}) collective-permute-start(bf16[32,2304]{1,0:T(8,128)(2,1)S(1)} %get-tuple-element.139), channel_id=1, source_target_pairs={{0,2},{1,3},{2,0},{3,1},{4,6},{5,7},{6,4},{7,5},{8,10},{9,11},{10,... | collective-permute-start | bytes 442376 | tf_op jit(solution)/shard_map/ppermute | solution.py:30
  83.1 8.8 %collective-permute-start.16 = (bf16[128,2304]{1,0:T(8,128)(2,1)}, bf16[128,2304]{1,0:T(8,128)(2,1)S(1)}, u32[]{:S(2)}, u32[]{:S(2)}) collective-permute-start(bf16[128,2304]{1,0:T(8,128)(2,1)} %copy-done.26), channel_id=1, source_target_pairs={{0,1},{1,0},{2,3},{3,2},{4,5},{5,4},{6,7},{7,6},{8,9},{9,8},{10,11... | collective-permute-start | bytes 1769480 | tf_op jit(solution)/shard_map/ppermute | solution.py:30
  83.1 11.7 %collective-permute-start.13 = (bf16[32,2304]{1,0:T(8,128)(2,1)S(1)}, bf16[32,2304]{1,0:T(8,128)(2,1)S(1)}, u32[]{:S(2)}, u32[]{:S(2)}) collective-permute-start(bf16[32,2304]{1,0:T(8,128)(2,1)S(1)} %get-tuple-element.138), channel_id=1, source_target_pairs={{0,2},{1,3},{2,0},{3,1},{4,6},{5,7},{6,4},{7,5},{8,10},{9,11},{10,... | collective-permute-start | bytes 442376 | tf_op jit(solution)/shard_map/ppermute | solution.py:30
  89.3 8.0 %collective-permute-start.15 = (bf16[32,2304]{1,0:T(8,128)(2,1)S(1)}, bf16[32,2304]{1,0:T(8,128)(2,1)S(1)}, u32[]{:S(2)}, u32[]{:S(2)}) collective-permute-start(bf16[32,2304]{1,0:T(8,128)(2,1)S(1)} %add_convert_fusion.7), channel_id=1, source_target_pairs={{0,4},{1,5},{2,6},{3,7},{4,0},{5,1},{6,2},{7,3},{8,12},{9,13},{10,... | collective-permute-start | bytes 442376 | tf_op jit(solution)/shard_map/ppermute | solution.py:30
  92.7 9.8 %collective-permute-start.18 = (bf16[32,2304]{1,0:T(8,128)(2,1)S(1)}, bf16[32,2304]{1,0:T(8,128)(2,1)S(1)}, u32[]{:S(2)}, u32[]{:S(2)}) collective-permute-start(bf16[32,2304]{1,0:T(8,128)(2,1)S(1)} %get-tuple-element.93), channel_id=1, source_target_pairs={{0,2},{1,3},{2,0},{3,1},{4,6},{5,7},{6,4},{7,5},{8,10},{9,11},{10,... | collective-permute-start | bytes 442376 | tf_op jit(solution)/shard_map/ppermute | solution.py:30
  94.2 17.3 %collective-permute-start.17 = (bf16[32,2304]{1,0:T(8,128)(2,1)}, bf16[32,2304]{1,0:T(8,128)(2,1)}, u32[]{:S(2)}, u32[]{:S(2)}) collective-permute-start(bf16[32,2304]{1,0:T(8,128)(2,1)} %get-tuple-element.92), channel_id=1, source_target_pairs={{0,2},{1,3},{2,0},{3,1},{4,6},{5,7},{6,4},{7,5},{8,10},{9,11},{10,... | collective-permute-start | bytes 442376 | tf_op jit(solution)/shard_map/ppermute | solution.py:30
  98.4 12.4 %collective-permute-start.20 = (bf16[32,2304]{1,0:T(8,128)(2,1)S(1)}, bf16[32,2304]{1,0:T(8,128)(2,1)S(1)}, u32[]{:S(2)}, u32[]{:S(2)}) collective-permute-start(bf16[32,2304]{1,0:T(8,128)(2,1)S(1)} %get-tuple-element.95.refs_0_), channel_id=1, source_target_pairs={{0,4},{1,5},{2,6},{3,7},{4,0},{5,1},{6,2},{7,3},{8,12},{9,13},{10,... | collective-permute-start | bytes 442376 | tf_op jit(solution)/shard_map/ppermute | solution.py:30
  102.6 9.8 %collective-permute-start.19 = (bf16[32,2304]{1,0:T(8,128)(2,1)S(1)}, bf16[32,2304]{1,0:T(8,128)(2,1)S(1)}, u32[]{:S(2)}, u32[]{:S(2)}) collective-permute-start(bf16[32,2304]{1,0:T(8,128)(2,1)S(1)} %add_convert_fusion.4), channel_id=1, source_target_pairs={{0,4},{1,5},{2,6},{3,7},{4,0},{5,1},{6,2},{7,3},{8,12},{9,13},{10,... | collective-permute-start | bytes 442376 | tf_op jit(solution)/shard_map/ppermute | solution.py:30
  102.6 10.9 %collective-permute-start.21 = (bf16[32,2304]{1,0:T(8,128)(2,1)S(1)}, bf16[32,2304]{1,0:T(8,128)(2,1)S(1)}, u32[]{:S(2)}, u32[]{:S(2)}) collective-permute-start(bf16[32,2304]{1,0:T(8,128)(2,1)S(1)} %get-tuple-element.95.refs_0_), channel_id=1, source_target_pairs={{0,2},{1,3},{2,0},{3,1},{4,6},{5,7},{6,4},{7,5},{8,10},{9,11},{10,... | collective-permute-start | bytes 442376 | tf_op jit(solution)/shard_map/ppermute | solution.py:30
  103.5 15.6 %collective-permute-start.23 = (bf16[32,2304]{1,0:T(8,128)(2,1)S(1)}, bf16[32,2304]{1,0:T(8,128)(2,1)S(1)}, u32[]{:S(2)}, u32[]{:S(2)}) collective-permute-start(bf16[32,2304]{1,0:T(8,128)(2,1)S(1)} %get-tuple-element.95.refs_0_), channel_id=1, source_target_pairs={{0,1},{1,0},{2,3},{3,2},{4,5},{5,4},{6,7},{7,6},{8,9},{9,8},{10,11... | collective-permute-start | bytes 442376 | tf_op jit(solution)/shard_map/ppermute | solution.py:30
  110.8 5.1 %collective-permute-start.22 = (bf16[32,2304]{1,0:T(8,128)(2,1)S(1)}, bf16[32,2304]{1,0:T(8,128)(2,1)S(1)}, u32[]{:S(2)}, u32[]{:S(2)}) collective-permute-start(bf16[32,2304]{1,0:T(8,128)(2,1)S(1)} %collective-permute-done.20.refs_2_), channel_id=1, source_target_pairs={{0,2},{1,3},{2,0},{3,1},{4,6},{5,7},{6,4},{7,5},{8,10},{9,11},{10,... | collective-permute-start | bytes 442376 | tf_op jit(solution)/shard_map/ppermute | solution.py:30
  113.4 7.7 %collective-permute-start.25 = (bf16[32,2304]{1,0:T(8,128)(2,1)S(1)}, bf16[32,2304]{1,0:T(8,128)(2,1)S(1)}, u32[]{:S(2)}, u32[]{:S(2)}) collective-permute-start(bf16[32,2304]{1,0:T(8,128)(2,1)S(1)} %collective-permute-done.20.refs_2_), channel_id=1, source_target_pairs={{0,1},{1,0},{2,3},{3,2},{4,5},{5,4},{6,7},{7,6},{8,9},{9,8},{10,11... | collective-permute-start | bytes 442376 | tf_op jit(solution)/shard_map/ppermute | solution.py:30
  113.5 7.6 %collective-permute-start.24 = (bf16[32,2304]{1,0:T(8,128)(2,1)S(1)}, bf16[32,2304]{1,0:T(8,128)(2,1)S(1)}, u32[]{:S(2)}, u32[]{:S(2)}) collective-permute-start(bf16[32,2304]{1,0:T(8,128)(2,1)S(1)} %collective-permute-done.21.refs_1_), channel_id=1, source_target_pairs={{0,1},{1,0},{2,3},{3,2},{4,5},{5,4},{6,7},{7,6},{8,9},{9,8},{10,11... | collective-permute-start | bytes 442376 | tf_op jit(solution)/shard_map/ppermute | solution.py:30
  115.9 5.2 %collective-permute-start.26 = (bf16[32,2304]{1,0:T(8,128)(2,1)S(1)}, bf16[32,2304]{1,0:T(8,128)(2,1)S(1)}, u32[]{:S(2)}, u32[]{:S(2)}) collective-permute-start(bf16[32,2304]{1,0:T(8,128)(2,1)S(1)} %collective-permute-done.22.refs_3_), channel_id=1, source_target_pairs={{0,1},{1,0},{2,3},{3,2},{4,5},{5,4},{6,7},{7,6},{8,9},{9,8},{10,11... | collective-permute-start | bytes 442376 | tf_op jit(solution)/shard_map/ppermute | solution.py:30
  116.9 19.7 %collective-permute-start.28 = (bf16[32,2304]{1,0:T(8,128)(2,1)S(1)}, bf16[32,2304]{1,0:T(8,128)(2,1)S(1)}, u32[]{:S(2)}, u32[]{:S(2)}) collective-permute-start(bf16[32,2304]{1,0:T(8,128)(2,1)S(1)} %get-tuple-element.106.refs_0_), channel_id=1, source_target_pairs={{0,4},{1,5},{2,6},{3,7},{4,0},{5,1},{6,2},{7,3},{8,12},{9,13},{10,... | collective-permute-start | bytes 442376 | tf_op jit(solution)/shard_map/ppermute | solution.py:30
  119.1 17.8 %collective-permute-start.27 = (bf16[32,2304]{1,0:T(8,128)(2,1)S(1)}, bf16[32,2304]{1,0:T(8,128)(2,1)S(1)}, u32[]{:S(2)}, u32[]{:S(2)}) collective-permute-start(bf16[32,2304]{1,0:T(8,128)(2,1)S(1)} %get-tuple-element.106.refs_0_), channel_id=1, source_target_pairs={{0,2},{1,3},{2,0},{3,1},{4,6},{5,7},{6,4},{7,5},{8,10},{9,11},{10,... | collective-permute-start | bytes 442376 | tf_op jit(solution)/shard_map/ppermute | solution.py:30
  121.2 22.8 %collective-permute-start.30 = (bf16[32,2304]{1,0:T(8,128)(2,1)S(1)}, bf16[32,2304]{1,0:T(8,128)(2,1)S(1)}, u32[]{:S(2)}, u32[]{:S(2)}) collective-permute-start(bf16[32,2304]{1,0:T(8,128)(2,1)S(1)} %get-tuple-element.106.refs_0_), channel_id=1, source_target_pairs={{0,1},{1,0},{2,3},{3,2},{4,5},{5,4},{6,7},{7,6},{8,9},{9,8},{10,11... | collective-permute-start | bytes 442376 | tf_op jit(solution)/shard_map/ppermute | solution.py:30
  133.9 8.8 %collective-permute-start.35 = (bf16[2,64,1024]{2,1,0:T(8,128)(2,1)S(1)}, bf16[2,64,1024]{2,1,0:T(8,128)(2,1)S(1)}, u32[]{:S(2)}, u32[]{:S(2)}) collective-permute-start(bf16[2,64,1024]{2,1,0:T(8,128)(2,1)S(1)} %get-tuple-element.105), channel_id=1, source_target_pairs={{0,16},{8,24},{16,0},{24,8},{1,17},{9,25},{17,1},{25,9},{2,18},{10... | collective-permute-start | bytes 786440 | tf_op jit(solution)/shard_map/ppermute | solution.py:30
  134.3 9.6 %collective-permute-start.34 = (bf16[2,64,1024]{2,1,0:T(8,128)(2,1)S(1)}, bf16[2,64,1024]{2,1,0:T(8,128)(2,1)S(1)}, u32[]{:S(2)}, u32[]{:S(2)}) collective-permute-start(bf16[2,64,1024]{2,1,0:T(8,128)(2,1)S(1)} %get-tuple-element.104), channel_id=1, source_target_pairs={{0,8},{8,0},{16,24},{24,16},{1,9},{9,1},{17,25},{25,17},{2,10},{10... | collective-permute-start | bytes 786440 | tf_op jit(solution)/shard_map/ppermute | solution.py:30
  136.6 6.1 %collective-permute-start.29 = (bf16[32,2304]{1,0:T(8,128)(2,1)S(1)}, bf16[32,2304]{1,0:T(8,128)(2,1)S(1)}, u32[]{:S(2)}, u32[]{:S(2)}) collective-permute-start(bf16[32,2304]{1,0:T(8,128)(2,1)S(1)} %collective-permute-done.28.refs_2_), channel_id=1, source_target_pairs={{0,2},{1,3},{2,0},{3,1},{4,6},{5,7},{6,4},{7,5},{8,10},{9,11},{10,... | collective-permute-start | bytes 442376 | tf_op jit(solution)/shard_map/ppermute | solution.py:30
  136.9 9.1 %collective-permute-start.32 = (bf16[32,2304]{1,0:T(8,128)(2,1)S(1)}, bf16[32,2304]{1,0:T(8,128)(2,1)S(1)}, u32[]{:S(2)}, u32[]{:S(2)}) collective-permute-start(bf16[32,2304]{1,0:T(8,128)(2,1)S(1)} %collective-permute-done.28.refs_2_), channel_id=1, source_target_pairs={{0,1},{1,0},{2,3},{3,2},{4,5},{5,4},{6,7},{7,6},{8,9},{9,8},{10,11... | collective-permute-start | bytes 442376 | tf_op jit(solution)/shard_map/ppermute | solution.py:30
  142.6 2.5 %collective-permute-start.31 = (bf16[32,2304]{1,0:T(8,128)(2,1)S(1)}, bf16[32,2304]{1,0:T(8,128)(2,1)S(1)}, u32[]{:S(2)}, u32[]{:S(2)}) collective-permute-start(bf16[32,2304]{1,0:T(8,128)(2,1)S(1)} %collective-permute-done.27.refs_1_), channel_id=1, source_target_pairs={{0,1},{1,0},{2,3},{3,2},{4,5},{5,4},{6,7},{7,6},{8,9},{9,8},{10,11... | collective-permute-start | bytes 442376 | tf_op jit(solution)/shard_map/ppermute | solution.py:30
  142.7 18.7 %collective-permute-start.43 = (bf16[2,64,1024]{2,1,0:T(8,128)(2,1)S(1)}, bf16[2,64,1024]{2,1,0:T(8,128)(2,1)S(1)}, u32[]{:S(2)}, u32[]{:S(2)}) collective-permute-start(bf16[2,64,1024]{2,1,0:T(8,128)(2,1)S(1)} %get-tuple-element.132), channel_id=1, source_target_pairs={{0,16},{8,24},{16,0},{24,8},{1,17},{9,25},{17,1},{25,9},{2,18},{10... | collective-permute-start | bytes 786440 | tf_op jit(solution)/shard_map/ppermute | solution.py:30
  143.9 3.3 %collective-permute-start.33 = (bf16[32,2304]{1,0:T(8,128)(2,1)S(1)}, bf16[32,2304]{1,0:T(8,128)(2,1)S(1)}, u32[]{:S(2)}, u32[]{:S(2)}) collective-permute-start(bf16[32,2304]{1,0:T(8,128)(2,1)S(1)} %collective-permute-done.29.refs_3_), channel_id=1, source_target_pairs={{0,1},{1,0},{2,3},{3,2},{4,5},{5,4},{6,7},{7,6},{8,9},{9,8},{10,11... | collective-permute-start | bytes 442376 | tf_op jit(solution)/shard_map/ppermute | solution.py:30
  143.9 18.6 %collective-permute-start.42 = (bf16[2,64,1024]{2,1,0:T(8,128)(2,1)S(1)}, bf16[2,64,1024]{2,1,0:T(8,128)(2,1)S(1)}, u32[]{:S(2)}, u32[]{:S(2)}) collective-permute-start(bf16[2,64,1024]{2,1,0:T(8,128)(2,1)S(1)} %get-tuple-element.130), channel_id=1, source_target_pairs={{0,8},{8,0},{16,24},{24,16},{1,9},{9,1},{17,25},{25,17},{2,10},{10... | collective-permute-start | bytes 786440 | tf_op jit(solution)/shard_map/ppermute | solution.py:30
  145.1 27.3 %collective-permute-start.45 = (bf16[2,64,1024]{2,1,0:T(8,128)(2,1)S(1)}, bf16[2,64,1024]{2,1,0:T(8,128)(2,1)S(1)}, u32[]{:S(2)}, u32[]{:S(2)}) collective-permute-start(bf16[2,64,1024]{2,1,0:T(8,128)(2,1)S(1)} %add_convert_fusion.2), channel_id=1, source_target_pairs={{0,8},{8,0},{16,24},{24,16},{1,9},{9,1},{17,25},{25,17},{2,10},{10... | collective-permute-start | bytes 786440 | tf_op jit(solution)/shard_map/ppermute | solution.py:30
  146.0 26.4 %collective-permute-start.44 = (bf16[2,64,1024]{2,1,0:T(8,128)(2,1)S(1)}, bf16[2,64,1024]{2,1,0:T(8,128)(2,1)S(1)}, u32[]{:S(2)}, u32[]{:S(2)}) collective-permute-start(bf16[2,64,1024]{2,1,0:T(8,128)(2,1)S(1)} %add_convert_fusion.3), channel_id=1, source_target_pairs={{0,16},{8,24},{16,0},{24,8},{1,17},{9,25},{17,1},{25,9},{2,18},{10... | collective-permute-start | bytes 786440 | tf_op jit(solution)/shard_map/ppermute | solution.py:30
  159.9 10.8 %collective-permute-start.38 = (bf16[2,64,1024]{2,1,0:T(8,128)(2,1)S(1)}, bf16[2,64,1024]{2,1,0:T(8,128)(2,1)S(1)}, u32[]{:S(2)}, u32[]{:S(2)}) collective-permute-start(bf16[2,64,1024]{2,1,0:T(8,128)(2,1)S(1)} %get-tuple-element.122), channel_id=1, source_target_pairs={{0,16},{8,24},{16,0},{24,8},{1,17},{9,25},{17,1},{25,9},{2,18},{10... | collective-permute-start | bytes 786440 | tf_op jit(solution)/shard_map/ppermute | solution.py:30
  161.4 10.8 %collective-permute-start.37 = (bf16[2,64,1024]{2,1,0:T(8,128)(2,1)S(1)}, bf16[2,64,1024]{2,1,0:T(8,128)(2,1)S(1)}, u32[]{:S(2)}, u32[]{:S(2)}) collective-permute-start(bf16[2,64,1024]{2,1,0:T(8,128)(2,1)S(1)} %get-tuple-element.119), channel_id=1, source_target_pairs={{0,8},{8,0},{16,24},{24,16},{1,9},{9,1},{17,25},{25,17},{2,10},{10... | collective-permute-start | bytes 786440 | tf_op jit(solution)/shard_map/ppermute | solution.py:30
  163.2 5.9 %collective-permute-start.36 = (f32[8,128]{1,0:T(8,128)S(1)}, f32[8,128]{1,0:T(8,128)S(1)}, u32[]{:S(2)}, u32[]{:S(2)}) collective-permute-start(f32[8,128]{1,0:T(8,128)S(1)} %broadcast_in_dim.11), channel_id=1, source_target_pairs={{0,8},{8,0},{16,24},{24,16},{1,9},{9,1},{17,25},{25,17},{2,10},{10... | collective-permute-start | bytes 12296 | tf_op jit(solution)/shard_map/ppermute | solution.py:30
  169.1 8.1 %collective-permute-start.41 = (bf16[2,64,1024]{2,1,0:T(8,128)(2,1)S(1)}, bf16[2,64,1024]{2,1,0:T(8,128)(2,1)S(1)}, u32[]{:S(2)}, u32[]{:S(2)}) collective-permute-start(bf16[2,64,1024]{2,1,0:T(8,128)(2,1)S(1)} %get-tuple-element.127), channel_id=1, source_target_pairs={{0,16},{8,24},{16,0},{24,8},{1,17},{9,25},{17,1},{25,9},{2,18},{10... | collective-permute-start | bytes 786440 | tf_op jit(solution)/shard_map/ppermute | solution.py:30
  170.7 9.0 %collective-permute-start.40 = (bf16[2,64,1024]{2,1,0:T(8,128)(2,1)S(1)}, bf16[2,64,1024]{2,1,0:T(8,128)(2,1)S(1)}, u32[]{:S(2)}, u32[]{:S(2)}) collective-permute-start(bf16[2,64,1024]{2,1,0:T(8,128)(2,1)S(1)} %get-tuple-element.125), channel_id=1, source_target_pairs={{0,8},{8,0},{16,24},{24,16},{1,9},{9,1},{17,25},{25,17},{2,10},{10... | collective-permute-start | bytes 786440 | tf_op jit(solution)/shard_map/ppermute | solution.py:30
  173.7 9.0 %collective-permute-start.47 = (bf16[2,64,1024]{2,1,0:T(8,128)(2,1)S(1)}, bf16[2,64,1024]{2,1,0:T(8,128)(2,1)S(1)}, u32[]{:S(2)}, u32[]{:S(2)}) collective-permute-start(bf16[2,64,1024]{2,1,0:T(8,128)(2,1)S(1)} %get-tuple-element.135), channel_id=1, source_target_pairs={{0,8},{8,0},{16,24},{24,16},{1,9},{9,1},{17,25},{25,17},{2,10},{10... | collective-permute-start | bytes 786440 | tf_op jit(solution)/shard_map/ppermute | solution.py:30
  174.3 8.4 %collective-permute-start.46 = (bf16[2,64,1024]{2,1,0:T(8,128)(2,1)S(1)}, bf16[2,64,1024]{2,1,0:T(8,128)(2,1)S(1)}, u32[]{:S(2)}, u32[]{:S(2)}) collective-permute-start(bf16[2,64,1024]{2,1,0:T(8,128)(2,1)S(1)} %get-tuple-element.133), channel_id=1, source_target_pairs={{0,16},{8,24},{16,0},{24,8},{1,17},{9,25},{17,1},{25,9},{2,18},{10... | collective-permute-start | bytes 786440 | tf_op jit(solution)/shard_map/ppermute | solution.py:30
  175.4 6.1 %collective-permute-start.39 = (f32[8,128]{1,0:T(8,128)S(1)}, f32[8,128]{1,0:T(8,128)S(1)}, u32[]{:S(2)}, u32[]{:S(2)}) collective-permute-start(f32[8,128]{1,0:T(8,128)S(1)} %broadcast_add_fusion), channel_id=1, source_target_pairs={{0,16},{8,24},{16,0},{24,8},{1,17},{9,25},{17,1},{25,9},{2,18},{10... | collective-permute-start | bytes 12296 | tf_op jit(solution)/shard_map/ppermute | solution.py:30
  (30 other events, 240.2 us)

commit v7 on v6

--- a/solution.py
+++ b/solution.py
@@ -4,7 +4,6 @@
 import jax.numpy as jnp
 from jax import lax
 from jax.experimental import pallas as pl
-from jax.experimental.layout import Layout, with_layout_constraint
 from jax.experimental.pallas import tpu as pltpu
 from jax.sharding import PartitionSpec as P
 
@@ -67,7 +66,8 @@
 
 
 def streamed(count, slots, copies_of, body):
-    for i in range(min(slots - 1, count)):
+    early = min(2, slots - 1, count)
+    for i in range(early):
         for copy in copies_of(i, i):
             copy.start()
 
@@ -75,14 +75,26 @@
     def _(i):
         ahead = i + slots - 1
 
-        @pl.when(ahead < count)
+        @pl.when(i == 0)
+        def _():
+            for copy in copies_of(0, 0):
+                copy.wait()
+            for later in range(early, min(slots, count)):
+                for copy in copies_of(later, later):
+                    copy.start()
+
+        @pl.when((i > 0) & (ahead < count))
         def _():
             for copy in copies_of(ahead, lax.rem(ahead, slots)):
                 copy.start()
 
         slot = lax.rem(i, slots)
-        for copy in copies_of(i, slot):
-            copy.wait()
+
+        @pl.when(i > 0)
+        def _():
+            for copy in copies_of(i, slot):
+                copy.wait()
+
         body(i, slot)
 
 
@@ -145,10 +157,35 @@
     )
 
 
-def decode_kernel(plan, index_ref, *refs):
-    n_in = plan.groups * plan.sources
+def arrange_kernel(plan, *refs):
+    parts, out_ref, stage = refs[:plan.sources], refs[-2], refs[-1]
+    count = stage.shape[0]
+
+    @pl.loop(0, plan.rows // count)
+    def _(i):
+        rows = pl.ds(pl.multiple_of(i * count, count), count)
+        for s in range(plan.sources):
+            stage[:, s, :] = parts[s][rows, :].astype(F32)
+        out_ref[rows] = stage[...].astype(BF16)
+
+
+def arrange(plan, encoded):
+    return call(
+        partial(arrange_kernel, plan),
+        "arrange",
+        [NEAR] * plan.sources,
+        jax.ShapeDtypeStruct((plan.rows, plan.sources, plan.width), BF16),
+        [pltpu.VMEM((ROW_TILE, plan.sources, plan.width), F32)],
+        encoded,
+    )
+
+
+def decode_kernel(plan, lo, hi, index_ref, *refs):
+    n_in = plan.groups * (hi - lo)
     pieces, w_ref, outs = refs[:n_in], refs[n_in], refs[n_in + 1:-4]
     x_buf, w_buf, x_sem, w_sem = refs[-4:]
+    if lo:
+        before_ref, outs, before_buf = outs[0], outs[1:-1], outs[-1]
     half = plan.tokens // 2
     core = index_ref[0]
     tile = w_buf.shape[2]
@@ -159,7 +196,7 @@
             place = index_ref[1 + plan.sources + j * plan.pairs + b] * plan.rows_feat
             for owner in range(2):
                 to = pl.multiple_of(place + jnp.where(core == owner, half, 0), ROW_TILE)
-                for s in range(plan.sources):
+                for s in range(hi - lo):
                     placing.append(pltpu.make_async_copy(
                         pieces[s * plan.groups + j].at[
                             pl.ds((2 * b + owner) * plan.rows_feat, plan.rows_feat)
@@ -174,29 +211,39 @@
 
     def copies_of(i, slot):
         cols = pl.ds(pl.multiple_of(i * tile, tile), tile)
-        return [
+        copies = [
             pltpu.make_async_copy(
                 w_ref.at[s, 0, :, cols],
-                w_buf.at[slot, pl.ds(s * plan.width, plan.width)],
-                w_sem.at[slot, s],
+                w_buf.at[slot, pl.ds((s - lo) * plan.width, plan.width)],
+                w_sem.at[slot, s - lo],
             )
-            for s in range(plan.sources)
+            for s in range(lo, hi)
         ]
+        if lo:
+            copies.append(pltpu.make_async_copy(
+                before_ref.at[:, cols], before_buf.at[slot], w_sem.at[slot, hi - lo]
+            ))
+        return copies
 
     def step(i, slot):
         @pl.when(i == 0)
         def _():
             for copy in placing:
                 copy.wait()
-            for s in range(plan.sources):
+            for s in range(lo, hi):
                 @pl.when(index_ref[1 + s] == 0)
-                def _(s=s):
+                def _(s=s - lo):
                     x_buf[:, s * plan.width:(s + 1) * plan.width] = jnp.zeros(
                         (plan.tokens, plan.width), BF16
                     )
 
         cols = pl.ds(pl.multiple_of(i * tile, tile), tile)
         product = jnp.dot(x_buf[...], w_buf[slot], preferred_element_type=F32)
+        if lo:
+            product = product + before_buf[slot]
+        if hi < plan.sources:
+            outs[0][:, cols] = product
+            return
         for c in range(plan.chunks):
             for d in range(plan.depth):
                 first = d * plan.rows_feat + c * plan.piece
@@ -207,24 +254,31 @@
     streamed(plan.model // tile, w_buf.shape[0], copies_of, step)
 
 
-def decode(plan, index, pieces, w_dec):
+def decode(plan, lo, hi, index, pieces, w_dec, before):
     tile = pick_tile(plan.model, 256)
     shape = (plan.depth * plan.piece, plan.model)
-    outs = call(
-        partial(decode_kernel, plan),
+    if hi < plan.sources:
+        out_shape = [jax.ShapeDtypeStruct((plan.tokens, plan.model), F32)]
+    else:
+        out_shape = [jax.ShapeDtypeStruct(shape, BF16)] * plan.chunks
+        out_shape += [jax.ShapeDtypeStruct(shape, F32)] * plan.chunks
+    scratch = [
+        pltpu.VMEM((plan.tokens, (hi - lo) * plan.width), BF16),
+        pltpu.VMEM((WEIGHT_SLOTS, (hi - lo) * plan.width, tile), BF16),
+        pltpu.SemaphoreType.DMA((len(pieces) * plan.per_group,)),
+        pltpu.SemaphoreType.DMA((WEIGHT_SLOTS, hi - lo + 1)),
+    ]
+    if before:
+        scratch = [pltpu.VMEM((WEIGHT_SLOTS, plan.tokens, tile), F32)] + scratch
+    return call(
+        partial(decode_kernel, plan, lo, hi),
         "decode",
-        [SCALARS] + [ANYWHERE] * len(pieces) + [FAR],
-        [jax.ShapeDtypeStruct(shape, BF16)] * plan.chunks
-        + [jax.ShapeDtypeStruct(shape, F32)] * plan.chunks,
-        [
-            pltpu.VMEM((plan.tokens, plan.sources * plan.width), BF16),
-            pltpu.VMEM((WEIGHT_SLOTS, plan.sources * plan.width, tile), BF16),
-            pltpu.SemaphoreType.DMA((len(pieces) * plan.per_group,)),
-            pltpu.SemaphoreType.DMA((WEIGHT_SLOTS, plan.sources)),
-        ],
-        (index, *pieces, w_dec),
-    )
-    return outs[:plan.chunks], outs[plan.chunks:]
+        [SCALARS] + [ANYWHERE] * len(pieces) + [FAR] * (1 + len(before)),
+        out_shape,
+        scratch,
+        (index, *pieces, w_dec, *before),
+        vmem=MOST_VMEM_BYTES,
+    )
 
 
 def gradient_kernel(plan, index_ref, *refs):
@@ -382,12 +436,12 @@
     index = jnp.concatenate([core[None], feeds, jnp.stack(offsets), jnp.stack(places)])
 
     encoded = [encode(plan, s, resid, w_enc, b_enc) for s in range(plan.sources)]
-    active = with_layout_constraint(jnp.stack(encoded, axis=1), Layout((0, 1, 2)))
+    active = arrange(plan, encoded)
 
     pieces, arrived = [], []
     for s, mine in enumerate(encoded):
         bits = plan.lanes[s % len(plan.lanes)]
-        mine, = after([mine], arrived[s - 2] if s >= 2 else [])
+        mine, = after([mine], arrived[min(s, 2) - 1] if s else [])
         held = {0: mine}
         for bit in bits:
             held.update(
@@ -396,8 +450,13 @@
         pieces += [held[j] for j in range(groups)]
         arrived.append([held[bit] for bit in bits])
 
-    sends, keeps = decode(plan, index, after(pieces, [active]), w_dec)
-    partial_rows = []
+    middle = plan.sources // 2
+    head, tail = pieces[:middle * groups], pieces[middle * groups:]
+    before = decode(plan, 0, middle, index, after(head, encoded), w_dec, [])
+    tail = after(tail, [active, *before])
+    decoded = decode(plan, middle, plan.sources, index, tail, w_dec, before)
+    sends, keeps = decoded[:chunks], decoded[chunks:]
+    recon_parts, errors, first_errors = [], [], []
     earlier = []
     for c in range(chunks):
         other = swap(sends[c], "feat", feats, 1)
@@ -406,29 +465,31 @@
             + other[d * plan.piece:(d + 1) * plan.piece].astype(F32)
             for d in range(plan.depth)
         }
-        for bit in plan.level_bits:
+        for step, bit in enumerate(plan.level_bits):
             away = {d: held.pop(d).astype(BF16) for d in sorted(held, reverse=True) if d & bit}
-            if bit == plan.level_bits[0]:
-                away = dict(zip(away, after(away.values(), earlier)))
+            wait = earlier if not step else first_errors[-1:]
+            away = dict(zip(away, after(away.values(), wait)))
             got = {d: swap(x, "feat", feats, 2 * bit) for d, x in away.items()}
-            if bit == plan.level_bits[0]:
+            if not step:
                 earlier = list(got.values())[:1]
             for d, x in got.items():
                 held[d ^ bit] = held[d ^ bit] + x.astype(F32)
-        partial_rows.append(held[0])
-
-    recon_parts, errors, first_errors = [], [], []
-    for c in range(chunks):
-        recon_rows, = after([partial_rows[c]], first_errors[-1:])
+        recon_rows, = after([held[0]], first_errors[-1:])
+
         first = feat * plan.rows_feat + c * plan.piece
         own_targets = lax.dynamic_slice_in_dim(targets[0], first, plan.piece, 0)
         difference = recon_rows - own_targets.astype(F32)
         recon_parts.append(recon_rows.astype(BF16))
-        held = {0: difference.astype(BF16)}
-        for bit in reversed(plan.level_bits):
-            held.update(
-                {d | bit: swap(x, "feat", feats, 2 * bit) for d, x in list(held.items())}
-            )
+        error = difference.astype(BF16)
+        held = {0: error}
+        if c:
+            for d in range(plan.depth - 1, 0, -1):
+                held[d] = swap(error, "feat", feats, 2 * d)
+        else:
+            for bit in reversed(plan.level_bits):
+                held.update(
+                    {d | bit: swap(x, "feat", feats, 2 * bit) for d, x in list(held.items())}
+                )
         first_errors.append(held[plan.level_bits[-1]])
         every = [held[d] for d in range(plan.depth)]
         errors.append(every + [swap(e, "feat", feats, 1) for e in every])
@@ -452,17 +513,18 @@
                     if not step:
                         first_got.append(got[0])
                         second += away
-                        away = after(away, [] if feat_grad is None else [feat_grad])
             kept_all.append(kept[0])
             got_all.append(got[0])
-        feat_grad = finish(plan, c, kept_all, got_all, feat_grad)
+        previous = feat_grad
+        feat_grad = finish(plan, c, kept_all, got_all, previous)
         earlier = second
 
+    squares, = after([squares], second)
     loss = jnp.full((8, 128), jnp.sum(squares), F32)
     for i, bit in enumerate(1 << i for i in range(groups.bit_length() - 1)):
         loss = loss + swap(loss, "grp", groups, bit)
-        if not i:
-            loss, = after([loss], first_got)
+        if not i and previous is not None:
+            loss, = after([loss], [previous])
     entries = targets.shape[0] * groups * plan.tokens * plan.model
     recon_loss = loss[0, 0] / entries
     recon = jnp.concatenate(recon_parts, axis=0)[None]

time: 186 us -> 193 us (1.038)
  local copies, waits for them, and re-layouts: 21.8 us -> 4.99 us
  waiting for transfers between devices: 41.6 us -> 54.6 us
  Pallas kernels: 59.4 us -> 71.3 us
    ppermute x48, waiting for transfers between devices: 41.6 us -> 54.6 us  [swap(): return lax.ppermute(x, axis, [(i, i ^ offset) for i in range(size)])]
    pallas_call x9 -> x11, Pallas kernels: 59.4 us -> 71.3 us  [call(): pl.pallas_call(kernel, in_specs=in_specs, out_shape=out_shape, scratch_sh...]
    unnamed x60 -> x38, local copies, waits for them, and re-layouts: 14.8 us -> 3.25 us
    another operation x4 -> x0, local copies, waits for them, and re-layouts: 5.8 us -> none  [per_device(): jnp.stack(encoded, axis=1)]
    another operation x1 -> x0, other arithmetic: 4.96 us -> none  [per_device(): jnp.stack(encoded, axis=1)]
    convert_element_type x3 -> x4, other arithmetic: 0.26 us -> 3.01 us  [per_device(): away, kept = ([x.astype(BF16) for x in sums[:cut]], sums[cut:])]
  transfers between devices with their start and end apart: 48 -> 48, of which waited for: 15 -> 14; matrix products, arithmetic and copies ran while one was open for 11% -> 6% of each run, Pallas kernels for 21% -> 28%
where the time goes in v7:
time: 193 us
  Pallas kernels  71.3 us (37%)
  waiting for transfers between devices  54.6 us (28%)
  starting transfers between devices  47.4 us (25%)
  other arithmetic  11.5 us (6%)
  local copies, waits for them, and re-layouts  4.99 us (3%)
  between operations  2.83 us (1%)
    pallas_call x11, Pallas kernels, call(): pl.pallas_call(kernel, in_specs=in_specs, out_shape=out_shape, scratch_sh...  71.3 us
    ppermute x48, waiting for transfers between devices, swap(): return lax.ppermute(x, axis, [(i, i ^ offset) for i in range(size)])  54.6 us
    ppermute x48, starting transfers between devices, swap(): return lax.ppermute(x, axis, [(i, i ^ offset) for i in range(size)])  47.4 us
  transfers between devices with their start and end apart: 48, of which 14 were waited for; matrix products, arithmetic and copies ran while one was open for 6% of the time, Pallas kernels for 28%

profile of v7, /device:TPU:0, one launch (start us, length us, event | category | flops | bytes accessed | tf_op | source)
XLA Modules:
  0.0 192.6 jit_solution(6887583004035842438)
XLA Ops:
  0.6 4.3 %encode.4.refs_0_ = bf16[128,1024]{1,0:T(8,128)(2,1)} custom-call(bf16[4,128,2304]{2,1,0:T(8,128)(2,1)} %resid_ref.7, bf16[4,2304,1024]{2,1,0:T(8,128)(2,1)} %w_ref.7, f32[4,1024]{1,0:T(4,128)} %b_ref.7), custom_call_target="tpu_custom_call" | custom-call | flops 1048576 | bytes 1024 | tf_op jit(solution)/shard_map/encode/pallas_call | solution.py:102
  4.9 3.0 %collective-permute-start = (bf16[128,1024]{1,0:T(8,128)(2,1)}, bf16[128,1024]{1,0:T(8,128)(2,1)S(1)}, u32[]{:S(2)}, u32[]{:S(2)}) collective-permute-start(bf16[128,1024]{1,0:T(8,128)(2,1)} %encode.4.refs_0_), channel_id=1, source_target_pairs={{0,8},{8,0},{16,24},{24,16},{1,9},{9,1},{17,25},{25,17},{2,10},{10... | collective-permute-start | bytes 786440 | tf_op jit(solution)/shard_map/ppermute | solution.py:29
  7.9 1.5 collective-permute-start.1
  9.4 4.3 %encode.5.refs_1_.refs_4_ = bf16[128,1024]{1,0:T(8,128)(2,1)} custom-call(bf16[4,128,2304]{2,1,0:T(8,128)(2,1)} %resid_ref.7, bf16[4,2304,1024]{2,1,0:T(8,128)(2,1)} %w_ref.7, f32[4,1024]{1,0:T(4,128)} %b_ref.7), custom_call_target="tpu_custom_call" | custom-call | flops 1048576 | bytes 1024 | tf_op jit(solution)/shard_map/encode/pallas_call | solution.py:102
  14.4 1.5 collective-permute-done.1.refs_2_
  15.9 1.5 collective-permute-start.2
  18.0 4.3 %encode.6.refs_2_.refs_0_ = bf16[128,1024]{1,0:T(8,128)(2,1)} custom-call(bf16[4,128,2304]{2,1,0:T(8,128)(2,1)} %resid_ref.7, bf16[4,2304,1024]{2,1,0:T(8,128)(2,1)} %w_ref.7, f32[4,1024]{1,0:T(4,128)} %b_ref.7), custom_call_target="tpu_custom_call" | custom-call | flops 1048576 | bytes 1024 | tf_op jit(solution)/shard_map/encode/pallas_call | solution.py:102
  22.3 4.4 %encode.7.refs_3_.refs_4_ = bf16[128,1024]{1,0:T(8,128)(2,1)} custom-call(bf16[4,128,2304]{2,1,0:T(8,128)(2,1)} %resid_ref.7, bf16[4,2304,1024]{2,1,0:T(8,128)(2,1)} %w_ref.7, f32[4,1024]{1,0:T(4,128)} %b_ref.7), custom_call_target="tpu_custom_call" | custom-call | flops 1048576 | bytes 1024 | tf_op jit(solution)/shard_map/encode/pallas_call | solution.py:102
  27.2 1.7 collective-permute-start.8
  28.9 1.5 collective-permute-start.4
  30.9 1.5 collective-permute-start.7
  32.4 3.6 %collective-permute-done.10.refs_3_ = bf16[128,1024]{1,0:T(8,128)(2,1)S(1)} collective-permute-done((bf16[128,1024]{1,0:T(8,128)(2,1)S(1)}, bf16[128,1024]{1,0:T(8,128)(2,1)S(1)}, u32[]{:S(2)}, u32[]{:S(2)}) %collective-permute-start.10) | collective-permute-done | bytes 262176 | tf_op jit(solution)/shard_map/ppermute | solution.py:29
  36.4 5.3 %collective-permute-done.8.refs_6_ = bf16[128,1024]{1,0:T(8,128)(2,1)S(1)} collective-permute-done((bf16[128,1024]{1,0:T(8,128)(2,1)}, bf16[128,1024]{1,0:T(8,128)(2,1)S(1)}, u32[]{:S(2)}, u32[]{:S(2)}) %collective-permute-start.8) | collective-permute-done | bytes 262176 | tf_op jit(solution)/shard_map/ppermute | solution.py:29
  41.6 1.5 collective-permute-start.9
  45.2 1.7 arrange.1
  47.7 11.9 %decode.2.refs_9_ = f32[512,2304]{1,0:T(8,128)} custom-call(s32[17]{0:T(128)} %concatenate.6.index_ref, bf16[128,1024]{1,0:T(8,128)(2,1)} %encode.4.refs_0_, bf16[128,1024]{1,0:T(8,128)(2,1)} %copy-done.6, bf16[128,1024]{1,0:T(8,128)(2,1)} %copy-done.7, bf16[128,1024]{1,0:T(8,128)(2,1)} %copy-done.13, bf16[128,1024]{1,0:T(8,128)(2,1)} %encode.5.refs_1_.refs_4_, ...), custom_call_target="tpu_custom_call" | custom-call | flops 1048576 | bytes 1024 | tf_op jit(solution)/shard_map/decode/pallas_call | solution.py:102
  61.2 11.9 %decode.3 = (bf16[128,2304]{1,0:T(8,128)(2,1)}, bf16[128,2304]{1,0:T(8,128)(2,1)}, f32[128,2304]{1,0:T(8,128)}, f32[128,2304]{1,0:T(8,128)}) custom-call(s32[17]{0:T(128)} %concatenate.6.index_ref, bf16[128,1024]{1,0:T(8,128)(2,1)} %encode.6.refs_2_.refs_0_, bf16[128,1024]{1,0:T(8,128)(2,1)} %copy-done.10, bf16[128,1024]{1,0:T(8,128)(2,1)} %copy-done.14, ...), custom_call_target="tpu_custom_call" | custom-call | flops 1048576 | bytes 1024 | tf_op jit(solution)/shard_map/decode/pallas_call | solution.py:102
  73.2 2.2 %collective-permute-done.12 = bf16[128,2304]{1,0:T(8,128)(2,1)S(1)} collective-permute-done((bf16[128,2304]{1,0:T(8,128)(2,1)}, bf16[128,2304]{1,0:T(8,128)(2,1)S(1)}, u32[]{:S(2)}, u32[]{:S(2)}) %collective-permute-start.12) | collective-permute-done | bytes 589856 | tf_op jit(solution)/shard_map/ppermute | solution.py:29
  75.4 1.1 add_convert_fusion.9
  76.5 1.6 collective-permute-start.14
  78.6 4.7 %collective-permute-done.14 = bf16[32,2304]{1,0:T(8,128)(2,1)S(1)} collective-permute-done((bf16[32,2304]{1,0:T(8,128)(2,1)S(1)}, bf16[32,2304]{1,0:T(8,128)(2,1)S(1)}, u32[]{:S(2)}, u32[]{:S(2)}) %collective-permute-start.14) | collective-permute-done | bytes 147488 | tf_op jit(solution)/shard_map/ppermute | solution.py:29
  83.3 1.0 add_convert_fusion.7
  84.3 2.7 %collective-permute-start.15 = (bf16[32,2304]{1,0:T(8,128)(2,1)S(1)}, bf16[32,2304]{1,0:T(8,128)(2,1)S(1)}, u32[]{:S(2)}, u32[]{:S(2)}) collective-permute-start(bf16[32,2304]{1,0:T(8,128)(2,1)S(1)} %add_convert_fusion.7), channel_id=1, source_target_pairs={{0,4},{1,5},{2,6},{3,7},{4,0},{5,1},{6,2},{7,3},{8,12},{9,13},{10,... | collective-permute-start | bytes 442376 | tf_op jit(solution)/shard_map/ppermute | solution.py:29
  87.0 1.6 collective-permute-start.18
  89.1 3.3 %collective-permute-done.15 = bf16[32,2304]{1,0:T(8,128)(2,1)S(1)} collective-permute-done((bf16[32,2304]{1,0:T(8,128)(2,1)S(1)}, bf16[32,2304]{1,0:T(8,128)(2,1)S(1)}, u32[]{:S(2)}, u32[]{:S(2)}) %collective-permute-start.15) | collective-permute-done | bytes 147488 | tf_op jit(solution)/shard_map/ppermute | solution.py:29
  92.3 1.1 fusion.3
  93.4 2.3 %collective-permute-start.19 = (bf16[32,2304]{1,0:T(8,128)(2,1)S(1)}, bf16[32,2304]{1,0:T(8,128)(2,1)S(1)}, u32[]{:S(2)}, u32[]{:S(2)}) collective-permute-start(bf16[32,2304]{1,0:T(8,128)(2,1)S(1)} %get-tuple-element.98.refs_0_), channel_id=1, source_target_pairs={{0,4},{1,5},{2,6},{3,7},{4,0},{5,1},{6,2},{7,3},{8,12},{9,13},{10,... | collective-permute-start | bytes 442376 | tf_op jit(solution)/shard_map/ppermute | solution.py:29
  95.8 2.2 %collective-permute-start.21 = (bf16[32,2304]{1,0:T(8,128)(2,1)S(1)}, bf16[32,2304]{1,0:T(8,128)(2,1)S(1)}, u32[]{:S(2)}, u32[]{:S(2)}) collective-permute-start(bf16[32,2304]{1,0:T(8,128)(2,1)S(1)} %get-tuple-element.98.refs_0_), channel_id=1, source_target_pairs={{0,2},{1,3},{2,0},{3,1},{4,6},{5,7},{6,4},{7,5},{8,10},{9,11},{10,... | collective-permute-start | bytes 442376 | tf_op jit(solution)/shard_map/ppermute | solution.py:29
  98.0 5.3 %collective-permute-done.19.refs_2_ = bf16[32,2304]{1,0:T(8,128)(2,1)S(1)} collective-permute-done((bf16[32,2304]{1,0:T(8,128)(2,1)S(1)}, bf16[32,2304]{1,0:T(8,128)(2,1)S(1)}, u32[]{:S(2)}, u32[]{:S(2)}) %collective-permute-start.19) | collective-permute-done | bytes 147488 | tf_op jit(solution)/shard_map/ppermute | solution.py:29
  103.5 3.0 %collective-permute-start.22 = (bf16[32,2304]{1,0:T(8,128)(2,1)S(1)}, bf16[32,2304]{1,0:T(8,128)(2,1)S(1)}, u32[]{:S(2)}, u32[]{:S(2)}) collective-permute-start(bf16[32,2304]{1,0:T(8,128)(2,1)S(1)} %collective-permute-done.19.refs_2_), channel_id=1, source_target_pairs={{0,2},{1,3},{2,0},{3,1},{4,6},{5,7},{6,4},{7,5},{8,10},{9,11},{10,... | collective-permute-start | bytes 442376 | tf_op jit(solution)/shard_map/ppermute | solution.py:29
  107.0 3.7 %collective-permute-done.20 = bf16[32,2304]{1,0:T(8,128)(2,1)S(1)} collective-permute-done((bf16[32,2304]{1,0:T(8,128)(2,1)S(1)}, bf16[32,2304]{1,0:T(8,128)(2,1)S(1)}, u32[]{:S(2)}, u32[]{:S(2)}) %collective-permute-start.20) | collective-permute-done | bytes 147488 | tf_op jit(solution)/shard_map/ppermute | solution.py:29
  110.8 1.8 collective-permute-done.22.refs_3_
  113.7 1.6 collective-permute-start.28
  115.4 2.6 %collective-permute-start.29 = (bf16[32,2304]{1,0:T(8,128)(2,1)S(1)}, bf16[32,2304]{1,0:T(8,128)(2,1)S(1)}, u32[]{:S(2)}, u32[]{:S(2)}) collective-permute-start(bf16[32,2304]{1,0:T(8,128)(2,1)S(1)} %get-tuple-element.109.refs_0_), channel_id=1, source_target_pairs={{0,6},{1,7},{2,4},{3,5},{4,2},{5,3},{6,0},{7,1},{8,14},{9,15},{10,... | collective-permute-start | bytes 442376 | tf_op jit(solution)/shard_map/ppermute | solution.py:29
  118.0 13.1 %gradient.2 = (bf16[2,64,1024]{2,1,0:T(8,128)(2,1)S(1)}, bf16[2,64,1024]{2,1,0:T(8,128)(2,1)S(1)}, f32[2,64,1024]{2,1,0:T(8,128)S(1)}, f32[2,64,1024]{2,1,0:T(8,...) custom-call(s32[17]{0:T(128)S(1)} %copy-done.4, ...), custom_call_target="tpu_custom_call" | custom-call | flops 1048576 | bytes 1024 | tf_op jit(solution)/shard_map/gradient/pallas_call | solution.py:102
  131.1 1.6 collective-permute-start.35
  135.0 5.2 %collective-permute-done.35 = bf16[2,64,1024]{2,1,0:T(8,128)(2,1)S(1)} collective-permute-done((bf16[2,64,1024]{2,1,0:T(8,128)(2,1)S(1)}, bf16[2,64,1024]{2,1,0:T(8,128)(2,1)S(1)}, u32[]{:S(2)}, u32[]{:S(2)}) %collective-permute-start.35) | collective-permute-done | bytes 262176 | tf_op jit(solution)/shard_map/ppermute | solution.py:29
  141.6 1.5 collective-permute-start.42
  143.9 1.5 collective-permute-start.41
  145.4 13.0 %gradient.3 = (bf16[2,64,1024]{2,1,0:T(8,128)(2,1)S(1)}, bf16[2,64,1024]{2,1,0:T(8,128)(2,1)S(1)}, f32[2,64,1024]{2,1,0:T(8,128)S(1)}, f32[2,64,1024]{2,1,0:T(8,...) custom-call(s32[17]{0:T(128)S(1)} %copy-done.4, ...), custom_call_target="tpu_custom_call" | custom-call | flops 1048576 | bytes 1024 | tf_op jit(solution)/shard_map/gradient/pallas_call | solution.py:102
  159.0 1.5 collective-permute-start.37
  161.3 10.7 %collective-permute-done.37 = bf16[2,64,1024]{2,1,0:T(8,128)(2,1)S(1)} collective-permute-done((bf16[2,64,1024]{2,1,0:T(8,128)(2,1)S(1)}, bf16[2,64,1024]{2,1,0:T(8,128)(2,1)S(1)}, u32[]{:S(2)}, u32[]{:S(2)}) %collective-permute-start.37) | collective-permute-done | bytes 262176 | tf_op jit(solution)/shard_map/ppermute | solution.py:29
  173.2 1.6 collective-permute-start.47
  179.0 1.2 finish.2.refs_4_
  180.2 4.4 %collective-permute-done.38 = f32[8,128]{1,0:T(8,128)S(1)} collective-permute-done((f32[8,128]{1,0:T(8,128)S(1)}, f32[8,128]{1,0:T(8,128)S(1)}, u32[]{:S(2)}, u32[]{:S(2)}) %collective-permute-start.38) | collective-permute-done | bytes 4128 | tf_op jit(solution)/shard_map/ppermute | solution.py:29
  185.9 1.0 convert_add_fusion.1.refs_0_
  186.9 2.1 %collective-permute-done.43 = f32[8,128]{1,0:T(8,128)S(1)} collective-permute-done((f32[8,128]{1,0:T(8,128)S(1)}, f32[8,128]{1,0:T(8,128)S(1)}, u32[]{:S(2)}, u32[]{:S(2)}) %collective-permute-start.43) | collective-permute-done | bytes 4128 | tf_op jit(solution)/shard_map/ppermute | solution.py:29
  190.2 1.2 finish.3
  (121 shorter events, 23.0 us)
Async XLA Ops:
  4.9 9.5 %collective-permute-start = (bf16[128,1024]{1,0:T(8,128)(2,1)}, bf16[128,1024]{1,0:T(8,128)(2,1)S(1)}, u32[]{:S(2)}, u32[]{:S(2)}) collective-permute-start(bf16[128,1024]{1,0:T(8,128)(2,1)} %encode.4.refs_0_), channel_id=1, source_target_pairs={{0,8},{8,0},{16,24},{24,16},{1,9},{9,1},{17,25},{25,17},{2,10},{10... | collective-permute-start | bytes 786440 | tf_op jit(solution)/shard_map/ppermute | solution.py:29
  7.9 8.0 %collective-permute-start.1 = (bf16[128,1024]{1,0:T(8,128)(2,1)}, bf16[128,1024]{1,0:T(8,128)(2,1)S(1)}, u32[]{:S(2)}, u32[]{:S(2)}) collective-permute-start(bf16[128,1024]{1,0:T(8,128)(2,1)} %encode.4.refs_0_), channel_id=1, source_target_pairs={{0,16},{8,24},{16,0},{24,8},{1,17},{9,25},{17,1},{25,9},{2,18},{10... | collective-permute-start | bytes 786440 | tf_op jit(solution)/shard_map/ppermute | solution.py:29
  15.9 11.2 %collective-permute-start.2 = (bf16[128,1024]{1,0:T(8,128)(2,1)}, bf16[128,1024]{1,0:T(8,128)(2,1)S(1)}, u32[]{:S(2)}, u32[]{:S(2)}) collective-permute-start(bf16[128,1024]{1,0:T(8,128)(2,1)} %encode.5.refs_1_.refs_4_), channel_id=1, source_target_pairs={{0,16},{8,24},{16,0},{24,8},{1,17},{9,25},{17,1},{25,9},{2,18},{10... | collective-permute-start | bytes 786440 | tf_op jit(solution)/shard_map/ppermute | solution.py:29
  17.4 9.7 %collective-permute-start.3 = (bf16[128,1024]{1,0:T(8,128)(2,1)}, bf16[128,1024]{1,0:T(8,128)(2,1)S(1)}, u32[]{:S(2)}, u32[]{:S(2)}) collective-permute-start(bf16[128,1024]{1,0:T(8,128)(2,1)} %encode.5.refs_1_.refs_4_), channel_id=1, source_target_pairs={{0,8},{8,0},{16,24},{24,16},{1,9},{9,1},{17,25},{25,17},{2,10},{10... | collective-permute-start | bytes 786440 | tf_op jit(solution)/shard_map/ppermute | solution.py:29
  26.7 9.3 %collective-permute-start.10 = (bf16[128,1024]{1,0:T(8,128)(2,1)S(1)}, bf16[128,1024]{1,0:T(8,128)(2,1)S(1)}, u32[]{:S(2)}, u32[]{:S(2)}) collective-permute-start(bf16[128,1024]{1,0:T(8,128)(2,1)S(1)} %collective-permute-done.refs_1_), channel_id=1, source_target_pairs={{0,16},{8,24},{16,0},{24,8},{1,17},{9,25},{17,1},{25,9},{2,18},{10... | collective-permute-start | bytes 786440 | tf_op jit(solution)/shard_map/ppermute | solution.py:29
  27.2 14.5 %collective-permute-start.8 = (bf16[128,1024]{1,0:T(8,128)(2,1)}, bf16[128,1024]{1,0:T(8,128)(2,1)S(1)}, u32[]{:S(2)}, u32[]{:S(2)}) collective-permute-start(bf16[128,1024]{1,0:T(8,128)(2,1)} %encode.7.refs_3_.refs_4_), channel_id=1, source_target_pairs={{0,16},{8,24},{16,0},{24,8},{1,17},{9,25},{17,1},{25,9},{2,18},{10... | collective-permute-start | bytes 786440 | tf_op jit(solution)/shard_map/ppermute | solution.py:29
  28.9 14.2 %collective-permute-start.4 = (bf16[128,1024]{1,0:T(8,128)(2,1)S(1)}, bf16[128,1024]{1,0:T(8,128)(2,1)S(1)}, u32[]{:S(2)}, u32[]{:S(2)}) collective-permute-start(bf16[128,1024]{1,0:T(8,128)(2,1)S(1)} %copy-done), channel_id=1, source_target_pairs={{0,8},{8,0},{16,24},{24,16},{1,9},{9,1},{17,25},{25,17},{2,10},{10... | collective-permute-start | bytes 786440 | tf_op jit(solution)/shard_map/ppermute | solution.py:29
  30.4 16.6 %collective-permute-start.11 = (bf16[128,1024]{1,0:T(8,128)(2,1)S(1)}, bf16[128,1024]{1,0:T(8,128)(2,1)S(1)}, u32[]{:S(2)}, u32[]{:S(2)}) collective-permute-start(bf16[128,1024]{1,0:T(8,128)(2,1)S(1)} %collective-permute-done.2.refs_6_), channel_id=1, source_target_pairs={{0,8},{8,0},{16,24},{24,16},{1,9},{9,1},{17,25},{25,17},{2,10},{10... | collective-permute-start | bytes 786440 | tf_op jit(solution)/shard_map/ppermute | solution.py:29
  30.9 28.7 %collective-permute-start.7 = (bf16[128,1024]{1,0:T(8,128)(2,1)}, bf16[128,1024]{1,0:T(8,128)(2,1)S(1)}, u32[]{:S(2)}, u32[]{:S(2)}) collective-permute-start(bf16[128,1024]{1,0:T(8,128)(2,1)} %encode.7.refs_3_.refs_4_), channel_id=1, source_target_pairs={{0,8},{8,0},{16,24},{24,16},{1,9},{9,1},{17,25},{25,17},{2,10},{10... | collective-permute-start | bytes 786440 | tf_op jit(solution)/shard_map/ppermute | solution.py:29
  36.0 23.6 %collective-permute-start.5 = (bf16[128,1024]{1,0:T(8,128)(2,1)S(1)}, bf16[128,1024]{1,0:T(8,128)(2,1)S(1)}, u32[]{:S(2)}, u32[]{:S(2)}) collective-permute-start(bf16[128,1024]{1,0:T(8,128)(2,1)S(1)} %copy-done), channel_id=1, source_target_pairs={{0,16},{8,24},{16,0},{24,8},{1,17},{9,25},{17,1},{25,9},{2,18},{10... | collective-permute-start | bytes 786440 | tf_op jit(solution)/shard_map/ppermute | solution.py:29
  41.6 18.0 %collective-permute-start.9 = (bf16[128,1024]{1,0:T(8,128)(2,1)S(1)}, bf16[128,1024]{1,0:T(8,128)(2,1)S(1)}, u32[]{:S(2)}, u32[]{:S(2)}) collective-permute-start(bf16[128,1024]{1,0:T(8,128)(2,1)S(1)} %collective-permute-done.8.refs_6_), channel_id=1, source_target_pairs={{0,8},{8,0},{16,24},{24,16},{1,9},{9,1},{17,25},{25,17},{2,10},{10... | collective-permute-start | bytes 786440 | tf_op jit(solution)/shard_map/ppermute | solution.py:29
  43.1 16.5 %collective-permute-start.6 = (bf16[128,1024]{1,0:T(8,128)(2,1)S(1)}, bf16[128,1024]{1,0:T(8,128)(2,1)S(1)}, u32[]{:S(2)}, u32[]{:S(2)}) collective-permute-start(bf16[128,1024]{1,0:T(8,128)(2,1)S(1)} %collective-permute-done.4.refs_1_), channel_id=1, source_target_pairs={{0,16},{8,24},{16,0},{24,8},{1,17},{9,25},{17,1},{25,9},{2,18},{10... | collective-permute-start | bytes 786440 | tf_op jit(solution)/shard_map/ppermute | solution.py:29
  73.1 2.3 %collective-permute-start.12 = (bf16[128,2304]{1,0:T(8,128)(2,1)}, bf16[128,2304]{1,0:T(8,128)(2,1)S(1)}, u32[]{:S(2)}, u32[]{:S(2)}) collective-permute-start(bf16[128,2304]{1,0:T(8,128)(2,1)} %get-tuple-element.91), channel_id=1, source_target_pairs={{0,1},{1,0},{2,3},{3,2},{4,5},{5,4},{6,7},{7,6},{8,9},{9,8},{10,11... | collective-permute-start | bytes 1769480 | tf_op jit(solution)/shard_map/ppermute | solution.py:29
  76.5 6.8 %collective-permute-start.14 = (bf16[32,2304]{1,0:T(8,128)(2,1)S(1)}, bf16[32,2304]{1,0:T(8,128)(2,1)S(1)}, u32[]{:S(2)}, u32[]{:S(2)}) collective-permute-start(bf16[32,2304]{1,0:T(8,128)(2,1)S(1)} %get-tuple-element.141), channel_id=1, source_target_pairs={{0,2},{1,3},{2,0},{3,1},{4,6},{5,7},{6,4},{7,5},{8,10},{9,11},{10,... | collective-permute-start | bytes 442376 | tf_op jit(solution)/shard_map/ppermute | solution.py:29
  78.1 8.9 %collective-permute-start.16 = (bf16[128,2304]{1,0:T(8,128)(2,1)}, bf16[128,2304]{1,0:T(8,128)(2,1)S(1)}, u32[]{:S(2)}, u32[]{:S(2)}) collective-permute-start(bf16[128,2304]{1,0:T(8,128)(2,1)} %get-tuple-element.93), channel_id=1, source_target_pairs={{0,1},{1,0},{2,3},{3,2},{4,5},{5,4},{6,7},{7,6},{8,9},{9,8},{10,11... | collective-permute-start | bytes 1769480 | tf_op jit(solution)/shard_map/ppermute | solution.py:29
  78.1 11.0 %collective-permute-start.13 = (bf16[32,2304]{1,0:T(8,128)(2,1)S(1)}, bf16[32,2304]{1,0:T(8,128)(2,1)S(1)}, u32[]{:S(2)}, u32[]{:S(2)}) collective-permute-start(bf16[32,2304]{1,0:T(8,128)(2,1)S(1)} %get-tuple-element.140), channel_id=1, source_target_pairs={{0,2},{1,3},{2,0},{3,1},{4,6},{5,7},{6,4},{7,5},{8,10},{9,11},{10,... | collective-permute-start | bytes 442376 | tf_op jit(solution)/shard_map/ppermute | solution.py:29
  84.3 8.1 %collective-permute-start.15 = (bf16[32,2304]{1,0:T(8,128)(2,1)S(1)}, bf16[32,2304]{1,0:T(8,128)(2,1)S(1)}, u32[]{:S(2)}, u32[]{:S(2)}) collective-permute-start(bf16[32,2304]{1,0:T(8,128)(2,1)S(1)} %add_convert_fusion.7), channel_id=1, source_target_pairs={{0,4},{1,5},{2,6},{3,7},{4,0},{5,1},{6,2},{7,3},{8,12},{9,13},{10,... | collective-permute-start | bytes 442376 | tf_op jit(solution)/shard_map/ppermute | solution.py:29
  87.0 10.9 %collective-permute-start.18 = (bf16[32,2304]{1,0:T(8,128)(2,1)S(1)}, bf16[32,2304]{1,0:T(8,128)(2,1)S(1)}, u32[]{:S(2)}, u32[]{:S(2)}) collective-permute-start(bf16[32,2304]{1,0:T(8,128)(2,1)S(1)} %get-tuple-element.95), channel_id=1, source_target_pairs={{0,2},{1,3},{2,0},{3,1},{4,6},{5,7},{6,4},{7,5},{8,10},{9,11},{10,... | collective-permute-start | bytes 442376 | tf_op jit(solution)/shard_map/ppermute | solution.py:29
  88.6 17.9 %collective-permute-start.17 = (bf16[32,2304]{1,0:T(8,128)(2,1)S(1)}, bf16[32,2304]{1,0:T(8,128)(2,1)S(1)}, u32[]{:S(2)}, u32[]{:S(2)}) collective-permute-start(bf16[32,2304]{1,0:T(8,128)(2,1)S(1)} %get-tuple-element.94), channel_id=1, source_target_pairs={{0,2},{1,3},{2,0},{3,1},{4,6},{5,7},{6,4},{7,5},{8,10},{9,11},{10,... | collective-permute-start | bytes 442376 | tf_op jit(solution)/shard_map/ppermute | solution.py:29
  93.4 9.9 %collective-permute-start.19 = (bf16[32,2304]{1,0:T(8,128)(2,1)S(1)}, bf16[32,2304]{1,0:T(8,128)(2,1)S(1)}, u32[]{:S(2)}, u32[]{:S(2)}) collective-permute-start(bf16[32,2304]{1,0:T(8,128)(2,1)S(1)} %get-tuple-element.98.refs_0_), channel_id=1, source_target_pairs={{0,4},{1,5},{2,6},{3,7},{4,0},{5,1},{6,2},{7,3},{8,12},{9,13},{10,... | collective-permute-start | bytes 442376 | tf_op jit(solution)/shard_map/ppermute | solution.py:29
  95.8 10.9 %collective-permute-start.21 = (bf16[32,2304]{1,0:T(8,128)(2,1)S(1)}, bf16[32,2304]{1,0:T(8,128)(2,1)S(1)}, u32[]{:S(2)}, u32[]{:S(2)}) collective-permute-start(bf16[32,2304]{1,0:T(8,128)(2,1)S(1)} %get-tuple-element.98.refs_0_), channel_id=1, source_target_pairs={{0,2},{1,3},{2,0},{3,1},{4,6},{5,7},{6,4},{7,5},{8,10},{9,11},{10,... | collective-permute-start | bytes 442376 | tf_op jit(solution)/shard_map/ppermute | solution.py:29
  103.3 7.4 %collective-permute-start.20 = (bf16[32,2304]{1,0:T(8,128)(2,1)S(1)}, bf16[32,2304]{1,0:T(8,128)(2,1)S(1)}, u32[]{:S(2)}, u32[]{:S(2)}) collective-permute-start(bf16[32,2304]{1,0:T(8,128)(2,1)S(1)} %add_convert_fusion.4), channel_id=1, source_target_pairs={{0,4},{1,5},{2,6},{3,7},{4,0},{5,1},{6,2},{7,3},{8,12},{9,13},{10,... | collective-permute-start | bytes 442376 | tf_op jit(solution)/shard_map/ppermute | solution.py:29
  103.5 10.2 %collective-permute-start.23 = (bf16[32,2304]{1,0:T(8,128)(2,1)S(1)}, bf16[32,2304]{1,0:T(8,128)(2,1)S(1)}, u32[]{:S(2)}, u32[]{:S(2)}) collective-permute-start(bf16[32,2304]{1,0:T(8,128)(2,1)S(1)} %get-tuple-element.98.refs_0_), channel_id=1, source_target_pairs={{0,1},{1,0},{2,3},{3,2},{4,5},{5,4},{6,7},{7,6},{8,9},{9,8},{10,11... | collective-permute-start | bytes 442376 | tf_op jit(solution)/shard_map/ppermute | solution.py:29
  103.5 9.1 %collective-permute-start.22 = (bf16[32,2304]{1,0:T(8,128)(2,1)S(1)}, bf16[32,2304]{1,0:T(8,128)(2,1)S(1)}, u32[]{:S(2)}, u32[]{:S(2)}) collective-permute-start(bf16[32,2304]{1,0:T(8,128)(2,1)S(1)} %collective-permute-done.19.refs_2_), channel_id=1, source_target_pairs={{0,2},{1,3},{2,0},{3,1},{4,6},{5,7},{6,4},{7,5},{8,10},{9,11},{10,... | collective-permute-start | bytes 442376 | tf_op jit(solution)/shard_map/ppermute | solution.py:29
  106.5 11.5 %collective-permute-start.25 = (bf16[32,2304]{1,0:T(8,128)(2,1)S(1)}, bf16[32,2304]{1,0:T(8,128)(2,1)S(1)}, u32[]{:S(2)}, u32[]{:S(2)}) collective-permute-start(bf16[32,2304]{1,0:T(8,128)(2,1)S(1)} %collective-permute-done.19.refs_2_), channel_id=1, source_target_pairs={{0,1},{1,0},{2,3},{3,2},{4,5},{5,4},{6,7},{7,6},{8,9},{9,8},{10,11... | collective-permute-start | bytes 442376 | tf_op jit(solution)/shard_map/ppermute | solution.py:29
  106.7 8.7 %collective-permute-start.24 = (bf16[32,2304]{1,0:T(8,128)(2,1)S(1)}, bf16[32,2304]{1,0:T(8,128)(2,1)S(1)}, u32[]{:S(2)}, u32[]{:S(2)}) collective-permute-start(bf16[32,2304]{1,0:T(8,128)(2,1)S(1)} %collective-permute-done.21.refs_1_), channel_id=1, source_target_pairs={{0,1},{1,0},{2,3},{3,2},{4,5},{5,4},{6,7},{7,6},{8,9},{9,8},{10,11... | collective-permute-start | bytes 442376 | tf_op jit(solution)/shard_map/ppermute | solution.py:29
  112.6 5.4 %collective-permute-start.26 = (bf16[32,2304]{1,0:T(8,128)(2,1)S(1)}, bf16[32,2304]{1,0:T(8,128)(2,1)S(1)}, u32[]{:S(2)}, u32[]{:S(2)}) collective-permute-start(bf16[32,2304]{1,0:T(8,128)(2,1)S(1)} %collective-permute-done.22.refs_3_), channel_id=1, source_target_pairs={{0,1},{1,0},{2,3},{3,2},{4,5},{5,4},{6,7},{7,6},{8,9},{9,8},{10,11... | collective-permute-start | bytes 442376 | tf_op jit(solution)/shard_map/ppermute | solution.py:29
  113.5 19.2 %collective-permute-start.27 = (bf16[32,2304]{1,0:T(8,128)(2,1)S(1)}, bf16[32,2304]{1,0:T(8,128)(2,1)S(1)}, u32[]{:S(2)}, u32[]{:S(2)}) collective-permute-start(bf16[32,2304]{1,0:T(8,128)(2,1)S(1)} %get-tuple-element.109.refs_0_), channel_id=1, source_target_pairs={{0,2},{1,3},{2,0},{3,1},{4,6},{5,7},{6,4},{7,5},{8,10},{9,11},{10,... | collective-permute-start | bytes 442376 | tf_op jit(solution)/shard_map/ppermute | solution.py:29
  113.7 20.1 %collective-permute-start.28 = (bf16[32,2304]{1,0:T(8,128)(2,1)S(1)}, bf16[32,2304]{1,0:T(8,128)(2,1)S(1)}, u32[]{:S(2)}, u32[]{:S(2)}) collective-permute-start(bf16[32,2304]{1,0:T(8,128)(2,1)S(1)} %get-tuple-element.109.refs_0_), channel_id=1, source_target_pairs={{0,4},{1,5},{2,6},{3,7},{4,0},{5,1},{6,2},{7,3},{8,12},{9,13},{10,... | collective-permute-start | bytes 442376 | tf_op jit(solution)/shard_map/ppermute | solution.py:29
  115.4 19.1 %collective-permute-start.29 = (bf16[32,2304]{1,0:T(8,128)(2,1)S(1)}, bf16[32,2304]{1,0:T(8,128)(2,1)S(1)}, u32[]{:S(2)}, u32[]{:S(2)}) collective-permute-start(bf16[32,2304]{1,0:T(8,128)(2,1)S(1)} %get-tuple-element.109.refs_0_), channel_id=1, source_target_pairs={{0,6},{1,7},{2,4},{3,5},{4,2},{5,3},{6,0},{7,1},{8,14},{9,15},{10,... | collective-permute-start | bytes 442376 | tf_op jit(solution)/shard_map/ppermute | solution.py:29
  118.0 16.5 %collective-permute-start.30 = (bf16[32,2304]{1,0:T(8,128)(2,1)S(1)}, bf16[32,2304]{1,0:T(8,128)(2,1)S(1)}, u32[]{:S(2)}, u32[]{:S(2)}) collective-permute-start(bf16[32,2304]{1,0:T(8,128)(2,1)S(1)} %get-tuple-element.109.refs_0_), channel_id=1, source_target_pairs={{0,1},{1,0},{2,3},{3,2},{4,5},{5,4},{6,7},{7,6},{8,9},{9,8},{10,11... | collective-permute-start | bytes 442376 | tf_op jit(solution)/shard_map/ppermute | solution.py:29
  131.1 9.2 %collective-permute-start.35 = (bf16[2,64,1024]{2,1,0:T(8,128)(2,1)S(1)}, bf16[2,64,1024]{2,1,0:T(8,128)(2,1)S(1)}, u32[]{:S(2)}, u32[]{:S(2)}) collective-permute-start(bf16[2,64,1024]{2,1,0:T(8,128)(2,1)S(1)} %get-tuple-element.108), channel_id=1, source_target_pairs={{0,16},{8,24},{16,0},{24,8},{1,17},{9,25},{17,1},{25,9},{2,18},{10... | collective-permute-start | bytes 786440 | tf_op jit(solution)/shard_map/ppermute | solution.py:29
  132.7 8.9 %collective-permute-start.34 = (bf16[2,64,1024]{2,1,0:T(8,128)(2,1)S(1)}, bf16[2,64,1024]{2,1,0:T(8,128)(2,1)S(1)}, u32[]{:S(2)}, u32[]{:S(2)}) collective-permute-start(bf16[2,64,1024]{2,1,0:T(8,128)(2,1)S(1)} %get-tuple-element.107), channel_id=1, source_target_pairs={{0,8},{8,0},{16,24},{24,16},{1,9},{9,1},{17,25},{25,17},{2,10},{10... | collective-permute-start | bytes 786440 | tf_op jit(solution)/shard_map/ppermute | solution.py:29
  133.8 25.2 %collective-permute-start.40 = (bf16[2,64,1024]{2,1,0:T(8,128)(2,1)S(1)}, bf16[2,64,1024]{2,1,0:T(8,128)(2,1)S(1)}, u32[]{:S(2)}, u32[]{:S(2)}) collective-permute-start(bf16[2,64,1024]{2,1,0:T(8,128)(2,1)S(1)} %get-tuple-element.132), channel_id=1, source_target_pairs={{0,16},{8,24},{16,0},{24,8},{1,17},{9,25},{17,1},{25,9},{2,18},{10... | collective-permute-start | bytes 786440 | tf_op jit(solution)/shard_map/ppermute | solution.py:29
  134.5 6.5 %collective-permute-start.31 = (bf16[32,2304]{1,0:T(8,128)(2,1)S(1)}, bf16[32,2304]{1,0:T(8,128)(2,1)S(1)}, u32[]{:S(2)}, u32[]{:S(2)}) collective-permute-start(bf16[32,2304]{1,0:T(8,128)(2,1)S(1)} %collective-permute-done.27.refs_1_), channel_id=1, source_target_pairs={{0,1},{1,0},{2,3},{3,2},{4,5},{5,4},{6,7},{7,6},{8,9},{9,8},{10,11... | collective-permute-start | bytes 442376 | tf_op jit(solution)/shard_map/ppermute | solution.py:29
  134.5 7.1 %collective-permute-start.32 = (bf16[32,2304]{1,0:T(8,128)(2,1)S(1)}, bf16[32,2304]{1,0:T(8,128)(2,1)S(1)}, u32[]{:S(2)}, u32[]{:S(2)}) collective-permute-start(bf16[32,2304]{1,0:T(8,128)(2,1)S(1)} %collective-permute-done.28.refs_2_), channel_id=1, source_target_pairs={{0,1},{1,0},{2,3},{3,2},{4,5},{5,4},{6,7},{7,6},{8,9},{9,8},{10,11... | collective-permute-start | bytes 442376 | tf_op jit(solution)/shard_map/ppermute | solution.py:29
  140.2 1.4 collective-permute-start.33
  141.0 19.6 %collective-permute-start.39 = (bf16[2,64,1024]{2,1,0:T(8,128)(2,1)S(1)}, bf16[2,64,1024]{2,1,0:T(8,128)(2,1)S(1)}, u32[]{:S(2)}, u32[]{:S(2)}) collective-permute-start(bf16[2,64,1024]{2,1,0:T(8,128)(2,1)S(1)} %get-tuple-element.130), channel_id=1, source_target_pairs={{0,8},{8,0},{16,24},{24,16},{1,9},{9,1},{17,25},{25,17},{2,10},{10... | collective-permute-start | bytes 786440 | tf_op jit(solution)/shard_map/ppermute | solution.py:29
  141.6 36.7 %collective-permute-start.42 = (bf16[2,64,1024]{2,1,0:T(8,128)(2,1)}, bf16[2,64,1024]{2,1,0:T(8,128)(2,1)S(1)}, u32[]{:S(2)}, u32[]{:S(2)}) collective-permute-start(bf16[2,64,1024]{2,1,0:T(8,128)(2,1)} %add_convert_fusion.2), channel_id=1, source_target_pairs={{0,8},{8,0},{16,24},{24,16},{1,9},{9,1},{17,25},{25,17},{2,10},{10... | collective-permute-start | bytes 786440 | tf_op jit(solution)/shard_map/ppermute | solution.py:29
  143.9 35.1 %collective-permute-start.41 = (bf16[2,64,1024]{2,1,0:T(8,128)(2,1)}, bf16[2,64,1024]{2,1,0:T(8,128)(2,1)S(1)}, u32[]{:S(2)}, u32[]{:S(2)}) collective-permute-start(bf16[2,64,1024]{2,1,0:T(8,128)(2,1)} %add_convert_fusion.3), channel_id=1, source_target_pairs={{0,16},{8,24},{16,0},{24,8},{1,17},{9,25},{17,1},{25,9},{2,18},{10... | collective-permute-start | bytes 786440 | tf_op jit(solution)/shard_map/ppermute | solution.py:29
  158.4 17.7 %collective-permute-start.45 = (bf16[2,64,1024]{2,1,0:T(8,128)(2,1)S(1)}, bf16[2,64,1024]{2,1,0:T(8,128)(2,1)}, u32[]{:S(2)}, u32[]{:S(2)}) collective-permute-start(bf16[2,64,1024]{2,1,0:T(8,128)(2,1)S(1)} %get-tuple-element.137), channel_id=1, source_target_pairs={{0,16},{8,24},{16,0},{24,8},{1,17},{9,25},{17,1},{25,9},{2,18},{10... | collective-permute-start | bytes 786440 | tf_op jit(solution)/shard_map/ppermute | solution.py:29
  159.0 13.0 %collective-permute-start.37 = (bf16[2,64,1024]{2,1,0:T(8,128)(2,1)S(1)}, bf16[2,64,1024]{2,1,0:T(8,128)(2,1)S(1)}, u32[]{:S(2)}, u32[]{:S(2)}) collective-permute-start(bf16[2,64,1024]{2,1,0:T(8,128)(2,1)S(1)} %get-tuple-element.127), channel_id=1, source_target_pairs={{0,16},{8,24},{16,0},{24,8},{1,17},{9,25},{17,1},{25,9},{2,18},{10... | collective-permute-start | bytes 786440 | tf_op jit(solution)/shard_map/ppermute | solution.py:29
  160.6 12.6 %collective-permute-start.36 = (bf16[2,64,1024]{2,1,0:T(8,128)(2,1)S(1)}, bf16[2,64,1024]{2,1,0:T(8,128)(2,1)S(1)}, u32[]{:S(2)}, u32[]{:S(2)}) collective-permute-start(bf16[2,64,1024]{2,1,0:T(8,128)(2,1)S(1)} %get-tuple-element.123), channel_id=1, source_target_pairs={{0,8},{8,0},{16,24},{24,16},{1,9},{9,1},{17,25},{25,17},{2,10},{10... | collective-permute-start | bytes 786440 | tf_op jit(solution)/shard_map/ppermute | solution.py:29
  172.0 13.9 %collective-permute-start.44 = (bf16[2,64,1024]{2,1,0:T(8,128)(2,1)S(1)}, bf16[2,64,1024]{2,1,0:T(8,128)(2,1)}, u32[]{:S(2)}, u32[]{:S(2)}) collective-permute-start(bf16[2,64,1024]{2,1,0:T(8,128)(2,1)S(1)} %get-tuple-element.135), channel_id=1, source_target_pairs={{0,8},{8,0},{16,24},{24,16},{1,9},{9,1},{17,25},{25,17},{2,10},{10... | collective-permute-start | bytes 786440 | tf_op jit(solution)/shard_map/ppermute | solution.py:29
  173.2 17.0 %collective-permute-start.47 = (bf16[2,64,1024]{2,1,0:T(8,128)(2,1)}, bf16[2,64,1024]{2,1,0:T(8,128)(2,1)S(1)}, u32[]{:S(2)}, u32[]{:S(2)}) collective-permute-start(bf16[2,64,1024]{2,1,0:T(8,128)(2,1)} %add_convert_fusion), channel_id=1, source_target_pairs={{0,8},{8,0},{16,24},{24,16},{1,9},{9,1},{17,25},{25,17},{2,10},{10... | collective-permute-start | bytes 786440 | tf_op jit(solution)/shard_map/ppermute | solution.py:29
  176.8 7.9 %collective-permute-start.38 = (f32[8,128]{1,0:T(8,128)S(1)}, f32[8,128]{1,0:T(8,128)S(1)}, u32[]{:S(2)}, u32[]{:S(2)}) collective-permute-start(f32[8,128]{1,0:T(8,128)S(1)} %broadcast_in_dim.11), channel_id=1, source_target_pairs={{0,8},{8,0},{16,24},{24,16},{1,9},{9,1},{17,25},{25,17},{2,10},{10... | collective-permute-start | bytes 12296 | tf_op jit(solution)/shard_map/ppermute | solution.py:29
  178.3 11.9 %collective-permute-start.46 = (bf16[2,64,1024]{2,1,0:T(8,128)(2,1)}, bf16[2,64,1024]{2,1,0:T(8,128)(2,1)S(1)}, u32[]{:S(2)}, u32[]{:S(2)}) collective-permute-start(bf16[2,64,1024]{2,1,0:T(8,128)(2,1)} %add_convert_fusion.1), channel_id=1, source_target_pairs={{0,16},{8,24},{16,0},{24,8},{1,17},{9,25},{17,1},{25,9},{2,18},{10... | collective-permute-start | bytes 786440 | tf_op jit(solution)/shard_map/ppermute | solution.py:29
  185.3 3.7 %collective-permute-start.43 = (f32[8,128]{1,0:T(8,128)S(1)}, f32[8,128]{1,0:T(8,128)S(1)}, u32[]{:S(2)}, u32[]{:S(2)}) collective-permute-start(f32[8,128]{1,0:T(8,128)S(1)} %broadcast_add_fusion), channel_id=1, source_target_pairs={{0,16},{8,24},{16,0},{24,8},{1,17},{9,25},{17,1},{25,9},{2,18},{10... | collective-permute-start | bytes 12296 | tf_op jit(solution)/shard_map/ppermute | solution.py:29
  (19 other events, 224.8 us)

commit v8 on v6

--- a/solution.py
+++ b/solution.py
@@ -4,7 +4,6 @@
 import jax.numpy as jnp
 from jax import lax
 from jax.experimental import pallas as pl
-from jax.experimental.layout import Layout, with_layout_constraint
 from jax.experimental.pallas import tpu as pltpu
 from jax.sharding import PartitionSpec as P
 
@@ -67,7 +66,8 @@
 
 
 def streamed(count, slots, copies_of, body):
-    for i in range(min(slots - 1, count)):
+    early = min(1, slots - 1, count)
+    for i in range(early):
         for copy in copies_of(i, i):
             copy.start()
 
@@ -75,14 +75,26 @@
     def _(i):
         ahead = i + slots - 1
 
-        @pl.when(ahead < count)
+        @pl.when(i == 0)
+        def _():
+            for copy in copies_of(0, 0):
+                copy.wait()
+            for later in range(early, min(slots, count)):
+                for copy in copies_of(later, later):
+                    copy.start()
+
+        @pl.when((i > 0) & (ahead < count))
         def _():
             for copy in copies_of(ahead, lax.rem(ahead, slots)):
                 copy.start()
 
         slot = lax.rem(i, slots)
-        for copy in copies_of(i, slot):
-            copy.wait()
+
+        @pl.when(i > 0)
+        def _():
+            for copy in copies_of(i, slot):
+                copy.wait()
+
         body(i, slot)
 
 
@@ -99,18 +111,22 @@
     )(*args)
 
 
-def encode_kernel(plan, source, resid_ref, w_ref, b_ref, out_ref, x_buf, w_buf, b_buf, x_sem, w_sem):
+def encode_kernel(plan, lo, hi, resid_ref, w_ref, b_ref, *refs):
+    outs, (x_buf, w_buf, b_buf, x_sem, w_sem) = refs[:hi - lo], refs[hi - lo:]
     tile = w_buf.shape[2]
+    steps = plan.width // tile
     near = [
-        pltpu.make_async_copy(resid_ref.at[source], x_buf, x_sem.at[0]),
+        pltpu.make_async_copy(resid_ref.at[pl.ds(lo, hi - lo)], x_buf, x_sem.at[0]),
         pltpu.make_async_copy(b_ref, b_buf, x_sem.at[1]),
     ]
     for copy in near:
         copy.start()
 
     def copies_of(i, slot):
-        cols = pl.ds(pl.multiple_of(i * tile, tile), tile)
-        return [pltpu.make_async_copy(w_ref.at[source, :, cols], w_buf.at[slot], w_sem.at[slot])]
+        cols = pl.ds(pl.multiple_of(lax.rem(i, steps) * tile, tile), tile)
+        return [pltpu.make_async_copy(
+            w_ref.at[lo + lax.div(i, steps), :, cols], w_buf.at[slot], w_sem.at[slot]
+        )]
 
     def step(i, slot):
         @pl.when(i == 0)
@@ -118,23 +134,28 @@
             for copy in near:
                 copy.wait()
 
-        cols = pl.ds(pl.multiple_of(i * tile, tile), tile)
-        product = jnp.dot(x_buf[...], w_buf[slot], preferred_element_type=F32)
-        value = jnp.maximum(product + b_buf[source:source + 1, cols], 0.0)
-        out_ref[:, cols] = value.astype(BF16)
-
-    streamed(plan.width // tile, w_buf.shape[0], copies_of, step)
-
-
-def encode(plan, source, resid, w_enc, b_enc):
+        source = lax.div(i, steps)
+        cols = pl.ds(pl.multiple_of(lax.rem(i, steps) * tile, tile), tile)
+        product = jnp.dot(x_buf[source], w_buf[slot], preferred_element_type=F32)
+        bias = b_buf[pl.ds(lo + source, 1), cols]
+        value = jnp.maximum(product + bias, 0.0).astype(BF16)
+        for s in range(hi - lo):
+            @pl.when(source == s)
+            def _():
+                outs[s][:, cols] = value
+
+    streamed((hi - lo) * steps, w_buf.shape[0], copies_of, step)
+
+
+def encode(plan, lo, hi, resid, w_enc, b_enc):
     tile = pick_tile(plan.width, 256)
     return call(
-        partial(encode_kernel, plan, source),
+        partial(encode_kernel, plan, lo, hi),
         "encode",
         [FAR, FAR, FAR],
-        jax.ShapeDtypeStruct((plan.rows, plan.width), BF16),
+        [jax.ShapeDtypeStruct((plan.rows, plan.width), BF16)] * (hi - lo),
         [
-            pltpu.VMEM((plan.rows, plan.model), BF16),
+            pltpu.VMEM((hi - lo, plan.rows, plan.model), BF16),
             pltpu.VMEM((WEIGHT_SLOTS + 1, plan.model, tile), BF16),
             pltpu.VMEM((plan.sources, plan.width), F32),
             pltpu.SemaphoreType.DMA((2,)),
@@ -145,13 +166,37 @@
     )
 
 
+def arrange_kernel(plan, *refs):
+    parts, out_ref, stage = refs[:plan.sources], refs[-2], refs[-1]
+    count = stage.shape[0]
+
+    @pl.loop(0, plan.rows // count)
+    def _(i):
+        rows = pl.ds(pl.multiple_of(i * count, count), count)
+        for s in range(plan.sources):
+            stage[:, s, :] = parts[s][rows, :].astype(F32)
+        out_ref[rows] = stage[...].astype(BF16)
+
+
+def arrange(plan, encoded):
+    return call(
+        partial(arrange_kernel, plan),
+        "arrange",
+        [NEAR] * plan.sources,
+        jax.ShapeDtypeStruct((plan.rows, plan.sources, plan.width), BF16),
+        [pltpu.VMEM((ROW_TILE, plan.sources, plan.width), F32)],
+        encoded,
+    )
+
+
 def decode_kernel(plan, index_ref, *refs):
     n_in = plan.groups * plan.sources
-    pieces, w_ref, outs = refs[:n_in], refs[n_in], refs[n_in + 1:-4]
-    x_buf, w_buf, x_sem, w_sem = refs[-4:]
+    pieces, w_ref, outs = refs[:n_in], refs[n_in], refs[n_in + 1:-7]
+    x_buf, w_buf, send_buf, keep_buf, x_sem, w_sem, out_sem = refs[-7:]
     half = plan.tokens // 2
     core = index_ref[0]
     tile = w_buf.shape[2]
+    count = plan.model // tile
 
     placing = []
     for j in range(plan.groups):
@@ -172,15 +217,29 @@
     for copy in placing:
         copy.start()
 
+    def columns(i):
+        return pl.ds(pl.multiple_of(i * tile, tile), tile)
+
     def copies_of(i, slot):
-        cols = pl.ds(pl.multiple_of(i * tile, tile), tile)
         return [
             pltpu.make_async_copy(
-                w_ref.at[s, 0, :, cols],
+                w_ref.at[s, 0, :, columns(i)],
                 w_buf.at[slot, pl.ds(s * plan.width, plan.width)],
                 w_sem.at[slot, s],
             )
             for s in range(plan.sources)
+        ]
+
+    def leaving(i):
+        slot = lax.rem(i, 2)
+        return [
+            pltpu.make_async_copy(
+                buf.at[slot, c],
+                outs[n * plan.chunks + c].at[:, columns(i)],
+                out_sem.at[slot, n * plan.chunks + c],
+            )
+            for n, buf in enumerate((send_buf, keep_buf))
+            for c in range(plan.chunks)
         ]
 
     def step(i, slot):
@@ -195,21 +254,32 @@
                         (plan.tokens, plan.width), BF16
                     )
 
-        cols = pl.ds(pl.multiple_of(i * tile, tile), tile)
+        @pl.when(i >= 2)
+        def _():
+            for copy in leaving(i - 2):
+                copy.wait()
+
         product = jnp.dot(x_buf[...], w_buf[slot], preferred_element_type=F32)
+        out_slot = lax.rem(i, 2)
         for c in range(plan.chunks):
             for d in range(plan.depth):
                 first = d * plan.rows_feat + c * plan.piece
                 to = slice(d * plan.piece, (d + 1) * plan.piece)
-                outs[c][to, cols] = product[first:first + plan.piece].astype(BF16)
-                outs[plan.chunks + c][to, cols] = product[half + first:half + first + plan.piece]
-
-    streamed(plan.model // tile, w_buf.shape[0], copies_of, step)
+                send_buf[out_slot, c, to, :] = product[first:first + plan.piece].astype(BF16)
+                keep_buf[out_slot, c, to, :] = product[half + first:half + first + plan.piece]
+        for copy in leaving(i):
+            copy.start()
+
+    streamed(count, w_buf.shape[0], copies_of, step)
+    for i in range(max(count - 2, 0), count):
+        for copy in leaving(i):
+            copy.wait()
 
 
 def decode(plan, index, pieces, w_dec):
     tile = pick_tile(plan.model, 256)
     shape = (plan.depth * plan.piece, plan.model)
+    near = (2, plan.chunks, plan.depth * plan.piece, tile)
     outs = call(
         partial(decode_kernel, plan),
         "decode",
@@ -219,10 +289,15 @@
         [
             pltpu.VMEM((plan.tokens, plan.sources * plan.width), BF16),
             pltpu.VMEM((WEIGHT_SLOTS, plan.sources * plan.width, tile), BF16),
+            pltpu.VMEM(near, BF16),
+            pltpu.VMEM(near, F32),
             pltpu.SemaphoreType.DMA((len(pieces) * plan.per_group,)),
             pltpu.SemaphoreType.DMA((WEIGHT_SLOTS, plan.sources)),
+            pltpu.SemaphoreType.DMA((2, 2 * plan.chunks)),
         ],
         (index, *pieces, w_dec),
+        vmem=MOST_VMEM_BYTES,
+        out_specs=[ANYWHERE] * (2 * plan.chunks),
     )
     return outs[:plan.chunks], outs[plan.chunks:]
 
@@ -321,11 +396,13 @@
 
 def finish_kernel(plan, chunk, with_previous, *refs):
     lanes = len(plan.lanes)
-    kept, got = refs[:lanes], refs[lanes:2 * lanes]
     out_ref, stage, sem = refs[-3:]
     for lane, (lo, hi) in enumerate(plan.lane_sources):
         for s in range(lo, hi):
-            stage[:, s, :] = kept[lane][s - lo] + got[lane][s - lo].astype(F32)
+            total = refs[lane][s - lo]
+            for got in refs[lanes + lane:lanes * (1 + lanes):lanes]:
+                total = total + got[s - lo].astype(F32)
+            stage[:, s, :] = total
     copies = [
         pltpu.make_async_copy(
             stage.at[pl.ds(b * plan.piece, plan.piece)],
@@ -343,12 +420,12 @@
 def finish(plan, chunk, kept, got, previous):
     options = {}
     if previous is not None:
-        options["input_output_aliases"] = {2 * len(kept): 0}
+        options["input_output_aliases"] = {len(kept) + len(got): 0}
     previous = [] if previous is None else [previous]
     return call(
         partial(finish_kernel, plan, chunk, bool(previous)),
         "finish",
-        [NEAR] * (2 * len(kept)) + [FAR] * len(previous),
+        [NEAR] * (len(kept) + len(got)) + [FAR] * len(previous),
         jax.ShapeDtypeStruct((plan.rows, plan.sources, plan.width), F32),
         [
             pltpu.VMEM((plan.block, plan.sources, plan.width), F32),
@@ -381,24 +458,31 @@
             places.append(place * 2 + (core ^ other))
     index = jnp.concatenate([core[None], feeds, jnp.stack(offsets), jnp.stack(places)])
 
-    encoded = [encode(plan, s, resid, w_enc, b_enc) for s in range(plan.sources)]
-    active = with_layout_constraint(jnp.stack(encoded, axis=1), Layout((0, 1, 2)))
-
-    pieces, arrived = [], []
-    for s, mine in enumerate(encoded):
-        bits = plan.lanes[s % len(plan.lanes)]
-        mine, = after([mine], arrived[s - 2] if s >= 2 else [])
-        held = {0: mine}
-        for bit in bits:
-            held.update(
-                {j | bit: swap(x, "grp", groups, bit) for j, x in list(held.items())}
-            )
-        pieces += [held[j] for j in range(groups)]
-        arrived.append([held[bit] for bit in bits])
+    encoded, batches = [], []
+    for lo, hi in plan.lane_sources:
+        batches.append(range(lo, hi))
+        encoded += encode(plan, lo, hi, resid, w_enc, b_enc)
+    active = arrange(plan, encoded)
+
+    pieces, arrived, forwarded = [], [], []
+    for batch in batches:
+        before, arrived, before_forward, forwarded = arrived, [], forwarded, []
+        for s in batch:
+            bits = plan.lanes[s % len(plan.lanes)]
+            mine, = after([encoded[s]], before)
+            held = {0: mine}
+            for bit in bits:
+                old = dict(held)
+                for j, x in old.items():
+                    if j:
+                        x, = after([x], before_forward)
+                    held[j | bit] = swap(x, "grp", groups, bit)
+            pieces += [held[j] for j in range(groups)]
+            arrived += [held[bit] for bit in bits]
+            forwarded += [held[j] for j in range(groups) if j & (j - 1)]
 
     sends, keeps = decode(plan, index, after(pieces, [active]), w_dec)
-    partial_rows = []
-    earlier = []
+    recon_parts, errors = [], []
     for c in range(chunks):
         other = swap(sends[c], "feat", feats, 1)
         held = {
@@ -408,61 +492,61 @@
         }
         for bit in plan.level_bits:
             away = {d: held.pop(d).astype(BF16) for d in sorted(held, reverse=True) if d & bit}
-            if bit == plan.level_bits[0]:
-                away = dict(zip(away, after(away.values(), earlier)))
-            got = {d: swap(x, "feat", feats, 2 * bit) for d, x in away.items()}
-            if bit == plan.level_bits[0]:
-                earlier = list(got.values())[:1]
-            for d, x in got.items():
-                held[d ^ bit] = held[d ^ bit] + x.astype(F32)
-        partial_rows.append(held[0])
-
-    recon_parts, errors, first_errors = [], [], []
-    for c in range(chunks):
-        recon_rows, = after([partial_rows[c]], first_errors[-1:])
+            for d, x in away.items():
+                held[d ^ bit] = held[d ^ bit] + swap(x, "feat", feats, 2 * bit).astype(F32)
+        recon_rows, = after([held[0]], [e[0] for e in errors])
+
         first = feat * plan.rows_feat + c * plan.piece
         own_targets = lax.dynamic_slice_in_dim(targets[0], first, plan.piece, 0)
         difference = recon_rows - own_targets.astype(F32)
         recon_parts.append(recon_rows.astype(BF16))
-        held = {0: difference.astype(BF16)}
-        for bit in reversed(plan.level_bits):
-            held.update(
-                {d | bit: swap(x, "feat", feats, 2 * bit) for d, x in list(held.items())}
-            )
-        first_errors.append(held[plan.level_bits[-1]])
+        error = difference.astype(BF16)
+        held = {0: error}
+        if c:
+            for d in range(plan.depth - 1, 0, -1):
+                held[d] = swap(error, "feat", feats, 2 * d)
+        else:
+            for bit in reversed(plan.level_bits):
+                held.update(
+                    {d | bit: swap(x, "feat", feats, 2 * bit) for d, x in list(held.items())}
+                )
         every = [held[d] for d in range(plan.depth)]
         errors.append(every + [swap(e, "feat", feats, 1) for e in every])
 
     squares = jnp.zeros((8, 128), F32)
     feat_grad = None
-    earlier, first_got = [], []
+    second, got_all = [], []
     for c in range(chunks):
-        ready = after(errors[c], [e[0] for e in errors[c + 1:c + 2]] + first_got)
+        ready = after(errors[c], [e[0] for e in errors[c + 1:c + 2]] + second)
         lanes, total = gradient(plan, index, ready, w_dec)
         squares = squares + total
-        kept_all, got_all, second, first_got = [], [], [], []
+        second = []
+        earlier = got_all + [x for every in errors[c + 1:c + 2] for x in every[1:plan.depth]]
+        lanes = [(after(away, earlier), kept) for away, kept in lanes]
+        kept_all = []
         for bits, (away, kept) in zip(plan.lanes, lanes):
-            away = after(away, earlier)
+            kept = [[x] for x in kept]
             for step, bit in enumerate(bits):
-                got = [swap(x, "grp", groups, bit) for x in away]
-                cut = len(got) // 2
+                cut = len(away) // 2
+                got = [swap(x, "grp", groups, bit) for x in away[:cut]]
+                rest = after(away[cut:], got[:1])
+                got += [swap(x, "grp", groups, bit) for x in rest]
+                for own, x in zip(kept, got):
+                    own.append(x)
                 if cut:
-                    sums = [x + y.astype(F32) for x, y in zip(kept, got)]
-                    away, kept = [x.astype(BF16) for x in sums[:cut]], sums[cut:]
-                    if not step:
-                        first_got.append(got[0])
-                        second += away
-                        away = after(away, [] if feat_grad is None else [feat_grad])
+                    away = [sum(x.astype(F32) for x in own).astype(BF16) for own in kept[:cut]]
+                    kept = kept[cut:]
+                    second += away if not step else []
             kept_all.append(kept[0])
-            got_all.append(got[0])
-        feat_grad = finish(plan, c, kept_all, got_all, feat_grad)
-        earlier = second
+        got_all = [own[i] for i in range(1, len(kept_all[0])) for own in kept_all]
+        previous = feat_grad
+        feat_grad = finish(plan, c, [own[0] for own in kept_all], got_all, previous)
 
     loss = jnp.full((8, 128), jnp.sum(squares), F32)
     for i, bit in enumerate(1 << i for i in range(groups.bit_length() - 1)):
         loss = loss + swap(loss, "grp", groups, bit)
         if not i:
-            loss, = after([loss], first_got)
+            loss, = after([loss], second + ([] if previous is None else [previous]))
     entries = targets.shape[0] * groups * plan.tokens * plan.model
     recon_loss = loss[0, 0] / entries
     recon = jnp.concatenate(recon_parts, axis=0)[None]

time: 186 us -> 179 us (0.962)
  waiting for transfers between devices: 41.6 us -> 59.5 us
  local copies, waits for them, and re-layouts: 21.8 us -> 4.35 us
  other arithmetic: 12.5 us -> 6.52 us
  starting transfers between devices: 46.9 us -> 44.2 us
    ppermute x48, waiting for transfers between devices: 41.6 us -> 59.5 us  [swap(): return lax.ppermute(x, axis, [(i, i ^ offset) for i in range(size)])]
    unnamed x60 -> x36, local copies, waits for them, and re-layouts: 14.8 us -> 2.58 us
    another operation x4 -> x0, local copies, waits for them, and re-layouts: 5.8 us -> none  [per_device(): jnp.stack(encoded, axis=1)]
    another operation x1 -> x0, other arithmetic: 4.96 us -> none  [per_device(): jnp.stack(encoded, axis=1)]
    ppermute x48, starting transfers between devices: 46.9 us -> 44.2 us  [swap(): return lax.ppermute(x, axis, [(i, i ^ offset) for i in range(size)])]
    pallas_call x9 -> x8, Pallas kernels: 59.4 us -> 61.1 us  [call(): pl.pallas_call(kernel, in_specs=in_specs, out_shape=out_shape, scratch_sh...]
  transfers between devices with their start and end apart: 48 -> 48, of which waited for: 15 -> 17; matrix products, arithmetic and copies ran while one was open for 11% -> 4% of each run, Pallas kernels for 21% -> 20%
where the time goes in v8:
time: 179 us
  Pallas kernels  61.1 us (34%)
  waiting for transfers between devices  59.5 us (33%)
  starting transfers between devices  44.2 us (25%)
  other arithmetic  6.52 us (4%)
  local copies, waits for them, and re-layouts  4.35 us (2%)
  between operations  2.85 us (2%)
    pallas_call x8, Pallas kernels, call(): pl.pallas_call(kernel, in_specs=in_specs, out_shape=out_shape, scratch_sh...  61.1 us
    ppermute x48, waiting for transfers between devices, swap(): return lax.ppermute(x, axis, [(i, i ^ offset) for i in range(size)])  59.5 us
    ppermute x48, starting transfers between devices, swap(): return lax.ppermute(x, axis, [(i, i ^ offset) for i in range(size)])  44.2 us
  transfers between devices with their start and end apart: 48, of which 17 were waited for; matrix products, arithmetic and copies ran while one was open for 4% of the time, Pallas kernels for 20%

profile of v8, /device:TPU:0, one launch (start us, length us, event | category | flops | bytes accessed | tf_op | source)
XLA Modules:
  0.0 178.5 jit_solution(8744084005321772307)
XLA Ops:
  0.6 6.5 %encode.2 = (bf16[128,1024]{1,0:T(8,128)(2,1)}, bf16[128,1024]{1,0:T(8,128)(2,1)}) custom-call(bf16[4,128,2304]{2,1,0:T(8,128)(2,1)} %resid_ref.3, bf16[4,2304,1024]{2,1,0:T(8,128)(2,1)} %w_ref.3, f32[4,1024]{1,0:T(4,128)} %b_ref.3), custom_call_target="tpu_custom_call" | custom-call | flops 1048576 | bytes 1024 | tf_op jit(solution)/shard_map/encode/pallas_call | solution.py:102
  7.1 3.0 %collective-permute-start = (bf16[128,1024]{1,0:T(8,128)(2,1)}, bf16[128,1024]{1,0:T(8,128)(2,1)S(1)}, u32[]{:S(2)}, u32[]{:S(2)}) collective-permute-start(bf16[128,1024]{1,0:T(8,128)(2,1)} %get-tuple-element.88.refs_0_), channel_id=1, source_target_pairs={{0,8},{8,0},{16,24},{24,16},{1,9},{9,1},{17,25},{25,17},{2,10},{10... | collective-permute-start | bytes 786440 | tf_op jit(solution)/shard_map/ppermute | solution.py:29
  10.1 1.5 collective-permute-start.4
  12.3 6.5 %encode.3 = (bf16[128,1024]{1,0:T(8,128)(2,1)}, bf16[128,1024]{1,0:T(8,128)(2,1)}) custom-call(bf16[4,128,2304]{2,1,0:T(8,128)(2,1)} %resid_ref.3, bf16[4,2304,1024]{2,1,0:T(8,128)(2,1)} %w_ref.3, f32[4,1024]{1,0:T(4,128)} %b_ref.3), custom_call_target="tpu_custom_call" | custom-call | flops 1048576 | bytes 1024 | tf_op jit(solution)/shard_map/encode/pallas_call | solution.py:102
  19.6 4.2 %collective-permute-done.1.refs_2_ = bf16[128,1024]{1,0:T(8,128)(2,1)S(1)} collective-permute-done((bf16[128,1024]{1,0:T(8,128)(2,1)}, bf16[128,1024]{1,0:T(8,128)(2,1)S(1)}, u32[]{:S(2)}, u32[]{:S(2)}) %collective-permute-start.1) | collective-permute-done | bytes 262176 | tf_op jit(solution)/shard_map/ppermute | solution.py:29
  23.7 1.6 collective-permute-start.10
  26.2 1.6 collective-permute-start.6
  27.9 1.5 collective-permute-start.7
  29.4 3.9 %collective-permute-done.10.refs_14_ = bf16[128,1024]{1,0:T(8,128)(2,1)S(1)} collective-permute-done((bf16[128,1024]{1,0:T(8,128)(2,1)}, bf16[128,1024]{1,0:T(8,128)(2,1)S(1)}, u32[]{:S(2)}, u32[]{:S(2)}) %collective-permute-start.10) | collective-permute-done | bytes 262176 | tf_op jit(solution)/shard_map/ppermute | solution.py:29
  33.6 5.2 %collective-permute-done.2.refs_3_ = bf16[128,1024]{1,0:T(8,128)(2,1)S(1)} collective-permute-done((bf16[128,1024]{1,0:T(8,128)(2,1)S(1)}, bf16[128,1024]{1,0:T(8,128)(2,1)S(1)}, u32[]{:S(2)}, u32[]{:S(2)}) %collective-permute-start.2) | collective-permute-done | bytes 262176 | tf_op jit(solution)/shard_map/ppermute | solution.py:29
  39.3 1.4 collective-permute-done.6.refs_9_
  40.7 1.5 collective-permute-start.8
  42.8 0.9 copy-done.2
  43.8 0.9 copy-done.3
  44.7 1.7 arrange.1
  46.5 2.5 %collective-permute-done.11.refs_15_ = bf16[128,1024]{1,0:T(8,128)(2,1)S(1)} collective-permute-done((bf16[128,1024]{1,0:T(8,128)(2,1)S(1)}, bf16[128,1024]{1,0:T(8,128)(2,1)S(1)}, u32[]{:S(2)}, u32[]{:S(2)}) %collective-permute-start.11) | collective-permute-done | bytes 262176 | tf_op jit(solution)/shard_map/ppermute | solution.py:29
  49.7 16.7 %decode.1 = (bf16[128,2304]{1,0:T(8,128)(2,1)}, bf16[128,2304]{1,0:T(8,128)(2,1)}, f32[128,2304]{1,0:T(8,128)}, f32[128,2304]{1,0:T(8,128)}) custom-call(s32[17]{0:T(128)} %concatenate.6.index_ref, bf16[128,1024]{1,0:T(8,128)(2,1)} %get-tuple-element.88.refs_0_, bf16[128,1024]{1,0:T(8,128)(2,1)} %copy-done.6, bf16[128,1024]{1,0:T(8,128)(2,1)} %copy-done.8, ...), custom_call_target="tpu_custom_call" | custom-call | flops 1048576 | bytes 1024 | tf_op jit(solution)/shard_map/decode/pallas_call | solution.py:102
  66.5 2.2 %collective-permute-done.12 = bf16[128,2304]{1,0:T(8,128)(2,1)S(1)} collective-permute-done((bf16[128,2304]{1,0:T(8,128)(2,1)}, bf16[128,2304]{1,0:T(8,128)(2,1)S(1)}, u32[]{:S(2)}, u32[]{:S(2)}) %collective-permute-start.12) | collective-permute-done | bytes 589856 | tf_op jit(solution)/shard_map/ppermute | solution.py:29
  68.7 1.1 add_convert_fusion.9
  69.8 1.7 collective-permute-start.14
  71.9 4.7 %collective-permute-done.14 = bf16[32,2304]{1,0:T(8,128)(2,1)S(1)} collective-permute-done((bf16[32,2304]{1,0:T(8,128)(2,1)S(1)}, bf16[32,2304]{1,0:T(8,128)(2,1)S(1)}, u32[]{:S(2)}, u32[]{:S(2)}) %collective-permute-start.14) | collective-permute-done | bytes 147488 | tf_op jit(solution)/shard_map/ppermute | solution.py:29
  76.6 1.0 add_convert_fusion.7
  77.6 2.7 %collective-permute-start.15 = (bf16[32,2304]{1,0:T(8,128)(2,1)S(1)}, bf16[32,2304]{1,0:T(8,128)(2,1)S(1)}, u32[]{:S(2)}, u32[]{:S(2)}) collective-permute-start(bf16[32,2304]{1,0:T(8,128)(2,1)S(1)} %add_convert_fusion.7), channel_id=1, source_target_pairs={{0,4},{1,5},{2,6},{3,7},{4,0},{5,1},{6,2},{7,3},{8,12},{9,13},{10,... | collective-permute-start | bytes 442376 | tf_op jit(solution)/shard_map/ppermute | solution.py:29
  80.3 1.6 collective-permute-start.18
  82.4 3.1 %collective-permute-done.15 = bf16[32,2304]{1,0:T(8,128)(2,1)S(1)} collective-permute-done((bf16[32,2304]{1,0:T(8,128)(2,1)S(1)}, bf16[32,2304]{1,0:T(8,128)(2,1)S(1)}, u32[]{:S(2)}, u32[]{:S(2)}) %collective-permute-start.15) | collective-permute-done | bytes 147488 | tf_op jit(solution)/shard_map/ppermute | solution.py:29
  85.6 1.1 fusion.3
  86.7 2.5 %collective-permute-start.21 = (bf16[32,2304]{1,0:T(8,128)(2,1)S(1)}, bf16[32,2304]{1,0:T(8,128)(2,1)S(1)}, u32[]{:S(2)}, u32[]{:S(2)}) collective-permute-start(bf16[32,2304]{1,0:T(8,128)(2,1)S(1)} %get-tuple-element.109.refs_0_), channel_id=1, source_target_pairs={{0,4},{1,5},{2,6},{3,7},{4,0},{5,1},{6,2},{7,3},{8,12},{9,13},{10,... | collective-permute-start | bytes 442376 | tf_op jit(solution)/shard_map/ppermute | solution.py:29
  89.1 1.2 collective-permute-done.18
  90.5 1.0 collective-permute-start.20
  91.5 7.4 %collective-permute-done.21.refs_2_ = bf16[32,2304]{1,0:T(8,128)(2,1)S(1)} collective-permute-done((bf16[32,2304]{1,0:T(8,128)(2,1)S(1)}, bf16[32,2304]{1,0:T(8,128)(2,1)S(1)}, u32[]{:S(2)}, u32[]{:S(2)}) %collective-permute-start.21) | collective-permute-done | bytes 147488 | tf_op jit(solution)/shard_map/ppermute | solution.py:29
  99.2 1.2 collective-permute-done.19
  101.1 2.9 %collective-permute-done.22.refs_3_ = bf16[32,2304]{1,0:T(8,128)(2,1)S(1)} collective-permute-done((bf16[32,2304]{1,0:T(8,128)(2,1)S(1)}, bf16[32,2304]{1,0:T(8,128)(2,1)S(1)}, u32[]{:S(2)}, u32[]{:S(2)}) %collective-permute-start.22) | collective-permute-done | bytes 147488 | tf_op jit(solution)/shard_map/ppermute | solution.py:29
  105.4 3.6 %collective-permute-start.28 = (bf16[32,2304]{1,0:T(8,128)(2,1)S(1)}, bf16[32,2304]{1,0:T(8,128)(2,1)S(1)}, u32[]{:S(2)}, u32[]{:S(2)}) collective-permute-start(bf16[32,2304]{1,0:T(8,128)(2,1)S(1)} %get-tuple-element.126.refs_0_), channel_id=1, source_target_pairs={{0,4},{1,5},{2,6},{3,7},{4,0},{5,1},{6,2},{7,3},{8,12},{9,13},{10,... | collective-permute-start | bytes 442376 | tf_op jit(solution)/shard_map/ppermute | solution.py:29
  109.4 13.5 %gradient.2 = (bf16[2,64,1024]{2,1,0:T(8,128)(2,1)S(1)}, bf16[2,64,1024]{2,1,0:T(8,128)(2,1)S(1)}, f32[2,64,1024]{2,1,0:T(8,128)S(1)}, f32[2,64,1024]{2,1,0:T(8,...) custom-call(s32[17]{0:T(128)S(1)} %copy-done.4, ...), custom_call_target="tpu_custom_call" | custom-call | flops 1048576 | bytes 1024 | tf_op jit(solution)/shard_map/gradient/pallas_call | solution.py:102
  123.0 1.6 collective-permute-start.35
  125.6 5.3 %collective-permute-done.35 = bf16[2,64,1024]{2,1,0:T(8,128)(2,1)S(1)} collective-permute-done((bf16[2,64,1024]{2,1,0:T(8,128)(2,1)S(1)}, bf16[2,64,1024]{2,1,0:T(8,128)(2,1)S(1)}, u32[]{:S(2)}, u32[]{:S(2)}) %collective-permute-start.35) | collective-permute-done | bytes 262176 | tf_op jit(solution)/shard_map/ppermute | solution.py:29
  130.9 1.5 collective-permute-start.38
  133.2 1.6 collective-permute-start.40
  135.2 1.4 collective-permute-done.33.refs_7_
  136.6 13.5 %gradient.3 = (bf16[2,64,1024]{2,1,0:T(8,128)(2,1)S(1)}, bf16[2,64,1024]{2,1,0:T(8,128)(2,1)S(1)}, f32[2,64,1024]{2,1,0:T(8,128)S(1)}, f32[2,64,1024]{2,1,0:T(8,...) custom-call(s32[17]{0:T(128)S(1)} %copy-done.4, ...), custom_call_target="tpu_custom_call" | custom-call | flops 1048576 | bytes 1024 | tf_op jit(solution)/shard_map/gradient/pallas_call | solution.py:102
  150.1 1.6 collective-permute-start.42
  153.5 1.6 collective-permute-start.36
  155.1 4.8 %collective-permute-done.36 = f32[8,128]{1,0:T(8,128)S(1)} collective-permute-done((f32[8,128]{1,0:T(8,128)S(1)}, f32[8,128]{1,0:T(8,128)S(1)}, u32[]{:S(2)}, u32[]{:S(2)}) %collective-permute-start.36) | collective-permute-done | bytes 4128 | tf_op jit(solution)/shard_map/ppermute | solution.py:29
  160.6 1.3 finish.2.refs_6_
  163.4 1.2 collective-permute-start.47
  164.7 1.6 collective-permute-start.46
  167.5 7.4 %collective-permute-done.43 = f32[8,128]{1,0:T(8,128)S(1)} collective-permute-done((f32[8,128]{1,0:T(8,128)S(1)}, f32[8,128]{1,0:T(8,128)S(1)}, u32[]{:S(2)}, u32[]{:S(2)}) %collective-permute-start.43) | collective-permute-done | bytes 4128 | tf_op jit(solution)/shard_map/ppermute | solution.py:29
  176.1 1.3 finish.3
  (111 shorter events, 16.2 us)
Async XLA Ops:
  7.1 11.6 %collective-permute-start = (bf16[128,1024]{1,0:T(8,128)(2,1)}, bf16[128,1024]{1,0:T(8,128)(2,1)S(1)}, u32[]{:S(2)}, u32[]{:S(2)}) collective-permute-start(bf16[128,1024]{1,0:T(8,128)(2,1)} %get-tuple-element.88.refs_0_), channel_id=1, source_target_pairs={{0,8},{8,0},{16,24},{24,16},{1,9},{9,1},{17,25},{25,17},{2,10},{10... | collective-permute-start | bytes 786440 | tf_op jit(solution)/shard_map/ppermute | solution.py:29
  10.1 9.4 %collective-permute-start.4 = (bf16[128,1024]{1,0:T(8,128)(2,1)}, bf16[128,1024]{1,0:T(8,128)(2,1)S(1)}, u32[]{:S(2)}, u32[]{:S(2)}) collective-permute-start(bf16[128,1024]{1,0:T(8,128)(2,1)} %get-tuple-element.92.refs_1_.refs_4_), channel_id=1, source_target_pairs={{0,16},{8,24},{16,0},{24,8},{1,17},{9,25},{17,1},{25,9},{2,18},{10... | collective-permute-start | bytes 786440 | tf_op jit(solution)/shard_map/ppermute | solution.py:29
  11.7 12.1 %collective-permute-start.1 = (bf16[128,1024]{1,0:T(8,128)(2,1)}, bf16[128,1024]{1,0:T(8,128)(2,1)S(1)}, u32[]{:S(2)}, u32[]{:S(2)}) collective-permute-start(bf16[128,1024]{1,0:T(8,128)(2,1)} %get-tuple-element.88.refs_0_), channel_id=1, source_target_pairs={{0,16},{8,24},{16,0},{24,8},{1,17},{9,25},{17,1},{25,9},{2,18},{10... | collective-permute-start | bytes 786440 | tf_op jit(solution)/shard_map/ppermute | solution.py:29
  12.2 11.6 %collective-permute-start.3 = (bf16[128,1024]{1,0:T(8,128)(2,1)}, bf16[128,1024]{1,0:T(8,128)(2,1)S(1)}, u32[]{:S(2)}, u32[]{:S(2)}) collective-permute-start(bf16[128,1024]{1,0:T(8,128)(2,1)} %get-tuple-element.92.refs_1_.refs_4_), channel_id=1, source_target_pairs={{0,8},{8,0},{16,24},{24,16},{1,9},{9,1},{17,25},{25,17},{2,10},{10... | collective-permute-start | bytes 786440 | tf_op jit(solution)/shard_map/ppermute | solution.py:29
  23.7 9.5 %collective-permute-start.10 = (bf16[128,1024]{1,0:T(8,128)(2,1)}, bf16[128,1024]{1,0:T(8,128)(2,1)S(1)}, u32[]{:S(2)}, u32[]{:S(2)}) collective-permute-start(bf16[128,1024]{1,0:T(8,128)(2,1)} %get-tuple-element.100.refs_3_.refs_12_), channel_id=1, source_target_pairs={{0,16},{8,24},{16,0},{24,8},{1,17},{9,25},{17,1},{25,9},{2,18},{10... | collective-permute-start | bytes 786440 | tf_op jit(solution)/shard_map/ppermute | solution.py:29
  25.3 13.5 %collective-permute-start.2 = (bf16[128,1024]{1,0:T(8,128)(2,1)S(1)}, bf16[128,1024]{1,0:T(8,128)(2,1)S(1)}, u32[]{:S(2)}, u32[]{:S(2)}) collective-permute-start(bf16[128,1024]{1,0:T(8,128)(2,1)S(1)} %collective-permute-done.refs_1_), channel_id=1, source_target_pairs={{0,16},{8,24},{16,0},{24,8},{1,17},{9,25},{17,1},{25,9},{2,18},{10... | collective-permute-start | bytes 786440 | tf_op jit(solution)/shard_map/ppermute | solution.py:29
  25.8 13.0 %collective-permute-start.5 = (bf16[128,1024]{1,0:T(8,128)(2,1)S(1)}, bf16[128,1024]{1,0:T(8,128)(2,1)S(1)}, u32[]{:S(2)}, u32[]{:S(2)}) collective-permute-start(bf16[128,1024]{1,0:T(8,128)(2,1)S(1)} %collective-permute-done.4.refs_6_), channel_id=1, source_target_pairs={{0,8},{8,0},{16,24},{24,16},{1,9},{9,1},{17,25},{25,17},{2,10},{10... | collective-permute-start | bytes 786440 | tf_op jit(solution)/shard_map/ppermute | solution.py:29
  26.2 14.5 %collective-permute-start.6 = (bf16[128,1024]{1,0:T(8,128)(2,1)}, bf16[128,1024]{1,0:T(8,128)(2,1)S(1)}, u32[]{:S(2)}, u32[]{:S(2)}) collective-permute-start(bf16[128,1024]{1,0:T(8,128)(2,1)} %get-tuple-element.96.refs_2_.refs_8_), channel_id=1, source_target_pairs={{0,8},{8,0},{16,24},{24,16},{1,9},{9,1},{17,25},{25,17},{2,10},{10... | collective-permute-start | bytes 786440 | tf_op jit(solution)/shard_map/ppermute | solution.py:29
  27.9 18.6 %collective-permute-start.7 = (bf16[128,1024]{1,0:T(8,128)(2,1)}, bf16[128,1024]{1,0:T(8,128)(2,1)S(1)}, u32[]{:S(2)}, u32[]{:S(2)}) collective-permute-start(bf16[128,1024]{1,0:T(8,128)(2,1)} %get-tuple-element.96.refs_2_.refs_8_), channel_id=1, source_target_pairs={{0,16},{8,24},{16,0},{24,8},{1,17},{9,25},{17,1},{25,9},{2,18},{10... | collective-permute-start | bytes 786440 | tf_op jit(solution)/shard_map/ppermute | solution.py:29
  33.3 13.2 %collective-permute-start.9 = (bf16[128,1024]{1,0:T(8,128)(2,1)}, bf16[128,1024]{1,0:T(8,128)(2,1)S(1)}, u32[]{:S(2)}, u32[]{:S(2)}) collective-permute-start(bf16[128,1024]{1,0:T(8,128)(2,1)} %get-tuple-element.100.refs_3_.refs_12_), channel_id=1, source_target_pairs={{0,8},{8,0},{16,24},{24,16},{1,9},{9,1},{17,25},{25,17},{2,10},{10... | collective-permute-start | bytes 786440 | tf_op jit(solution)/shard_map/ppermute | solution.py:29
  38.9 10.1 %collective-permute-start.11 = (bf16[128,1024]{1,0:T(8,128)(2,1)S(1)}, bf16[128,1024]{1,0:T(8,128)(2,1)S(1)}, u32[]{:S(2)}, u32[]{:S(2)}) collective-permute-start(bf16[128,1024]{1,0:T(8,128)(2,1)S(1)} %collective-permute-done.10.refs_14_), channel_id=1, source_target_pairs={{0,8},{8,0},{16,24},{24,16},{1,9},{9,1},{17,25},{25,17},{2,10},{10... | collective-permute-start | bytes 786440 | tf_op jit(solution)/shard_map/ppermute | solution.py:29
  40.7 8.3 %collective-permute-start.8 = (bf16[128,1024]{1,0:T(8,128)(2,1)S(1)}, bf16[128,1024]{1,0:T(8,128)(2,1)}, u32[]{:S(2)}, u32[]{:S(2)}) collective-permute-start(bf16[128,1024]{1,0:T(8,128)(2,1)S(1)} %collective-permute-done.6.refs_9_), channel_id=1, source_target_pairs={{0,16},{8,24},{16,0},{24,8},{1,17},{9,25},{17,1},{25,9},{2,18},{10... | collective-permute-start | bytes 786440 | tf_op jit(solution)/shard_map/ppermute | solution.py:29
  66.4 2.3 %collective-permute-start.12 = (bf16[128,2304]{1,0:T(8,128)(2,1)}, bf16[128,2304]{1,0:T(8,128)(2,1)S(1)}, u32[]{:S(2)}, u32[]{:S(2)}) collective-permute-start(bf16[128,2304]{1,0:T(8,128)(2,1)} %get-tuple-element.105), channel_id=1, source_target_pairs={{0,1},{1,0},{2,3},{3,2},{4,5},{5,4},{6,7},{7,6},{8,9},{9,8},{10,11... | collective-permute-start | bytes 1769480 | tf_op jit(solution)/shard_map/ppermute | solution.py:29
  69.8 6.8 %collective-permute-start.14 = (bf16[32,2304]{1,0:T(8,128)(2,1)S(1)}, bf16[32,2304]{1,0:T(8,128)(2,1)S(1)}, u32[]{:S(2)}, u32[]{:S(2)}) collective-permute-start(bf16[32,2304]{1,0:T(8,128)(2,1)S(1)} %get-tuple-element.159), channel_id=1, source_target_pairs={{0,2},{1,3},{2,0},{3,1},{4,6},{5,7},{6,4},{7,5},{8,10},{9,11},{10,... | collective-permute-start | bytes 442376 | tf_op jit(solution)/shard_map/ppermute | solution.py:29
  71.5 8.8 %collective-permute-start.16 = (bf16[128,2304]{1,0:T(8,128)(2,1)}, bf16[128,2304]{1,0:T(8,128)(2,1)S(1)}, u32[]{:S(2)}, u32[]{:S(2)}) collective-permute-start(bf16[128,2304]{1,0:T(8,128)(2,1)} %get-tuple-element.107), channel_id=1, source_target_pairs={{0,1},{1,0},{2,3},{3,2},{4,5},{5,4},{6,7},{7,6},{8,9},{9,8},{10,11... | collective-permute-start | bytes 1769480 | tf_op jit(solution)/shard_map/ppermute | solution.py:29
  71.5 10.9 %collective-permute-start.13 = (bf16[32,2304]{1,0:T(8,128)(2,1)S(1)}, bf16[32,2304]{1,0:T(8,128)(2,1)S(1)}, u32[]{:S(2)}, u32[]{:S(2)}) collective-permute-start(bf16[32,2304]{1,0:T(8,128)(2,1)S(1)} %get-tuple-element.158), channel_id=1, source_target_pairs={{0,2},{1,3},{2,0},{3,1},{4,6},{5,7},{6,4},{7,5},{8,10},{9,11},{10,... | collective-permute-start | bytes 442376 | tf_op jit(solution)/shard_map/ppermute | solution.py:29
  77.6 8.0 %collective-permute-start.15 = (bf16[32,2304]{1,0:T(8,128)(2,1)S(1)}, bf16[32,2304]{1,0:T(8,128)(2,1)S(1)}, u32[]{:S(2)}, u32[]{:S(2)}) collective-permute-start(bf16[32,2304]{1,0:T(8,128)(2,1)S(1)} %add_convert_fusion.7), channel_id=1, source_target_pairs={{0,4},{1,5},{2,6},{3,7},{4,0},{5,1},{6,2},{7,3},{8,12},{9,13},{10,... | collective-permute-start | bytes 442376 | tf_op jit(solution)/shard_map/ppermute | solution.py:29
  80.3 10.0 %collective-permute-start.18 = (bf16[32,2304]{1,0:T(8,128)(2,1)S(1)}, bf16[32,2304]{1,0:T(8,128)(2,1)S(1)}, u32[]{:S(2)}, u32[]{:S(2)}) collective-permute-start(bf16[32,2304]{1,0:T(8,128)(2,1)S(1)} %get-tuple-element.161), channel_id=1, source_target_pairs={{0,2},{1,3},{2,0},{3,1},{4,6},{5,7},{6,4},{7,5},{8,10},{9,11},{10,... | collective-permute-start | bytes 442376 | tf_op jit(solution)/shard_map/ppermute | solution.py:29
  82.0 17.2 %collective-permute-start.17 = (bf16[32,2304]{1,0:T(8,128)(2,1)S(1)}, bf16[32,2304]{1,0:T(8,128)(2,1)S(1)}, u32[]{:S(2)}, u32[]{:S(2)}) collective-permute-start(bf16[32,2304]{1,0:T(8,128)(2,1)S(1)} %get-tuple-element.160), channel_id=1, source_target_pairs={{0,2},{1,3},{2,0},{3,1},{4,6},{5,7},{6,4},{7,5},{8,10},{9,11},{10,... | collective-permute-start | bytes 442376 | tf_op jit(solution)/shard_map/ppermute | solution.py:29
  86.7 12.2 %collective-permute-start.21 = (bf16[32,2304]{1,0:T(8,128)(2,1)S(1)}, bf16[32,2304]{1,0:T(8,128)(2,1)S(1)}, u32[]{:S(2)}, u32[]{:S(2)}) collective-permute-start(bf16[32,2304]{1,0:T(8,128)(2,1)S(1)} %get-tuple-element.109.refs_0_), channel_id=1, source_target_pairs={{0,4},{1,5},{2,6},{3,7},{4,0},{5,1},{6,2},{7,3},{8,12},{9,13},{10,... | collective-permute-start | bytes 442376 | tf_op jit(solution)/shard_map/ppermute | solution.py:29
  90.4 10.1 %collective-permute-start.19 = (bf16[32,2304]{1,0:T(8,128)(2,1)S(1)}, bf16[32,2304]{1,0:T(8,128)(2,1)S(1)}, u32[]{:S(2)}, u32[]{:S(2)}) collective-permute-start(bf16[32,2304]{1,0:T(8,128)(2,1)S(1)} %add_convert_fusion.4), channel_id=1, source_target_pairs={{0,4},{1,5},{2,6},{3,7},{4,0},{5,1},{6,2},{7,3},{8,12},{9,13},{10,... | collective-permute-start | bytes 442376 | tf_op jit(solution)/shard_map/ppermute | solution.py:29
  90.5 10.2 %collective-permute-start.20 = (bf16[32,2304]{1,0:T(8,128)(2,1)S(1)}, bf16[32,2304]{1,0:T(8,128)(2,1)S(1)}, u32[]{:S(2)}, u32[]{:S(2)}) collective-permute-start(bf16[32,2304]{1,0:T(8,128)(2,1)S(1)} %get-tuple-element.109.refs_0_), channel_id=1, source_target_pairs={{0,2},{1,3},{2,0},{3,1},{4,6},{5,7},{6,4},{7,5},{8,10},{9,11},{10,... | collective-permute-start | bytes 442376 | tf_op jit(solution)/shard_map/ppermute | solution.py:29
  91.5 13.9 %collective-permute-start.23 = (bf16[32,2304]{1,0:T(8,128)(2,1)S(1)}, bf16[32,2304]{1,0:T(8,128)(2,1)S(1)}, u32[]{:S(2)}, u32[]{:S(2)}) collective-permute-start(bf16[32,2304]{1,0:T(8,128)(2,1)S(1)} %get-tuple-element.109.refs_0_), channel_id=1, source_target_pairs={{0,1},{1,0},{2,3},{3,2},{4,5},{5,4},{6,7},{7,6},{8,9},{9,8},{10,11... | collective-permute-start | bytes 442376 | tf_op jit(solution)/shard_map/ppermute | solution.py:29
  98.9 5.1 %collective-permute-start.22 = (bf16[32,2304]{1,0:T(8,128)(2,1)S(1)}, bf16[32,2304]{1,0:T(8,128)(2,1)S(1)}, u32[]{:S(2)}, u32[]{:S(2)}) collective-permute-start(bf16[32,2304]{1,0:T(8,128)(2,1)S(1)} %collective-permute-done.21.refs_2_), channel_id=1, source_target_pairs={{0,2},{1,3},{2,0},{3,1},{4,6},{5,7},{6,4},{7,5},{8,10},{9,11},{10,... | collective-permute-start | bytes 442376 | tf_op jit(solution)/shard_map/ppermute | solution.py:29
  100.5 8.9 %collective-permute-start.25 = (bf16[32,2304]{1,0:T(8,128)(2,1)S(1)}, bf16[32,2304]{1,0:T(8,128)(2,1)S(1)}, u32[]{:S(2)}, u32[]{:S(2)}) collective-permute-start(bf16[32,2304]{1,0:T(8,128)(2,1)S(1)} %collective-permute-done.21.refs_2_), channel_id=1, source_target_pairs={{0,1},{1,0},{2,3},{3,2},{4,5},{5,4},{6,7},{7,6},{8,9},{9,8},{10,11... | collective-permute-start | bytes 442376 | tf_op jit(solution)/shard_map/ppermute | solution.py:29
  100.6 8.4 %collective-permute-start.24 = (bf16[32,2304]{1,0:T(8,128)(2,1)S(1)}, bf16[32,2304]{1,0:T(8,128)(2,1)S(1)}, u32[]{:S(2)}, u32[]{:S(2)}) collective-permute-start(bf16[32,2304]{1,0:T(8,128)(2,1)S(1)} %collective-permute-done.20.refs_1_), channel_id=1, source_target_pairs={{0,1},{1,0},{2,3},{3,2},{4,5},{5,4},{6,7},{7,6},{8,9},{9,8},{10,11... | collective-permute-start | bytes 442376 | tf_op jit(solution)/shard_map/ppermute | solution.py:29
  104.0 5.4 %collective-permute-start.26 = (bf16[32,2304]{1,0:T(8,128)(2,1)S(1)}, bf16[32,2304]{1,0:T(8,128)(2,1)S(1)}, u32[]{:S(2)}, u32[]{:S(2)}) collective-permute-start(bf16[32,2304]{1,0:T(8,128)(2,1)S(1)} %collective-permute-done.22.refs_3_), channel_id=1, source_target_pairs={{0,1},{1,0},{2,3},{3,2},{4,5},{5,4},{6,7},{7,6},{8,9},{9,8},{10,11... | collective-permute-start | bytes 442376 | tf_op jit(solution)/shard_map/ppermute | solution.py:29
  105.0 18.0 %collective-permute-start.27 = (bf16[32,2304]{1,0:T(8,128)(2,1)S(1)}, bf16[32,2304]{1,0:T(8,128)(2,1)S(1)}, u32[]{:S(2)}, u32[]{:S(2)}) collective-permute-start(bf16[32,2304]{1,0:T(8,128)(2,1)S(1)} %get-tuple-element.126.refs_0_), channel_id=1, source_target_pairs={{0,2},{1,3},{2,0},{3,1},{4,6},{5,7},{6,4},{7,5},{8,10},{9,11},{10,... | collective-permute-start | bytes 442376 | tf_op jit(solution)/shard_map/ppermute | solution.py:29
  105.4 17.6 %collective-permute-start.28 = (bf16[32,2304]{1,0:T(8,128)(2,1)S(1)}, bf16[32,2304]{1,0:T(8,128)(2,1)S(1)}, u32[]{:S(2)}, u32[]{:S(2)}) collective-permute-start(bf16[32,2304]{1,0:T(8,128)(2,1)S(1)} %get-tuple-element.126.refs_0_), channel_id=1, source_target_pairs={{0,4},{1,5},{2,6},{3,7},{4,0},{5,1},{6,2},{7,3},{8,12},{9,13},{10,... | collective-permute-start | bytes 442376 | tf_op jit(solution)/shard_map/ppermute | solution.py:29
  109.0 14.0 %collective-permute-start.29 = (bf16[32,2304]{1,0:T(8,128)(2,1)S(1)}, bf16[32,2304]{1,0:T(8,128)(2,1)S(1)}, u32[]{:S(2)}, u32[]{:S(2)}) collective-permute-start(bf16[32,2304]{1,0:T(8,128)(2,1)S(1)} %get-tuple-element.126.refs_0_), channel_id=1, source_target_pairs={{0,6},{1,7},{2,4},{3,5},{4,2},{5,3},{6,0},{7,1},{8,14},{9,15},{10,... | collective-permute-start | bytes 442376 | tf_op jit(solution)/shard_map/ppermute | solution.py:29
  123.0 7.9 %collective-permute-start.35 = (bf16[2,64,1024]{2,1,0:T(8,128)(2,1)S(1)}, bf16[2,64,1024]{2,1,0:T(8,128)(2,1)S(1)}, u32[]{:S(2)}, u32[]{:S(2)}) collective-permute-start(bf16[2,64,1024]{2,1,0:T(8,128)(2,1)S(1)} %get-tuple-element.125), channel_id=1, source_target_pairs={{0,16},{8,24},{16,0},{24,8},{1,17},{9,25},{17,1},{25,9},{2,18},{10... | collective-permute-start | bytes 786440 | tf_op jit(solution)/shard_map/ppermute | solution.py:29
  124.6 7.9 %collective-permute-start.34 = (bf16[2,64,1024]{2,1,0:T(8,128)(2,1)S(1)}, bf16[2,64,1024]{2,1,0:T(8,128)(2,1)S(1)}, u32[]{:S(2)}, u32[]{:S(2)}) collective-permute-start(bf16[2,64,1024]{2,1,0:T(8,128)(2,1)S(1)} %get-tuple-element.121), channel_id=1, source_target_pairs={{0,8},{8,0},{16,24},{24,16},{1,9},{9,1},{17,25},{25,17},{2,10},{10... | collective-permute-start | bytes 786440 | tf_op jit(solution)/shard_map/ppermute | solution.py:29
  125.1 8.0 %collective-permute-start.30 = (bf16[32,2304]{1,0:T(8,128)(2,1)S(1)}, bf16[32,2304]{1,0:T(8,128)(2,1)S(1)}, u32[]{:S(2)}, u32[]{:S(2)}) collective-permute-start(bf16[32,2304]{1,0:T(8,128)(2,1)S(1)} %get-tuple-element.126.refs_0_), channel_id=1, source_target_pairs={{0,1},{1,0},{2,3},{3,2},{4,5},{5,4},{6,7},{7,6},{8,9},{9,8},{10,11... | collective-permute-start | bytes 442376 | tf_op jit(solution)/shard_map/ppermute | solution.py:29
  125.1 9.6 %collective-permute-start.31 = (bf16[32,2304]{1,0:T(8,128)(2,1)S(1)}, bf16[32,2304]{1,0:T(8,128)(2,1)S(1)}, u32[]{:S(2)}, u32[]{:S(2)}) collective-permute-start(bf16[32,2304]{1,0:T(8,128)(2,1)S(1)} %collective-permute-done.27.refs_1_), channel_id=1, source_target_pairs={{0,1},{1,0},{2,3},{3,2},{4,5},{5,4},{6,7},{7,6},{8,9},{9,8},{10,11... | collective-permute-start | bytes 442376 | tf_op jit(solution)/shard_map/ppermute | solution.py:29
  125.6 9.6 %collective-permute-start.32 = (bf16[32,2304]{1,0:T(8,128)(2,1)S(1)}, bf16[32,2304]{1,0:T(8,128)(2,1)S(1)}, u32[]{:S(2)}, u32[]{:S(2)}) collective-permute-start(bf16[32,2304]{1,0:T(8,128)(2,1)S(1)} %collective-permute-done.28.refs_2_), channel_id=1, source_target_pairs={{0,1},{1,0},{2,3},{3,2},{4,5},{5,4},{6,7},{7,6},{8,9},{9,8},{10,11... | collective-permute-start | bytes 442376 | tf_op jit(solution)/shard_map/ppermute | solution.py:29
  130.9 19.2 %collective-permute-start.38 = (bf16[2,64,1024]{2,1,0:T(8,128)(2,1)S(1)}, bf16[2,64,1024]{2,1,0:T(8,128)(2,1)S(1)}, u32[]{:S(2)}, u32[]{:S(2)}) collective-permute-start(bf16[2,64,1024]{2,1,0:T(8,128)(2,1)S(1)} %get-tuple-element.141), channel_id=1, source_target_pairs={{0,16},{8,24},{16,0},{24,8},{1,17},{9,25},{17,1},{25,9},{2,18},{10... | collective-permute-start | bytes 786440 | tf_op jit(solution)/shard_map/ppermute | solution.py:29
  132.5 17.6 %collective-permute-start.37 = (bf16[2,64,1024]{2,1,0:T(8,128)(2,1)S(1)}, bf16[2,64,1024]{2,1,0:T(8,128)(2,1)S(1)}, u32[]{:S(2)}, u32[]{:S(2)}) collective-permute-start(bf16[2,64,1024]{2,1,0:T(8,128)(2,1)S(1)} %get-tuple-element.139), channel_id=1, source_target_pairs={{0,8},{8,0},{16,24},{24,16},{1,9},{9,1},{17,25},{25,17},{2,10},{10... | collective-permute-start | bytes 786440 | tf_op jit(solution)/shard_map/ppermute | solution.py:29
  133.2 17.0 %collective-permute-start.40 = (bf16[2,64,1024]{2,1,0:T(8,128)(2,1)S(1)}, bf16[2,64,1024]{2,1,0:T(8,128)(2,1)S(1)}, u32[]{:S(2)}, u32[]{:S(2)}) collective-permute-start(bf16[2,64,1024]{2,1,0:T(8,128)(2,1)S(1)} %add_convert_fusion.2), channel_id=1, source_target_pairs={{0,8},{8,0},{16,24},{24,16},{1,9},{9,1},{17,25},{25,17},{2,10},{10... | collective-permute-start | bytes 786440 | tf_op jit(solution)/shard_map/ppermute | solution.py:29
  134.7 15.4 %collective-permute-start.39 = (bf16[2,64,1024]{2,1,0:T(8,128)(2,1)S(1)}, bf16[2,64,1024]{2,1,0:T(8,128)(2,1)S(1)}, u32[]{:S(2)}, u32[]{:S(2)}) collective-permute-start(bf16[2,64,1024]{2,1,0:T(8,128)(2,1)S(1)} %add_convert_fusion.3), channel_id=1, source_target_pairs={{0,16},{8,24},{16,0},{24,8},{1,17},{9,25},{17,1},{25,9},{2,18},{10... | collective-permute-start | bytes 786440 | tf_op jit(solution)/shard_map/ppermute | solution.py:29
  135.2 1.4 collective-permute-start.33
  150.1 11.8 %collective-permute-start.42 = (bf16[2,64,1024]{2,1,0:T(8,128)(2,1)S(1)}, bf16[2,64,1024]{2,1,0:T(8,128)(2,1)S(1)}, u32[]{:S(2)}, u32[]{:S(2)}) collective-permute-start(bf16[2,64,1024]{2,1,0:T(8,128)(2,1)S(1)} %get-tuple-element.146), channel_id=1, source_target_pairs={{0,16},{8,24},{16,0},{24,8},{1,17},{9,25},{17,1},{25,9},{2,18},{10... | collective-permute-start | bytes 786440 | tf_op jit(solution)/shard_map/ppermute | solution.py:29
  151.7 10.7 %collective-permute-start.41 = (bf16[2,64,1024]{2,1,0:T(8,128)(2,1)S(1)}, bf16[2,64,1024]{2,1,0:T(8,128)(2,1)S(1)}, u32[]{:S(2)}, u32[]{:S(2)}) collective-permute-start(bf16[2,64,1024]{2,1,0:T(8,128)(2,1)S(1)} %get-tuple-element.142), channel_id=1, source_target_pairs={{0,8},{8,0},{16,24},{24,16},{1,9},{9,1},{17,25},{25,17},{2,10},{10... | collective-permute-start | bytes 786440 | tf_op jit(solution)/shard_map/ppermute | solution.py:29
  153.5 6.4 %collective-permute-start.36 = (f32[8,128]{1,0:T(8,128)S(1)}, f32[8,128]{1,0:T(8,128)S(1)}, u32[]{:S(2)}, u32[]{:S(2)}) collective-permute-start(f32[8,128]{1,0:T(8,128)S(1)} %broadcast_in_dim.11), channel_id=1, source_target_pairs={{0,8},{8,0},{16,24},{24,16},{1,9},{9,1},{17,25},{25,17},{2,10},{10... | collective-permute-start | bytes 12296 | tf_op jit(solution)/shard_map/ppermute | solution.py:29
  161.9 14.2 %collective-permute-start.45 = (bf16[2,64,1024]{2,1,0:T(8,128)(2,1)S(1)}, bf16[2,64,1024]{2,1,0:T(8,128)(2,1)S(1)}, u32[]{:S(2)}, u32[]{:S(2)}) collective-permute-start(bf16[2,64,1024]{2,1,0:T(8,128)(2,1)S(1)} %get-tuple-element.155), channel_id=1, source_target_pairs={{0,16},{8,24},{16,0},{24,8},{1,17},{9,25},{17,1},{25,9},{2,18},{10... | collective-permute-start | bytes 786440 | tf_op jit(solution)/shard_map/ppermute | solution.py:29
  162.4 13.6 %collective-permute-start.44 = (bf16[2,64,1024]{2,1,0:T(8,128)(2,1)S(1)}, bf16[2,64,1024]{2,1,0:T(8,128)(2,1)S(1)}, u32[]{:S(2)}, u32[]{:S(2)}) collective-permute-start(bf16[2,64,1024]{2,1,0:T(8,128)(2,1)S(1)} %get-tuple-element.153), channel_id=1, source_target_pairs={{0,8},{8,0},{16,24},{24,16},{1,9},{9,1},{17,25},{25,17},{2,10},{10... | collective-permute-start | bytes 786440 | tf_op jit(solution)/shard_map/ppermute | solution.py:29
  163.4 12.7 %collective-permute-start.47 = (bf16[2,64,1024]{2,1,0:T(8,128)(2,1)S(1)}, bf16[2,64,1024]{2,1,0:T(8,128)(2,1)S(1)}, u32[]{:S(2)}, u32[]{:S(2)}) collective-permute-start(bf16[2,64,1024]{2,1,0:T(8,128)(2,1)S(1)} %add_convert_fusion), channel_id=1, source_target_pairs={{0,8},{8,0},{16,24},{24,16},{1,9},{9,1},{17,25},{25,17},{2,10},{10... | collective-permute-start | bytes 786440 | tf_op jit(solution)/shard_map/ppermute | solution.py:29
  164.7 11.4 %collective-permute-start.46 = (bf16[2,64,1024]{2,1,0:T(8,128)(2,1)S(1)}, bf16[2,64,1024]{2,1,0:T(8,128)(2,1)S(1)}, u32[]{:S(2)}, u32[]{:S(2)}) collective-permute-start(bf16[2,64,1024]{2,1,0:T(8,128)(2,1)S(1)} %add_convert_fusion.1), channel_id=1, source_target_pairs={{0,16},{8,24},{16,0},{24,8},{1,17},{9,25},{17,1},{25,9},{2,18},{10... | collective-permute-start | bytes 786440 | tf_op jit(solution)/shard_map/ppermute | solution.py:29
  166.3 8.6 %collective-permute-start.43 = (f32[8,128]{1,0:T(8,128)S(1)}, f32[8,128]{1,0:T(8,128)S(1)}, u32[]{:S(2)}, u32[]{:S(2)}) collective-permute-start(f32[8,128]{1,0:T(8,128)S(1)} %broadcast_add_fusion), channel_id=1, source_target_pairs={{0,16},{8,24},{16,0},{24,8},{1,17},{9,25},{17,1},{25,9},{2,18},{10... | collective-permute-start | bytes 12296 | tf_op jit(solution)/shard_map/ppermute | solution.py:29
  (18 other events, 302.8 us)

commit v9 on v8

--- a/solution.py
+++ b/solution.py
@@ -66,7 +66,7 @@
 
 
 def streamed(count, slots, copies_of, body):
-    early = min(1, slots - 1, count)
+    early = min(slots - 1, count)
     for i in range(early):
         for copy in copies_of(i, i):
             copy.start()
@@ -156,10 +156,10 @@
         [jax.ShapeDtypeStruct((plan.rows, plan.width), BF16)] * (hi - lo),
         [
             pltpu.VMEM((hi - lo, plan.rows, plan.model), BF16),
-            pltpu.VMEM((WEIGHT_SLOTS + 1, plan.model, tile), BF16),
+            pltpu.VMEM((2 * WEIGHT_SLOTS, plan.model, tile), BF16),
             pltpu.VMEM((plan.sources, plan.width), F32),
             pltpu.SemaphoreType.DMA((2,)),
-            pltpu.SemaphoreType.DMA((WEIGHT_SLOTS + 1,)),
+            pltpu.SemaphoreType.DMA((2 * WEIGHT_SLOTS,)),
         ],
         (resid, w_enc, b_enc),
         vmem=MOST_VMEM_BYTES,
@@ -306,7 +306,7 @@
     n_in = 2 * plan.depth
     errors, w_ref, outs = refs[:n_in], refs[n_in], refs[n_in + 1:-4]
     e_buf, w_buf, e_sem, w_sem = refs[-4:]
-    depth = pick_tile(plan.width, 256)
+    depth = pick_tile(plan.width, 512)
     steps = plan.width // depth
     base = 1 + plan.sources + plan.groups * plan.pairs
 
@@ -339,8 +339,8 @@
         source = lax.div(i, steps)
         cols = pl.ds(pl.multiple_of(lax.rem(i, steps) * depth, depth), depth)
         product = lax.dot_general(
-            e_buf[...], w_buf[slot], (((1,), (1,)), ((), ())), preferred_element_type=F32
-        )
+            w_buf[slot], e_buf[...], (((1,), (1,)), ((), ())), preferred_element_type=F32
+        ).T
         product = jnp.where(index_ref[1 + source] > 0, product, 0.0)
         for lane, (lo, hi) in enumerate(plan.lane_sources):
             first, kept = plan.lanes[lane][0], plan.kept_order(lane)
@@ -370,7 +370,7 @@
 
 
 def gradient(plan, index, errors, w_dec):
-    depth = pick_tile(plan.width, 256)
+    depth = pick_tile(plan.width, 512)
     half = plan.groups // 2
     out_shape = []
     for lo, hi in plan.lane_sources:
@@ -384,9 +384,9 @@
         out_shape + [jax.ShapeDtypeStruct((8, 128), F32)],
         [
             pltpu.VMEM((plan.chunk_rows, plan.model), BF16),
-            pltpu.VMEM((2 * WEIGHT_SLOTS, depth, plan.model), BF16),
+            pltpu.VMEM((WEIGHT_SLOTS, depth, plan.model), BF16),
             pltpu.SemaphoreType.DMA((len(errors),)),
-            pltpu.SemaphoreType.DMA((2 * WEIGHT_SLOTS,)),
+            pltpu.SemaphoreType.DMA((WEIGHT_SLOTS,)),
         ],
         (index, *errors, w_dec),
     )
@@ -464,9 +464,9 @@
         encoded += encode(plan, lo, hi, resid, w_enc, b_enc)
     active = arrange(plan, encoded)
 
-    pieces, arrived, forwarded = [], [], []
+    pieces, arrived, also, forwarded = [], [], [], []
     for batch in batches:
-        before, arrived, before_forward, forwarded = arrived, [], forwarded, []
+        before, arrived, before_forward, forwarded = arrived, [], also + forwarded, []
         for s in batch:
             bits = plan.lanes[s % len(plan.lanes)]
             mine, = after([encoded[s]], before)
@@ -478,22 +478,38 @@
                         x, = after([x], before_forward)
                     held[j | bit] = swap(x, "grp", groups, bit)
             pieces += [held[j] for j in range(groups)]
-            arrived += [held[bit] for bit in bits]
+            arrived.append(held[bits[0]])
+            also += [held[bit] for bit in bits[1:]]
             forwarded += [held[j] for j in range(groups) if j & (j - 1)]
 
     sends, keeps = decode(plan, index, after(pieces, [active]), w_dec)
-    recon_parts, errors = [], []
+    held_all, others = [], []
     for c in range(chunks):
-        other = swap(sends[c], "feat", feats, 1)
-        held = {
+        send, = after([sends[c]], others[-1:])
+        other = swap(send, "feat", feats, 1)
+        others.append(other)
+        held_all.append({
             d: keeps[c][d * plan.piece:(d + 1) * plan.piece]
             + other[d * plan.piece:(d + 1) * plan.piece].astype(F32)
             for d in range(plan.depth)
-        }
-        for bit in plan.level_bits:
-            away = {d: held.pop(d).astype(BF16) for d in sorted(held, reverse=True) if d & bit}
-            for d, x in away.items():
-                held[d ^ bit] = held[d ^ bit] + swap(x, "feat", feats, 2 * bit).astype(F32)
+        })
+    for bit in plan.level_bits:
+        away_all = [
+            {d: held.pop(d).astype(BF16) for d in sorted(held, reverse=True) if d & bit}
+            for held in held_all
+        ]
+        for c in range(1, chunks):
+            ready = after(away_all[c].values(), away_all[c - 1].values())
+            away_all[c] = dict(zip(away_all[c], ready))
+        for c, (held, away) in enumerate(zip(held_all, away_all)):
+            got = [swap(x, "feat", feats, 2 * bit) for x in away.values()]
+            later = [x for away_later in away_all[c + 1:c + 2] for x in away_later.values()]
+            got = [after([x], later)[0] for x in got]
+            for d, x in zip(away, got):
+                held[d ^ bit] = held[d ^ bit] + x.astype(F32)
+
+    recon_parts, errors = [], []
+    for c, held in enumerate(held_all):
         recon_rows, = after([held[0]], [e[0] for e in errors])
 
         first = feat * plan.rows_feat + c * plan.piece
@@ -514,13 +530,13 @@
         errors.append(every + [swap(e, "feat", feats, 1) for e in every])
 
     squares = jnp.zeros((8, 128), F32)
-    feat_grad = None
+    unfinished = []
     second, got_all = [], []
     for c in range(chunks):
         ready = after(errors[c], [e[0] for e in errors[c + 1:c + 2]] + second)
         lanes, total = gradient(plan, index, ready, w_dec)
         squares = squares + total
-        second = []
+        second, near = [], []
         earlier = got_all + [x for every in errors[c + 1:c + 2] for x in every[1:plan.depth]]
         lanes = [(after(away, earlier), kept) for away, kept in lanes]
         kept_all = []
@@ -531,6 +547,8 @@
                 got = [swap(x, "grp", groups, bit) for x in away[:cut]]
                 rest = after(away[cut:], got[:1])
                 got += [swap(x, "grp", groups, bit) for x in rest]
+                if not step:
+                    near += got[-1:]
                 for own, x in zip(kept, got):
                     own.append(x)
                 if cut:
@@ -539,14 +557,19 @@
                     second += away if not step else []
             kept_all.append(kept[0])
         got_all = [own[i] for i in range(1, len(kept_all[0])) for own in kept_all]
-        previous = feat_grad
-        feat_grad = finish(plan, c, [own[0] for own in kept_all], got_all, previous)
+        unfinished.append(([own[0] for own in kept_all], got_all))
+
+    feat_grad = None
+    for c, (kept, got) in enumerate(unfinished):
+        if c + 1 < chunks:
+            kept = after(kept, near)
+        feat_grad = finish(plan, c, kept, got, feat_grad)
 
     loss = jnp.full((8, 128), jnp.sum(squares), F32)
     for i, bit in enumerate(1 << i for i in range(groups.bit_length() - 1)):
         loss = loss + swap(loss, "grp", groups, bit)
         if not i:
-            loss, = after([loss], second + ([] if previous is None else [previous]))
+            loss, = after([loss], second)
     entries = targets.shape[0] * groups * plan.tokens * plan.model
     recon_loss = loss[0, 0] / entries
     recon = jnp.concatenate(recon_parts, axis=0)[None]

time: 179 us -> 180 us (level)
  transfers between devices with their start and end apart: 48 -> 48, of which waited for: 17 -> 18; matrix products, arithmetic and copies ran while one was open for 4% -> 5% of each run, Pallas kernels for 20% -> 19%
where the time goes in v9:
time: 180 us; the launch traced here: 179 us
  waiting for transfers between devices  60.5 us (34%)
  Pallas kernels  59.6 us (33%)
  starting transfers between devices  44.3 us (25%)
  other arithmetic  7.59 us (4%)
  local copies, waits for them, and re-layouts  4.59 us (3%)
  between operations  2.85 us (2%)
    ppermute x48, waiting for transfers between devices, swap(): return lax.ppermute(x, axis, [(i, i ^ offset) for i in range(size)])  60.5 us
    pallas_call x8, Pallas kernels, call(): pl.pallas_call(kernel, in_specs=in_specs, out_shape=out_shape, scratch_sh...  59.6 us
    ppermute x48, starting transfers between devices, swap(): return lax.ppermute(x, axis, [(i, i ^ offset) for i in range(size)])  44.3 us
  transfers between devices with their start and end apart: 48, of which 18 were waited for; matrix products, arithmetic and copies ran while one was open for 5% of the time, Pallas kernels for 19%

profile of v9, /device:TPU:0, one launch (start us, length us, event | category | flops | bytes accessed | tf_op | source)
XLA Modules:
  0.0 179.5 jit_solution(6900331568298081785)
XLA Ops:
  0.6 7.1 %encode.2 = (bf16[128,1024]{1,0:T(8,128)(2,1)}, bf16[128,1024]{1,0:T(8,128)(2,1)}) custom-call(bf16[4,128,2304]{2,1,0:T(8,128)(2,1)} %resid_ref.3, bf16[4,2304,1024]{2,1,0:T(8,128)(2,1)} %w_ref.3, f32[4,1024]{1,0:T(4,128)} %b_ref.3), custom_call_target="tpu_custom_call" | custom-call | flops 1048576 | bytes 1024 | tf_op jit(solution)/shard_map/encode/pallas_call | solution.py:102
  7.7 3.0 %collective-permute-start = (bf16[128,1024]{1,0:T(8,128)(2,1)}, bf16[128,1024]{1,0:T(8,128)(2,1)S(1)}, u32[]{:S(2)}, u32[]{:S(2)}) collective-permute-start(bf16[128,1024]{1,0:T(8,128)(2,1)} %get-tuple-element.97.refs_0_), channel_id=1, source_target_pairs={{0,8},{8,0},{16,24},{24,16},{1,9},{9,1},{17,25},{25,17},{2,10},{10... | collective-permute-start | bytes 786440 | tf_op jit(solution)/shard_map/ppermute | solution.py:29
  10.7 1.5 collective-permute-start.4
  12.8 6.9 %encode.3 = (bf16[128,1024]{1,0:T(8,128)(2,1)}, bf16[128,1024]{1,0:T(8,128)(2,1)}) custom-call(bf16[4,128,2304]{2,1,0:T(8,128)(2,1)} %resid_ref.3, bf16[4,2304,1024]{2,1,0:T(8,128)(2,1)} %w_ref.3, f32[4,1024]{1,0:T(4,128)} %b_ref.3), custom_call_target="tpu_custom_call" | custom-call | flops 1048576 | bytes 1024 | tf_op jit(solution)/shard_map/encode/pallas_call | solution.py:102
  20.2 1.7 collective-permute-start.10
  22.2 1.7 collective-permute-start.5
  23.8 1.9 %collective-permute-done.1.refs_2_ = bf16[128,1024]{1,0:T(8,128)(2,1)S(1)} collective-permute-done((bf16[128,1024]{1,0:T(8,128)(2,1)}, bf16[128,1024]{1,0:T(8,128)(2,1)S(1)}, u32[]{:S(2)}, u32[]{:S(2)}) %collective-permute-start.1) | collective-permute-done | bytes 262176 | tf_op jit(solution)/shard_map/ppermute | solution.py:29
  25.8 2.0 %collective-permute-start.7 = (bf16[128,1024]{1,0:T(8,128)(2,1)}, bf16[128,1024]{1,0:T(8,128)(2,1)S(1)}, u32[]{:S(2)}, u32[]{:S(2)}) collective-permute-start(bf16[128,1024]{1,0:T(8,128)(2,1)} %get-tuple-element.105.refs_2_.refs_8_), channel_id=1, source_target_pairs={{0,16},{8,24},{16,0},{24,8},{1,17},{9,25},{17,1},{25,9},{2,18},{10... | collective-permute-start | bytes 786440 | tf_op jit(solution)/shard_map/ppermute | solution.py:29
  27.8 3.5 %collective-permute-done.10.refs_14_ = bf16[128,1024]{1,0:T(8,128)(2,1)S(1)} collective-permute-done((bf16[128,1024]{1,0:T(8,128)(2,1)}, bf16[128,1024]{1,0:T(8,128)(2,1)S(1)}, u32[]{:S(2)}, u32[]{:S(2)}) %collective-permute-start.10) | collective-permute-done | bytes 262176 | tf_op jit(solution)/shard_map/ppermute | solution.py:29
  31.5 5.5 %collective-permute-done.2.refs_3_ = bf16[128,1024]{1,0:T(8,128)(2,1)S(1)} collective-permute-done((bf16[128,1024]{1,0:T(8,128)(2,1)S(1)}, bf16[128,1024]{1,0:T(8,128)(2,1)S(1)}, u32[]{:S(2)}, u32[]{:S(2)}) %collective-permute-start.2) | collective-permute-done | bytes 262176 | tf_op jit(solution)/shard_map/ppermute | solution.py:29
  37.1 2.0 %collective-permute-start.8 = (bf16[128,1024]{1,0:T(8,128)(2,1)S(1)}, bf16[128,1024]{1,0:T(8,128)(2,1)}, u32[]{:S(2)}, u32[]{:S(2)}) collective-permute-start(bf16[128,1024]{1,0:T(8,128)(2,1)S(1)} %collective-permute-done.6.refs_9_), channel_id=1, source_target_pairs={{0,16},{8,24},{16,0},{24,8},{1,17},{9,25},{17,1},{25,9},{2,18},{10... | collective-permute-start | bytes 786440 | tf_op jit(solution)/shard_map/ppermute | solution.py:29
  39.8 0.9 copy-done.2
  41.7 1.7 arrange.1
  43.5 1.9 %collective-permute-done.11.refs_15_ = bf16[128,1024]{1,0:T(8,128)(2,1)S(1)} collective-permute-done((bf16[128,1024]{1,0:T(8,128)(2,1)S(1)}, bf16[128,1024]{1,0:T(8,128)(2,1)S(1)}, u32[]{:S(2)}, u32[]{:S(2)}) %collective-permute-start.11) | collective-permute-done | bytes 262176 | tf_op jit(solution)/shard_map/ppermute | solution.py:29
  45.4 1.5 collective-permute-done.8.refs_11_
  47.0 17.7 %decode.1 = (bf16[128,2304]{1,0:T(8,128)(2,1)}, bf16[128,2304]{1,0:T(8,128)(2,1)}, f32[128,2304]{1,0:T(8,128)}, f32[128,2304]{1,0:T(8,128)}) custom-call(s32[17]{0:T(128)} %concatenate.6.index_ref, bf16[128,1024]{1,0:T(8,128)(2,1)} %get-tuple-element.97.refs_0_, bf16[128,1024]{1,0:T(8,128)(2,1)} %copy-done.8, bf16[128,1024]{1,0:T(8,128)(2,1)} %copy-done.10, ...), custom_call_target="tpu_custom_call" | custom-call | flops 1048576 | bytes 1024 | tf_op jit(solution)/shard_map/decode/pallas_call | solution.py:102
  64.8 2.2 %collective-permute-done.12 = bf16[128,2304]{1,0:T(8,128)(2,1)S(1)} collective-permute-done((bf16[128,2304]{1,0:T(8,128)(2,1)}, bf16[128,2304]{1,0:T(8,128)(2,1)S(1)}, u32[]{:S(2)}, u32[]{:S(2)}) %collective-permute-start.12) | collective-permute-done | bytes 589856 | tf_op jit(solution)/shard_map/ppermute | solution.py:29
  68.0 1.2 add_convert_fusion.9
  69.1 1.6 collective-permute-start.13
  71.3 1.1 add_convert_fusion.7
  72.4 1.6 collective-permute-start.17
  74.0 5.1 %collective-permute-done.15 = bf16[32,2304]{1,0:T(8,128)(2,1)S(1)} collective-permute-done((bf16[32,2304]{1,0:T(8,128)(2,1)S(1)}, bf16[32,2304]{1,0:T(8,128)(2,1)S(1)}, u32[]{:S(2)}, u32[]{:S(2)}) %collective-permute-start.15) | collective-permute-done | bytes 147488 | tf_op jit(solution)/shard_map/ppermute | solution.py:29
  79.1 1.0 add_convert_fusion.5
  80.0 2.7 %collective-permute-start.16 = (bf16[32,2304]{1,0:T(8,128)(2,1)S(1)}, bf16[32,2304]{1,0:T(8,128)(2,1)S(1)}, u32[]{:S(2)}, u32[]{:S(2)}) collective-permute-start(bf16[32,2304]{1,0:T(8,128)(2,1)S(1)} %add_convert_fusion.5), channel_id=1, source_target_pairs={{0,4},{1,5},{2,6},{3,7},{4,0},{5,1},{6,2},{7,3},{8,12},{9,13},{10,... | collective-permute-start | bytes 442376 | tf_op jit(solution)/shard_map/ppermute | solution.py:29
  82.7 6.2 %collective-permute-done.16 = bf16[32,2304]{1,0:T(8,128)(2,1)S(1)} collective-permute-done((bf16[32,2304]{1,0:T(8,128)(2,1)S(1)}, bf16[32,2304]{1,0:T(8,128)(2,1)S(1)}, u32[]{:S(2)}, u32[]{:S(2)}) %collective-permute-start.16) | collective-permute-done | bytes 147488 | tf_op jit(solution)/shard_map/ppermute | solution.py:29
  88.9 1.1 fusion.3
  90.1 4.0 %collective-permute-start.18 = (bf16[32,2304]{1,0:T(8,128)(2,1)S(1)}, bf16[32,2304]{1,0:T(8,128)(2,1)S(1)}, u32[]{:S(2)}, u32[]{:S(2)}) collective-permute-start(bf16[32,2304]{1,0:T(8,128)(2,1)S(1)} %get-tuple-element.119), channel_id=1, source_target_pairs={{0,2},{1,3},{2,0},{3,1},{4,6},{5,7},{6,4},{7,5},{8,10},{9,11},{10,... | collective-permute-start | bytes 442376 | tf_op jit(solution)/shard_map/ppermute | solution.py:29
  95.0 5.9 %collective-permute-done.21.refs_2_ = bf16[32,2304]{1,0:T(8,128)(2,1)S(1)} collective-permute-done((bf16[32,2304]{1,0:T(8,128)(2,1)S(1)}, bf16[32,2304]{1,0:T(8,128)(2,1)S(1)}, u32[]{:S(2)}, u32[]{:S(2)}) %collective-permute-start.21) | collective-permute-done | bytes 147488 | tf_op jit(solution)/shard_map/ppermute | solution.py:29
  100.9 1.0 collective-permute-done.18
  102.0 3.3 %collective-permute-done.19 = bf16[32,2304]{1,0:T(8,128)(2,1)S(1)} collective-permute-done((bf16[32,2304]{1,0:T(8,128)(2,1)S(1)}, bf16[32,2304]{1,0:T(8,128)(2,1)S(1)}, u32[]{:S(2)}, u32[]{:S(2)}) %collective-permute-start.19) | collective-permute-done | bytes 147488 | tf_op jit(solution)/shard_map/ppermute | solution.py:29
  105.4 1.2 collective-permute-done.20.refs_1_
  106.7 1.9 %collective-permute-done.22.refs_3_ = bf16[32,2304]{1,0:T(8,128)(2,1)S(1)} collective-permute-done((bf16[32,2304]{1,0:T(8,128)(2,1)S(1)}, bf16[32,2304]{1,0:T(8,128)(2,1)S(1)}, u32[]{:S(2)}, u32[]{:S(2)}) %collective-permute-start.22) | collective-permute-done | bytes 147488 | tf_op jit(solution)/shard_map/ppermute | solution.py:29
  109.7 3.5 %collective-permute-start.28 = (bf16[32,2304]{1,0:T(8,128)(2,1)S(1)}, bf16[32,2304]{1,0:T(8,128)(2,1)S(1)}, u32[]{:S(2)}, u32[]{:S(2)}) collective-permute-start(bf16[32,2304]{1,0:T(8,128)(2,1)S(1)} %get-tuple-element.142.refs_0_), channel_id=1, source_target_pairs={{0,4},{1,5},{2,6},{3,7},{4,0},{5,1},{6,2},{7,3},{8,12},{9,13},{10,... | collective-permute-start | bytes 442376 | tf_op jit(solution)/shard_map/ppermute | solution.py:29
  114.0 11.8 %gradient.2 = (bf16[2,64,1024]{2,1,0:T(8,128)(2,1)S(1)}, bf16[2,64,1024]{2,1,0:T(8,128)(2,1)S(1)}, f32[2,64,1024]{2,1,0:T(8,128)S(1)}, f32[2,64,1024]{2,1,0:T(8,...) custom-call(s32[17]{0:T(128)S(1)} %copy-done.4, ...), custom_call_target="tpu_custom_call" | custom-call | flops 1048576 | bytes 1024 | tf_op jit(solution)/shard_map/gradient/pallas_call | solution.py:102
  125.8 1.5 collective-permute-start.35
  128.5 5.3 %collective-permute-done.35 = bf16[2,64,1024]{2,1,0:T(8,128)(2,1)S(1)} collective-permute-done((bf16[2,64,1024]{2,1,0:T(8,128)(2,1)S(1)}, bf16[2,64,1024]{2,1,0:T(8,128)(2,1)S(1)}, u32[]{:S(2)}, u32[]{:S(2)}) %collective-permute-start.35) | collective-permute-done | bytes 262176 | tf_op jit(solution)/shard_map/ppermute | solution.py:29
  133.7 1.4 collective-permute-start.38
  136.0 1.5 collective-permute-start.40
  138.0 1.4 collective-permute-done.33.refs_7_
  139.4 11.8 %gradient.3 = (bf16[2,64,1024]{2,1,0:T(8,128)(2,1)S(1)}, bf16[2,64,1024]{2,1,0:T(8,128)(2,1)S(1)}, f32[2,64,1024]{2,1,0:T(8,128)S(1)}, f32[2,64,1024]{2,1,0:T(8,...) custom-call(s32[17]{0:T(128)S(1)} %copy-done.4, ...), custom_call_target="tpu_custom_call" | custom-call | flops 1048576 | bytes 1024 | tf_op jit(solution)/shard_map/gradient/pallas_call | solution.py:102
  151.2 1.5 collective-permute-start.42
  154.6 1.5 collective-permute-start.36
  156.1 4.8 %collective-permute-done.36 = f32[8,128]{1,0:T(8,128)S(1)} collective-permute-done((f32[8,128]{1,0:T(8,128)S(1)}, f32[8,128]{1,0:T(8,128)S(1)}, u32[]{:S(2)}, u32[]{:S(2)}) %collective-permute-start.36) | collective-permute-done | bytes 4128 | tf_op jit(solution)/shard_map/ppermute | solution.py:29
  163.0 1.3 collective-permute-start.47
  164.4 1.5 collective-permute-start.46
  167.2 7.3 %collective-permute-done.43 = f32[8,128]{1,0:T(8,128)S(1)} collective-permute-done((f32[8,128]{1,0:T(8,128)S(1)}, f32[8,128]{1,0:T(8,128)S(1)}, u32[]{:S(2)}, u32[]{:S(2)}) %collective-permute-start.43) | collective-permute-done | bytes 4128 | tf_op jit(solution)/shard_map/ppermute | solution.py:29
  175.7 1.3 finish.2.refs_6_
  177.0 1.3 finish.3
  (115 shorter events, 16.2 us)
Async XLA Ops:
  7.7 12.1 %collective-permute-start = (bf16[128,1024]{1,0:T(8,128)(2,1)}, bf16[128,1024]{1,0:T(8,128)(2,1)S(1)}, u32[]{:S(2)}, u32[]{:S(2)}) collective-permute-start(bf16[128,1024]{1,0:T(8,128)(2,1)} %get-tuple-element.97.refs_0_), channel_id=1, source_target_pairs={{0,8},{8,0},{16,24},{24,16},{1,9},{9,1},{17,25},{25,17},{2,10},{10... | collective-permute-start | bytes 786440 | tf_op jit(solution)/shard_map/ppermute | solution.py:29
  10.7 9.4 %collective-permute-start.4 = (bf16[128,1024]{1,0:T(8,128)(2,1)}, bf16[128,1024]{1,0:T(8,128)(2,1)S(1)}, u32[]{:S(2)}, u32[]{:S(2)}) collective-permute-start(bf16[128,1024]{1,0:T(8,128)(2,1)} %get-tuple-element.101.refs_1_.refs_4_), channel_id=1, source_target_pairs={{0,16},{8,24},{16,0},{24,8},{1,17},{9,25},{17,1},{25,9},{2,18},{10... | collective-permute-start | bytes 786440 | tf_op jit(solution)/shard_map/ppermute | solution.py:29
  12.2 13.5 %collective-permute-start.1 = (bf16[128,1024]{1,0:T(8,128)(2,1)}, bf16[128,1024]{1,0:T(8,128)(2,1)S(1)}, u32[]{:S(2)}, u32[]{:S(2)}) collective-permute-start(bf16[128,1024]{1,0:T(8,128)(2,1)} %get-tuple-element.97.refs_0_), channel_id=1, source_target_pairs={{0,16},{8,24},{16,0},{24,8},{1,17},{9,25},{17,1},{25,9},{2,18},{10... | collective-permute-start | bytes 786440 | tf_op jit(solution)/shard_map/ppermute | solution.py:29
  12.7 13.1 %collective-permute-start.3 = (bf16[128,1024]{1,0:T(8,128)(2,1)}, bf16[128,1024]{1,0:T(8,128)(2,1)S(1)}, u32[]{:S(2)}, u32[]{:S(2)}) collective-permute-start(bf16[128,1024]{1,0:T(8,128)(2,1)} %get-tuple-element.101.refs_1_.refs_4_), channel_id=1, source_target_pairs={{0,8},{8,0},{16,24},{24,16},{1,9},{9,1},{17,25},{25,17},{2,10},{10... | collective-permute-start | bytes 786440 | tf_op jit(solution)/shard_map/ppermute | solution.py:29
  20.2 11.2 %collective-permute-start.10 = (bf16[128,1024]{1,0:T(8,128)(2,1)}, bf16[128,1024]{1,0:T(8,128)(2,1)S(1)}, u32[]{:S(2)}, u32[]{:S(2)}) collective-permute-start(bf16[128,1024]{1,0:T(8,128)(2,1)} %get-tuple-element.109.refs_3_.refs_12_), channel_id=1, source_target_pairs={{0,16},{8,24},{16,0},{24,8},{1,17},{9,25},{17,1},{25,9},{2,18},{10... | collective-permute-start | bytes 786440 | tf_op jit(solution)/shard_map/ppermute | solution.py:29
  21.8 15.2 %collective-permute-start.2 = (bf16[128,1024]{1,0:T(8,128)(2,1)S(1)}, bf16[128,1024]{1,0:T(8,128)(2,1)S(1)}, u32[]{:S(2)}, u32[]{:S(2)}) collective-permute-start(bf16[128,1024]{1,0:T(8,128)(2,1)S(1)} %collective-permute-done.refs_1_), channel_id=1, source_target_pairs={{0,16},{8,24},{16,0},{24,8},{1,17},{9,25},{17,1},{25,9},{2,18},{10... | collective-permute-start | bytes 786440 | tf_op jit(solution)/shard_map/ppermute | solution.py:29
  22.2 14.8 %collective-permute-start.5 = (bf16[128,1024]{1,0:T(8,128)(2,1)S(1)}, bf16[128,1024]{1,0:T(8,128)(2,1)S(1)}, u32[]{:S(2)}, u32[]{:S(2)}) collective-permute-start(bf16[128,1024]{1,0:T(8,128)(2,1)S(1)} %collective-permute-done.4.refs_6_), channel_id=1, source_target_pairs={{0,8},{8,0},{16,24},{24,16},{1,9},{9,1},{17,25},{25,17},{2,10},{10... | collective-permute-start | bytes 786440 | tf_op jit(solution)/shard_map/ppermute | solution.py:29
  25.8 11.4 %collective-permute-start.6 = (bf16[128,1024]{1,0:T(8,128)(2,1)}, bf16[128,1024]{1,0:T(8,128)(2,1)S(1)}, u32[]{:S(2)}, u32[]{:S(2)}) collective-permute-start(bf16[128,1024]{1,0:T(8,128)(2,1)} %get-tuple-element.105.refs_2_.refs_8_), channel_id=1, source_target_pairs={{0,8},{8,0},{16,24},{24,16},{1,9},{9,1},{17,25},{25,17},{2,10},{10... | collective-permute-start | bytes 786440 | tf_op jit(solution)/shard_map/ppermute | solution.py:29
  25.8 17.6 %collective-permute-start.7 = (bf16[128,1024]{1,0:T(8,128)(2,1)}, bf16[128,1024]{1,0:T(8,128)(2,1)S(1)}, u32[]{:S(2)}, u32[]{:S(2)}) collective-permute-start(bf16[128,1024]{1,0:T(8,128)(2,1)} %get-tuple-element.105.refs_2_.refs_8_), channel_id=1, source_target_pairs={{0,16},{8,24},{16,0},{24,8},{1,17},{9,25},{17,1},{25,9},{2,18},{10... | collective-permute-start | bytes 786440 | tf_op jit(solution)/shard_map/ppermute | solution.py:29
  31.4 12.1 %collective-permute-start.9 = (bf16[128,1024]{1,0:T(8,128)(2,1)}, bf16[128,1024]{1,0:T(8,128)(2,1)S(1)}, u32[]{:S(2)}, u32[]{:S(2)}) collective-permute-start(bf16[128,1024]{1,0:T(8,128)(2,1)} %get-tuple-element.109.refs_3_.refs_12_), channel_id=1, source_target_pairs={{0,8},{8,0},{16,24},{24,16},{1,9},{9,1},{17,25},{25,17},{2,10},{10... | collective-permute-start | bytes 786440 | tf_op jit(solution)/shard_map/ppermute | solution.py:29
  37.0 8.4 %collective-permute-start.11 = (bf16[128,1024]{1,0:T(8,128)(2,1)S(1)}, bf16[128,1024]{1,0:T(8,128)(2,1)S(1)}, u32[]{:S(2)}, u32[]{:S(2)}) collective-permute-start(bf16[128,1024]{1,0:T(8,128)(2,1)S(1)} %collective-permute-done.10.refs_14_), channel_id=1, source_target_pairs={{0,8},{8,0},{16,24},{24,16},{1,9},{9,1},{17,25},{25,17},{2,10},{10... | collective-permute-start | bytes 786440 | tf_op jit(solution)/shard_map/ppermute | solution.py:29
  37.1 9.7 %collective-permute-start.8 = (bf16[128,1024]{1,0:T(8,128)(2,1)S(1)}, bf16[128,1024]{1,0:T(8,128)(2,1)}, u32[]{:S(2)}, u32[]{:S(2)}) collective-permute-start(bf16[128,1024]{1,0:T(8,128)(2,1)S(1)} %collective-permute-done.6.refs_9_), channel_id=1, source_target_pairs={{0,16},{8,24},{16,0},{24,8},{1,17},{9,25},{17,1},{25,9},{2,18},{10... | collective-permute-start | bytes 786440 | tf_op jit(solution)/shard_map/ppermute | solution.py:29
  64.7 2.3 %collective-permute-start.12 = (bf16[128,2304]{1,0:T(8,128)(2,1)}, bf16[128,2304]{1,0:T(8,128)(2,1)S(1)}, u32[]{:S(2)}, u32[]{:S(2)}) collective-permute-start(bf16[128,2304]{1,0:T(8,128)(2,1)} %get-tuple-element.114), channel_id=1, source_target_pairs={{0,1},{1,0},{2,3},{3,2},{4,5},{5,4},{6,7},{7,6},{8,9},{9,8},{10,11... | collective-permute-start | bytes 1769480 | tf_op jit(solution)/shard_map/ppermute | solution.py:29
  67.8 3.4 %collective-permute-start.14 = (bf16[128,2304]{1,0:T(8,128)(2,1)}, bf16[128,2304]{1,0:T(8,128)(2,1)S(1)}, u32[]{:S(2)}, u32[]{:S(2)}) collective-permute-start(bf16[128,2304]{1,0:T(8,128)(2,1)} %get-tuple-element.117), channel_id=1, source_target_pairs={{0,1},{1,0},{2,3},{3,2},{4,5},{5,4},{6,7},{7,6},{8,9},{9,8},{10,11... | collective-permute-start | bytes 1769480 | tf_op jit(solution)/shard_map/ppermute | solution.py:29
  69.1 10.9 %collective-permute-start.13 = (bf16[32,2304]{1,0:T(8,128)(2,1)S(1)}, bf16[32,2304]{1,0:T(8,128)(2,1)S(1)}, u32[]{:S(2)}, u32[]{:S(2)}) collective-permute-start(bf16[32,2304]{1,0:T(8,128)(2,1)S(1)} %get-tuple-element.176), channel_id=1, source_target_pairs={{0,2},{1,3},{2,0},{3,1},{4,6},{5,7},{6,4},{7,5},{8,10},{9,11},{10,... | collective-permute-start | bytes 442376 | tf_op jit(solution)/shard_map/ppermute | solution.py:29
  70.7 8.3 %collective-permute-start.15 = (bf16[32,2304]{1,0:T(8,128)(2,1)S(1)}, bf16[32,2304]{1,0:T(8,128)(2,1)S(1)}, u32[]{:S(2)}, u32[]{:S(2)}) collective-permute-start(bf16[32,2304]{1,0:T(8,128)(2,1)S(1)} %get-tuple-element.177), channel_id=1, source_target_pairs={{0,2},{1,3},{2,0},{3,1},{4,6},{5,7},{6,4},{7,5},{8,10},{9,11},{10,... | collective-permute-start | bytes 442376 | tf_op jit(solution)/shard_map/ppermute | solution.py:29
  72.4 10.3 %collective-permute-start.17 = (bf16[32,2304]{1,0:T(8,128)(2,1)S(1)}, bf16[32,2304]{1,0:T(8,128)(2,1)S(1)}, u32[]{:S(2)}, u32[]{:S(2)}) collective-permute-start(bf16[32,2304]{1,0:T(8,128)(2,1)S(1)} %get-tuple-element.118), channel_id=1, source_target_pairs={{0,2},{1,3},{2,0},{3,1},{4,6},{5,7},{6,4},{7,5},{8,10},{9,11},{10,... | collective-permute-start | bytes 442376 | tf_op jit(solution)/shard_map/ppermute | solution.py:29
  80.0 8.9 %collective-permute-start.16 = (bf16[32,2304]{1,0:T(8,128)(2,1)S(1)}, bf16[32,2304]{1,0:T(8,128)(2,1)S(1)}, u32[]{:S(2)}, u32[]{:S(2)}) collective-permute-start(bf16[32,2304]{1,0:T(8,128)(2,1)S(1)} %add_convert_fusion.5), channel_id=1, source_target_pairs={{0,4},{1,5},{2,6},{3,7},{4,0},{5,1},{6,2},{7,3},{8,12},{9,13},{10,... | collective-permute-start | bytes 442376 | tf_op jit(solution)/shard_map/ppermute | solution.py:29
  90.0 10.9 %collective-permute-start.21 = (bf16[32,2304]{1,0:T(8,128)(2,1)S(1)}, bf16[32,2304]{1,0:T(8,128)(2,1)S(1)}, u32[]{:S(2)}, u32[]{:S(2)}) collective-permute-start(bf16[32,2304]{1,0:T(8,128)(2,1)S(1)} %get-tuple-element.125.refs_0_), channel_id=1, source_target_pairs={{0,4},{1,5},{2,6},{3,7},{4,0},{5,1},{6,2},{7,3},{8,12},{9,13},{10,... | collective-permute-start | bytes 442376 | tf_op jit(solution)/shard_map/ppermute | solution.py:29
  90.1 11.9 %collective-permute-start.18 = (bf16[32,2304]{1,0:T(8,128)(2,1)S(1)}, bf16[32,2304]{1,0:T(8,128)(2,1)S(1)}, u32[]{:S(2)}, u32[]{:S(2)}) collective-permute-start(bf16[32,2304]{1,0:T(8,128)(2,1)S(1)} %get-tuple-element.119), channel_id=1, source_target_pairs={{0,2},{1,3},{2,0},{3,1},{4,6},{5,7},{6,4},{7,5},{8,10},{9,11},{10,... | collective-permute-start | bytes 442376 | tf_op jit(solution)/shard_map/ppermute | solution.py:29
  94.1 11.2 %collective-permute-start.19 = (bf16[32,2304]{1,0:T(8,128)(2,1)S(1)}, bf16[32,2304]{1,0:T(8,128)(2,1)S(1)}, u32[]{:S(2)}, u32[]{:S(2)}) collective-permute-start(bf16[32,2304]{1,0:T(8,128)(2,1)S(1)} %add_convert_fusion.4), channel_id=1, source_target_pairs={{0,4},{1,5},{2,6},{3,7},{4,0},{5,1},{6,2},{7,3},{8,12},{9,13},{10,... | collective-permute-start | bytes 442376 | tf_op jit(solution)/shard_map/ppermute | solution.py:29
  94.2 12.5 %collective-permute-start.20 = (bf16[32,2304]{1,0:T(8,128)(2,1)S(1)}, bf16[32,2304]{1,0:T(8,128)(2,1)S(1)}, u32[]{:S(2)}, u32[]{:S(2)}) collective-permute-start(bf16[32,2304]{1,0:T(8,128)(2,1)S(1)} %get-tuple-element.125.refs_0_), channel_id=1, source_target_pairs={{0,2},{1,3},{2,0},{3,1},{4,6},{5,7},{6,4},{7,5},{8,10},{9,11},{10,... | collective-permute-start | bytes 442376 | tf_op jit(solution)/shard_map/ppermute | solution.py:29
  95.0 14.7 %collective-permute-start.23 = (bf16[32,2304]{1,0:T(8,128)(2,1)S(1)}, bf16[32,2304]{1,0:T(8,128)(2,1)S(1)}, u32[]{:S(2)}, u32[]{:S(2)}) collective-permute-start(bf16[32,2304]{1,0:T(8,128)(2,1)S(1)} %get-tuple-element.125.refs_0_), channel_id=1, source_target_pairs={{0,1},{1,0},{2,3},{3,2},{4,5},{5,4},{6,7},{7,6},{8,9},{9,8},{10,11... | collective-permute-start | bytes 442376 | tf_op jit(solution)/shard_map/ppermute | solution.py:29
  100.9 7.6 %collective-permute-start.22 = (bf16[32,2304]{1,0:T(8,128)(2,1)S(1)}, bf16[32,2304]{1,0:T(8,128)(2,1)S(1)}, u32[]{:S(2)}, u32[]{:S(2)}) collective-permute-start(bf16[32,2304]{1,0:T(8,128)(2,1)S(1)} %collective-permute-done.21.refs_2_), channel_id=1, source_target_pairs={{0,2},{1,3},{2,0},{3,1},{4,6},{5,7},{6,4},{7,5},{8,10},{9,11},{10,... | collective-permute-start | bytes 442376 | tf_op jit(solution)/shard_map/ppermute | solution.py:29
  105.3 8.6 %collective-permute-start.25 = (bf16[32,2304]{1,0:T(8,128)(2,1)S(1)}, bf16[32,2304]{1,0:T(8,128)(2,1)S(1)}, u32[]{:S(2)}, u32[]{:S(2)}) collective-permute-start(bf16[32,2304]{1,0:T(8,128)(2,1)S(1)} %collective-permute-done.21.refs_2_), channel_id=1, source_target_pairs={{0,1},{1,0},{2,3},{3,2},{4,5},{5,4},{6,7},{7,6},{8,9},{9,8},{10,11... | collective-permute-start | bytes 442376 | tf_op jit(solution)/shard_map/ppermute | solution.py:29
  106.6 6.6 %collective-permute-start.24 = (bf16[32,2304]{1,0:T(8,128)(2,1)S(1)}, bf16[32,2304]{1,0:T(8,128)(2,1)S(1)}, u32[]{:S(2)}, u32[]{:S(2)}) collective-permute-start(bf16[32,2304]{1,0:T(8,128)(2,1)S(1)} %collective-permute-done.20.refs_1_), channel_id=1, source_target_pairs={{0,1},{1,0},{2,3},{3,2},{4,5},{5,4},{6,7},{7,6},{8,9},{9,8},{10,11... | collective-permute-start | bytes 442376 | tf_op jit(solution)/shard_map/ppermute | solution.py:29
  108.6 5.4 %collective-permute-start.26 = (bf16[32,2304]{1,0:T(8,128)(2,1)S(1)}, bf16[32,2304]{1,0:T(8,128)(2,1)S(1)}, u32[]{:S(2)}, u32[]{:S(2)}) collective-permute-start(bf16[32,2304]{1,0:T(8,128)(2,1)S(1)} %collective-permute-done.22.refs_3_), channel_id=1, source_target_pairs={{0,1},{1,0},{2,3},{3,2},{4,5},{5,4},{6,7},{7,6},{8,9},{9,8},{10,11... | collective-permute-start | bytes 442376 | tf_op jit(solution)/shard_map/ppermute | solution.py:29
  109.5 16.3 %collective-permute-start.27 = (bf16[32,2304]{1,0:T(8,128)(2,1)S(1)}, bf16[32,2304]{1,0:T(8,128)(2,1)S(1)}, u32[]{:S(2)}, u32[]{:S(2)}) collective-permute-start(bf16[32,2304]{1,0:T(8,128)(2,1)S(1)} %get-tuple-element.142.refs_0_), channel_id=1, source_target_pairs={{0,2},{1,3},{2,0},{3,1},{4,6},{5,7},{6,4},{7,5},{8,10},{9,11},{10,... | collective-permute-start | bytes 442376 | tf_op jit(solution)/shard_map/ppermute | solution.py:29
  109.7 16.0 %collective-permute-start.28 = (bf16[32,2304]{1,0:T(8,128)(2,1)S(1)}, bf16[32,2304]{1,0:T(8,128)(2,1)S(1)}, u32[]{:S(2)}, u32[]{:S(2)}) collective-permute-start(bf16[32,2304]{1,0:T(8,128)(2,1)S(1)} %get-tuple-element.142.refs_0_), channel_id=1, source_target_pairs={{0,4},{1,5},{2,6},{3,7},{4,0},{5,1},{6,2},{7,3},{8,12},{9,13},{10,... | collective-permute-start | bytes 442376 | tf_op jit(solution)/shard_map/ppermute | solution.py:29
  113.3 12.5 %collective-permute-start.29 = (bf16[32,2304]{1,0:T(8,128)(2,1)S(1)}, bf16[32,2304]{1,0:T(8,128)(2,1)S(1)}, u32[]{:S(2)}, u32[]{:S(2)}) collective-permute-start(bf16[32,2304]{1,0:T(8,128)(2,1)S(1)} %get-tuple-element.142.refs_0_), channel_id=1, source_target_pairs={{0,6},{1,7},{2,4},{3,5},{4,2},{5,3},{6,0},{7,1},{8,14},{9,15},{10,... | collective-permute-start | bytes 442376 | tf_op jit(solution)/shard_map/ppermute | solution.py:29
  125.8 7.9 %collective-permute-start.35 = (bf16[2,64,1024]{2,1,0:T(8,128)(2,1)S(1)}, bf16[2,64,1024]{2,1,0:T(8,128)(2,1)S(1)}, u32[]{:S(2)}, u32[]{:S(2)}) collective-permute-start(bf16[2,64,1024]{2,1,0:T(8,128)(2,1)S(1)} %get-tuple-element.141), channel_id=1, source_target_pairs={{0,16},{8,24},{16,0},{24,8},{1,17},{9,25},{17,1},{25,9},{2,18},{10... | collective-permute-start | bytes 786440 | tf_op jit(solution)/shard_map/ppermute | solution.py:29
  127.3 7.9 %collective-permute-start.34 = (bf16[2,64,1024]{2,1,0:T(8,128)(2,1)S(1)}, bf16[2,64,1024]{2,1,0:T(8,128)(2,1)S(1)}, u32[]{:S(2)}, u32[]{:S(2)}) collective-permute-start(bf16[2,64,1024]{2,1,0:T(8,128)(2,1)S(1)} %get-tuple-element.137), channel_id=1, source_target_pairs={{0,8},{8,0},{16,24},{24,16},{1,9},{9,1},{17,25},{25,17},{2,10},{10... | collective-permute-start | bytes 786440 | tf_op jit(solution)/shard_map/ppermute | solution.py:29
  127.9 8.0 %collective-permute-start.30 = (bf16[32,2304]{1,0:T(8,128)(2,1)S(1)}, bf16[32,2304]{1,0:T(8,128)(2,1)S(1)}, u32[]{:S(2)}, u32[]{:S(2)}) collective-permute-start(bf16[32,2304]{1,0:T(8,128)(2,1)S(1)} %get-tuple-element.142.refs_0_), channel_id=1, source_target_pairs={{0,1},{1,0},{2,3},{3,2},{4,5},{5,4},{6,7},{7,6},{8,9},{9,8},{10,11... | collective-permute-start | bytes 442376 | tf_op jit(solution)/shard_map/ppermute | solution.py:29
  128.0 9.5 %collective-permute-start.31 = (bf16[32,2304]{1,0:T(8,128)(2,1)S(1)}, bf16[32,2304]{1,0:T(8,128)(2,1)S(1)}, u32[]{:S(2)}, u32[]{:S(2)}) collective-permute-start(bf16[32,2304]{1,0:T(8,128)(2,1)S(1)} %collective-permute-done.27.refs_1_), channel_id=1, source_target_pairs={{0,1},{1,0},{2,3},{3,2},{4,5},{5,4},{6,7},{7,6},{8,9},{9,8},{10,11... | collective-permute-start | bytes 442376 | tf_op jit(solution)/shard_map/ppermute | solution.py:29
  128.5 9.5 %collective-permute-start.32 = (bf16[32,2304]{1,0:T(8,128)(2,1)S(1)}, bf16[32,2304]{1,0:T(8,128)(2,1)S(1)}, u32[]{:S(2)}, u32[]{:S(2)}) collective-permute-start(bf16[32,2304]{1,0:T(8,128)(2,1)S(1)} %collective-permute-done.28.refs_2_), channel_id=1, source_target_pairs={{0,1},{1,0},{2,3},{3,2},{4,5},{5,4},{6,7},{7,6},{8,9},{9,8},{10,11... | collective-permute-start | bytes 442376 | tf_op jit(solution)/shard_map/ppermute | solution.py:29
  133.7 17.4 %collective-permute-start.38 = (bf16[2,64,1024]{2,1,0:T(8,128)(2,1)S(1)}, bf16[2,64,1024]{2,1,0:T(8,128)(2,1)S(1)}, u32[]{:S(2)}, u32[]{:S(2)}) collective-permute-start(bf16[2,64,1024]{2,1,0:T(8,128)(2,1)S(1)} %get-tuple-element.157), channel_id=1, source_target_pairs={{0,16},{8,24},{16,0},{24,8},{1,17},{9,25},{17,1},{25,9},{2,18},{10... | collective-permute-start | bytes 786440 | tf_op jit(solution)/shard_map/ppermute | solution.py:29
  135.2 16.0 %collective-permute-start.37 = (bf16[2,64,1024]{2,1,0:T(8,128)(2,1)S(1)}, bf16[2,64,1024]{2,1,0:T(8,128)(2,1)S(1)}, u32[]{:S(2)}, u32[]{:S(2)}) collective-permute-start(bf16[2,64,1024]{2,1,0:T(8,128)(2,1)S(1)} %get-tuple-element.155), channel_id=1, source_target_pairs={{0,8},{8,0},{16,24},{24,16},{1,9},{9,1},{17,25},{25,17},{2,10},{10... | collective-permute-start | bytes 786440 | tf_op jit(solution)/shard_map/ppermute | solution.py:29
  136.0 15.2 %collective-permute-start.40 = (bf16[2,64,1024]{2,1,0:T(8,128)(2,1)S(1)}, bf16[2,64,1024]{2,1,0:T(8,128)(2,1)S(1)}, u32[]{:S(2)}, u32[]{:S(2)}) collective-permute-start(bf16[2,64,1024]{2,1,0:T(8,128)(2,1)S(1)} %add_convert_fusion.2), channel_id=1, source_target_pairs={{0,8},{8,0},{16,24},{24,16},{1,9},{9,1},{17,25},{25,17},{2,10},{10... | collective-permute-start | bytes 786440 | tf_op jit(solution)/shard_map/ppermute | solution.py:29
  137.4 13.8 %collective-permute-start.39 = (bf16[2,64,1024]{2,1,0:T(8,128)(2,1)S(1)}, bf16[2,64,1024]{2,1,0:T(8,128)(2,1)S(1)}, u32[]{:S(2)}, u32[]{:S(2)}) collective-permute-start(bf16[2,64,1024]{2,1,0:T(8,128)(2,1)S(1)} %add_convert_fusion.3), channel_id=1, source_target_pairs={{0,16},{8,24},{16,0},{24,8},{1,17},{9,25},{17,1},{25,9},{2,18},{10... | collective-permute-start | bytes 786440 | tf_op jit(solution)/shard_map/ppermute | solution.py:29
  138.0 1.4 collective-permute-start.33
  151.2 10.3 %collective-permute-start.42 = (bf16[2,64,1024]{2,1,0:T(8,128)(2,1)S(1)}, bf16[2,64,1024]{2,1,0:T(8,128)(2,1)S(1)}, u32[]{:S(2)}, u32[]{:S(2)}) collective-permute-start(bf16[2,64,1024]{2,1,0:T(8,128)(2,1)S(1)} %get-tuple-element.162), channel_id=1, source_target_pairs={{0,16},{8,24},{16,0},{24,8},{1,17},{9,25},{17,1},{25,9},{2,18},{10... | collective-permute-start | bytes 786440 | tf_op jit(solution)/shard_map/ppermute | solution.py:29
  152.7 9.5 %collective-permute-start.41 = (bf16[2,64,1024]{2,1,0:T(8,128)(2,1)S(1)}, bf16[2,64,1024]{2,1,0:T(8,128)(2,1)S(1)}, u32[]{:S(2)}, u32[]{:S(2)}) collective-permute-start(bf16[2,64,1024]{2,1,0:T(8,128)(2,1)S(1)} %get-tuple-element.158), channel_id=1, source_target_pairs={{0,8},{8,0},{16,24},{24,16},{1,9},{9,1},{17,25},{25,17},{2,10},{10... | collective-permute-start | bytes 786440 | tf_op jit(solution)/shard_map/ppermute | solution.py:29
  154.6 6.3 %collective-permute-start.36 = (f32[8,128]{1,0:T(8,128)S(1)}, f32[8,128]{1,0:T(8,128)S(1)}, u32[]{:S(2)}, u32[]{:S(2)}) collective-permute-start(f32[8,128]{1,0:T(8,128)S(1)} %broadcast_in_dim.11), channel_id=1, source_target_pairs={{0,8},{8,0},{16,24},{24,16},{1,9},{9,1},{17,25},{25,17},{2,10},{10... | collective-permute-start | bytes 12296 | tf_op jit(solution)/shard_map/ppermute | solution.py:29
  161.5 14.2 %collective-permute-start.45 = (bf16[2,64,1024]{2,1,0:T(8,128)(2,1)S(1)}, bf16[2,64,1024]{2,1,0:T(8,128)(2,1)S(1)}, u32[]{:S(2)}, u32[]{:S(2)}) collective-permute-start(bf16[2,64,1024]{2,1,0:T(8,128)(2,1)S(1)} %get-tuple-element.169), channel_id=1, source_target_pairs={{0,16},{8,24},{16,0},{24,8},{1,17},{9,25},{17,1},{25,9},{2,18},{10... | collective-permute-start | bytes 786440 | tf_op jit(solution)/shard_map/ppermute | solution.py:29
  162.2 13.5 %collective-permute-start.44 = (bf16[2,64,1024]{2,1,0:T(8,128)(2,1)S(1)}, bf16[2,64,1024]{2,1,0:T(8,128)(2,1)S(1)}, u32[]{:S(2)}, u32[]{:S(2)}) collective-permute-start(bf16[2,64,1024]{2,1,0:T(8,128)(2,1)S(1)} %get-tuple-element.167), channel_id=1, source_target_pairs={{0,8},{8,0},{16,24},{24,16},{1,9},{9,1},{17,25},{25,17},{2,10},{10... | collective-permute-start | bytes 786440 | tf_op jit(solution)/shard_map/ppermute | solution.py:29
  163.0 14.0 %collective-permute-start.47 = (bf16[2,64,1024]{2,1,0:T(8,128)(2,1)S(1)}, bf16[2,64,1024]{2,1,0:T(8,128)(2,1)S(1)}, u32[]{:S(2)}, u32[]{:S(2)}) collective-permute-start(bf16[2,64,1024]{2,1,0:T(8,128)(2,1)S(1)} %add_convert_fusion), channel_id=1, source_target_pairs={{0,8},{8,0},{16,24},{24,16},{1,9},{9,1},{17,25},{25,17},{2,10},{10... | collective-permute-start | bytes 786440 | tf_op jit(solution)/shard_map/ppermute | solution.py:29
  164.4 12.6 %collective-permute-start.46 = (bf16[2,64,1024]{2,1,0:T(8,128)(2,1)S(1)}, bf16[2,64,1024]{2,1,0:T(8,128)(2,1)S(1)}, u32[]{:S(2)}, u32[]{:S(2)}) collective-permute-start(bf16[2,64,1024]{2,1,0:T(8,128)(2,1)S(1)} %add_convert_fusion.1), channel_id=1, source_target_pairs={{0,16},{8,24},{16,0},{24,8},{1,17},{9,25},{17,1},{25,9},{2,18},{10... | collective-permute-start | bytes 786440 | tf_op jit(solution)/shard_map/ppermute | solution.py:29
  165.9 8.6 %collective-permute-start.43 = (f32[8,128]{1,0:T(8,128)S(1)}, f32[8,128]{1,0:T(8,128)S(1)}, u32[]{:S(2)}, u32[]{:S(2)}) collective-permute-start(f32[8,128]{1,0:T(8,128)S(1)} %broadcast_add_fusion), channel_id=1, source_target_pairs={{0,16},{8,24},{16,0},{24,8},{1,17},{9,25},{17,1},{25,9},{2,18},{10... | collective-permute-start | bytes 12296 | tf_op jit(solution)/shard_map/ppermute | solution.py:29
  (20 other events, 312.9 us)

commit v10 on v8

--- a/solution.py
+++ b/solution.py
@@ -12,6 +12,7 @@
 WANTED_CHUNKS = 2
 ROW_TILE = 16
 WEIGHT_SLOTS = 4
+IN_FLIGHT = 3
 VMEM_BYTES = 44 << 20
 MOST_VMEM_BYTES = 59 << 20
 SMALL_COST = pl.CostEstimate(flops=1 << 20, bytes_accessed=1 << 10, transcendentals=0)
@@ -66,7 +67,7 @@
 
 
 def streamed(count, slots, copies_of, body):
-    early = min(1, slots - 1, count)
+    early = min(2, slots - 1, count)
     for i in range(early):
         for copy in copies_of(i, i):
             copy.start()
@@ -112,54 +113,60 @@
 
 
 def encode_kernel(plan, lo, hi, resid_ref, w_ref, b_ref, *refs):
-    outs, (x_buf, w_buf, b_buf, x_sem, w_sem) = refs[:hi - lo], refs[hi - lo:]
-    tile = w_buf.shape[2]
-    steps = plan.width // tile
+    outs, (x_buf, w_buf, b_buf, total, x_sem, w_sem) = refs[:hi - lo], refs[hi - lo:]
+    steps = w_sem.shape[0] // (hi - lo)
+    depth = plan.model // steps
     near = [
         pltpu.make_async_copy(resid_ref.at[pl.ds(lo, hi - lo)], x_buf, x_sem.at[0]),
         pltpu.make_async_copy(b_ref, b_buf, x_sem.at[1]),
     ]
-    for copy in near:
+    copies = [
+        pltpu.make_async_copy(
+            w_ref.at[lo + s, pl.ds(i * depth, depth)],
+            w_buf.at[s, pl.ds(i * depth, depth)],
+            w_sem.at[s * steps + i],
+        )
+        for s in range(hi - lo)
+        for i in range(steps)
+    ]
+    near[0].start()
+    for copy in copies[:IN_FLIGHT]:
         copy.start()
-
-    def copies_of(i, slot):
-        cols = pl.ds(pl.multiple_of(lax.rem(i, steps) * tile, tile), tile)
-        return [pltpu.make_async_copy(
-            w_ref.at[lo + lax.div(i, steps), :, cols], w_buf.at[slot], w_sem.at[slot]
-        )]
-
-    def step(i, slot):
-        @pl.when(i == 0)
-        def _():
-            for copy in near:
-                copy.wait()
-
-        source = lax.div(i, steps)
-        cols = pl.ds(pl.multiple_of(lax.rem(i, steps) * tile, tile), tile)
-        product = jnp.dot(x_buf[source], w_buf[slot], preferred_element_type=F32)
-        bias = b_buf[pl.ds(lo + source, 1), cols]
-        value = jnp.maximum(product + bias, 0.0).astype(BF16)
-        for s in range(hi - lo):
-            @pl.when(source == s)
-            def _():
-                outs[s][:, cols] = value
-
-    streamed((hi - lo) * steps, w_buf.shape[0], copies_of, step)
+    near[1].start()
+    near[0].wait()
+    for s in range(hi - lo):
+        for i in range(steps):
+            step = s * steps + i
+            copies[step].wait()
+            for copy in copies[step + IN_FLIGHT:step + IN_FLIGHT + 1]:
+                copy.start()
+            part = slice(i * depth, (i + 1) * depth)
+            product = jnp.dot(x_buf[s, :, part], w_buf[s, part, :], preferred_element_type=F32)
+            if i:
+                product = total[...] + product
+            if i < steps - 1:
+                total[...] = product
+        if not s:
+            near[1].wait()
+        value = jnp.maximum(product + b_buf[lo + s:lo + s + 1, :], 0.0)
+        outs[s][...] = value.astype(BF16)
 
 
 def encode(plan, lo, hi, resid, w_enc, b_enc):
-    tile = pick_tile(plan.width, 256)
+    n = hi - lo
+    steps = plan.model // pick_tile(plan.model, 768)
     return call(
         partial(encode_kernel, plan, lo, hi),
         "encode",
         [FAR, FAR, FAR],
-        [jax.ShapeDtypeStruct((plan.rows, plan.width), BF16)] * (hi - lo),
+        [jax.ShapeDtypeStruct((plan.rows, plan.width), BF16)] * n,
         [
-            pltpu.VMEM((hi - lo, plan.rows, plan.model), BF16),
-            pltpu.VMEM((WEIGHT_SLOTS + 1, plan.model, tile), BF16),
+            pltpu.VMEM((n, plan.rows, plan.model), BF16),
+            pltpu.VMEM((n, plan.model, plan.width), BF16),
             pltpu.VMEM((plan.sources, plan.width), F32),
+            pltpu.VMEM((plan.rows, plan.width), F32),
             pltpu.SemaphoreType.DMA((2,)),
-            pltpu.SemaphoreType.DMA((WEIGHT_SLOTS + 1,)),
+            pltpu.SemaphoreType.DMA((n * steps,)),
         ],
         (resid, w_enc, b_enc),
         vmem=MOST_VMEM_BYTES,
@@ -191,95 +198,82 @@
 
 def decode_kernel(plan, index_ref, *refs):
     n_in = plan.groups * plan.sources
-    pieces, w_ref, outs = refs[:n_in], refs[n_in], refs[n_in + 1:-7]
-    x_buf, w_buf, send_buf, keep_buf, x_sem, w_sem, out_sem = refs[-7:]
+    pieces, w_ref, outs = refs[:n_in], refs[n_in], refs[n_in + 1:-5]
+    x_buf, w_buf, total, x_sem, w_sem = refs[-5:]
     half = plan.tokens // 2
     core = index_ref[0]
     tile = w_buf.shape[2]
-    count = plan.model // tile
-
-    placing = []
-    for j in range(plan.groups):
-        for b in range(plan.pairs):
-            place = index_ref[1 + plan.sources + j * plan.pairs + b] * plan.rows_feat
-            for owner in range(2):
-                to = pl.multiple_of(place + jnp.where(core == owner, half, 0), ROW_TILE)
-                for s in range(plan.sources):
-                    placing.append(pltpu.make_async_copy(
+
+    placing = [[] for _ in range(plan.sources)]
+    for s in range(plan.sources):
+        for j in range(plan.groups):
+            for b in range(plan.pairs):
+                place = index_ref[1 + plan.sources + j * plan.pairs + b] * plan.rows_feat
+                for owner in range(2):
+                    to = pl.multiple_of(place + jnp.where(core == owner, half, 0), ROW_TILE)
+                    placing[s].append(pltpu.make_async_copy(
                         pieces[s * plan.groups + j].at[
                             pl.ds((2 * b + owner) * plan.rows_feat, plan.rows_feat)
                         ],
-                        x_buf.at[
-                            pl.ds(to, plan.rows_feat), pl.ds(s * plan.width, plan.width)
-                        ],
-                        x_sem.at[len(placing)],
+                        x_buf.at[s, pl.ds(to, plan.rows_feat)],
+                        x_sem.at[s, len(placing[s])],
                     ))
-    for copy in placing:
-        copy.start()
+    for copies in placing:
+        for copy in copies:
+            copy.start()
 
     def columns(i):
-        return pl.ds(pl.multiple_of(i * tile, tile), tile)
+        return pl.ds(pl.multiple_of(lax.div(i, plan.sources) * tile, tile), tile)
 
     def copies_of(i, slot):
-        return [
-            pltpu.make_async_copy(
-                w_ref.at[s, 0, :, columns(i)],
-                w_buf.at[slot, pl.ds(s * plan.width, plan.width)],
-                w_sem.at[slot, s],
-            )
-            for s in range(plan.sources)
-        ]
-
-    def leaving(i):
-        slot = lax.rem(i, 2)
-        return [
-            pltpu.make_async_copy(
-                buf.at[slot, c],
-                outs[n * plan.chunks + c].at[:, columns(i)],
-                out_sem.at[slot, n * plan.chunks + c],
-            )
-            for n, buf in enumerate((send_buf, keep_buf))
-            for c in range(plan.chunks)
-        ]
+        return [pltpu.make_async_copy(
+            w_ref.at[lax.rem(i, plan.sources), 0, :, columns(i)], w_buf.at[slot], w_sem.at[slot]
+        )]
 
     def step(i, slot):
-        @pl.when(i == 0)
-        def _():
-            for copy in placing:
-                copy.wait()
-            for s in range(plan.sources):
+        source = lax.rem(i, plan.sources)
+        for s in range(plan.sources):
+            @pl.when(i == s)
+            def _(s=s):
+                for copy in placing[s]:
+                    copy.wait()
+
                 @pl.when(index_ref[1 + s] == 0)
-                def _(s=s):
-                    x_buf[:, s * plan.width:(s + 1) * plan.width] = jnp.zeros(
-                        (plan.tokens, plan.width), BF16
+                def _():
+                    x_buf[s] = jnp.zeros(x_buf.shape[1:], BF16)
+
+        product = jnp.dot(x_buf[source], w_buf[slot], preferred_element_type=F32)
+
+        @pl.when(source == 0)
+        def _():
+            total[...] = product
+
+        @pl.when((source > 0) & (source < plan.sources - 1))
+        def _():
+            total[...] = total[...] + product
+
+        @pl.when(source == plan.sources - 1)
+        def _():
+            cols = columns(i)
+            for c in range(plan.chunks):
+                for d in range(plan.depth):
+                    first = d * plan.rows_feat + c * plan.piece
+                    last = half + first
+                    to = slice(d * plan.piece, (d + 1) * plan.piece)
+                    outs[c][to, cols] = (
+                        total[first:first + plan.piece] + product[first:first + plan.piece]
+                    ).astype(BF16)
+                    outs[plan.chunks + c][to, cols] = (
+                        total[last:last + plan.piece] + product[last:last + plan.piece]
                     )
 
-        @pl.when(i >= 2)
-        def _():
-            for copy in leaving(i - 2):
-                copy.wait()
-
-        product = jnp.dot(x_buf[...], w_buf[slot], preferred_element_type=F32)
-        out_slot = lax.rem(i, 2)
-        for c in range(plan.chunks):
-            for d in range(plan.depth):
-                first = d * plan.rows_feat + c * plan.piece
-                to = slice(d * plan.piece, (d + 1) * plan.piece)
-                send_buf[out_slot, c, to, :] = product[first:first + plan.piece].astype(BF16)
-                keep_buf[out_slot, c, to, :] = product[half + first:half + first + plan.piece]
-        for copy in leaving(i):
-            copy.start()
-
+    count = plan.model // tile * plan.sources
     streamed(count, w_buf.shape[0], copies_of, step)
-    for i in range(max(count - 2, 0), count):
-        for copy in leaving(i):
-            copy.wait()
 
 
 def decode(plan, index, pieces, w_dec):
-    tile = pick_tile(plan.model, 256)
+    tile = pick_tile(plan.model, 768)
     shape = (plan.depth * plan.piece, plan.model)
-    near = (2, plan.chunks, plan.depth * plan.piece, tile)
     outs = call(
         partial(decode_kernel, plan),
         "decode",
@@ -287,17 +281,14 @@
         [jax.ShapeDtypeStruct(shape, BF16)] * plan.chunks
         + [jax.ShapeDtypeStruct(shape, F32)] * plan.chunks,
         [
-            pltpu.VMEM((plan.tokens, plan.sources * plan.width), BF16),
-            pltpu.VMEM((WEIGHT_SLOTS, plan.sources * plan.width, tile), BF16),
-            pltpu.VMEM(near, BF16),
-            pltpu.VMEM(near, F32),
-            pltpu.SemaphoreType.DMA((len(pieces) * plan.per_group,)),
-            pltpu.SemaphoreType.DMA((WEIGHT_SLOTS, plan.sources)),
-            pltpu.SemaphoreType.DMA((2, 2 * plan.chunks)),
+            pltpu.VMEM((plan.sources, plan.tokens, plan.width), BF16),
+            pltpu.VMEM((WEIGHT_SLOTS, plan.width, tile), BF16),
+            pltpu.VMEM((plan.tokens, tile), F32),
+            pltpu.SemaphoreType.DMA((plan.sources, plan.groups * plan.per_group)),
+            pltpu.SemaphoreType.DMA((WEIGHT_SLOTS,)),
         ],
         (index, *pieces, w_dec),
         vmem=MOST_VMEM_BYTES,
-        out_specs=[ANYWHERE] * (2 * plan.chunks),
     )
     return outs[:plan.chunks], outs[plan.chunks:]
 
@@ -306,7 +297,7 @@
     n_in = 2 * plan.depth
     errors, w_ref, outs = refs[:n_in], refs[n_in], refs[n_in + 1:-4]
     e_buf, w_buf, e_sem, w_sem = refs[-4:]
-    depth = pick_tile(plan.width, 256)
+    depth = pick_tile(plan.width, 512)
     steps = plan.width // depth
     base = 1 + plan.sources + plan.groups * plan.pairs
 
@@ -323,10 +314,19 @@
     for copy in placing:
         copy.start()
     def copies_of(i, slot):
-        rows = pl.ds(pl.multiple_of(lax.rem(i, steps) * depth, depth), depth)
-        return [pltpu.make_async_copy(
-            w_ref.at[lax.div(i, steps), 0, rows], w_buf.at[slot], w_sem.at[slot]
-        )]
+        part = depth // 4
+        return [
+            pltpu.make_async_copy(
+                w_ref.at[
+                    lax.div(i, steps),
+                    0,
+                    pl.ds(pl.multiple_of(lax.rem(i, steps) * depth + p * part, part), part),
+                ],
+                w_buf.at[slot, pl.ds(p * part, part)],
+                w_sem.at[slot, p],
+            )
+            for p in range(4)
+        ]
 
     half = plan.groups // 2
 
@@ -339,8 +339,8 @@
         source = lax.div(i, steps)
         cols = pl.ds(pl.multiple_of(lax.rem(i, steps) * depth, depth), depth)
         product = lax.dot_general(
-            e_buf[...], w_buf[slot], (((1,), (1,)), ((), ())), preferred_element_type=F32
-        )
+            w_buf[slot], e_buf[...], (((1,), (1,)), ((), ())), preferred_element_type=F32
+        ).T
         product = jnp.where(index_ref[1 + source] > 0, product, 0.0)
         for lane, (lo, hi) in enumerate(plan.lane_sources):
             first, kept = plan.lanes[lane][0], plan.kept_order(lane)
@@ -370,7 +370,7 @@
 
 
 def gradient(plan, index, errors, w_dec):
-    depth = pick_tile(plan.width, 256)
+    depth = pick_tile(plan.width, 512)
     half = plan.groups // 2
     out_shape = []
     for lo, hi in plan.lane_sources:
@@ -384,9 +384,9 @@
         out_shape + [jax.ShapeDtypeStruct((8, 128), F32)],
         [
             pltpu.VMEM((plan.chunk_rows, plan.model), BF16),
-            pltpu.VMEM((2 * WEIGHT_SLOTS, depth, plan.model), BF16),
+            pltpu.VMEM((WEIGHT_SLOTS, depth, plan.model), BF16),
             pltpu.SemaphoreType.DMA((len(errors),)),
-            pltpu.SemaphoreType.DMA((2 * WEIGHT_SLOTS,)),
+            pltpu.SemaphoreType.DMA((WEIGHT_SLOTS, 4)),
         ],
         (index, *errors, w_dec),
     )
@@ -464,9 +464,9 @@
         encoded += encode(plan, lo, hi, resid, w_enc, b_enc)
     active = arrange(plan, encoded)
 
-    pieces, arrived, forwarded = [], [], []
+    pieces, arrived, also, forwarded = [], [], [], []
     for batch in batches:
-        before, arrived, before_forward, forwarded = arrived, [], forwarded, []
+        before, arrived, before_forward, forwarded = arrived, [], also + forwarded, []
         for s in batch:
             bits = plan.lanes[s % len(plan.lanes)]
             mine, = after([encoded[s]], before)
@@ -478,11 +478,12 @@
                         x, = after([x], before_forward)
                     held[j | bit] = swap(x, "grp", groups, bit)
             pieces += [held[j] for j in range(groups)]
-            arrived += [held[bit] for bit in bits]
+            arrived.append(held[bits[0]])
+            also += [held[bit] for bit in bits[1:]]
             forwarded += [held[j] for j in range(groups) if j & (j - 1)]
 
     sends, keeps = decode(plan, index, after(pieces, [active]), w_dec)
-    recon_parts, errors = [], []
+    recon_parts, errors, first_errors = [], [], []
     for c in range(chunks):
         other = swap(sends[c], "feat", feats, 1)
         held = {
@@ -510,43 +511,58 @@
                 held.update(
                     {d | bit: swap(x, "feat", feats, 2 * bit) for d, x in list(held.items())}
                 )
+        first_errors.append([held[d] for d in range(1, plan.depth)])
         every = [held[d] for d in range(plan.depth)]
         errors.append(every + [swap(e, "feat", feats, 1) for e in every])
 
     squares = jnp.zeros((8, 128), F32)
-    feat_grad = None
-    second, got_all = [], []
+    totals, results = [], []
     for c in range(chunks):
-        ready = after(errors[c], [e[0] for e in errors[c + 1:c + 2]] + second)
+        ready = after(errors[c], [e[0] for e in errors[c + 1:c + 2]] + totals[-1:])
         lanes, total = gradient(plan, index, ready, w_dec)
+        totals.append(total)
         squares = squares + total
-        second = []
-        earlier = got_all + [x for every in errors[c + 1:c + 2] for x in every[1:plan.depth]]
-        lanes = [(after(away, earlier), kept) for away, kept in lanes]
-        kept_all = []
+        results.append(lanes)
+
+    unfinished = []
+    for c, lanes in enumerate(results):
+        earlier = [x for each in first_errors[c + 1:c + 2] for x in each]
+        first_step = []
         for bits, (away, kept) in zip(plan.lanes, lanes):
-            kept = [[x] for x in kept]
-            for step, bit in enumerate(bits):
-                cut = len(away) // 2
-                got = [swap(x, "grp", groups, bit) for x in away[:cut]]
-                rest = after(away[cut:], got[:1])
-                got += [swap(x, "grp", groups, bit) for x in rest]
-                for own, x in zip(kept, got):
-                    own.append(x)
-                if cut:
-                    away = [sum(x.astype(F32) for x in own).astype(BF16) for own in kept[:cut]]
-                    kept = kept[cut:]
-                    second += away if not step else []
+            away = after(away, earlier)
+            cut = len(away) // 2
+            got = [swap(x, "grp", groups, bits[0]) for x in away[:cut]]
+            rest = away[cut:] if c + 1 < chunks else after(away[cut:], got[:1])
+            got += [swap(x, "grp", groups, bits[0]) for x in rest]
+            first_step.append(got)
+        wait = totals[c + 1:c + 2]
+        if wait:
+            wait = wait + [got[-1] for got in first_step]
+        second, kept_all = [], []
+        for bits, (away, kept), got in zip(plan.lanes, lanes, first_step):
+            kept = [[x, after([y], wait)[0]] for x, y in zip(kept, got)]
+            for bit in bits[1:]:
+                cut = len(kept) // 2
+                away = [sum(x.astype(F32) for x in own).astype(BF16) for own in kept[:cut]]
+                second += away
+                kept = kept[cut:]
+                for own, x in zip(kept, away):
+                    own.append(swap(x, "grp", groups, bit))
             kept_all.append(kept[0])
         got_all = [own[i] for i in range(1, len(kept_all[0])) for own in kept_all]
-        previous = feat_grad
-        feat_grad = finish(plan, c, [own[0] for own in kept_all], got_all, previous)
+        unfinished.append(([own[0] for own in kept_all], got_all))
+
+    feat_grad = None
+    for c, (kept, got) in enumerate(unfinished):
+        before_last = feat_grad
+        feat_grad = finish(plan, c, kept, got, feat_grad)
 
     loss = jnp.full((8, 128), jnp.sum(squares), F32)
-    for i, bit in enumerate(1 << i for i in range(groups.bit_length() - 1)):
-        loss = loss + swap(loss, "grp", groups, bit)
-        if not i:
-            loss, = after([loss], second + ([] if previous is None else [previous]))
+    parts = [loss] + [swap(loss, "grp", groups, j) for j in range(1, groups)]
+    parts = after(parts, second + ([] if before_last is None else [before_last]))
+    while len(parts) > 1:
+        parts = [x + y for x, y in zip(parts[::2], parts[1::2])]
+    loss = parts[0]
     entries = targets.shape[0] * groups * plan.tokens * plan.model
     recon_loss = loss[0, 0] / entries
     recon = jnp.concatenate(recon_parts, axis=0)[None]

time: 179 us -> 181 us (1.011)
  starting transfers between devices: 44.2 us -> 50.5 us
  Pallas kernels: 61.1 us -> 58.9 us
    ppermute x48 -> x49, starting transfers between devices: 44.2 us -> 50.5 us  [swap(): return lax.ppermute(x, axis, [(i, i ^ offset) for i in range(size)])]
    pallas_call x8, Pallas kernels: 61.1 us -> 58.9 us  [call(): pl.pallas_call(kernel, in_specs=in_specs, out_shape=out_shape, scratch_sh...]
    ppermute x48 -> x49, waiting for transfers between devices: 59.5 us -> 58.2 us  [swap(): return lax.ppermute(x, axis, [(i, i ^ offset) for i in range(size)])]
  transfers between devices with their start and end apart: 48 -> 49, of which waited for: 17 -> 20; matrix products, arithmetic and copies ran while one was open for 4% -> 4% of each run, Pallas kernels for 20% -> 18%
where the time goes in v10:
time: 181 us
  Pallas kernels  58.9 us (33%)
  waiting for transfers between devices  58.2 us (32%)
  starting transfers between devices  50.5 us (28%)
  other arithmetic  5.88 us (3%)
  local copies, waits for them, and re-layouts  4.36 us (2%)
  between operations  2.8 us (2%)
    pallas_call x8, Pallas kernels, call(): pl.pallas_call(kernel, in_specs=in_specs, out_shape=out_shape, scratch_sh...  58.9 us
    ppermute x49, waiting for transfers between devices, swap(): return lax.ppermute(x, axis, [(i, i ^ offset) for i in range(size)])  58.2 us
    ppermute x49, starting transfers between devices, swap(): return lax.ppermute(x, axis, [(i, i ^ offset) for i in range(size)])  50.5 us
  transfers between devices with their start and end apart: 49, of which 20 were waited for; matrix products, arithmetic and copies ran while one was open for 4% of the time, Pallas kernels for 18%

profile of v10, /device:TPU:0, one launch (start us, length us, event | category | flops | bytes accessed | tf_op | source)
XLA Modules:
  0.0 180.6 jit_solution(7929767791264688283)
XLA Ops:
  0.6 5.5 %encode.2 = (bf16[128,1024]{1,0:T(8,128)(2,1)}, bf16[128,1024]{1,0:T(8,128)(2,1)}) custom-call(bf16[4,128,2304]{2,1,0:T(8,128)(2,1)} %resid_ref.3, bf16[4,2304,1024]{2,1,0:T(8,128)(2,1)} %w_ref.3, f32[4,1024]{1,0:T(4,128)} %b_ref.3), custom_call_target="tpu_custom_call" | custom-call | flops 1048576 | bytes 1024 | tf_op jit(solution)/shard_map/encode/pallas_call | solution.py:103
  6.1 3.0 %collective-permute-start = (bf16[128,1024]{1,0:T(8,128)(2,1)}, bf16[128,1024]{1,0:T(8,128)(2,1)S(1)}, u32[]{:S(2)}, u32[]{:S(2)}) collective-permute-start(bf16[128,1024]{1,0:T(8,128)(2,1)} %get-tuple-element.89.refs_0_), channel_id=1, source_target_pairs={{0,8},{8,0},{16,24},{24,16},{1,9},{9,1},{17,25},{25,17},{2,10},{10... | collective-permute-start | bytes 786440 | tf_op jit(solution)/shard_map/ppermute | solution.py:30
  9.1 1.5 collective-permute-start.4
  11.3 5.5 %encode.3 = (bf16[128,1024]{1,0:T(8,128)(2,1)}, bf16[128,1024]{1,0:T(8,128)(2,1)}) custom-call(bf16[4,128,2304]{2,1,0:T(8,128)(2,1)} %resid_ref.3, bf16[4,2304,1024]{2,1,0:T(8,128)(2,1)} %w_ref.3, f32[4,1024]{1,0:T(4,128)} %b_ref.3), custom_call_target="tpu_custom_call" | custom-call | flops 1048576 | bytes 1024 | tf_op jit(solution)/shard_map/encode/pallas_call | solution.py:103
  16.8 1.8 %collective-permute-done.4.refs_6_ = bf16[128,1024]{1,0:T(8,128)(2,1)S(1)} collective-permute-done((bf16[128,1024]{1,0:T(8,128)(2,1)}, bf16[128,1024]{1,0:T(8,128)(2,1)S(1)}, u32[]{:S(2)}, u32[]{:S(2)}) %collective-permute-start.4) | collective-permute-done | bytes 262176 | tf_op jit(solution)/shard_map/ppermute | solution.py:30
  18.6 1.5 collective-permute-start.2
  20.8 3.4 %collective-permute-done.1.refs_2_ = bf16[128,1024]{1,0:T(8,128)(2,1)S(1)} collective-permute-done((bf16[128,1024]{1,0:T(8,128)(2,1)}, bf16[128,1024]{1,0:T(8,128)(2,1)S(1)}, u32[]{:S(2)}, u32[]{:S(2)}) %collective-permute-start.1) | collective-permute-done | bytes 262176 | tf_op jit(solution)/shard_map/ppermute | solution.py:30
  24.3 2.0 %collective-permute-start.7 = (bf16[128,1024]{1,0:T(8,128)(2,1)}, bf16[128,1024]{1,0:T(8,128)(2,1)S(1)}, u32[]{:S(2)}, u32[]{:S(2)}) collective-permute-start(bf16[128,1024]{1,0:T(8,128)(2,1)} %get-tuple-element.97.refs_2_.refs_8_), channel_id=1, source_target_pairs={{0,16},{8,24},{16,0},{24,8},{1,17},{9,25},{17,1},{25,9},{2,18},{10... | collective-permute-start | bytes 786440 | tf_op jit(solution)/shard_map/ppermute | solution.py:30
  26.3 3.6 %collective-permute-done.2.refs_3_ = bf16[128,1024]{1,0:T(8,128)(2,1)S(1)} collective-permute-done((bf16[128,1024]{1,0:T(8,128)(2,1)S(1)}, bf16[128,1024]{1,0:T(8,128)(2,1)S(1)}, u32[]{:S(2)}, u32[]{:S(2)}) %collective-permute-start.2) | collective-permute-done | bytes 262176 | tf_op jit(solution)/shard_map/ppermute | solution.py:30
  29.9 5.5 %collective-permute-done.10.refs_14_ = bf16[128,1024]{1,0:T(8,128)(2,1)S(1)} collective-permute-done((bf16[128,1024]{1,0:T(8,128)(2,1)}, bf16[128,1024]{1,0:T(8,128)(2,1)S(1)}, u32[]{:S(2)}, u32[]{:S(2)}) %collective-permute-start.10) | collective-permute-done | bytes 262176 | tf_op jit(solution)/shard_map/ppermute | solution.py:30
  35.5 1.6 collective-permute-start.8
  40.1 1.7 arrange.1
  41.9 3.3 %collective-permute-done.8.refs_11_ = bf16[128,1024]{1,0:T(8,128)(2,1)S(1)} collective-permute-done((bf16[128,1024]{1,0:T(8,128)(2,1)S(1)}, bf16[128,1024]{1,0:T(8,128)(2,1)S(1)}, u32[]{:S(2)}, u32[]{:S(2)}) %collective-permute-start.8) | collective-permute-done | bytes 262176 | tf_op jit(solution)/shard_map/ppermute | solution.py:30
  45.9 19.6 %decode.1 = (bf16[128,2304]{1,0:T(8,128)(2,1)}, bf16[128,2304]{1,0:T(8,128)(2,1)}, f32[128,2304]{1,0:T(8,128)}, f32[128,2304]{1,0:T(8,128)}) custom-call(s32[17]{0:T(128)} %concatenate.6.index_ref, bf16[128,1024]{1,0:T(8,128)(2,1)} %get-tuple-element.89.refs_0_, bf16[128,1024]{1,0:T(8,128)(2,1)} %copy-done.7, bf16[128,1024]{1,0:T(8,128)(2,1)} %copy-done.9, ...), custom_call_target="tpu_custom_call" | custom-call | flops 1048576 | bytes 1024 | tf_op jit(solution)/shard_map/decode/pallas_call | solution.py:103
  66.1 1.7 collective-permute-done.12
  67.8 1.1 add_convert_fusion.9
  68.9 1.6 collective-permute-start.13
  71.0 1.1 add_convert_fusion.6
  72.1 1.6 collective-permute-start.17
  74.2 4.6 %collective-permute-done.14 = bf16[32,2304]{1,0:T(8,128)(2,1)S(1)} collective-permute-done((bf16[32,2304]{1,0:T(8,128)(2,1)S(1)}, bf16[32,2304]{1,0:T(8,128)(2,1)S(1)}, u32[]{:S(2)}, u32[]{:S(2)}) %collective-permute-start.14) | collective-permute-done | bytes 147488 | tf_op jit(solution)/shard_map/ppermute | solution.py:30
  78.9 2.7 %collective-permute-start.15 = (bf16[32,2304]{1,0:T(8,128)(2,1)S(1)}, bf16[32,2304]{1,0:T(8,128)(2,1)S(1)}, u32[]{:S(2)}, u32[]{:S(2)}) collective-permute-start(bf16[32,2304]{1,0:T(8,128)(2,1)S(1)} %add_convert_fusion.7), channel_id=1, source_target_pairs={{0,4},{1,5},{2,6},{3,7},{4,0},{5,1},{6,2},{7,3},{8,12},{9,13},{10,... | collective-permute-start | bytes 442376 | tf_op jit(solution)/shard_map/ppermute | solution.py:30
  81.6 5.9 %collective-permute-done.18 = bf16[32,2304]{1,0:T(8,128)(2,1)S(1)} collective-permute-done((bf16[32,2304]{1,0:T(8,128)(2,1)S(1)}, bf16[32,2304]{1,0:T(8,128)(2,1)S(1)}, u32[]{:S(2)}, u32[]{:S(2)}) %collective-permute-start.18) | collective-permute-done | bytes 147488 | tf_op jit(solution)/shard_map/ppermute | solution.py:30
  87.6 1.0 collective-permute-start.19
  88.5 1.0 fusion.3
  89.6 2.1 %collective-permute-start.21 = (bf16[32,2304]{1,0:T(8,128)(2,1)S(1)}, bf16[32,2304]{1,0:T(8,128)(2,1)S(1)}, u32[]{:S(2)}, u32[]{:S(2)}) collective-permute-start(bf16[32,2304]{1,0:T(8,128)(2,1)S(1)} %get-tuple-element.110.refs_0_), channel_id=1, source_target_pairs={{0,4},{1,5},{2,6},{3,7},{4,0},{5,1},{6,2},{7,3},{8,12},{9,13},{10,... | collective-permute-start | bytes 442376 | tf_op jit(solution)/shard_map/ppermute | solution.py:30
  91.7 1.7 collective-permute-start.20
  93.4 6.8 %collective-permute-done.19 = bf16[32,2304]{1,0:T(8,128)(2,1)S(1)} collective-permute-done((bf16[32,2304]{1,0:T(8,128)(2,1)S(1)}, bf16[32,2304]{1,0:T(8,128)(2,1)S(1)}, u32[]{:S(2)}, u32[]{:S(2)}) %collective-permute-start.19) | collective-permute-done | bytes 147488 | tf_op jit(solution)/shard_map/ppermute | solution.py:30
  100.2 2.8 %collective-permute-done.21.refs_2_ = bf16[32,2304]{1,0:T(8,128)(2,1)S(1)} collective-permute-done((bf16[32,2304]{1,0:T(8,128)(2,1)S(1)}, bf16[32,2304]{1,0:T(8,128)(2,1)S(1)}, u32[]{:S(2)}, u32[]{:S(2)}) %collective-permute-start.21) | collective-permute-done | bytes 147488 | tf_op jit(solution)/shard_map/ppermute | solution.py:30
  104.0 1.9 %collective-permute-start.29 = (bf16[32,2304]{1,0:T(8,128)(2,1)S(1)}, bf16[32,2304]{1,0:T(8,128)(2,1)S(1)}, u32[]{:S(2)}, u32[]{:S(2)}) collective-permute-start(bf16[32,2304]{1,0:T(8,128)(2,1)S(1)} %get-tuple-element.119.refs_0_), channel_id=1, source_target_pairs={{0,6},{1,7},{2,4},{3,5},{4,2},{5,3},{6,0},{7,1},{8,14},{9,15},{10,... | collective-permute-start | bytes 442376 | tf_op jit(solution)/shard_map/ppermute | solution.py:30
  106.5 2.5 %collective-permute-done.22.refs_3_ = bf16[32,2304]{1,0:T(8,128)(2,1)S(1)} collective-permute-done((bf16[32,2304]{1,0:T(8,128)(2,1)S(1)}, bf16[32,2304]{1,0:T(8,128)(2,1)S(1)}, u32[]{:S(2)}, u32[]{:S(2)}) %collective-permute-start.22) | collective-permute-done | bytes 147488 | tf_op jit(solution)/shard_map/ppermute | solution.py:30
  109.9 2.2 %collective-permute-done.29.refs_3_ = bf16[32,2304]{1,0:T(8,128)(2,1)S(1)} collective-permute-done((bf16[32,2304]{1,0:T(8,128)(2,1)S(1)}, bf16[32,2304]{1,0:T(8,128)(2,1)S(1)}, u32[]{:S(2)}, u32[]{:S(2)}) %collective-permute-start.29) | collective-permute-done | bytes 147488 | tf_op jit(solution)/shard_map/ppermute | solution.py:30
  112.1 6.7 %collective-permute-start.27 = (bf16[32,2304]{1,0:T(8,128)(2,1)S(1)}, bf16[32,2304]{1,0:T(8,128)(2,1)S(1)}, u32[]{:S(2)}, u32[]{:S(2)}) collective-permute-start(bf16[32,2304]{1,0:T(8,128)(2,1)S(1)} %get-tuple-element.119.refs_0_), channel_id=1, source_target_pairs={{0,2},{1,3},{2,0},{3,1},{4,6},{5,7},{6,4},{7,5},{8,10},{9,11},{10,... | collective-permute-start | bytes 442376 | tf_op jit(solution)/shard_map/ppermute | solution.py:30
  119.4 12.0 %gradient.2 = (bf16[2,64,1024]{2,1,0:T(8,128)(2,1)S(1)}, bf16[2,64,1024]{2,1,0:T(8,128)(2,1)S(1)}, f32[2,64,1024]{2,1,0:T(8,128)S(1)}, f32[2,64,1024]{2,1,0:T(8,...) custom-call(s32[17]{0:T(128)S(1)} %copy-done.4, ...), custom_call_target="tpu_custom_call" | custom-call | flops 1048576 | bytes 1024 | tf_op jit(solution)/shard_map/gradient/pallas_call | solution.py:103
  131.4 1.9 %collective-permute-start.39 = (bf16[2,64,1024]{2,1,0:T(8,128)(2,1)S(1)}, bf16[2,64,1024]{2,1,0:T(8,128)(2,1)S(1)}, u32[]{:S(2)}, u32[]{:S(2)}) collective-permute-start(bf16[2,64,1024]{2,1,0:T(8,128)(2,1)S(1)} %get-tuple-element.136), channel_id=1, source_target_pairs={{0,8},{8,0},{16,24},{24,16},{1,9},{9,1},{17,25},{25,17},{2,10},{10... | collective-permute-start | bytes 786440 | tf_op jit(solution)/shard_map/ppermute | solution.py:30
  135.1 1.9 %collective-permute-start.43 = (bf16[2,64,1024]{2,1,0:T(8,128)(2,1)S(1)}, bf16[2,64,1024]{2,1,0:T(8,128)(2,1)S(1)}, u32[]{:S(2)}, u32[]{:S(2)}) collective-permute-start(bf16[2,64,1024]{2,1,0:T(8,128)(2,1)S(1)} %get-tuple-element.146), channel_id=1, source_target_pairs={{0,16},{8,24},{16,0},{24,8},{1,17},{9,25},{17,1},{25,9},{2,18},{10... | collective-permute-start | bytes 786440 | tf_op jit(solution)/shard_map/ppermute | solution.py:30
  137.1 12.0 %gradient.3 = (bf16[2,64,1024]{2,1,0:T(8,128)(2,1)S(1)}, bf16[2,64,1024]{2,1,0:T(8,128)(2,1)S(1)}, f32[2,64,1024]{2,1,0:T(8,128)S(1)}, f32[2,64,1024]{2,1,0:T(8,...) custom-call(s32[17]{0:T(128)S(1)} %copy-done.4, ...), custom_call_target="tpu_custom_call" | custom-call | flops 1048576 | bytes 1024 | tf_op jit(solution)/shard_map/gradient/pallas_call | solution.py:103
  150.3 1.4 collective-permute-start.36
  151.9 2.0 %collective-permute-start.37 = (bf16[2,64,1024]{2,1,0:T(8,128)(2,1)S(1)}, bf16[2,64,1024]{2,1,0:T(8,128)(2,1)S(1)}, u32[]{:S(2)}, u32[]{:S(2)}) collective-permute-start(bf16[2,64,1024]{2,1,0:T(8,128)(2,1)S(1)} %get-tuple-element.129), channel_id=1, source_target_pairs={{0,8},{8,0},{16,24},{24,16},{1,9},{9,1},{17,25},{25,17},{2,10},{10... | collective-permute-start | bytes 786440 | tf_op jit(solution)/shard_map/ppermute | solution.py:30
  154.0 2.0 %collective-permute-start.42 = (bf16[2,64,1024]{2,1,0:T(8,128)(2,1)S(1)}, bf16[2,64,1024]{2,1,0:T(8,128)(2,1)S(1)}, u32[]{:S(2)}, u32[]{:S(2)}) collective-permute-start(bf16[2,64,1024]{2,1,0:T(8,128)(2,1)S(1)} %add_convert_fusion.1), channel_id=1, source_target_pairs={{0,16},{8,24},{16,0},{24,8},{1,17},{9,25},{17,1},{25,9},{2,18},{10... | collective-permute-start | bytes 786440 | tf_op jit(solution)/shard_map/ppermute | solution.py:30
  156.1 3.7 %collective-permute-done.37 = bf16[2,64,1024]{2,1,0:T(8,128)(2,1)S(1)} collective-permute-done((bf16[2,64,1024]{2,1,0:T(8,128)(2,1)S(1)}, bf16[2,64,1024]{2,1,0:T(8,128)(2,1)S(1)}, u32[]{:S(2)}, u32[]{:S(2)}) %collective-permute-start.37) | collective-permute-done | bytes 262176 | tf_op jit(solution)/shard_map/ppermute | solution.py:30
  159.8 1.7 collective-permute-start.44
  161.6 1.5 collective-permute-done.38
  163.3 2.0 %collective-permute-start.45 = (bf16[2,64,1024]{2,1,0:T(8,128)(2,1)S(1)}, bf16[2,64,1024]{2,1,0:T(8,128)(2,1)S(1)}, u32[]{:S(2)}, u32[]{:S(2)}) collective-permute-start(bf16[2,64,1024]{2,1,0:T(8,128)(2,1)S(1)} %get-tuple-element.155), channel_id=1, source_target_pairs={{0,8},{8,0},{16,24},{24,16},{1,9},{9,1},{17,25},{25,17},{2,10},{10... | collective-permute-start | bytes 786440 | tf_op jit(solution)/shard_map/ppermute | solution.py:30
  165.4 3.4 %collective-permute-done.42.refs_4_ = bf16[2,64,1024]{2,1,0:T(8,128)(2,1)S(1)} collective-permute-done((bf16[2,64,1024]{2,1,0:T(8,128)(2,1)S(1)}, bf16[2,64,1024]{2,1,0:T(8,128)(2,1)S(1)}, u32[]{:S(2)}, u32[]{:S(2)}) %collective-permute-start.42) | collective-permute-done | bytes 262176 | tf_op jit(solution)/shard_map/ppermute | solution.py:30
  169.1 1.7 collective-permute-start.48
  171.5 1.3 finish.2.refs_6_
  174.8 3.4 %collective-permute-done.46.refs_3_ = bf16[2,64,1024]{2,1,0:T(8,128)(2,1)S(1)} collective-permute-done((bf16[2,64,1024]{2,1,0:T(8,128)(2,1)S(1)}, bf16[2,64,1024]{2,1,0:T(8,128)(2,1)S(1)}, u32[]{:S(2)}, u32[]{:S(2)}) %collective-permute-start.46) | collective-permute-done | bytes 262176 | tf_op jit(solution)/shard_map/ppermute | solution.py:30
  178.2 1.3 finish.3
  (114 shorter events, 16.1 us)
Async XLA Ops:
  6.1 10.6 %collective-permute-start = (bf16[128,1024]{1,0:T(8,128)(2,1)}, bf16[128,1024]{1,0:T(8,128)(2,1)S(1)}, u32[]{:S(2)}, u32[]{:S(2)}) collective-permute-start(bf16[128,1024]{1,0:T(8,128)(2,1)} %get-tuple-element.89.refs_0_), channel_id=1, source_target_pairs={{0,8},{8,0},{16,24},{24,16},{1,9},{9,1},{17,25},{25,17},{2,10},{10... | collective-permute-start | bytes 786440 | tf_op jit(solution)/shard_map/ppermute | solution.py:30
  9.1 9.4 %collective-permute-start.4 = (bf16[128,1024]{1,0:T(8,128)(2,1)}, bf16[128,1024]{1,0:T(8,128)(2,1)S(1)}, u32[]{:S(2)}, u32[]{:S(2)}) collective-permute-start(bf16[128,1024]{1,0:T(8,128)(2,1)} %get-tuple-element.93.refs_1_.refs_4_), channel_id=1, source_target_pairs={{0,16},{8,24},{16,0},{24,8},{1,17},{9,25},{17,1},{25,9},{2,18},{10... | collective-permute-start | bytes 786440 | tf_op jit(solution)/shard_map/ppermute | solution.py:30
  10.7 13.5 %collective-permute-start.1 = (bf16[128,1024]{1,0:T(8,128)(2,1)}, bf16[128,1024]{1,0:T(8,128)(2,1)S(1)}, u32[]{:S(2)}, u32[]{:S(2)}) collective-permute-start(bf16[128,1024]{1,0:T(8,128)(2,1)} %get-tuple-element.89.refs_0_), channel_id=1, source_target_pairs={{0,16},{8,24},{16,0},{24,8},{1,17},{9,25},{17,1},{25,9},{2,18},{10... | collective-permute-start | bytes 786440 | tf_op jit(solution)/shard_map/ppermute | solution.py:30
  11.2 13.1 %collective-permute-start.3 = (bf16[128,1024]{1,0:T(8,128)(2,1)}, bf16[128,1024]{1,0:T(8,128)(2,1)S(1)}, u32[]{:S(2)}, u32[]{:S(2)}) collective-permute-start(bf16[128,1024]{1,0:T(8,128)(2,1)} %get-tuple-element.93.refs_1_.refs_4_), channel_id=1, source_target_pairs={{0,8},{8,0},{16,24},{24,16},{1,9},{9,1},{17,25},{25,17},{2,10},{10... | collective-permute-start | bytes 786440 | tf_op jit(solution)/shard_map/ppermute | solution.py:30
  18.6 11.2 %collective-permute-start.2 = (bf16[128,1024]{1,0:T(8,128)(2,1)S(1)}, bf16[128,1024]{1,0:T(8,128)(2,1)S(1)}, u32[]{:S(2)}, u32[]{:S(2)}) collective-permute-start(bf16[128,1024]{1,0:T(8,128)(2,1)S(1)} %collective-permute-done.refs_1_), channel_id=1, source_target_pairs={{0,16},{8,24},{16,0},{24,8},{1,17},{9,25},{17,1},{25,9},{2,18},{10... | collective-permute-start | bytes 786440 | tf_op jit(solution)/shard_map/ppermute | solution.py:30
  20.1 15.3 %collective-permute-start.10 = (bf16[128,1024]{1,0:T(8,128)(2,1)}, bf16[128,1024]{1,0:T(8,128)(2,1)S(1)}, u32[]{:S(2)}, u32[]{:S(2)}) collective-permute-start(bf16[128,1024]{1,0:T(8,128)(2,1)} %get-tuple-element.101.refs_3_.refs_12_), channel_id=1, source_target_pairs={{0,16},{8,24},{16,0},{24,8},{1,17},{9,25},{17,1},{25,9},{2,18},{10... | collective-permute-start | bytes 786440 | tf_op jit(solution)/shard_map/ppermute | solution.py:30
  20.6 14.8 %collective-permute-start.5 = (bf16[128,1024]{1,0:T(8,128)(2,1)S(1)}, bf16[128,1024]{1,0:T(8,128)(2,1)S(1)}, u32[]{:S(2)}, u32[]{:S(2)}) collective-permute-start(bf16[128,1024]{1,0:T(8,128)(2,1)S(1)} %collective-permute-done.4.refs_6_), channel_id=1, source_target_pairs={{0,8},{8,0},{16,24},{24,16},{1,9},{9,1},{17,25},{25,17},{2,10},{10... | collective-permute-start | bytes 786440 | tf_op jit(solution)/shard_map/ppermute | solution.py:30
  24.2 11.2 %collective-permute-start.6 = (bf16[128,1024]{1,0:T(8,128)(2,1)}, bf16[128,1024]{1,0:T(8,128)(2,1)S(1)}, u32[]{:S(2)}, u32[]{:S(2)}) collective-permute-start(bf16[128,1024]{1,0:T(8,128)(2,1)} %get-tuple-element.97.refs_2_.refs_8_), channel_id=1, source_target_pairs={{0,8},{8,0},{16,24},{24,16},{1,9},{9,1},{17,25},{25,17},{2,10},{10... | collective-permute-start | bytes 786440 | tf_op jit(solution)/shard_map/ppermute | solution.py:30
  24.3 17.6 %collective-permute-start.7 = (bf16[128,1024]{1,0:T(8,128)(2,1)}, bf16[128,1024]{1,0:T(8,128)(2,1)S(1)}, u32[]{:S(2)}, u32[]{:S(2)}) collective-permute-start(bf16[128,1024]{1,0:T(8,128)(2,1)} %get-tuple-element.97.refs_2_.refs_8_), channel_id=1, source_target_pairs={{0,16},{8,24},{16,0},{24,8},{1,17},{9,25},{17,1},{25,9},{2,18},{10... | collective-permute-start | bytes 786440 | tf_op jit(solution)/shard_map/ppermute | solution.py:30
  29.8 12.1 %collective-permute-start.9 = (bf16[128,1024]{1,0:T(8,128)(2,1)}, bf16[128,1024]{1,0:T(8,128)(2,1)S(1)}, u32[]{:S(2)}, u32[]{:S(2)}) collective-permute-start(bf16[128,1024]{1,0:T(8,128)(2,1)} %get-tuple-element.101.refs_3_.refs_12_), channel_id=1, source_target_pairs={{0,8},{8,0},{16,24},{24,16},{1,9},{9,1},{17,25},{25,17},{2,10},{10... | collective-permute-start | bytes 786440 | tf_op jit(solution)/shard_map/ppermute | solution.py:30
  35.5 9.7 %collective-permute-start.8 = (bf16[128,1024]{1,0:T(8,128)(2,1)S(1)}, bf16[128,1024]{1,0:T(8,128)(2,1)S(1)}, u32[]{:S(2)}, u32[]{:S(2)}) collective-permute-start(bf16[128,1024]{1,0:T(8,128)(2,1)S(1)} %collective-permute-done.6.refs_9_), channel_id=1, source_target_pairs={{0,16},{8,24},{16,0},{24,8},{1,17},{9,25},{17,1},{25,9},{2,18},{10... | collective-permute-start | bytes 786440 | tf_op jit(solution)/shard_map/ppermute | solution.py:30
  37.0 8.2 %collective-permute-start.11 = (bf16[128,1024]{1,0:T(8,128)(2,1)S(1)}, bf16[128,1024]{1,0:T(8,128)(2,1)}, u32[]{:S(2)}, u32[]{:S(2)}) collective-permute-start(bf16[128,1024]{1,0:T(8,128)(2,1)S(1)} %collective-permute-done.10.refs_14_), channel_id=1, source_target_pairs={{0,8},{8,0},{16,24},{24,16},{1,9},{9,1},{17,25},{25,17},{2,10},{10... | collective-permute-start | bytes 786440 | tf_op jit(solution)/shard_map/ppermute | solution.py:30
  65.5 2.3 %collective-permute-start.12 = (bf16[128,2304]{1,0:T(8,128)(2,1)}, bf16[128,2304]{1,0:T(8,128)(2,1)S(1)}, u32[]{:S(2)}, u32[]{:S(2)}) collective-permute-start(bf16[128,2304]{1,0:T(8,128)(2,1)} %get-tuple-element.106), channel_id=1, source_target_pairs={{0,1},{1,0},{2,3},{3,2},{4,5},{5,4},{6,7},{7,6},{8,9},{9,8},{10,11... | collective-permute-start | bytes 1769480 | tf_op jit(solution)/shard_map/ppermute | solution.py:30
  65.6 5.4 %collective-permute-start.16 = (bf16[128,2304]{1,0:T(8,128)(2,1)}, bf16[128,2304]{1,0:T(8,128)(2,1)S(1)}, u32[]{:S(2)}, u32[]{:S(2)}) collective-permute-start(bf16[128,2304]{1,0:T(8,128)(2,1)} %get-tuple-element.108), channel_id=1, source_target_pairs={{0,1},{1,0},{2,3},{3,2},{4,5},{5,4},{6,7},{7,6},{8,9},{9,8},{10,11... | collective-permute-start | bytes 1769480 | tf_op jit(solution)/shard_map/ppermute | solution.py:30
  68.9 19.6 %collective-permute-start.13 = (bf16[32,2304]{1,0:T(8,128)(2,1)S(1)}, bf16[32,2304]{1,0:T(8,128)(2,1)S(1)}, u32[]{:S(2)}, u32[]{:S(2)}) collective-permute-start(bf16[32,2304]{1,0:T(8,128)(2,1)S(1)} %get-tuple-element.160), channel_id=1, source_target_pairs={{0,2},{1,3},{2,0},{3,1},{4,6},{5,7},{6,4},{7,5},{8,10},{9,11},{10,... | collective-permute-start | bytes 442376 | tf_op jit(solution)/shard_map/ppermute | solution.py:30
  70.5 8.3 %collective-permute-start.14 = (bf16[32,2304]{1,0:T(8,128)(2,1)S(1)}, bf16[32,2304]{1,0:T(8,128)(2,1)S(1)}, u32[]{:S(2)}, u32[]{:S(2)}) collective-permute-start(bf16[32,2304]{1,0:T(8,128)(2,1)S(1)} %get-tuple-element.161), channel_id=1, source_target_pairs={{0,2},{1,3},{2,0},{3,1},{4,6},{5,7},{6,4},{7,5},{8,10},{9,11},{10,... | collective-permute-start | bytes 442376 | tf_op jit(solution)/shard_map/ppermute | solution.py:30
  72.1 21.3 %collective-permute-start.17 = (bf16[32,2304]{1,0:T(8,128)(2,1)S(1)}, bf16[32,2304]{1,0:T(8,128)(2,1)S(1)}, u32[]{:S(2)}, u32[]{:S(2)}) collective-permute-start(bf16[32,2304]{1,0:T(8,128)(2,1)S(1)} %get-tuple-element.162), channel_id=1, source_target_pairs={{0,2},{1,3},{2,0},{3,1},{4,6},{5,7},{6,4},{7,5},{8,10},{9,11},{10,... | collective-permute-start | bytes 442376 | tf_op jit(solution)/shard_map/ppermute | solution.py:30
  73.7 13.8 %collective-permute-start.18 = (bf16[32,2304]{1,0:T(8,128)(2,1)S(1)}, bf16[32,2304]{1,0:T(8,128)(2,1)S(1)}, u32[]{:S(2)}, u32[]{:S(2)}) collective-permute-start(bf16[32,2304]{1,0:T(8,128)(2,1)S(1)} %get-tuple-element.163), channel_id=1, source_target_pairs={{0,2},{1,3},{2,0},{3,1},{4,6},{5,7},{6,4},{7,5},{8,10},{9,11},{10,... | collective-permute-start | bytes 442376 | tf_op jit(solution)/shard_map/ppermute | solution.py:30
  78.9 9.7 %collective-permute-start.15 = (bf16[32,2304]{1,0:T(8,128)(2,1)S(1)}, bf16[32,2304]{1,0:T(8,128)(2,1)S(1)}, u32[]{:S(2)}, u32[]{:S(2)}) collective-permute-start(bf16[32,2304]{1,0:T(8,128)(2,1)S(1)} %add_convert_fusion.7), channel_id=1, source_target_pairs={{0,4},{1,5},{2,6},{3,7},{4,0},{5,1},{6,2},{7,3},{8,12},{9,13},{10,... | collective-permute-start | bytes 442376 | tf_op jit(solution)/shard_map/ppermute | solution.py:30
  87.6 12.6 %collective-permute-start.19 = (bf16[32,2304]{1,0:T(8,128)(2,1)S(1)}, bf16[32,2304]{1,0:T(8,128)(2,1)S(1)}, u32[]{:S(2)}, u32[]{:S(2)}) collective-permute-start(bf16[32,2304]{1,0:T(8,128)(2,1)S(1)} %add_convert_fusion.4), channel_id=1, source_target_pairs={{0,4},{1,5},{2,6},{3,7},{4,0},{5,1},{6,2},{7,3},{8,12},{9,13},{10,... | collective-permute-start | bytes 442376 | tf_op jit(solution)/shard_map/ppermute | solution.py:30
  89.5 19.4 %collective-permute-start.23 = (bf16[32,2304]{1,0:T(8,128)(2,1)S(1)}, bf16[32,2304]{1,0:T(8,128)(2,1)S(1)}, u32[]{:S(2)}, u32[]{:S(2)}) collective-permute-start(bf16[32,2304]{1,0:T(8,128)(2,1)S(1)} %get-tuple-element.110.refs_0_), channel_id=1, source_target_pairs={{0,1},{1,0},{2,3},{3,2},{4,5},{5,4},{6,7},{7,6},{8,9},{9,8},{10,11... | collective-permute-start | bytes 442376 | tf_op jit(solution)/shard_map/ppermute | solution.py:30
  89.6 13.4 %collective-permute-start.21 = (bf16[32,2304]{1,0:T(8,128)(2,1)S(1)}, bf16[32,2304]{1,0:T(8,128)(2,1)S(1)}, u32[]{:S(2)}, u32[]{:S(2)}) collective-permute-start(bf16[32,2304]{1,0:T(8,128)(2,1)S(1)} %get-tuple-element.110.refs_0_), channel_id=1, source_target_pairs={{0,4},{1,5},{2,6},{3,7},{4,0},{5,1},{6,2},{7,3},{8,12},{9,13},{10,... | collective-permute-start | bytes 442376 | tf_op jit(solution)/shard_map/ppermute | solution.py:30
  91.7 14.3 %collective-permute-start.20 = (bf16[32,2304]{1,0:T(8,128)(2,1)S(1)}, bf16[32,2304]{1,0:T(8,128)(2,1)S(1)}, u32[]{:S(2)}, u32[]{:S(2)}) collective-permute-start(bf16[32,2304]{1,0:T(8,128)(2,1)S(1)} %get-tuple-element.110.refs_0_), channel_id=1, source_target_pairs={{0,2},{1,3},{2,0},{3,1},{4,6},{5,7},{6,4},{7,5},{8,10},{9,11},{10,... | collective-permute-start | bytes 442376 | tf_op jit(solution)/shard_map/ppermute | solution.py:30
  103.1 5.9 %collective-permute-start.22 = (bf16[32,2304]{1,0:T(8,128)(2,1)S(1)}, bf16[32,2304]{1,0:T(8,128)(2,1)S(1)}, u32[]{:S(2)}, u32[]{:S(2)}) collective-permute-start(bf16[32,2304]{1,0:T(8,128)(2,1)S(1)} %collective-permute-done.21.refs_2_), channel_id=1, source_target_pairs={{0,2},{1,3},{2,0},{3,1},{4,6},{5,7},{6,4},{7,5},{8,10},{9,11},{10,... | collective-permute-start | bytes 442376 | tf_op jit(solution)/shard_map/ppermute | solution.py:30
  104.0 8.1 %collective-permute-start.29 = (bf16[32,2304]{1,0:T(8,128)(2,1)S(1)}, bf16[32,2304]{1,0:T(8,128)(2,1)S(1)}, u32[]{:S(2)}, u32[]{:S(2)}) collective-permute-start(bf16[32,2304]{1,0:T(8,128)(2,1)S(1)} %get-tuple-element.119.refs_0_), channel_id=1, source_target_pairs={{0,6},{1,7},{2,4},{3,5},{4,2},{5,3},{6,0},{7,1},{8,14},{9,15},{10,... | collective-permute-start | bytes 442376 | tf_op jit(solution)/shard_map/ppermute | solution.py:30
  106.0 12.9 %collective-permute-start.25 = (bf16[32,2304]{1,0:T(8,128)(2,1)S(1)}, bf16[32,2304]{1,0:T(8,128)(2,1)S(1)}, u32[]{:S(2)}, u32[]{:S(2)}) collective-permute-start(bf16[32,2304]{1,0:T(8,128)(2,1)S(1)} %collective-permute-done.21.refs_2_), channel_id=1, source_target_pairs={{0,1},{1,0},{2,3},{3,2},{4,5},{5,4},{6,7},{7,6},{8,9},{9,8},{10,11... | collective-permute-start | bytes 442376 | tf_op jit(solution)/shard_map/ppermute | solution.py:30
  106.0 12.9 %collective-permute-start.24 = (bf16[32,2304]{1,0:T(8,128)(2,1)S(1)}, bf16[32,2304]{1,0:T(8,128)(2,1)S(1)}, u32[]{:S(2)}, u32[]{:S(2)}) collective-permute-start(bf16[32,2304]{1,0:T(8,128)(2,1)S(1)} %collective-permute-done.20.refs_1_), channel_id=1, source_target_pairs={{0,1},{1,0},{2,3},{3,2},{4,5},{5,4},{6,7},{7,6},{8,9},{9,8},{10,11... | collective-permute-start | bytes 442376 | tf_op jit(solution)/shard_map/ppermute | solution.py:30
  109.0 10.4 %collective-permute-start.26 = (bf16[32,2304]{1,0:T(8,128)(2,1)S(1)}, bf16[32,2304]{1,0:T(8,128)(2,1)S(1)}, u32[]{:S(2)}, u32[]{:S(2)}) collective-permute-start(bf16[32,2304]{1,0:T(8,128)(2,1)S(1)} %collective-permute-done.22.refs_3_), channel_id=1, source_target_pairs={{0,1},{1,0},{2,3},{3,2},{4,5},{5,4},{6,7},{7,6},{8,9},{9,8},{10,11... | collective-permute-start | bytes 442376 | tf_op jit(solution)/shard_map/ppermute | solution.py:30
  109.0 22.4 %collective-permute-start.28 = (bf16[32,2304]{1,0:T(8,128)(2,1)S(1)}, bf16[32,2304]{1,0:T(8,128)(2,1)S(1)}, u32[]{:S(2)}, u32[]{:S(2)}) collective-permute-start(bf16[32,2304]{1,0:T(8,128)(2,1)S(1)} %get-tuple-element.119.refs_0_), channel_id=1, source_target_pairs={{0,4},{1,5},{2,6},{3,7},{4,0},{5,1},{6,2},{7,3},{8,12},{9,13},{10,... | collective-permute-start | bytes 442376 | tf_op jit(solution)/shard_map/ppermute | solution.py:30
  112.1 19.2 %collective-permute-start.27 = (bf16[32,2304]{1,0:T(8,128)(2,1)S(1)}, bf16[32,2304]{1,0:T(8,128)(2,1)S(1)}, u32[]{:S(2)}, u32[]{:S(2)}) collective-permute-start(bf16[32,2304]{1,0:T(8,128)(2,1)S(1)} %get-tuple-element.119.refs_0_), channel_id=1, source_target_pairs={{0,2},{1,3},{2,0},{3,1},{4,6},{5,7},{6,4},{7,5},{8,10},{9,11},{10,... | collective-permute-start | bytes 442376 | tf_op jit(solution)/shard_map/ppermute | solution.py:30
  118.8 14.7 %collective-permute-start.30 = (bf16[32,2304]{1,0:T(8,128)(2,1)S(1)}, bf16[32,2304]{1,0:T(8,128)(2,1)S(1)}, u32[]{:S(2)}, u32[]{:S(2)}) collective-permute-start(bf16[32,2304]{1,0:T(8,128)(2,1)S(1)} %get-tuple-element.119.refs_0_), channel_id=1, source_target_pairs={{0,1},{1,0},{2,3},{3,2},{4,5},{5,4},{6,7},{7,6},{8,9},{9,8},{10,11... | collective-permute-start | bytes 442376 | tf_op jit(solution)/shard_map/ppermute | solution.py:30
  118.8 14.7 %collective-permute-start.33 = (bf16[32,2304]{1,0:T(8,128)(2,1)S(1)}, bf16[32,2304]{1,0:T(8,128)(2,1)S(1)}, u32[]{:S(2)}, u32[]{:S(2)}) collective-permute-start(bf16[32,2304]{1,0:T(8,128)(2,1)S(1)} %collective-permute-done.29.refs_3_), channel_id=1, source_target_pairs={{0,1},{1,0},{2,3},{3,2},{4,5},{5,4},{6,7},{7,6},{8,9},{9,8},{10,11... | collective-permute-start | bytes 442376 | tf_op jit(solution)/shard_map/ppermute | solution.py:30
  131.4 20.3 %collective-permute-start.40 = (bf16[2,64,1024]{2,1,0:T(8,128)(2,1)S(1)}, bf16[2,64,1024]{2,1,0:T(8,128)(2,1)S(1)}, u32[]{:S(2)}, u32[]{:S(2)}) collective-permute-start(bf16[2,64,1024]{2,1,0:T(8,128)(2,1)S(1)} %get-tuple-element.139), channel_id=1, source_target_pairs={{0,16},{8,24},{16,0},{24,8},{1,17},{9,25},{17,1},{25,9},{2,18},{10... | collective-permute-start | bytes 786440 | tf_op jit(solution)/shard_map/ppermute | solution.py:30
  131.4 20.4 %collective-permute-start.39 = (bf16[2,64,1024]{2,1,0:T(8,128)(2,1)S(1)}, bf16[2,64,1024]{2,1,0:T(8,128)(2,1)S(1)}, u32[]{:S(2)}, u32[]{:S(2)}) collective-permute-start(bf16[2,64,1024]{2,1,0:T(8,128)(2,1)S(1)} %get-tuple-element.136), channel_id=1, source_target_pairs={{0,8},{8,0},{16,24},{24,16},{1,9},{9,1},{17,25},{25,17},{2,10},{10... | collective-permute-start | bytes 786440 | tf_op jit(solution)/shard_map/ppermute | solution.py:30
  133.3 20.6 %collective-permute-start.41 = (bf16[2,64,1024]{2,1,0:T(8,128)(2,1)S(1)}, bf16[2,64,1024]{2,1,0:T(8,128)(2,1)S(1)}, u32[]{:S(2)}, u32[]{:S(2)}) collective-permute-start(bf16[2,64,1024]{2,1,0:T(8,128)(2,1)S(1)} %get-tuple-element.143), channel_id=1, source_target_pairs={{0,8},{8,0},{16,24},{24,16},{1,9},{9,1},{17,25},{25,17},{2,10},{10... | collective-permute-start | bytes 786440 | tf_op jit(solution)/shard_map/ppermute | solution.py:30
  133.6 1.6 collective-permute-start.31
  135.1 18.9 %collective-permute-start.43 = (bf16[2,64,1024]{2,1,0:T(8,128)(2,1)S(1)}, bf16[2,64,1024]{2,1,0:T(8,128)(2,1)S(1)}, u32[]{:S(2)}, u32[]{:S(2)}) collective-permute-start(bf16[2,64,1024]{2,1,0:T(8,128)(2,1)S(1)} %get-tuple-element.146), channel_id=1, source_target_pairs={{0,16},{8,24},{16,0},{24,8},{1,17},{9,25},{17,1},{25,9},{2,18},{10... | collective-permute-start | bytes 786440 | tf_op jit(solution)/shard_map/ppermute | solution.py:30
  150.3 12.9 %collective-permute-start.36 = (f32[8,128]{1,0:T(8,128)S(1)}, f32[8,128]{1,0:T(8,128)S(1)}, u32[]{:S(2)}, u32[]{:S(2)}) collective-permute-start(f32[8,128]{1,0:T(8,128)S(1)} %broadcast_in_dim.11), channel_id=1, source_target_pairs={{0,24},{8,16},{16,8},{24,0},{1,25},{9,17},{17,9},{25,1},{2,26},{10... | collective-permute-start | bytes 12296 | tf_op jit(solution)/shard_map/ppermute | solution.py:30
  151.7 13.6 %collective-permute-start.35 = (f32[8,128]{1,0:T(8,128)S(1)}, f32[8,128]{1,0:T(8,128)S(1)}, u32[]{:S(2)}, u32[]{:S(2)}) collective-permute-start(f32[8,128]{1,0:T(8,128)S(1)} %broadcast_in_dim.11), channel_id=1, source_target_pairs={{0,16},{8,24},{16,0},{24,8},{1,17},{9,25},{17,1},{25,9},{2,18},{10... | collective-permute-start | bytes 12296 | tf_op jit(solution)/shard_map/ppermute | solution.py:30
  151.9 7.9 %collective-permute-start.37 = (bf16[2,64,1024]{2,1,0:T(8,128)(2,1)S(1)}, bf16[2,64,1024]{2,1,0:T(8,128)(2,1)S(1)}, u32[]{:S(2)}, u32[]{:S(2)}) collective-permute-start(bf16[2,64,1024]{2,1,0:T(8,128)(2,1)S(1)} %get-tuple-element.129), channel_id=1, source_target_pairs={{0,8},{8,0},{16,24},{24,16},{1,9},{9,1},{17,25},{25,17},{2,10},{10... | collective-permute-start | bytes 786440 | tf_op jit(solution)/shard_map/ppermute | solution.py:30
  153.9 9.2 %collective-permute-start.38 = (bf16[2,64,1024]{2,1,0:T(8,128)(2,1)S(1)}, bf16[2,64,1024]{2,1,0:T(8,128)(2,1)S(1)}, u32[]{:S(2)}, u32[]{:S(2)}) collective-permute-start(bf16[2,64,1024]{2,1,0:T(8,128)(2,1)S(1)} %get-tuple-element.131), channel_id=1, source_target_pairs={{0,16},{8,24},{16,0},{24,8},{1,17},{9,25},{17,1},{25,9},{2,18},{10... | collective-permute-start | bytes 786440 | tf_op jit(solution)/shard_map/ppermute | solution.py:30
  154.0 14.7 %collective-permute-start.42 = (bf16[2,64,1024]{2,1,0:T(8,128)(2,1)S(1)}, bf16[2,64,1024]{2,1,0:T(8,128)(2,1)S(1)}, u32[]{:S(2)}, u32[]{:S(2)}) collective-permute-start(bf16[2,64,1024]{2,1,0:T(8,128)(2,1)S(1)} %add_convert_fusion.1), channel_id=1, source_target_pairs={{0,16},{8,24},{16,0},{24,8},{1,17},{9,25},{17,1},{25,9},{2,18},{10... | collective-permute-start | bytes 786440 | tf_op jit(solution)/shard_map/ppermute | solution.py:30
  159.8 9.2 %collective-permute-start.44 = (bf16[2,64,1024]{2,1,0:T(8,128)(2,1)S(1)}, bf16[2,64,1024]{2,1,0:T(8,128)(2,1)S(1)}, u32[]{:S(2)}, u32[]{:S(2)}) collective-permute-start(bf16[2,64,1024]{2,1,0:T(8,128)(2,1)S(1)} %add_convert_fusion), channel_id=1, source_target_pairs={{0,8},{8,0},{16,24},{24,16},{1,9},{9,1},{17,25},{25,17},{2,10},{10... | collective-permute-start | bytes 786440 | tf_op jit(solution)/shard_map/ppermute | solution.py:30
  163.1 9.7 %collective-permute-start.34 = (f32[8,128]{1,0:T(8,128)S(1)}, f32[8,128]{1,0:T(8,128)S(1)}, u32[]{:S(2)}, u32[]{:S(2)}) collective-permute-start(f32[8,128]{1,0:T(8,128)S(1)} %broadcast_in_dim.11), channel_id=1, source_target_pairs={{0,8},{8,0},{16,24},{24,16},{1,9},{9,1},{17,25},{25,17},{2,10},{10... | collective-permute-start | bytes 12296 | tf_op jit(solution)/shard_map/ppermute | solution.py:30
  163.3 11.5 %collective-permute-start.45 = (bf16[2,64,1024]{2,1,0:T(8,128)(2,1)S(1)}, bf16[2,64,1024]{2,1,0:T(8,128)(2,1)S(1)}, u32[]{:S(2)}, u32[]{:S(2)}) collective-permute-start(bf16[2,64,1024]{2,1,0:T(8,128)(2,1)S(1)} %get-tuple-element.155), channel_id=1, source_target_pairs={{0,8},{8,0},{16,24},{24,16},{1,9},{9,1},{17,25},{25,17},{2,10},{10... | collective-permute-start | bytes 786440 | tf_op jit(solution)/shard_map/ppermute | solution.py:30
  165.3 9.5 %collective-permute-start.47 = (bf16[2,64,1024]{2,1,0:T(8,128)(2,1)S(1)}, bf16[2,64,1024]{2,1,0:T(8,128)(2,1)S(1)}, u32[]{:S(2)}, u32[]{:S(2)}) collective-permute-start(bf16[2,64,1024]{2,1,0:T(8,128)(2,1)S(1)} %add_convert_fusion.3), channel_id=1, source_target_pairs={{0,16},{8,24},{16,0},{24,8},{1,17},{9,25},{17,1},{25,9},{2,18},{10... | collective-permute-start | bytes 786440 | tf_op jit(solution)/shard_map/ppermute | solution.py:30
  168.7 9.4 %collective-permute-start.46 = (bf16[2,64,1024]{2,1,0:T(8,128)(2,1)S(1)}, bf16[2,64,1024]{2,1,0:T(8,128)(2,1)S(1)}, u32[]{:S(2)}, u32[]{:S(2)}) collective-permute-start(bf16[2,64,1024]{2,1,0:T(8,128)(2,1)S(1)} %get-tuple-element.157), channel_id=1, source_target_pairs={{0,16},{8,24},{16,0},{24,8},{1,17},{9,25},{17,1},{25,9},{2,18},{10... | collective-permute-start | bytes 786440 | tf_op jit(solution)/shard_map/ppermute | solution.py:30
  169.1 9.1 %collective-permute-start.48 = (bf16[2,64,1024]{2,1,0:T(8,128)(2,1)S(1)}, bf16[2,64,1024]{2,1,0:T(8,128)(2,1)S(1)}, u32[]{:S(2)}, u32[]{:S(2)}) collective-permute-start(bf16[2,64,1024]{2,1,0:T(8,128)(2,1)S(1)} %add_convert_fusion.2), channel_id=1, source_target_pairs={{0,8},{8,0},{16,24},{24,16},{1,9},{9,1},{17,25},{25,17},{2,10},{10... | collective-permute-start | bytes 786440 | tf_op jit(solution)/shard_map/ppermute | solution.py:30
  (20 other events, 320.3 us)

commit v11 on v10

--- a/solution.py
+++ b/solution.py
@@ -66,8 +66,8 @@
         return kept
 
 
-def streamed(count, slots, copies_of, body):
-    early = min(2, slots - 1, count)
+def streamed(count, slots, copies_of, body, first):
+    early = min(first, slots - 1, count)
     for i in range(early):
         for copy in copies_of(i, i):
             copy.start()
@@ -198,81 +198,68 @@
 
 def decode_kernel(plan, index_ref, *refs):
     n_in = plan.groups * plan.sources
-    pieces, w_ref, outs = refs[:n_in], refs[n_in], refs[n_in + 1:-5]
-    x_buf, w_buf, total, x_sem, w_sem = refs[-5:]
+    pieces, w_ref, outs = refs[:n_in], refs[n_in], refs[n_in + 1:-4]
+    x_buf, w_buf, x_sem, w_sem = refs[-4:]
     half = plan.tokens // 2
     core = index_ref[0]
     tile = w_buf.shape[2]
 
-    placing = [[] for _ in range(plan.sources)]
-    for s in range(plan.sources):
-        for j in range(plan.groups):
-            for b in range(plan.pairs):
-                place = index_ref[1 + plan.sources + j * plan.pairs + b] * plan.rows_feat
-                for owner in range(2):
-                    to = pl.multiple_of(place + jnp.where(core == owner, half, 0), ROW_TILE)
-                    placing[s].append(pltpu.make_async_copy(
+    placing = []
+    for j in range(plan.groups):
+        for b in range(plan.pairs):
+            place = index_ref[1 + plan.sources + j * plan.pairs + b] * plan.rows_feat
+            for owner in range(2):
+                to = pl.multiple_of(place + jnp.where(core == owner, half, 0), ROW_TILE)
+                for s in range(plan.sources):
+                    placing.append(pltpu.make_async_copy(
                         pieces[s * plan.groups + j].at[
                             pl.ds((2 * b + owner) * plan.rows_feat, plan.rows_feat)
                         ],
-                        x_buf.at[s, pl.ds(to, plan.rows_feat)],
-                        x_sem.at[s, len(placing[s])],
+                        x_buf.at[
+                            pl.ds(to, plan.rows_feat), pl.ds(s * plan.width, plan.width)
+                        ],
+                        x_sem.at[len(placing)],
                     ))
-    for copies in placing:
-        for copy in copies:
-            copy.start()
-
-    def columns(i):
-        return pl.ds(pl.multiple_of(lax.div(i, plan.sources) * tile, tile), tile)
+    for copy in placing:
+        copy.start()
 
     def copies_of(i, slot):
-        return [pltpu.make_async_copy(
-            w_ref.at[lax.rem(i, plan.sources), 0, :, columns(i)], w_buf.at[slot], w_sem.at[slot]
-        )]
+        cols = pl.ds(pl.multiple_of(i * tile, tile), tile)
+        return [
+            pltpu.make_async_copy(
+                w_ref.at[s, 0, :, cols],
+                w_buf.at[slot, pl.ds(s * plan.width, plan.width)],
+                w_sem.at[slot, s],
+            )
+            for s in range(plan.sources)
+        ]
 
     def step(i, slot):
-        source = lax.rem(i, plan.sources)
-        for s in range(plan.sources):
-            @pl.when(i == s)
-            def _(s=s):
-                for copy in placing[s]:
-                    copy.wait()
-
+        @pl.when(i == 0)
+        def _():
+            for copy in placing:
+                copy.wait()
+            for s in range(plan.sources):
                 @pl.when(index_ref[1 + s] == 0)
-                def _():
-                    x_buf[s] = jnp.zeros(x_buf.shape[1:], BF16)
-
-        product = jnp.dot(x_buf[source], w_buf[slot], preferred_element_type=F32)
-
-        @pl.when(source == 0)
-        def _():
-            total[...] = product
-
-        @pl.when((source > 0) & (source < plan.sources - 1))
-        def _():
-            total[...] = total[...] + product
-
-        @pl.when(source == plan.sources - 1)
-        def _():
-            cols = columns(i)
-            for c in range(plan.chunks):
-                for d in range(plan.depth):
-                    first = d * plan.rows_feat + c * plan.piece
-                    last = half + first
-                    to = slice(d * plan.piece, (d + 1) * plan.piece)
-                    outs[c][to, cols] = (
-                        total[first:first + plan.piece] + product[first:first + plan.piece]
-                    ).astype(BF16)
-                    outs[plan.chunks + c][to, cols] = (
-                        total[last:last + plan.piece] + product[last:last + plan.piece]
+                def _(s=s):
+                    x_buf[:, s * plan.width:(s + 1) * plan.width] = jnp.zeros(
+                        (plan.tokens, plan.width), BF16
                     )
 
-    count = plan.model // tile * plan.sources
-    streamed(count, w_buf.shape[0], copies_of, step)
+        cols = pl.ds(pl.multiple_of(i * tile, tile), tile)
+        product = jnp.dot(x_buf[...], w_buf[slot], preferred_element_type=F32)
+        for c in range(plan.chunks):
+            for d in range(plan.depth):
+                first = d * plan.rows_feat + c * plan.piece
+                to = slice(d * plan.piece, (d + 1) * plan.piece)
+                outs[c][to, cols] = product[first:first + plan.piece].astype(BF16)
+                outs[plan.chunks + c][to, cols] = product[half + first:half + first + plan.piece]
+
+    streamed(plan.model // tile, w_buf.shape[0], copies_of, step, 1)
 
 
 def decode(plan, index, pieces, w_dec):
-    tile = pick_tile(plan.model, 768)
+    tile = pick_tile(plan.model, 256)
     shape = (plan.depth * plan.piece, plan.model)
     outs = call(
         partial(decode_kernel, plan),
@@ -281,11 +268,10 @@
         [jax.ShapeDtypeStruct(shape, BF16)] * plan.chunks
         + [jax.ShapeDtypeStruct(shape, F32)] * plan.chunks,
         [
-            pltpu.VMEM((plan.sources, plan.tokens, plan.width), BF16),
-            pltpu.VMEM((WEIGHT_SLOTS, plan.width, tile), BF16),
-            pltpu.VMEM((plan.tokens, tile), F32),
-            pltpu.SemaphoreType.DMA((plan.sources, plan.groups * plan.per_group)),
-            pltpu.SemaphoreType.DMA((WEIGHT_SLOTS,)),
+            pltpu.VMEM((plan.tokens, plan.sources * plan.width), BF16),
+            pltpu.VMEM((WEIGHT_SLOTS, plan.sources * plan.width, tile), BF16),
+            pltpu.SemaphoreType.DMA((len(pieces) * plan.per_group,)),
+            pltpu.SemaphoreType.DMA((WEIGHT_SLOTS, plan.sources)),
         ],
         (index, *pieces, w_dec),
         vmem=MOST_VMEM_BYTES,
@@ -314,19 +300,10 @@
     for copy in placing:
         copy.start()
     def copies_of(i, slot):
-        part = depth // 4
-        return [
-            pltpu.make_async_copy(
-                w_ref.at[
-                    lax.div(i, steps),
-                    0,
-                    pl.ds(pl.multiple_of(lax.rem(i, steps) * depth + p * part, part), part),
-                ],
-                w_buf.at[slot, pl.ds(p * part, part)],
-                w_sem.at[slot, p],
-            )
-            for p in range(4)
-        ]
+        rows = pl.ds(pl.multiple_of(lax.rem(i, steps) * depth, depth), depth)
+        return [pltpu.make_async_copy(
+            w_ref.at[lax.div(i, steps), 0, rows], w_buf.at[slot], w_sem.at[slot]
+        )]
 
     half = plan.groups // 2
 
@@ -353,7 +330,7 @@
                     away[p][source - lo, :, cols] = product[far:far + plan.block].astype(BF16)
                     keep[p][source - lo, :, cols] = product[j * plan.block:(j + 1) * plan.block]
 
-    streamed(plan.sources * steps, w_buf.shape[0], copies_of, step)
+    streamed(plan.sources * steps, w_buf.shape[0], copies_of, step, 3)
 
     def add_squares(i, total):
         rows = pl.ds(pl.multiple_of(i * ROW_TILE, ROW_TILE), ROW_TILE)
@@ -386,7 +363,7 @@
             pltpu.VMEM((plan.chunk_rows, plan.model), BF16),
             pltpu.VMEM((WEIGHT_SLOTS, depth, plan.model), BF16),
             pltpu.SemaphoreType.DMA((len(errors),)),
-            pltpu.SemaphoreType.DMA((WEIGHT_SLOTS, 4)),
+            pltpu.SemaphoreType.DMA((WEIGHT_SLOTS,)),
         ],
         (index, *errors, w_dec),
     )
@@ -483,7 +460,7 @@
             forwarded += [held[j] for j in range(groups) if j & (j - 1)]
 
     sends, keeps = decode(plan, index, after(pieces, [active]), w_dec)
-    recon_parts, errors, first_errors = [], [], []
+    recon_parts, errors, first_errors, earlier = [], [], [], []
     for c in range(chunks):
         other = swap(sends[c], "feat", feats, 1)
         held = {
@@ -491,10 +468,15 @@
             + other[d * plan.piece:(d + 1) * plan.piece].astype(F32)
             for d in range(plan.depth)
         }
-        for bit in plan.level_bits:
+        for step, bit in enumerate(plan.level_bits):
             away = {d: held.pop(d).astype(BF16) for d in sorted(held, reverse=True) if d & bit}
-            for d, x in away.items():
-                held[d ^ bit] = held[d ^ bit] + swap(x, "feat", feats, 2 * bit).astype(F32)
+            wait = earlier if not step else [e[0] for e in errors]
+            away = dict(zip(away, after(away.values(), wait)))
+            got = {d: swap(x, "feat", feats, 2 * bit) for d, x in away.items()}
+            if not step:
+                earlier = list(got.values())[:1]
+            for d, x in got.items():
+                held[d ^ bit] = held[d ^ bit] + x.astype(F32)
         recon_rows, = after([held[0]], [e[0] for e in errors])
 
         first = feat * plan.rows_feat + c * plan.piece
@@ -512,19 +494,20 @@
                     {d | bit: swap(x, "feat", feats, 2 * bit) for d, x in list(held.items())}
                 )
         first_errors.append([held[d] for d in range(1, plan.depth)])
-        every = [held[d] for d in range(plan.depth)]
-        errors.append(every + [swap(e, "feat", feats, 1) for e in every])
+        errors.append([held[d] for d in range(plan.depth)])
 
     squares = jnp.zeros((8, 128), F32)
     totals, results = [], []
     for c in range(chunks):
-        ready = after(errors[c], [e[0] for e in errors[c + 1:c + 2]] + totals[-1:])
+        every = after(errors[c], totals[-1:])
+        every += [swap(x, "feat", feats, 1) for x in every]
+        ready = after(every, [e[0] for e in errors[c + 1:c + 2]])
         lanes, total = gradient(plan, index, ready, w_dec)
         totals.append(total)
         squares = squares + total
         results.append(lanes)
 
-    unfinished = []
+    unfinished, seconds = [], []
     for c, lanes in enumerate(results):
         earlier = [x for each in first_errors[c + 1:c + 2] for x in each]
         first_step = []
@@ -551,12 +534,14 @@
             kept_all.append(kept[0])
         got_all = [own[i] for i in range(1, len(kept_all[0])) for own in kept_all]
         unfinished.append(([own[0] for own in kept_all], got_all))
+        seconds.append(second)
 
     feat_grad = None
     for c, (kept, got) in enumerate(unfinished):
         before_last = feat_grad
         feat_grad = finish(plan, c, kept, got, feat_grad)
 
+    squares, = after([squares], seconds[0])
     loss = jnp.full((8, 128), jnp.sum(squares), F32)
     parts = [loss] + [swap(loss, "grp", groups, j) for j in range(1, groups)]
     parts = after(parts, second + ([] if before_last is None else [before_last]))

time: 181 us -> 171 us (0.945)
  waiting for transfers between devices: 58.2 us -> 49.6 us
  starting transfers between devices: 50.5 us -> 44.4 us
  other arithmetic: 5.88 us -> 11.9 us
    ppermute x49, waiting for transfers between devices: 58.2 us -> 49.6 us  [swap(): return lax.ppermute(x, axis, [(i, i ^ offset) for i in range(size)])]
    ppermute x49, starting transfers between devices: 50.5 us -> 44.4 us  [swap(): return lax.ppermute(x, axis, [(i, i ^ offset) for i in range(size)])]
    convert_element_type x4, other arithmetic: 0.21 us -> 3.59 us  [per_device(): sum((x.astype(F32) for x in own)).astype(BF16)]
  transfers between devices with their start and end apart: 49 -> 49, of which waited for: 20 -> 19; matrix products, arithmetic and copies ran while one was open for 4% -> 7% of each run, Pallas kernels for 18% -> 19%
where the time goes in v11:
time: 171 us; the launch traced here: 170 us
  Pallas kernels  57.2 us (33%)
  waiting for transfers between devices  49.6 us (29%)
  starting transfers between devices  44.4 us (26%)
  other arithmetic  11.9 us (7%)
  local copies, waits for them, and re-layouts  4.49 us (3%)
  between operations  2.83 us (2%)
    pallas_call x8, Pallas kernels, call(): pl.pallas_call(kernel, in_specs=in_specs, out_shape=out_shape, scratch_sh...  57.2 us
    ppermute x49, waiting for transfers between devices, swap(): return lax.ppermute(x, axis, [(i, i ^ offset) for i in range(size)])  49.6 us
    ppermute x49, starting transfers between devices, swap(): return lax.ppermute(x, axis, [(i, i ^ offset) for i in range(size)])  44.4 us
    convert_element_type x4, other arithmetic, per_device(): sum((x.astype(F32) for x in own)).astype(BF16)  3.59 us
  transfers between devices with their start and end apart: 49, of which 19 were waited for; matrix products, arithmetic and copies ran while one was open for 7% of the time, Pallas kernels for 19%

profile of v11, /device:TPU:0, one launch (start us, length us, event | category | flops | bytes accessed | tf_op | source)
XLA Modules:
  0.0 170.4 jit_solution(15375511303802071745)
XLA Ops:
  0.6 5.5 %encode.2 = (bf16[128,1024]{1,0:T(8,128)(2,1)}, bf16[128,1024]{1,0:T(8,128)(2,1)}) custom-call(bf16[4,128,2304]{2,1,0:T(8,128)(2,1)} %resid_ref.3, bf16[4,2304,1024]{2,1,0:T(8,128)(2,1)} %w_ref.3, f32[4,1024]{1,0:T(4,128)} %b_ref.3), custom_call_target="tpu_custom_call" | custom-call | flops 1048576 | bytes 1024 | tf_op jit(solution)/shard_map/encode/pallas_call | solution.py:103
  6.1 3.0 %collective-permute-start = (bf16[128,1024]{1,0:T(8,128)(2,1)}, bf16[128,1024]{1,0:T(8,128)(2,1)S(1)}, u32[]{:S(2)}, u32[]{:S(2)}) collective-permute-start(bf16[128,1024]{1,0:T(8,128)(2,1)} %get-tuple-element.89.refs_0_), channel_id=1, source_target_pairs={{0,8},{8,0},{16,24},{24,16},{1,9},{9,1},{17,25},{25,17},{2,10},{10... | collective-permute-start | bytes 786440 | tf_op jit(solution)/shard_map/ppermute | solution.py:30
  9.1 1.5 collective-permute-start.4
  11.3 5.5 %encode.3 = (bf16[128,1024]{1,0:T(8,128)(2,1)}, bf16[128,1024]{1,0:T(8,128)(2,1)}) custom-call(bf16[4,128,2304]{2,1,0:T(8,128)(2,1)} %resid_ref.3, bf16[4,2304,1024]{2,1,0:T(8,128)(2,1)} %w_ref.3, f32[4,1024]{1,0:T(4,128)} %b_ref.3), custom_call_target="tpu_custom_call" | custom-call | flops 1048576 | bytes 1024 | tf_op jit(solution)/shard_map/encode/pallas_call | solution.py:103
  16.8 1.8 %collective-permute-done.4.refs_6_ = bf16[128,1024]{1,0:T(8,128)(2,1)S(1)} collective-permute-done((bf16[128,1024]{1,0:T(8,128)(2,1)}, bf16[128,1024]{1,0:T(8,128)(2,1)S(1)}, u32[]{:S(2)}, u32[]{:S(2)}) %collective-permute-start.4) | collective-permute-done | bytes 262176 | tf_op jit(solution)/shard_map/ppermute | solution.py:30
  18.6 1.5 collective-permute-start.2
  20.8 3.4 %collective-permute-done.1.refs_2_ = bf16[128,1024]{1,0:T(8,128)(2,1)S(1)} collective-permute-done((bf16[128,1024]{1,0:T(8,128)(2,1)}, bf16[128,1024]{1,0:T(8,128)(2,1)S(1)}, u32[]{:S(2)}, u32[]{:S(2)}) %collective-permute-start.1) | collective-permute-done | bytes 262176 | tf_op jit(solution)/shard_map/ppermute | solution.py:30
  24.3 2.0 %collective-permute-start.7 = (bf16[128,1024]{1,0:T(8,128)(2,1)}, bf16[128,1024]{1,0:T(8,128)(2,1)S(1)}, u32[]{:S(2)}, u32[]{:S(2)}) collective-permute-start(bf16[128,1024]{1,0:T(8,128)(2,1)} %get-tuple-element.97.refs_2_.refs_8_), channel_id=1, source_target_pairs={{0,16},{8,24},{16,0},{24,8},{1,17},{9,25},{17,1},{25,9},{2,18},{10... | collective-permute-start | bytes 786440 | tf_op jit(solution)/shard_map/ppermute | solution.py:30
  26.2 3.6 %collective-permute-done.2.refs_3_ = bf16[128,1024]{1,0:T(8,128)(2,1)S(1)} collective-permute-done((bf16[128,1024]{1,0:T(8,128)(2,1)S(1)}, bf16[128,1024]{1,0:T(8,128)(2,1)S(1)}, u32[]{:S(2)}, u32[]{:S(2)}) %collective-permute-start.2) | collective-permute-done | bytes 262176 | tf_op jit(solution)/shard_map/ppermute | solution.py:30
  29.9 5.5 %collective-permute-done.10.refs_14_ = bf16[128,1024]{1,0:T(8,128)(2,1)S(1)} collective-permute-done((bf16[128,1024]{1,0:T(8,128)(2,1)}, bf16[128,1024]{1,0:T(8,128)(2,1)S(1)}, u32[]{:S(2)}, u32[]{:S(2)}) %collective-permute-start.10) | collective-permute-done | bytes 262176 | tf_op jit(solution)/shard_map/ppermute | solution.py:30
  35.4 1.6 collective-permute-start.8
  40.1 1.7 %arrange.1 = bf16[128,4,1024]{2,1,0:T(4,128)(2,1)} custom-call(bf16[128,1024]{1,0:T(8,128)(2,1)S(1)} %copy-done, bf16[128,1024]{1,0:T(8,128)(2,1)S(1)} %copy-done.1, bf16[128,1024]{1,0:T(8,128)(2,1)S(1)} %copy-done.2, bf16[128,1024]{1,0:T(8,128)(2,1)S(1)} %copy-done.3), custom_call_target="tpu_custom_call" | custom-call | flops 1048576 | bytes 1024 | tf_op jit(solution)/shard_map/arrange/pallas_call | solution.py:103
  41.9 3.3 %collective-permute-done.8.refs_11_ = bf16[128,1024]{1,0:T(8,128)(2,1)S(1)} collective-permute-done((bf16[128,1024]{1,0:T(8,128)(2,1)S(1)}, bf16[128,1024]{1,0:T(8,128)(2,1)S(1)}, u32[]{:S(2)}, u32[]{:S(2)}) %collective-permute-start.8) | collective-permute-done | bytes 262176 | tf_op jit(solution)/shard_map/ppermute | solution.py:30
  45.9 17.6 %decode.1 = (bf16[128,2304]{1,0:T(8,128)(2,1)}, bf16[128,2304]{1,0:T(8,128)(2,1)}, f32[128,2304]{1,0:T(8,128)}, f32[128,2304]{1,0:T(8,128)}) custom-call(s32[17]{0:T(128)} %concatenate.6.index_ref, bf16[128,1024]{1,0:T(8,128)(2,1)} %get-tuple-element.89.refs_0_, bf16[128,1024]{1,0:T(8,128)(2,1)} %copy-done.14, bf16[128,1024]{1,0:T(8,128)(2,1)} %copy-done.16, ...), custom_call_target="tpu_custom_call" | custom-call | flops 1048576 | bytes 1024 | tf_op jit(solution)/shard_map/decode/pallas_call | solution.py:103
  63.6 2.2 %collective-permute-done.12 = bf16[128,2304]{1,0:T(8,128)(2,1)S(1)} collective-permute-done((bf16[128,2304]{1,0:T(8,128)(2,1)}, bf16[128,2304]{1,0:T(8,128)(2,1)S(1)}, u32[]{:S(2)}, u32[]{:S(2)}) %collective-permute-start.12) | collective-permute-done | bytes 589856 | tf_op jit(solution)/shard_map/ppermute | solution.py:30
  65.8 1.1 add_convert_fusion.9
  66.9 1.6 collective-permute-start.14
  69.0 4.7 %collective-permute-done.14 = bf16[32,2304]{1,0:T(8,128)(2,1)S(1)} collective-permute-done((bf16[32,2304]{1,0:T(8,128)(2,1)S(1)}, bf16[32,2304]{1,0:T(8,128)(2,1)S(1)}, u32[]{:S(2)}, u32[]{:S(2)}) %collective-permute-start.14) | collective-permute-done | bytes 147488 | tf_op jit(solution)/shard_map/ppermute | solution.py:30
  73.7 1.0 add_convert_fusion.7
  74.7 2.7 %collective-permute-start.15 = (bf16[32,2304]{1,0:T(8,128)(2,1)S(1)}, bf16[32,2304]{1,0:T(8,128)(2,1)S(1)}, u32[]{:S(2)}, u32[]{:S(2)}) collective-permute-start(bf16[32,2304]{1,0:T(8,128)(2,1)S(1)} %add_convert_fusion.7), channel_id=1, source_target_pairs={{0,4},{1,5},{2,6},{3,7},{4,0},{5,1},{6,2},{7,3},{8,12},{9,13},{10,... | collective-permute-start | bytes 442376 | tf_op jit(solution)/shard_map/ppermute | solution.py:30
  77.4 1.6 collective-permute-start.17
  79.5 3.2 %collective-permute-done.15 = bf16[32,2304]{1,0:T(8,128)(2,1)S(1)} collective-permute-done((bf16[32,2304]{1,0:T(8,128)(2,1)S(1)}, bf16[32,2304]{1,0:T(8,128)(2,1)S(1)}, u32[]{:S(2)}, u32[]{:S(2)}) %collective-permute-start.15) | collective-permute-done | bytes 147488 | tf_op jit(solution)/shard_map/ppermute | solution.py:30
  82.7 1.7 %fusion.3 = (bf16[32,2304]{1,0:T(8,128)(2,1)}, bf16[32,2304]{1,0:T(8,128)(2,1)S(1)}) fusion(bf16[32,2304]{1,0:T(8,128)(2,1)S(1)} %collective-permute-done.15, bf16[32,2304]{1,0:T(8,128)(2,1)S(1)} %collective-permute-done.13, bf16[128,2304]{1,0:T(8,128)(2,1)S(1)} %collective-permute-done.12, f32[128,2304]{1,0:T(8,128)} %get-tuple-element.105, ...), kind=kLoop, calls=%fused_computation.20 | loop fusion | flops 737280 | bytes 1179652 | tf_op jit(solution)/shard_map/convert_element_type | solution.py:485
  84.4 2.3 %collective-permute-start.21 = (bf16[32,2304]{1,0:T(8,128)(2,1)S(1)}, bf16[32,2304]{1,0:T(8,128)(2,1)S(1)}, u32[]{:S(2)}, u32[]{:S(2)}) collective-permute-start(bf16[32,2304]{1,0:T(8,128)(2,1)S(1)} %get-tuple-element.113.refs_0_), channel_id=1, source_target_pairs={{0,4},{1,5},{2,6},{3,7},{4,0},{5,1},{6,2},{7,3},{8,12},{9,13},{10,... | collective-permute-start | bytes 442376 | tf_op jit(solution)/shard_map/ppermute | solution.py:30
  86.8 1.3 collective-permute-done.18
  88.3 2.2 %collective-permute-start.20 = (bf16[32,2304]{1,0:T(8,128)(2,1)S(1)}, bf16[32,2304]{1,0:T(8,128)(2,1)S(1)}, u32[]{:S(2)}, u32[]{:S(2)}) collective-permute-start(bf16[32,2304]{1,0:T(8,128)(2,1)S(1)} %get-tuple-element.113.refs_0_), channel_id=1, source_target_pairs={{0,2},{1,3},{2,0},{3,1},{4,6},{5,7},{6,4},{7,5},{8,10},{9,11},{10,... | collective-permute-start | bytes 442376 | tf_op jit(solution)/shard_map/ppermute | solution.py:30
  90.4 6.9 %collective-permute-done.21.refs_2_ = bf16[32,2304]{1,0:T(8,128)(2,1)S(1)} collective-permute-done((bf16[32,2304]{1,0:T(8,128)(2,1)S(1)}, bf16[32,2304]{1,0:T(8,128)(2,1)S(1)}, u32[]{:S(2)}, u32[]{:S(2)}) %collective-permute-start.21) | collective-permute-done | bytes 147488 | tf_op jit(solution)/shard_map/ppermute | solution.py:30
  97.4 1.6 collective-permute-done.19
  99.6 2.9 %collective-permute-done.22.refs_3_ = bf16[32,2304]{1,0:T(8,128)(2,1)S(1)} collective-permute-done((bf16[32,2304]{1,0:T(8,128)(2,1)S(1)}, bf16[32,2304]{1,0:T(8,128)(2,1)S(1)}, u32[]{:S(2)}, u32[]{:S(2)}) %collective-permute-start.22) | collective-permute-done | bytes 147488 | tf_op jit(solution)/shard_map/ppermute | solution.py:30
  102.5 1.6 fusion
  104.1 4.8 %collective-permute-start.29 = (bf16[32,2304]{1,0:T(8,128)(2,1)S(1)}, bf16[32,2304]{1,0:T(8,128)(2,1)S(1)}, u32[]{:S(2)}, u32[]{:S(2)}) collective-permute-start(bf16[32,2304]{1,0:T(8,128)(2,1)S(1)} %get-tuple-element.122.refs_0_), channel_id=1, source_target_pairs={{0,6},{1,7},{2,4},{3,5},{4,2},{5,3},{6,0},{7,1},{8,14},{9,15},{10,... | collective-permute-start | bytes 442376 | tf_op jit(solution)/shard_map/ppermute | solution.py:30
  109.5 11.8 %gradient.2 = (bf16[2,64,1024]{2,1,0:T(8,128)(2,1)S(1)}, bf16[2,64,1024]{2,1,0:T(8,128)(2,1)S(1)}, f32[2,64,1024]{2,1,0:T(8,128)S(1)}, f32[2,64,1024]{2,1,0:T(8,...) custom-call(s32[17]{0:T(128)S(1)} %copy-done.6, ...), custom_call_target="tpu_custom_call" | custom-call | flops 1048576 | bytes 1024 | tf_op jit(solution)/shard_map/gradient/pallas_call | solution.py:103
  121.9 1.5 collective-permute-start.36
  125.8 1.5 collective-permute-start.34
  127.3 12.5 %gradient.3 = (bf16[2,64,1024]{2,1,0:T(8,128)(2,1)}, bf16[2,64,1024]{2,1,0:T(8,128)(2,1)S(1)}, f32[2,64,1024]{2,1,0:T(8,128)S(1)}, f32[2,64,1024]{2,1,0:T(8,128)...) custom-call(s32[17]{0:T(128)S(1)} %copy-done.6, ...), custom_call_target="tpu_custom_call" | custom-call | flops 1048576 | bytes 1024 | tf_op jit(solution)/shard_map/gradient/pallas_call | solution.py:103
  141.0 1.5 collective-permute-start.42
  144.2 1.3 reduce_sum.9
  146.2 1.5 collective-permute-start.40
  147.7 1.5 collective-permute-start.39
  150.3 1.0 add_convert_fusion.1
  151.3 1.6 collective-permute-start.38
  152.8 1.0 add_convert_fusion
  154.5 1.5 collective-permute-start.47
  156.0 2.0 %collective-permute-done.43.refs_4_ = bf16[2,64,1024]{2,1,0:T(8,128)(2,1)S(1)} collective-permute-done((bf16[2,64,1024]{2,1,0:T(8,128)(2,1)}, bf16[2,64,1024]{2,1,0:T(8,128)(2,1)S(1)}, u32[]{:S(2)}, u32[]{:S(2)}) %collective-permute-start.43) | collective-permute-done | bytes 262176 | tf_op jit(solution)/shard_map/ppermute | solution.py:30
  160.3 1.3 finish.2.refs_6_
  162.8 1.8 %collective-permute-done.45.refs_2_ = bf16[2,64,1024]{2,1,0:T(8,128)(2,1)S(1)} collective-permute-done((bf16[2,64,1024]{2,1,0:T(8,128)(2,1)S(1)}, bf16[2,64,1024]{2,1,0:T(8,128)(2,1)S(1)}, u32[]{:S(2)}, u32[]{:S(2)}) %collective-permute-start.45) | collective-permute-done | bytes 262176 | tf_op jit(solution)/shard_map/ppermute | solution.py:30
  164.6 3.1 %collective-permute-done.46.refs_3_ = bf16[2,64,1024]{2,1,0:T(8,128)(2,1)S(1)} collective-permute-done((bf16[2,64,1024]{2,1,0:T(8,128)(2,1)S(1)}, bf16[2,64,1024]{2,1,0:T(8,128)(2,1)S(1)}, u32[]{:S(2)}, u32[]{:S(2)}) %collective-permute-start.46) | collective-permute-done | bytes 262176 | tf_op jit(solution)/shard_map/ppermute | solution.py:30
  168.0 1.3 finish.3
  (129 shorter events, 18.9 us)
Async XLA Ops:
  6.1 10.6 %collective-permute-start = (bf16[128,1024]{1,0:T(8,128)(2,1)}, bf16[128,1024]{1,0:T(8,128)(2,1)S(1)}, u32[]{:S(2)}, u32[]{:S(2)}) collective-permute-start(bf16[128,1024]{1,0:T(8,128)(2,1)} %get-tuple-element.89.refs_0_), channel_id=1, source_target_pairs={{0,8},{8,0},{16,24},{24,16},{1,9},{9,1},{17,25},{25,17},{2,10},{10... | collective-permute-start | bytes 786440 | tf_op jit(solution)/shard_map/ppermute | solution.py:30
  9.1 9.4 %collective-permute-start.4 = (bf16[128,1024]{1,0:T(8,128)(2,1)}, bf16[128,1024]{1,0:T(8,128)(2,1)S(1)}, u32[]{:S(2)}, u32[]{:S(2)}) collective-permute-start(bf16[128,1024]{1,0:T(8,128)(2,1)} %get-tuple-element.93.refs_1_.refs_4_), channel_id=1, source_target_pairs={{0,16},{8,24},{16,0},{24,8},{1,17},{9,25},{17,1},{25,9},{2,18},{10... | collective-permute-start | bytes 786440 | tf_op jit(solution)/shard_map/ppermute | solution.py:30
  10.6 13.5 %collective-permute-start.1 = (bf16[128,1024]{1,0:T(8,128)(2,1)}, bf16[128,1024]{1,0:T(8,128)(2,1)S(1)}, u32[]{:S(2)}, u32[]{:S(2)}) collective-permute-start(bf16[128,1024]{1,0:T(8,128)(2,1)} %get-tuple-element.89.refs_0_), channel_id=1, source_target_pairs={{0,16},{8,24},{16,0},{24,8},{1,17},{9,25},{17,1},{25,9},{2,18},{10... | collective-permute-start | bytes 786440 | tf_op jit(solution)/shard_map/ppermute | solution.py:30
  11.2 13.1 %collective-permute-start.3 = (bf16[128,1024]{1,0:T(8,128)(2,1)}, bf16[128,1024]{1,0:T(8,128)(2,1)S(1)}, u32[]{:S(2)}, u32[]{:S(2)}) collective-permute-start(bf16[128,1024]{1,0:T(8,128)(2,1)} %get-tuple-element.93.refs_1_.refs_4_), channel_id=1, source_target_pairs={{0,8},{8,0},{16,24},{24,16},{1,9},{9,1},{17,25},{25,17},{2,10},{10... | collective-permute-start | bytes 786440 | tf_op jit(solution)/shard_map/ppermute | solution.py:30
  18.6 11.2 %collective-permute-start.2 = (bf16[128,1024]{1,0:T(8,128)(2,1)S(1)}, bf16[128,1024]{1,0:T(8,128)(2,1)S(1)}, u32[]{:S(2)}, u32[]{:S(2)}) collective-permute-start(bf16[128,1024]{1,0:T(8,128)(2,1)S(1)} %collective-permute-done.refs_1_), channel_id=1, source_target_pairs={{0,16},{8,24},{16,0},{24,8},{1,17},{9,25},{17,1},{25,9},{2,18},{10... | collective-permute-start | bytes 786440 | tf_op jit(solution)/shard_map/ppermute | solution.py:30
  20.1 15.3 %collective-permute-start.10 = (bf16[128,1024]{1,0:T(8,128)(2,1)}, bf16[128,1024]{1,0:T(8,128)(2,1)S(1)}, u32[]{:S(2)}, u32[]{:S(2)}) collective-permute-start(bf16[128,1024]{1,0:T(8,128)(2,1)} %get-tuple-element.101.refs_3_.refs_12_), channel_id=1, source_target_pairs={{0,16},{8,24},{16,0},{24,8},{1,17},{9,25},{17,1},{25,9},{2,18},{10... | collective-permute-start | bytes 786440 | tf_op jit(solution)/shard_map/ppermute | solution.py:30
  20.6 14.8 %collective-permute-start.5 = (bf16[128,1024]{1,0:T(8,128)(2,1)S(1)}, bf16[128,1024]{1,0:T(8,128)(2,1)S(1)}, u32[]{:S(2)}, u32[]{:S(2)}) collective-permute-start(bf16[128,1024]{1,0:T(8,128)(2,1)S(1)} %collective-permute-done.4.refs_6_), channel_id=1, source_target_pairs={{0,8},{8,0},{16,24},{24,16},{1,9},{9,1},{17,25},{25,17},{2,10},{10... | collective-permute-start | bytes 786440 | tf_op jit(solution)/shard_map/ppermute | solution.py:30
  24.2 11.2 %collective-permute-start.6 = (bf16[128,1024]{1,0:T(8,128)(2,1)}, bf16[128,1024]{1,0:T(8,128)(2,1)S(1)}, u32[]{:S(2)}, u32[]{:S(2)}) collective-permute-start(bf16[128,1024]{1,0:T(8,128)(2,1)} %get-tuple-element.97.refs_2_.refs_8_), channel_id=1, source_target_pairs={{0,8},{8,0},{16,24},{24,16},{1,9},{9,1},{17,25},{25,17},{2,10},{10... | collective-permute-start | bytes 786440 | tf_op jit(solution)/shard_map/ppermute | solution.py:30
  24.3 17.6 %collective-permute-start.7 = (bf16[128,1024]{1,0:T(8,128)(2,1)}, bf16[128,1024]{1,0:T(8,128)(2,1)S(1)}, u32[]{:S(2)}, u32[]{:S(2)}) collective-permute-start(bf16[128,1024]{1,0:T(8,128)(2,1)} %get-tuple-element.97.refs_2_.refs_8_), channel_id=1, source_target_pairs={{0,16},{8,24},{16,0},{24,8},{1,17},{9,25},{17,1},{25,9},{2,18},{10... | collective-permute-start | bytes 786440 | tf_op jit(solution)/shard_map/ppermute | solution.py:30
  29.8 12.1 %collective-permute-start.9 = (bf16[128,1024]{1,0:T(8,128)(2,1)}, bf16[128,1024]{1,0:T(8,128)(2,1)S(1)}, u32[]{:S(2)}, u32[]{:S(2)}) collective-permute-start(bf16[128,1024]{1,0:T(8,128)(2,1)} %get-tuple-element.101.refs_3_.refs_12_), channel_id=1, source_target_pairs={{0,8},{8,0},{16,24},{24,16},{1,9},{9,1},{17,25},{25,17},{2,10},{10... | collective-permute-start | bytes 786440 | tf_op jit(solution)/shard_map/ppermute | solution.py:30
  35.4 9.7 %collective-permute-start.8 = (bf16[128,1024]{1,0:T(8,128)(2,1)S(1)}, bf16[128,1024]{1,0:T(8,128)(2,1)S(1)}, u32[]{:S(2)}, u32[]{:S(2)}) collective-permute-start(bf16[128,1024]{1,0:T(8,128)(2,1)S(1)} %collective-permute-done.6.refs_9_), channel_id=1, source_target_pairs={{0,16},{8,24},{16,0},{24,8},{1,17},{9,25},{17,1},{25,9},{2,18},{10... | collective-permute-start | bytes 786440 | tf_op jit(solution)/shard_map/ppermute | solution.py:30
  37.0 8.2 %collective-permute-start.11 = (bf16[128,1024]{1,0:T(8,128)(2,1)S(1)}, bf16[128,1024]{1,0:T(8,128)(2,1)}, u32[]{:S(2)}, u32[]{:S(2)}) collective-permute-start(bf16[128,1024]{1,0:T(8,128)(2,1)S(1)} %collective-permute-done.10.refs_14_), channel_id=1, source_target_pairs={{0,8},{8,0},{16,24},{24,16},{1,9},{9,1},{17,25},{25,17},{2,10},{10... | collective-permute-start | bytes 786440 | tf_op jit(solution)/shard_map/ppermute | solution.py:30
  63.5 2.3 %collective-permute-start.12 = (bf16[128,2304]{1,0:T(8,128)(2,1)}, bf16[128,2304]{1,0:T(8,128)(2,1)S(1)}, u32[]{:S(2)}, u32[]{:S(2)}) collective-permute-start(bf16[128,2304]{1,0:T(8,128)(2,1)} %get-tuple-element.106), channel_id=1, source_target_pairs={{0,1},{1,0},{2,3},{3,2},{4,5},{5,4},{6,7},{7,6},{8,9},{9,8},{10,11... | collective-permute-start | bytes 1769480 | tf_op jit(solution)/shard_map/ppermute | solution.py:30
  66.9 6.8 %collective-permute-start.14 = (bf16[32,2304]{1,0:T(8,128)(2,1)S(1)}, bf16[32,2304]{1,0:T(8,128)(2,1)S(1)}, u32[]{:S(2)}, u32[]{:S(2)}) collective-permute-start(bf16[32,2304]{1,0:T(8,128)(2,1)S(1)} %get-tuple-element.161), channel_id=1, source_target_pairs={{0,2},{1,3},{2,0},{3,1},{4,6},{5,7},{6,4},{7,5},{8,10},{9,11},{10,... | collective-permute-start | bytes 442376 | tf_op jit(solution)/shard_map/ppermute | solution.py:30
  68.6 8.8 %collective-permute-start.16 = (bf16[128,2304]{1,0:T(8,128)(2,1)}, bf16[128,2304]{1,0:T(8,128)(2,1)S(1)}, u32[]{:S(2)}, u32[]{:S(2)}) collective-permute-start(bf16[128,2304]{1,0:T(8,128)(2,1)} %get-tuple-element.108), channel_id=1, source_target_pairs={{0,1},{1,0},{2,3},{3,2},{4,5},{5,4},{6,7},{7,6},{8,9},{9,8},{10,11... | collective-permute-start | bytes 1769480 | tf_op jit(solution)/shard_map/ppermute | solution.py:30
  68.6 10.9 %collective-permute-start.13 = (bf16[32,2304]{1,0:T(8,128)(2,1)S(1)}, bf16[32,2304]{1,0:T(8,128)(2,1)S(1)}, u32[]{:S(2)}, u32[]{:S(2)}) collective-permute-start(bf16[32,2304]{1,0:T(8,128)(2,1)S(1)} %get-tuple-element.160), channel_id=1, source_target_pairs={{0,2},{1,3},{2,0},{3,1},{4,6},{5,7},{6,4},{7,5},{8,10},{9,11},{10,... | collective-permute-start | bytes 442376 | tf_op jit(solution)/shard_map/ppermute | solution.py:30
  74.7 8.0 %collective-permute-start.15 = (bf16[32,2304]{1,0:T(8,128)(2,1)S(1)}, bf16[32,2304]{1,0:T(8,128)(2,1)S(1)}, u32[]{:S(2)}, u32[]{:S(2)}) collective-permute-start(bf16[32,2304]{1,0:T(8,128)(2,1)S(1)} %add_convert_fusion.7), channel_id=1, source_target_pairs={{0,4},{1,5},{2,6},{3,7},{4,0},{5,1},{6,2},{7,3},{8,12},{9,13},{10,... | collective-permute-start | bytes 442376 | tf_op jit(solution)/shard_map/ppermute | solution.py:30
  77.4 19.9 %collective-permute-start.17 = (bf16[32,2304]{1,0:T(8,128)(2,1)S(1)}, bf16[32,2304]{1,0:T(8,128)(2,1)S(1)}, u32[]{:S(2)}, u32[]{:S(2)}) collective-permute-start(bf16[32,2304]{1,0:T(8,128)(2,1)S(1)} %get-tuple-element.109), channel_id=1, source_target_pairs={{0,2},{1,3},{2,0},{3,1},{4,6},{5,7},{6,4},{7,5},{8,10},{9,11},{10,... | collective-permute-start | bytes 442376 | tf_op jit(solution)/shard_map/ppermute | solution.py:30
  79.0 9.0 %collective-permute-start.18 = (bf16[32,2304]{1,0:T(8,128)(2,1)S(1)}, bf16[32,2304]{1,0:T(8,128)(2,1)S(1)}, u32[]{:S(2)}, u32[]{:S(2)}) collective-permute-start(bf16[32,2304]{1,0:T(8,128)(2,1)S(1)} %get-tuple-element.110), channel_id=1, source_target_pairs={{0,2},{1,3},{2,0},{3,1},{4,6},{5,7},{6,4},{7,5},{8,10},{9,11},{10,... | collective-permute-start | bytes 442376 | tf_op jit(solution)/shard_map/ppermute | solution.py:30
  84.4 12.9 %collective-permute-start.21 = (bf16[32,2304]{1,0:T(8,128)(2,1)S(1)}, bf16[32,2304]{1,0:T(8,128)(2,1)S(1)}, u32[]{:S(2)}, u32[]{:S(2)}) collective-permute-start(bf16[32,2304]{1,0:T(8,128)(2,1)S(1)} %get-tuple-element.113.refs_0_), channel_id=1, source_target_pairs={{0,4},{1,5},{2,6},{3,7},{4,0},{5,1},{6,2},{7,3},{8,12},{9,13},{10,... | collective-permute-start | bytes 442376 | tf_op jit(solution)/shard_map/ppermute | solution.py:30
  88.1 10.9 %collective-permute-start.19 = (bf16[32,2304]{1,0:T(8,128)(2,1)S(1)}, bf16[32,2304]{1,0:T(8,128)(2,1)S(1)}, u32[]{:S(2)}, u32[]{:S(2)}) collective-permute-start(bf16[32,2304]{1,0:T(8,128)(2,1)S(1)} %add_convert_fusion.4), channel_id=1, source_target_pairs={{0,4},{1,5},{2,6},{3,7},{4,0},{5,1},{6,2},{7,3},{8,12},{9,13},{10,... | collective-permute-start | bytes 442376 | tf_op jit(solution)/shard_map/ppermute | solution.py:30
  88.3 20.6 %collective-permute-start.23 = (bf16[32,2304]{1,0:T(8,128)(2,1)S(1)}, bf16[32,2304]{1,0:T(8,128)(2,1)S(1)}, u32[]{:S(2)}, u32[]{:S(2)}) collective-permute-start(bf16[32,2304]{1,0:T(8,128)(2,1)S(1)} %get-tuple-element.113.refs_0_), channel_id=1, source_target_pairs={{0,1},{1,0},{2,3},{3,2},{4,5},{5,4},{6,7},{7,6},{8,9},{9,8},{10,11... | collective-permute-start | bytes 442376 | tf_op jit(solution)/shard_map/ppermute | solution.py:30
  88.3 11.1 %collective-permute-start.20 = (bf16[32,2304]{1,0:T(8,128)(2,1)S(1)}, bf16[32,2304]{1,0:T(8,128)(2,1)S(1)}, u32[]{:S(2)}, u32[]{:S(2)}) collective-permute-start(bf16[32,2304]{1,0:T(8,128)(2,1)S(1)} %get-tuple-element.113.refs_0_), channel_id=1, source_target_pairs={{0,2},{1,3},{2,0},{3,1},{4,6},{5,7},{6,4},{7,5},{8,10},{9,11},{10,... | collective-permute-start | bytes 442376 | tf_op jit(solution)/shard_map/ppermute | solution.py:30
  97.3 5.1 %collective-permute-start.22 = (bf16[32,2304]{1,0:T(8,128)(2,1)S(1)}, bf16[32,2304]{1,0:T(8,128)(2,1)S(1)}, u32[]{:S(2)}, u32[]{:S(2)}) collective-permute-start(bf16[32,2304]{1,0:T(8,128)(2,1)S(1)} %collective-permute-done.21.refs_2_), channel_id=1, source_target_pairs={{0,2},{1,3},{2,0},{3,1},{4,6},{5,7},{6,4},{7,5},{8,10},{9,11},{10,... | collective-permute-start | bytes 442376 | tf_op jit(solution)/shard_map/ppermute | solution.py:30
  99.0 9.9 %collective-permute-start.25 = (bf16[32,2304]{1,0:T(8,128)(2,1)S(1)}, bf16[32,2304]{1,0:T(8,128)(2,1)S(1)}, u32[]{:S(2)}, u32[]{:S(2)}) collective-permute-start(bf16[32,2304]{1,0:T(8,128)(2,1)S(1)} %collective-permute-done.21.refs_2_), channel_id=1, source_target_pairs={{0,1},{1,0},{2,3},{3,2},{4,5},{5,4},{6,7},{7,6},{8,9},{9,8},{10,11... | collective-permute-start | bytes 442376 | tf_op jit(solution)/shard_map/ppermute | solution.py:30
  99.4 10.1 %collective-permute-start.24 = (bf16[32,2304]{1,0:T(8,128)(2,1)S(1)}, bf16[32,2304]{1,0:T(8,128)(2,1)S(1)}, u32[]{:S(2)}, u32[]{:S(2)}) collective-permute-start(bf16[32,2304]{1,0:T(8,128)(2,1)S(1)} %collective-permute-done.20.refs_1_), channel_id=1, source_target_pairs={{0,1},{1,0},{2,3},{3,2},{4,5},{5,4},{6,7},{7,6},{8,9},{9,8},{10,11... | collective-permute-start | bytes 442376 | tf_op jit(solution)/shard_map/ppermute | solution.py:30
  102.5 7.0 %collective-permute-start.26 = (bf16[32,2304]{1,0:T(8,128)(2,1)S(1)}, bf16[32,2304]{1,0:T(8,128)(2,1)S(1)}, u32[]{:S(2)}, u32[]{:S(2)}) collective-permute-start(bf16[32,2304]{1,0:T(8,128)(2,1)S(1)} %collective-permute-done.22.refs_3_), channel_id=1, source_target_pairs={{0,1},{1,0},{2,3},{3,2},{4,5},{5,4},{6,7},{7,6},{8,9},{9,8},{10,11... | collective-permute-start | bytes 442376 | tf_op jit(solution)/shard_map/ppermute | solution.py:30
  104.1 17.2 %collective-permute-start.29 = (bf16[32,2304]{1,0:T(8,128)(2,1)S(1)}, bf16[32,2304]{1,0:T(8,128)(2,1)S(1)}, u32[]{:S(2)}, u32[]{:S(2)}) collective-permute-start(bf16[32,2304]{1,0:T(8,128)(2,1)S(1)} %get-tuple-element.122.refs_0_), channel_id=1, source_target_pairs={{0,6},{1,7},{2,4},{3,5},{4,2},{5,3},{6,0},{7,1},{8,14},{9,15},{10,... | collective-permute-start | bytes 442376 | tf_op jit(solution)/shard_map/ppermute | solution.py:30
  108.9 12.4 %collective-permute-start.28 = (bf16[32,2304]{1,0:T(8,128)(2,1)S(1)}, bf16[32,2304]{1,0:T(8,128)(2,1)S(1)}, u32[]{:S(2)}, u32[]{:S(2)}) collective-permute-start(bf16[32,2304]{1,0:T(8,128)(2,1)S(1)} %get-tuple-element.122.refs_0_), channel_id=1, source_target_pairs={{0,4},{1,5},{2,6},{3,7},{4,0},{5,1},{6,2},{7,3},{8,12},{9,13},{10,... | collective-permute-start | bytes 442376 | tf_op jit(solution)/shard_map/ppermute | solution.py:30
  108.9 12.4 %collective-permute-start.27 = (bf16[32,2304]{1,0:T(8,128)(2,1)S(1)}, bf16[32,2304]{1,0:T(8,128)(2,1)S(1)}, u32[]{:S(2)}, u32[]{:S(2)}) collective-permute-start(bf16[32,2304]{1,0:T(8,128)(2,1)S(1)} %get-tuple-element.122.refs_0_), channel_id=1, source_target_pairs={{0,2},{1,3},{2,0},{3,1},{4,6},{5,7},{6,4},{7,5},{8,10},{9,11},{10,... | collective-permute-start | bytes 442376 | tf_op jit(solution)/shard_map/ppermute | solution.py:30
  121.3 3.1 %collective-permute-start.30 = (bf16[32,2304]{1,0:T(8,128)(2,1)S(1)}, bf16[32,2304]{1,0:T(8,128)(2,1)S(1)}, u32[]{:S(2)}, u32[]{:S(2)}) collective-permute-start(bf16[32,2304]{1,0:T(8,128)(2,1)S(1)} %get-tuple-element.122.refs_0_), channel_id=1, source_target_pairs={{0,1},{1,0},{2,3},{3,2},{4,5},{5,4},{6,7},{7,6},{8,9},{9,8},{10,11... | collective-permute-start | bytes 442376 | tf_op jit(solution)/shard_map/ppermute | solution.py:30
  121.4 3.0 %collective-permute-start.31 = (bf16[32,2304]{1,0:T(8,128)(2,1)S(1)}, bf16[32,2304]{1,0:T(8,128)(2,1)S(1)}, u32[]{:S(2)}, u32[]{:S(2)}) collective-permute-start(bf16[32,2304]{1,0:T(8,128)(2,1)S(1)} %collective-permute-done.27.refs_1_), channel_id=1, source_target_pairs={{0,1},{1,0},{2,3},{3,2},{4,5},{5,4},{6,7},{7,6},{8,9},{9,8},{10,11... | collective-permute-start | bytes 442376 | tf_op jit(solution)/shard_map/ppermute | solution.py:30
  121.9 19.1 %collective-permute-start.36 = (bf16[2,64,1024]{2,1,0:T(8,128)(2,1)S(1)}, bf16[2,64,1024]{2,1,0:T(8,128)(2,1)S(1)}, u32[]{:S(2)}, u32[]{:S(2)}) collective-permute-start(bf16[2,64,1024]{2,1,0:T(8,128)(2,1)S(1)} %get-tuple-element.134), channel_id=1, source_target_pairs={{0,16},{8,24},{16,0},{24,8},{1,17},{9,25},{17,1},{25,9},{2,18},{10... | collective-permute-start | bytes 786440 | tf_op jit(solution)/shard_map/ppermute | solution.py:30
  123.4 19.2 %collective-permute-start.37 = (bf16[2,64,1024]{2,1,0:T(8,128)(2,1)S(1)}, bf16[2,64,1024]{2,1,0:T(8,128)(2,1)S(1)}, u32[]{:S(2)}, u32[]{:S(2)}) collective-permute-start(bf16[2,64,1024]{2,1,0:T(8,128)(2,1)S(1)} %get-tuple-element.137), channel_id=1, source_target_pairs={{0,16},{8,24},{16,0},{24,8},{1,17},{9,25},{17,1},{25,9},{2,18},{10... | collective-permute-start | bytes 786440 | tf_op jit(solution)/shard_map/ppermute | solution.py:30
  123.9 18.7 %collective-permute-start.35 = (bf16[2,64,1024]{2,1,0:T(8,128)(2,1)S(1)}, bf16[2,64,1024]{2,1,0:T(8,128)(2,1)S(1)}, u32[]{:S(2)}, u32[]{:S(2)}) collective-permute-start(bf16[2,64,1024]{2,1,0:T(8,128)(2,1)S(1)} %get-tuple-element.131), channel_id=1, source_target_pairs={{0,8},{8,0},{16,24},{24,16},{1,9},{9,1},{17,25},{25,17},{2,10},{10... | collective-permute-start | bytes 786440 | tf_op jit(solution)/shard_map/ppermute | solution.py:30
  124.4 2.9 %collective-permute-start.33 = (bf16[32,2304]{1,0:T(8,128)(2,1)S(1)}, bf16[32,2304]{1,0:T(8,128)(2,1)S(1)}, u32[]{:S(2)}, u32[]{:S(2)}) collective-permute-start(bf16[32,2304]{1,0:T(8,128)(2,1)S(1)} %collective-permute-done.29.refs_3_), channel_id=1, source_target_pairs={{0,1},{1,0},{2,3},{3,2},{4,5},{5,4},{6,7},{7,6},{8,9},{9,8},{10,11... | collective-permute-start | bytes 442376 | tf_op jit(solution)/shard_map/ppermute | solution.py:30
  125.8 17.6 %collective-permute-start.34 = (bf16[2,64,1024]{2,1,0:T(8,128)(2,1)S(1)}, bf16[2,64,1024]{2,1,0:T(8,128)(2,1)S(1)}, u32[]{:S(2)}, u32[]{:S(2)}) collective-permute-start(bf16[2,64,1024]{2,1,0:T(8,128)(2,1)S(1)} %get-tuple-element.130), channel_id=1, source_target_pairs={{0,8},{8,0},{16,24},{24,16},{1,9},{9,1},{17,25},{25,17},{2,10},{10... | collective-permute-start | bytes 786440 | tf_op jit(solution)/shard_map/ppermute | solution.py:30
  140.5 9.2 %collective-permute-start.41 = (bf16[2,64,1024]{2,1,0:T(8,128)(2,1)}, bf16[2,64,1024]{2,1,0:T(8,128)(2,1)}, u32[]{:S(2)}, u32[]{:S(2)}) collective-permute-start(bf16[2,64,1024]{2,1,0:T(8,128)(2,1)} %get-tuple-element.141), channel_id=1, source_target_pairs={{0,8},{8,0},{16,24},{24,16},{1,9},{9,1},{17,25},{25,17},{2,10},{10... | collective-permute-start | bytes 786440 | tf_op jit(solution)/shard_map/ppermute | solution.py:30
  141.0 10.3 %collective-permute-start.42 = (bf16[2,64,1024]{2,1,0:T(8,128)(2,1)}, bf16[2,64,1024]{2,1,0:T(8,128)(2,1)}, u32[]{:S(2)}, u32[]{:S(2)}) collective-permute-start(bf16[2,64,1024]{2,1,0:T(8,128)(2,1)} %get-tuple-element.143), channel_id=1, source_target_pairs={{0,16},{8,24},{16,0},{24,8},{1,17},{9,25},{17,1},{25,9},{2,18},{10... | collective-permute-start | bytes 786440 | tf_op jit(solution)/shard_map/ppermute | solution.py:30
  146.2 7.6 %collective-permute-start.40 = (f32[8,128]{1,0:T(8,128)S(1)}, f32[8,128]{1,0:T(8,128)S(1)}, u32[]{:S(2)}, u32[]{:S(2)}) collective-permute-start(f32[8,128]{1,0:T(8,128)S(1)} %broadcast_in_dim.11), channel_id=1, source_target_pairs={{0,24},{8,16},{16,8},{24,0},{1,25},{9,17},{17,9},{25,1},{2,26},{10... | collective-permute-start | bytes 12296 | tf_op jit(solution)/shard_map/ppermute | solution.py:30
  147.7 6.8 %collective-permute-start.39 = (f32[8,128]{1,0:T(8,128)S(1)}, f32[8,128]{1,0:T(8,128)S(1)}, u32[]{:S(2)}, u32[]{:S(2)}) collective-permute-start(f32[8,128]{1,0:T(8,128)S(1)} %broadcast_in_dim.11), channel_id=1, source_target_pairs={{0,16},{8,24},{16,0},{24,8},{1,17},{9,25},{17,1},{25,9},{2,18},{10... | collective-permute-start | bytes 12296 | tf_op jit(solution)/shard_map/ppermute | solution.py:30
  149.2 8.8 %collective-permute-start.43 = (bf16[2,64,1024]{2,1,0:T(8,128)(2,1)}, bf16[2,64,1024]{2,1,0:T(8,128)(2,1)S(1)}, u32[]{:S(2)}, u32[]{:S(2)}) collective-permute-start(bf16[2,64,1024]{2,1,0:T(8,128)(2,1)} %add_convert_fusion.3), channel_id=1, source_target_pairs={{0,16},{8,24},{16,0},{24,8},{1,17},{9,25},{17,1},{25,9},{2,18},{10... | collective-permute-start | bytes 786440 | tf_op jit(solution)/shard_map/ppermute | solution.py:30
  149.7 9.2 %collective-permute-start.44 = (bf16[2,64,1024]{2,1,0:T(8,128)(2,1)}, bf16[2,64,1024]{2,1,0:T(8,128)(2,1)S(1)}, u32[]{:S(2)}, u32[]{:S(2)}) collective-permute-start(bf16[2,64,1024]{2,1,0:T(8,128)(2,1)} %add_convert_fusion.2), channel_id=1, source_target_pairs={{0,8},{8,0},{16,24},{24,16},{1,9},{9,1},{17,25},{25,17},{2,10},{10... | collective-permute-start | bytes 786440 | tf_op jit(solution)/shard_map/ppermute | solution.py:30
  151.3 10.3 %collective-permute-start.38 = (f32[8,128]{1,0:T(8,128)S(1)}, f32[8,128]{1,0:T(8,128)S(1)}, u32[]{:S(2)}, u32[]{:S(2)}) collective-permute-start(f32[8,128]{1,0:T(8,128)S(1)} %broadcast_in_dim.11), channel_id=1, source_target_pairs={{0,8},{8,0},{16,24},{24,16},{1,9},{9,1},{17,25},{25,17},{2,10},{10... | collective-permute-start | bytes 12296 | tf_op jit(solution)/shard_map/ppermute | solution.py:30
  153.9 10.7 %collective-permute-start.45 = (bf16[2,64,1024]{2,1,0:T(8,128)(2,1)S(1)}, bf16[2,64,1024]{2,1,0:T(8,128)(2,1)S(1)}, u32[]{:S(2)}, u32[]{:S(2)}) collective-permute-start(bf16[2,64,1024]{2,1,0:T(8,128)(2,1)S(1)} %copy-done.10), channel_id=1, source_target_pairs={{0,8},{8,0},{16,24},{24,16},{1,9},{9,1},{17,25},{25,17},{2,10},{10... | collective-permute-start | bytes 786440 | tf_op jit(solution)/shard_map/ppermute | solution.py:30
  154.5 10.1 %collective-permute-start.47 = (bf16[2,64,1024]{2,1,0:T(8,128)(2,1)S(1)}, bf16[2,64,1024]{2,1,0:T(8,128)(2,1)S(1)}, u32[]{:S(2)}, u32[]{:S(2)}) collective-permute-start(bf16[2,64,1024]{2,1,0:T(8,128)(2,1)S(1)} %add_convert_fusion.1), channel_id=1, source_target_pairs={{0,16},{8,24},{16,0},{24,8},{1,17},{9,25},{17,1},{25,9},{2,18},{10... | collective-permute-start | bytes 786440 | tf_op jit(solution)/shard_map/ppermute | solution.py:30
  158.0 9.7 %collective-permute-start.46 = (bf16[2,64,1024]{2,1,0:T(8,128)(2,1)S(1)}, bf16[2,64,1024]{2,1,0:T(8,128)(2,1)S(1)}, u32[]{:S(2)}, u32[]{:S(2)}) collective-permute-start(bf16[2,64,1024]{2,1,0:T(8,128)(2,1)S(1)} %copy-done.8), channel_id=1, source_target_pairs={{0,16},{8,24},{16,0},{24,8},{1,17},{9,25},{17,1},{25,9},{2,18},{10... | collective-permute-start | bytes 786440 | tf_op jit(solution)/shard_map/ppermute | solution.py:30
  158.9 9.0 %collective-permute-start.48 = (bf16[2,64,1024]{2,1,0:T(8,128)(2,1)S(1)}, bf16[2,64,1024]{2,1,0:T(8,128)(2,1)S(1)}, u32[]{:S(2)}, u32[]{:S(2)}) collective-permute-start(bf16[2,64,1024]{2,1,0:T(8,128)(2,1)S(1)} %add_convert_fusion), channel_id=1, source_target_pairs={{0,8},{8,0},{16,24},{24,16},{1,9},{9,1},{17,25},{25,17},{2,10},{10... | collective-permute-start | bytes 786440 | tf_op jit(solution)/shard_map/ppermute | solution.py:30
  (27 other events, 359.9 us)

commit v12 on v11

--- a/solution.py
+++ b/solution.py
@@ -255,7 +255,7 @@
                 outs[c][to, cols] = product[first:first + plan.piece].astype(BF16)
                 outs[plan.chunks + c][to, cols] = product[half + first:half + first + plan.piece]
 
-    streamed(plan.model // tile, w_buf.shape[0], copies_of, step, 1)
+    streamed(plan.model // tile, w_buf.shape[0], copies_of, step, 2)
 
 
 def decode(plan, index, pieces, w_dec):
@@ -507,7 +507,7 @@
         squares = squares + total
         results.append(lanes)
 
-    unfinished, seconds = [], []
+    unfinished = []
     for c, lanes in enumerate(results):
         earlier = [x for each in first_errors[c + 1:c + 2] for x in each]
         first_step = []
@@ -534,22 +534,21 @@
             kept_all.append(kept[0])
         got_all = [own[i] for i in range(1, len(kept_all[0])) for own in kept_all]
         unfinished.append(([own[0] for own in kept_all], got_all))
-        seconds.append(second)
 
     feat_grad = None
     for c, (kept, got) in enumerate(unfinished):
         before_last = feat_grad
         feat_grad = finish(plan, c, kept, got, feat_grad)
 
-    squares, = after([squares], seconds[0])
-    loss = jnp.full((8, 128), jnp.sum(squares), F32)
-    parts = [loss] + [swap(loss, "grp", groups, j) for j in range(1, groups)]
+    arrived = unfinished[0][1][-len(plan.lanes):] if chunks > 1 else []
+    squares, = after([squares], arrived + second)
+    parts = [squares] + [swap(squares, "grp", groups, j) for j in range(1, groups)]
     parts = after(parts, second + ([] if before_last is None else [before_last]))
     while len(parts) > 1:
         parts = [x + y for x, y in zip(parts[::2], parts[1::2])]
-    loss = parts[0]
+    loss = jnp.sum(parts[0])
     entries = targets.shape[0] * groups * plan.tokens * plan.model
-    recon_loss = loss[0, 0] / entries
+    recon_loss = loss / entries
     recon = jnp.concatenate(recon_parts, axis=0)[None]
     return active, recon, recon_loss, feat_grad
 

time: 171 us -> 173 us (1.012)
  waiting for transfers between devices: 49.6 us -> 58.8 us
  other arithmetic: 11.9 us -> 5.88 us
    ppermute x49, waiting for transfers between devices: 49.6 us -> 58.8 us  [swap(): return lax.ppermute(x, axis, [(i, i ^ offset) for i in range(size)])]
    convert_element_type x4, other arithmetic: 3.59 us -> 0.21 us  [per_device(): sum((x.astype(F32) for x in own)).astype(BF16)]
  transfers between devices with their start and end apart: 49 -> 49, of which waited for: 19 -> 18; matrix products, arithmetic and copies ran while one was open for 7% -> 3% of each run, Pallas kernels for 19% -> 19%
where the time goes in v12:
time: 173 us
  waiting for transfers between devices  58.8 us (34%)
  Pallas kernels  56.8 us (33%)
  starting transfers between devices  45 us (26%)
  other arithmetic  5.88 us (3%)
  local copies, waits for them, and re-layouts  3.24 us (2%)
  between operations  2.81 us (2%)
    ppermute x49, waiting for transfers between devices, swap(): return lax.ppermute(x, axis, [(i, i ^ offset) for i in range(size)])  58.8 us
    pallas_call x8, Pallas kernels, call(): pl.pallas_call(kernel, in_specs=in_specs, out_shape=out_shape, scratch_sh...  56.8 us
    ppermute x49, starting transfers between devices, swap(): return lax.ppermute(x, axis, [(i, i ^ offset) for i in range(size)])  45 us
  transfers between devices with their start and end apart: 49, of which 18 were waited for; matrix products, arithmetic and copies ran while one was open for 3% of the time, Pallas kernels for 19%

profile of v12, /device:TPU:0, one launch (start us, length us, event | category | flops | bytes accessed | tf_op | source)
XLA Modules:
  0.0 172.5 jit_solution(16721311405291855462)
XLA Ops:
  0.6 5.5 %encode.2 = (bf16[128,1024]{1,0:T(8,128)(2,1)}, bf16[128,1024]{1,0:T(8,128)(2,1)}) custom-call(bf16[4,128,2304]{2,1,0:T(8,128)(2,1)} %resid_ref.3, bf16[4,2304,1024]{2,1,0:T(8,128)(2,1)} %w_ref.3, f32[4,1024]{1,0:T(4,128)} %b_ref.3), custom_call_target="tpu_custom_call" | custom-call | flops 1048576 | bytes 1024 | tf_op jit(solution)/shard_map/encode/pallas_call | solution.py:103
  6.1 3.0 %collective-permute-start = (bf16[128,1024]{1,0:T(8,128)(2,1)}, bf16[128,1024]{1,0:T(8,128)(2,1)S(1)}, u32[]{:S(2)}, u32[]{:S(2)}) collective-permute-start(bf16[128,1024]{1,0:T(8,128)(2,1)} %get-tuple-element.89.refs_0_), channel_id=1, source_target_pairs={{0,8},{8,0},{16,24},{24,16},{1,9},{9,1},{17,25},{25,17},{2,10},{10... | collective-permute-start | bytes 786440 | tf_op jit(solution)/shard_map/ppermute | solution.py:30
  9.1 1.5 collective-permute-start.4
  11.3 5.5 %encode.3 = (bf16[128,1024]{1,0:T(8,128)(2,1)}, bf16[128,1024]{1,0:T(8,128)(2,1)}) custom-call(bf16[4,128,2304]{2,1,0:T(8,128)(2,1)} %resid_ref.3, bf16[4,2304,1024]{2,1,0:T(8,128)(2,1)} %w_ref.3, f32[4,1024]{1,0:T(4,128)} %b_ref.3), custom_call_target="tpu_custom_call" | custom-call | flops 1048576 | bytes 1024 | tf_op jit(solution)/shard_map/encode/pallas_call | solution.py:103
  16.7 1.8 %collective-permute-done.4.refs_6_ = bf16[128,1024]{1,0:T(8,128)(2,1)S(1)} collective-permute-done((bf16[128,1024]{1,0:T(8,128)(2,1)}, bf16[128,1024]{1,0:T(8,128)(2,1)S(1)}, u32[]{:S(2)}, u32[]{:S(2)}) %collective-permute-start.4) | collective-permute-done | bytes 262176 | tf_op jit(solution)/shard_map/ppermute | solution.py:30
  18.6 1.5 collective-permute-start.2
  20.8 3.4 %collective-permute-done.1.refs_2_ = bf16[128,1024]{1,0:T(8,128)(2,1)S(1)} collective-permute-done((bf16[128,1024]{1,0:T(8,128)(2,1)}, bf16[128,1024]{1,0:T(8,128)(2,1)S(1)}, u32[]{:S(2)}, u32[]{:S(2)}) %collective-permute-start.1) | collective-permute-done | bytes 262176 | tf_op jit(solution)/shard_map/ppermute | solution.py:30
  24.3 2.0 %collective-permute-start.7 = (bf16[128,1024]{1,0:T(8,128)(2,1)}, bf16[128,1024]{1,0:T(8,128)(2,1)S(1)}, u32[]{:S(2)}, u32[]{:S(2)}) collective-permute-start(bf16[128,1024]{1,0:T(8,128)(2,1)} %get-tuple-element.97.refs_2_.refs_8_), channel_id=1, source_target_pairs={{0,16},{8,24},{16,0},{24,8},{1,17},{9,25},{17,1},{25,9},{2,18},{10... | collective-permute-start | bytes 786440 | tf_op jit(solution)/shard_map/ppermute | solution.py:30
  26.3 3.5 %collective-permute-done.2.refs_3_ = bf16[128,1024]{1,0:T(8,128)(2,1)S(1)} collective-permute-done((bf16[128,1024]{1,0:T(8,128)(2,1)S(1)}, bf16[128,1024]{1,0:T(8,128)(2,1)S(1)}, u32[]{:S(2)}, u32[]{:S(2)}) %collective-permute-start.2) | collective-permute-done | bytes 262176 | tf_op jit(solution)/shard_map/ppermute | solution.py:30
  29.9 5.5 %collective-permute-done.10.refs_14_ = bf16[128,1024]{1,0:T(8,128)(2,1)S(1)} collective-permute-done((bf16[128,1024]{1,0:T(8,128)(2,1)}, bf16[128,1024]{1,0:T(8,128)(2,1)S(1)}, u32[]{:S(2)}, u32[]{:S(2)}) %collective-permute-start.10) | collective-permute-done | bytes 262176 | tf_op jit(solution)/shard_map/ppermute | solution.py:30
  35.4 1.6 collective-permute-start.8
  38.3 0.9 copy-done.2
  39.2 0.9 copy-done.3
  40.2 1.7 %arrange.1 = bf16[128,4,1024]{2,1,0:T(4,128)(2,1)} custom-call(bf16[128,1024]{1,0:T(8,128)(2,1)S(1)} %copy-done, bf16[128,1024]{1,0:T(8,128)(2,1)S(1)} %copy-done.1, bf16[128,1024]{1,0:T(8,128)(2,1)S(1)} %copy-done.2, bf16[128,1024]{1,0:T(8,128)(2,1)S(1)} %copy-done.3), custom_call_target="tpu_custom_call" | custom-call | flops 1048576 | bytes 1024 | tf_op jit(solution)/shard_map/arrange/pallas_call | solution.py:103
  41.9 3.3 %collective-permute-done.8.refs_11_ = bf16[128,1024]{1,0:T(8,128)(2,1)S(1)} collective-permute-done((bf16[128,1024]{1,0:T(8,128)(2,1)S(1)}, bf16[128,1024]{1,0:T(8,128)(2,1)S(1)}, u32[]{:S(2)}, u32[]{:S(2)}) %collective-permute-start.8) | collective-permute-done | bytes 262176 | tf_op jit(solution)/shard_map/ppermute | solution.py:30
  45.9 18.0 %decode.1 = (bf16[128,2304]{1,0:T(8,128)(2,1)}, bf16[128,2304]{1,0:T(8,128)(2,1)}, f32[128,2304]{1,0:T(8,128)}, f32[128,2304]{1,0:T(8,128)}) custom-call(s32[17]{0:T(128)} %concatenate.6.index_ref, bf16[128,1024]{1,0:T(8,128)(2,1)} %get-tuple-element.89.refs_0_, bf16[128,1024]{1,0:T(8,128)(2,1)} %copy-done.6, bf16[128,1024]{1,0:T(8,128)(2,1)} %copy-done.8, ...), custom_call_target="tpu_custom_call" | custom-call | flops 1048576 | bytes 1024 | tf_op jit(solution)/shard_map/decode/pallas_call | solution.py:103
  64.0 2.2 %collective-permute-done.12 = bf16[128,2304]{1,0:T(8,128)(2,1)S(1)} collective-permute-done((bf16[128,2304]{1,0:T(8,128)(2,1)}, bf16[128,2304]{1,0:T(8,128)(2,1)S(1)}, u32[]{:S(2)}, u32[]{:S(2)}) %collective-permute-start.12) | collective-permute-done | bytes 589856 | tf_op jit(solution)/shard_map/ppermute | solution.py:30
  66.2 1.1 add_convert_fusion.9
  67.3 1.6 collective-permute-start.14
  69.4 4.7 %collective-permute-done.14 = bf16[32,2304]{1,0:T(8,128)(2,1)S(1)} collective-permute-done((bf16[32,2304]{1,0:T(8,128)(2,1)S(1)}, bf16[32,2304]{1,0:T(8,128)(2,1)S(1)}, u32[]{:S(2)}, u32[]{:S(2)}) %collective-permute-start.14) | collective-permute-done | bytes 147488 | tf_op jit(solution)/shard_map/ppermute | solution.py:30
  74.1 1.0 add_convert_fusion.7
  75.1 2.5 %collective-permute-start.15 = (bf16[32,2304]{1,0:T(8,128)(2,1)S(1)}, bf16[32,2304]{1,0:T(8,128)(2,1)S(1)}, u32[]{:S(2)}, u32[]{:S(2)}) collective-permute-start(bf16[32,2304]{1,0:T(8,128)(2,1)S(1)} %add_convert_fusion.7), channel_id=1, source_target_pairs={{0,4},{1,5},{2,6},{3,7},{4,0},{5,1},{6,2},{7,3},{8,12},{9,13},{10,... | collective-permute-start | bytes 442376 | tf_op jit(solution)/shard_map/ppermute | solution.py:30
  77.7 1.6 collective-permute-start.17
  79.8 3.4 %collective-permute-done.15 = bf16[32,2304]{1,0:T(8,128)(2,1)S(1)} collective-permute-done((bf16[32,2304]{1,0:T(8,128)(2,1)S(1)}, bf16[32,2304]{1,0:T(8,128)(2,1)S(1)}, u32[]{:S(2)}, u32[]{:S(2)}) %collective-permute-start.15) | collective-permute-done | bytes 147488 | tf_op jit(solution)/shard_map/ppermute | solution.py:30
  83.2 1.1 fusion.3
  84.3 2.2 %collective-permute-start.21 = (bf16[32,2304]{1,0:T(8,128)(2,1)S(1)}, bf16[32,2304]{1,0:T(8,128)(2,1)S(1)}, u32[]{:S(2)}, u32[]{:S(2)}) collective-permute-start(bf16[32,2304]{1,0:T(8,128)(2,1)S(1)} %get-tuple-element.113.refs_0_), channel_id=1, source_target_pairs={{0,4},{1,5},{2,6},{3,7},{4,0},{5,1},{6,2},{7,3},{8,12},{9,13},{10,... | collective-permute-start | bytes 442376 | tf_op jit(solution)/shard_map/ppermute | solution.py:30
  86.5 1.9 %collective-permute-done.18 = bf16[32,2304]{1,0:T(8,128)(2,1)S(1)} collective-permute-done((bf16[32,2304]{1,0:T(8,128)(2,1)S(1)}, bf16[32,2304]{1,0:T(8,128)(2,1)S(1)}, u32[]{:S(2)}, u32[]{:S(2)}) %collective-permute-start.18) | collective-permute-done | bytes 147488 | tf_op jit(solution)/shard_map/ppermute | solution.py:30
  88.8 2.0 %collective-permute-start.20 = (bf16[32,2304]{1,0:T(8,128)(2,1)S(1)}, bf16[32,2304]{1,0:T(8,128)(2,1)S(1)}, u32[]{:S(2)}, u32[]{:S(2)}) collective-permute-start(bf16[32,2304]{1,0:T(8,128)(2,1)S(1)} %get-tuple-element.113.refs_0_), channel_id=1, source_target_pairs={{0,2},{1,3},{2,0},{3,1},{4,6},{5,7},{6,4},{7,5},{8,10},{9,11},{10,... | collective-permute-start | bytes 442376 | tf_op jit(solution)/shard_map/ppermute | solution.py:30
  90.8 6.3 %collective-permute-done.21.refs_2_ = bf16[32,2304]{1,0:T(8,128)(2,1)S(1)} collective-permute-done((bf16[32,2304]{1,0:T(8,128)(2,1)S(1)}, bf16[32,2304]{1,0:T(8,128)(2,1)S(1)}, u32[]{:S(2)}, u32[]{:S(2)}) %collective-permute-start.21) | collective-permute-done | bytes 147488 | tf_op jit(solution)/shard_map/ppermute | solution.py:30
  97.1 1.9 %collective-permute-done.19 = bf16[32,2304]{1,0:T(8,128)(2,1)S(1)} collective-permute-done((bf16[32,2304]{1,0:T(8,128)(2,1)S(1)}, bf16[32,2304]{1,0:T(8,128)(2,1)S(1)}, u32[]{:S(2)}, u32[]{:S(2)}) %collective-permute-start.19) | collective-permute-done | bytes 147488 | tf_op jit(solution)/shard_map/ppermute | solution.py:30
  99.2 0.9 collective-permute-done.20.refs_1_
  100.1 2.9 %collective-permute-done.22.refs_3_ = bf16[32,2304]{1,0:T(8,128)(2,1)S(1)} collective-permute-done((bf16[32,2304]{1,0:T(8,128)(2,1)S(1)}, bf16[32,2304]{1,0:T(8,128)(2,1)S(1)}, u32[]{:S(2)}, u32[]{:S(2)}) %collective-permute-start.22) | collective-permute-done | bytes 147488 | tf_op jit(solution)/shard_map/ppermute | solution.py:30
  103.0 0.9 fusion
  103.9 4.4 %collective-permute-start.29 = (bf16[32,2304]{1,0:T(8,128)(2,1)S(1)}, bf16[32,2304]{1,0:T(8,128)(2,1)S(1)}, u32[]{:S(2)}, u32[]{:S(2)}) collective-permute-start(bf16[32,2304]{1,0:T(8,128)(2,1)S(1)} %get-tuple-element.122.refs_0_), channel_id=1, source_target_pairs={{0,6},{1,7},{2,4},{3,5},{4,2},{5,3},{6,0},{7,1},{8,14},{9,15},{10,... | collective-permute-start | bytes 442376 | tf_op jit(solution)/shard_map/ppermute | solution.py:30
  109.0 11.8 %gradient.2 = (bf16[2,64,1024]{2,1,0:T(8,128)(2,1)S(1)}, bf16[2,64,1024]{2,1,0:T(8,128)(2,1)S(1)}, f32[2,64,1024]{2,1,0:T(8,128)S(1)}, f32[2,64,1024]{2,1,0:T(8,...) custom-call(s32[17]{0:T(128)S(1)} %copy-done.4, ...), custom_call_target="tpu_custom_call" | custom-call | flops 1048576 | bytes 1024 | tf_op jit(solution)/shard_map/gradient/pallas_call | solution.py:103
  121.4 1.5 collective-permute-start.36
  123.3 1.6 collective-permute-start.35
  126.8 11.8 %gradient.3 = (bf16[2,64,1024]{2,1,0:T(8,128)(2,1)S(1)}, bf16[2,64,1024]{2,1,0:T(8,128)(2,1)S(1)}, f32[2,64,1024]{2,1,0:T(8,128)S(1)}, f32[2,64,1024]{2,1,0:T(8,...) custom-call(s32[17]{0:T(128)S(1)} %copy-done.4, ...), custom_call_target="tpu_custom_call" | custom-call | flops 1048576 | bytes 1024 | tf_op jit(solution)/shard_map/gradient/pallas_call | solution.py:103
  139.1 1.5 collective-permute-start.41
  141.4 1.6 collective-permute-start.39
  143.0 4.9 %collective-permute-done.40 = bf16[2,64,1024]{2,1,0:T(8,128)(2,1)S(1)} collective-permute-done((bf16[2,64,1024]{2,1,0:T(8,128)(2,1)S(1)}, bf16[2,64,1024]{2,1,0:T(8,128)(2,1)S(1)}, u32[]{:S(2)}, u32[]{:S(2)}) %collective-permute-start.40) | collective-permute-done | bytes 262176 | tf_op jit(solution)/shard_map/ppermute | solution.py:30
  148.4 4.2 %collective-permute-done.37.refs_4_ = bf16[2,64,1024]{2,1,0:T(8,128)(2,1)S(1)} collective-permute-done((bf16[2,64,1024]{2,1,0:T(8,128)(2,1)S(1)}, bf16[2,64,1024]{2,1,0:T(8,128)(2,1)S(1)}, u32[]{:S(2)}, u32[]{:S(2)}) %collective-permute-start.37) | collective-permute-done | bytes 262176 | tf_op jit(solution)/shard_map/ppermute | solution.py:30
  152.7 2.4 %collective-permute-start.44 = (f32[8,128]{1,0:T(8,128)S(1)}, f32[8,128]{1,0:T(8,128)S(1)}, u32[]{:S(2)}, u32[]{:S(2)}) collective-permute-start(f32[8,128]{1,0:T(8,128)S(1)} %add.152), channel_id=1, source_target_pairs={{0,24},{8,16},{16,8},{24,0},{1,25},{9,17},{17,9},{25,1},{2,26},{10... | collective-permute-start | bytes 12296 | tf_op jit(solution)/shard_map/ppermute | solution.py:30
  155.7 1.4 collective-permute-start.47
  157.5 1.6 collective-permute-start.45
  160.9 1.3 finish.2.refs_6_
  162.2 6.6 %collective-permute-done.42 = f32[8,128]{1,0:T(8,128)S(1)} collective-permute-done((f32[8,128]{1,0:T(8,128)S(1)}, f32[8,128]{1,0:T(8,128)S(1)}, u32[]{:S(2)}, u32[]{:S(2)}) %collective-permute-start.42) | collective-permute-done | bytes 4128 | tf_op jit(solution)/shard_map/ppermute | solution.py:30
  170.1 1.3 finish.3
  (110 shorter events, 14.0 us)
Async XLA Ops:
  6.1 10.6 %collective-permute-start = (bf16[128,1024]{1,0:T(8,128)(2,1)}, bf16[128,1024]{1,0:T(8,128)(2,1)S(1)}, u32[]{:S(2)}, u32[]{:S(2)}) collective-permute-start(bf16[128,1024]{1,0:T(8,128)(2,1)} %get-tuple-element.89.refs_0_), channel_id=1, source_target_pairs={{0,8},{8,0},{16,24},{24,16},{1,9},{9,1},{17,25},{25,17},{2,10},{10... | collective-permute-start | bytes 786440 | tf_op jit(solution)/shard_map/ppermute | solution.py:30
  9.1 9.4 %collective-permute-start.4 = (bf16[128,1024]{1,0:T(8,128)(2,1)}, bf16[128,1024]{1,0:T(8,128)(2,1)S(1)}, u32[]{:S(2)}, u32[]{:S(2)}) collective-permute-start(bf16[128,1024]{1,0:T(8,128)(2,1)} %get-tuple-element.93.refs_1_.refs_4_), channel_id=1, source_target_pairs={{0,16},{8,24},{16,0},{24,8},{1,17},{9,25},{17,1},{25,9},{2,18},{10... | collective-permute-start | bytes 786440 | tf_op jit(solution)/shard_map/ppermute | solution.py:30
  10.6 13.5 %collective-permute-start.1 = (bf16[128,1024]{1,0:T(8,128)(2,1)}, bf16[128,1024]{1,0:T(8,128)(2,1)S(1)}, u32[]{:S(2)}, u32[]{:S(2)}) collective-permute-start(bf16[128,1024]{1,0:T(8,128)(2,1)} %get-tuple-element.89.refs_0_), channel_id=1, source_target_pairs={{0,16},{8,24},{16,0},{24,8},{1,17},{9,25},{17,1},{25,9},{2,18},{10... | collective-permute-start | bytes 786440 | tf_op jit(solution)/shard_map/ppermute | solution.py:30
  11.1 13.1 %collective-permute-start.3 = (bf16[128,1024]{1,0:T(8,128)(2,1)}, bf16[128,1024]{1,0:T(8,128)(2,1)S(1)}, u32[]{:S(2)}, u32[]{:S(2)}) collective-permute-start(bf16[128,1024]{1,0:T(8,128)(2,1)} %get-tuple-element.93.refs_1_.refs_4_), channel_id=1, source_target_pairs={{0,8},{8,0},{16,24},{24,16},{1,9},{9,1},{17,25},{25,17},{2,10},{10... | collective-permute-start | bytes 786440 | tf_op jit(solution)/shard_map/ppermute | solution.py:30
  18.6 11.2 %collective-permute-start.2 = (bf16[128,1024]{1,0:T(8,128)(2,1)S(1)}, bf16[128,1024]{1,0:T(8,128)(2,1)S(1)}, u32[]{:S(2)}, u32[]{:S(2)}) collective-permute-start(bf16[128,1024]{1,0:T(8,128)(2,1)S(1)} %collective-permute-done.refs_1_), channel_id=1, source_target_pairs={{0,16},{8,24},{16,0},{24,8},{1,17},{9,25},{17,1},{25,9},{2,18},{10... | collective-permute-start | bytes 786440 | tf_op jit(solution)/shard_map/ppermute | solution.py:30
  20.1 15.3 %collective-permute-start.10 = (bf16[128,1024]{1,0:T(8,128)(2,1)}, bf16[128,1024]{1,0:T(8,128)(2,1)S(1)}, u32[]{:S(2)}, u32[]{:S(2)}) collective-permute-start(bf16[128,1024]{1,0:T(8,128)(2,1)} %get-tuple-element.101.refs_3_.refs_12_), channel_id=1, source_target_pairs={{0,16},{8,24},{16,0},{24,8},{1,17},{9,25},{17,1},{25,9},{2,18},{10... | collective-permute-start | bytes 786440 | tf_op jit(solution)/shard_map/ppermute | solution.py:30
  20.6 14.8 %collective-permute-start.5 = (bf16[128,1024]{1,0:T(8,128)(2,1)S(1)}, bf16[128,1024]{1,0:T(8,128)(2,1)S(1)}, u32[]{:S(2)}, u32[]{:S(2)}) collective-permute-start(bf16[128,1024]{1,0:T(8,128)(2,1)S(1)} %collective-permute-done.4.refs_6_), channel_id=1, source_target_pairs={{0,8},{8,0},{16,24},{24,16},{1,9},{9,1},{17,25},{25,17},{2,10},{10... | collective-permute-start | bytes 786440 | tf_op jit(solution)/shard_map/ppermute | solution.py:30
  24.2 11.2 %collective-permute-start.6 = (bf16[128,1024]{1,0:T(8,128)(2,1)}, bf16[128,1024]{1,0:T(8,128)(2,1)S(1)}, u32[]{:S(2)}, u32[]{:S(2)}) collective-permute-start(bf16[128,1024]{1,0:T(8,128)(2,1)} %get-tuple-element.97.refs_2_.refs_8_), channel_id=1, source_target_pairs={{0,8},{8,0},{16,24},{24,16},{1,9},{9,1},{17,25},{25,17},{2,10},{10... | collective-permute-start | bytes 786440 | tf_op jit(solution)/shard_map/ppermute | solution.py:30
  24.3 17.7 %collective-permute-start.7 = (bf16[128,1024]{1,0:T(8,128)(2,1)}, bf16[128,1024]{1,0:T(8,128)(2,1)S(1)}, u32[]{:S(2)}, u32[]{:S(2)}) collective-permute-start(bf16[128,1024]{1,0:T(8,128)(2,1)} %get-tuple-element.97.refs_2_.refs_8_), channel_id=1, source_target_pairs={{0,16},{8,24},{16,0},{24,8},{1,17},{9,25},{17,1},{25,9},{2,18},{10... | collective-permute-start | bytes 786440 | tf_op jit(solution)/shard_map/ppermute | solution.py:30
  29.8 12.1 %collective-permute-start.9 = (bf16[128,1024]{1,0:T(8,128)(2,1)}, bf16[128,1024]{1,0:T(8,128)(2,1)S(1)}, u32[]{:S(2)}, u32[]{:S(2)}) collective-permute-start(bf16[128,1024]{1,0:T(8,128)(2,1)} %get-tuple-element.101.refs_3_.refs_12_), channel_id=1, source_target_pairs={{0,8},{8,0},{16,24},{24,16},{1,9},{9,1},{17,25},{25,17},{2,10},{10... | collective-permute-start | bytes 786440 | tf_op jit(solution)/shard_map/ppermute | solution.py:30
  35.4 9.7 %collective-permute-start.8 = (bf16[128,1024]{1,0:T(8,128)(2,1)S(1)}, bf16[128,1024]{1,0:T(8,128)(2,1)S(1)}, u32[]{:S(2)}, u32[]{:S(2)}) collective-permute-start(bf16[128,1024]{1,0:T(8,128)(2,1)S(1)} %collective-permute-done.6.refs_9_), channel_id=1, source_target_pairs={{0,16},{8,24},{16,0},{24,8},{1,17},{9,25},{17,1},{25,9},{2,18},{10... | collective-permute-start | bytes 786440 | tf_op jit(solution)/shard_map/ppermute | solution.py:30
  37.0 8.2 %collective-permute-start.11 = (bf16[128,1024]{1,0:T(8,128)(2,1)S(1)}, bf16[128,1024]{1,0:T(8,128)(2,1)}, u32[]{:S(2)}, u32[]{:S(2)}) collective-permute-start(bf16[128,1024]{1,0:T(8,128)(2,1)S(1)} %collective-permute-done.10.refs_14_), channel_id=1, source_target_pairs={{0,8},{8,0},{16,24},{24,16},{1,9},{9,1},{17,25},{25,17},{2,10},{10... | collective-permute-start | bytes 786440 | tf_op jit(solution)/shard_map/ppermute | solution.py:30
  63.9 2.3 %collective-permute-start.12 = (bf16[128,2304]{1,0:T(8,128)(2,1)}, bf16[128,2304]{1,0:T(8,128)(2,1)S(1)}, u32[]{:S(2)}, u32[]{:S(2)}) collective-permute-start(bf16[128,2304]{1,0:T(8,128)(2,1)} %get-tuple-element.106), channel_id=1, source_target_pairs={{0,1},{1,0},{2,3},{3,2},{4,5},{5,4},{6,7},{7,6},{8,9},{9,8},{10,11... | collective-permute-start | bytes 1769480 | tf_op jit(solution)/shard_map/ppermute | solution.py:30
  67.3 6.8 %collective-permute-start.14 = (bf16[32,2304]{1,0:T(8,128)(2,1)S(1)}, bf16[32,2304]{1,0:T(8,128)(2,1)S(1)}, u32[]{:S(2)}, u32[]{:S(2)}) collective-permute-start(bf16[32,2304]{1,0:T(8,128)(2,1)S(1)} %get-tuple-element.161), channel_id=1, source_target_pairs={{0,2},{1,3},{2,0},{3,1},{4,6},{5,7},{6,4},{7,5},{8,10},{9,11},{10,... | collective-permute-start | bytes 442376 | tf_op jit(solution)/shard_map/ppermute | solution.py:30
  68.9 8.7 %collective-permute-start.16 = (bf16[128,2304]{1,0:T(8,128)(2,1)}, bf16[128,2304]{1,0:T(8,128)(2,1)S(1)}, u32[]{:S(2)}, u32[]{:S(2)}) collective-permute-start(bf16[128,2304]{1,0:T(8,128)(2,1)} %get-tuple-element.108), channel_id=1, source_target_pairs={{0,1},{1,0},{2,3},{3,2},{4,5},{5,4},{6,7},{7,6},{8,9},{9,8},{10,11... | collective-permute-start | bytes 1769480 | tf_op jit(solution)/shard_map/ppermute | solution.py:30
  68.9 10.9 %collective-permute-start.13 = (bf16[32,2304]{1,0:T(8,128)(2,1)S(1)}, bf16[32,2304]{1,0:T(8,128)(2,1)S(1)}, u32[]{:S(2)}, u32[]{:S(2)}) collective-permute-start(bf16[32,2304]{1,0:T(8,128)(2,1)S(1)} %get-tuple-element.160), channel_id=1, source_target_pairs={{0,2},{1,3},{2,0},{3,1},{4,6},{5,7},{6,4},{7,5},{8,10},{9,11},{10,... | collective-permute-start | bytes 442376 | tf_op jit(solution)/shard_map/ppermute | solution.py:30
  75.1 8.1 %collective-permute-start.15 = (bf16[32,2304]{1,0:T(8,128)(2,1)S(1)}, bf16[32,2304]{1,0:T(8,128)(2,1)S(1)}, u32[]{:S(2)}, u32[]{:S(2)}) collective-permute-start(bf16[32,2304]{1,0:T(8,128)(2,1)S(1)} %add_convert_fusion.7), channel_id=1, source_target_pairs={{0,4},{1,5},{2,6},{3,7},{4,0},{5,1},{6,2},{7,3},{8,12},{9,13},{10,... | collective-permute-start | bytes 442376 | tf_op jit(solution)/shard_map/ppermute | solution.py:30
  77.7 19.4 %collective-permute-start.17 = (bf16[32,2304]{1,0:T(8,128)(2,1)S(1)}, bf16[32,2304]{1,0:T(8,128)(2,1)S(1)}, u32[]{:S(2)}, u32[]{:S(2)}) collective-permute-start(bf16[32,2304]{1,0:T(8,128)(2,1)S(1)} %get-tuple-element.109), channel_id=1, source_target_pairs={{0,2},{1,3},{2,0},{3,1},{4,6},{5,7},{6,4},{7,5},{8,10},{9,11},{10,... | collective-permute-start | bytes 442376 | tf_op jit(solution)/shard_map/ppermute | solution.py:30
  79.3 9.1 %collective-permute-start.18 = (bf16[32,2304]{1,0:T(8,128)(2,1)S(1)}, bf16[32,2304]{1,0:T(8,128)(2,1)S(1)}, u32[]{:S(2)}, u32[]{:S(2)}) collective-permute-start(bf16[32,2304]{1,0:T(8,128)(2,1)S(1)} %get-tuple-element.110), channel_id=1, source_target_pairs={{0,2},{1,3},{2,0},{3,1},{4,6},{5,7},{6,4},{7,5},{8,10},{9,11},{10,... | collective-permute-start | bytes 442376 | tf_op jit(solution)/shard_map/ppermute | solution.py:30
  84.3 12.8 %collective-permute-start.21 = (bf16[32,2304]{1,0:T(8,128)(2,1)S(1)}, bf16[32,2304]{1,0:T(8,128)(2,1)S(1)}, u32[]{:S(2)}, u32[]{:S(2)}) collective-permute-start(bf16[32,2304]{1,0:T(8,128)(2,1)S(1)} %get-tuple-element.113.refs_0_), channel_id=1, source_target_pairs={{0,4},{1,5},{2,6},{3,7},{4,0},{5,1},{6,2},{7,3},{8,12},{9,13},{10,... | collective-permute-start | bytes 442376 | tf_op jit(solution)/shard_map/ppermute | solution.py:30
  88.5 10.6 %collective-permute-start.19 = (bf16[32,2304]{1,0:T(8,128)(2,1)S(1)}, bf16[32,2304]{1,0:T(8,128)(2,1)S(1)}, u32[]{:S(2)}, u32[]{:S(2)}) collective-permute-start(bf16[32,2304]{1,0:T(8,128)(2,1)S(1)} %add_convert_fusion.4), channel_id=1, source_target_pairs={{0,4},{1,5},{2,6},{3,7},{4,0},{5,1},{6,2},{7,3},{8,12},{9,13},{10,... | collective-permute-start | bytes 442376 | tf_op jit(solution)/shard_map/ppermute | solution.py:30
  88.8 19.5 %collective-permute-start.23 = (bf16[32,2304]{1,0:T(8,128)(2,1)S(1)}, bf16[32,2304]{1,0:T(8,128)(2,1)S(1)}, u32[]{:S(2)}, u32[]{:S(2)}) collective-permute-start(bf16[32,2304]{1,0:T(8,128)(2,1)S(1)} %get-tuple-element.113.refs_0_), channel_id=1, source_target_pairs={{0,1},{1,0},{2,3},{3,2},{4,5},{5,4},{6,7},{7,6},{8,9},{9,8},{10,11... | collective-permute-start | bytes 442376 | tf_op jit(solution)/shard_map/ppermute | solution.py:30
  88.8 11.3 %collective-permute-start.20 = (bf16[32,2304]{1,0:T(8,128)(2,1)S(1)}, bf16[32,2304]{1,0:T(8,128)(2,1)S(1)}, u32[]{:S(2)}, u32[]{:S(2)}) collective-permute-start(bf16[32,2304]{1,0:T(8,128)(2,1)S(1)} %get-tuple-element.113.refs_0_), channel_id=1, source_target_pairs={{0,2},{1,3},{2,0},{3,1},{4,6},{5,7},{6,4},{7,5},{8,10},{9,11},{10,... | collective-permute-start | bytes 442376 | tf_op jit(solution)/shard_map/ppermute | solution.py:30
  97.1 5.9 %collective-permute-start.22 = (bf16[32,2304]{1,0:T(8,128)(2,1)S(1)}, bf16[32,2304]{1,0:T(8,128)(2,1)S(1)}, u32[]{:S(2)}, u32[]{:S(2)}) collective-permute-start(bf16[32,2304]{1,0:T(8,128)(2,1)S(1)} %collective-permute-done.21.refs_2_), channel_id=1, source_target_pairs={{0,2},{1,3},{2,0},{3,1},{4,6},{5,7},{6,4},{7,5},{8,10},{9,11},{10,... | collective-permute-start | bytes 442376 | tf_op jit(solution)/shard_map/ppermute | solution.py:30
  99.1 9.3 %collective-permute-start.25 = (bf16[32,2304]{1,0:T(8,128)(2,1)S(1)}, bf16[32,2304]{1,0:T(8,128)(2,1)S(1)}, u32[]{:S(2)}, u32[]{:S(2)}) collective-permute-start(bf16[32,2304]{1,0:T(8,128)(2,1)S(1)} %collective-permute-done.21.refs_2_), channel_id=1, source_target_pairs={{0,1},{1,0},{2,3},{3,2},{4,5},{5,4},{6,7},{7,6},{8,9},{9,8},{10,11... | collective-permute-start | bytes 442376 | tf_op jit(solution)/shard_map/ppermute | solution.py:30
  100.1 8.9 %collective-permute-start.24 = (bf16[32,2304]{1,0:T(8,128)(2,1)S(1)}, bf16[32,2304]{1,0:T(8,128)(2,1)S(1)}, u32[]{:S(2)}, u32[]{:S(2)}) collective-permute-start(bf16[32,2304]{1,0:T(8,128)(2,1)S(1)} %collective-permute-done.20.refs_1_), channel_id=1, source_target_pairs={{0,1},{1,0},{2,3},{3,2},{4,5},{5,4},{6,7},{7,6},{8,9},{9,8},{10,11... | collective-permute-start | bytes 442376 | tf_op jit(solution)/shard_map/ppermute | solution.py:30
  103.0 6.0 %collective-permute-start.26 = (bf16[32,2304]{1,0:T(8,128)(2,1)S(1)}, bf16[32,2304]{1,0:T(8,128)(2,1)S(1)}, u32[]{:S(2)}, u32[]{:S(2)}) collective-permute-start(bf16[32,2304]{1,0:T(8,128)(2,1)S(1)} %collective-permute-done.22.refs_3_), channel_id=1, source_target_pairs={{0,1},{1,0},{2,3},{3,2},{4,5},{5,4},{6,7},{7,6},{8,9},{9,8},{10,11... | collective-permute-start | bytes 442376 | tf_op jit(solution)/shard_map/ppermute | solution.py:30
  103.9 16.9 %collective-permute-start.29 = (bf16[32,2304]{1,0:T(8,128)(2,1)S(1)}, bf16[32,2304]{1,0:T(8,128)(2,1)S(1)}, u32[]{:S(2)}, u32[]{:S(2)}) collective-permute-start(bf16[32,2304]{1,0:T(8,128)(2,1)S(1)} %get-tuple-element.122.refs_0_), channel_id=1, source_target_pairs={{0,6},{1,7},{2,4},{3,5},{4,2},{5,3},{6,0},{7,1},{8,14},{9,15},{10,... | collective-permute-start | bytes 442376 | tf_op jit(solution)/shard_map/ppermute | solution.py:30
  108.3 12.5 %collective-permute-start.28 = (bf16[32,2304]{1,0:T(8,128)(2,1)S(1)}, bf16[32,2304]{1,0:T(8,128)(2,1)S(1)}, u32[]{:S(2)}, u32[]{:S(2)}) collective-permute-start(bf16[32,2304]{1,0:T(8,128)(2,1)S(1)} %get-tuple-element.122.refs_0_), channel_id=1, source_target_pairs={{0,4},{1,5},{2,6},{3,7},{4,0},{5,1},{6,2},{7,3},{8,12},{9,13},{10,... | collective-permute-start | bytes 442376 | tf_op jit(solution)/shard_map/ppermute | solution.py:30
  108.4 12.5 %collective-permute-start.27 = (bf16[32,2304]{1,0:T(8,128)(2,1)S(1)}, bf16[32,2304]{1,0:T(8,128)(2,1)S(1)}, u32[]{:S(2)}, u32[]{:S(2)}) collective-permute-start(bf16[32,2304]{1,0:T(8,128)(2,1)S(1)} %get-tuple-element.122.refs_0_), channel_id=1, source_target_pairs={{0,2},{1,3},{2,0},{3,1},{4,6},{5,7},{6,4},{7,5},{8,10},{9,11},{10,... | collective-permute-start | bytes 442376 | tf_op jit(solution)/shard_map/ppermute | solution.py:30
  120.8 4.1 %collective-permute-start.30 = (bf16[32,2304]{1,0:T(8,128)(2,1)S(1)}, bf16[32,2304]{1,0:T(8,128)(2,1)S(1)}, u32[]{:S(2)}, u32[]{:S(2)}) collective-permute-start(bf16[32,2304]{1,0:T(8,128)(2,1)S(1)} %get-tuple-element.122.refs_0_), channel_id=1, source_target_pairs={{0,1},{1,0},{2,3},{3,2},{4,5},{5,4},{6,7},{7,6},{8,9},{9,8},{10,11... | collective-permute-start | bytes 442376 | tf_op jit(solution)/shard_map/ppermute | solution.py:30
  120.9 4.0 %collective-permute-start.31 = (bf16[32,2304]{1,0:T(8,128)(2,1)S(1)}, bf16[32,2304]{1,0:T(8,128)(2,1)S(1)}, u32[]{:S(2)}, u32[]{:S(2)}) collective-permute-start(bf16[32,2304]{1,0:T(8,128)(2,1)S(1)} %collective-permute-done.27.refs_1_), channel_id=1, source_target_pairs={{0,1},{1,0},{2,3},{3,2},{4,5},{5,4},{6,7},{7,6},{8,9},{9,8},{10,11... | collective-permute-start | bytes 442376 | tf_op jit(solution)/shard_map/ppermute | solution.py:30
  121.4 17.7 %collective-permute-start.36 = (bf16[2,64,1024]{2,1,0:T(8,128)(2,1)S(1)}, bf16[2,64,1024]{2,1,0:T(8,128)(2,1)S(1)}, u32[]{:S(2)}, u32[]{:S(2)}) collective-permute-start(bf16[2,64,1024]{2,1,0:T(8,128)(2,1)S(1)} %get-tuple-element.134), channel_id=1, source_target_pairs={{0,16},{8,24},{16,0},{24,8},{1,17},{9,25},{17,1},{25,9},{2,18},{10... | collective-permute-start | bytes 786440 | tf_op jit(solution)/shard_map/ppermute | solution.py:30
  122.9 17.7 %collective-permute-start.34 = (bf16[2,64,1024]{2,1,0:T(8,128)(2,1)S(1)}, bf16[2,64,1024]{2,1,0:T(8,128)(2,1)S(1)}, u32[]{:S(2)}, u32[]{:S(2)}) collective-permute-start(bf16[2,64,1024]{2,1,0:T(8,128)(2,1)S(1)} %get-tuple-element.130), channel_id=1, source_target_pairs={{0,8},{8,0},{16,24},{24,16},{1,9},{9,1},{17,25},{25,17},{2,10},{10... | collective-permute-start | bytes 786440 | tf_op jit(solution)/shard_map/ppermute | solution.py:30
  123.3 17.3 %collective-permute-start.35 = (bf16[2,64,1024]{2,1,0:T(8,128)(2,1)S(1)}, bf16[2,64,1024]{2,1,0:T(8,128)(2,1)S(1)}, u32[]{:S(2)}, u32[]{:S(2)}) collective-permute-start(bf16[2,64,1024]{2,1,0:T(8,128)(2,1)S(1)} %get-tuple-element.131), channel_id=1, source_target_pairs={{0,8},{8,0},{16,24},{24,16},{1,9},{9,1},{17,25},{25,17},{2,10},{10... | collective-permute-start | bytes 786440 | tf_op jit(solution)/shard_map/ppermute | solution.py:30
  124.9 1.9 %collective-permute-start.33 = (bf16[32,2304]{1,0:T(8,128)(2,1)S(1)}, bf16[32,2304]{1,0:T(8,128)(2,1)S(1)}, u32[]{:S(2)}, u32[]{:S(2)}) collective-permute-start(bf16[32,2304]{1,0:T(8,128)(2,1)S(1)} %collective-permute-done.29.refs_3_), channel_id=1, source_target_pairs={{0,1},{1,0},{2,3},{3,2},{4,5},{5,4},{6,7},{7,6},{8,9},{9,8},{10,11... | collective-permute-start | bytes 442376 | tf_op jit(solution)/shard_map/ppermute | solution.py:30
  126.3 14.4 %collective-permute-start.38 = (bf16[2,64,1024]{2,1,0:T(8,128)(2,1)S(1)}, bf16[2,64,1024]{2,1,0:T(8,128)(2,1)S(1)}, u32[]{:S(2)}, u32[]{:S(2)}) collective-permute-start(bf16[2,64,1024]{2,1,0:T(8,128)(2,1)S(1)} %get-tuple-element.137), channel_id=1, source_target_pairs={{0,16},{8,24},{16,0},{24,8},{1,17},{9,25},{17,1},{25,9},{2,18},{10... | collective-permute-start | bytes 786440 | tf_op jit(solution)/shard_map/ppermute | solution.py:30
  138.6 9.2 %collective-permute-start.40 = (bf16[2,64,1024]{2,1,0:T(8,128)(2,1)S(1)}, bf16[2,64,1024]{2,1,0:T(8,128)(2,1)S(1)}, u32[]{:S(2)}, u32[]{:S(2)}) collective-permute-start(bf16[2,64,1024]{2,1,0:T(8,128)(2,1)S(1)} %get-tuple-element.140), channel_id=1, source_target_pairs={{0,8},{8,0},{16,24},{24,16},{1,9},{9,1},{17,25},{25,17},{2,10},{10... | collective-permute-start | bytes 786440 | tf_op jit(solution)/shard_map/ppermute | solution.py:30
  139.1 9.2 %collective-permute-start.41 = (bf16[2,64,1024]{2,1,0:T(8,128)(2,1)S(1)}, bf16[2,64,1024]{2,1,0:T(8,128)(2,1)S(1)}, u32[]{:S(2)}, u32[]{:S(2)}) collective-permute-start(bf16[2,64,1024]{2,1,0:T(8,128)(2,1)S(1)} %get-tuple-element.142), channel_id=1, source_target_pairs={{0,16},{8,24},{16,0},{24,8},{1,17},{9,25},{17,1},{25,9},{2,18},{10... | collective-permute-start | bytes 786440 | tf_op jit(solution)/shard_map/ppermute | solution.py:30
  140.7 12.0 %collective-permute-start.37 = (bf16[2,64,1024]{2,1,0:T(8,128)(2,1)S(1)}, bf16[2,64,1024]{2,1,0:T(8,128)(2,1)S(1)}, u32[]{:S(2)}, u32[]{:S(2)}) collective-permute-start(bf16[2,64,1024]{2,1,0:T(8,128)(2,1)S(1)} %add_convert_fusion.3), channel_id=1, source_target_pairs={{0,16},{8,24},{16,0},{24,8},{1,17},{9,25},{17,1},{25,9},{2,18},{10... | collective-permute-start | bytes 786440 | tf_op jit(solution)/shard_map/ppermute | solution.py:30
  141.4 11.3 %collective-permute-start.39 = (bf16[2,64,1024]{2,1,0:T(8,128)(2,1)S(1)}, bf16[2,64,1024]{2,1,0:T(8,128)(2,1)S(1)}, u32[]{:S(2)}, u32[]{:S(2)}) collective-permute-start(bf16[2,64,1024]{2,1,0:T(8,128)(2,1)S(1)} %add_convert_fusion.2), channel_id=1, source_target_pairs={{0,8},{8,0},{16,24},{24,16},{1,9},{9,1},{17,25},{25,17},{2,10},{10... | collective-permute-start | bytes 786440 | tf_op jit(solution)/shard_map/ppermute | solution.py:30
  152.7 6.4 %collective-permute-start.44 = (f32[8,128]{1,0:T(8,128)S(1)}, f32[8,128]{1,0:T(8,128)S(1)}, u32[]{:S(2)}, u32[]{:S(2)}) collective-permute-start(f32[8,128]{1,0:T(8,128)S(1)} %add.152), channel_id=1, source_target_pairs={{0,24},{8,16},{16,8},{24,0},{1,25},{9,17},{17,9},{25,1},{2,26},{10... | collective-permute-start | bytes 12296 | tf_op jit(solution)/shard_map/ppermute | solution.py:30
  155.0 4.7 %collective-permute-start.43 = (f32[8,128]{1,0:T(8,128)S(1)}, f32[8,128]{1,0:T(8,128)S(1)}, u32[]{:S(2)}, u32[]{:S(2)}) collective-permute-start(f32[8,128]{1,0:T(8,128)S(1)} %add.152), channel_id=1, source_target_pairs={{0,16},{8,24},{16,0},{24,8},{1,17},{9,25},{17,1},{25,9},{2,18},{10... | collective-permute-start | bytes 12296 | tf_op jit(solution)/shard_map/ppermute | solution.py:30
  155.7 14.4 %collective-permute-start.47 = (bf16[2,64,1024]{2,1,0:T(8,128)(2,1)S(1)}, bf16[2,64,1024]{2,1,0:T(8,128)(2,1)S(1)}, u32[]{:S(2)}, u32[]{:S(2)}) collective-permute-start(bf16[2,64,1024]{2,1,0:T(8,128)(2,1)S(1)} %add_convert_fusion.1), channel_id=1, source_target_pairs={{0,16},{8,24},{16,0},{24,8},{1,17},{9,25},{17,1},{25,9},{2,18},{10... | collective-permute-start | bytes 786440 | tf_op jit(solution)/shard_map/ppermute | solution.py:30
  157.1 13.0 %collective-permute-start.48 = (bf16[2,64,1024]{2,1,0:T(8,128)(2,1)S(1)}, bf16[2,64,1024]{2,1,0:T(8,128)(2,1)S(1)}, u32[]{:S(2)}, u32[]{:S(2)}) collective-permute-start(bf16[2,64,1024]{2,1,0:T(8,128)(2,1)S(1)} %add_convert_fusion), channel_id=1, source_target_pairs={{0,8},{8,0},{16,24},{24,16},{1,9},{9,1},{17,25},{25,17},{2,10},{10... | collective-permute-start | bytes 786440 | tf_op jit(solution)/shard_map/ppermute | solution.py:30
  157.5 12.5 %collective-permute-start.45 = (bf16[2,64,1024]{2,1,0:T(8,128)(2,1)S(1)}, bf16[2,64,1024]{2,1,0:T(8,128)(2,1)S(1)}, u32[]{:S(2)}, u32[]{:S(2)}) collective-permute-start(bf16[2,64,1024]{2,1,0:T(8,128)(2,1)S(1)} %get-tuple-element.155), channel_id=1, source_target_pairs={{0,8},{8,0},{16,24},{24,16},{1,9},{9,1},{17,25},{25,17},{2,10},{10... | collective-permute-start | bytes 786440 | tf_op jit(solution)/shard_map/ppermute | solution.py:30
  159.1 11.0 %collective-permute-start.46 = (bf16[2,64,1024]{2,1,0:T(8,128)(2,1)S(1)}, bf16[2,64,1024]{2,1,0:T(8,128)(2,1)S(1)}, u32[]{:S(2)}, u32[]{:S(2)}) collective-permute-start(bf16[2,64,1024]{2,1,0:T(8,128)(2,1)S(1)} %get-tuple-element.157), channel_id=1, source_target_pairs={{0,16},{8,24},{16,0},{24,8},{1,17},{9,25},{17,1},{25,9},{2,18},{10... | collective-permute-start | bytes 786440 | tf_op jit(solution)/shard_map/ppermute | solution.py:30
  159.7 9.1 %collective-permute-start.42 = (f32[8,128]{1,0:T(8,128)S(1)}, f32[8,128]{1,0:T(8,128)S(1)}, u32[]{:S(2)}, u32[]{:S(2)}) collective-permute-start(f32[8,128]{1,0:T(8,128)S(1)} %add.152), channel_id=1, source_target_pairs={{0,8},{8,0},{16,24},{24,16},{1,9},{9,1},{17,25},{25,17},{2,10},{10... | collective-permute-start | bytes 12296 | tf_op jit(solution)/shard_map/ppermute | solution.py:30
  (19 other events, 284.5 us)

commit v13 on v11

--- a/solution.py
+++ b/solution.py
@@ -542,14 +542,13 @@
         feat_grad = finish(plan, c, kept, got, feat_grad)
 
     squares, = after([squares], seconds[0])
-    loss = jnp.full((8, 128), jnp.sum(squares), F32)
-    parts = [loss] + [swap(loss, "grp", groups, j) for j in range(1, groups)]
+    parts = [squares] + [swap(squares, "grp", groups, j) for j in range(1, groups)]
     parts = after(parts, second + ([] if before_last is None else [before_last]))
     while len(parts) > 1:
         parts = [x + y for x, y in zip(parts[::2], parts[1::2])]
-    loss = parts[0]
+    loss = jnp.sum(parts[0])
     entries = targets.shape[0] * groups * plan.tokens * plan.model
-    recon_loss = loss[0, 0] / entries
+    recon_loss = loss / entries
     recon = jnp.concatenate(recon_parts, axis=0)[None]
     return active, recon, recon_loss, feat_grad
 

time: 171 us -> 168 us (0.982)
  other arithmetic: 11.9 us -> 5.9 us
  waiting for transfers between devices: 49.6 us -> 52.8 us
  starting transfers between devices: 44.4 us -> 46.2 us
    convert_element_type x4, other arithmetic: 3.59 us -> 0.23 us  [per_device(): sum((x.astype(F32) for x in own)).astype(BF16)]
    ppermute x49, waiting for transfers between devices: 49.6 us -> 52.8 us  [swap(): return lax.ppermute(x, axis, [(i, i ^ offset) for i in range(size)])]
    ppermute x49, starting transfers between devices: 44.4 us -> 46.2 us  [swap(): return lax.ppermute(x, axis, [(i, i ^ offset) for i in range(size)])]
  transfers between devices with their start and end apart: 49 -> 49, of which waited for: 19 -> 21; matrix products, arithmetic and copies ran while one was open for 7% -> 3% of each run, Pallas kernels for 19% -> 19%
where the time goes in v13:
time: 168 us; the launch traced here: 167 us
  Pallas kernels  56.4 us (34%)
  waiting for transfers between devices  52.8 us (31%)
  starting transfers between devices  46.2 us (28%)
  other arithmetic  5.9 us (4%)
  local copies, waits for them, and re-layouts  3.24 us (2%)
  between operations  2.79 us (2%)
    pallas_call x8, Pallas kernels, call(): pl.pallas_call(kernel, in_specs=in_specs, out_shape=out_shape, scratch_sh...  56.4 us
    ppermute x49, waiting for transfers between devices, swap(): return lax.ppermute(x, axis, [(i, i ^ offset) for i in range(size)])  52.8 us
    ppermute x49, starting transfers between devices, swap(): return lax.ppermute(x, axis, [(i, i ^ offset) for i in range(size)])  46.2 us
  transfers between devices with their start and end apart: 49, of which 21 were waited for; matrix products, arithmetic and copies ran while one was open for 3% of the time, Pallas kernels for 19%

profile of v13, /device:TPU:0, one launch (start us, length us, event | category | flops | bytes accessed | tf_op | source)
XLA Modules:
  0.0 167.4 jit_solution(17100699365609441881)
XLA Ops:
  0.6 5.5 %encode.2 = (bf16[128,1024]{1,0:T(8,128)(2,1)}, bf16[128,1024]{1,0:T(8,128)(2,1)}) custom-call(bf16[4,128,2304]{2,1,0:T(8,128)(2,1)} %resid_ref.3, bf16[4,2304,1024]{2,1,0:T(8,128)(2,1)} %w_ref.3, f32[4,1024]{1,0:T(4,128)} %b_ref.3), custom_call_target="tpu_custom_call" | custom-call | flops 1048576 | bytes 1024 | tf_op jit(solution)/shard_map/encode/pallas_call | solution.py:103
  6.1 3.0 %collective-permute-start = (bf16[128,1024]{1,0:T(8,128)(2,1)}, bf16[128,1024]{1,0:T(8,128)(2,1)S(1)}, u32[]{:S(2)}, u32[]{:S(2)}) collective-permute-start(bf16[128,1024]{1,0:T(8,128)(2,1)} %get-tuple-element.89.refs_0_), channel_id=1, source_target_pairs={{0,8},{8,0},{16,24},{24,16},{1,9},{9,1},{17,25},{25,17},{2,10},{10... | collective-permute-start | bytes 786440 | tf_op jit(solution)/shard_map/ppermute | solution.py:30
  9.1 1.5 collective-permute-start.4
  11.3 5.5 %encode.3 = (bf16[128,1024]{1,0:T(8,128)(2,1)}, bf16[128,1024]{1,0:T(8,128)(2,1)}) custom-call(bf16[4,128,2304]{2,1,0:T(8,128)(2,1)} %resid_ref.3, bf16[4,2304,1024]{2,1,0:T(8,128)(2,1)} %w_ref.3, f32[4,1024]{1,0:T(4,128)} %b_ref.3), custom_call_target="tpu_custom_call" | custom-call | flops 1048576 | bytes 1024 | tf_op jit(solution)/shard_map/encode/pallas_call | solution.py:103
  16.7 1.8 %collective-permute-done.4.refs_6_ = bf16[128,1024]{1,0:T(8,128)(2,1)S(1)} collective-permute-done((bf16[128,1024]{1,0:T(8,128)(2,1)}, bf16[128,1024]{1,0:T(8,128)(2,1)S(1)}, u32[]{:S(2)}, u32[]{:S(2)}) %collective-permute-start.4) | collective-permute-done | bytes 262176 | tf_op jit(solution)/shard_map/ppermute | solution.py:30
  18.6 1.5 collective-permute-start.2
  20.8 3.4 %collective-permute-done.1.refs_2_ = bf16[128,1024]{1,0:T(8,128)(2,1)S(1)} collective-permute-done((bf16[128,1024]{1,0:T(8,128)(2,1)}, bf16[128,1024]{1,0:T(8,128)(2,1)S(1)}, u32[]{:S(2)}, u32[]{:S(2)}) %collective-permute-start.1) | collective-permute-done | bytes 262176 | tf_op jit(solution)/shard_map/ppermute | solution.py:30
  24.3 2.0 %collective-permute-start.7 = (bf16[128,1024]{1,0:T(8,128)(2,1)}, bf16[128,1024]{1,0:T(8,128)(2,1)S(1)}, u32[]{:S(2)}, u32[]{:S(2)}) collective-permute-start(bf16[128,1024]{1,0:T(8,128)(2,1)} %get-tuple-element.97.refs_2_.refs_8_), channel_id=1, source_target_pairs={{0,16},{8,24},{16,0},{24,8},{1,17},{9,25},{17,1},{25,9},{2,18},{10... | collective-permute-start | bytes 786440 | tf_op jit(solution)/shard_map/ppermute | solution.py:30
  26.3 3.5 %collective-permute-done.2.refs_3_ = bf16[128,1024]{1,0:T(8,128)(2,1)S(1)} collective-permute-done((bf16[128,1024]{1,0:T(8,128)(2,1)S(1)}, bf16[128,1024]{1,0:T(8,128)(2,1)S(1)}, u32[]{:S(2)}, u32[]{:S(2)}) %collective-permute-start.2) | collective-permute-done | bytes 262176 | tf_op jit(solution)/shard_map/ppermute | solution.py:30
  29.9 5.5 %collective-permute-done.10.refs_14_ = bf16[128,1024]{1,0:T(8,128)(2,1)S(1)} collective-permute-done((bf16[128,1024]{1,0:T(8,128)(2,1)}, bf16[128,1024]{1,0:T(8,128)(2,1)S(1)}, u32[]{:S(2)}, u32[]{:S(2)}) %collective-permute-start.10) | collective-permute-done | bytes 262176 | tf_op jit(solution)/shard_map/ppermute | solution.py:30
  35.4 1.6 collective-permute-start.8
  40.2 1.7 %arrange.1 = bf16[128,4,1024]{2,1,0:T(4,128)(2,1)} custom-call(bf16[128,1024]{1,0:T(8,128)(2,1)S(1)} %copy-done, bf16[128,1024]{1,0:T(8,128)(2,1)S(1)} %copy-done.1, bf16[128,1024]{1,0:T(8,128)(2,1)S(1)} %copy-done.2, bf16[128,1024]{1,0:T(8,128)(2,1)S(1)} %copy-done.3), custom_call_target="tpu_custom_call" | custom-call | flops 1048576 | bytes 1024 | tf_op jit(solution)/shard_map/arrange/pallas_call | solution.py:103
  41.9 3.3 %collective-permute-done.8.refs_11_ = bf16[128,1024]{1,0:T(8,128)(2,1)S(1)} collective-permute-done((bf16[128,1024]{1,0:T(8,128)(2,1)S(1)}, bf16[128,1024]{1,0:T(8,128)(2,1)S(1)}, u32[]{:S(2)}, u32[]{:S(2)}) %collective-permute-start.8) | collective-permute-done | bytes 262176 | tf_op jit(solution)/shard_map/ppermute | solution.py:30
  45.9 17.6 %decode.1 = (bf16[128,2304]{1,0:T(8,128)(2,1)}, bf16[128,2304]{1,0:T(8,128)(2,1)}, f32[128,2304]{1,0:T(8,128)}, f32[128,2304]{1,0:T(8,128)}) custom-call(s32[17]{0:T(128)} %concatenate.6.index_ref, bf16[128,1024]{1,0:T(8,128)(2,1)} %get-tuple-element.89.refs_0_, bf16[128,1024]{1,0:T(8,128)(2,1)} %copy-done.6, bf16[128,1024]{1,0:T(8,128)(2,1)} %copy-done.8, ...), custom_call_target="tpu_custom_call" | custom-call | flops 1048576 | bytes 1024 | tf_op jit(solution)/shard_map/decode/pallas_call | solution.py:103
  63.6 2.2 %collective-permute-done.12 = bf16[128,2304]{1,0:T(8,128)(2,1)S(1)} collective-permute-done((bf16[128,2304]{1,0:T(8,128)(2,1)}, bf16[128,2304]{1,0:T(8,128)(2,1)S(1)}, u32[]{:S(2)}, u32[]{:S(2)}) %collective-permute-start.12) | collective-permute-done | bytes 589856 | tf_op jit(solution)/shard_map/ppermute | solution.py:30
  65.8 1.1 add_convert_fusion.9
  66.9 1.6 collective-permute-start.14
  69.0 4.7 %collective-permute-done.14 = bf16[32,2304]{1,0:T(8,128)(2,1)S(1)} collective-permute-done((bf16[32,2304]{1,0:T(8,128)(2,1)S(1)}, bf16[32,2304]{1,0:T(8,128)(2,1)S(1)}, u32[]{:S(2)}, u32[]{:S(2)}) %collective-permute-start.14) | collective-permute-done | bytes 147488 | tf_op jit(solution)/shard_map/ppermute | solution.py:30
  73.7 1.0 add_convert_fusion.7
  74.7 2.7 %collective-permute-start.15 = (bf16[32,2304]{1,0:T(8,128)(2,1)S(1)}, bf16[32,2304]{1,0:T(8,128)(2,1)S(1)}, u32[]{:S(2)}, u32[]{:S(2)}) collective-permute-start(bf16[32,2304]{1,0:T(8,128)(2,1)S(1)} %add_convert_fusion.7), channel_id=1, source_target_pairs={{0,4},{1,5},{2,6},{3,7},{4,0},{5,1},{6,2},{7,3},{8,12},{9,13},{10,... | collective-permute-start | bytes 442376 | tf_op jit(solution)/shard_map/ppermute | solution.py:30
  77.5 1.6 collective-permute-start.17
  79.6 3.2 %collective-permute-done.15 = bf16[32,2304]{1,0:T(8,128)(2,1)S(1)} collective-permute-done((bf16[32,2304]{1,0:T(8,128)(2,1)S(1)}, bf16[32,2304]{1,0:T(8,128)(2,1)S(1)}, u32[]{:S(2)}, u32[]{:S(2)}) %collective-permute-start.15) | collective-permute-done | bytes 147488 | tf_op jit(solution)/shard_map/ppermute | solution.py:30
  82.7 1.1 fusion.3
  83.8 2.4 %collective-permute-start.21 = (bf16[32,2304]{1,0:T(8,128)(2,1)S(1)}, bf16[32,2304]{1,0:T(8,128)(2,1)S(1)}, u32[]{:S(2)}, u32[]{:S(2)}) collective-permute-start(bf16[32,2304]{1,0:T(8,128)(2,1)S(1)} %get-tuple-element.113.refs_0_), channel_id=1, source_target_pairs={{0,4},{1,5},{2,6},{3,7},{4,0},{5,1},{6,2},{7,3},{8,12},{9,13},{10,... | collective-permute-start | bytes 442376 | tf_op jit(solution)/shard_map/ppermute | solution.py:30
  86.2 1.8 %collective-permute-done.18 = bf16[32,2304]{1,0:T(8,128)(2,1)S(1)} collective-permute-done((bf16[32,2304]{1,0:T(8,128)(2,1)S(1)}, bf16[32,2304]{1,0:T(8,128)(2,1)S(1)}, u32[]{:S(2)}, u32[]{:S(2)}) %collective-permute-start.18) | collective-permute-done | bytes 147488 | tf_op jit(solution)/shard_map/ppermute | solution.py:30
  88.5 1.9 %collective-permute-start.20 = (bf16[32,2304]{1,0:T(8,128)(2,1)S(1)}, bf16[32,2304]{1,0:T(8,128)(2,1)S(1)}, u32[]{:S(2)}, u32[]{:S(2)}) collective-permute-start(bf16[32,2304]{1,0:T(8,128)(2,1)S(1)} %get-tuple-element.113.refs_0_), channel_id=1, source_target_pairs={{0,2},{1,3},{2,0},{3,1},{4,6},{5,7},{6,4},{7,5},{8,10},{9,11},{10,... | collective-permute-start | bytes 442376 | tf_op jit(solution)/shard_map/ppermute | solution.py:30
  90.5 6.5 %collective-permute-done.21.refs_2_ = bf16[32,2304]{1,0:T(8,128)(2,1)S(1)} collective-permute-done((bf16[32,2304]{1,0:T(8,128)(2,1)S(1)}, bf16[32,2304]{1,0:T(8,128)(2,1)S(1)}, u32[]{:S(2)}, u32[]{:S(2)}) %collective-permute-start.21) | collective-permute-done | bytes 147488 | tf_op jit(solution)/shard_map/ppermute | solution.py:30
  96.9 1.8 %collective-permute-done.19 = bf16[32,2304]{1,0:T(8,128)(2,1)S(1)} collective-permute-done((bf16[32,2304]{1,0:T(8,128)(2,1)S(1)}, bf16[32,2304]{1,0:T(8,128)(2,1)S(1)}, u32[]{:S(2)}, u32[]{:S(2)}) %collective-permute-start.19) | collective-permute-done | bytes 147488 | tf_op jit(solution)/shard_map/ppermute | solution.py:30
  99.7 2.9 %collective-permute-done.22.refs_3_ = bf16[32,2304]{1,0:T(8,128)(2,1)S(1)} collective-permute-done((bf16[32,2304]{1,0:T(8,128)(2,1)S(1)}, bf16[32,2304]{1,0:T(8,128)(2,1)S(1)}, u32[]{:S(2)}, u32[]{:S(2)}) %collective-permute-start.22) | collective-permute-done | bytes 147488 | tf_op jit(solution)/shard_map/ppermute | solution.py:30
  103.6 4.4 %collective-permute-start.29 = (bf16[32,2304]{1,0:T(8,128)(2,1)S(1)}, bf16[32,2304]{1,0:T(8,128)(2,1)S(1)}, u32[]{:S(2)}, u32[]{:S(2)}) collective-permute-start(bf16[32,2304]{1,0:T(8,128)(2,1)S(1)} %get-tuple-element.122.refs_0_), channel_id=1, source_target_pairs={{0,6},{1,7},{2,4},{3,5},{4,2},{5,3},{6,0},{7,1},{8,14},{9,15},{10,... | collective-permute-start | bytes 442376 | tf_op jit(solution)/shard_map/ppermute | solution.py:30
  108.7 11.8 %gradient.2 = (bf16[2,64,1024]{2,1,0:T(8,128)(2,1)S(1)}, bf16[2,64,1024]{2,1,0:T(8,128)(2,1)S(1)}, f32[2,64,1024]{2,1,0:T(8,128)S(1)}, f32[2,64,1024]{2,1,0:T(8,...) custom-call(s32[17]{0:T(128)S(1)} %copy-done.4, ...), custom_call_target="tpu_custom_call" | custom-call | flops 1048576 | bytes 1024 | tf_op jit(solution)/shard_map/gradient/pallas_call | solution.py:103
  121.1 1.5 collective-permute-start.36
  125.0 1.5 collective-permute-start.34
  126.5 11.8 %gradient.3 = (bf16[2,64,1024]{2,1,0:T(8,128)(2,1)S(1)}, bf16[2,64,1024]{2,1,0:T(8,128)(2,1)S(1)}, f32[2,64,1024]{2,1,0:T(8,128)S(1)}, f32[2,64,1024]{2,1,0:T(8,...) custom-call(s32[17]{0:T(128)S(1)} %copy-done.4, ...), custom_call_target="tpu_custom_call" | custom-call | flops 1048576 | bytes 1024 | tf_op jit(solution)/shard_map/gradient/pallas_call | solution.py:103
  138.9 1.5 collective-permute-start.42
  140.5 1.5 collective-permute-start.40
  142.0 1.5 collective-permute-start.39
  144.1 2.4 %collective-permute-done.41 = bf16[2,64,1024]{2,1,0:T(8,128)(2,1)S(1)} collective-permute-done((bf16[2,64,1024]{2,1,0:T(8,128)(2,1)S(1)}, bf16[2,64,1024]{2,1,0:T(8,128)(2,1)S(1)}, u32[]{:S(2)}, u32[]{:S(2)}) %collective-permute-start.41) | collective-permute-done | bytes 262176 | tf_op jit(solution)/shard_map/ppermute | solution.py:30
  148.2 1.5 collective-permute-start.38
  150.3 1.5 collective-permute-start.47
  151.9 2.0 %collective-permute-done.43.refs_4_ = bf16[2,64,1024]{2,1,0:T(8,128)(2,1)S(1)} collective-permute-done((bf16[2,64,1024]{2,1,0:T(8,128)(2,1)S(1)}, bf16[2,64,1024]{2,1,0:T(8,128)(2,1)S(1)}, u32[]{:S(2)}, u32[]{:S(2)}) %collective-permute-start.43) | collective-permute-done | bytes 262176 | tf_op jit(solution)/shard_map/ppermute | solution.py:30
  153.9 1.5 collective-permute-start.46
  155.7 1.2 collective-permute-start.48
  157.7 1.3 finish.2.refs_6_
  160.2 1.2 collective-permute-done.45.refs_2_
  161.4 2.4 %collective-permute-done.46.refs_3_ = bf16[2,64,1024]{2,1,0:T(8,128)(2,1)S(1)} collective-permute-done((bf16[2,64,1024]{2,1,0:T(8,128)(2,1)S(1)}, bf16[2,64,1024]{2,1,0:T(8,128)(2,1)S(1)}, u32[]{:S(2)}, u32[]{:S(2)}) %collective-permute-start.46) | collective-permute-done | bytes 262176 | tf_op jit(solution)/shard_map/ppermute | solution.py:30
  163.8 1.1 collective-permute-done.48.refs_5_
  165.0 1.3 finish.3
  (110 shorter events, 17.5 us)
Async XLA Ops:
  6.1 10.6 %collective-permute-start = (bf16[128,1024]{1,0:T(8,128)(2,1)}, bf16[128,1024]{1,0:T(8,128)(2,1)S(1)}, u32[]{:S(2)}, u32[]{:S(2)}) collective-permute-start(bf16[128,1024]{1,0:T(8,128)(2,1)} %get-tuple-element.89.refs_0_), channel_id=1, source_target_pairs={{0,8},{8,0},{16,24},{24,16},{1,9},{9,1},{17,25},{25,17},{2,10},{10... | collective-permute-start | bytes 786440 | tf_op jit(solution)/shard_map/ppermute | solution.py:30
  9.1 9.4 %collective-permute-start.4 = (bf16[128,1024]{1,0:T(8,128)(2,1)}, bf16[128,1024]{1,0:T(8,128)(2,1)S(1)}, u32[]{:S(2)}, u32[]{:S(2)}) collective-permute-start(bf16[128,1024]{1,0:T(8,128)(2,1)} %get-tuple-element.93.refs_1_.refs_4_), channel_id=1, source_target_pairs={{0,16},{8,24},{16,0},{24,8},{1,17},{9,25},{17,1},{25,9},{2,18},{10... | collective-permute-start | bytes 786440 | tf_op jit(solution)/shard_map/ppermute | solution.py:30
  10.6 13.5 %collective-permute-start.1 = (bf16[128,1024]{1,0:T(8,128)(2,1)}, bf16[128,1024]{1,0:T(8,128)(2,1)S(1)}, u32[]{:S(2)}, u32[]{:S(2)}) collective-permute-start(bf16[128,1024]{1,0:T(8,128)(2,1)} %get-tuple-element.89.refs_0_), channel_id=1, source_target_pairs={{0,16},{8,24},{16,0},{24,8},{1,17},{9,25},{17,1},{25,9},{2,18},{10... | collective-permute-start | bytes 786440 | tf_op jit(solution)/shard_map/ppermute | solution.py:30
  11.1 13.1 %collective-permute-start.3 = (bf16[128,1024]{1,0:T(8,128)(2,1)}, bf16[128,1024]{1,0:T(8,128)(2,1)S(1)}, u32[]{:S(2)}, u32[]{:S(2)}) collective-permute-start(bf16[128,1024]{1,0:T(8,128)(2,1)} %get-tuple-element.93.refs_1_.refs_4_), channel_id=1, source_target_pairs={{0,8},{8,0},{16,24},{24,16},{1,9},{9,1},{17,25},{25,17},{2,10},{10... | collective-permute-start | bytes 786440 | tf_op jit(solution)/shard_map/ppermute | solution.py:30
  18.6 11.2 %collective-permute-start.2 = (bf16[128,1024]{1,0:T(8,128)(2,1)S(1)}, bf16[128,1024]{1,0:T(8,128)(2,1)S(1)}, u32[]{:S(2)}, u32[]{:S(2)}) collective-permute-start(bf16[128,1024]{1,0:T(8,128)(2,1)S(1)} %collective-permute-done.refs_1_), channel_id=1, source_target_pairs={{0,16},{8,24},{16,0},{24,8},{1,17},{9,25},{17,1},{25,9},{2,18},{10... | collective-permute-start | bytes 786440 | tf_op jit(solution)/shard_map/ppermute | solution.py:30
  20.1 15.3 %collective-permute-start.10 = (bf16[128,1024]{1,0:T(8,128)(2,1)}, bf16[128,1024]{1,0:T(8,128)(2,1)S(1)}, u32[]{:S(2)}, u32[]{:S(2)}) collective-permute-start(bf16[128,1024]{1,0:T(8,128)(2,1)} %get-tuple-element.101.refs_3_.refs_12_), channel_id=1, source_target_pairs={{0,16},{8,24},{16,0},{24,8},{1,17},{9,25},{17,1},{25,9},{2,18},{10... | collective-permute-start | bytes 786440 | tf_op jit(solution)/shard_map/ppermute | solution.py:30
  20.6 14.8 %collective-permute-start.5 = (bf16[128,1024]{1,0:T(8,128)(2,1)S(1)}, bf16[128,1024]{1,0:T(8,128)(2,1)S(1)}, u32[]{:S(2)}, u32[]{:S(2)}) collective-permute-start(bf16[128,1024]{1,0:T(8,128)(2,1)S(1)} %collective-permute-done.4.refs_6_), channel_id=1, source_target_pairs={{0,8},{8,0},{16,24},{24,16},{1,9},{9,1},{17,25},{25,17},{2,10},{10... | collective-permute-start | bytes 786440 | tf_op jit(solution)/shard_map/ppermute | solution.py:30
  24.2 11.2 %collective-permute-start.6 = (bf16[128,1024]{1,0:T(8,128)(2,1)}, bf16[128,1024]{1,0:T(8,128)(2,1)S(1)}, u32[]{:S(2)}, u32[]{:S(2)}) collective-permute-start(bf16[128,1024]{1,0:T(8,128)(2,1)} %get-tuple-element.97.refs_2_.refs_8_), channel_id=1, source_target_pairs={{0,8},{8,0},{16,24},{24,16},{1,9},{9,1},{17,25},{25,17},{2,10},{10... | collective-permute-start | bytes 786440 | tf_op jit(solution)/shard_map/ppermute | solution.py:30
  24.3 17.7 %collective-permute-start.7 = (bf16[128,1024]{1,0:T(8,128)(2,1)}, bf16[128,1024]{1,0:T(8,128)(2,1)S(1)}, u32[]{:S(2)}, u32[]{:S(2)}) collective-permute-start(bf16[128,1024]{1,0:T(8,128)(2,1)} %get-tuple-element.97.refs_2_.refs_8_), channel_id=1, source_target_pairs={{0,16},{8,24},{16,0},{24,8},{1,17},{9,25},{17,1},{25,9},{2,18},{10... | collective-permute-start | bytes 786440 | tf_op jit(solution)/shard_map/ppermute | solution.py:30
  29.8 12.1 %collective-permute-start.9 = (bf16[128,1024]{1,0:T(8,128)(2,1)}, bf16[128,1024]{1,0:T(8,128)(2,1)S(1)}, u32[]{:S(2)}, u32[]{:S(2)}) collective-permute-start(bf16[128,1024]{1,0:T(8,128)(2,1)} %get-tuple-element.101.refs_3_.refs_12_), channel_id=1, source_target_pairs={{0,8},{8,0},{16,24},{24,16},{1,9},{9,1},{17,25},{25,17},{2,10},{10... | collective-permute-start | bytes 786440 | tf_op jit(solution)/shard_map/ppermute | solution.py:30
  35.4 9.7 %collective-permute-start.8 = (bf16[128,1024]{1,0:T(8,128)(2,1)S(1)}, bf16[128,1024]{1,0:T(8,128)(2,1)S(1)}, u32[]{:S(2)}, u32[]{:S(2)}) collective-permute-start(bf16[128,1024]{1,0:T(8,128)(2,1)S(1)} %collective-permute-done.6.refs_9_), channel_id=1, source_target_pairs={{0,16},{8,24},{16,0},{24,8},{1,17},{9,25},{17,1},{25,9},{2,18},{10... | collective-permute-start | bytes 786440 | tf_op jit(solution)/shard_map/ppermute | solution.py:30
  37.0 8.2 %collective-permute-start.11 = (bf16[128,1024]{1,0:T(8,128)(2,1)S(1)}, bf16[128,1024]{1,0:T(8,128)(2,1)}, u32[]{:S(2)}, u32[]{:S(2)}) collective-permute-start(bf16[128,1024]{1,0:T(8,128)(2,1)S(1)} %collective-permute-done.10.refs_14_), channel_id=1, source_target_pairs={{0,8},{8,0},{16,24},{24,16},{1,9},{9,1},{17,25},{25,17},{2,10},{10... | collective-permute-start | bytes 786440 | tf_op jit(solution)/shard_map/ppermute | solution.py:30
  63.5 2.3 %collective-permute-start.12 = (bf16[128,2304]{1,0:T(8,128)(2,1)}, bf16[128,2304]{1,0:T(8,128)(2,1)S(1)}, u32[]{:S(2)}, u32[]{:S(2)}) collective-permute-start(bf16[128,2304]{1,0:T(8,128)(2,1)} %get-tuple-element.106), channel_id=1, source_target_pairs={{0,1},{1,0},{2,3},{3,2},{4,5},{5,4},{6,7},{7,6},{8,9},{9,8},{10,11... | collective-permute-start | bytes 1769480 | tf_op jit(solution)/shard_map/ppermute | solution.py:30
  66.9 6.8 %collective-permute-start.14 = (bf16[32,2304]{1,0:T(8,128)(2,1)S(1)}, bf16[32,2304]{1,0:T(8,128)(2,1)S(1)}, u32[]{:S(2)}, u32[]{:S(2)}) collective-permute-start(bf16[32,2304]{1,0:T(8,128)(2,1)S(1)} %get-tuple-element.161), channel_id=1, source_target_pairs={{0,2},{1,3},{2,0},{3,1},{4,6},{5,7},{6,4},{7,5},{8,10},{9,11},{10,... | collective-permute-start | bytes 442376 | tf_op jit(solution)/shard_map/ppermute | solution.py:30
  68.6 8.8 %collective-permute-start.16 = (bf16[128,2304]{1,0:T(8,128)(2,1)}, bf16[128,2304]{1,0:T(8,128)(2,1)S(1)}, u32[]{:S(2)}, u32[]{:S(2)}) collective-permute-start(bf16[128,2304]{1,0:T(8,128)(2,1)} %get-tuple-element.108), channel_id=1, source_target_pairs={{0,1},{1,0},{2,3},{3,2},{4,5},{5,4},{6,7},{7,6},{8,9},{9,8},{10,11... | collective-permute-start | bytes 1769480 | tf_op jit(solution)/shard_map/ppermute | solution.py:30
  68.6 11.0 %collective-permute-start.13 = (bf16[32,2304]{1,0:T(8,128)(2,1)S(1)}, bf16[32,2304]{1,0:T(8,128)(2,1)S(1)}, u32[]{:S(2)}, u32[]{:S(2)}) collective-permute-start(bf16[32,2304]{1,0:T(8,128)(2,1)S(1)} %get-tuple-element.160), channel_id=1, source_target_pairs={{0,2},{1,3},{2,0},{3,1},{4,6},{5,7},{6,4},{7,5},{8,10},{9,11},{10,... | collective-permute-start | bytes 442376 | tf_op jit(solution)/shard_map/ppermute | solution.py:30
  74.7 8.0 %collective-permute-start.15 = (bf16[32,2304]{1,0:T(8,128)(2,1)S(1)}, bf16[32,2304]{1,0:T(8,128)(2,1)S(1)}, u32[]{:S(2)}, u32[]{:S(2)}) collective-permute-start(bf16[32,2304]{1,0:T(8,128)(2,1)S(1)} %add_convert_fusion.7), channel_id=1, source_target_pairs={{0,4},{1,5},{2,6},{3,7},{4,0},{5,1},{6,2},{7,3},{8,12},{9,13},{10,... | collective-permute-start | bytes 442376 | tf_op jit(solution)/shard_map/ppermute | solution.py:30
  77.5 19.5 %collective-permute-start.17 = (bf16[32,2304]{1,0:T(8,128)(2,1)S(1)}, bf16[32,2304]{1,0:T(8,128)(2,1)S(1)}, u32[]{:S(2)}, u32[]{:S(2)}) collective-permute-start(bf16[32,2304]{1,0:T(8,128)(2,1)S(1)} %get-tuple-element.109), channel_id=1, source_target_pairs={{0,2},{1,3},{2,0},{3,1},{4,6},{5,7},{6,4},{7,5},{8,10},{9,11},{10,... | collective-permute-start | bytes 442376 | tf_op jit(solution)/shard_map/ppermute | solution.py:30
  79.1 9.0 %collective-permute-start.18 = (bf16[32,2304]{1,0:T(8,128)(2,1)S(1)}, bf16[32,2304]{1,0:T(8,128)(2,1)S(1)}, u32[]{:S(2)}, u32[]{:S(2)}) collective-permute-start(bf16[32,2304]{1,0:T(8,128)(2,1)S(1)} %get-tuple-element.110), channel_id=1, source_target_pairs={{0,2},{1,3},{2,0},{3,1},{4,6},{5,7},{6,4},{7,5},{8,10},{9,11},{10,... | collective-permute-start | bytes 442376 | tf_op jit(solution)/shard_map/ppermute | solution.py:30
  83.8 13.1 %collective-permute-start.21 = (bf16[32,2304]{1,0:T(8,128)(2,1)S(1)}, bf16[32,2304]{1,0:T(8,128)(2,1)S(1)}, u32[]{:S(2)}, u32[]{:S(2)}) collective-permute-start(bf16[32,2304]{1,0:T(8,128)(2,1)S(1)} %get-tuple-element.113.refs_0_), channel_id=1, source_target_pairs={{0,4},{1,5},{2,6},{3,7},{4,0},{5,1},{6,2},{7,3},{8,12},{9,13},{10,... | collective-permute-start | bytes 442376 | tf_op jit(solution)/shard_map/ppermute | solution.py:30
  88.1 10.7 %collective-permute-start.19 = (bf16[32,2304]{1,0:T(8,128)(2,1)S(1)}, bf16[32,2304]{1,0:T(8,128)(2,1)S(1)}, u32[]{:S(2)}, u32[]{:S(2)}) collective-permute-start(bf16[32,2304]{1,0:T(8,128)(2,1)S(1)} %add_convert_fusion.4), channel_id=1, source_target_pairs={{0,4},{1,5},{2,6},{3,7},{4,0},{5,1},{6,2},{7,3},{8,12},{9,13},{10,... | collective-permute-start | bytes 442376 | tf_op jit(solution)/shard_map/ppermute | solution.py:30
  88.5 19.5 %collective-permute-start.23 = (bf16[32,2304]{1,0:T(8,128)(2,1)S(1)}, bf16[32,2304]{1,0:T(8,128)(2,1)S(1)}, u32[]{:S(2)}, u32[]{:S(2)}) collective-permute-start(bf16[32,2304]{1,0:T(8,128)(2,1)S(1)} %get-tuple-element.113.refs_0_), channel_id=1, source_target_pairs={{0,1},{1,0},{2,3},{3,2},{4,5},{5,4},{6,7},{7,6},{8,9},{9,8},{10,11... | collective-permute-start | bytes 442376 | tf_op jit(solution)/shard_map/ppermute | solution.py:30
  88.5 11.2 %collective-permute-start.20 = (bf16[32,2304]{1,0:T(8,128)(2,1)S(1)}, bf16[32,2304]{1,0:T(8,128)(2,1)S(1)}, u32[]{:S(2)}, u32[]{:S(2)}) collective-permute-start(bf16[32,2304]{1,0:T(8,128)(2,1)S(1)} %get-tuple-element.113.refs_0_), channel_id=1, source_target_pairs={{0,2},{1,3},{2,0},{3,1},{4,6},{5,7},{6,4},{7,5},{8,10},{9,11},{10,... | collective-permute-start | bytes 442376 | tf_op jit(solution)/shard_map/ppermute | solution.py:30
  96.9 5.7 %collective-permute-start.22 = (bf16[32,2304]{1,0:T(8,128)(2,1)S(1)}, bf16[32,2304]{1,0:T(8,128)(2,1)S(1)}, u32[]{:S(2)}, u32[]{:S(2)}) collective-permute-start(bf16[32,2304]{1,0:T(8,128)(2,1)S(1)} %collective-permute-done.21.refs_2_), channel_id=1, source_target_pairs={{0,2},{1,3},{2,0},{3,1},{4,6},{5,7},{6,4},{7,5},{8,10},{9,11},{10,... | collective-permute-start | bytes 442376 | tf_op jit(solution)/shard_map/ppermute | solution.py:30
  98.9 9.2 %collective-permute-start.25 = (bf16[32,2304]{1,0:T(8,128)(2,1)S(1)}, bf16[32,2304]{1,0:T(8,128)(2,1)S(1)}, u32[]{:S(2)}, u32[]{:S(2)}) collective-permute-start(bf16[32,2304]{1,0:T(8,128)(2,1)S(1)} %collective-permute-done.21.refs_2_), channel_id=1, source_target_pairs={{0,1},{1,0},{2,3},{3,2},{4,5},{5,4},{6,7},{7,6},{8,9},{9,8},{10,11... | collective-permute-start | bytes 442376 | tf_op jit(solution)/shard_map/ppermute | solution.py:30
  99.7 8.9 %collective-permute-start.24 = (bf16[32,2304]{1,0:T(8,128)(2,1)S(1)}, bf16[32,2304]{1,0:T(8,128)(2,1)S(1)}, u32[]{:S(2)}, u32[]{:S(2)}) collective-permute-start(bf16[32,2304]{1,0:T(8,128)(2,1)S(1)} %collective-permute-done.20.refs_1_), channel_id=1, source_target_pairs={{0,1},{1,0},{2,3},{3,2},{4,5},{5,4},{6,7},{7,6},{8,9},{9,8},{10,11... | collective-permute-start | bytes 442376 | tf_op jit(solution)/shard_map/ppermute | solution.py:30
  102.6 6.0 %collective-permute-start.26 = (bf16[32,2304]{1,0:T(8,128)(2,1)S(1)}, bf16[32,2304]{1,0:T(8,128)(2,1)S(1)}, u32[]{:S(2)}, u32[]{:S(2)}) collective-permute-start(bf16[32,2304]{1,0:T(8,128)(2,1)S(1)} %collective-permute-done.22.refs_3_), channel_id=1, source_target_pairs={{0,1},{1,0},{2,3},{3,2},{4,5},{5,4},{6,7},{7,6},{8,9},{9,8},{10,11... | collective-permute-start | bytes 442376 | tf_op jit(solution)/shard_map/ppermute | solution.py:30
  103.6 16.9 %collective-permute-start.29 = (bf16[32,2304]{1,0:T(8,128)(2,1)S(1)}, bf16[32,2304]{1,0:T(8,128)(2,1)S(1)}, u32[]{:S(2)}, u32[]{:S(2)}) collective-permute-start(bf16[32,2304]{1,0:T(8,128)(2,1)S(1)} %get-tuple-element.122.refs_0_), channel_id=1, source_target_pairs={{0,6},{1,7},{2,4},{3,5},{4,2},{5,3},{6,0},{7,1},{8,14},{9,15},{10,... | collective-permute-start | bytes 442376 | tf_op jit(solution)/shard_map/ppermute | solution.py:30
  108.0 12.5 %collective-permute-start.28 = (bf16[32,2304]{1,0:T(8,128)(2,1)S(1)}, bf16[32,2304]{1,0:T(8,128)(2,1)S(1)}, u32[]{:S(2)}, u32[]{:S(2)}) collective-permute-start(bf16[32,2304]{1,0:T(8,128)(2,1)S(1)} %get-tuple-element.122.refs_0_), channel_id=1, source_target_pairs={{0,4},{1,5},{2,6},{3,7},{4,0},{5,1},{6,2},{7,3},{8,12},{9,13},{10,... | collective-permute-start | bytes 442376 | tf_op jit(solution)/shard_map/ppermute | solution.py:30
  108.0 12.5 %collective-permute-start.27 = (bf16[32,2304]{1,0:T(8,128)(2,1)S(1)}, bf16[32,2304]{1,0:T(8,128)(2,1)S(1)}, u32[]{:S(2)}, u32[]{:S(2)}) collective-permute-start(bf16[32,2304]{1,0:T(8,128)(2,1)S(1)} %get-tuple-element.122.refs_0_), channel_id=1, source_target_pairs={{0,2},{1,3},{2,0},{3,1},{4,6},{5,7},{6,4},{7,5},{8,10},{9,11},{10,... | collective-permute-start | bytes 442376 | tf_op jit(solution)/shard_map/ppermute | solution.py:30
  120.5 3.1 %collective-permute-start.30 = (bf16[32,2304]{1,0:T(8,128)(2,1)S(1)}, bf16[32,2304]{1,0:T(8,128)(2,1)S(1)}, u32[]{:S(2)}, u32[]{:S(2)}) collective-permute-start(bf16[32,2304]{1,0:T(8,128)(2,1)S(1)} %get-tuple-element.122.refs_0_), channel_id=1, source_target_pairs={{0,1},{1,0},{2,3},{3,2},{4,5},{5,4},{6,7},{7,6},{8,9},{9,8},{10,11... | collective-permute-start | bytes 442376 | tf_op jit(solution)/shard_map/ppermute | solution.py:30
  120.6 3.1 %collective-permute-start.31 = (bf16[32,2304]{1,0:T(8,128)(2,1)S(1)}, bf16[32,2304]{1,0:T(8,128)(2,1)S(1)}, u32[]{:S(2)}, u32[]{:S(2)}) collective-permute-start(bf16[32,2304]{1,0:T(8,128)(2,1)S(1)} %collective-permute-done.27.refs_1_), channel_id=1, source_target_pairs={{0,1},{1,0},{2,3},{3,2},{4,5},{5,4},{6,7},{7,6},{8,9},{9,8},{10,11... | collective-permute-start | bytes 442376 | tf_op jit(solution)/shard_map/ppermute | solution.py:30
  121.1 17.8 %collective-permute-start.36 = (bf16[2,64,1024]{2,1,0:T(8,128)(2,1)S(1)}, bf16[2,64,1024]{2,1,0:T(8,128)(2,1)S(1)}, u32[]{:S(2)}, u32[]{:S(2)}) collective-permute-start(bf16[2,64,1024]{2,1,0:T(8,128)(2,1)S(1)} %get-tuple-element.134), channel_id=1, source_target_pairs={{0,16},{8,24},{16,0},{24,8},{1,17},{9,25},{17,1},{25,9},{2,18},{10... | collective-permute-start | bytes 786440 | tf_op jit(solution)/shard_map/ppermute | solution.py:30
  122.6 17.8 %collective-permute-start.37 = (bf16[2,64,1024]{2,1,0:T(8,128)(2,1)S(1)}, bf16[2,64,1024]{2,1,0:T(8,128)(2,1)S(1)}, u32[]{:S(2)}, u32[]{:S(2)}) collective-permute-start(bf16[2,64,1024]{2,1,0:T(8,128)(2,1)S(1)} %get-tuple-element.137), channel_id=1, source_target_pairs={{0,16},{8,24},{16,0},{24,8},{1,17},{9,25},{17,1},{25,9},{2,18},{10... | collective-permute-start | bytes 786440 | tf_op jit(solution)/shard_map/ppermute | solution.py:30
  123.1 17.3 %collective-permute-start.35 = (bf16[2,64,1024]{2,1,0:T(8,128)(2,1)S(1)}, bf16[2,64,1024]{2,1,0:T(8,128)(2,1)S(1)}, u32[]{:S(2)}, u32[]{:S(2)}) collective-permute-start(bf16[2,64,1024]{2,1,0:T(8,128)(2,1)S(1)} %get-tuple-element.131), channel_id=1, source_target_pairs={{0,8},{8,0},{16,24},{24,16},{1,9},{9,1},{17,25},{25,17},{2,10},{10... | collective-permute-start | bytes 786440 | tf_op jit(solution)/shard_map/ppermute | solution.py:30
  123.6 2.9 %collective-permute-start.33 = (bf16[32,2304]{1,0:T(8,128)(2,1)S(1)}, bf16[32,2304]{1,0:T(8,128)(2,1)S(1)}, u32[]{:S(2)}, u32[]{:S(2)}) collective-permute-start(bf16[32,2304]{1,0:T(8,128)(2,1)S(1)} %collective-permute-done.29.refs_3_), channel_id=1, source_target_pairs={{0,1},{1,0},{2,3},{3,2},{4,5},{5,4},{6,7},{7,6},{8,9},{9,8},{10,11... | collective-permute-start | bytes 442376 | tf_op jit(solution)/shard_map/ppermute | solution.py:30
  125.0 15.5 %collective-permute-start.34 = (bf16[2,64,1024]{2,1,0:T(8,128)(2,1)S(1)}, bf16[2,64,1024]{2,1,0:T(8,128)(2,1)S(1)}, u32[]{:S(2)}, u32[]{:S(2)}) collective-permute-start(bf16[2,64,1024]{2,1,0:T(8,128)(2,1)S(1)} %get-tuple-element.130), channel_id=1, source_target_pairs={{0,8},{8,0},{16,24},{24,16},{1,9},{9,1},{17,25},{25,17},{2,10},{10... | collective-permute-start | bytes 786440 | tf_op jit(solution)/shard_map/ppermute | solution.py:30
  138.3 8.2 %collective-permute-start.41 = (bf16[2,64,1024]{2,1,0:T(8,128)(2,1)S(1)}, bf16[2,64,1024]{2,1,0:T(8,128)(2,1)S(1)}, u32[]{:S(2)}, u32[]{:S(2)}) collective-permute-start(bf16[2,64,1024]{2,1,0:T(8,128)(2,1)S(1)} %get-tuple-element.141), channel_id=1, source_target_pairs={{0,8},{8,0},{16,24},{24,16},{1,9},{9,1},{17,25},{25,17},{2,10},{10... | collective-permute-start | bytes 786440 | tf_op jit(solution)/shard_map/ppermute | solution.py:30
  138.9 9.3 %collective-permute-start.42 = (bf16[2,64,1024]{2,1,0:T(8,128)(2,1)S(1)}, bf16[2,64,1024]{2,1,0:T(8,128)(2,1)S(1)}, u32[]{:S(2)}, u32[]{:S(2)}) collective-permute-start(bf16[2,64,1024]{2,1,0:T(8,128)(2,1)S(1)} %get-tuple-element.143), channel_id=1, source_target_pairs={{0,16},{8,24},{16,0},{24,8},{1,17},{9,25},{17,1},{25,9},{2,18},{10... | collective-permute-start | bytes 786440 | tf_op jit(solution)/shard_map/ppermute | solution.py:30
  140.5 9.2 %collective-permute-start.40 = (f32[8,128]{1,0:T(8,128)S(1)}, f32[8,128]{1,0:T(8,128)S(1)}, u32[]{:S(2)}, u32[]{:S(2)}) collective-permute-start(f32[8,128]{1,0:T(8,128)S(1)} %add.152), channel_id=1, source_target_pairs={{0,24},{8,16},{16,8},{24,0},{1,25},{9,17},{17,9},{25,1},{2,26},{10... | collective-permute-start | bytes 12296 | tf_op jit(solution)/shard_map/ppermute | solution.py:30
  142.0 8.3 %collective-permute-start.39 = (f32[8,128]{1,0:T(8,128)S(1)}, f32[8,128]{1,0:T(8,128)S(1)}, u32[]{:S(2)}, u32[]{:S(2)}) collective-permute-start(f32[8,128]{1,0:T(8,128)S(1)} %add.152), channel_id=1, source_target_pairs={{0,16},{8,24},{16,0},{24,8},{1,17},{9,25},{17,1},{25,9},{2,18},{10... | collective-permute-start | bytes 12296 | tf_op jit(solution)/shard_map/ppermute | solution.py:30
  143.6 10.3 %collective-permute-start.43 = (bf16[2,64,1024]{2,1,0:T(8,128)(2,1)S(1)}, bf16[2,64,1024]{2,1,0:T(8,128)(2,1)S(1)}, u32[]{:S(2)}, u32[]{:S(2)}) collective-permute-start(bf16[2,64,1024]{2,1,0:T(8,128)(2,1)S(1)} %add_convert_fusion.3), channel_id=1, source_target_pairs={{0,16},{8,24},{16,0},{24,8},{1,17},{9,25},{17,1},{25,9},{2,18},{10... | collective-permute-start | bytes 786440 | tf_op jit(solution)/shard_map/ppermute | solution.py:30
  146.5 9.2 %collective-permute-start.44 = (bf16[2,64,1024]{2,1,0:T(8,128)(2,1)S(1)}, bf16[2,64,1024]{2,1,0:T(8,128)(2,1)S(1)}, u32[]{:S(2)}, u32[]{:S(2)}) collective-permute-start(bf16[2,64,1024]{2,1,0:T(8,128)(2,1)S(1)} %add_convert_fusion.2), channel_id=1, source_target_pairs={{0,8},{8,0},{16,24},{24,16},{1,9},{9,1},{17,25},{25,17},{2,10},{10... | collective-permute-start | bytes 786440 | tf_op jit(solution)/shard_map/ppermute | solution.py:30
  148.2 10.8 %collective-permute-start.38 = (f32[8,128]{1,0:T(8,128)S(1)}, f32[8,128]{1,0:T(8,128)S(1)}, u32[]{:S(2)}, u32[]{:S(2)}) collective-permute-start(f32[8,128]{1,0:T(8,128)S(1)} %add.152), channel_id=1, source_target_pairs={{0,8},{8,0},{16,24},{24,16},{1,9},{9,1},{17,25},{25,17},{2,10},{10... | collective-permute-start | bytes 12296 | tf_op jit(solution)/shard_map/ppermute | solution.py:30
  149.8 11.6 %collective-permute-start.45 = (bf16[2,64,1024]{2,1,0:T(8,128)(2,1)S(1)}, bf16[2,64,1024]{2,1,0:T(8,128)(2,1)S(1)}, u32[]{:S(2)}, u32[]{:S(2)}) collective-permute-start(bf16[2,64,1024]{2,1,0:T(8,128)(2,1)S(1)} %get-tuple-element.155), channel_id=1, source_target_pairs={{0,8},{8,0},{16,24},{24,16},{1,9},{9,1},{17,25},{25,17},{2,10},{10... | collective-permute-start | bytes 786440 | tf_op jit(solution)/shard_map/ppermute | solution.py:30
  150.3 11.1 %collective-permute-start.47 = (bf16[2,64,1024]{2,1,0:T(8,128)(2,1)S(1)}, bf16[2,64,1024]{2,1,0:T(8,128)(2,1)S(1)}, u32[]{:S(2)}, u32[]{:S(2)}) collective-permute-start(bf16[2,64,1024]{2,1,0:T(8,128)(2,1)S(1)} %add_convert_fusion.1), channel_id=1, source_target_pairs={{0,16},{8,24},{16,0},{24,8},{1,17},{9,25},{17,1},{25,9},{2,18},{10... | collective-permute-start | bytes 786440 | tf_op jit(solution)/shard_map/ppermute | solution.py:30
  153.9 9.9 %collective-permute-start.46 = (bf16[2,64,1024]{2,1,0:T(8,128)(2,1)S(1)}, bf16[2,64,1024]{2,1,0:T(8,128)(2,1)S(1)}, u32[]{:S(2)}, u32[]{:S(2)}) collective-permute-start(bf16[2,64,1024]{2,1,0:T(8,128)(2,1)S(1)} %get-tuple-element.157), channel_id=1, source_target_pairs={{0,16},{8,24},{16,0},{24,8},{1,17},{9,25},{17,1},{25,9},{2,18},{10... | collective-permute-start | bytes 786440 | tf_op jit(solution)/shard_map/ppermute | solution.py:30
  155.7 9.2 %collective-permute-start.48 = (bf16[2,64,1024]{2,1,0:T(8,128)(2,1)S(1)}, bf16[2,64,1024]{2,1,0:T(8,128)(2,1)S(1)}, u32[]{:S(2)}, u32[]{:S(2)}) collective-permute-start(bf16[2,64,1024]{2,1,0:T(8,128)(2,1)S(1)} %add_convert_fusion), channel_id=1, source_target_pairs={{0,8},{8,0},{16,24},{24,16},{1,9},{9,1},{17,25},{25,17},{2,10},{10... | collective-permute-start | bytes 786440 | tf_op jit(solution)/shard_map/ppermute | solution.py:30
  (19 other events, 284.5 us)

commit v14 on v13

--- a/solution.py
+++ b/solution.py
@@ -15,6 +15,7 @@
 IN_FLIGHT = 3
 VMEM_BYTES = 44 << 20
 MOST_VMEM_BYTES = 59 << 20
+DECODE_VMEM_BYTES = 56 << 20
 SMALL_COST = pl.CostEstimate(flops=1 << 20, bytes_accessed=1 << 10, transcendentals=0)
 FAR = pl.BlockSpec(memory_space=pltpu.HBM)
 ANYWHERE = pl.BlockSpec(memory_space=pl.ANY)
@@ -274,7 +275,7 @@
             pltpu.SemaphoreType.DMA((WEIGHT_SLOTS, plan.sources)),
         ],
         (index, *pieces, w_dec),
-        vmem=MOST_VMEM_BYTES,
+        vmem=DECODE_VMEM_BYTES,
     )
     return outs[:plan.chunks], outs[plan.chunks:]
 

time: 168 us -> 168 us (level)
  no operation moved by 1% of the time
where the time goes in v14:
time: 168 us; the launch traced here: 167 us
  Pallas kernels  56.4 us (34%)
  waiting for transfers between devices  52.8 us (31%)
  starting transfers between devices  46.2 us (28%)
  other arithmetic  5.9 us (4%)
  local copies, waits for them, and re-layouts  3.24 us (2%)
  between operations  2.79 us (2%)
    pallas_call x8, Pallas kernels, call(): pl.pallas_call(kernel, in_specs=in_specs, out_shape=out_shape, scratch_sh...  56.4 us
    ppermute x49, waiting for transfers between devices, swap(): return lax.ppermute(x, axis, [(i, i ^ offset) for i in range(size)])  52.8 us
    ppermute x49, starting transfers between devices, swap(): return lax.ppermute(x, axis, [(i, i ^ offset) for i in range(size)])  46.2 us
  transfers between devices with their start and end apart: 49, of which 21 were waited for; matrix products, arithmetic and copies ran while one was open for 3% of the time, Pallas kernels for 19%

profile of v14, /device:TPU:0, one launch (start us, length us, event | category | flops | bytes accessed | tf_op | source)
XLA Modules:
  0.0 167.4 jit_solution(17100699365609441881)
XLA Ops:
  0.6 5.5 %encode.2 = (bf16[128,1024]{1,0:T(8,128)(2,1)}, bf16[128,1024]{1,0:T(8,128)(2,1)}) custom-call(bf16[4,128,2304]{2,1,0:T(8,128)(2,1)} %resid_ref.3, bf16[4,2304,1024]{2,1,0:T(8,128)(2,1)} %w_ref.3, f32[4,1024]{1,0:T(4,128)} %b_ref.3), custom_call_target="tpu_custom_call" | custom-call | flops 1048576 | bytes 1024 | tf_op jit(solution)/shard_map/encode/pallas_call | solution.py:104
  6.1 3.0 %collective-permute-start = (bf16[128,1024]{1,0:T(8,128)(2,1)}, bf16[128,1024]{1,0:T(8,128)(2,1)S(1)}, u32[]{:S(2)}, u32[]{:S(2)}) collective-permute-start(bf16[128,1024]{1,0:T(8,128)(2,1)} %get-tuple-element.89.refs_0_), channel_id=1, source_target_pairs={{0,8},{8,0},{16,24},{24,16},{1,9},{9,1},{17,25},{25,17},{2,10},{10... | collective-permute-start | bytes 786440 | tf_op jit(solution)/shard_map/ppermute | solution.py:31
  9.1 1.5 collective-permute-start.4
  11.3 5.5 %encode.3 = (bf16[128,1024]{1,0:T(8,128)(2,1)}, bf16[128,1024]{1,0:T(8,128)(2,1)}) custom-call(bf16[4,128,2304]{2,1,0:T(8,128)(2,1)} %resid_ref.3, bf16[4,2304,1024]{2,1,0:T(8,128)(2,1)} %w_ref.3, f32[4,1024]{1,0:T(4,128)} %b_ref.3), custom_call_target="tpu_custom_call" | custom-call | flops 1048576 | bytes 1024 | tf_op jit(solution)/shard_map/encode/pallas_call | solution.py:104
  16.7 1.8 %collective-permute-done.4.refs_6_ = bf16[128,1024]{1,0:T(8,128)(2,1)S(1)} collective-permute-done((bf16[128,1024]{1,0:T(8,128)(2,1)}, bf16[128,1024]{1,0:T(8,128)(2,1)S(1)}, u32[]{:S(2)}, u32[]{:S(2)}) %collective-permute-start.4) | collective-permute-done | bytes 262176 | tf_op jit(solution)/shard_map/ppermute | solution.py:31
  18.6 1.5 collective-permute-start.2
  20.8 3.4 %collective-permute-done.1.refs_2_ = bf16[128,1024]{1,0:T(8,128)(2,1)S(1)} collective-permute-done((bf16[128,1024]{1,0:T(8,128)(2,1)}, bf16[128,1024]{1,0:T(8,128)(2,1)S(1)}, u32[]{:S(2)}, u32[]{:S(2)}) %collective-permute-start.1) | collective-permute-done | bytes 262176 | tf_op jit(solution)/shard_map/ppermute | solution.py:31
  24.3 2.0 %collective-permute-start.7 = (bf16[128,1024]{1,0:T(8,128)(2,1)}, bf16[128,1024]{1,0:T(8,128)(2,1)S(1)}, u32[]{:S(2)}, u32[]{:S(2)}) collective-permute-start(bf16[128,1024]{1,0:T(8,128)(2,1)} %get-tuple-element.97.refs_2_.refs_8_), channel_id=1, source_target_pairs={{0,16},{8,24},{16,0},{24,8},{1,17},{9,25},{17,1},{25,9},{2,18},{10... | collective-permute-start | bytes 786440 | tf_op jit(solution)/shard_map/ppermute | solution.py:31
  26.3 3.5 %collective-permute-done.2.refs_3_ = bf16[128,1024]{1,0:T(8,128)(2,1)S(1)} collective-permute-done((bf16[128,1024]{1,0:T(8,128)(2,1)S(1)}, bf16[128,1024]{1,0:T(8,128)(2,1)S(1)}, u32[]{:S(2)}, u32[]{:S(2)}) %collective-permute-start.2) | collective-permute-done | bytes 262176 | tf_op jit(solution)/shard_map/ppermute | solution.py:31
  29.9 5.5 %collective-permute-done.10.refs_14_ = bf16[128,1024]{1,0:T(8,128)(2,1)S(1)} collective-permute-done((bf16[128,1024]{1,0:T(8,128)(2,1)}, bf16[128,1024]{1,0:T(8,128)(2,1)S(1)}, u32[]{:S(2)}, u32[]{:S(2)}) %collective-permute-start.10) | collective-permute-done | bytes 262176 | tf_op jit(solution)/shard_map/ppermute | solution.py:31
  35.4 1.6 collective-permute-start.8
  40.2 1.7 %arrange.1 = bf16[128,4,1024]{2,1,0:T(4,128)(2,1)} custom-call(bf16[128,1024]{1,0:T(8,128)(2,1)S(1)} %copy-done, bf16[128,1024]{1,0:T(8,128)(2,1)S(1)} %copy-done.1, bf16[128,1024]{1,0:T(8,128)(2,1)S(1)} %copy-done.2, bf16[128,1024]{1,0:T(8,128)(2,1)S(1)} %copy-done.3), custom_call_target="tpu_custom_call" | custom-call | flops 1048576 | bytes 1024 | tf_op jit(solution)/shard_map/arrange/pallas_call | solution.py:104
  41.9 3.3 %collective-permute-done.8.refs_11_ = bf16[128,1024]{1,0:T(8,128)(2,1)S(1)} collective-permute-done((bf16[128,1024]{1,0:T(8,128)(2,1)S(1)}, bf16[128,1024]{1,0:T(8,128)(2,1)S(1)}, u32[]{:S(2)}, u32[]{:S(2)}) %collective-permute-start.8) | collective-permute-done | bytes 262176 | tf_op jit(solution)/shard_map/ppermute | solution.py:31
  45.9 17.6 %decode.1 = (bf16[128,2304]{1,0:T(8,128)(2,1)}, bf16[128,2304]{1,0:T(8,128)(2,1)}, f32[128,2304]{1,0:T(8,128)}, f32[128,2304]{1,0:T(8,128)}) custom-call(s32[17]{0:T(128)} %concatenate.6.index_ref, bf16[128,1024]{1,0:T(8,128)(2,1)} %get-tuple-element.89.refs_0_, bf16[128,1024]{1,0:T(8,128)(2,1)} %copy-done.6, bf16[128,1024]{1,0:T(8,128)(2,1)} %copy-done.8, ...), custom_call_target="tpu_custom_call" | custom-call | flops 1048576 | bytes 1024 | tf_op jit(solution)/shard_map/decode/pallas_call | solution.py:104
  63.6 2.2 %collective-permute-done.12 = bf16[128,2304]{1,0:T(8,128)(2,1)S(1)} collective-permute-done((bf16[128,2304]{1,0:T(8,128)(2,1)}, bf16[128,2304]{1,0:T(8,128)(2,1)S(1)}, u32[]{:S(2)}, u32[]{:S(2)}) %collective-permute-start.12) | collective-permute-done | bytes 589856 | tf_op jit(solution)/shard_map/ppermute | solution.py:31
  65.8 1.1 add_convert_fusion.9
  66.9 1.7 collective-permute-start.14
  69.0 4.7 %collective-permute-done.14 = bf16[32,2304]{1,0:T(8,128)(2,1)S(1)} collective-permute-done((bf16[32,2304]{1,0:T(8,128)(2,1)S(1)}, bf16[32,2304]{1,0:T(8,128)(2,1)S(1)}, u32[]{:S(2)}, u32[]{:S(2)}) %collective-permute-start.14) | collective-permute-done | bytes 147488 | tf_op jit(solution)/shard_map/ppermute | solution.py:31
  73.7 1.0 add_convert_fusion.7
  74.7 2.7 %collective-permute-start.15 = (bf16[32,2304]{1,0:T(8,128)(2,1)S(1)}, bf16[32,2304]{1,0:T(8,128)(2,1)S(1)}, u32[]{:S(2)}, u32[]{:S(2)}) collective-permute-start(bf16[32,2304]{1,0:T(8,128)(2,1)S(1)} %add_convert_fusion.7), channel_id=1, source_target_pairs={{0,4},{1,5},{2,6},{3,7},{4,0},{5,1},{6,2},{7,3},{8,12},{9,13},{10,... | collective-permute-start | bytes 442376 | tf_op jit(solution)/shard_map/ppermute | solution.py:31
  77.5 1.6 collective-permute-start.17
  79.6 3.1 %collective-permute-done.15 = bf16[32,2304]{1,0:T(8,128)(2,1)S(1)} collective-permute-done((bf16[32,2304]{1,0:T(8,128)(2,1)S(1)}, bf16[32,2304]{1,0:T(8,128)(2,1)S(1)}, u32[]{:S(2)}, u32[]{:S(2)}) %collective-permute-start.15) | collective-permute-done | bytes 147488 | tf_op jit(solution)/shard_map/ppermute | solution.py:31
  82.7 1.1 fusion.3
  83.8 2.5 %collective-permute-start.21 = (bf16[32,2304]{1,0:T(8,128)(2,1)S(1)}, bf16[32,2304]{1,0:T(8,128)(2,1)S(1)}, u32[]{:S(2)}, u32[]{:S(2)}) collective-permute-start(bf16[32,2304]{1,0:T(8,128)(2,1)S(1)} %get-tuple-element.113.refs_0_), channel_id=1, source_target_pairs={{0,4},{1,5},{2,6},{3,7},{4,0},{5,1},{6,2},{7,3},{8,12},{9,13},{10,... | collective-permute-start | bytes 442376 | tf_op jit(solution)/shard_map/ppermute | solution.py:31
  86.2 1.8 %collective-permute-done.18 = bf16[32,2304]{1,0:T(8,128)(2,1)S(1)} collective-permute-done((bf16[32,2304]{1,0:T(8,128)(2,1)S(1)}, bf16[32,2304]{1,0:T(8,128)(2,1)S(1)}, u32[]{:S(2)}, u32[]{:S(2)}) %collective-permute-start.18) | collective-permute-done | bytes 147488 | tf_op jit(solution)/shard_map/ppermute | solution.py:31
  88.5 1.9 %collective-permute-start.20 = (bf16[32,2304]{1,0:T(8,128)(2,1)S(1)}, bf16[32,2304]{1,0:T(8,128)(2,1)S(1)}, u32[]{:S(2)}, u32[]{:S(2)}) collective-permute-start(bf16[32,2304]{1,0:T(8,128)(2,1)S(1)} %get-tuple-element.113.refs_0_), channel_id=1, source_target_pairs={{0,2},{1,3},{2,0},{3,1},{4,6},{5,7},{6,4},{7,5},{8,10},{9,11},{10,... | collective-permute-start | bytes 442376 | tf_op jit(solution)/shard_map/ppermute | solution.py:31
  90.5 6.4 %collective-permute-done.21.refs_2_ = bf16[32,2304]{1,0:T(8,128)(2,1)S(1)} collective-permute-done((bf16[32,2304]{1,0:T(8,128)(2,1)S(1)}, bf16[32,2304]{1,0:T(8,128)(2,1)S(1)}, u32[]{:S(2)}, u32[]{:S(2)}) %collective-permute-start.21) | collective-permute-done | bytes 147488 | tf_op jit(solution)/shard_map/ppermute | solution.py:31
  96.9 1.9 %collective-permute-done.19 = bf16[32,2304]{1,0:T(8,128)(2,1)S(1)} collective-permute-done((bf16[32,2304]{1,0:T(8,128)(2,1)S(1)}, bf16[32,2304]{1,0:T(8,128)(2,1)S(1)}, u32[]{:S(2)}, u32[]{:S(2)}) %collective-permute-start.19) | collective-permute-done | bytes 147488 | tf_op jit(solution)/shard_map/ppermute | solution.py:31
  99.8 2.8 %collective-permute-done.22.refs_3_ = bf16[32,2304]{1,0:T(8,128)(2,1)S(1)} collective-permute-done((bf16[32,2304]{1,0:T(8,128)(2,1)S(1)}, bf16[32,2304]{1,0:T(8,128)(2,1)S(1)}, u32[]{:S(2)}, u32[]{:S(2)}) %collective-permute-start.22) | collective-permute-done | bytes 147488 | tf_op jit(solution)/shard_map/ppermute | solution.py:31
  103.6 4.4 %collective-permute-start.29 = (bf16[32,2304]{1,0:T(8,128)(2,1)S(1)}, bf16[32,2304]{1,0:T(8,128)(2,1)S(1)}, u32[]{:S(2)}, u32[]{:S(2)}) collective-permute-start(bf16[32,2304]{1,0:T(8,128)(2,1)S(1)} %get-tuple-element.122.refs_0_), channel_id=1, source_target_pairs={{0,6},{1,7},{2,4},{3,5},{4,2},{5,3},{6,0},{7,1},{8,14},{9,15},{10,... | collective-permute-start | bytes 442376 | tf_op jit(solution)/shard_map/ppermute | solution.py:31
  108.7 11.8 %gradient.2 = (bf16[2,64,1024]{2,1,0:T(8,128)(2,1)S(1)}, bf16[2,64,1024]{2,1,0:T(8,128)(2,1)S(1)}, f32[2,64,1024]{2,1,0:T(8,128)S(1)}, f32[2,64,1024]{2,1,0:T(8,...) custom-call(s32[17]{0:T(128)S(1)} %copy-done.4, ...), custom_call_target="tpu_custom_call" | custom-call | flops 1048576 | bytes 1024 | tf_op jit(solution)/shard_map/gradient/pallas_call | solution.py:104
  121.1 1.5 collective-permute-start.36
  125.0 1.5 collective-permute-start.34
  126.5 11.8 %gradient.3 = (bf16[2,64,1024]{2,1,0:T(8,128)(2,1)S(1)}, bf16[2,64,1024]{2,1,0:T(8,128)(2,1)S(1)}, f32[2,64,1024]{2,1,0:T(8,128)S(1)}, f32[2,64,1024]{2,1,0:T(8,...) custom-call(s32[17]{0:T(128)S(1)} %copy-done.4, ...), custom_call_target="tpu_custom_call" | custom-call | flops 1048576 | bytes 1024 | tf_op jit(solution)/shard_map/gradient/pallas_call | solution.py:104
  138.9 1.5 collective-permute-start.42
  140.5 1.6 collective-permute-start.40
  142.1 1.5 collective-permute-start.39
  144.1 2.4 %collective-permute-done.41 = bf16[2,64,1024]{2,1,0:T(8,128)(2,1)S(1)} collective-permute-done((bf16[2,64,1024]{2,1,0:T(8,128)(2,1)S(1)}, bf16[2,64,1024]{2,1,0:T(8,128)(2,1)S(1)}, u32[]{:S(2)}, u32[]{:S(2)}) %collective-permute-start.41) | collective-permute-done | bytes 262176 | tf_op jit(solution)/shard_map/ppermute | solution.py:31
  148.2 1.6 collective-permute-start.38
  150.3 1.5 collective-permute-start.47
  151.9 2.0 %collective-permute-done.43.refs_4_ = bf16[2,64,1024]{2,1,0:T(8,128)(2,1)S(1)} collective-permute-done((bf16[2,64,1024]{2,1,0:T(8,128)(2,1)S(1)}, bf16[2,64,1024]{2,1,0:T(8,128)(2,1)S(1)}, u32[]{:S(2)}, u32[]{:S(2)}) %collective-permute-start.43) | collective-permute-done | bytes 262176 | tf_op jit(solution)/shard_map/ppermute | solution.py:31
  153.9 1.5 collective-permute-start.46
  155.8 1.2 collective-permute-start.48
  157.7 1.3 finish.2.refs_6_
  160.2 1.2 collective-permute-done.45.refs_2_
  161.5 2.4 %collective-permute-done.46.refs_3_ = bf16[2,64,1024]{2,1,0:T(8,128)(2,1)S(1)} collective-permute-done((bf16[2,64,1024]{2,1,0:T(8,128)(2,1)S(1)}, bf16[2,64,1024]{2,1,0:T(8,128)(2,1)S(1)}, u32[]{:S(2)}, u32[]{:S(2)}) %collective-permute-start.46) | collective-permute-done | bytes 262176 | tf_op jit(solution)/shard_map/ppermute | solution.py:31
  163.9 1.1 collective-permute-done.48.refs_5_
  165.0 1.3 finish.3
  (110 shorter events, 17.5 us)
Async XLA Ops:
  6.1 10.6 %collective-permute-start = (bf16[128,1024]{1,0:T(8,128)(2,1)}, bf16[128,1024]{1,0:T(8,128)(2,1)S(1)}, u32[]{:S(2)}, u32[]{:S(2)}) collective-permute-start(bf16[128,1024]{1,0:T(8,128)(2,1)} %get-tuple-element.89.refs_0_), channel_id=1, source_target_pairs={{0,8},{8,0},{16,24},{24,16},{1,9},{9,1},{17,25},{25,17},{2,10},{10... | collective-permute-start | bytes 786440 | tf_op jit(solution)/shard_map/ppermute | solution.py:31
  9.1 9.4 %collective-permute-start.4 = (bf16[128,1024]{1,0:T(8,128)(2,1)}, bf16[128,1024]{1,0:T(8,128)(2,1)S(1)}, u32[]{:S(2)}, u32[]{:S(2)}) collective-permute-start(bf16[128,1024]{1,0:T(8,128)(2,1)} %get-tuple-element.93.refs_1_.refs_4_), channel_id=1, source_target_pairs={{0,16},{8,24},{16,0},{24,8},{1,17},{9,25},{17,1},{25,9},{2,18},{10... | collective-permute-start | bytes 786440 | tf_op jit(solution)/shard_map/ppermute | solution.py:31
  10.6 13.5 %collective-permute-start.1 = (bf16[128,1024]{1,0:T(8,128)(2,1)}, bf16[128,1024]{1,0:T(8,128)(2,1)S(1)}, u32[]{:S(2)}, u32[]{:S(2)}) collective-permute-start(bf16[128,1024]{1,0:T(8,128)(2,1)} %get-tuple-element.89.refs_0_), channel_id=1, source_target_pairs={{0,16},{8,24},{16,0},{24,8},{1,17},{9,25},{17,1},{25,9},{2,18},{10... | collective-permute-start | bytes 786440 | tf_op jit(solution)/shard_map/ppermute | solution.py:31
  11.1 13.1 %collective-permute-start.3 = (bf16[128,1024]{1,0:T(8,128)(2,1)}, bf16[128,1024]{1,0:T(8,128)(2,1)S(1)}, u32[]{:S(2)}, u32[]{:S(2)}) collective-permute-start(bf16[128,1024]{1,0:T(8,128)(2,1)} %get-tuple-element.93.refs_1_.refs_4_), channel_id=1, source_target_pairs={{0,8},{8,0},{16,24},{24,16},{1,9},{9,1},{17,25},{25,17},{2,10},{10... | collective-permute-start | bytes 786440 | tf_op jit(solution)/shard_map/ppermute | solution.py:31
  18.6 11.2 %collective-permute-start.2 = (bf16[128,1024]{1,0:T(8,128)(2,1)S(1)}, bf16[128,1024]{1,0:T(8,128)(2,1)S(1)}, u32[]{:S(2)}, u32[]{:S(2)}) collective-permute-start(bf16[128,1024]{1,0:T(8,128)(2,1)S(1)} %collective-permute-done.refs_1_), channel_id=1, source_target_pairs={{0,16},{8,24},{16,0},{24,8},{1,17},{9,25},{17,1},{25,9},{2,18},{10... | collective-permute-start | bytes 786440 | tf_op jit(solution)/shard_map/ppermute | solution.py:31
  20.1 15.3 %collective-permute-start.10 = (bf16[128,1024]{1,0:T(8,128)(2,1)}, bf16[128,1024]{1,0:T(8,128)(2,1)S(1)}, u32[]{:S(2)}, u32[]{:S(2)}) collective-permute-start(bf16[128,1024]{1,0:T(8,128)(2,1)} %get-tuple-element.101.refs_3_.refs_12_), channel_id=1, source_target_pairs={{0,16},{8,24},{16,0},{24,8},{1,17},{9,25},{17,1},{25,9},{2,18},{10... | collective-permute-start | bytes 786440 | tf_op jit(solution)/shard_map/ppermute | solution.py:31
  20.6 14.8 %collective-permute-start.5 = (bf16[128,1024]{1,0:T(8,128)(2,1)S(1)}, bf16[128,1024]{1,0:T(8,128)(2,1)S(1)}, u32[]{:S(2)}, u32[]{:S(2)}) collective-permute-start(bf16[128,1024]{1,0:T(8,128)(2,1)S(1)} %collective-permute-done.4.refs_6_), channel_id=1, source_target_pairs={{0,8},{8,0},{16,24},{24,16},{1,9},{9,1},{17,25},{25,17},{2,10},{10... | collective-permute-start | bytes 786440 | tf_op jit(solution)/shard_map/ppermute | solution.py:31
  24.2 11.2 %collective-permute-start.6 = (bf16[128,1024]{1,0:T(8,128)(2,1)}, bf16[128,1024]{1,0:T(8,128)(2,1)S(1)}, u32[]{:S(2)}, u32[]{:S(2)}) collective-permute-start(bf16[128,1024]{1,0:T(8,128)(2,1)} %get-tuple-element.97.refs_2_.refs_8_), channel_id=1, source_target_pairs={{0,8},{8,0},{16,24},{24,16},{1,9},{9,1},{17,25},{25,17},{2,10},{10... | collective-permute-start | bytes 786440 | tf_op jit(solution)/shard_map/ppermute | solution.py:31
  24.3 17.7 %collective-permute-start.7 = (bf16[128,1024]{1,0:T(8,128)(2,1)}, bf16[128,1024]{1,0:T(8,128)(2,1)S(1)}, u32[]{:S(2)}, u32[]{:S(2)}) collective-permute-start(bf16[128,1024]{1,0:T(8,128)(2,1)} %get-tuple-element.97.refs_2_.refs_8_), channel_id=1, source_target_pairs={{0,16},{8,24},{16,0},{24,8},{1,17},{9,25},{17,1},{25,9},{2,18},{10... | collective-permute-start | bytes 786440 | tf_op jit(solution)/shard_map/ppermute | solution.py:31
  29.8 12.1 %collective-permute-start.9 = (bf16[128,1024]{1,0:T(8,128)(2,1)}, bf16[128,1024]{1,0:T(8,128)(2,1)S(1)}, u32[]{:S(2)}, u32[]{:S(2)}) collective-permute-start(bf16[128,1024]{1,0:T(8,128)(2,1)} %get-tuple-element.101.refs_3_.refs_12_), channel_id=1, source_target_pairs={{0,8},{8,0},{16,24},{24,16},{1,9},{9,1},{17,25},{25,17},{2,10},{10... | collective-permute-start | bytes 786440 | tf_op jit(solution)/shard_map/ppermute | solution.py:31
  35.4 9.7 %collective-permute-start.8 = (bf16[128,1024]{1,0:T(8,128)(2,1)S(1)}, bf16[128,1024]{1,0:T(8,128)(2,1)S(1)}, u32[]{:S(2)}, u32[]{:S(2)}) collective-permute-start(bf16[128,1024]{1,0:T(8,128)(2,1)S(1)} %collective-permute-done.6.refs_9_), channel_id=1, source_target_pairs={{0,16},{8,24},{16,0},{24,8},{1,17},{9,25},{17,1},{25,9},{2,18},{10... | collective-permute-start | bytes 786440 | tf_op jit(solution)/shard_map/ppermute | solution.py:31
  37.0 8.2 %collective-permute-start.11 = (bf16[128,1024]{1,0:T(8,128)(2,1)S(1)}, bf16[128,1024]{1,0:T(8,128)(2,1)}, u32[]{:S(2)}, u32[]{:S(2)}) collective-permute-start(bf16[128,1024]{1,0:T(8,128)(2,1)S(1)} %collective-permute-done.10.refs_14_), channel_id=1, source_target_pairs={{0,8},{8,0},{16,24},{24,16},{1,9},{9,1},{17,25},{25,17},{2,10},{10... | collective-permute-start | bytes 786440 | tf_op jit(solution)/shard_map/ppermute | solution.py:31
  63.5 2.3 %collective-permute-start.12 = (bf16[128,2304]{1,0:T(8,128)(2,1)}, bf16[128,2304]{1,0:T(8,128)(2,1)S(1)}, u32[]{:S(2)}, u32[]{:S(2)}) collective-permute-start(bf16[128,2304]{1,0:T(8,128)(2,1)} %get-tuple-element.106), channel_id=1, source_target_pairs={{0,1},{1,0},{2,3},{3,2},{4,5},{5,4},{6,7},{7,6},{8,9},{9,8},{10,11... | collective-permute-start | bytes 1769480 | tf_op jit(solution)/shard_map/ppermute | solution.py:31
  66.9 6.8 %collective-permute-start.14 = (bf16[32,2304]{1,0:T(8,128)(2,1)S(1)}, bf16[32,2304]{1,0:T(8,128)(2,1)S(1)}, u32[]{:S(2)}, u32[]{:S(2)}) collective-permute-start(bf16[32,2304]{1,0:T(8,128)(2,1)S(1)} %get-tuple-element.161), channel_id=1, source_target_pairs={{0,2},{1,3},{2,0},{3,1},{4,6},{5,7},{6,4},{7,5},{8,10},{9,11},{10,... | collective-permute-start | bytes 442376 | tf_op jit(solution)/shard_map/ppermute | solution.py:31
  68.6 8.8 %collective-permute-start.16 = (bf16[128,2304]{1,0:T(8,128)(2,1)}, bf16[128,2304]{1,0:T(8,128)(2,1)S(1)}, u32[]{:S(2)}, u32[]{:S(2)}) collective-permute-start(bf16[128,2304]{1,0:T(8,128)(2,1)} %get-tuple-element.108), channel_id=1, source_target_pairs={{0,1},{1,0},{2,3},{3,2},{4,5},{5,4},{6,7},{7,6},{8,9},{9,8},{10,11... | collective-permute-start | bytes 1769480 | tf_op jit(solution)/shard_map/ppermute | solution.py:31
  68.6 11.0 %collective-permute-start.13 = (bf16[32,2304]{1,0:T(8,128)(2,1)S(1)}, bf16[32,2304]{1,0:T(8,128)(2,1)S(1)}, u32[]{:S(2)}, u32[]{:S(2)}) collective-permute-start(bf16[32,2304]{1,0:T(8,128)(2,1)S(1)} %get-tuple-element.160), channel_id=1, source_target_pairs={{0,2},{1,3},{2,0},{3,1},{4,6},{5,7},{6,4},{7,5},{8,10},{9,11},{10,... | collective-permute-start | bytes 442376 | tf_op jit(solution)/shard_map/ppermute | solution.py:31
  74.7 8.0 %collective-permute-start.15 = (bf16[32,2304]{1,0:T(8,128)(2,1)S(1)}, bf16[32,2304]{1,0:T(8,128)(2,1)S(1)}, u32[]{:S(2)}, u32[]{:S(2)}) collective-permute-start(bf16[32,2304]{1,0:T(8,128)(2,1)S(1)} %add_convert_fusion.7), channel_id=1, source_target_pairs={{0,4},{1,5},{2,6},{3,7},{4,0},{5,1},{6,2},{7,3},{8,12},{9,13},{10,... | collective-permute-start | bytes 442376 | tf_op jit(solution)/shard_map/ppermute | solution.py:31
  77.5 19.5 %collective-permute-start.17 = (bf16[32,2304]{1,0:T(8,128)(2,1)S(1)}, bf16[32,2304]{1,0:T(8,128)(2,1)S(1)}, u32[]{:S(2)}, u32[]{:S(2)}) collective-permute-start(bf16[32,2304]{1,0:T(8,128)(2,1)S(1)} %get-tuple-element.109), channel_id=1, source_target_pairs={{0,2},{1,3},{2,0},{3,1},{4,6},{5,7},{6,4},{7,5},{8,10},{9,11},{10,... | collective-permute-start | bytes 442376 | tf_op jit(solution)/shard_map/ppermute | solution.py:31
  79.1 9.0 %collective-permute-start.18 = (bf16[32,2304]{1,0:T(8,128)(2,1)S(1)}, bf16[32,2304]{1,0:T(8,128)(2,1)S(1)}, u32[]{:S(2)}, u32[]{:S(2)}) collective-permute-start(bf16[32,2304]{1,0:T(8,128)(2,1)S(1)} %get-tuple-element.110), channel_id=1, source_target_pairs={{0,2},{1,3},{2,0},{3,1},{4,6},{5,7},{6,4},{7,5},{8,10},{9,11},{10,... | collective-permute-start | bytes 442376 | tf_op jit(solution)/shard_map/ppermute | solution.py:31
  83.8 13.1 %collective-permute-start.21 = (bf16[32,2304]{1,0:T(8,128)(2,1)S(1)}, bf16[32,2304]{1,0:T(8,128)(2,1)S(1)}, u32[]{:S(2)}, u32[]{:S(2)}) collective-permute-start(bf16[32,2304]{1,0:T(8,128)(2,1)S(1)} %get-tuple-element.113.refs_0_), channel_id=1, source_target_pairs={{0,4},{1,5},{2,6},{3,7},{4,0},{5,1},{6,2},{7,3},{8,12},{9,13},{10,... | collective-permute-start | bytes 442376 | tf_op jit(solution)/shard_map/ppermute | solution.py:31
  88.1 10.7 %collective-permute-start.19 = (bf16[32,2304]{1,0:T(8,128)(2,1)S(1)}, bf16[32,2304]{1,0:T(8,128)(2,1)S(1)}, u32[]{:S(2)}, u32[]{:S(2)}) collective-permute-start(bf16[32,2304]{1,0:T(8,128)(2,1)S(1)} %add_convert_fusion.4), channel_id=1, source_target_pairs={{0,4},{1,5},{2,6},{3,7},{4,0},{5,1},{6,2},{7,3},{8,12},{9,13},{10,... | collective-permute-start | bytes 442376 | tf_op jit(solution)/shard_map/ppermute | solution.py:31
  88.5 19.5 %collective-permute-start.23 = (bf16[32,2304]{1,0:T(8,128)(2,1)S(1)}, bf16[32,2304]{1,0:T(8,128)(2,1)S(1)}, u32[]{:S(2)}, u32[]{:S(2)}) collective-permute-start(bf16[32,2304]{1,0:T(8,128)(2,1)S(1)} %get-tuple-element.113.refs_0_), channel_id=1, source_target_pairs={{0,1},{1,0},{2,3},{3,2},{4,5},{5,4},{6,7},{7,6},{8,9},{9,8},{10,11... | collective-permute-start | bytes 442376 | tf_op jit(solution)/shard_map/ppermute | solution.py:31
  88.5 11.3 %collective-permute-start.20 = (bf16[32,2304]{1,0:T(8,128)(2,1)S(1)}, bf16[32,2304]{1,0:T(8,128)(2,1)S(1)}, u32[]{:S(2)}, u32[]{:S(2)}) collective-permute-start(bf16[32,2304]{1,0:T(8,128)(2,1)S(1)} %get-tuple-element.113.refs_0_), channel_id=1, source_target_pairs={{0,2},{1,3},{2,0},{3,1},{4,6},{5,7},{6,4},{7,5},{8,10},{9,11},{10,... | collective-permute-start | bytes 442376 | tf_op jit(solution)/shard_map/ppermute | solution.py:31
  96.9 5.7 %collective-permute-start.22 = (bf16[32,2304]{1,0:T(8,128)(2,1)S(1)}, bf16[32,2304]{1,0:T(8,128)(2,1)S(1)}, u32[]{:S(2)}, u32[]{:S(2)}) collective-permute-start(bf16[32,2304]{1,0:T(8,128)(2,1)S(1)} %collective-permute-done.21.refs_2_), channel_id=1, source_target_pairs={{0,2},{1,3},{2,0},{3,1},{4,6},{5,7},{6,4},{7,5},{8,10},{9,11},{10,... | collective-permute-start | bytes 442376 | tf_op jit(solution)/shard_map/ppermute | solution.py:31
  98.9 9.2 %collective-permute-start.25 = (bf16[32,2304]{1,0:T(8,128)(2,1)S(1)}, bf16[32,2304]{1,0:T(8,128)(2,1)S(1)}, u32[]{:S(2)}, u32[]{:S(2)}) collective-permute-start(bf16[32,2304]{1,0:T(8,128)(2,1)S(1)} %collective-permute-done.21.refs_2_), channel_id=1, source_target_pairs={{0,1},{1,0},{2,3},{3,2},{4,5},{5,4},{6,7},{7,6},{8,9},{9,8},{10,11... | collective-permute-start | bytes 442376 | tf_op jit(solution)/shard_map/ppermute | solution.py:31
  99.8 8.9 %collective-permute-start.24 = (bf16[32,2304]{1,0:T(8,128)(2,1)S(1)}, bf16[32,2304]{1,0:T(8,128)(2,1)S(1)}, u32[]{:S(2)}, u32[]{:S(2)}) collective-permute-start(bf16[32,2304]{1,0:T(8,128)(2,1)S(1)} %collective-permute-done.20.refs_1_), channel_id=1, source_target_pairs={{0,1},{1,0},{2,3},{3,2},{4,5},{5,4},{6,7},{7,6},{8,9},{9,8},{10,11... | collective-permute-start | bytes 442376 | tf_op jit(solution)/shard_map/ppermute | solution.py:31
  102.7 6.0 %collective-permute-start.26 = (bf16[32,2304]{1,0:T(8,128)(2,1)S(1)}, bf16[32,2304]{1,0:T(8,128)(2,1)S(1)}, u32[]{:S(2)}, u32[]{:S(2)}) collective-permute-start(bf16[32,2304]{1,0:T(8,128)(2,1)S(1)} %collective-permute-done.22.refs_3_), channel_id=1, source_target_pairs={{0,1},{1,0},{2,3},{3,2},{4,5},{5,4},{6,7},{7,6},{8,9},{9,8},{10,11... | collective-permute-start | bytes 442376 | tf_op jit(solution)/shard_map/ppermute | solution.py:31
  103.6 16.9 %collective-permute-start.29 = (bf16[32,2304]{1,0:T(8,128)(2,1)S(1)}, bf16[32,2304]{1,0:T(8,128)(2,1)S(1)}, u32[]{:S(2)}, u32[]{:S(2)}) collective-permute-start(bf16[32,2304]{1,0:T(8,128)(2,1)S(1)} %get-tuple-element.122.refs_0_), channel_id=1, source_target_pairs={{0,6},{1,7},{2,4},{3,5},{4,2},{5,3},{6,0},{7,1},{8,14},{9,15},{10,... | collective-permute-start | bytes 442376 | tf_op jit(solution)/shard_map/ppermute | solution.py:31
  108.0 12.5 %collective-permute-start.28 = (bf16[32,2304]{1,0:T(8,128)(2,1)S(1)}, bf16[32,2304]{1,0:T(8,128)(2,1)S(1)}, u32[]{:S(2)}, u32[]{:S(2)}) collective-permute-start(bf16[32,2304]{1,0:T(8,128)(2,1)S(1)} %get-tuple-element.122.refs_0_), channel_id=1, source_target_pairs={{0,4},{1,5},{2,6},{3,7},{4,0},{5,1},{6,2},{7,3},{8,12},{9,13},{10,... | collective-permute-start | bytes 442376 | tf_op jit(solution)/shard_map/ppermute | solution.py:31
  108.1 12.5 %collective-permute-start.27 = (bf16[32,2304]{1,0:T(8,128)(2,1)S(1)}, bf16[32,2304]{1,0:T(8,128)(2,1)S(1)}, u32[]{:S(2)}, u32[]{:S(2)}) collective-permute-start(bf16[32,2304]{1,0:T(8,128)(2,1)S(1)} %get-tuple-element.122.refs_0_), channel_id=1, source_target_pairs={{0,2},{1,3},{2,0},{3,1},{4,6},{5,7},{6,4},{7,5},{8,10},{9,11},{10,... | collective-permute-start | bytes 442376 | tf_op jit(solution)/shard_map/ppermute | solution.py:31
  120.5 3.1 %collective-permute-start.30 = (bf16[32,2304]{1,0:T(8,128)(2,1)S(1)}, bf16[32,2304]{1,0:T(8,128)(2,1)S(1)}, u32[]{:S(2)}, u32[]{:S(2)}) collective-permute-start(bf16[32,2304]{1,0:T(8,128)(2,1)S(1)} %get-tuple-element.122.refs_0_), channel_id=1, source_target_pairs={{0,1},{1,0},{2,3},{3,2},{4,5},{5,4},{6,7},{7,6},{8,9},{9,8},{10,11... | collective-permute-start | bytes 442376 | tf_op jit(solution)/shard_map/ppermute | solution.py:31
  120.6 3.0 %collective-permute-start.31 = (bf16[32,2304]{1,0:T(8,128)(2,1)S(1)}, bf16[32,2304]{1,0:T(8,128)(2,1)S(1)}, u32[]{:S(2)}, u32[]{:S(2)}) collective-permute-start(bf16[32,2304]{1,0:T(8,128)(2,1)S(1)} %collective-permute-done.27.refs_1_), channel_id=1, source_target_pairs={{0,1},{1,0},{2,3},{3,2},{4,5},{5,4},{6,7},{7,6},{8,9},{9,8},{10,11... | collective-permute-start | bytes 442376 | tf_op jit(solution)/shard_map/ppermute | solution.py:31
  121.1 17.8 %collective-permute-start.36 = (bf16[2,64,1024]{2,1,0:T(8,128)(2,1)S(1)}, bf16[2,64,1024]{2,1,0:T(8,128)(2,1)S(1)}, u32[]{:S(2)}, u32[]{:S(2)}) collective-permute-start(bf16[2,64,1024]{2,1,0:T(8,128)(2,1)S(1)} %get-tuple-element.134), channel_id=1, source_target_pairs={{0,16},{8,24},{16,0},{24,8},{1,17},{9,25},{17,1},{25,9},{2,18},{10... | collective-permute-start | bytes 786440 | tf_op jit(solution)/shard_map/ppermute | solution.py:31
  122.6 17.8 %collective-permute-start.37 = (bf16[2,64,1024]{2,1,0:T(8,128)(2,1)S(1)}, bf16[2,64,1024]{2,1,0:T(8,128)(2,1)S(1)}, u32[]{:S(2)}, u32[]{:S(2)}) collective-permute-start(bf16[2,64,1024]{2,1,0:T(8,128)(2,1)S(1)} %get-tuple-element.137), channel_id=1, source_target_pairs={{0,16},{8,24},{16,0},{24,8},{1,17},{9,25},{17,1},{25,9},{2,18},{10... | collective-permute-start | bytes 786440 | tf_op jit(solution)/shard_map/ppermute | solution.py:31
  123.1 17.3 %collective-permute-start.35 = (bf16[2,64,1024]{2,1,0:T(8,128)(2,1)S(1)}, bf16[2,64,1024]{2,1,0:T(8,128)(2,1)S(1)}, u32[]{:S(2)}, u32[]{:S(2)}) collective-permute-start(bf16[2,64,1024]{2,1,0:T(8,128)(2,1)S(1)} %get-tuple-element.131), channel_id=1, source_target_pairs={{0,8},{8,0},{16,24},{24,16},{1,9},{9,1},{17,25},{25,17},{2,10},{10... | collective-permute-start | bytes 786440 | tf_op jit(solution)/shard_map/ppermute | solution.py:31
  123.6 2.9 %collective-permute-start.33 = (bf16[32,2304]{1,0:T(8,128)(2,1)S(1)}, bf16[32,2304]{1,0:T(8,128)(2,1)S(1)}, u32[]{:S(2)}, u32[]{:S(2)}) collective-permute-start(bf16[32,2304]{1,0:T(8,128)(2,1)S(1)} %collective-permute-done.29.refs_3_), channel_id=1, source_target_pairs={{0,1},{1,0},{2,3},{3,2},{4,5},{5,4},{6,7},{7,6},{8,9},{9,8},{10,11... | collective-permute-start | bytes 442376 | tf_op jit(solution)/shard_map/ppermute | solution.py:31
  125.0 15.5 %collective-permute-start.34 = (bf16[2,64,1024]{2,1,0:T(8,128)(2,1)S(1)}, bf16[2,64,1024]{2,1,0:T(8,128)(2,1)S(1)}, u32[]{:S(2)}, u32[]{:S(2)}) collective-permute-start(bf16[2,64,1024]{2,1,0:T(8,128)(2,1)S(1)} %get-tuple-element.130), channel_id=1, source_target_pairs={{0,8},{8,0},{16,24},{24,16},{1,9},{9,1},{17,25},{25,17},{2,10},{10... | collective-permute-start | bytes 786440 | tf_op jit(solution)/shard_map/ppermute | solution.py:31
  138.3 8.2 %collective-permute-start.41 = (bf16[2,64,1024]{2,1,0:T(8,128)(2,1)S(1)}, bf16[2,64,1024]{2,1,0:T(8,128)(2,1)S(1)}, u32[]{:S(2)}, u32[]{:S(2)}) collective-permute-start(bf16[2,64,1024]{2,1,0:T(8,128)(2,1)S(1)} %get-tuple-element.141), channel_id=1, source_target_pairs={{0,8},{8,0},{16,24},{24,16},{1,9},{9,1},{17,25},{25,17},{2,10},{10... | collective-permute-start | bytes 786440 | tf_op jit(solution)/shard_map/ppermute | solution.py:31
  138.9 9.3 %collective-permute-start.42 = (bf16[2,64,1024]{2,1,0:T(8,128)(2,1)S(1)}, bf16[2,64,1024]{2,1,0:T(8,128)(2,1)S(1)}, u32[]{:S(2)}, u32[]{:S(2)}) collective-permute-start(bf16[2,64,1024]{2,1,0:T(8,128)(2,1)S(1)} %get-tuple-element.143), channel_id=1, source_target_pairs={{0,16},{8,24},{16,0},{24,8},{1,17},{9,25},{17,1},{25,9},{2,18},{10... | collective-permute-start | bytes 786440 | tf_op jit(solution)/shard_map/ppermute | solution.py:31
  140.5 9.3 %collective-permute-start.40 = (f32[8,128]{1,0:T(8,128)S(1)}, f32[8,128]{1,0:T(8,128)S(1)}, u32[]{:S(2)}, u32[]{:S(2)}) collective-permute-start(f32[8,128]{1,0:T(8,128)S(1)} %add.152), channel_id=1, source_target_pairs={{0,24},{8,16},{16,8},{24,0},{1,25},{9,17},{17,9},{25,1},{2,26},{10... | collective-permute-start | bytes 12296 | tf_op jit(solution)/shard_map/ppermute | solution.py:31
  142.1 8.3 %collective-permute-start.39 = (f32[8,128]{1,0:T(8,128)S(1)}, f32[8,128]{1,0:T(8,128)S(1)}, u32[]{:S(2)}, u32[]{:S(2)}) collective-permute-start(f32[8,128]{1,0:T(8,128)S(1)} %add.152), channel_id=1, source_target_pairs={{0,16},{8,24},{16,0},{24,8},{1,17},{9,25},{17,1},{25,9},{2,18},{10... | collective-permute-start | bytes 12296 | tf_op jit(solution)/shard_map/ppermute | solution.py:31
  143.6 10.3 %collective-permute-start.43 = (bf16[2,64,1024]{2,1,0:T(8,128)(2,1)S(1)}, bf16[2,64,1024]{2,1,0:T(8,128)(2,1)S(1)}, u32[]{:S(2)}, u32[]{:S(2)}) collective-permute-start(bf16[2,64,1024]{2,1,0:T(8,128)(2,1)S(1)} %add_convert_fusion.3), channel_id=1, source_target_pairs={{0,16},{8,24},{16,0},{24,8},{1,17},{9,25},{17,1},{25,9},{2,18},{10... | collective-permute-start | bytes 786440 | tf_op jit(solution)/shard_map/ppermute | solution.py:31
  146.5 9.2 %collective-permute-start.44 = (bf16[2,64,1024]{2,1,0:T(8,128)(2,1)S(1)}, bf16[2,64,1024]{2,1,0:T(8,128)(2,1)S(1)}, u32[]{:S(2)}, u32[]{:S(2)}) collective-permute-start(bf16[2,64,1024]{2,1,0:T(8,128)(2,1)S(1)} %add_convert_fusion.2), channel_id=1, source_target_pairs={{0,8},{8,0},{16,24},{24,16},{1,9},{9,1},{17,25},{25,17},{2,10},{10... | collective-permute-start | bytes 786440 | tf_op jit(solution)/shard_map/ppermute | solution.py:31
  148.2 10.8 %collective-permute-start.38 = (f32[8,128]{1,0:T(8,128)S(1)}, f32[8,128]{1,0:T(8,128)S(1)}, u32[]{:S(2)}, u32[]{:S(2)}) collective-permute-start(f32[8,128]{1,0:T(8,128)S(1)} %add.152), channel_id=1, source_target_pairs={{0,8},{8,0},{16,24},{24,16},{1,9},{9,1},{17,25},{25,17},{2,10},{10... | collective-permute-start | bytes 12296 | tf_op jit(solution)/shard_map/ppermute | solution.py:31
  149.8 11.6 %collective-permute-start.45 = (bf16[2,64,1024]{2,1,0:T(8,128)(2,1)S(1)}, bf16[2,64,1024]{2,1,0:T(8,128)(2,1)S(1)}, u32[]{:S(2)}, u32[]{:S(2)}) collective-permute-start(bf16[2,64,1024]{2,1,0:T(8,128)(2,1)S(1)} %get-tuple-element.155), channel_id=1, source_target_pairs={{0,8},{8,0},{16,24},{24,16},{1,9},{9,1},{17,25},{25,17},{2,10},{10... | collective-permute-start | bytes 786440 | tf_op jit(solution)/shard_map/ppermute | solution.py:31
  150.3 11.1 %collective-permute-start.47 = (bf16[2,64,1024]{2,1,0:T(8,128)(2,1)S(1)}, bf16[2,64,1024]{2,1,0:T(8,128)(2,1)S(1)}, u32[]{:S(2)}, u32[]{:S(2)}) collective-permute-start(bf16[2,64,1024]{2,1,0:T(8,128)(2,1)S(1)} %add_convert_fusion.1), channel_id=1, source_target_pairs={{0,16},{8,24},{16,0},{24,8},{1,17},{9,25},{17,1},{25,9},{2,18},{10... | collective-permute-start | bytes 786440 | tf_op jit(solution)/shard_map/ppermute | solution.py:31
  153.9 10.0 %collective-permute-start.46 = (bf16[2,64,1024]{2,1,0:T(8,128)(2,1)S(1)}, bf16[2,64,1024]{2,1,0:T(8,128)(2,1)S(1)}, u32[]{:S(2)}, u32[]{:S(2)}) collective-permute-start(bf16[2,64,1024]{2,1,0:T(8,128)(2,1)S(1)} %get-tuple-element.157), channel_id=1, source_target_pairs={{0,16},{8,24},{16,0},{24,8},{1,17},{9,25},{17,1},{25,9},{2,18},{10... | collective-permute-start | bytes 786440 | tf_op jit(solution)/shard_map/ppermute | solution.py:31
  155.8 9.2 %collective-permute-start.48 = (bf16[2,64,1024]{2,1,0:T(8,128)(2,1)S(1)}, bf16[2,64,1024]{2,1,0:T(8,128)(2,1)S(1)}, u32[]{:S(2)}, u32[]{:S(2)}) collective-permute-start(bf16[2,64,1024]{2,1,0:T(8,128)(2,1)S(1)} %add_convert_fusion), channel_id=1, source_target_pairs={{0,8},{8,0},{16,24},{24,16},{1,9},{9,1},{17,25},{25,17},{2,10},{10... | collective-permute-start | bytes 786440 | tf_op jit(solution)/shard_map/ppermute | solution.py:31
  (19 other events, 284.6 us)
